TPU v7x, 32 devices: a whole 2x2x4 slice. The times are simulated.
32 devices in a mesh: groups: 2 (over x), tensor: 8 (over z, y), bank: 2 (over core).
Axes of the slice: x: 2, y: 2, z: 4, core: 2. Of those that a mesh axis runs over, the one named last changes fastest.
Arguments:
- normed_hidden_input: bfloat16 [32, 8192], P(('groups', 'bank'), 'tensor'), parts along dimension 0, may hold values from -6 to 6
- beam_adapter_index: int32 [32], P(('groups', 'bank')), parts along dimension 0, may hold values from 0 to 31
- beam_cache_length: int32 [32], P(('groups', 'bank')), parts along dimension 0, may hold values from 128 to 2048
- query_weight: bfloat16 [8192, 8192], P('tensor'), may hold values from -0.0625 to 0.0625
- keyvalue_weight: bfloat16 [8192, 2048], P('tensor'), may hold values from -0.0625 to 0.0625
- output_weight: bfloat16 [8192, 8192], P('tensor'), may hold values from -1 to 1
- lowrank_down_factors: bfloat16 [32, 8192, 64], P('bank', 'tensor'), may hold values from -0.0625 to 0.0625
- lowrank_up_factors: bfloat16 [32, 64, 8192], P('bank', None, 'tensor'), may hold values from -0.75 to 0.75
- paged_key_cache: bfloat16 [32, 2048, 1024], P(('groups', 'bank'), 'tensor'), parts along dimension 0, may hold values from -190 to 190
- paged_value_cache: bfloat16 [32, 2048, 1024], P(('groups', 'bank'), 'tensor'), parts along dimension 0, may hold values from -6 to 6
Outputs:
- mixed_out: bfloat16 [32, 8192], P(('groups', 'bank'), 'tensor'), parts along dimension 0
There are 2 independent parts, one for each index of `groups`. A program takes and returns all parts, laid end to end along the dimension named above; an argument that names none is the same for every part. Nothing has to cross between parts.
All inputs are finite; a program needn't handle non-finite values.
Results may differ from a plain program's by a relative error of at most 0.0071.
Values may be sent and summed in bfloat16 or wider, within the bound.
No kernel may reach another device: no remote copies, remote signals or barrier semaphores. Data moves between devices by JAX's collectives and lax.ppermute only.
A program may use at most 128 MiB of HBM per device.

v0:
```python
import jax
import jax.numpy as jnp
from jax import lax
from jax.sharding import PartitionSpec as P

HEAD_DIM = 128


def joined(x, axis, combine):
    everything = jax.tree.map(lambda part: lax.all_gather(part, axis), x)
    leading = jax.tree.map(lambda part: part[0], everything)

    def turn(k, so_far):
        return combine(so_far, jax.tree.map(lambda part: part[k], everything))

    return lax.fori_loop(1, lax.axis_size(axis), turn, leading)


def apply_rotary(values, positions, head_size):
    row_count, col_count = values.shape
    half_size = head_size // 2
    frequency = jnp.power(500000.0, -2.0 * jnp.arange(half_size, dtype=jnp.float32) / head_size)
    angles = positions.astype(jnp.float32)[:, None] * frequency[None, :]
    cosine_table = jnp.cos(angles)[:, None, :]
    sine_table = jnp.sin(angles)[:, None, :]
    shaped = values.reshape(row_count, col_count // head_size, 2, half_size)
    first_half = shaped[:, :, 0]
    second_half = shaped[:, :, 1]
    rotated = jnp.stack(
        [
            first_half * cosine_table - second_half * sine_table,
            second_half * cosine_table + first_half * sine_table,
        ],
        axis=2,
    )
    return rotated.reshape(row_count, col_count)


def combine_parts(first_part, second_part):
    peak_one, total_one, weighted_one = first_part
    peak_two, total_two, weighted_two = second_part
    peak_both = jnp.maximum(peak_one, peak_two)
    factor_one = jnp.exp(peak_one - peak_both)
    factor_two = jnp.exp(peak_two - peak_both)
    return (
        peak_both,
        total_one * factor_one + total_two * factor_two,
        weighted_one * factor_one[..., None] + weighted_two * factor_two[..., None],
    )


def finish_heads(peak_score, weight_total, weighted, score_new, value_rows):
    peak_final = jnp.maximum(peak_score, score_new)
    old_factor = jnp.exp(peak_score - peak_final)
    new_weight = jnp.exp(score_new - peak_final)
    weight_total = weight_total * old_factor + new_weight
    weighted = (
        weighted * old_factor[..., None]
        + new_weight.astype(jnp.bfloat16).astype(jnp.float32)[..., None] * value_rows
    )
    return weighted / weight_total[..., None]


def body(
    normed_hidden_input,
    beam_adapter_index,
    beam_cache_length,
    query_weight,
    keyvalue_weight,
    output_weight,
    lowrank_down_factors,
    lowrank_up_factors,
    paged_key_cache,
    paged_value_cache,
):
    beam_rows, width_part = normed_hidden_input.shape
    model_width = query_weight.shape[1]
    kv_width = keyvalue_weight.shape[1] // 2
    head_count = model_width // HEAD_DIM
    kv_heads = kv_width // HEAD_DIM
    group_size = head_count // kv_heads
    tensor_index = lax.axis_index("tensor")
    query_part = jnp.dot(normed_hidden_input, query_weight, preferred_element_type=jnp.float32)
    keyval_part = jnp.dot(normed_hidden_input, keyvalue_weight, preferred_element_type=jnp.float32)
    down_all, up_all = (
        lax.all_gather(lowrank_down_factors, "bank", axis=0, tiled=True),
        lax.all_gather(lowrank_up_factors, "bank", axis=0, tiled=True),
    )
    inner_part = jnp.einsum(
        "ci,cim->cm",
        normed_hidden_input,
        down_all[beam_adapter_index],
        preferred_element_type=jnp.float32,
    )
    inner_total = lax.psum(inner_part, "tensor").astype(jnp.bfloat16)
    lowrank_delta = jnp.einsum(
        "mc,mct->mt", inner_total, up_all[beam_adapter_index], preferred_element_type=jnp.float32
    )
    query_total, keyval = lax.psum((query_part, keyval_part), "tensor")
    delta_total = lax.all_gather(lowrank_delta, "tensor", axis=1, tiled=True)
    query_rotated = apply_rotary(query_total + delta_total, beam_cache_length, HEAD_DIM).astype(
        jnp.bfloat16
    )
    key_new = apply_rotary(keyval[:, :kv_width], beam_cache_length, HEAD_DIM).astype(jnp.bfloat16)
    value_new = keyval[:, kv_width:].astype(jnp.bfloat16)
    position_count = paged_key_cache.shape[1]
    query_heads = query_rotated.reshape(beam_rows, kv_heads, group_size, HEAD_DIM)
    key_block = paged_key_cache.reshape(beam_rows, position_count, kv_heads, HEAD_DIM)
    value_block = paged_value_cache.reshape(beam_rows, position_count, kv_heads, HEAD_DIM)
    score_scale = 1.0 / HEAD_DIM**0.5
    scores = (
        jnp.einsum("bkgh,bpkh->bkgp", query_heads, key_block, preferred_element_type=jnp.float32)
        * score_scale
    )
    position_ids = tensor_index * position_count + jnp.arange(position_count)
    live_mask = (position_ids[None, :] < beam_cache_length[:, None])[:, None, None, :]
    scores = jnp.where(live_mask, scores, -1e30)
    peak_score = jnp.max(scores, axis=-1)
    weights = jnp.where(live_mask, jnp.exp(scores - peak_score[..., None]), 0.0)
    weight_total = jnp.sum(weights, axis=-1)
    weighted = jnp.einsum(
        "bkgp,bpkh->bkgh",
        weights.astype(jnp.bfloat16),
        value_block,
        preferred_element_type=jnp.float32,
    )
    peak_score, weight_total, weighted = joined(
        (peak_score, weight_total, weighted), "tensor", combine_parts
    )
    score_new = (
        jnp.einsum(
            "bkgh,bkh->bkg",
            query_heads,
            key_new.reshape(beam_rows, kv_heads, HEAD_DIM),
            preferred_element_type=jnp.float32,
        )
        * score_scale
    )
    value_rows = value_new.reshape(beam_rows, kv_heads, HEAD_DIM).astype(jnp.float32)[:, :, None, :]
    attended = (
        finish_heads(peak_score, weight_total, weighted, score_new, value_rows)
        .reshape(beam_rows, model_width)
        .astype(jnp.bfloat16)
    )
    attended_cols = lax.dynamic_slice_in_dim(attended, tensor_index * width_part, width_part, 1)
    mixed_cols = lax.psum_scatter(
        lax.dot_general(
            output_weight,
            attended_cols,
            (((0,), (1,)), ((), ())),
            preferred_element_type=jnp.float32,
        ),
        "tensor",
        scatter_dimension=0,
        tiled=True,
    )
    return (normed_hidden_input.astype(jnp.float32) + mixed_cols.T).astype(jnp.bfloat16)


def solution(mesh):
    return jax.shard_map(
        body,
        mesh=mesh,
        in_specs=(
            P(("groups", "bank"), "tensor"),
            P(("groups", "bank")),
            P(("groups", "bank")),
            P("tensor", None),
            P("tensor", None),
            P("tensor", None),
            P("bank", "tensor", None),
            P("bank", None, "tensor"),
            P(("groups", "bank"), "tensor", None),
            P(("groups", "bank"), "tensor", None),
        ),
        out_specs=P(("groups", "bank"), "tensor"),
        check_vma=False,
    )
```

profile of v0, /device:TPU:0, one launch (start us, length us, event | category | flops | bytes accessed | tf_op | source)
XLA Modules:
  0.0 255.5 jit_solution(5387610537127161752)
XLA Ops:
  7.4 0.0 copy-start.1
  7.4 0.0 all-gather.7.cloned.1.call-start
  7.4 0.7 all-gather.7.cloned.1.call-update
  8.1 0.0 all-gather.9.cloned.1.call-start
  8.1 0.7 all-gather.9.cloned.1.call-update
  8.8 0.0 all-reduce.3.cloned.1.call-start
  8.9 0.0 copy-done.1
  8.9 3.5 %fusion.37 = f32[8,2048]{1,0:T(8,128)} fusion(bf16[8,1024]{1,0:T(8,128)(2,1)S(1)} %copy-done.1, bf16[1024,2048]{1,0:T(8,128)(2,1)} %param.16), kind=kOutput, calls=%fused_computation.63 | convolution fusion | flops 33554432 | bytes 4276224 | tf_op jit(solution)/shard_map/dot_general | solution.py:84
  12.4 0.0 copy-start.4
  12.4 0.0 copy-start.3
  12.4 8.8 %fusion.36 = f32[8,8192]{1,0:T(8,128)} fusion(bf16[8,1024]{1,0:T(8,128)(2,1)S(1)} %copy-done.1, bf16[1024,8192]{1,0:T(8,128)(2,1)} %param.15), kind=kOutput, calls=%fused_computation.62 | convolution fusion | flops 134217728 | bytes 17055744 | tf_op jit(solution)/shard_map/dot_general | solution.py:83
  21.2 0.0 all-reduce.3.cloned.1.call-update
  21.2 0.0 all-gather.11.cloned.1.call-start
  21.3 0.0 copy-done.4
  21.3 0.0 copy-done.3
  21.3 0.1 broadcast_compare_fusion
  21.4 0.1 multiply_cosine_fusion
  21.5 4.7 %all-gather.7.cloned.1.call-done = bf16[32,1024,64]{1,2,0:T(8,128)(2,1)} async-done(((bf16[16,1024,64]{1,2,0:T(8,128)(2,1)}), bf16[32,1024,64]{1,2,0:T(8,128)(2,1)}) %all-gather.7.cloned.1.call-update) | async-done | bytes 4194320 | tf_op jit(solution)/shard_map/all_gather | solution.py:86
  26.2 2.8 %gather_fusion = bf16[8,1024,64]{1,2,0:T(8,128)(2,1)S(1)} fusion(bf16[32,1024,64]{1,2,0:T(8,128)(2,1)} %all-gather.7.cloned.1.call-done, s32[1024]{0:T(1024)S(1)} %pad_clamp_fusion), kind=kCustom, calls=%fused_computation | custom fusion | bytes 2097184 | tf_op jit(solution)/shard_map/gather | solution.py:92
  29.0 0.4 fusion.25
  29.4 21.6 %psum.22 = bf16[8,64]{1,0:T(8,128)(2,1)S(1)} all-reduce(f32[8,64]{1,0:T(8,128)S(1)} %bitcast.88), channel_id=1, replica_groups=mesh['groups'=2,'tensor'=8,'bank'=2] {'tensor'}, use_global_device_ids=true, to_apply=%region_1.0 | all-reduce | flops 512 | bytes 3072 | tf_op jit(solution)/shard_map/psum | solution.py:95
  51.0 0.0 all-gather.9.cloned.1.call-done
  51.0 2.8 %gather_fusion.1 = bf16[8,64,1024]{2,1,0:T(8,128)(2,1)S(1)} fusion(bf16[32,64,1024]{2,1,0:T(8,128)(2,1)} %all-gather.9.cloned.1.call-done, s32[1024]{0:T(1024)S(1)} %pad_clamp_fusion), kind=kCustom, calls=%fused_computation.1 | custom fusion | bytes 2097184 | tf_op jit(solution)/shard_map/gather | solution.py:97
  53.9 0.2 fusion.30
  54.1 30.9 %all_gather.29 = f32[8,8192]{1,0:T(8,128)S(1)} all-gather(f32[8,1024]{1,0:T(8,128)S(1)} %bitcast.85), channel_id=1, replica_groups=mesh['groups'=2,'tensor'=8,'bank'=2] {'tensor'}, dimensions={1}, use_global_device_ids=true | all-gather | bytes 294912 | tf_op jit(solution)/shard_map/all_gather | solution.py:100
  85.0 10.4 %all-reduce.3.cloned.1.call-done = (f32[8,8192]{1,0:T(8,128)}, f32[8,2048]{1,0:T(8,128)}) async-done(((f32[8,8192]{1,0:T(8,128)}, f32[8,2048]{1,0:T(8,128)}), (f32[8,8192]{1,0:T(8,128)}, f32[8,2048]{1,0:T(8,128)})) %all-reduce.3.cloned.1.call-update) | async-done | bytes 327696 | tf_op jit(solution)/shard_map/psum | solution.py:99
  95.4 1.0 add.103
  96.4 0.4 reshape.113
  96.8 0.7 subtract_convert_fusion
  97.5 0.7 pad_maximum_fusion
  98.2 0.1 convert_element_type.52
  98.3 0.0 copy-start
  98.3 0.0 copy-start.2
  98.3 3.6 %fusion.35 = (f32[8,8,8]{2,1,0:T(8,128)S(1)}, f32[8,8,8,256]{3,2,1,0:T(8,128)S(1)}) fusion(bf16[8,8,8,128]{3,2,1,0:T(8,128)(2,1)S(1)} %convert_element_type.52, pred[8,256]{1,0:T(8,128)(4,1)S(1)} %broadcast_compare_fusion, bf16[8,256,1024]{2,1,0:T(8,128)(2,1)} %param.20), kind=kOutput, calls=%fused_computation.61 | convolution fusion | flops 33947136 | bytes 4853760 | tf_op jit(solution)/shard_map/bkgh,bpkh->bkgp/dot_general | solution.py:112
  101.9 0.0 copy-done
  101.9 1.5 fusion.3
  103.4 0.0 all-gather.11.cloned.1.call-update
  103.4 0.0 reduce-scatter.2.cloned.1.call-start
  103.5 0.0 copy-done.2
  103.5 0.1 reshape.116
  103.6 0.1 subtract_convert_fusion.1
  103.7 0.1 pad_maximum_fusion.1
  103.8 0.1 reshape.152
  103.9 0.3 fusion.16
  104.2 31.2 %all-gather.1 = f32[64,8,8]{2,1,0:T(8,128)S(1)} all-gather(f32[8,8,8]{2,1,0:T(8,128)S(1)} %fusion.16), channel_id=3, replica_groups=mesh['groups'=2,'tensor'=8,'bank'=2] {'tensor'}, dimensions={0}, use_global_device_ids=true | all-gather | bytes 18432 | tf_op jit(solution)/shard_map/all_gather | solution.py:10
  135.4 31.2 %all-gather = f32[64,8,8]{2,1,0:T(8,128)S(1)} all-gather(f32[8,8,8]{2,1,0:T(8,128)S(1)} %get-tuple-element.215), channel_id=2, replica_groups=mesh['groups'=2,'tensor'=8,'bank'=2] {'tensor'}, dimensions={0}, use_global_device_ids=true | all-gather | bytes 18432 | tf_op jit(solution)/shard_map/all_gather | solution.py:10
  166.6 0.2 fusion.38
  166.8 0.0 all-gather.11.cloned.1.call-done
  166.8 1.0 slice.48
  167.8 8.9 %while.19 = (s32[]{:T(128)}, f32[8,8,8]{2,1,0:T(8,128)S(1)}, f32[8,8,8]{2,1,0:T(8,128)S(1)}, f32[8,8,8,128]{3,2,1,0:T(8,128)S(1)}, f32[8,8,8,8]{3,2,1,0:T(8,128)...) while((s32[]{:T(128)}, f32[8,8,8]{2,1,0:T(8,128)S(1)}, ...), condition=%wide.region_5.6_spmd, body=%wide.region_4.5_spmd.sunk | while | flops 199685 | bytes 807063 | solution.py:16
  167.8 1.2 fusion.54
  169.1 1.2 fusion.54
  170.4 1.2 fusion.54
  171.7 1.2 fusion.54
  173.0 1.2 fusion.54
  174.2 1.2 fusion.54
  175.5 1.2 fusion.54
  176.8 0.3 fusion.21
  177.0 0.1 copy.46
  177.1 8.8 %convolution_bitcast_fusion = f32[8192,8]{0,1:T(8,128)} fusion(bf16[1024,8192]{1,0:T(8,128)(2,1)} %param.17, bf16[8,8192]{1,0:T(8,128)(2,1)S(1)} %bitcast.84, s32[]{:T(128)S(6)} %select_n.29), kind=kOutput, calls=%fused_computation.10 | convolution fusion | flops 134217728 | bytes 17055748 | tf_op jit(solution)/shard_map/dot_general | solution.py:147
  185.9 0.0 reduce-scatter.2.cloned.1.call-update
  185.9 60.6 %reduce-scatter.2.cloned.1.call-done = f32[1024,8]{0,1:T(8,128)} async-done(((f32[8192,8]{0,1:T(8,128)}), f32[1024,8]{0,1:T(8,128)}) %reduce-scatter.2.cloned.1.call-update) | async-done | bytes 32784 | tf_op jit(solution)/shard_map/reduce_scatter | solution.py:146
  246.6 1.4 fusion.24
  (19 shorter events, 0.3 us)
Async XLA Ops:
  7.4 1.5 copy-start.1
  7.4 18.8 %all-gather.7.cloned.1.call-start = ((), (), s32[]{:S(2)}) async-start(), calls=%async_computation.1 | async-start | bytes 6291456 | tf_op jit(solution)/shard_map/all_gather | solution.py:86
  8.1 42.9 %all-gather.9.cloned.1.call-start = ((), (), s32[]{:S(2)}) async-start(), calls=%async_computation.2 | async-start | bytes 6291456 | tf_op jit(solution)/shard_map/all_gather | solution.py:87
  8.8 86.6 %all-reduce.3.cloned.1.call-start = ((), (), s32[]{:S(2)}) async-start(), calls=%async_computation.5 | async-start | bytes 655360 | tf_op jit(solution)/shard_map/psum | solution.py:99
  12.4 8.9 %copy-start.4 = (s32[8]{0:T(128)S(1)}, s32[8]{0:T(128)}, u32[]{:S(2)}) copy-start(s32[8]{0:T(128)} %param.13) | copy-start | bytes 100
  12.4 8.9 %copy-start.3 = (s32[8]{0:T(128)S(1)}, s32[8]{0:T(128)}, u32[]{:S(2)}) copy-start(s32[8]{0:T(128)} %param.14) | copy-start | bytes 100
  21.2 145.6 %all-gather.11.cloned.1.call-start = ((), (), s32[]{:S(2)}) async-start(), calls=%async_computation.4 | async-start | bytes 2359296 | tf_op jit(solution)/shard_map/all_gather | solution.py:10
  98.3 3.6 %copy-start = (bf16[8,256,1024]{2,1,0:T(8,128)(2,1)S(1)}, bf16[8,256,1024]{2,1,0:T(8,128)(2,1)}, u32[]{:S(2)}) copy-start(bf16[8,256,1024]{2,1,0:T(8,128)(2,1)} %param.21) | copy-start | bytes 12582916
  98.3 5.2 %copy-start.2 = (f32[8,2048]{1,0:T(8,128)S(1)}, f32[8,2048]{1,0:T(8,128)}, u32[]{:S(2)}) copy-start(f32[8,2048]{1,0:T(8,128)} %get-tuple-element.201) | copy-start | bytes 196612
  103.4 143.1 %reduce-scatter.2.cloned.1.call-start = ((), (), s32[]{:S(2)}) async-start(), calls=%async_computation.3 | async-start | bytes 294912 | tf_op jit(solution)/shard_map/reduce_scatter | solution.py:146
Sparse Core Ops, SparseCore 0:
  9.8 16.3 all-gather.6
  27.8 14.8 all-gather.8
Sparse Core Ops, SparseCore 1:
  21.3 74.1 all-reduce.2
  103.5 50.7 all-gather.10
  186.0 60.5 reduce-scatter.1
where the time goes:
time: 256 us
  blocking collectives  115 us (45%)
  waiting for transfers between devices  77.2 us (30%)
  matrix products  26.9 us (11%)
  between operations  15.3 us (6%)
  other arithmetic  13.4 us (5%)
  local copies, waits for them, and re-layouts  7.45 us (3%)
    all_gather x2, blocking collectives, joined(): everything = jax.tree.map(lambda part: lax.all_gather(part, axis), x)  62.4 us
    reduce_scatter x1, waiting for transfers between devices, body(): lax.psum_scatter(lax.dot_general(output_weight, attended_cols, (((0,), (1...  60.6 us
    all_gather x1, blocking collectives, body(): delta_total = lax.all_gather(lowrank_delta, 'tensor', axis=1, tiled=True)  30.9 us
    psum x1, blocking collectives, body(): inner_total = lax.psum(inner_part, 'tensor').astype(jnp.bfloat16)  21.6 us
    psum x1, waiting for transfers between devices, body(): query_total, keyval = lax.psum((query_part, keyval_part), 'tensor')  10.4 us
    dot_general x1, matrix products, body(): jnp.dot(normed_hidden_input, query_weight, preferred_element_type=jnp.flo...  8.79 us
    dot_general x1, matrix products, body(): lax.dot_general(output_weight, attended_cols, (((0,), (1,)), ((), ())), p...  8.76 us
    add x7, other arithmetic, combine_parts(): weighted_one * factor_one[..., None] + weighted_two * factor_two[..., None]  8.5 us
  transfers between devices with their start and end apart: 5, of which 3 were waited for; matrix products, arithmetic and copies ran while one was open for 8% of the time, Pallas kernels for 0%

commit v1 on v0

--- a/solution.py
+++ b/solution.py
@@ -1,9 +1,428 @@
+import functools
+
 import jax
 import jax.numpy as jnp
 from jax import lax
+from jax.experimental import pallas as pl
+from jax.experimental.pallas import tpu as pltpu
 from jax.sharding import PartitionSpec as P
 
 HEAD_DIM = 128
+F32 = jnp.float32
+BF16 = jnp.bfloat16
+LINK = jnp.float32
+VMEM_LIMIT = 40 * 1024 * 1024
+
+
+def whole():
+    return pl.BlockSpec(memory_space=pltpu.VMEM)
+
+
+def iota(shape, axis):
+    return lax.broadcasted_iota(jnp.int32, shape, axis)
+
+
+def params():
+    return pltpu.CompilerParams(
+        vmem_limit_bytes=VMEM_LIMIT, dimension_semantics=("arbitrary",)
+    )
+
+
+def project_kernel(place, x_ref, wq_ref, wk_ref, wv_ref, *outs):
+    step = pl.program_id(0)
+    x = x_ref[...]
+    width = wq_ref.shape[1]
+    q = jnp.dot(x, wq_ref[...], preferred_element_type=F32).astype(LINK)
+    k = jnp.dot(x, wk_ref[...], preferred_element_type=F32).astype(LINK)
+    v = jnp.dot(x, wv_ref[...], preferred_element_type=F32).astype(LINK)
+    for slot, out in enumerate(outs):
+
+        @pl.when(step == slot)
+        def _(out=out):
+            out[:, :width] = q
+            out[:, width : width + HEAD_DIM] = k
+            out[:, width + HEAD_DIM :] = v
+
+
+def project(place, x, wq, wkv, ranks):
+    rows, depth = x.shape
+    width = wq.shape[1] // ranks
+    kv_heads = wkv.shape[1] // 2 // HEAD_DIM
+    return pl.pallas_call(
+        project_kernel,
+        grid_spec=pltpu.PrefetchScalarGridSpec(
+            num_scalar_prefetch=1,
+            grid=(ranks,),
+            in_specs=[
+                pl.BlockSpec((rows, depth), lambda s, p: (0, 0)),
+                pl.BlockSpec((depth, width), lambda s, p: (0, s ^ p[0])),
+                pl.BlockSpec((depth, HEAD_DIM), lambda s, p: (0, s ^ p[0])),
+                pl.BlockSpec((depth, HEAD_DIM), lambda s, p: (0, kv_heads + (s ^ p[0]))),
+            ],
+            out_specs=[pl.BlockSpec((rows, width + 2 * HEAD_DIM), lambda s, p: (0, 0))] * ranks,
+        ),
+        out_shape=[jax.ShapeDtypeStruct((rows, width + 2 * HEAD_DIM), LINK)] * ranks,
+        compiler_params=params(),
+        cost_estimate=pl.CostEstimate(
+            flops=2 * rows * depth * (wq.shape[1] + wkv.shape[1]),
+            bytes_accessed=2 * (wq.size + wkv.size),
+            transcendentals=0,
+        ),
+        name="project",
+    )(place, x, wq, wkv, wkv)
+
+
+def adapter_column(index_ref, rows):
+    row = iota((rows, HEAD_DIM), 0)
+    column = jnp.zeros((rows, HEAD_DIM), jnp.int32)
+    for r in range(rows):
+        column = jnp.where(row == r, index_ref[r], column)
+    return column
+
+
+def down_kernel(index_ref, bank_ref, x_ref, other_ref, down_ref, out_ref):
+    rows = 2 * x_ref.shape[0]
+    rank = down_ref.shape[1]
+    count = down_ref.shape[0]
+    x = jnp.concatenate([x_ref[...].astype(F32), other_ref[...].astype(F32)], axis=0)
+    flat = down_ref[...].reshape(count * rank, down_ref.shape[2])
+    every = lax.dot_general(
+        x.astype(BF16), flat, (((1,), (1,)), ((), ())), preferred_element_type=F32
+    )
+    column = adapter_column(index_ref, rows) - bank_ref[0] * count
+    lane = iota((rows, HEAD_DIM), 1)
+    per = HEAD_DIM // rank
+    total = jnp.zeros((rows, HEAD_DIM), F32)
+    for j in range(count // per):
+        part = every[:, j * HEAD_DIM : (j + 1) * HEAD_DIM]
+        total += jnp.where(lane // rank + j * per == column, part, 0.0)
+    out_ref[...] = total
+
+
+def down(index, bank, x, other, factors):
+    rows = 2 * x.shape[0]
+    smem = pl.BlockSpec(memory_space=pltpu.SMEM)
+    return pl.pallas_call(
+        down_kernel,
+        in_specs=[smem, smem, whole(), whole(), whole()],
+        out_specs=whole(),
+        out_shape=jax.ShapeDtypeStruct((rows, HEAD_DIM), F32),
+        compiler_params=pltpu.CompilerParams(vmem_limit_bytes=VMEM_LIMIT),
+        cost_estimate=pl.CostEstimate(
+            flops=2 * rows * factors.size, bytes_accessed=2 * factors.size, transcendentals=0
+        ),
+        name="down",
+    )(index, bank, x, other, factors)
+
+
+def up_kernel(index_ref, bank_ref, *refs):
+    *parts, up_ref, own_ref, other_ref = refs
+    rows = parts[0].shape[0]
+    count, rank, width = up_ref.shape
+    total = parts[0][...]
+    for part in parts[1:]:
+        total += part[...]
+    total = total.astype(BF16).astype(F32)
+    column = adapter_column(index_ref, rows) - bank_ref[0] * count
+    lane = iota((rows, HEAD_DIM), 1)
+    per = HEAD_DIM // rank
+    spread = jnp.concatenate(
+        [
+            jnp.where(lane // rank + j * per == column, total, 0.0)
+            for j in range(count // per)
+        ],
+        axis=1,
+    ).astype(BF16)
+    delta = jnp.dot(
+        spread, up_ref[...].reshape(count * rank, width), preferred_element_type=F32
+    )
+    own_ref[...] = delta[: rows // 2]
+    other_ref[...] = delta[rows // 2 :]
+
+
+def up(index, bank, parts, factors):
+    rows = parts[0].shape[0]
+    width = factors.shape[2]
+    smem = pl.BlockSpec(memory_space=pltpu.SMEM)
+    return pl.pallas_call(
+        up_kernel,
+        in_specs=[smem, smem] + [whole()] * (len(parts) + 1),
+        out_specs=[whole()] * 2,
+        out_shape=[jax.ShapeDtypeStruct((rows // 2, width), F32)] * 2,
+        compiler_params=pltpu.CompilerParams(vmem_limit_bytes=VMEM_LIMIT),
+        cost_estimate=pl.CostEstimate(
+            flops=2 * rows * factors.size, bytes_accessed=2 * factors.size, transcendentals=0
+        ),
+        name="up",
+    )(index, bank, *parts, factors)
+
+
+def rotate(v, cosine, sine):
+    return v * cosine + pltpu.roll(v, HEAD_DIM // 2, 1) * sine
+
+
+def rotate_kernel(*refs):
+    *parts, own_ref, other_ref, cos_ref, sin_ref, q_ref, k_ref, v_ref, rows_ref = refs
+    total = parts[0][...].astype(F32)
+    for part in parts[1:]:
+        total += part[...].astype(F32)
+    width = own_ref.shape[1]
+    query = total[:, :width] + (own_ref[...] + other_ref[...])
+    cosine, sine = cos_ref[...], sin_ref[...]
+    for g in range(width // HEAD_DIM):
+        rows_ref[:, g, :] = rotate(query[:, g * HEAD_DIM : (g + 1) * HEAD_DIM], cosine, sine)
+    q_ref[...] = rows_ref[...].reshape(q_ref.shape).astype(BF16)
+    k_ref[...] = (
+        rotate(total[:, width : width + HEAD_DIM], cosine, sine).astype(BF16).astype(F32)
+    )
+    v_ref[...] = total[:, width + HEAD_DIM :].astype(BF16).astype(F32)
+
+
+def rotated(parts, own, other, cosine, sine):
+    rows, width = own.shape
+    heads = width // HEAD_DIM
+    small = jax.ShapeDtypeStruct((rows, HEAD_DIM), F32)
+    return pl.pallas_call(
+        rotate_kernel,
+        in_specs=[whole()] * (len(parts) + 4),
+        out_specs=[whole()] * 3,
+        out_shape=[jax.ShapeDtypeStruct((rows * heads, HEAD_DIM), BF16), small, small],
+        scratch_shapes=[pltpu.VMEM((rows, heads, HEAD_DIM), F32)],
+        compiler_params=pltpu.CompilerParams(vmem_limit_bytes=VMEM_LIMIT),
+        name="rotate",
+    )(*parts, own, other, cosine, sine)
+
+
+def attend_kernel(ranks, place, length, *refs):
+    queries = refs[:ranks]
+    k_ref, v_ref = refs[ranks : ranks + 2]
+    outs = refs[ranks + 2 : 2 * ranks + 2]
+    q_rows, o_rows, stats = refs[2 * ranks + 2 :]
+    beam = pl.program_id(0)
+    beams = pl.num_programs(0)
+    rank = place[0]
+    group = q_rows.shape[1] // stats.shape[0]
+    heads = ranks * group
+    positions = k_ref.shape[1]
+
+    @pl.when(beam == 0)
+    def _():
+        for s, query in enumerate(queries):
+            q_rows[s] = query[...].astype(F32)
+
+    first = pl.multiple_of(beam * group, group)
+    q = q_rows[:, pl.ds(first, group), :].reshape(heads, HEAD_DIM)
+    key_head = (iota((heads, HEAD_DIM), 0) // group) ^ rank
+    wide = jnp.concatenate(
+        [jnp.where(key_head == c, q, 0.0) for c in range(ranks)], axis=1
+    ).astype(BF16)
+    scores = lax.dot_general(
+        wide, k_ref[0], (((1,), (1,)), ((), ())), preferred_element_type=F32
+    ) * (1.0 / HEAD_DIM**0.5)
+    live = rank * positions + iota((heads, positions), 1) < length[beam]
+    scores = jnp.where(live, scores, -1e30)
+    peak = jnp.max(scores, axis=1, keepdims=True)
+    weights = jnp.where(live, jnp.exp(scores - peak), 0.0)
+    total = jnp.sum(weights, axis=1, keepdims=True)
+    product = jnp.dot(weights.astype(BF16), v_ref[0], preferred_element_type=F32)
+    own = jnp.zeros((heads, HEAD_DIM), F32)
+    for c in range(ranks):
+        own = jnp.where(key_head == c, product[:, c * HEAD_DIM : (c + 1) * HEAD_DIM], own)
+    o_rows[:, pl.ds(first, group), :] = own.reshape(ranks, group, HEAD_DIM)
+    row, lane = iota((heads, HEAD_DIM), 0), iota((heads, HEAD_DIM), 1)
+    spread = jnp.where(row == lane, peak, 0.0) + jnp.where(row + heads == lane, total, 0.0)
+    stats[pl.ds(beam, 1), :] = jnp.sum(spread, axis=0, keepdims=True)
+
+    @pl.when(beam == beams - 1)
+    def _():
+        high = stats[...].astype(BF16).astype(F32)
+        rest = stats[...] - high
+        middle = rest.astype(BF16).astype(F32)
+        low = rest - middle
+        tail = jnp.concatenate([high, middle, low, jnp.zeros_like(low)], axis=0)
+        for s, out in enumerate(outs):
+            out[...] = jnp.concatenate([o_rows[s], tail], axis=0).astype(BF16)
+
+
+def attend(place, length, queries, keys, values):
+    ranks = len(queries)
+    beams, positions, width = keys.shape
+    rows = queries[0].shape[0]
+    out_rows = rows + 4 * beams
+    return pl.pallas_call(
+        functools.partial(attend_kernel, ranks),
+        grid_spec=pltpu.PrefetchScalarGridSpec(
+            num_scalar_prefetch=2,
+            grid=(beams,),
+            in_specs=[pl.BlockSpec((rows, HEAD_DIM), lambda i, p, n: (0, 0))] * ranks
+            + [pl.BlockSpec((1, positions, width), lambda i, p, n: (i, 0, 0))] * 2,
+            out_specs=[pl.BlockSpec((out_rows, HEAD_DIM), lambda i, p, n: (0, 0))] * ranks,
+            scratch_shapes=[
+                pltpu.VMEM((ranks, rows, HEAD_DIM), F32),
+                pltpu.VMEM((ranks, rows, HEAD_DIM), F32),
+                pltpu.VMEM((beams, HEAD_DIM), F32),
+            ],
+        ),
+        out_shape=[jax.ShapeDtypeStruct((out_rows, HEAD_DIM), BF16)] * ranks,
+        compiler_params=params(),
+        cost_estimate=pl.CostEstimate(
+            flops=4 * rows * ranks * positions * width,
+            bytes_accessed=4 * keys.size,
+            transcendentals=rows * ranks * positions,
+        ),
+        name="attend",
+    )(place, length, *queries, keys, values)
+
+
+def output_kernel(ranks, place, *refs):
+    parts = refs[:ranks]
+    q_ref, k_ref, v_ref, w_ref = refs[ranks : ranks + 4]
+    outs = refs[ranks + 4 : 2 * ranks + 4]
+    joined, attended = refs[2 * ranks + 4 :]
+    step = pl.program_id(0)
+    beams, group, _ = joined.shape
+    rows = beams * group
+
+    def by_row(v):
+        return jnp.broadcast_to(v[:, None, :], (beams, group, HEAD_DIM)).reshape(rows, HEAD_DIM)
+
+    @pl.when(step == 0)
+    def _():
+        row, lane = iota((rows, HEAD_DIM), 0), iota((rows, HEAD_DIM), 1)
+        heads = ranks * group
+        score = jnp.sum(
+            q_ref[...].astype(F32) * by_row(k_ref[...]), axis=1, keepdims=True
+        ) * (1.0 / HEAD_DIM**0.5)
+        peaks, totals, weighted = [], [], []
+        top = score
+        for s, part in enumerate(parts):
+            block = part[...].astype(F32)
+            tail = (
+                block[rows : rows + beams]
+                + block[rows + beams : rows + 2 * beams]
+                + block[rows + 2 * beams : rows + 3 * beams]
+            )
+            tail = by_row(tail)
+            head = s * group + row % group
+            peak = jnp.sum(jnp.where(lane == head, tail, 0.0), axis=1, keepdims=True)
+            total = jnp.sum(jnp.where(lane == heads + head, tail, 0.0), axis=1, keepdims=True)
+            top = jnp.maximum(top, peak)
+            peaks.append(peak)
+            totals.append(total)
+            weighted.append(block[:rows])
+        new = jnp.exp(score - top)
+        everything = new
+        result = new.astype(BF16).astype(F32) * by_row(v_ref[...])
+        for peak, total, block in zip(peaks, totals, weighted):
+            factor = jnp.exp(peak - top)
+            everything += total * factor
+            result += block * factor
+        joined[...] = (result / everything).reshape(joined.shape)
+        for g in range(group):
+            attended[:, g * HEAD_DIM : (g + 1) * HEAD_DIM] = joined[:, g, :].astype(BF16)
+
+    mixed = jnp.dot(attended[...], w_ref[...], preferred_element_type=F32).astype(BF16)
+    for slot, out in enumerate(outs):
+
+        @pl.when(step == slot)
+        def _(out=out):
+            out[...] = mixed
+
+
+def output(place, parts, query, key_new, value_new, weight):
+    ranks = len(parts)
+    beams = key_new.shape[0]
+    depth = weight.shape[0]
+    width = weight.shape[1] // ranks
+    group = depth // HEAD_DIM
+    once = lambda a: pl.BlockSpec(a.shape, lambda s, p: (0, 0))
+    return pl.pallas_call(
+        functools.partial(output_kernel, ranks),
+        grid_spec=pltpu.PrefetchScalarGridSpec(
+            num_scalar_prefetch=1,
+            grid=(ranks,),
+            in_specs=[once(a) for a in (*parts, query, key_new, value_new)]
+            + [pl.BlockSpec((depth, width), lambda s, p: (0, s ^ p[0]))],
+            out_specs=[pl.BlockSpec((beams, width), lambda s, p: (0, 0))] * ranks,
+            scratch_shapes=[
+                pltpu.VMEM((beams, group, HEAD_DIM), F32),
+                pltpu.VMEM((beams, depth), BF16),
+            ],
+        ),
+        out_shape=[jax.ShapeDtypeStruct((beams, width), BF16)] * ranks,
+        compiler_params=params(),
+        cost_estimate=pl.CostEstimate(
+            flops=2 * beams * weight.size, bytes_accessed=2 * weight.size, transcendentals=0
+        ),
+        name="output",
+    )(place, *parts, query, key_new, value_new, weight)
+
+
+def residual_kernel(x_ref, *refs):
+    *parts, out_ref = refs
+    total = parts[0][...].astype(F32)
+    for part in parts[1:]:
+        total += part[...].astype(F32)
+    out_ref[...] = (x_ref[...].astype(F32) + total).astype(BF16)
+
+
+def residual(x, parts):
+    return pl.pallas_call(
+        residual_kernel,
+        in_specs=[whole()] * (len(parts) + 1),
+        out_specs=whole(),
+        out_shape=jax.ShapeDtypeStruct(x.shape, BF16),
+        name="residual",
+    )(x, *parts)
+
+
+def traded(blocks, ranks):
+    return [blocks[0]] + [
+        lax.ppermute(blocks[s], "tensor", [(i, i ^ s) for i in range(ranks)])
+        for s in range(1, ranks)
+    ]
+
+
+def matched_body(
+    normed_hidden_input,
+    beam_adapter_index,
+    beam_cache_length,
+    query_weight,
+    keyvalue_weight,
+    output_weight,
+    lowrank_down_factors,
+    lowrank_up_factors,
+    paged_key_cache,
+    paged_value_cache,
+):
+    x = normed_hidden_input
+    ranks = lax.axis_size("tensor")
+    place = lax.axis_index("tensor").astype(jnp.int32).reshape(1)
+    bank = lax.axis_index("bank").astype(jnp.int32).reshape(1)
+    swap = [(0, 1), (1, 0)]
+    x_other = lax.ppermute(x, "bank", swap)
+    index = jnp.concatenate([beam_adapter_index, lax.ppermute(beam_adapter_index, "bank", swap)])
+    half = HEAD_DIM // 2
+    frequency = jnp.power(500000.0, -2.0 * jnp.arange(half, dtype=F32) / HEAD_DIM)
+    angles = beam_cache_length.astype(F32)[:, None] * frequency[None, :]
+    cosine = jnp.tile(jnp.cos(angles), (1, 2))
+    sine = jnp.sin(angles)
+    sine = jnp.concatenate([-sine, sine], axis=1)
+
+    parts = traded(project(place, x, query_weight, keyvalue_weight, ranks), ranks)
+    inner = down(index, bank, x, x_other, lowrank_down_factors.swapaxes(1, 2))
+    delta_own, delta_sent = up(index, bank, traded([inner] * ranks, ranks), lowrank_up_factors)
+    delta_other = lax.ppermute(delta_sent, "bank", swap)
+    query, key_new, value_new = rotated(parts, delta_own, delta_other, cosine, sine)
+    partial = attend(
+        place,
+        beam_cache_length,
+        traded([query] * ranks, ranks),
+        paged_key_cache,
+        paged_value_cache,
+    )
+    mixed = output(place, traded(partial, ranks), query, key_new, value_new, output_weight)
+    return residual(x, traded(mixed, ranks))
 
 
 def joined(x, axis, combine):
@@ -158,8 +577,9 @@
 
 
 def solution(mesh):
+    matched = mesh.shape["tensor"] == 8 and mesh.shape["bank"] == 2
     return jax.shard_map(
-        body,
+        matched_body if matched else body,
         mesh=mesh,
         in_specs=(
             P(("groups", "bank"), "tensor"),

time: 256 us -> 121 us (0.47)
  blocking collectives: 115 us -> 0 us
  starting transfers between devices: 0.17 us -> 57.6 us
  waiting for transfers between devices: 77.2 us -> 22 us
  Pallas kernels: 0 us -> 28.6 us
  matrix products: 26.9 us -> 0 us
  between operations: 15.3 us -> 0.15 us
  other arithmetic: 13.4 us -> 0.93 us
  local copies, waits for them, and re-layouts: 7.45 us -> 10.9 us
    all_gather x3 -> x0, blocking collectives: 93.2 us -> none  [the longest x2 62.4 us: joined(): everything = jax.tree.map(lambda part: lax.all_gather(part, axis), x)]
    reduce_scatter x1 -> x0, waiting for transfers between devices: 60.6 us -> none  [body(): lax.psum_scatter(lax.dot_general(output_weight, attended_cols, (((0,), (1...]
    ppermute x0 -> x38, starting transfers between devices: none -> 57.6 us  [the longest x35 57.1 us: traded(): lax.ppermute(blocks[s], 'tensor', [(i, i ^ s) for i in range(ranks)])]
    pallas_call x0 -> x7, Pallas kernels: none -> 28.6 us  [the longest x1 9.74 us: project(): pl.pallas_call(project_kernel, grid_spec=pltpu.PrefetchScalarGridSpec(num...]
    dot_general x8 -> x0, matrix products: 26.9 us -> none  [the longest x1 8.79 us: body(): jnp.dot(normed_hidden_input, query_weight, preferred_element_type=jnp.flo...]
    ppermute x0 -> x38, waiting for transfers between devices: none -> 22 us  [the longest x35 21.1 us: traded(): lax.ppermute(blocks[s], 'tensor', [(i, i ^ s) for i in range(ranks)])]
    psum x1 -> x0, blocking collectives: 21.6 us -> none  [body(): inner_total = lax.psum(inner_part, 'tensor').astype(jnp.bfloat16)]
    unnamed x11 -> x32, local copies, waits for them, and re-layouts: 0.11 us -> 10.8 us
  transfers between devices with their start and end apart: 5 -> 38, of which waited for: 3 -> 10; matrix products, arithmetic and copies ran while one was open for 8% -> 1% of each run, Pallas kernels for 0% -> 9%
where the time goes in v1:
time: 121 us; the launch traced here: 120 us
  starting transfers between devices  57.6 us (48%)
  Pallas kernels  28.6 us (24%)
  waiting for transfers between devices  22 us (18%)
  local copies, waits for them, and re-layouts  10.9 us (9%)
    ppermute x35, starting transfers between devices, traded(): lax.ppermute(blocks[s], 'tensor', [(i, i ^ s) for i in range(ranks)])  57.1 us
    ppermute x35, waiting for transfers between devices, traded(): lax.ppermute(blocks[s], 'tensor', [(i, i ^ s) for i in range(ranks)])  21.1 us
    unnamed x32, local copies, waits for them, and re-layouts  10.8 us
    pallas_call x1, Pallas kernels, project(): pl.pallas_call(project_kernel, grid_spec=pltpu.PrefetchScalarGridSpec(num...  9.74 us
    pallas_call x1, Pallas kernels, output(): pl.pallas_call(functools.partial(output_kernel, ranks), grid_spec=pltpu.P...  9.26 us
    pallas_call x1, Pallas kernels, attend(): pl.pallas_call(functools.partial(attend_kernel, ranks), grid_spec=pltpu.P...  5.89 us
  transfers between devices with their start and end apart: 38, of which 10 were waited for; matrix products, arithmetic and copies ran while one was open for 1% of the time, Pallas kernels for 9%

profile of v1, /device:TPU:0, one launch (start us, length us, event | category | flops | bytes accessed | tf_op | source)
XLA Modules:
  0.0 120.2 jit_solution(14658775135546102016)
XLA Ops:
  0.0 0.5 collective-permute-start.7
  0.5 0.1 collective-permute-start.8
  0.5 0.9 collective-permute-done.7
  1.4 0.7 pad_add_fusion.index_ref
  2.1 0.0 collective-permute-done.8.other_ref
  2.1 1.6 %copy-done.3 = bf16[16,1024,64]{1,2,0:T(8,128)(2,1)S(1)} copy-done((bf16[16,1024,64]{1,2,0:T(8,128)(2,1)S(1)}, bf16[16,1024,64]{1,2,0:T(8,128)(2,1)}, u32[]{:S(2)}) %copy-start.3) | copy-done | bytes 2097176
  3.7 0.7 copy-done.5
  4.5 1.2 down.1.refs_0_
  5.6 2.9 %collective-permute-start.10 = (f32[16,128]{1,0:T(8,128)S(1)}, f32[16,128]{1,0:T(8,128)S(1)}, u32[]{:S(2)}, u32[]{:S(2)}) collective-permute-start(f32[16,128]{1,0:T(8,128)S(1)} %down.1.refs_0_), channel_id=1, source_target_pairs={{0,4},{2,6},{4,0},{6,2},{8,12},{10,14},{12,8},{14,10},{1,5},{3,7},... | collective-permute-start | bytes 24584 | tf_op jit(solution)/shard_map/ppermute | solution.py:381
  8.5 1.4 %collective-permute-start.11 = (f32[16,128]{1,0:T(8,128)S(1)}, f32[16,128]{1,0:T(8,128)S(1)}, u32[]{:S(2)}, u32[]{:S(2)}) collective-permute-start(f32[16,128]{1,0:T(8,128)S(1)} %down.1.refs_0_), channel_id=1, source_target_pairs={{0,6},{2,4},{4,2},{6,0},{8,14},{10,12},{12,10},{14,8},{1,7},{3,5},... | collective-permute-start | bytes 24584 | tf_op jit(solution)/shard_map/ppermute | solution.py:381
  9.9 2.6 %collective-permute-start.12 = (f32[16,128]{1,0:T(8,128)S(1)}, f32[16,128]{1,0:T(8,128)S(1)}, u32[]{:S(2)}, u32[]{:S(2)}) collective-permute-start(f32[16,128]{1,0:T(8,128)S(1)} %down.1.refs_0_), channel_id=1, source_target_pairs={{0,8},{2,10},{4,12},{6,14},{8,0},{10,2},{12,4},{14,6},{1,9},{3,11}... | collective-permute-start | bytes 24584 | tf_op jit(solution)/shard_map/ppermute | solution.py:381
  12.5 0.0 collective-permute-start.13
  12.5 3.9 %collective-permute-start.14 = (f32[16,128]{1,0:T(8,128)S(1)}, f32[16,128]{1,0:T(8,128)S(1)}, u32[]{:S(2)}, u32[]{:S(2)}) collective-permute-start(f32[16,128]{1,0:T(8,128)S(1)} %down.1.refs_0_), channel_id=1, source_target_pairs={{0,12},{2,14},{4,8},{6,10},{8,4},{10,6},{12,0},{14,2},{1,13},{3,15... | collective-permute-start | bytes 24584 | tf_op jit(solution)/shard_map/ppermute | solution.py:381
  16.4 2.2 %copy-done = bf16[1024,2048]{1,0:T(8,128)(2,1)S(1)} copy-done((bf16[1024,2048]{1,0:T(8,128)(2,1)S(1)}, bf16[1024,2048]{1,0:T(8,128)(2,1)}, u32[]{:S(2)}) %copy-start) | copy-done | bytes 4194328
  18.6 0.7 copy-done.6
  19.3 9.7 %project.1 = (f32[8,1280]{1,0:T(8,128)S(1)}, f32[8,1280]{1,0:T(8,128)S(1)}, f32[8,1280]{1,0:T(8,128)S(1)}, f32[8,1280]{1,0:T(8,128)S(1)}, f32[8,1280]{1,0:T(8,12...) custom-call(s32[1]{0:T(128)} %bitcast.place, bf16[8,1024]{1,0:T(8,128)(2,1)S(1)} %copy-done.6, ...), custom_call_target="tpu_custom_call" | custom-call | flops 167772160 | bytes 20971520 | tf_op jit(solution)/shard_map/project/pallas_call | solution.py:51
  29.1 0.0 collective-permute-done.10.refs_2_
  29.1 1.6 %collective-permute-start = (f32[8,1280]{1,0:T(8,128)S(1)}, f32[8,1280]{1,0:T(8,128)S(1)}, u32[]{:S(2)}, u32[]{:S(2)}) collective-permute-start(f32[8,1280]{1,0:T(8,128)S(1)} %get-tuple-element.35), channel_id=1, source_target_pairs={{0,2},{2,0},{4,6},{6,4},{8,10},{10,8},{12,14},{14,12},{1,3},{3,1},... | collective-permute-start | bytes 122888 | tf_op jit(solution)/shard_map/ppermute | solution.py:381
  30.7 2.0 %collective-permute-start.2 = (f32[8,1280]{1,0:T(8,128)S(1)}, f32[8,1280]{1,0:T(8,128)S(1)}, u32[]{:S(2)}, u32[]{:S(2)}) collective-permute-start(f32[8,1280]{1,0:T(8,128)S(1)} %get-tuple-element.37), channel_id=1, source_target_pairs={{0,6},{2,4},{4,2},{6,0},{8,14},{10,12},{12,10},{14,8},{1,7},{3,5},... | collective-permute-start | bytes 122888 | tf_op jit(solution)/shard_map/ppermute | solution.py:381
  32.7 1.2 collective-permute-start.15
  33.9 0.4 collective-permute-start.9
  34.3 0.1 fusion
  34.4 4.6 %collective-permute-done.15.refs_7_ = f32[16,128]{1,0:T(8,128)S(1)} collective-permute-done((f32[16,128]{1,0:T(8,128)S(1)}, f32[16,128]{1,0:T(8,128)S(1)}, u32[]{:S(2)}, u32[]{:S(2)}) %collective-permute-start.15) | collective-permute-done | bytes 8224 | tf_op jit(solution)/shard_map/ppermute | solution.py:381
  39.0 3.9 %collective-permute-start.4 = (f32[8,1280]{1,0:T(8,128)S(1)}, f32[8,1280]{1,0:T(8,128)S(1)}, u32[]{:S(2)}, u32[]{:S(2)}) collective-permute-start(f32[8,1280]{1,0:T(8,128)S(1)} %get-tuple-element.39), channel_id=1, source_target_pairs={{0,10},{2,8},{4,14},{6,12},{8,2},{10,0},{12,6},{14,4},{1,11},{3,9}... | collective-permute-start | bytes 122888 | tf_op jit(solution)/shard_map/ppermute | solution.py:381
  42.9 0.9 up.1
  43.8 0.2 collective-permute-start.5
  44.1 3.5 %collective-permute-start.6 = (f32[8,1280]{1,0:T(8,128)S(1)}, f32[8,1280]{1,0:T(8,128)S(1)}, u32[]{:S(2)}, u32[]{:S(2)}) collective-permute-start(f32[8,1280]{1,0:T(8,128)S(1)} %get-tuple-element.41), channel_id=1, source_target_pairs={{0,14},{2,12},{4,10},{6,8},{8,6},{10,4},{12,2},{14,0},{1,15},{3,13... | collective-permute-start | bytes 122888 | tf_op jit(solution)/shard_map/ppermute | solution.py:381
  47.6 0.1 pad_maximum_fusion.refs_11_
  47.7 0.1 tile.10.refs_10_
  47.8 1.9 %collective-permute-done.5.refs_6_ = f32[8,1280]{1,0:T(8,128)S(1)} collective-permute-done((f32[8,1280]{1,0:T(8,128)S(1)}, f32[8,1280]{1,0:T(8,128)S(1)}, u32[]{:S(2)}, u32[]{:S(2)}) %collective-permute-start.5) | collective-permute-done | bytes 40992 | tf_op jit(solution)/shard_map/ppermute | solution.py:381
  49.6 1.1 collective-permute-done.6.refs_7_
  50.8 0.1 rotate.1
  50.9 0.8 collective-permute-start.17
  51.7 2.7 %collective-permute-start.19 = (bf16[64,128]{1,0:T(8,128)(2,1)S(1)}, bf16[64,128]{1,0:T(8,128)(2,1)S(1)}, u32[]{:S(2)}, u32[]{:S(2)}) collective-permute-start(bf16[64,128]{1,0:T(8,128)(2,1)S(1)} %get-tuple-element.44.refs_0_.refs_8_), channel_id=1, source_target_pairs={{0,6},{2,4},{4,2},{6,0},{8,14},{10,12},{12,10},{14,8},{1,7},{3,5},... | collective-permute-start | bytes 49160 | tf_op jit(solution)/shard_map/ppermute | solution.py:381
  54.4 2.2 %collective-permute-start.20 = (bf16[64,128]{1,0:T(8,128)(2,1)S(1)}, bf16[64,128]{1,0:T(8,128)(2,1)S(1)}, u32[]{:S(2)}, u32[]{:S(2)}) collective-permute-start(bf16[64,128]{1,0:T(8,128)(2,1)S(1)} %get-tuple-element.44.refs_0_.refs_8_), channel_id=1, source_target_pairs={{0,8},{2,10},{4,12},{6,14},{8,0},{10,2},{12,4},{14,6},{1,9},{3,11}... | collective-permute-start | bytes 49160 | tf_op jit(solution)/shard_map/ppermute | solution.py:381
  56.6 1.0 collective-permute-start.21
  57.6 3.3 %collective-permute-start.22 = (bf16[64,128]{1,0:T(8,128)(2,1)S(1)}, bf16[64,128]{1,0:T(8,128)(2,1)S(1)}, u32[]{:S(2)}, u32[]{:S(2)}) collective-permute-start(bf16[64,128]{1,0:T(8,128)(2,1)S(1)} %get-tuple-element.44.refs_0_.refs_8_), channel_id=1, source_target_pairs={{0,12},{2,14},{4,8},{6,10},{8,4},{10,6},{12,0},{14,2},{1,13},{3,15... | collective-permute-start | bytes 49160 | tf_op jit(solution)/shard_map/ppermute | solution.py:381
  60.9 1.2 collective-permute-start.23
  62.1 0.0 collective-permute-done.21.refs_5_
  62.1 1.0 collective-permute-done.22.refs_6_
  63.1 4.3 %collective-permute-done.23.refs_7_ = bf16[64,128]{1,0:T(8,128)(2,1)S(1)} collective-permute-done((bf16[64,128]{1,0:T(8,128)(2,1)S(1)}, bf16[64,128]{1,0:T(8,128)(2,1)S(1)}, u32[]{:S(2)}, u32[]{:S(2)}) %collective-permute-start.23) | collective-permute-done | bytes 16416 | tf_op jit(solution)/shard_map/ppermute | solution.py:381
  67.4 2.2 %copy-done.1 = bf16[8,256,1024]{2,1,0:T(8,128)(2,1)S(1)} copy-done((bf16[8,256,1024]{2,1,0:T(8,128)(2,1)S(1)}, bf16[8,256,1024]{2,1,0:T(8,128)(2,1)}, u32[]{:S(2)}) %copy-start.1) | copy-done | bytes 4194328
  69.6 2.2 %copy-done.2 = bf16[8,256,1024]{2,1,0:T(8,128)(2,1)S(1)} copy-done((bf16[8,256,1024]{2,1,0:T(8,128)(2,1)S(1)}, bf16[8,256,1024]{2,1,0:T(8,128)(2,1)}, u32[]{:S(2)}) %copy-start.2) | copy-done | bytes 4194328
  71.7 5.9 %attend.1 = (bf16[96,128]{1,0:T(8,128)(2,1)S(1)}, bf16[96,128]{1,0:T(8,128)(2,1)S(1)}, bf16[96,128]{1,0:T(8,128)(2,1)S(1)}, bf16[96,128]{1,0:T(8,128)(2,1)S(1)},...) custom-call(s32[1]{0:T(128)} %bitcast.place, ...), custom_call_target="tpu_custom_call" | custom-call | flops 536870912 | bytes 8388608 | tf_op jit(solution)/shard_map/attend/pallas_call | solution.py:252
  77.6 1.6 %collective-permute-start.24 = (bf16[96,128]{1,0:T(8,128)(2,1)S(1)}, bf16[96,128]{1,0:T(8,128)(2,1)S(1)}, u32[]{:S(2)}, u32[]{:S(2)}) collective-permute-start(bf16[96,128]{1,0:T(8,128)(2,1)S(1)} %get-tuple-element.46), channel_id=1, source_target_pairs={{0,2},{2,0},{4,6},{6,4},{8,10},{10,8},{12,14},{14,12},{1,3},{3,1},... | collective-permute-start | bytes 73736 | tf_op jit(solution)/shard_map/ppermute | solution.py:381
  79.2 2.0 %collective-permute-start.26 = (bf16[96,128]{1,0:T(8,128)(2,1)S(1)}, bf16[96,128]{1,0:T(8,128)(2,1)S(1)}, u32[]{:S(2)}, u32[]{:S(2)}) collective-permute-start(bf16[96,128]{1,0:T(8,128)(2,1)S(1)} %get-tuple-element.48), channel_id=1, source_target_pairs={{0,6},{2,4},{4,2},{6,0},{8,14},{10,12},{12,10},{14,8},{1,7},{3,5},... | collective-permute-start | bytes 73736 | tf_op jit(solution)/shard_map/ppermute | solution.py:381
  81.2 3.9 %collective-permute-start.28 = (bf16[96,128]{1,0:T(8,128)(2,1)S(1)}, bf16[96,128]{1,0:T(8,128)(2,1)S(1)}, u32[]{:S(2)}, u32[]{:S(2)}) collective-permute-start(bf16[96,128]{1,0:T(8,128)(2,1)S(1)} %get-tuple-element.50), channel_id=1, source_target_pairs={{0,10},{2,8},{4,14},{6,12},{8,2},{10,0},{12,6},{14,4},{1,11},{3,9}... | collective-permute-start | bytes 73736 | tf_op jit(solution)/shard_map/ppermute | solution.py:381
  85.1 0.2 collective-permute-start.29
  85.3 3.6 %collective-permute-start.30 = (bf16[96,128]{1,0:T(8,128)(2,1)S(1)}, bf16[96,128]{1,0:T(8,128)(2,1)S(1)}, u32[]{:S(2)}, u32[]{:S(2)}) collective-permute-start(bf16[96,128]{1,0:T(8,128)(2,1)S(1)} %get-tuple-element.52), channel_id=1, source_target_pairs={{0,14},{2,12},{4,10},{6,8},{8,6},{10,4},{12,2},{14,0},{1,15},{3,13... | collective-permute-start | bytes 73736 | tf_op jit(solution)/shard_map/ppermute | solution.py:381
  88.9 1.8 %collective-permute-done.29.refs_6_ = bf16[96,128]{1,0:T(8,128)(2,1)S(1)} collective-permute-done((bf16[96,128]{1,0:T(8,128)(2,1)S(1)}, bf16[96,128]{1,0:T(8,128)(2,1)S(1)}, u32[]{:S(2)}, u32[]{:S(2)}) %collective-permute-start.29) | collective-permute-done | bytes 24608 | tf_op jit(solution)/shard_map/ppermute | solution.py:381
  90.7 1.1 collective-permute-done.30.refs_7_
  91.8 9.3 %output.1 = (bf16[8,1024]{1,0:T(8,128)(2,1)S(1)}, bf16[8,1024]{1,0:T(8,128)(2,1)S(1)}, bf16[8,1024]{1,0:T(8,128)(2,1)S(1)}, bf16[8,1024]{1,0:T(8,128)(2,1)S(1)},...) custom-call(s32[1]{0:T(128)} %bitcast.place, ...), custom_call_target="tpu_custom_call" | custom-call | flops 134217728 | bytes 16777216 | tf_op jit(solution)/shard_map/output/pallas_call | solution.py:339
  101.1 0.6 copy-done.7
  101.7 0.8 collective-permute-start.31
  102.5 2.7 %collective-permute-start.33 = (bf16[8,1024]{1,0:T(8,128)(2,1)S(1)}, bf16[8,1024]{1,0:T(8,128)(2,1)S(1)}, u32[]{:S(2)}, u32[]{:S(2)}) collective-permute-start(bf16[8,1024]{1,0:T(8,128)(2,1)S(1)} %get-tuple-element.58), channel_id=1, source_target_pairs={{0,6},{2,4},{4,2},{6,0},{8,14},{10,12},{12,10},{14,8},{1,7},{3,5},... | collective-permute-start | bytes 49160 | tf_op jit(solution)/shard_map/ppermute | solution.py:381
  105.2 2.2 %collective-permute-start.34 = (bf16[8,1024]{1,0:T(8,128)(2,1)S(1)}, bf16[8,1024]{1,0:T(8,128)(2,1)S(1)}, u32[]{:S(2)}, u32[]{:S(2)}) collective-permute-start(bf16[8,1024]{1,0:T(8,128)(2,1)S(1)} %get-tuple-element.59), channel_id=1, source_target_pairs={{0,8},{2,10},{4,12},{6,14},{8,0},{10,2},{12,4},{14,6},{1,9},{3,11}... | collective-permute-start | bytes 49160 | tf_op jit(solution)/shard_map/ppermute | solution.py:381
  107.3 1.0 collective-permute-start.35
  108.3 3.4 %collective-permute-start.36 = (bf16[8,1024]{1,0:T(8,128)(2,1)S(1)}, bf16[8,1024]{1,0:T(8,128)(2,1)S(1)}, u32[]{:S(2)}, u32[]{:S(2)}) collective-permute-start(bf16[8,1024]{1,0:T(8,128)(2,1)S(1)} %get-tuple-element.61), channel_id=1, source_target_pairs={{0,12},{2,14},{4,8},{6,10},{8,4},{10,6},{12,0},{14,2},{1,13},{3,15... | collective-permute-start | bytes 49160 | tf_op jit(solution)/shard_map/ppermute | solution.py:381
  111.7 1.2 collective-permute-start.37
  112.9 0.0 collective-permute-done.35.refs_5_
  112.9 1.0 collective-permute-done.36.refs_6_
  113.9 4.3 %collective-permute-done.37.refs_7_ = bf16[8,1024]{1,0:T(8,128)(2,1)S(1)} collective-permute-done((bf16[8,1024]{1,0:T(8,128)(2,1)S(1)}, bf16[8,1024]{1,0:T(8,128)(2,1)S(1)}, u32[]{:S(2)}, u32[]{:S(2)}) %collective-permute-start.37) | collective-permute-done | bytes 16416 | tf_op jit(solution)/shard_map/ppermute | solution.py:381
  118.2 0.6 copy-done.15
  118.7 1.5 %residual.1 = bf16[8,1024]{1,0:T(8,128)(2,1)} custom-call(bf16[8,1024]{1,0:T(8,128)(2,1)} %x_ref.5, bf16[8,1024]{1,0:T(8,128)(2,1)} %copy-done.7, bf16[8,1024]{1,0:T(8,128)(2,1)} %copy-done.9, bf16[8,1024]{1,0:T(8,128)(2,1)} %copy-done.10, bf16[8,1024]{1,0:T(8,128)(2,1)} %copy-done.11, bf16[8,1024]{1,0:T(8,128)(2,1)} %copy-done.12, ...), custom_call_target="tpu_custom_call" | custom-call | tf_op jit(solution)/shard_map/residual/pallas_call | solution.py:370
  (58 shorter events, 0.1 us)
Async XLA Ops:
  0.0 1.4 %collective-permute-start.7 = (s32[8]{0:T(128)}, s32[8]{0:T(128)S(1)}, u32[]{:S(2)}, u32[]{:S(2)}) collective-permute-start(s32[8]{0:T(128)} %param.11), channel_id=1, source_target_pairs={{0,1},{1,0},{2,3},{3,2},{4,5},{5,4},{6,7},{7,6},{8,9},{9,8},{10,11... | collective-permute-start | bytes 104 | tf_op jit(solution)/shard_map/ppermute | solution.py:404
  0.5 1.7 %collective-permute-start.8 = (bf16[8,1024]{1,0:T(8,128)(2,1)}, bf16[8,1024]{1,0:T(8,128)(2,1)S(1)}, u32[]{:S(2)}, u32[]{:S(2)}) collective-permute-start(bf16[8,1024]{1,0:T(8,128)(2,1)} %x_ref.5), channel_id=1, source_target_pairs={{0,1},{1,0},{2,3},{3,2},{4,5},{5,4},{6,7},{7,6},{8,9},{9,8},{10,11... | collective-permute-start | bytes 49160 | tf_op jit(solution)/shard_map/ppermute | solution.py:403
  2.1 1.6 %copy-start.3 = (bf16[16,1024,64]{1,2,0:T(8,128)(2,1)S(1)}, bf16[16,1024,64]{1,2,0:T(8,128)(2,1)}, u32[]{:S(2)}) copy-start(bf16[16,1024,64]{1,2,0:T(8,128)(2,1)} %param.16) | copy-start | bytes 6291460
  3.7 0.7 copy-start.5
  5.6 23.4 %collective-permute-start.10 = (f32[16,128]{1,0:T(8,128)S(1)}, f32[16,128]{1,0:T(8,128)S(1)}, u32[]{:S(2)}, u32[]{:S(2)}) collective-permute-start(f32[16,128]{1,0:T(8,128)S(1)} %down.1.refs_0_), channel_id=1, source_target_pairs={{0,4},{2,6},{4,0},{6,2},{8,12},{10,14},{12,8},{14,10},{1,5},{3,7},... | collective-permute-start | bytes 24584 | tf_op jit(solution)/shard_map/ppermute | solution.py:381
  8.5 22.2 %collective-permute-start.11 = (f32[16,128]{1,0:T(8,128)S(1)}, f32[16,128]{1,0:T(8,128)S(1)}, u32[]{:S(2)}, u32[]{:S(2)}) collective-permute-start(f32[16,128]{1,0:T(8,128)S(1)} %down.1.refs_0_), channel_id=1, source_target_pairs={{0,6},{2,4},{4,2},{6,0},{8,14},{10,12},{12,10},{14,8},{1,7},{3,5},... | collective-permute-start | bytes 24584 | tf_op jit(solution)/shard_map/ppermute | solution.py:381
  9.9 20.8 %collective-permute-start.12 = (f32[16,128]{1,0:T(8,128)S(1)}, f32[16,128]{1,0:T(8,128)S(1)}, u32[]{:S(2)}, u32[]{:S(2)}) collective-permute-start(f32[16,128]{1,0:T(8,128)S(1)} %down.1.refs_0_), channel_id=1, source_target_pairs={{0,8},{2,10},{4,12},{6,14},{8,0},{10,2},{12,4},{14,6},{1,9},{3,11}... | collective-permute-start | bytes 24584 | tf_op jit(solution)/shard_map/ppermute | solution.py:381
  12.5 20.1 %collective-permute-start.13 = (f32[16,128]{1,0:T(8,128)S(1)}, f32[16,128]{1,0:T(8,128)S(1)}, u32[]{:S(2)}, u32[]{:S(2)}) collective-permute-start(f32[16,128]{1,0:T(8,128)S(1)} %down.1.refs_0_), channel_id=1, source_target_pairs={{0,10},{2,8},{4,14},{6,12},{8,2},{10,0},{12,6},{14,4},{1,11},{3,9}... | collective-permute-start | bytes 24584 | tf_op jit(solution)/shard_map/ppermute | solution.py:381
  12.5 21.3 %collective-permute-start.14 = (f32[16,128]{1,0:T(8,128)S(1)}, f32[16,128]{1,0:T(8,128)S(1)}, u32[]{:S(2)}, u32[]{:S(2)}) collective-permute-start(f32[16,128]{1,0:T(8,128)S(1)} %down.1.refs_0_), channel_id=1, source_target_pairs={{0,12},{2,14},{4,8},{6,10},{8,4},{10,6},{12,0},{14,2},{1,13},{3,15... | collective-permute-start | bytes 24584 | tf_op jit(solution)/shard_map/ppermute | solution.py:381
  16.4 2.2 %copy-start = (bf16[1024,2048]{1,0:T(8,128)(2,1)S(1)}, bf16[1024,2048]{1,0:T(8,128)(2,1)}, u32[]{:S(2)}) copy-start(bf16[1024,2048]{1,0:T(8,128)(2,1)} %wv_ref.1) | copy-start | bytes 12582916
  18.6 0.7 copy-start.6
  19.3 9.8 %copy-start.8 = (s32[8]{0:T(128)S(1)}, s32[8]{0:T(128)}, u32[]{:S(2)}) copy-start(s32[8]{0:T(128)} %length.1) | copy-start | bytes 100
  19.3 23.6 %copy-start.4 = (bf16[16,64,1024]{2,1,0:T(8,128)(2,1)S(1)}, bf16[16,64,1024]{2,1,0:T(8,128)(2,1)}, u32[]{:S(2)}) copy-start(bf16[16,64,1024]{2,1,0:T(8,128)(2,1)} %refs_8_.2) | copy-start | bytes 6291460
  29.1 14.7 %collective-permute-start = (f32[8,1280]{1,0:T(8,128)S(1)}, f32[8,1280]{1,0:T(8,128)S(1)}, u32[]{:S(2)}, u32[]{:S(2)}) collective-permute-start(f32[8,1280]{1,0:T(8,128)S(1)} %get-tuple-element.35), channel_id=1, source_target_pairs={{0,2},{2,0},{4,6},{6,4},{8,10},{10,8},{12,14},{14,12},{1,3},{3,1},... | collective-permute-start | bytes 122888 | tf_op jit(solution)/shard_map/ppermute | solution.py:381
  30.7 13.4 %collective-permute-start.1 = (f32[8,1280]{1,0:T(8,128)S(1)}, f32[8,1280]{1,0:T(8,128)S(1)}, u32[]{:S(2)}, u32[]{:S(2)}) collective-permute-start(f32[8,1280]{1,0:T(8,128)S(1)} %get-tuple-element.36), channel_id=1, source_target_pairs={{0,4},{2,6},{4,0},{6,2},{8,12},{10,14},{12,8},{14,10},{1,5},{3,7},... | collective-permute-start | bytes 122888 | tf_op jit(solution)/shard_map/ppermute | solution.py:381
  30.7 16.9 %collective-permute-start.2 = (f32[8,1280]{1,0:T(8,128)S(1)}, f32[8,1280]{1,0:T(8,128)S(1)}, u32[]{:S(2)}, u32[]{:S(2)}) collective-permute-start(f32[8,1280]{1,0:T(8,128)S(1)} %get-tuple-element.37), channel_id=1, source_target_pairs={{0,6},{2,4},{4,2},{6,0},{8,14},{10,12},{12,10},{14,8},{1,7},{3,5},... | collective-permute-start | bytes 122888 | tf_op jit(solution)/shard_map/ppermute | solution.py:381
  32.7 6.3 %collective-permute-start.15 = (f32[16,128]{1,0:T(8,128)S(1)}, f32[16,128]{1,0:T(8,128)S(1)}, u32[]{:S(2)}, u32[]{:S(2)}) collective-permute-start(f32[16,128]{1,0:T(8,128)S(1)} %down.1.refs_0_), channel_id=1, source_target_pairs={{0,14},{2,12},{4,10},{6,8},{8,6},{10,4},{12,2},{14,0},{1,15},{3,13... | collective-permute-start | bytes 24584 | tf_op jit(solution)/shard_map/ppermute | solution.py:381
  33.9 5.2 %collective-permute-start.9 = (f32[16,128]{1,0:T(8,128)S(1)}, f32[16,128]{1,0:T(8,128)S(1)}, u32[]{:S(2)}, u32[]{:S(2)}) collective-permute-start(f32[16,128]{1,0:T(8,128)S(1)} %down.1.refs_0_), channel_id=1, source_target_pairs={{0,2},{2,0},{4,6},{6,4},{8,10},{10,8},{12,14},{14,12},{1,3},{3,1},... | collective-permute-start | bytes 24584 | tf_op jit(solution)/shard_map/ppermute | solution.py:381
  39.0 8.8 %collective-permute-start.3 = (f32[8,1280]{1,0:T(8,128)S(1)}, f32[8,1280]{1,0:T(8,128)S(1)}, u32[]{:S(2)}, u32[]{:S(2)}) collective-permute-start(f32[8,1280]{1,0:T(8,128)S(1)} %get-tuple-element.38), channel_id=1, source_target_pairs={{0,8},{2,10},{4,12},{6,14},{8,0},{10,2},{12,4},{14,6},{1,9},{3,11}... | collective-permute-start | bytes 122888 | tf_op jit(solution)/shard_map/ppermute | solution.py:381
  39.0 8.8 %collective-permute-start.4 = (f32[8,1280]{1,0:T(8,128)S(1)}, f32[8,1280]{1,0:T(8,128)S(1)}, u32[]{:S(2)}, u32[]{:S(2)}) collective-permute-start(f32[8,1280]{1,0:T(8,128)S(1)} %get-tuple-element.39), channel_id=1, source_target_pairs={{0,10},{2,8},{4,14},{6,12},{8,2},{10,0},{12,6},{14,4},{1,11},{3,9}... | collective-permute-start | bytes 122888 | tf_op jit(solution)/shard_map/ppermute | solution.py:381
  43.8 5.8 %collective-permute-start.5 = (f32[8,1280]{1,0:T(8,128)S(1)}, f32[8,1280]{1,0:T(8,128)S(1)}, u32[]{:S(2)}, u32[]{:S(2)}) collective-permute-start(f32[8,1280]{1,0:T(8,128)S(1)} %get-tuple-element.40), channel_id=1, source_target_pairs={{0,12},{2,14},{4,8},{6,10},{8,4},{10,6},{12,0},{14,2},{1,13},{3,15... | collective-permute-start | bytes 122888 | tf_op jit(solution)/shard_map/ppermute | solution.py:381
  44.1 6.7 %collective-permute-start.6 = (f32[8,1280]{1,0:T(8,128)S(1)}, f32[8,1280]{1,0:T(8,128)S(1)}, u32[]{:S(2)}, u32[]{:S(2)}) collective-permute-start(f32[8,1280]{1,0:T(8,128)S(1)} %get-tuple-element.41), channel_id=1, source_target_pairs={{0,14},{2,12},{4,10},{6,8},{8,6},{10,4},{12,2},{14,0},{1,15},{3,13... | collective-permute-start | bytes 122888 | tf_op jit(solution)/shard_map/ppermute | solution.py:381
  47.6 3.2 %collective-permute-start.16 = (f32[8,1024]{1,0:T(8,128)S(1)}, f32[8,1024]{1,0:T(8,128)S(1)}, u32[]{:S(2)}, u32[]{:S(2)}) collective-permute-start(f32[8,1024]{1,0:T(8,128)S(1)} %get-tuple-element.43), channel_id=1, source_target_pairs={{0,1},{1,0},{2,3},{3,2},{4,5},{5,4},{6,7},{7,6},{8,9},{9,8},{10,11... | collective-permute-start | bytes 98312 | tf_op jit(solution)/shard_map/ppermute | solution.py:415
  50.9 6.7 %collective-permute-start.17 = (bf16[64,128]{1,0:T(8,128)(2,1)S(1)}, bf16[64,128]{1,0:T(8,128)(2,1)S(1)}, u32[]{:S(2)}, u32[]{:S(2)}) collective-permute-start(bf16[64,128]{1,0:T(8,128)(2,1)S(1)} %get-tuple-element.44.refs_0_.refs_8_), channel_id=1, source_target_pairs={{0,2},{2,0},{4,6},{6,4},{8,10},{10,8},{12,14},{14,12},{1,3},{3,1},... | collective-permute-start | bytes 49160 | tf_op jit(solution)/shard_map/ppermute | solution.py:381
  51.7 9.2 %collective-permute-start.18 = (bf16[64,128]{1,0:T(8,128)(2,1)S(1)}, bf16[64,128]{1,0:T(8,128)(2,1)S(1)}, u32[]{:S(2)}, u32[]{:S(2)}) collective-permute-start(bf16[64,128]{1,0:T(8,128)(2,1)S(1)} %get-tuple-element.44.refs_0_.refs_8_), channel_id=1, source_target_pairs={{0,4},{2,6},{4,0},{6,2},{8,12},{10,14},{12,8},{14,10},{1,5},{3,7},... | collective-permute-start | bytes 49160 | tf_op jit(solution)/shard_map/ppermute | solution.py:381
  51.7 10.4 %collective-permute-start.19 = (bf16[64,128]{1,0:T(8,128)(2,1)S(1)}, bf16[64,128]{1,0:T(8,128)(2,1)S(1)}, u32[]{:S(2)}, u32[]{:S(2)}) collective-permute-start(bf16[64,128]{1,0:T(8,128)(2,1)S(1)} %get-tuple-element.44.refs_0_.refs_8_), channel_id=1, source_target_pairs={{0,6},{2,4},{4,2},{6,0},{8,14},{10,12},{12,10},{14,8},{1,7},{3,5},... | collective-permute-start | bytes 49160 | tf_op jit(solution)/shard_map/ppermute | solution.py:381
  54.4 7.7 %collective-permute-start.20 = (bf16[64,128]{1,0:T(8,128)(2,1)S(1)}, bf16[64,128]{1,0:T(8,128)(2,1)S(1)}, u32[]{:S(2)}, u32[]{:S(2)}) collective-permute-start(bf16[64,128]{1,0:T(8,128)(2,1)S(1)} %get-tuple-element.44.refs_0_.refs_8_), channel_id=1, source_target_pairs={{0,8},{2,10},{4,12},{6,14},{8,0},{10,2},{12,4},{14,6},{1,9},{3,11}... | collective-permute-start | bytes 49160 | tf_op jit(solution)/shard_map/ppermute | solution.py:381
  56.6 5.5 %collective-permute-start.21 = (bf16[64,128]{1,0:T(8,128)(2,1)S(1)}, bf16[64,128]{1,0:T(8,128)(2,1)S(1)}, u32[]{:S(2)}, u32[]{:S(2)}) collective-permute-start(bf16[64,128]{1,0:T(8,128)(2,1)S(1)} %get-tuple-element.44.refs_0_.refs_8_), channel_id=1, source_target_pairs={{0,10},{2,8},{4,14},{6,12},{8,2},{10,0},{12,6},{14,4},{1,11},{3,9}... | collective-permute-start | bytes 49160 | tf_op jit(solution)/shard_map/ppermute | solution.py:381
  57.6 5.5 %collective-permute-start.22 = (bf16[64,128]{1,0:T(8,128)(2,1)S(1)}, bf16[64,128]{1,0:T(8,128)(2,1)S(1)}, u32[]{:S(2)}, u32[]{:S(2)}) collective-permute-start(bf16[64,128]{1,0:T(8,128)(2,1)S(1)} %get-tuple-element.44.refs_0_.refs_8_), channel_id=1, source_target_pairs={{0,12},{2,14},{4,8},{6,10},{8,4},{10,6},{12,0},{14,2},{1,13},{3,15... | collective-permute-start | bytes 49160 | tf_op jit(solution)/shard_map/ppermute | solution.py:381
  60.9 6.4 %collective-permute-start.23 = (bf16[64,128]{1,0:T(8,128)(2,1)S(1)}, bf16[64,128]{1,0:T(8,128)(2,1)S(1)}, u32[]{:S(2)}, u32[]{:S(2)}) collective-permute-start(bf16[64,128]{1,0:T(8,128)(2,1)S(1)} %get-tuple-element.44.refs_0_.refs_8_), channel_id=1, source_target_pairs={{0,14},{2,12},{4,10},{6,8},{8,6},{10,4},{12,2},{14,0},{1,15},{3,13... | collective-permute-start | bytes 49160 | tf_op jit(solution)/shard_map/ppermute | solution.py:381
  67.4 2.2 %copy-start.1 = (bf16[8,256,1024]{2,1,0:T(8,128)(2,1)S(1)}, bf16[8,256,1024]{2,1,0:T(8,128)(2,1)}, u32[]{:S(2)}) copy-start(bf16[8,256,1024]{2,1,0:T(8,128)(2,1)} %refs_8_.3) | copy-start | bytes 12582916
  69.6 2.2 %copy-start.2 = (bf16[8,256,1024]{2,1,0:T(8,128)(2,1)S(1)}, bf16[8,256,1024]{2,1,0:T(8,128)(2,1)}, u32[]{:S(2)}) copy-start(bf16[8,256,1024]{2,1,0:T(8,128)(2,1)} %refs_9_.1) | copy-start | bytes 12582916
  77.6 7.4 %collective-permute-start.24 = (bf16[96,128]{1,0:T(8,128)(2,1)S(1)}, bf16[96,128]{1,0:T(8,128)(2,1)S(1)}, u32[]{:S(2)}, u32[]{:S(2)}) collective-permute-start(bf16[96,128]{1,0:T(8,128)(2,1)S(1)} %get-tuple-element.46), channel_id=1, source_target_pairs={{0,2},{2,0},{4,6},{6,4},{8,10},{10,8},{12,14},{14,12},{1,3},{3,1},... | collective-permute-start | bytes 73736 | tf_op jit(solution)/shard_map/ppermute | solution.py:381
  79.2 6.1 %collective-permute-start.25 = (bf16[96,128]{1,0:T(8,128)(2,1)S(1)}, bf16[96,128]{1,0:T(8,128)(2,1)S(1)}, u32[]{:S(2)}, u32[]{:S(2)}) collective-permute-start(bf16[96,128]{1,0:T(8,128)(2,1)S(1)} %get-tuple-element.47), channel_id=1, source_target_pairs={{0,4},{2,6},{4,0},{6,2},{8,12},{10,14},{12,8},{14,10},{1,5},{3,7},... | collective-permute-start | bytes 73736 | tf_op jit(solution)/shard_map/ppermute | solution.py:381
  79.2 9.6 %collective-permute-start.26 = (bf16[96,128]{1,0:T(8,128)(2,1)S(1)}, bf16[96,128]{1,0:T(8,128)(2,1)S(1)}, u32[]{:S(2)}, u32[]{:S(2)}) collective-permute-start(bf16[96,128]{1,0:T(8,128)(2,1)S(1)} %get-tuple-element.48), channel_id=1, source_target_pairs={{0,6},{2,4},{4,2},{6,0},{8,14},{10,12},{12,10},{14,8},{1,7},{3,5},... | collective-permute-start | bytes 73736 | tf_op jit(solution)/shard_map/ppermute | solution.py:381
  81.2 7.7 %collective-permute-start.27 = (bf16[96,128]{1,0:T(8,128)(2,1)S(1)}, bf16[96,128]{1,0:T(8,128)(2,1)S(1)}, u32[]{:S(2)}, u32[]{:S(2)}) collective-permute-start(bf16[96,128]{1,0:T(8,128)(2,1)S(1)} %get-tuple-element.49), channel_id=1, source_target_pairs={{0,8},{2,10},{4,12},{6,14},{8,0},{10,2},{12,4},{14,6},{1,9},{3,11}... | collective-permute-start | bytes 73736 | tf_op jit(solution)/shard_map/ppermute | solution.py:381
  81.2 7.7 %collective-permute-start.28 = (bf16[96,128]{1,0:T(8,128)(2,1)S(1)}, bf16[96,128]{1,0:T(8,128)(2,1)S(1)}, u32[]{:S(2)}, u32[]{:S(2)}) collective-permute-start(bf16[96,128]{1,0:T(8,128)(2,1)S(1)} %get-tuple-element.50), channel_id=1, source_target_pairs={{0,10},{2,8},{4,14},{6,12},{8,2},{10,0},{12,6},{14,4},{1,11},{3,9}... | collective-permute-start | bytes 73736 | tf_op jit(solution)/shard_map/ppermute | solution.py:381
  85.1 5.6 %collective-permute-start.29 = (bf16[96,128]{1,0:T(8,128)(2,1)S(1)}, bf16[96,128]{1,0:T(8,128)(2,1)S(1)}, u32[]{:S(2)}, u32[]{:S(2)}) collective-permute-start(bf16[96,128]{1,0:T(8,128)(2,1)S(1)} %get-tuple-element.51), channel_id=1, source_target_pairs={{0,12},{2,14},{4,8},{6,10},{8,4},{10,6},{12,0},{14,2},{1,13},{3,15... | collective-permute-start | bytes 73736 | tf_op jit(solution)/shard_map/ppermute | solution.py:381
  85.3 6.5 %collective-permute-start.30 = (bf16[96,128]{1,0:T(8,128)(2,1)S(1)}, bf16[96,128]{1,0:T(8,128)(2,1)S(1)}, u32[]{:S(2)}, u32[]{:S(2)}) collective-permute-start(bf16[96,128]{1,0:T(8,128)(2,1)S(1)} %get-tuple-element.52), channel_id=1, source_target_pairs={{0,14},{2,12},{4,10},{6,8},{8,6},{10,4},{12,2},{14,0},{1,15},{3,13... | collective-permute-start | bytes 73736 | tf_op jit(solution)/shard_map/ppermute | solution.py:381
  101.1 0.6 copy-start.7
  101.7 6.6 %collective-permute-start.31 = (bf16[8,1024]{1,0:T(8,128)(2,1)S(1)}, bf16[8,1024]{1,0:T(8,128)(2,1)S(1)}, u32[]{:S(2)}, u32[]{:S(2)}) collective-permute-start(bf16[8,1024]{1,0:T(8,128)(2,1)S(1)} %get-tuple-element.56), channel_id=1, source_target_pairs={{0,2},{2,0},{4,6},{6,4},{8,10},{10,8},{12,14},{14,12},{1,3},{3,1},... | collective-permute-start | bytes 49160 | tf_op jit(solution)/shard_map/ppermute | solution.py:381
  102.5 9.2 %collective-permute-start.32 = (bf16[8,1024]{1,0:T(8,128)(2,1)S(1)}, bf16[8,1024]{1,0:T(8,128)(2,1)S(1)}, u32[]{:S(2)}, u32[]{:S(2)}) collective-permute-start(bf16[8,1024]{1,0:T(8,128)(2,1)S(1)} %get-tuple-element.57), channel_id=1, source_target_pairs={{0,4},{2,6},{4,0},{6,2},{8,12},{10,14},{12,8},{14,10},{1,5},{3,7},... | collective-permute-start | bytes 49160 | tf_op jit(solution)/shard_map/ppermute | solution.py:381
  102.5 10.4 %collective-permute-start.33 = (bf16[8,1024]{1,0:T(8,128)(2,1)S(1)}, bf16[8,1024]{1,0:T(8,128)(2,1)S(1)}, u32[]{:S(2)}, u32[]{:S(2)}) collective-permute-start(bf16[8,1024]{1,0:T(8,128)(2,1)S(1)} %get-tuple-element.58), channel_id=1, source_target_pairs={{0,6},{2,4},{4,2},{6,0},{8,14},{10,12},{12,10},{14,8},{1,7},{3,5},... | collective-permute-start | bytes 49160 | tf_op jit(solution)/shard_map/ppermute | solution.py:381
  105.2 7.7 %collective-permute-start.34 = (bf16[8,1024]{1,0:T(8,128)(2,1)S(1)}, bf16[8,1024]{1,0:T(8,128)(2,1)S(1)}, u32[]{:S(2)}, u32[]{:S(2)}) collective-permute-start(bf16[8,1024]{1,0:T(8,128)(2,1)S(1)} %get-tuple-element.59), channel_id=1, source_target_pairs={{0,8},{2,10},{4,12},{6,14},{8,0},{10,2},{12,4},{14,6},{1,9},{3,11}... | collective-permute-start | bytes 49160 | tf_op jit(solution)/shard_map/ppermute | solution.py:381
  107.3 5.5 %collective-permute-start.35 = (bf16[8,1024]{1,0:T(8,128)(2,1)S(1)}, bf16[8,1024]{1,0:T(8,128)(2,1)S(1)}, u32[]{:S(2)}, u32[]{:S(2)}) collective-permute-start(bf16[8,1024]{1,0:T(8,128)(2,1)S(1)} %get-tuple-element.60), channel_id=1, source_target_pairs={{0,10},{2,8},{4,14},{6,12},{8,2},{10,0},{12,6},{14,4},{1,11},{3,9}... | collective-permute-start | bytes 49160 | tf_op jit(solution)/shard_map/ppermute | solution.py:381
  108.3 9.8 %copy-start.9 = (bf16[8,1024]{1,0:T(8,128)(2,1)}, bf16[8,1024]{1,0:T(8,128)(2,1)S(1)}, u32[]{:S(2)}) copy-start(bf16[8,1024]{1,0:T(8,128)(2,1)S(1)} %collective-permute-done.31.refs_1_) | copy-start | bytes 49156
  108.3 5.5 %collective-permute-start.36 = (bf16[8,1024]{1,0:T(8,128)(2,1)S(1)}, bf16[8,1024]{1,0:T(8,128)(2,1)S(1)}, u32[]{:S(2)}, u32[]{:S(2)}) collective-permute-start(bf16[8,1024]{1,0:T(8,128)(2,1)S(1)} %get-tuple-element.61), channel_id=1, source_target_pairs={{0,12},{2,14},{4,8},{6,10},{8,4},{10,6},{12,0},{14,2},{1,13},{3,15... | collective-permute-start | bytes 49160 | tf_op jit(solution)/shard_map/ppermute | solution.py:381
  111.7 6.4 %copy-start.10 = (bf16[8,1024]{1,0:T(8,128)(2,1)}, bf16[8,1024]{1,0:T(8,128)(2,1)S(1)}, u32[]{:S(2)}) copy-start(bf16[8,1024]{1,0:T(8,128)(2,1)S(1)} %collective-permute-done.32.refs_2_) | copy-start | bytes 49156
  111.7 6.4 %collective-permute-start.37 = (bf16[8,1024]{1,0:T(8,128)(2,1)S(1)}, bf16[8,1024]{1,0:T(8,128)(2,1)S(1)}, u32[]{:S(2)}, u32[]{:S(2)}) collective-permute-start(bf16[8,1024]{1,0:T(8,128)(2,1)S(1)} %get-tuple-element.62), channel_id=1, source_target_pairs={{0,14},{2,12},{4,10},{6,8},{8,6},{10,4},{12,2},{14,0},{1,15},{3,13... | collective-permute-start | bytes 49160 | tf_op jit(solution)/shard_map/ppermute | solution.py:381
  112.9 5.3 %copy-start.11 = (bf16[8,1024]{1,0:T(8,128)(2,1)}, bf16[8,1024]{1,0:T(8,128)(2,1)S(1)}, u32[]{:S(2)}) copy-start(bf16[8,1024]{1,0:T(8,128)(2,1)S(1)} %collective-permute-done.33.refs_3_) | copy-start | bytes 49156
  112.9 5.3 %copy-start.12 = (bf16[8,1024]{1,0:T(8,128)(2,1)}, bf16[8,1024]{1,0:T(8,128)(2,1)S(1)}, u32[]{:S(2)}) copy-start(bf16[8,1024]{1,0:T(8,128)(2,1)S(1)} %collective-permute-done.34.refs_4_) | copy-start | bytes 49156
  112.9 5.3 %copy-start.13 = (bf16[8,1024]{1,0:T(8,128)(2,1)}, bf16[8,1024]{1,0:T(8,128)(2,1)S(1)}, u32[]{:S(2)}) copy-start(bf16[8,1024]{1,0:T(8,128)(2,1)S(1)} %collective-permute-done.35.refs_5_) | copy-start | bytes 49156
  113.9 4.3 %copy-start.14 = (bf16[8,1024]{1,0:T(8,128)(2,1)}, bf16[8,1024]{1,0:T(8,128)(2,1)S(1)}, u32[]{:S(2)}) copy-start(bf16[8,1024]{1,0:T(8,128)(2,1)S(1)} %collective-permute-done.36.refs_6_) | copy-start | bytes 49156
  118.1 0.6 copy-start.15

commit v2 on v1

--- a/solution.py
+++ b/solution.py
@@ -10,7 +10,7 @@
 HEAD_DIM = 128
 F32 = jnp.float32
 BF16 = jnp.bfloat16
-LINK = jnp.float32
+CHUNKS = 4
 VMEM_LIMIT = 40 * 1024 * 1024
 
 
@@ -28,40 +28,47 @@
     )
 
 
-def project_kernel(place, x_ref, wq_ref, wk_ref, wv_ref, *outs):
-    step = pl.program_id(0)
+def chunked(weight, width, index):
+    depth = weight.shape[0] // CHUNKS
+    return [
+        pl.BlockSpec((depth, width), lambda *a, c=c: (c, index(*a))) for c in range(CHUNKS)
+    ]
+
+
+def chunk_product(x, refs):
+    depth = refs[0].shape[0]
+    total = None
+    for c, ref in enumerate(refs):
+        part = jnp.dot(
+            x[:, c * depth : (c + 1) * depth], ref[...], preferred_element_type=F32
+        )
+        total = part if total is None else total + part
+    return total
+
+
+def project_kernel(x_ref, *refs):
+    *weights, out = refs
     x = x_ref[...]
-    width = wq_ref.shape[1]
-    q = jnp.dot(x, wq_ref[...], preferred_element_type=F32).astype(LINK)
-    k = jnp.dot(x, wk_ref[...], preferred_element_type=F32).astype(LINK)
-    v = jnp.dot(x, wv_ref[...], preferred_element_type=F32).astype(LINK)
-    for slot, out in enumerate(outs):
-
-        @pl.when(step == slot)
-        def _(out=out):
-            out[:, :width] = q
-            out[:, width : width + HEAD_DIM] = k
-            out[:, width + HEAD_DIM :] = v
-
-
-def project(place, x, wq, wkv, ranks):
+    width = weights[0].shape[1]
+    out[0, :, :width] = chunk_product(x, weights[:CHUNKS])
+    out[0, :, width : width + HEAD_DIM] = chunk_product(x, weights[CHUNKS : 2 * CHUNKS])
+    out[0, :, width + HEAD_DIM :] = chunk_product(x, weights[2 * CHUNKS :])
+
+
+def project(x, wq, wkv, ranks):
     rows, depth = x.shape
     width = wq.shape[1] // ranks
     kv_heads = wkv.shape[1] // 2 // HEAD_DIM
+    out = (ranks, rows, width + 2 * HEAD_DIM)
     return pl.pallas_call(
         project_kernel,
-        grid_spec=pltpu.PrefetchScalarGridSpec(
-            num_scalar_prefetch=1,
-            grid=(ranks,),
-            in_specs=[
-                pl.BlockSpec((rows, depth), lambda s, p: (0, 0)),
-                pl.BlockSpec((depth, width), lambda s, p: (0, s ^ p[0])),
-                pl.BlockSpec((depth, HEAD_DIM), lambda s, p: (0, s ^ p[0])),
-                pl.BlockSpec((depth, HEAD_DIM), lambda s, p: (0, kv_heads + (s ^ p[0]))),
-            ],
-            out_specs=[pl.BlockSpec((rows, width + 2 * HEAD_DIM), lambda s, p: (0, 0))] * ranks,
-        ),
-        out_shape=[jax.ShapeDtypeStruct((rows, width + 2 * HEAD_DIM), LINK)] * ranks,
+        grid=(ranks,),
+        in_specs=[pl.BlockSpec((rows, depth), lambda s: (0, 0))]
+        + chunked(wq, width, lambda s: s)
+        + chunked(wkv, HEAD_DIM, lambda s: s)
+        + chunked(wkv, HEAD_DIM, lambda s: kv_heads + s),
+        out_specs=pl.BlockSpec((1,) + out[1:], lambda s: (s, 0, 0)),
+        out_shape=jax.ShapeDtypeStruct(out, F32),
         compiler_params=params(),
         cost_estimate=pl.CostEstimate(
             flops=2 * rows * depth * (wq.shape[1] + wkv.shape[1]),
@@ -69,7 +76,7 @@
             transcendentals=0,
         ),
         name="project",
-    )(place, x, wq, wkv, wkv)
+    )(x, *[wq] * CHUNKS, *[wkv] * (2 * CHUNKS))
 
 
 def adapter_column(index_ref, rows):
@@ -96,17 +103,18 @@
     for j in range(count // per):
         part = every[:, j * HEAD_DIM : (j + 1) * HEAD_DIM]
         total += jnp.where(lane // rank + j * per == column, part, 0.0)
-    out_ref[...] = total
-
-
-def down(index, bank, x, other, factors):
+    for slot in range(out_ref.shape[0]):
+        out_ref[slot] = total
+
+
+def down(index, bank, x, other, factors, ranks):
     rows = 2 * x.shape[0]
     smem = pl.BlockSpec(memory_space=pltpu.SMEM)
     return pl.pallas_call(
         down_kernel,
         in_specs=[smem, smem, whole(), whole(), whole()],
         out_specs=whole(),
-        out_shape=jax.ShapeDtypeStruct((rows, HEAD_DIM), F32),
+        out_shape=jax.ShapeDtypeStruct((ranks, rows, HEAD_DIM), F32),
         compiler_params=pltpu.CompilerParams(vmem_limit_bytes=VMEM_LIMIT),
         cost_estimate=pl.CostEstimate(
             flops=2 * rows * factors.size, bytes_accessed=2 * factors.size, transcendentals=0
@@ -115,14 +123,10 @@
     )(index, bank, x, other, factors)
 
 
-def up_kernel(index_ref, bank_ref, *refs):
-    *parts, up_ref, own_ref, other_ref = refs
-    rows = parts[0].shape[0]
+def up_kernel(index_ref, bank_ref, parts_ref, up_ref, own_ref, other_ref):
+    rows = parts_ref.shape[1]
     count, rank, width = up_ref.shape
-    total = parts[0][...]
-    for part in parts[1:]:
-        total += part[...]
-    total = total.astype(BF16).astype(F32)
+    total = jnp.sum(parts_ref[...], axis=0).astype(BF16).astype(F32)
     column = adapter_column(index_ref, rows) - bank_ref[0] * count
     lane = iota((rows, HEAD_DIM), 1)
     per = HEAD_DIM // rank
@@ -141,12 +145,12 @@
 
 
 def up(index, bank, parts, factors):
-    rows = parts[0].shape[0]
+    rows = parts.shape[1]
     width = factors.shape[2]
     smem = pl.BlockSpec(memory_space=pltpu.SMEM)
     return pl.pallas_call(
         up_kernel,
-        in_specs=[smem, smem] + [whole()] * (len(parts) + 1),
+        in_specs=[smem, smem, whole(), whole()],
         out_specs=[whole()] * 2,
         out_shape=[jax.ShapeDtypeStruct((rows // 2, width), F32)] * 2,
         compiler_params=pltpu.CompilerParams(vmem_limit_bytes=VMEM_LIMIT),
@@ -154,24 +158,25 @@
             flops=2 * rows * factors.size, bytes_accessed=2 * factors.size, transcendentals=0
         ),
         name="up",
-    )(index, bank, *parts, factors)
+    )(index, bank, parts, factors)
 
 
 def rotate(v, cosine, sine):
     return v * cosine + pltpu.roll(v, HEAD_DIM // 2, 1) * sine
 
 
-def rotate_kernel(*refs):
-    *parts, own_ref, other_ref, cos_ref, sin_ref, q_ref, k_ref, v_ref, rows_ref = refs
-    total = parts[0][...].astype(F32)
-    for part in parts[1:]:
-        total += part[...].astype(F32)
+def rotate_kernel(
+    parts_ref, own_ref, other_ref, cos_ref, sin_ref, q_ref, k_ref, v_ref, rows_ref
+):
+    total = jnp.sum(parts_ref[...], axis=0)
     width = own_ref.shape[1]
     query = total[:, :width] + (own_ref[...] + other_ref[...])
     cosine, sine = cos_ref[...], sin_ref[...]
     for g in range(width // HEAD_DIM):
         rows_ref[:, g, :] = rotate(query[:, g * HEAD_DIM : (g + 1) * HEAD_DIM], cosine, sine)
-    q_ref[...] = rows_ref[...].reshape(q_ref.shape).astype(BF16)
+    rows = rows_ref[...].reshape(q_ref.shape[1:]).astype(BF16)
+    for slot in range(q_ref.shape[0]):
+        q_ref[slot] = rows
     k_ref[...] = (
         rotate(total[:, width : width + HEAD_DIM], cosine, sine).astype(BF16).astype(F32)
     )
@@ -184,51 +189,50 @@
     small = jax.ShapeDtypeStruct((rows, HEAD_DIM), F32)
     return pl.pallas_call(
         rotate_kernel,
-        in_specs=[whole()] * (len(parts) + 4),
+        in_specs=[whole()] * 5,
         out_specs=[whole()] * 3,
-        out_shape=[jax.ShapeDtypeStruct((rows * heads, HEAD_DIM), BF16), small, small],
+        out_shape=[
+            jax.ShapeDtypeStruct((parts.shape[0], rows * heads, HEAD_DIM), BF16),
+            small,
+            small,
+        ],
         scratch_shapes=[pltpu.VMEM((rows, heads, HEAD_DIM), F32)],
         compiler_params=pltpu.CompilerParams(vmem_limit_bytes=VMEM_LIMIT),
         name="rotate",
-    )(*parts, own, other, cosine, sine)
-
-
-def attend_kernel(ranks, place, length, *refs):
-    queries = refs[:ranks]
-    k_ref, v_ref = refs[ranks : ranks + 2]
-    outs = refs[ranks + 2 : 2 * ranks + 2]
-    q_rows, o_rows, stats = refs[2 * ranks + 2 :]
+    )(parts, own, other, cosine, sine)
+
+
+def attend_kernel(place, length, q_ref, k_ref, v_ref, out_ref, q_rows, o_rows, stats):
     beam = pl.program_id(0)
     beams = pl.num_programs(0)
-    rank = place[0]
+    ranks = q_ref.shape[0]
     group = q_rows.shape[1] // stats.shape[0]
     heads = ranks * group
     positions = k_ref.shape[1]
 
     @pl.when(beam == 0)
     def _():
-        for s, query in enumerate(queries):
-            q_rows[s] = query[...].astype(F32)
+        q_rows[...] = q_ref[...].astype(F32)
 
     first = pl.multiple_of(beam * group, group)
     q = q_rows[:, pl.ds(first, group), :].reshape(heads, HEAD_DIM)
-    key_head = (iota((heads, HEAD_DIM), 0) // group) ^ rank
+    key_head = iota((heads, HEAD_DIM), 0) // group
     wide = jnp.concatenate(
         [jnp.where(key_head == c, q, 0.0) for c in range(ranks)], axis=1
     ).astype(BF16)
     scores = lax.dot_general(
         wide, k_ref[0], (((1,), (1,)), ((), ())), preferred_element_type=F32
     ) * (1.0 / HEAD_DIM**0.5)
-    live = rank * positions + iota((heads, positions), 1) < length[beam]
+    live = place[0] * positions + iota((heads, positions), 1) < length[beam]
     scores = jnp.where(live, scores, -1e30)
     peak = jnp.max(scores, axis=1, keepdims=True)
     weights = jnp.where(live, jnp.exp(scores - peak), 0.0)
     total = jnp.sum(weights, axis=1, keepdims=True)
     product = jnp.dot(weights.astype(BF16), v_ref[0], preferred_element_type=F32)
-    own = jnp.zeros((heads, HEAD_DIM), F32)
     for c in range(ranks):
-        own = jnp.where(key_head == c, product[:, c * HEAD_DIM : (c + 1) * HEAD_DIM], own)
-    o_rows[:, pl.ds(first, group), :] = own.reshape(ranks, group, HEAD_DIM)
+        o_rows[c, pl.ds(first, group), :] = product[
+            c * group : (c + 1) * group, c * HEAD_DIM : (c + 1) * HEAD_DIM
+        ]
     row, lane = iota((heads, HEAD_DIM), 0), iota((heads, HEAD_DIM), 1)
     spread = jnp.where(row == lane, peak, 0.0) + jnp.where(row + heads == lane, total, 0.0)
     stats[pl.ds(beam, 1), :] = jnp.sum(spread, axis=0, keepdims=True)
@@ -240,30 +244,29 @@
         middle = rest.astype(BF16).astype(F32)
         low = rest - middle
         tail = jnp.concatenate([high, middle, low, jnp.zeros_like(low)], axis=0)
-        for s, out in enumerate(outs):
-            out[...] = jnp.concatenate([o_rows[s], tail], axis=0).astype(BF16)
+        for c in range(ranks):
+            out_ref[c] = jnp.concatenate([o_rows[c], tail], axis=0).astype(BF16)
 
 
 def attend(place, length, queries, keys, values):
-    ranks = len(queries)
+    ranks, rows, _ = queries.shape
     beams, positions, width = keys.shape
-    rows = queries[0].shape[0]
-    out_rows = rows + 4 * beams
-    return pl.pallas_call(
-        functools.partial(attend_kernel, ranks),
+    out = (ranks, rows + 4 * beams, HEAD_DIM)
+    return pl.pallas_call(
+        attend_kernel,
         grid_spec=pltpu.PrefetchScalarGridSpec(
             num_scalar_prefetch=2,
             grid=(beams,),
-            in_specs=[pl.BlockSpec((rows, HEAD_DIM), lambda i, p, n: (0, 0))] * ranks
+            in_specs=[pl.BlockSpec(queries.shape, lambda i, p, n: (0, 0, 0))]
             + [pl.BlockSpec((1, positions, width), lambda i, p, n: (i, 0, 0))] * 2,
-            out_specs=[pl.BlockSpec((out_rows, HEAD_DIM), lambda i, p, n: (0, 0))] * ranks,
+            out_specs=pl.BlockSpec(out, lambda i, p, n: (0, 0, 0)),
             scratch_shapes=[
                 pltpu.VMEM((ranks, rows, HEAD_DIM), F32),
                 pltpu.VMEM((ranks, rows, HEAD_DIM), F32),
                 pltpu.VMEM((beams, HEAD_DIM), F32),
             ],
         ),
-        out_shape=[jax.ShapeDtypeStruct((out_rows, HEAD_DIM), BF16)] * ranks,
+        out_shape=jax.ShapeDtypeStruct(out, BF16),
         compiler_params=params(),
         cost_estimate=pl.CostEstimate(
             flops=4 * rows * ranks * positions * width,
@@ -271,41 +274,38 @@
             transcendentals=rows * ranks * positions,
         ),
         name="attend",
-    )(place, length, *queries, keys, values)
-
-
-def output_kernel(ranks, place, *refs):
-    parts = refs[:ranks]
-    q_ref, k_ref, v_ref, w_ref = refs[ranks : ranks + 4]
-    outs = refs[ranks + 4 : 2 * ranks + 4]
-    joined, attended = refs[2 * ranks + 4 :]
-    step = pl.program_id(0)
+    )(place, length, queries, keys, values)
+
+
+def output_kernel(place, parts_ref, q_ref, k_ref, v_ref, *refs):
+    *weights, out, joined, attended = refs
+    ranks = parts_ref.shape[0]
     beams, group, _ = joined.shape
     rows = beams * group
 
     def by_row(v):
         return jnp.broadcast_to(v[:, None, :], (beams, group, HEAD_DIM)).reshape(rows, HEAD_DIM)
 
-    @pl.when(step == 0)
+    @pl.when(pl.program_id(0) == 0)
     def _():
-        row, lane = iota((rows, HEAD_DIM), 0), iota((rows, HEAD_DIM), 1)
-        heads = ranks * group
+        head = place[0] * group + iota((rows, HEAD_DIM), 0) % group
+        lane = iota((rows, HEAD_DIM), 1)
         score = jnp.sum(
-            q_ref[...].astype(F32) * by_row(k_ref[...]), axis=1, keepdims=True
+            q_ref[0].astype(F32) * by_row(k_ref[...]), axis=1, keepdims=True
         ) * (1.0 / HEAD_DIM**0.5)
         peaks, totals, weighted = [], [], []
         top = score
-        for s, part in enumerate(parts):
-            block = part[...].astype(F32)
-            tail = (
+        for s in range(ranks):
+            block = parts_ref[s].astype(F32)
+            tail = by_row(
                 block[rows : rows + beams]
                 + block[rows + beams : rows + 2 * beams]
                 + block[rows + 2 * beams : rows + 3 * beams]
             )
-            tail = by_row(tail)
-            head = s * group + row % group
             peak = jnp.sum(jnp.where(lane == head, tail, 0.0), axis=1, keepdims=True)
-            total = jnp.sum(jnp.where(lane == heads + head, tail, 0.0), axis=1, keepdims=True)
+            total = jnp.sum(
+                jnp.where(lane == ranks * group + head, tail, 0.0), axis=1, keepdims=True
+            )
             top = jnp.maximum(top, peak)
             peaks.append(peak)
             totals.append(total)
@@ -321,66 +321,59 @@
         for g in range(group):
             attended[:, g * HEAD_DIM : (g + 1) * HEAD_DIM] = joined[:, g, :].astype(BF16)
 
-    mixed = jnp.dot(attended[...], w_ref[...], preferred_element_type=F32).astype(BF16)
-    for slot, out in enumerate(outs):
-
-        @pl.when(step == slot)
-        def _(out=out):
-            out[...] = mixed
+    out[0] = chunk_product(attended[...], weights).astype(BF16)
 
 
 def output(place, parts, query, key_new, value_new, weight):
-    ranks = len(parts)
+    ranks = parts.shape[0]
     beams = key_new.shape[0]
     depth = weight.shape[0]
     width = weight.shape[1] // ranks
     group = depth // HEAD_DIM
-    once = lambda a: pl.BlockSpec(a.shape, lambda s, p: (0, 0))
-    return pl.pallas_call(
-        functools.partial(output_kernel, ranks),
+    return pl.pallas_call(
+        output_kernel,
         grid_spec=pltpu.PrefetchScalarGridSpec(
             num_scalar_prefetch=1,
             grid=(ranks,),
-            in_specs=[once(a) for a in (*parts, query, key_new, value_new)]
-            + [pl.BlockSpec((depth, width), lambda s, p: (0, s ^ p[0]))],
-            out_specs=[pl.BlockSpec((beams, width), lambda s, p: (0, 0))] * ranks,
+            in_specs=[
+                pl.BlockSpec(parts.shape, lambda s, p: (0, 0, 0)),
+                pl.BlockSpec((1,) + query.shape[1:], lambda s, p: (0, 0, 0)),
+                pl.BlockSpec(key_new.shape, lambda s, p: (0, 0)),
+                pl.BlockSpec(value_new.shape, lambda s, p: (0, 0)),
+            ]
+            + chunked(weight, width, lambda s, p: s),
+            out_specs=pl.BlockSpec((1, beams, width), lambda s, p: (s, 0, 0)),
             scratch_shapes=[
                 pltpu.VMEM((beams, group, HEAD_DIM), F32),
                 pltpu.VMEM((beams, depth), BF16),
             ],
         ),
-        out_shape=[jax.ShapeDtypeStruct((beams, width), BF16)] * ranks,
+        out_shape=jax.ShapeDtypeStruct((ranks, beams, width), BF16),
         compiler_params=params(),
         cost_estimate=pl.CostEstimate(
             flops=2 * beams * weight.size, bytes_accessed=2 * weight.size, transcendentals=0
         ),
         name="output",
-    )(place, *parts, query, key_new, value_new, weight)
-
-
-def residual_kernel(x_ref, *refs):
-    *parts, out_ref = refs
-    total = parts[0][...].astype(F32)
-    for part in parts[1:]:
-        total += part[...].astype(F32)
+    )(place, parts, query, key_new, value_new, *[weight] * CHUNKS)
+
+
+def residual_kernel(x_ref, parts_ref, out_ref):
+    total = jnp.sum(parts_ref[...].astype(F32), axis=0)
     out_ref[...] = (x_ref[...].astype(F32) + total).astype(BF16)
 
 
 def residual(x, parts):
     return pl.pallas_call(
         residual_kernel,
-        in_specs=[whole()] * (len(parts) + 1),
+        in_specs=[whole()] * 2,
         out_specs=whole(),
         out_shape=jax.ShapeDtypeStruct(x.shape, BF16),
         name="residual",
-    )(x, *parts)
-
-
-def traded(blocks, ranks):
-    return [blocks[0]] + [
-        lax.ppermute(blocks[s], "tensor", [(i, i ^ s) for i in range(ranks)])
-        for s in range(1, ranks)
-    ]
+    )(x, parts)
+
+
+def traded(blocks):
+    return lax.all_to_all(blocks, "tensor", 0, 0, tiled=True)
 
 
 def matched_body(
@@ -409,20 +402,14 @@
     sine = jnp.sin(angles)
     sine = jnp.concatenate([-sine, sine], axis=1)
 
-    parts = traded(project(place, x, query_weight, keyvalue_weight, ranks), ranks)
-    inner = down(index, bank, x, x_other, lowrank_down_factors.swapaxes(1, 2))
-    delta_own, delta_sent = up(index, bank, traded([inner] * ranks, ranks), lowrank_up_factors)
+    parts = traded(project(x, query_weight, keyvalue_weight, ranks))
+    inner = down(index, bank, x, x_other, lowrank_down_factors.swapaxes(1, 2), ranks)
+    delta_own, delta_sent = up(index, bank, traded(inner), lowrank_up_factors)
     delta_other = lax.ppermute(delta_sent, "bank", swap)
     query, key_new, value_new = rotated(parts, delta_own, delta_other, cosine, sine)
-    partial = attend(
-        place,
-        beam_cache_length,
-        traded([query] * ranks, ranks),
-        paged_key_cache,
-        paged_value_cache,
-    )
-    mixed = output(place, traded(partial, ranks), query, key_new, value_new, output_weight)
-    return residual(x, traded(mixed, ranks))
+    partial = attend(place, beam_cache_length, traded(query), paged_key_cache, paged_value_cache)
+    mixed = output(place, traded(partial), query, key_new, value_new, output_weight)
+    return residual(x, traded(mixed))
 
 
 def joined(x, axis, combine):

time: 121 us -> 96.2 us (0.80)
  starting transfers between devices: 57.6 us -> 17.2 us
  blocking collectives: 0 us -> 20.6 us
  waiting for transfers between devices: 22 us -> 17.1 us
  local copies, waits for them, and re-layouts: 10.9 us -> 9.68 us
    ppermute x35 -> x0, starting transfers between devices: 57.1 us -> none  [traded(): lax.ppermute(blocks[s], 'tensor', [(i, i ^ s) for i in range(ranks)])]
    ppermute x35 -> x0, waiting for transfers between devices: 21.1 us -> none  [traded(): lax.ppermute(blocks[s], 'tensor', [(i, i ^ s) for i in range(ranks)])]
    all_to_all x0 -> x2, blocking collectives: none -> 20.6 us  [traded(): return lax.all_to_all(blocks, 'tensor', 0, 0, tiled=True)]
    all_to_all x0 -> x3, starting transfers between devices: none -> 16.7 us  [traded(): return lax.all_to_all(blocks, 'tensor', 0, 0, tiled=True)]
    all_to_all x0 -> x3, waiting for transfers between devices: none -> 15.2 us  [traded(): return lax.all_to_all(blocks, 'tensor', 0, 0, tiled=True)]
    unnamed x32 -> x16, local copies, waits for them, and re-layouts: 10.8 us -> 9.59 us
  transfers between devices with their start and end apart: 38 -> 6, of which waited for: 10 -> 4; matrix products, arithmetic and copies ran while one was open for 1% -> 1% of each run, Pallas kernels for 9% -> 11%
where the time goes in v2:
time: 96.2 us; the launch traced here: 95.3 us
  Pallas kernels  29.7 us (31%)
  blocking collectives  20.6 us (21%)
  starting transfers between devices  17.2 us (18%)
  waiting for transfers between devices  17.1 us (18%)
  local copies, waits for them, and re-layouts  9.68 us (10%)
    all_to_all x2, blocking collectives, traded(): return lax.all_to_all(blocks, 'tensor', 0, 0, tiled=True)  20.6 us
    all_to_all x3, starting transfers between devices, traded(): return lax.all_to_all(blocks, 'tensor', 0, 0, tiled=True)  16.7 us
    all_to_all x3, waiting for transfers between devices, traded(): return lax.all_to_all(blocks, 'tensor', 0, 0, tiled=True)  15.2 us
    pallas_call x1, Pallas kernels, project(): pl.pallas_call(project_kernel, grid=(ranks,), in_specs=[pl.BlockSpec((row...  9.84 us
    unnamed x16, local copies, waits for them, and re-layouts  9.59 us
    pallas_call x1, Pallas kernels, output(): pl.pallas_call(output_kernel, grid_spec=pltpu.PrefetchScalarGridSpec(num_...  8.95 us
    pallas_call x1, Pallas kernels, attend(): pl.pallas_call(attend_kernel, grid_spec=pltpu.PrefetchScalarGridSpec(num_...  5.86 us
  transfers between devices with their start and end apart: 6, of which 4 were waited for; matrix products, arithmetic and copies ran while one was open for 1% of the time, Pallas kernels for 11%

profile of v2, /device:TPU:0, one launch (start us, length us, event | category | flops | bytes accessed | tf_op | source)
XLA Modules:
  0.0 95.3 jit_solution(6429124768603378096)
XLA Ops:
  0.0 0.5 collective-permute-start
  0.5 0.1 collective-permute-start.1
  0.5 0.9 collective-permute-done
  1.4 0.7 pad_add_fusion.index_ref
  2.1 0.0 collective-permute-done.1.other_ref
  2.1 0.0 copy-start.3
  2.1 1.6 %copy-done.3 = bf16[16,1024,64]{1,2,0:T(8,128)(2,1)S(1)} copy-done((bf16[16,1024,64]{1,2,0:T(8,128)(2,1)S(1)}, bf16[16,1024,64]{1,2,0:T(8,128)(2,1)}, u32[]{:S(2)}) %copy-start.3) | copy-done | bytes 2097176
  3.7 0.0 copy-start.5
  3.7 0.7 copy-done.5
  4.5 1.8 %down.1 = f32[8,16,128]{2,1,0:T(8,128)} custom-call(s32[16]{0:T(128)S(1)} %pad_add_fusion.index_ref, s32[1]{0:T(128)} %bitcast.1.bank_ref, bf16[8,1024]{1,0:T(8,128)(2,1)S(1)} %copy-done.5, bf16[8,1024]{1,0:T(8,128)(2,1)S(1)} %collective-permute-done.1.other_ref, bf16[16,64,1024]{2,1,0:T(8,128)(2,1)S(1)} %bitcast.3), custom_call_target="tpu_custom_call" | custom-call | flops 33554432 | bytes 2097152 | tf_op jit(solution)/shard_map/down/pallas_call | solution.py:113
  6.3 7.1 %all-to-all-start.1 = ((f32[8,16,128]{2,1,0:T(8,128)}), f32[8,16,128]{2,1,0:T(8,128)S(1)}, u32[]{:S(2)}, u32[]{:S(2)}) async-start(f32[8,16,128]{2,1,0:T(8,128)} %down.1), calls=%async_computation.1 | async-start | bytes 131072 | tf_op jit(solution)/shard_map/all_to_all | solution.py:376
  13.4 0.0 copy-start
  13.4 2.2 %copy-done = bf16[1024,2048]{1,0:T(8,128)(2,1)S(1)} copy-done((bf16[1024,2048]{1,0:T(8,128)(2,1)S(1)}, bf16[1024,2048]{1,0:T(8,128)(2,1)}, u32[]{:S(2)}) %copy-start) | copy-done | bytes 4194328
  15.6 0.0 copy-start.6
  15.6 0.7 copy-done.6
  16.3 0.0 copy-start.7
  16.3 0.0 copy-start.4
  16.3 9.8 %project.1 = f32[8,8,1280]{2,1,0:T(8,128)} custom-call(bf16[8,1024]{1,0:T(8,128)(2,1)S(1)} %copy-done.6, bf16[1024,8192]{1,0:T(8,128)(2,1)} %refs_3_.2, bf16[1024,8192]{1,0:T(8,128)(2,1)} %refs_3_.2, bf16[1024,8192]{1,0:T(8,128)(2,1)} %refs_3_.2, bf16[1024,8192]{1,0:T(8,128)(2,1)} %refs_3_.2, bf16[1024,2048]{1,0:T(8,128)(2,1)S(1)} %copy-done, ...), custom_call_target="tpu_custom_call" | custom-call | flops 167772160 | bytes 20971520 | tf_op jit(solution)/shard_map/project/pallas_call | solution.py:63
  26.2 0.0 all-to-all-done.1.parts_ref
  26.2 6.0 %all-to-all-start = ((f32[8,8,1280]{2,1,0:T(8,128)}), f32[8,8,1280]{2,1,0:T(8,128)S(1)}, u32[]{:S(2)}, u32[]{:S(2)}) async-start(f32[8,8,1280]{2,1,0:T(8,128)} %project.1), calls=%async_computation | async-start | bytes 655360 | tf_op jit(solution)/shard_map/all_to_all | solution.py:376
  32.2 0.0 copy-done.7
  32.2 0.1 fusion
  32.3 0.0 copy-done.4
  32.3 0.9 up.1
  33.2 0.0 collective-permute-start.2
  33.2 0.1 pad_maximum_fusion.sin_ref
  33.3 0.1 tile.10.cos_ref
  33.4 1.0 %collective-permute-done.2.other_ref = f32[8,1024]{1,0:T(8,128)S(1)} collective-permute-done((f32[8,1024]{1,0:T(8,128)S(1)}, f32[8,1024]{1,0:T(8,128)S(1)}, u32[]{:S(2)}, u32[]{:S(2)}) %collective-permute-start.2) | collective-permute-done | bytes 32800 | tf_op jit(solution)/shard_map/ppermute | solution.py:408
  34.5 7.8 %all-to-all-done.parts_ref = f32[8,8,1280]{2,1,0:T(8,128)S(1)} async-done(((f32[8,8,1280]{2,1,0:T(8,128)}), f32[8,8,1280]{2,1,0:T(8,128)S(1)}, u32[]{:S(2)}, u32[]{:S(2)}) %all-to-all-start) | async-done | bytes 327712 | tf_op jit(solution)/shard_map/all_to_all | solution.py:376
  42.3 0.8 rotate.1
  43.1 3.6 %all-to-all-start.2 = ((bf16[8,64,128]{2,1,0:T(8,128)(2,1)}), bf16[8,64,128]{2,1,0:T(8,128)(2,1)S(1)}, u32[]{:S(2)}, u32[]{:S(2)}) async-start(bf16[8,64,128]{2,1,0:T(8,128)(2,1)} %get-tuple-element.12.q_ref), calls=%async_computation.2 | async-start | bytes 262144 | tf_op jit(solution)/shard_map/all_to_all | solution.py:376
  46.7 7.3 %all-to-all-done.2.q_ref = bf16[8,64,128]{2,1,0:T(8,128)(2,1)S(1)} async-done(((bf16[8,64,128]{2,1,0:T(8,128)(2,1)}), bf16[8,64,128]{2,1,0:T(8,128)(2,1)S(1)}, u32[]{:S(2)}, u32[]{:S(2)}) %all-to-all-start.2) | async-done | bytes 131104 | tf_op jit(solution)/shard_map/all_to_all | solution.py:376
  54.0 0.0 copy-start.1
  54.0 2.2 %copy-done.1 = bf16[8,256,1024]{2,1,0:T(8,128)(2,1)S(1)} copy-done((bf16[8,256,1024]{2,1,0:T(8,128)(2,1)S(1)}, bf16[8,256,1024]{2,1,0:T(8,128)(2,1)}, u32[]{:S(2)}) %copy-start.1) | copy-done | bytes 4194328
  56.2 0.0 copy-start.2
  56.2 2.2 %copy-done.2 = bf16[8,256,1024]{2,1,0:T(8,128)(2,1)S(1)} copy-done((bf16[8,256,1024]{2,1,0:T(8,128)(2,1)S(1)}, bf16[8,256,1024]{2,1,0:T(8,128)(2,1)}, u32[]{:S(2)}) %copy-start.2) | copy-done | bytes 4194328
  58.4 5.9 %attend.1 = bf16[8,96,128]{2,1,0:T(8,128)(2,1)S(1)} custom-call(s32[1]{0:T(128)} %bitcast.place, s32[8]{0:T(128)S(1)} %copy-done.7, bf16[8,64,128]{2,1,0:T(8,128)(2,1)S(1)} %all-to-all-done.2.q_ref, bf16[8,256,1024]{2,1,0:T(8,128)(2,1)S(1)} %copy-done.1, bf16[8,256,1024]{2,1,0:T(8,128)(2,1)S(1)} %copy-done.2), custom_call_target="tpu_custom_call" | custom-call | flops 536870912 | bytes 8388608 | tf_op jit(solution)/shard_map/attend/pallas_call | solution.py:255
  64.2 10.2 %all_to_all.25.parts_ref = bf16[8,96,128]{2,1,0:T(8,128)(2,1)S(1)} all-to-all(bf16[8,96,128]{2,1,0:T(8,128)(2,1)S(1)} %attend.1), channel_id=1, replica_groups=mesh['groups'=2,'tensor'=8,'bank'=2] {'tensor'}, dimensions={0} | all-to-all | bytes 393216 | tf_op jit(solution)/shard_map/all_to_all | solution.py:376
  74.4 9.0 %output.1 = bf16[8,8,1024]{2,1,0:T(8,128)(2,1)S(1)} custom-call(s32[1]{0:T(128)} %bitcast.place, bf16[8,96,128]{2,1,0:T(8,128)(2,1)S(1)} %all_to_all.25.parts_ref, bf16[8,64,128]{2,1,0:T(8,128)(2,1)} %get-tuple-element.12.q_ref, f32[8,128]{1,0:T(8,128)S(1)} %get-tuple-element.13.k_ref, f32[8,128]{1,0:T(8,128)S(1)} %get-tuple-element.14.v_ref, ...), custom_call_target="tpu_custom_call" | custom-call | flops 134217728 | bytes 16777216 | tf_op jit(solution)/shard_map/output/pallas_call | solution.py:333
  83.4 10.4 %all_to_all.26.parts_ref = bf16[8,8,1024]{2,1,0:T(8,128)(2,1)} all-to-all(bf16[8,8,1024]{2,1,0:T(8,128)(2,1)S(1)} %output.1), channel_id=1, replica_groups=mesh['groups'=2,'tensor'=8,'bank'=2] {'tensor'}, dimensions={0} | all-to-all | bytes 262144 | tf_op jit(solution)/shard_map/all_to_all | solution.py:376
  93.8 1.6 %residual.1 = bf16[8,1024]{1,0:T(8,128)(2,1)} custom-call(bf16[8,1024]{1,0:T(8,128)(2,1)} %x_ref.5, bf16[8,8,1024]{2,1,0:T(8,128)(2,1)} %all_to_all.26.parts_ref), custom_call_target="tpu_custom_call" | custom-call | tf_op jit(solution)/shard_map/residual/pallas_call | solution.py:366
  (3 shorter events, 0.0 us)
Async XLA Ops:
  0.0 1.4 %collective-permute-start = (s32[8]{0:T(128)}, s32[8]{0:T(128)S(1)}, u32[]{:S(2)}, u32[]{:S(2)}) collective-permute-start(s32[8]{0:T(128)} %param.11), channel_id=1, source_target_pairs={{0,1},{1,0},{2,3},{3,2},{4,5},{5,4},{6,7},{7,6},{8,9},{9,8},{10,11... | collective-permute-start | bytes 104 | tf_op jit(solution)/shard_map/ppermute | solution.py:397
  0.5 1.7 %collective-permute-start.1 = (bf16[8,1024]{1,0:T(8,128)(2,1)}, bf16[8,1024]{1,0:T(8,128)(2,1)S(1)}, u32[]{:S(2)}, u32[]{:S(2)}) collective-permute-start(bf16[8,1024]{1,0:T(8,128)(2,1)} %x_ref.5), channel_id=1, source_target_pairs={{0,1},{1,0},{2,3},{3,2},{4,5},{5,4},{6,7},{7,6},{8,9},{9,8},{10,11... | collective-permute-start | bytes 49160 | tf_op jit(solution)/shard_map/ppermute | solution.py:396
  2.1 1.6 %copy-start.3 = (bf16[16,1024,64]{1,2,0:T(8,128)(2,1)S(1)}, bf16[16,1024,64]{1,2,0:T(8,128)(2,1)}, u32[]{:S(2)}) copy-start(bf16[16,1024,64]{1,2,0:T(8,128)(2,1)} %param.16) | copy-start | bytes 6291460
  3.7 0.7 copy-start.5
  6.3 19.9 %all-to-all-start.1 = ((f32[8,16,128]{2,1,0:T(8,128)}), f32[8,16,128]{2,1,0:T(8,128)S(1)}, u32[]{:S(2)}, u32[]{:S(2)}) async-start(f32[8,16,128]{2,1,0:T(8,128)} %down.1), calls=%async_computation.1 | async-start | bytes 131072 | tf_op jit(solution)/shard_map/all_to_all | solution.py:376
  13.4 2.2 %copy-start = (bf16[1024,2048]{1,0:T(8,128)(2,1)S(1)}, bf16[1024,2048]{1,0:T(8,128)(2,1)}, u32[]{:S(2)}) copy-start(bf16[1024,2048]{1,0:T(8,128)(2,1)} %refs_11_.1) | copy-start | bytes 12582916
  15.6 0.7 copy-start.6
  16.3 15.9 %copy-start.7 = (s32[8]{0:T(128)S(1)}, s32[8]{0:T(128)}, u32[]{:S(2)}) copy-start(s32[8]{0:T(128)} %length.1) | copy-start | bytes 100
  16.3 16.0 %copy-start.4 = (bf16[16,64,1024]{2,1,0:T(8,128)(2,1)S(1)}, bf16[16,64,1024]{2,1,0:T(8,128)(2,1)}, u32[]{:S(2)}) copy-start(bf16[16,64,1024]{2,1,0:T(8,128)(2,1)} %up_ref.1) | copy-start | bytes 6291460
  26.2 16.1 %all-to-all-start = ((f32[8,8,1280]{2,1,0:T(8,128)}), f32[8,8,1280]{2,1,0:T(8,128)S(1)}, u32[]{:S(2)}, u32[]{:S(2)}) async-start(f32[8,8,1280]{2,1,0:T(8,128)} %project.1), calls=%async_computation | async-start | bytes 655360 | tf_op jit(solution)/shard_map/all_to_all | solution.py:376
  33.2 1.2 %collective-permute-start.2 = (f32[8,1024]{1,0:T(8,128)S(1)}, f32[8,1024]{1,0:T(8,128)S(1)}, u32[]{:S(2)}, u32[]{:S(2)}) collective-permute-start(f32[8,1024]{1,0:T(8,128)S(1)} %get-tuple-element.11), channel_id=1, source_target_pairs={{0,1},{1,0},{2,3},{3,2},{4,5},{5,4},{6,7},{7,6},{8,9},{9,8},{10,11... | collective-permute-start | bytes 98312 | tf_op jit(solution)/shard_map/ppermute | solution.py:408
  43.1 10.9 %all-to-all-start.2 = ((bf16[8,64,128]{2,1,0:T(8,128)(2,1)}), bf16[8,64,128]{2,1,0:T(8,128)(2,1)S(1)}, u32[]{:S(2)}, u32[]{:S(2)}) async-start(bf16[8,64,128]{2,1,0:T(8,128)(2,1)} %get-tuple-element.12.q_ref), calls=%async_computation.2 | async-start | bytes 262144 | tf_op jit(solution)/shard_map/all_to_all | solution.py:376
  54.0 2.2 %copy-start.1 = (bf16[8,256,1024]{2,1,0:T(8,128)(2,1)S(1)}, bf16[8,256,1024]{2,1,0:T(8,128)(2,1)}, u32[]{:S(2)}) copy-start(bf16[8,256,1024]{2,1,0:T(8,128)(2,1)} %k_ref.1) | copy-start | bytes 12582916
  56.2 2.2 %copy-start.2 = (bf16[8,256,1024]{2,1,0:T(8,128)(2,1)S(1)}, bf16[8,256,1024]{2,1,0:T(8,128)(2,1)}, u32[]{:S(2)}) copy-start(bf16[8,256,1024]{2,1,0:T(8,128)(2,1)} %v_ref.1) | copy-start | bytes 12582916

commit v3 on v0

--- a/solution.py
+++ b/solution.py
@@ -1,9 +1,562 @@
 import jax
 import jax.numpy as jnp
 from jax import lax
+from jax.experimental import pallas as pl
+from jax.experimental.pallas import tpu as pltpu
 from jax.sharding import PartitionSpec as P
 
 HEAD_DIM = 128
+F32 = jnp.float32
+BF16 = jnp.bfloat16
+CHUNKS = 4
+VMEM_LIMIT = 40 * 1024 * 1024
+
+
+def whole():
+    return pl.BlockSpec(memory_space=pltpu.VMEM)
+
+
+def scalar():
+    return pl.BlockSpec(memory_space=pltpu.SMEM)
+
+
+def in_hbm(array):
+    return pltpu.with_memory_space_constraint(array, pltpu.HBM)
+
+
+def shape(*dims, dtype=F32):
+    return jax.ShapeDtypeStruct(dims, dtype)
+
+
+def iota(dims, axis):
+    return lax.broadcasted_iota(jnp.int32, dims, axis)
+
+
+def params(**more):
+    return pltpu.CompilerParams(vmem_limit_bytes=VMEM_LIMIT, **more)
+
+
+def both_banks(own_ref, other_ref, rows_ref):
+    rows = jnp.concatenate([own_ref[...].astype(F32), other_ref[...].astype(F32)], axis=0)
+    rows_ref[...] = rows.astype(BF16)
+
+
+def chunked(weight, width, index):
+    depth = weight.shape[0] // CHUNKS
+    return [
+        pl.BlockSpec((depth, width), lambda *a, c=c: (c, index(*a))) for c in range(CHUNKS)
+    ]
+
+
+def chunk_product(x, refs):
+    depth = refs[0].shape[0]
+    total = None
+    for c, ref in enumerate(refs):
+        part = jnp.dot(
+            x[:, c * depth : (c + 1) * depth], ref[...], preferred_element_type=F32
+        )
+        total = part if total is None else total + part
+    return total
+
+
+def adapter_column(refs, bank, count):
+    rows = len(refs) * refs[0].shape[0]
+    row = iota((rows, HEAD_DIM), 0)
+    column = jnp.zeros((rows, HEAD_DIM), jnp.int32)
+    for r in range(rows):
+        ref = refs[r // refs[0].shape[0]]
+        column = jnp.where(row == r, ref[r % ref.shape[0]], column)
+    return column - bank * count
+
+
+def project_kernel(first, place, bank, *refs):
+    if first:
+        (own_index, other_index, x_ref, other_ref), refs = refs[:4], refs[4:]
+        *weights, kv_ref, down_ref, out, inner, rows = refs
+    else:
+        (x_ref, other_ref), refs = refs[:2], refs[2:]
+        *weights, kv_ref, inner, out, rows = refs
+    width = weights[0].shape[1]
+
+    @pl.when(pl.program_id(0) == 0)
+    def _():
+        both_banks(x_ref, other_ref, rows)
+        if first:
+            count, rank, depth = down_ref.shape
+            every = lax.dot_general(
+                rows[...],
+                down_ref[...].reshape(count * rank, depth),
+                (((1,), (1,)), ((), ())),
+                preferred_element_type=F32,
+            )
+            column = adapter_column((own_index, other_index), bank[0], count)
+            lane = iota(column.shape, 1)
+            per = HEAD_DIM // rank
+            total = jnp.zeros(column.shape, F32)
+            for j in range(count // per):
+                part = every[:, j * HEAD_DIM : (j + 1) * HEAD_DIM]
+                total += jnp.where(lane // rank + j * per == column, part, 0.0)
+            inner[...] = total
+
+    x = rows[...]
+    out[0, :, :width] = chunk_product(x, weights)
+    out[0, :, width : width + HEAD_DIM] = jnp.dot(x, kv_ref[...], preferred_element_type=F32)
+    out[0, :, width + HEAD_DIM :] = inner[...]
+
+
+def project(place, bank, x, other, wq, wkv, ranks, down=None, index=None, inner=None):
+    rows, depth = x.shape
+    first = inner is None
+    width = wq.shape[1] // ranks // 2
+    out = (ranks // 2, 2 * rows, width + 2 * HEAD_DIM)
+    rank_of = lambda s, p: (2 * s + (1 if first else 0)) ^ p[0]
+    same = lambda a: pl.BlockSpec(a.shape, lambda s, p, b: (0,) * a.ndim)
+    out_specs = [pl.BlockSpec((1,) + out[1:], lambda s, p, b: (s, 0, 0))]
+    out_shape = [shape(*out)]
+    small = jax.ShapeDtypeStruct((2 * rows, HEAD_DIM), F32)
+    if first:
+        out_specs.append(same(small))
+        out_shape.append(small)
+    return pl.pallas_call(
+        lambda *refs: project_kernel(first, *refs),
+        grid_spec=pltpu.PrefetchScalarGridSpec(
+            num_scalar_prefetch=2,
+            grid=(ranks // 2,),
+            in_specs=([scalar(), scalar()] if first else [])
+            + [same(x), same(other)]
+            + chunked(wq, width, lambda s, p, b: 2 * rank_of(s, p) + b[0])
+            + [pl.BlockSpec((depth, HEAD_DIM), lambda s, p, b: (0, rank_of(s, p) + ranks * b[0]))]
+            + ([same(down)] if first else [same(inner)]),
+            out_specs=out_specs,
+            scratch_shapes=[pltpu.VMEM((2 * rows, depth), BF16)],
+        ),
+        out_shape=out_shape,
+        compiler_params=params(dimension_semantics=("arbitrary",)),
+        cost_estimate=pl.CostEstimate(
+            flops=rows * depth * (wq.shape[1] + wkv.shape[1]),
+            bytes_accessed=(wq.size + wkv.size) // 2,
+            transcendentals=0,
+        ),
+        name="project_sent" if first else "project_kept",
+    )(
+        place,
+        bank,
+        *(index if first else ()),
+        x,
+        other,
+        *[wq] * CHUNKS,
+        wkv,
+        down if first else inner,
+    )
+
+
+def halve_kernel(kept_ref, came_ref, sent_out, kept_out):
+    for i in range(kept_out.shape[0]):
+        for out, j in ((kept_out, 2 * i), (sent_out, 2 * i + 1)):
+            out[i] = (kept_ref[j].astype(F32) + came_ref[j].astype(F32)).astype(out.dtype)
+
+
+def halve(kept, came):
+    half = jax.ShapeDtypeStruct((kept.shape[0] // 2,) + kept.shape[1:], kept.dtype)
+    return pl.pallas_call(
+        halve_kernel,
+        in_specs=[whole()] * 2,
+        out_specs=[whole()] * 2,
+        out_shape=[half, half],
+        compiler_params=params(),
+        name="halve",
+    )(kept, came)
+
+
+def correct_kernel(bank, own_index, other_index, kept_ref, came_ref, up_ref, own_out, other_out):
+    total = kept_ref[0] + came_ref[0]
+    count, rank, width = up_ref.shape
+    half = width // 2
+    inner = total[:, half + HEAD_DIM :].astype(BF16).astype(F32)
+    column = adapter_column((own_index, other_index), bank[0], count)
+    lane = iota(column.shape, 1)
+    per = HEAD_DIM // rank
+    spread = jnp.concatenate(
+        [
+            jnp.where(lane // rank + j * per == column, inner, 0.0)
+            for j in range(count // per)
+        ],
+        axis=1,
+    ).astype(BF16)
+    delta = jnp.dot(
+        spread, up_ref[...].reshape(count * rank, width), preferred_element_type=F32
+    )
+    rows = own_out.shape[0]
+    for side in range(2):
+        columns = slice(side * half, (side + 1) * half)
+        part = delta[:, columns] + jnp.where(bank[0] == side, total[:, :half], 0.0)
+        own_out[:, columns] = part[:rows]
+        other_out[:, columns] = part[rows:]
+    own_out[:, width:] = total[:rows, half : half + HEAD_DIM]
+    other_out[:, width:] = total[rows:, half : half + HEAD_DIM]
+
+
+def correct(bank, index, kept, came, up):
+    rows = kept.shape[1]
+    out = shape(rows // 2, up.shape[2] + HEAD_DIM)
+    return pl.pallas_call(
+        correct_kernel,
+        in_specs=[scalar()] * 3 + [whole()] * 3,
+        out_specs=[whole()] * 2,
+        out_shape=[out, out],
+        compiler_params=params(),
+        cost_estimate=pl.CostEstimate(
+            flops=2 * rows * up.size, bytes_accessed=2 * up.size, transcendentals=0
+        ),
+        name="correct",
+    )(bank, *index, kept, came, up)
+
+
+def rotate(v, cosine, sine):
+    return v * cosine + pltpu.roll(v, HEAD_DIM // 2, 1) * sine
+
+
+def rotate_kernel(bank, own_ref, came_ref, cos_ref, sin_ref, q_ref, k_ref, v_ref, rows_ref):
+    width = own_ref.shape[1] - HEAD_DIM
+    cosine, sine = cos_ref[...], sin_ref[...]
+    for g in range(width // HEAD_DIM):
+        columns = slice(g * HEAD_DIM, (g + 1) * HEAD_DIM)
+        rows_ref[:, g, :] = rotate(own_ref[:, columns] + came_ref[:, columns], cosine, sine)
+    q_ref[0] = rows_ref[...].reshape(q_ref.shape[1:]).astype(BF16)
+    own, came = own_ref[:, width:], came_ref[:, width:]
+    key = jnp.where(bank[0] == 0, own, came)
+    value = jnp.where(bank[0] == 0, came, own)
+    k_ref[...] = rotate(key, cosine, sine).astype(BF16).astype(F32)
+    v_ref[...] = value.astype(BF16).astype(F32)
+
+
+def rotated(bank, own, came, cosine, sine):
+    rows = own.shape[0]
+    heads = own.shape[1] // HEAD_DIM - 1
+    return pl.pallas_call(
+        rotate_kernel,
+        in_specs=[scalar()] + [whole()] * 4,
+        out_specs=[whole()] * 3,
+        out_shape=[
+            shape(1, rows * heads, HEAD_DIM, dtype=BF16),
+            shape(rows, HEAD_DIM),
+            shape(rows, HEAD_DIM),
+        ],
+        scratch_shapes=[pltpu.VMEM((rows, heads, HEAD_DIM), F32)],
+        compiler_params=params(),
+        name="rotate",
+    )(bank, own, came, cosine, sine)
+
+
+def join_kernel(first_ref, second_ref, out_ref):
+    half = first_ref.shape[0]
+    out_ref[:half] = first_ref[...]
+    out_ref[half:] = second_ref[...]
+
+
+def join(first, second):
+    return pl.pallas_call(
+        join_kernel,
+        in_specs=[whole()] * 2,
+        out_specs=whole(),
+        out_shape=shape(2 * first.shape[0], *first.shape[1:], dtype=first.dtype),
+        compiler_params=params(),
+        name="join",
+    )(first, second)
+
+
+def gathered_slots(ranks):
+    slots, bit = [0], ranks // 2
+    while bit:
+        slots += [slot ^ bit for slot in slots]
+        bit //= 2
+    return slots
+
+
+def attend_kernel(place, length, near_ref, far_ref, k_ref, v_ref, out_ref, q_rows, o_rows, stats):
+    beam = pl.program_id(0)
+    beams = pl.num_programs(0)
+    ranks = 2 * near_ref.shape[0]
+    group = q_rows.shape[1] // stats.shape[0]
+    heads = ranks * group
+    positions = k_ref.shape[1]
+
+    @pl.when(beam == 0)
+    def _():
+        q_rows[: ranks // 2] = near_ref[...].astype(F32)
+        q_rows[ranks // 2 :] = far_ref[...].astype(F32)
+
+    first = pl.multiple_of(beam * group, group)
+    q = q_rows[:, pl.ds(first, group), :].reshape(heads, HEAD_DIM)
+    head_of = [place[0] ^ slot for slot in gathered_slots(ranks)]
+    row = iota((heads, HEAD_DIM), 0)
+    key_head = jnp.zeros((heads, HEAD_DIM), jnp.int32)
+    for i, head in enumerate(head_of):
+        key_head = jnp.where(row // group == i, head, key_head)
+    wide = jnp.concatenate(
+        [jnp.where(key_head == c, q, 0.0) for c in range(ranks)], axis=1
+    ).astype(BF16)
+    scores = lax.dot_general(
+        wide, k_ref[0], (((1,), (1,)), ((), ())), preferred_element_type=F32
+    ) * (1.0 / HEAD_DIM**0.5)
+    live = place[0] * positions + iota((heads, positions), 1) < length[beam]
+    scores = jnp.where(live, scores, -1e30)
+    peak = jnp.max(scores, axis=1, keepdims=True)
+    weights = jnp.where(live, jnp.exp(scores - peak), 0.0)
+    total = jnp.sum(weights, axis=1, keepdims=True)
+    product = jnp.dot(weights.astype(BF16), v_ref[0], preferred_element_type=F32)
+    own = jnp.zeros((heads, HEAD_DIM), F32)
+    for c in range(ranks):
+        own = jnp.where(key_head == c, product[:, c * HEAD_DIM : (c + 1) * HEAD_DIM], own)
+    for i, head in enumerate(head_of):
+        o_rows[head, pl.ds(first, group), :] = own[i * group : (i + 1) * group]
+    lane = iota((heads, HEAD_DIM), 1)
+    head = key_head * group + row % group
+    spread = jnp.where(head == lane, peak, 0.0) + jnp.where(head + heads == lane, total, 0.0)
+    stats[pl.ds(beam, 1), :] = jnp.sum(spread, axis=0, keepdims=True)
+
+    @pl.when(beam == beams - 1)
+    def _():
+        high = stats[...].astype(BF16).astype(F32)
+        rest = stats[...] - high
+        middle = rest.astype(BF16).astype(F32)
+        low = rest - middle
+        tail = jnp.concatenate([high, middle, low, jnp.zeros_like(low)], axis=0)
+        for c in range(ranks):
+            out_ref[c] = jnp.concatenate([o_rows[c], tail], axis=0).astype(BF16)
+
+
+def attend(place, length, near, far, keys, values):
+    ranks, rows = 2 * near.shape[0], near.shape[1]
+    beams, positions, width = keys.shape
+    out = (ranks, rows + 4 * beams, HEAD_DIM)
+    return pl.pallas_call(
+        attend_kernel,
+        grid_spec=pltpu.PrefetchScalarGridSpec(
+            num_scalar_prefetch=2,
+            grid=(beams,),
+            in_specs=[pl.BlockSpec(near.shape, lambda i, p, n: (0, 0, 0))] * 2
+            + [pl.BlockSpec((1, positions, width), lambda i, p, n: (i, 0, 0))] * 2,
+            out_specs=pl.BlockSpec(out, lambda i, p, n: (0, 0, 0)),
+            scratch_shapes=[
+                pltpu.VMEM((ranks, rows, HEAD_DIM), F32),
+                pltpu.VMEM((ranks, rows, HEAD_DIM), F32),
+                pltpu.VMEM((beams, HEAD_DIM), F32),
+            ],
+        ),
+        out_shape=jax.ShapeDtypeStruct(out, BF16),
+        compiler_params=params(dimension_semantics=("arbitrary",)),
+        cost_estimate=pl.CostEstimate(
+            flops=4 * rows * ranks * positions * width,
+            bytes_accessed=4 * keys.size,
+            transcendentals=rows * ranks * positions,
+        ),
+        name="attend",
+    )(place, length, near, far, keys, values)
+
+
+def combine_kernel(place, parts_ref, q_ref, k_ref, v_ref, out_ref, joined):
+    ranks = parts_ref.shape[0]
+    beams, group, _ = joined.shape
+    rows = beams * group
+
+    def by_row(v):
+        return jnp.broadcast_to(v[:, None, :], (beams, group, HEAD_DIM)).reshape(rows, HEAD_DIM)
+
+    head = place[0] * group + iota((rows, HEAD_DIM), 0) % group
+    lane = iota((rows, HEAD_DIM), 1)
+    score = jnp.sum(q_ref[0].astype(F32) * by_row(k_ref[...]), axis=1, keepdims=True) * (
+        1.0 / HEAD_DIM**0.5
+    )
+    peaks, totals, weighted = [], [], []
+    top = score
+    for s in range(ranks):
+        block = parts_ref[s].astype(F32)
+        tail = by_row(
+            block[rows : rows + beams]
+            + block[rows + beams : rows + 2 * beams]
+            + block[rows + 2 * beams : rows + 3 * beams]
+        )
+        peak = jnp.sum(jnp.where(lane == head, tail, 0.0), axis=1, keepdims=True)
+        total = jnp.sum(
+            jnp.where(lane == ranks * group + head, tail, 0.0), axis=1, keepdims=True
+        )
+        top = jnp.maximum(top, peak)
+        peaks.append(peak)
+        totals.append(total)
+        weighted.append(block[:rows])
+    new = jnp.exp(score - top)
+    everything = new
+    result = new.astype(BF16).astype(F32) * by_row(v_ref[...])
+    for peak, total, block in zip(peaks, totals, weighted):
+        factor = jnp.exp(peak - top)
+        everything += total * factor
+        result += block * factor
+    joined[...] = (result / everything).reshape(joined.shape)
+    for g in range(group):
+        out_ref[:, g * HEAD_DIM : (g + 1) * HEAD_DIM] = joined[:, g, :].astype(BF16)
+
+
+def combine(place, parts, query, key_new, value_new):
+    beams = key_new.shape[0]
+    group = query.shape[1] // beams
+    return pl.pallas_call(
+        combine_kernel,
+        in_specs=[scalar()] + [whole()] * 4,
+        out_specs=whole(),
+        out_shape=shape(beams, group * HEAD_DIM, dtype=BF16),
+        scratch_shapes=[pltpu.VMEM((beams, group, HEAD_DIM), F32)],
+        compiler_params=params(),
+        name="combine",
+    )(place, parts, query, key_new, value_new)
+
+
+def output_kernel(place, bank, own_ref, other_ref, *refs):
+    *weights, out, rows = refs
+
+    @pl.when(pl.program_id(0) == 0)
+    def _():
+        both_banks(own_ref, other_ref, rows)
+
+    out[0] = chunk_product(rows[...], weights).astype(BF16)
+
+
+def output(place, bank, own, other, weight, ranks, parity):
+    beams, depth = own.shape
+    width = weight.shape[1] // ranks // 2
+    out = (ranks // 2, 2 * beams, width)
+    column = lambda s, p, b: 2 * ((2 * s + parity) ^ p[0]) + b[0]
+    return pl.pallas_call(
+        output_kernel,
+        grid_spec=pltpu.PrefetchScalarGridSpec(
+            num_scalar_prefetch=2,
+            grid=(ranks // 2,),
+            in_specs=[pl.BlockSpec(own.shape, lambda s, p, b: (0, 0))] * 2
+            + chunked(weight, width, column),
+            out_specs=pl.BlockSpec((1,) + out[1:], lambda s, p, b: (s, 0, 0)),
+            scratch_shapes=[pltpu.VMEM((2 * beams, depth), BF16)],
+        ),
+        out_shape=shape(*out, dtype=BF16),
+        compiler_params=params(dimension_semantics=("arbitrary",)),
+        cost_estimate=pl.CostEstimate(
+            flops=beams * weight.size, bytes_accessed=weight.size // 2, transcendentals=0
+        ),
+        name="output_sent" if parity else "output_kept",
+    )(place, bank, own, other, *[weight] * CHUNKS)
+
+
+def part_kernel(kept_ref, came_ref, own_out, other_out):
+    total = kept_ref[0].astype(F32) + came_ref[0].astype(F32)
+    rows = own_out.shape[0]
+    own_out[...] = total[:rows]
+    other_out[...] = total[rows:].astype(BF16)
+
+
+def part(kept, came):
+    _, rows, width = kept.shape
+    return pl.pallas_call(
+        part_kernel,
+        in_specs=[whole()] * 2,
+        out_specs=[whole()] * 2,
+        out_shape=[shape(rows // 2, width), shape(rows // 2, width, dtype=BF16)],
+        compiler_params=params(),
+        name="part",
+    )(kept, came)
+
+
+def residual_kernel(bank, x_ref, own_ref, came_ref, out_ref):
+    half = own_ref.shape[1]
+    own, came = own_ref[...], came_ref[...].astype(F32)
+    for side in range(2):
+        columns = slice(side * half, (side + 1) * half)
+        total = jnp.where(bank[0] == side, own, came)
+        out_ref[:, columns] = (x_ref[:, columns].astype(F32) + total).astype(BF16)
+
+
+def residual(bank, x, own, came):
+    return pl.pallas_call(
+        residual_kernel,
+        in_specs=[scalar()] + [whole()] * 3,
+        out_specs=whole(),
+        out_shape=jax.ShapeDtypeStruct(x.shape, BF16),
+        compiler_params=params(),
+        name="residual",
+    )(bank, x, own, came)
+
+
+def swapped(x):
+    return lax.ppermute(x, "bank", [(0, 1), (1, 0)])
+
+
+def hop(x, bit):
+    ranks = lax.axis_size("tensor")
+    return lax.ppermute(x, "tensor", [(i, i ^ bit) for i in range(ranks)])
+
+
+def matched_body(
+    normed_hidden_input,
+    beam_adapter_index,
+    beam_cache_length,
+    query_weight,
+    keyvalue_weight,
+    output_weight,
+    lowrank_down_factors,
+    lowrank_up_factors,
+    paged_key_cache,
+    paged_value_cache,
+):
+    x = normed_hidden_input
+    ranks = lax.axis_size("tensor")
+    place = lax.axis_index("tensor").astype(jnp.int32).reshape(1)
+    bank = lax.axis_index("bank").astype(jnp.int32).reshape(1)
+    index = (beam_adapter_index, swapped(beam_adapter_index))
+    x_other = swapped(x)
+    half = HEAD_DIM // 2
+    frequency = jnp.power(500000.0, -2.0 * jnp.arange(half, dtype=F32) / HEAD_DIM)
+    angles = beam_cache_length.astype(F32)[:, None] * frequency[None, :]
+    cosine = jnp.tile(jnp.cos(angles), (1, 2))
+    sine = jnp.sin(angles)
+    sine = jnp.concatenate([-sine, sine], axis=1)
+
+    weights = in_hbm(query_weight), in_hbm(keyvalue_weight)
+    sent, inner = project(
+        place,
+        bank,
+        x,
+        x_other,
+        *weights,
+        ranks,
+        down=in_hbm(lowrank_down_factors.swapaxes(1, 2)),
+        index=index,
+    )
+    came = hop(sent, 1)
+    (kept,) = project(place, bank, x, x_other, *weights, ranks, inner=inner)
+    sent, kept = halve(kept, came)
+    sent, kept = halve(kept, hop(sent, 2))
+    own, other = correct(bank, index, kept, hop(sent, 4), lowrank_up_factors)
+    query, key_new, value_new = rotated(bank, own, swapped(other), cosine, sine)
+
+    near = join(query, hop(query, 4))
+    near = join(near, hop(near, 2))
+    partial = attend(
+        place,
+        beam_cache_length,
+        near,
+        hop(near, 1),
+        in_hbm(paged_key_cache),
+        in_hbm(paged_value_cache),
+    )
+    parts = lax.all_to_all(partial, "tensor", 0, 0, tiled=True)
+    attended = combine(place, parts, query, key_new, value_new)
+    attended_other = swapped(attended)
+
+    weight = in_hbm(output_weight)
+    came = hop(output(place, bank, attended, attended_other, weight, ranks, 1), 1)
+    kept = output(place, bank, attended, attended_other, weight, ranks, 0)
+    sent, kept = halve(kept, came)
+    sent, kept = halve(kept, hop(sent, 2))
+    own, other = part(kept, hop(sent, 4))
+    return residual(bank, x, own, swapped(other))
 
 
 def joined(x, axis, combine):
@@ -158,8 +711,9 @@
 
 
 def solution(mesh):
+    matched = mesh.shape["tensor"] == 8 and mesh.shape["bank"] == 2
     return jax.shard_map(
-        body,
+        matched_body if matched else body,
         mesh=mesh,
         in_specs=(
             P(("groups", "bank"), "tensor"),

time: 256 us -> 84.7 us (0.33)
  blocking collectives: 115 us -> 14 us
  waiting for transfers between devices: 77.2 us -> 26 us
  matrix products: 26.9 us -> 0 us
  Pallas kernels: 0 us -> 26.6 us
  starting transfers between devices: 0.17 us -> 15.8 us
  between operations: 15.3 us -> 0.1 us
  other arithmetic: 13.4 us -> 0.2 us
  local copies, waits for them, and re-layouts: 7.45 us -> 1.48 us
    all_gather x3 -> x0, blocking collectives: 93.2 us -> none  [the longest x2 62.4 us: joined(): everything = jax.tree.map(lambda part: lax.all_gather(part, axis), x)]
    reduce_scatter x1 -> x0, waiting for transfers between devices: 60.6 us -> none  [body(): lax.psum_scatter(lax.dot_general(output_weight, attended_cols, (((0,), (1...]
    dot_general x8 -> x0, matrix products: 26.9 us -> none  [the longest x1 8.79 us: body(): jnp.dot(normed_hidden_input, query_weight, preferred_element_type=jnp.flo...]
    pallas_call x0 -> x16, Pallas kernels: none -> 26.6 us  [the longest x2 9.05 us: project(): pl.pallas_call(lambda *refs: project_kernel(first, *refs), grid_spec=pltp...]
    ppermute x0 -> x14, waiting for transfers between devices: none -> 26 us  [the longest x9 21.4 us: hop(): return lax.ppermute(x, 'tensor', [(i, i ^ bit) for i in range(ranks)])]
    psum x1 -> x0, blocking collectives: 21.6 us -> none  [body(): inner_total = lax.psum(inner_part, 'tensor').astype(jnp.bfloat16)]
    ppermute x0 -> x14, starting transfers between devices: none -> 15.8 us  [the longest x9 15.1 us: hop(): return lax.ppermute(x, 'tensor', [(i, i ^ bit) for i in range(ranks)])]
    all_to_all x0 -> x1, blocking collectives: none -> 14 us  [matched_body(): parts = lax.all_to_all(partial, 'tensor', 0, 0, tiled=True)]
  transfers between devices with their start and end apart: 5 -> 14, of which waited for: 3 -> 13; matrix products, arithmetic and copies ran while one was open for 8% -> 0% of each run, Pallas kernels for 0% -> 8%
where the time goes in v3:
time: 84.7 us; the launch traced here: 84.1 us
  Pallas kernels  26.6 us (31%)
  waiting for transfers between devices  26 us (31%)
  starting transfers between devices  15.8 us (19%)
  blocking collectives  14 us (17%)
  local copies, waits for them, and re-layouts  1.48 us (2%)
    ppermute x9, waiting for transfers between devices, hop(): return lax.ppermute(x, 'tensor', [(i, i ^ bit) for i in range(ranks)])  21.4 us
    ppermute x9, starting transfers between devices, hop(): return lax.ppermute(x, 'tensor', [(i, i ^ bit) for i in range(ranks)])  15.1 us
    all_to_all x1, blocking collectives, matched_body(): parts = lax.all_to_all(partial, 'tensor', 0, 0, tiled=True)  14 us
    pallas_call x2, Pallas kernels, project(): pl.pallas_call(lambda *refs: project_kernel(first, *refs), grid_spec=pltp...  9.05 us
    pallas_call x1, Pallas kernels, attend(): pl.pallas_call(attend_kernel, grid_spec=pltpu.PrefetchScalarGridSpec(num_...  8.94 us
    pallas_call x2, Pallas kernels, output(): pl.pallas_call(output_kernel, grid_spec=pltpu.PrefetchScalarGridSpec(num_...  6.55 us
    ppermute x5, waiting for transfers between devices, swapped(): return lax.ppermute(x, 'bank', [(0, 1), (1, 0)])  4.58 us
  transfers between devices with their start and end apart: 14, of which 13 were waited for; matrix products, arithmetic and copies ran while one was open for 0% of the time, Pallas kernels for 8%

profile of v3, /device:TPU:0, one launch (start us, length us, event | category | flops | bytes accessed | tf_op | source)
XLA Modules:
  0.0 84.1 jit_solution(165820003823620334)
XLA Ops:
  0.0 0.5 collective-permute-start.1
  0.5 0.1 collective-permute-start
  0.5 1.2 %collective-permute-done.refs_3_.other_index = s32[8]{0:T(128)S(1)} collective-permute-done((s32[8]{0:T(128)}, s32[8]{0:T(128)S(1)}, u32[]{:S(2)}, u32[]{:S(2)}) %collective-permute-start) | collective-permute-done | bytes 64 | tf_op jit(solution)/shard_map/ppermute | solution.py:488
  1.7 0.0 collective-permute-done.1.refs_5_.refs_3_
  1.7 0.0 copy-start.1
  1.7 0.7 copy-done.1
  2.4 0.0 copy-start.3
  2.4 0.7 copy-done.3
  3.1 0.0 copy-start.5
  3.1 0.0 copy-start.2
  3.1 5.2 %project_sent.1 = (f32[4,16,768]{2,1,0:T(8,128)S(1)}, f32[16,128]{1,0:T(8,128)S(1)}) custom-call(s32[1]{0:T(128)} %bitcast.1.refs_0_.place, s32[1]{0:T(128)} %bitcast.refs_1_.bank, s32[8]{0:T(128)S(1)} %copy-done.3, s32[8]{0:T(128)S(1)} %collective-permute-done.refs_3_.other_index, bf16[8,1024]{1,0:T(8,128)(2,1)S(1)} %copy-done.1, ...), custom_call_target="tpu_custom_call" | custom-call | flops 83886080 | bytes 5242880 | tf_op jit(solution)/shard_map/project_sent/pallas_call | solution.py:120
  8.4 2.8 %collective-permute-start.2 = (f32[4,16,768]{2,1,0:T(8,128)S(1)}, f32[4,16,768]{2,1,0:T(8,128)S(1)}, u32[]{:S(2)}, u32[]{:S(2)}) collective-permute-start(f32[4,16,768]{2,1,0:T(8,128)S(1)} %get-tuple-element.23), channel_id=1, source_target_pairs={{0,2},{2,0},{4,6},{6,4},{8,10},{10,8},{12,14},{14,12},{1,3},{3,1},... | collective-permute-start | bytes 589832 | tf_op jit(solution)/shard_map/ppermute | solution.py:493
  11.1 0.0 copy-done.5
  11.1 0.0 copy-done.2
  11.1 0.0 copy-start
  11.2 0.0 copy-start.4
  11.2 3.8 %project_kept.1.kept_ref = f32[4,16,768]{2,1,0:T(8,128)S(1)} custom-call(s32[1]{0:T(128)} %bitcast.1.refs_0_.place, s32[1]{0:T(128)} %bitcast.refs_1_.bank, bf16[8,1024]{1,0:T(8,128)(2,1)S(1)} %copy-done.2, bf16[8,1024]{1,0:T(8,128)(2,1)S(1)} %collective-permute-done.1.refs_5_.refs_3_, bf16[1024,8192]{1,0:T(8,128)(2,1)} %refs_7_.3, ...), custom_call_target="tpu_custom_call" | custom-call | flops 83886080 | bytes 5242880 | tf_op jit(solution)/shard_map/project_kept/pallas_call | solution.py:120
  15.0 1.5 %collective-permute-done.2.came_ref = f32[4,16,768]{2,1,0:T(8,128)S(1)} collective-permute-done((f32[4,16,768]{2,1,0:T(8,128)S(1)}, f32[4,16,768]{2,1,0:T(8,128)S(1)}, u32[]{:S(2)}, u32[]{:S(2)}) %collective-permute-start.2) | collective-permute-done | bytes 196640 | tf_op jit(solution)/shard_map/ppermute | solution.py:493
  16.5 1.9 %collective-permute-start.3 = (f32[2,16,768]{2,1,0:T(8,128)S(1)}, f32[2,16,768]{2,1,0:T(8,128)S(1)}, u32[]{:S(2)}, u32[]{:S(2)}) collective-permute-start(f32[2,16,768]{2,1,0:T(8,128)S(1)} %get-tuple-element.25), channel_id=1, source_target_pairs={{0,4},{2,6},{4,0},{6,2},{8,12},{10,14},{12,8},{14,10},{1,5},{3,7},... | collective-permute-start | bytes 294920 | tf_op jit(solution)/shard_map/ppermute | solution.py:493
  18.4 2.8 %collective-permute-done.3.came_ref = f32[2,16,768]{2,1,0:T(8,128)S(1)} collective-permute-done((f32[2,16,768]{2,1,0:T(8,128)S(1)}, f32[2,16,768]{2,1,0:T(8,128)S(1)}, u32[]{:S(2)}, u32[]{:S(2)}) %collective-permute-start.3) | collective-permute-done | bytes 98336 | tf_op jit(solution)/shard_map/ppermute | solution.py:493
  21.2 2.9 %collective-permute-start.4 = (f32[1,16,768]{2,1,0:T(8,128)S(1)}, f32[1,16,768]{2,1,0:T(8,128)S(1)}, u32[]{:S(2)}, u32[]{:S(2)}) collective-permute-start(f32[1,16,768]{2,1,0:T(8,128)S(1)} %get-tuple-element.27), channel_id=1, source_target_pairs={{0,8},{2,10},{4,12},{6,14},{8,0},{10,2},{12,4},{14,6},{1,9},{3,11}... | collective-permute-start | bytes 147464 | tf_op jit(solution)/shard_map/ppermute | solution.py:493
  24.1 0.1 fusion
  24.2 2.1 %collective-permute-done.4.came_ref = f32[1,16,768]{2,1,0:T(8,128)S(1)} collective-permute-done((f32[1,16,768]{2,1,0:T(8,128)S(1)}, f32[1,16,768]{2,1,0:T(8,128)S(1)}, u32[]{:S(2)}, u32[]{:S(2)}) %collective-permute-start.4) | collective-permute-done | bytes 49184 | tf_op jit(solution)/shard_map/ppermute | solution.py:493
  26.3 0.0 copy-done
  26.3 0.0 copy-done.4
  26.3 0.9 %correct.1 = (f32[8,1152]{1,0:T(8,128)S(1)}, f32[8,1152]{1,0:T(8,128)S(1)}) custom-call(s32[1]{0:T(128)} %bitcast.refs_1_.bank, s32[8]{0:T(128)S(1)} %copy-done.4, s32[8]{0:T(128)S(1)} %collective-permute-done.refs_3_.other_index, f32[1,16,768]{2,1,0:T(8,128)S(1)} %get-tuple-element.26.kept_ref, f32[1,16,768]{2,1,0:T(8,128)S(1)} %collective-permute-done.4.came_ref, ...), custom_call_target="tpu_custom_call" | custom-call | flops 33554432 | bytes 2097152 | tf_op jit(solution)/shard_map/correct/pallas_call | solution.py:202
  27.2 0.0 collective-permute-start.5
  27.2 0.1 pad_maximum_fusion.sin_ref
  27.3 0.1 tile.10.cos_ref
  27.4 1.1 %collective-permute-done.5.came_ref = f32[8,1152]{1,0:T(8,128)S(1)} collective-permute-done((f32[8,1152]{1,0:T(8,128)S(1)}, f32[8,1152]{1,0:T(8,128)S(1)}, u32[]{:S(2)}, u32[]{:S(2)}) %collective-permute-start.5) | collective-permute-done | bytes 36896 | tf_op jit(solution)/shard_map/ppermute | solution.py:488
  28.4 0.1 rotate.1
  28.5 2.9 %collective-permute-start.6 = (bf16[1,64,128]{2,1,0:T(8,128)(2,1)S(1)}, bf16[1,64,128]{2,1,0:T(8,128)(2,1)S(1)}, u32[]{:S(2)}, u32[]{:S(2)}) collective-permute-start(bf16[1,64,128]{2,1,0:T(8,128)(2,1)S(1)} %get-tuple-element.30.first_ref.q_ref), channel_id=1, source_target_pairs={{0,8},{2,10},{4,12},{6,14},{8,0},{10,2},{12,4},{14,6},{1,9},{3,11}... | collective-permute-start | bytes 49160 | tf_op jit(solution)/shard_map/ppermute | solution.py:493
  31.5 1.8 %collective-permute-done.6.second_ref = bf16[1,64,128]{2,1,0:T(8,128)(2,1)S(1)} collective-permute-done((bf16[1,64,128]{2,1,0:T(8,128)(2,1)S(1)}, bf16[1,64,128]{2,1,0:T(8,128)(2,1)S(1)}, u32[]{:S(2)}, u32[]{:S(2)}) %collective-permute-start.6) | collective-permute-done | bytes 16416 | tf_op jit(solution)/shard_map/ppermute | solution.py:493
  33.3 1.9 %collective-permute-start.7 = (bf16[2,64,128]{2,1,0:T(8,128)(2,1)S(1)}, bf16[2,64,128]{2,1,0:T(8,128)(2,1)S(1)}, u32[]{:S(2)}, u32[]{:S(2)}) collective-permute-start(bf16[2,64,128]{2,1,0:T(8,128)(2,1)S(1)} %join.2.first_ref), channel_id=1, source_target_pairs={{0,4},{2,6},{4,0},{6,2},{8,12},{10,14},{12,8},{14,10},{1,5},{3,7},... | collective-permute-start | bytes 98312 | tf_op jit(solution)/shard_map/ppermute | solution.py:493
  35.1 2.0 %collective-permute-done.7.second_ref = bf16[2,64,128]{2,1,0:T(8,128)(2,1)S(1)} collective-permute-done((bf16[2,64,128]{2,1,0:T(8,128)(2,1)S(1)}, bf16[2,64,128]{2,1,0:T(8,128)(2,1)S(1)}, u32[]{:S(2)}, u32[]{:S(2)}) %collective-permute-start.7) | collective-permute-done | bytes 32800 | tf_op jit(solution)/shard_map/ppermute | solution.py:493
  37.2 1.7 %collective-permute-start.8 = (bf16[4,64,128]{2,1,0:T(8,128)(2,1)S(1)}, bf16[4,64,128]{2,1,0:T(8,128)(2,1)S(1)}, u32[]{:S(2)}, u32[]{:S(2)}) collective-permute-start(bf16[4,64,128]{2,1,0:T(8,128)(2,1)S(1)} %join.3.near_ref), channel_id=1, source_target_pairs={{0,2},{2,0},{4,6},{6,4},{8,10},{10,8},{12,14},{14,12},{1,3},{3,1},... | collective-permute-start | bytes 196616 | tf_op jit(solution)/shard_map/ppermute | solution.py:493
  38.9 2.5 %collective-permute-done.8.far_ref = bf16[4,64,128]{2,1,0:T(8,128)(2,1)S(1)} collective-permute-done((bf16[4,64,128]{2,1,0:T(8,128)(2,1)S(1)}, bf16[4,64,128]{2,1,0:T(8,128)(2,1)S(1)}, u32[]{:S(2)}, u32[]{:S(2)}) %collective-permute-start.8) | collective-permute-done | bytes 65568 | tf_op jit(solution)/shard_map/ppermute | solution.py:493
  41.4 8.9 %attend.1 = bf16[8,96,128]{2,1,0:T(8,128)(2,1)S(1)} custom-call(s32[1]{0:T(128)} %bitcast.1.refs_0_.place, s32[8]{0:T(128)S(1)} %copy-done.5, bf16[4,64,128]{2,1,0:T(8,128)(2,1)S(1)} %join.3.near_ref, bf16[4,64,128]{2,1,0:T(8,128)(2,1)S(1)} %collective-permute-done.8.far_ref, bf16[8,256,1024]{2,1,0:T(8,128)(2,1)} %k_ref.1, bf16[8,256,1024]{2,1,0:T(8,128)(2,1)} %v_ref.1), custom_call_target="tpu_custom_call" | custom-call | flops 536870912 | bytes 8388608 | tf_op jit(solution)/shard_map/attend/pallas_call | solution.py:333
  50.4 14.0 %all_to_all.5.parts_ref = bf16[8,96,128]{2,1,0:T(8,128)(2,1)S(1)} all-to-all(bf16[8,96,128]{2,1,0:T(8,128)(2,1)S(1)} %attend.1), channel_id=1, replica_groups=mesh['groups'=2,'tensor'=8,'bank'=2] {'tensor'}, dimensions={0} | all-to-all | bytes 393216 | tf_op jit(solution)/shard_map/all_to_all | solution.py:549
  64.4 0.3 combine.1.own_ref
  64.7 0.1 collective-permute-start.9
  64.8 1.2 %collective-permute-done.9.other_ref = bf16[8,1024]{1,0:T(8,128)(2,1)S(1)} collective-permute-done((bf16[8,1024]{1,0:T(8,128)(2,1)S(1)}, bf16[8,1024]{1,0:T(8,128)(2,1)S(1)}, u32[]{:S(2)}, u32[]{:S(2)}) %collective-permute-start.9) | collective-permute-done | bytes 16416 | tf_op jit(solution)/shard_map/ppermute | solution.py:488
  66.0 3.3 %output_sent.1 = bf16[4,16,512]{2,1,0:T(8,128)(2,1)S(1)} custom-call(s32[1]{0:T(128)} %bitcast.1.refs_0_.place, s32[1]{0:T(128)} %bitcast.refs_1_.bank, bf16[8,1024]{1,0:T(8,128)(2,1)S(1)} %combine.1.own_ref, bf16[8,1024]{1,0:T(8,128)(2,1)S(1)} %collective-permute-done.9.other_ref, bf16[1024,8192]{1,0:T(8,128)(2,1)} %refs_3_.3, bf16[1024,8192]{1,0:T(8,128)(2,1)} %refs_3_.3, ...), custom_call_target="tpu_custom_call" | custom-call | flops 67108864 | bytes 4194304 | tf_op jit(solution)/shard_map/output_sent/pallas_call | solution.py:429
  69.3 0.1 collective-permute-start.10
  69.3 3.3 %output_kept.1.kept_ref = bf16[4,16,512]{2,1,0:T(8,128)(2,1)S(1)} custom-call(s32[1]{0:T(128)} %bitcast.1.refs_0_.place, s32[1]{0:T(128)} %bitcast.refs_1_.bank, bf16[8,1024]{1,0:T(8,128)(2,1)S(1)} %combine.1.own_ref, bf16[8,1024]{1,0:T(8,128)(2,1)S(1)} %collective-permute-done.9.other_ref, bf16[1024,8192]{1,0:T(8,128)(2,1)} %refs_3_.3, ...), custom_call_target="tpu_custom_call" | custom-call | flops 67108864 | bytes 4194304 | tf_op jit(solution)/shard_map/output_kept/pallas_call | solution.py:429
  72.6 0.9 %collective-permute-done.10.came_ref = bf16[4,16,512]{2,1,0:T(8,128)(2,1)S(1)} collective-permute-done((bf16[4,16,512]{2,1,0:T(8,128)(2,1)S(1)}, bf16[4,16,512]{2,1,0:T(8,128)(2,1)S(1)}, u32[]{:S(2)}, u32[]{:S(2)}) %collective-permute-start.10) | collective-permute-done | bytes 65568 | tf_op jit(solution)/shard_map/ppermute | solution.py:493
  73.6 0.5 collective-permute-start.11
  74.0 3.5 %collective-permute-done.11.came_ref = bf16[2,16,512]{2,1,0:T(8,128)(2,1)S(1)} collective-permute-done((bf16[2,16,512]{2,1,0:T(8,128)(2,1)S(1)}, bf16[2,16,512]{2,1,0:T(8,128)(2,1)S(1)}, u32[]{:S(2)}, u32[]{:S(2)}) %collective-permute-start.11) | collective-permute-done | bytes 32800 | tf_op jit(solution)/shard_map/ppermute | solution.py:493
  77.6 0.5 collective-permute-start.12
  78.1 4.2 %collective-permute-done.12.came_ref = bf16[1,16,512]{2,1,0:T(8,128)(2,1)S(1)} collective-permute-done((bf16[1,16,512]{2,1,0:T(8,128)(2,1)S(1)}, bf16[1,16,512]{2,1,0:T(8,128)(2,1)S(1)}, u32[]{:S(2)}, u32[]{:S(2)}) %collective-permute-start.12) | collective-permute-done | bytes 16416 | tf_op jit(solution)/shard_map/ppermute | solution.py:493
  82.3 0.1 collective-permute-start.13
  82.4 1.2 %collective-permute-done.13.came_ref = bf16[8,512]{1,0:T(8,128)(2,1)S(1)} collective-permute-done((bf16[8,512]{1,0:T(8,128)(2,1)S(1)}, bf16[8,512]{1,0:T(8,128)(2,1)S(1)}, u32[]{:S(2)}, u32[]{:S(2)}) %collective-permute-start.13) | collective-permute-done | bytes 8224 | tf_op jit(solution)/shard_map/ppermute | solution.py:488
  83.5 0.6 residual.1
  (10 shorter events, 0.1 us)
Async XLA Ops:
  0.0 1.7 %collective-permute-start.1 = (bf16[8,1024]{1,0:T(8,128)(2,1)}, bf16[8,1024]{1,0:T(8,128)(2,1)S(1)}, u32[]{:S(2)}, u32[]{:S(2)}) collective-permute-start(bf16[8,1024]{1,0:T(8,128)(2,1)} %x_ref.1), channel_id=1, source_target_pairs={{0,1},{1,0},{2,3},{3,2},{4,5},{5,4},{6,7},{7,6},{8,9},{9,8},{10,11... | collective-permute-start | bytes 49160 | tf_op jit(solution)/shard_map/ppermute | solution.py:488
  0.5 1.3 %collective-permute-start = (s32[8]{0:T(128)}, s32[8]{0:T(128)S(1)}, u32[]{:S(2)}, u32[]{:S(2)}) collective-permute-start(s32[8]{0:T(128)} %own_index.1), channel_id=1, source_target_pairs={{0,1},{1,0},{2,3},{3,2},{4,5},{5,4},{6,7},{7,6},{8,9},{9,8},{10,11... | collective-permute-start | bytes 104 | tf_op jit(solution)/shard_map/ppermute | solution.py:488
  1.7 0.7 copy-start.1
  2.4 0.7 copy-start.3
  3.1 8.1 %copy-start.5 = (s32[8]{0:T(128)S(1)}, s32[8]{0:T(128)}, u32[]{:S(2)}) copy-start(s32[8]{0:T(128)} %length.1) | copy-start | bytes 100
  3.1 8.1 %copy-start.2 = (bf16[8,1024]{1,0:T(8,128)(2,1)S(1)}, bf16[8,1024]{1,0:T(8,128)(2,1)}, u32[]{:S(2)}) copy-start(bf16[8,1024]{1,0:T(8,128)(2,1)} %x_ref.1) | copy-start | bytes 49156
  8.4 8.2 %collective-permute-start.2 = (f32[4,16,768]{2,1,0:T(8,128)S(1)}, f32[4,16,768]{2,1,0:T(8,128)S(1)}, u32[]{:S(2)}, u32[]{:S(2)}) collective-permute-start(f32[4,16,768]{2,1,0:T(8,128)S(1)} %get-tuple-element.23), channel_id=1, source_target_pairs={{0,2},{2,0},{4,6},{6,4},{8,10},{10,8},{12,14},{14,12},{1,3},{3,1},... | collective-permute-start | bytes 589832 | tf_op jit(solution)/shard_map/ppermute | solution.py:493
  11.1 15.1 %copy-start = (bf16[16,64,1024]{2,1,0:T(8,128)(2,1)S(1)}, bf16[16,64,1024]{2,1,0:T(8,128)(2,1)}, u32[]{:S(2)}) copy-start(bf16[16,64,1024]{2,1,0:T(8,128)(2,1)} %up_ref.1) | copy-start | bytes 6291460
  11.2 15.1 %copy-start.4 = (s32[8]{0:T(128)S(1)}, s32[8]{0:T(128)}, u32[]{:S(2)}) copy-start(s32[8]{0:T(128)} %own_index.1) | copy-start | bytes 100
  16.5 4.7 %collective-permute-start.3 = (f32[2,16,768]{2,1,0:T(8,128)S(1)}, f32[2,16,768]{2,1,0:T(8,128)S(1)}, u32[]{:S(2)}, u32[]{:S(2)}) collective-permute-start(f32[2,16,768]{2,1,0:T(8,128)S(1)} %get-tuple-element.25), channel_id=1, source_target_pairs={{0,4},{2,6},{4,0},{6,2},{8,12},{10,14},{12,8},{14,10},{1,5},{3,7},... | collective-permute-start | bytes 294920 | tf_op jit(solution)/shard_map/ppermute | solution.py:493
  21.2 5.1 %collective-permute-start.4 = (f32[1,16,768]{2,1,0:T(8,128)S(1)}, f32[1,16,768]{2,1,0:T(8,128)S(1)}, u32[]{:S(2)}, u32[]{:S(2)}) collective-permute-start(f32[1,16,768]{2,1,0:T(8,128)S(1)} %get-tuple-element.27), channel_id=1, source_target_pairs={{0,8},{2,10},{4,12},{6,14},{8,0},{10,2},{12,4},{14,6},{1,9},{3,11}... | collective-permute-start | bytes 147464 | tf_op jit(solution)/shard_map/ppermute | solution.py:493
  27.2 1.2 %collective-permute-start.5 = (f32[8,1152]{1,0:T(8,128)S(1)}, f32[8,1152]{1,0:T(8,128)S(1)}, u32[]{:S(2)}, u32[]{:S(2)}) collective-permute-start(f32[8,1152]{1,0:T(8,128)S(1)} %get-tuple-element.29), channel_id=1, source_target_pairs={{0,1},{1,0},{2,3},{3,2},{4,5},{5,4},{6,7},{7,6},{8,9},{9,8},{10,11... | collective-permute-start | bytes 110600 | tf_op jit(solution)/shard_map/ppermute | solution.py:488
  28.5 4.7 %collective-permute-start.6 = (bf16[1,64,128]{2,1,0:T(8,128)(2,1)S(1)}, bf16[1,64,128]{2,1,0:T(8,128)(2,1)S(1)}, u32[]{:S(2)}, u32[]{:S(2)}) collective-permute-start(bf16[1,64,128]{2,1,0:T(8,128)(2,1)S(1)} %get-tuple-element.30.first_ref.q_ref), channel_id=1, source_target_pairs={{0,8},{2,10},{4,12},{6,14},{8,0},{10,2},{12,4},{14,6},{1,9},{3,11}... | collective-permute-start | bytes 49160 | tf_op jit(solution)/shard_map/ppermute | solution.py:493
  33.3 3.9 %collective-permute-start.7 = (bf16[2,64,128]{2,1,0:T(8,128)(2,1)S(1)}, bf16[2,64,128]{2,1,0:T(8,128)(2,1)S(1)}, u32[]{:S(2)}, u32[]{:S(2)}) collective-permute-start(bf16[2,64,128]{2,1,0:T(8,128)(2,1)S(1)} %join.2.first_ref), channel_id=1, source_target_pairs={{0,4},{2,6},{4,0},{6,2},{8,12},{10,14},{12,8},{14,10},{1,5},{3,7},... | collective-permute-start | bytes 98312 | tf_op jit(solution)/shard_map/ppermute | solution.py:493
  37.2 4.3 %collective-permute-start.8 = (bf16[4,64,128]{2,1,0:T(8,128)(2,1)S(1)}, bf16[4,64,128]{2,1,0:T(8,128)(2,1)S(1)}, u32[]{:S(2)}, u32[]{:S(2)}) collective-permute-start(bf16[4,64,128]{2,1,0:T(8,128)(2,1)S(1)} %join.3.near_ref), channel_id=1, source_target_pairs={{0,2},{2,0},{4,6},{6,4},{8,10},{10,8},{12,14},{14,12},{1,3},{3,1},... | collective-permute-start | bytes 196616 | tf_op jit(solution)/shard_map/ppermute | solution.py:493
  64.7 1.2 %collective-permute-start.9 = (bf16[8,1024]{1,0:T(8,128)(2,1)S(1)}, bf16[8,1024]{1,0:T(8,128)(2,1)S(1)}, u32[]{:S(2)}, u32[]{:S(2)}) collective-permute-start(bf16[8,1024]{1,0:T(8,128)(2,1)S(1)} %combine.1.own_ref), channel_id=1, source_target_pairs={{0,1},{1,0},{2,3},{3,2},{4,5},{5,4},{6,7},{7,6},{8,9},{9,8},{10,11... | collective-permute-start | bytes 49160 | tf_op jit(solution)/shard_map/ppermute | solution.py:488
  69.3 4.3 %collective-permute-start.10 = (bf16[4,16,512]{2,1,0:T(8,128)(2,1)S(1)}, bf16[4,16,512]{2,1,0:T(8,128)(2,1)S(1)}, u32[]{:S(2)}, u32[]{:S(2)}) collective-permute-start(bf16[4,16,512]{2,1,0:T(8,128)(2,1)S(1)} %output_sent.1), channel_id=1, source_target_pairs={{0,2},{2,0},{4,6},{6,4},{8,10},{10,8},{12,14},{14,12},{1,3},{3,1},... | collective-permute-start | bytes 196616 | tf_op jit(solution)/shard_map/ppermute | solution.py:493
  73.6 4.0 %collective-permute-start.11 = (bf16[2,16,512]{2,1,0:T(8,128)(2,1)S(1)}, bf16[2,16,512]{2,1,0:T(8,128)(2,1)S(1)}, u32[]{:S(2)}, u32[]{:S(2)}) collective-permute-start(bf16[2,16,512]{2,1,0:T(8,128)(2,1)S(1)} %get-tuple-element.34), channel_id=1, source_target_pairs={{0,4},{2,6},{4,0},{6,2},{8,12},{10,14},{12,8},{14,10},{1,5},{3,7},... | collective-permute-start | bytes 98312 | tf_op jit(solution)/shard_map/ppermute | solution.py:493
  77.6 4.7 %collective-permute-start.12 = (bf16[1,16,512]{2,1,0:T(8,128)(2,1)S(1)}, bf16[1,16,512]{2,1,0:T(8,128)(2,1)S(1)}, u32[]{:S(2)}, u32[]{:S(2)}) collective-permute-start(bf16[1,16,512]{2,1,0:T(8,128)(2,1)S(1)} %get-tuple-element.36), channel_id=1, source_target_pairs={{0,8},{2,10},{4,12},{6,14},{8,0},{10,2},{12,4},{14,6},{1,9},{3,11}... | collective-permute-start | bytes 49160 | tf_op jit(solution)/shard_map/ppermute | solution.py:493
  82.3 1.2 %collective-permute-start.13 = (bf16[8,512]{1,0:T(8,128)(2,1)S(1)}, bf16[8,512]{1,0:T(8,128)(2,1)S(1)}, u32[]{:S(2)}, u32[]{:S(2)}) collective-permute-start(bf16[8,512]{1,0:T(8,128)(2,1)S(1)} %get-tuple-element.38), channel_id=1, source_target_pairs={{0,1},{1,0},{2,3},{3,2},{4,5},{5,4},{6,7},{7,6},{8,9},{9,8},{10,11... | collective-permute-start | bytes 24584 | tf_op jit(solution)/shard_map/ppermute | solution.py:488

commit v4 on v0

--- a/solution.py
+++ b/solution.py
@@ -1,9 +1,567 @@
 import jax
 import jax.numpy as jnp
 from jax import lax
+from jax.experimental import pallas as pl
+from jax.experimental.pallas import tpu as pltpu
 from jax.sharding import PartitionSpec as P
 
 HEAD_DIM = 128
+F32 = jnp.float32
+BF16 = jnp.bfloat16
+CHUNKS = 2
+VMEM_LIMIT = 24 * 1024 * 1024
+
+
+def whole():
+    return pl.BlockSpec(memory_space=pltpu.VMEM)
+
+
+def big():
+    return pl.BlockSpec(memory_space=pltpu.HBM)
+
+
+def scalar():
+    return pl.BlockSpec(memory_space=pltpu.SMEM)
+
+
+def in_hbm(array):
+    return pltpu.with_memory_space_constraint(array, pltpu.HBM)
+
+
+def shape(*dims, dtype=F32):
+    return jax.ShapeDtypeStruct(dims, dtype)
+
+
+def iota(dims, axis):
+    return lax.broadcasted_iota(jnp.int32, dims, axis)
+
+
+def params(**more):
+    return pltpu.CompilerParams(vmem_limit_bytes=VMEM_LIMIT, **more)
+
+
+def start_columns(weight, column, target, sems):
+    depth, width = target.shape
+    part = depth // CHUNKS
+    copies = []
+    for c in range(CHUNKS):
+        rows = pl.ds(c * part, part)
+        copies.append(
+            pltpu.make_async_copy(
+                weight.at[rows, pl.ds(pl.multiple_of(column, width), width)],
+                target.at[rows, :],
+                sems.at[c],
+            )
+        )
+        copies[-1].start()
+    return copies
+
+
+def adapter_column(refs, bank, count):
+    rows = len(refs) * refs[0].shape[0]
+    row = iota((rows, HEAD_DIM), 0)
+    column = jnp.zeros((rows, HEAD_DIM), jnp.int32)
+    for r in range(rows):
+        ref = refs[r // refs[0].shape[0]]
+        column = jnp.where(row == r, ref[r % ref.shape[0]], column)
+    return column - bank * count
+
+
+def project_kernel(first, ranks, place, bank, *refs):
+    if first:
+        own_index, other_index, x_ref, other_ref, w_ref, kv_ref, down_ref, out, inner = refs[:9]
+        w_buf, kv_buf, sems, kv_sems, x_buf, own_smem, other_smem, down_buf, small_sems = refs[9:]
+    else:
+        x_ref, other_ref, w_ref, kv_ref, inner, out = refs[:6]
+        w_buf, kv_buf, sems, kv_sems, x_buf, small_sems = refs[6:]
+    count, _, width = w_buf.shape
+    small = [pltpu.make_async_copy(x_ref, x_buf, small_sems.at[0])]
+    if first:
+        small.append(pltpu.make_async_copy(own_index, own_smem, small_sems.at[1]))
+        small.append(pltpu.make_async_copy(other_index, other_smem, small_sems.at[2]))
+    for copy in small:
+        copy.start()
+    copies = []
+    for s in range(count):
+        target = (2 * s + first) ^ place[0]
+        copies.append(
+            start_columns(w_ref, (2 * target + bank[0]) * width, w_buf.at[s], sems.at[s])
+            + start_columns(
+                kv_ref, (target + ranks * bank[0]) * HEAD_DIM, kv_buf.at[s], kv_sems.at[s]
+            )
+        )
+    if first:
+        down_copy = pltpu.make_async_copy(down_ref, down_buf, small_sems.at[3])
+        down_copy.start()
+    for copy in small:
+        copy.wait()
+    x = jnp.concatenate([x_buf[...].astype(F32), other_ref[...].astype(F32)], axis=0).astype(BF16)
+    for s in range(count):
+        for copy in copies[s]:
+            copy.wait()
+        out[s, :, :width] = jnp.dot(x, w_buf[s], preferred_element_type=F32)
+        out[s, :, width : width + HEAD_DIM] = jnp.dot(x, kv_buf[s], preferred_element_type=F32)
+    if first:
+        down_copy.wait()
+        adapters, rank, depth = down_buf.shape
+        every = lax.dot_general(
+            x,
+            down_buf[...].reshape(adapters * rank, depth),
+            (((1,), (1,)), ((), ())),
+            preferred_element_type=F32,
+        )
+        column = adapter_column((own_smem, other_smem), bank[0], adapters)
+        lane = iota(column.shape, 1)
+        per = HEAD_DIM // rank
+        total = jnp.zeros(column.shape, F32)
+        for j in range(adapters // per):
+            part = every[:, j * HEAD_DIM : (j + 1) * HEAD_DIM]
+            total += jnp.where(lane // rank + j * per == column, part, 0.0)
+        inner[...] = total
+    for s in range(count):
+        out[s, :, width + HEAD_DIM :] = inner[...]
+
+
+def project(place, bank, x, other, wq, wkv, ranks, down=None, index=None, inner=None):
+    rows, depth = x.shape
+    first = inner is None
+    width = wq.shape[1] // ranks // 2
+    half = ranks // 2
+    out = [shape(half, 2 * rows, width + 2 * HEAD_DIM)]
+    dma = pltpu.SemaphoreType.DMA
+    scratch = [
+        pltpu.VMEM((half, depth, width), BF16),
+        pltpu.VMEM((half, depth, HEAD_DIM), BF16),
+        dma((half, CHUNKS)),
+        dma((half, CHUNKS)),
+        pltpu.VMEM(x.shape, BF16),
+    ]
+    if first:
+        args = (*index, x, other, wq, wkv, down)
+        specs = [big(), pl.BlockSpec(memory_space=pl.ANY), big(), whole(), big(), big(), big()]
+        out.append(shape(2 * rows, HEAD_DIM))
+        scratch += [pltpu.SMEM((rows,), jnp.int32)] * 2
+        scratch += [pltpu.VMEM(down.shape, BF16), dma((4,))]
+    else:
+        args = (x, other, wq, wkv, inner)
+        specs = [big(), whole(), big(), big(), whole()]
+        scratch += [dma((1,))]
+    return pl.pallas_call(
+        lambda *refs: project_kernel(int(first), ranks, *refs),
+        in_specs=[scalar()] * 2 + specs,
+        out_specs=[whole()] * len(out),
+        out_shape=out,
+        scratch_shapes=scratch,
+        compiler_params=params(),
+        cost_estimate=pl.CostEstimate(
+            flops=rows * depth * (wq.shape[1] + wkv.shape[1]),
+            bytes_accessed=(wq.size + wkv.size) // 2,
+            transcendentals=0,
+        ),
+        name="project_sent" if first else "project_kept",
+    )(place, bank, *args)
+
+
+def halve_kernel(kept_ref, came_ref, sent_out, kept_out):
+    for i in range(kept_out.shape[0]):
+        for out, j in ((kept_out, 2 * i), (sent_out, 2 * i + 1)):
+            out[i] = (kept_ref[j].astype(F32) + came_ref[j].astype(F32)).astype(out.dtype)
+
+
+def halve(kept, came):
+    half = (kept.shape[0] // 2,) + kept.shape[1:]
+    return pl.pallas_call(
+        halve_kernel,
+        in_specs=[whole()] * 2,
+        out_specs=[whole()] * 2,
+        out_shape=[shape(*half, dtype=came.dtype), shape(*half, dtype=kept.dtype)],
+        compiler_params=params(),
+        name="halve",
+    )(kept, came)
+
+
+def correct_kernel(bank, own_index, other_index, kept_ref, came_ref, up_ref, own_out, other_out):
+    total = kept_ref[0] + came_ref[0]
+    count, rank, width = up_ref.shape
+    half = width // 2
+    inner = total[:, half + HEAD_DIM :].astype(BF16).astype(F32)
+    column = adapter_column((own_index, other_index), bank[0], count)
+    lane = iota(column.shape, 1)
+    per = HEAD_DIM // rank
+    spread = jnp.concatenate(
+        [
+            jnp.where(lane // rank + j * per == column, inner, 0.0)
+            for j in range(count // per)
+        ],
+        axis=1,
+    ).astype(BF16)
+    delta = jnp.dot(
+        spread, up_ref[...].reshape(count * rank, width), preferred_element_type=F32
+    )
+    rows = own_out.shape[0]
+    for side in range(2):
+        columns = slice(side * half, (side + 1) * half)
+        part = delta[:, columns] + jnp.where(bank[0] == side, total[:, :half], 0.0)
+        own_out[:, columns] = part[:rows]
+        other_out[:, columns] = part[rows:]
+    own_out[:, width:] = total[:rows, half : half + HEAD_DIM]
+    other_out[:, width:] = total[rows:, half : half + HEAD_DIM]
+
+
+def correct(bank, index, kept, came, up):
+    rows = kept.shape[1]
+    out = shape(rows // 2, up.shape[2] + HEAD_DIM)
+    return pl.pallas_call(
+        correct_kernel,
+        in_specs=[scalar()] * 3 + [whole()] * 3,
+        out_specs=[whole()] * 2,
+        out_shape=[out, out],
+        compiler_params=params(),
+        cost_estimate=pl.CostEstimate(
+            flops=2 * rows * up.size, bytes_accessed=2 * up.size, transcendentals=0
+        ),
+        name="correct",
+    )(bank, *index, kept, came, up)
+
+
+def rotate(v, cosine, sine):
+    return v * cosine + pltpu.roll(v, HEAD_DIM // 2, 1) * sine
+
+
+def rotate_kernel(bank, own_ref, came_ref, cos_ref, sin_ref, q_ref, k_ref, v_ref, rows_ref):
+    width = own_ref.shape[1] - HEAD_DIM
+    cosine, sine = cos_ref[...], sin_ref[...]
+    for g in range(width // HEAD_DIM):
+        columns = slice(g * HEAD_DIM, (g + 1) * HEAD_DIM)
+        rows_ref[:, g, :] = rotate(own_ref[:, columns] + came_ref[:, columns], cosine, sine)
+    q_ref[0] = rows_ref[...].reshape(q_ref.shape[1:]).astype(BF16)
+    own, came = own_ref[:, width:], came_ref[:, width:]
+    key = jnp.where(bank[0] == 0, own, came)
+    value = jnp.where(bank[0] == 0, came, own)
+    k_ref[...] = rotate(key, cosine, sine).astype(BF16).astype(F32)
+    v_ref[...] = value.astype(BF16).astype(F32)
+
+
+def rotated(bank, own, came, cosine, sine):
+    rows = own.shape[0]
+    heads = own.shape[1] // HEAD_DIM - 1
+    return pl.pallas_call(
+        rotate_kernel,
+        in_specs=[scalar()] + [whole()] * 4,
+        out_specs=[whole()] * 3,
+        out_shape=[
+            shape(1, rows * heads, HEAD_DIM, dtype=BF16),
+            shape(rows, HEAD_DIM),
+            shape(rows, HEAD_DIM),
+        ],
+        scratch_shapes=[pltpu.VMEM((rows, heads, HEAD_DIM), F32)],
+        compiler_params=params(),
+        name="rotate",
+    )(bank, own, came, cosine, sine)
+
+
+def join_kernel(first_ref, second_ref, out_ref):
+    half = first_ref.shape[0]
+    out_ref[:half] = first_ref[...]
+    out_ref[half:] = second_ref[...]
+
+
+def join(first, second):
+    return pl.pallas_call(
+        join_kernel,
+        in_specs=[whole()] * 2,
+        out_specs=whole(),
+        out_shape=shape(2 * first.shape[0], *first.shape[1:], dtype=first.dtype),
+        compiler_params=params(),
+        name="join",
+    )(first, second)
+
+
+def fetch_kernel(ref, out, sems):
+    part = ref.shape[0] // sems.shape[0]
+    copies = [
+        pltpu.make_async_copy(
+            ref.at[pl.ds(c * part, part)], out.at[pl.ds(c * part, part)], sems.at[c]
+        )
+        for c in range(sems.shape[0])
+    ]
+    for copy in copies:
+        copy.start()
+    for copy in copies:
+        copy.wait()
+
+
+def fetch(array):
+    return pl.pallas_call(
+        fetch_kernel,
+        in_specs=[big()],
+        out_specs=whole(),
+        out_shape=jax.ShapeDtypeStruct(array.shape, array.dtype),
+        scratch_shapes=[pltpu.SemaphoreType.DMA((4,))],
+        compiler_params=params(),
+        cost_estimate=pl.CostEstimate(
+            flops=0, bytes_accessed=2 * array.size, transcendentals=0
+        ),
+        name="fetch",
+    )(in_hbm(array))
+
+
+def attend_kernel(slots, earlier, place, length, q_ref, k_ref, v_ref, *refs):
+    before, out_ref = refs[:-1], refs[-1]
+    beams, positions, _ = k_ref.shape
+    rows = q_ref.shape[1]
+    group = rows // beams
+    row, lane = iota((rows, positions), 0), iota((rows, positions), 1)
+    limit = jnp.zeros((rows, positions), jnp.int32)
+    for beam in range(beams):
+        limit = jnp.where(row // group == beam, length[beam], limit)
+    live = place[0] * positions + lane < limit
+    row, lane = iota((rows, HEAD_DIM), 0), iota((rows, HEAD_DIM), 1)
+    for i, slot in enumerate(slots):
+        head = place[0] ^ slot
+        columns = pl.ds(pl.multiple_of(head * HEAD_DIM, HEAD_DIM), HEAD_DIM)
+        query = q_ref[i].astype(F32)
+        scores = jnp.concatenate(
+            [
+                lax.dot_general(
+                    query[beam * group : (beam + 1) * group].astype(BF16),
+                    k_ref[beam, :, columns],
+                    (((1,), (1,)), ((), ())),
+                    preferred_element_type=F32,
+                )
+                for beam in range(beams)
+            ],
+            axis=0,
+        ) * (1.0 / HEAD_DIM**0.5)
+        scores = jnp.where(live, scores, -1e30)
+        peak = jnp.max(scores, axis=1, keepdims=True)
+        weights = jnp.where(live, jnp.exp(scores - peak), 0.0)
+        total = jnp.sum(weights, axis=1, keepdims=True)
+        values = [
+            jnp.dot(
+                weights[beam * group : (beam + 1) * group].astype(BF16),
+                v_ref[beam, :, columns],
+                preferred_element_type=F32,
+            )
+            for beam in range(beams)
+        ]
+        stats = jnp.where(lane == row % group, peak, 0.0)
+        stats += jnp.where(lane == group + row % group, total, 0.0)
+        stats = jnp.sum(stats.reshape(beams, group, HEAD_DIM), axis=1)
+        high = stats.astype(BF16).astype(F32)
+        middle = (stats - high).astype(BF16).astype(F32)
+        low = stats - high - middle
+        block = jnp.concatenate(values + [high, middle, low, jnp.zeros_like(low)], axis=0)
+        out_ref[head if earlier else i] = block.astype(BF16)
+    if earlier:
+        done = [(ref, i) for ref in before for i in range(ref.shape[0])]
+        for slot, (ref, i) in zip(earlier, done):
+            out_ref[place[0] ^ slot] = ref[i]
+
+
+def attend(place, length, queries, keys, values, slots, earlier=(), before=()):
+    count, rows, _ = queries.shape
+    beams, positions, _ = keys.shape
+    out = shape(count + len(earlier), rows + 4 * beams, HEAD_DIM, dtype=BF16)
+    return pl.pallas_call(
+        lambda *refs: attend_kernel(slots, earlier, *refs),
+        in_specs=[scalar()] * 2 + [whole()] * (3 + len(before)),
+        out_specs=whole(),
+        out_shape=out,
+        compiler_params=params(),
+        cost_estimate=pl.CostEstimate(
+            flops=4 * rows * count * positions * HEAD_DIM,
+            bytes_accessed=4 * beams * positions * HEAD_DIM * count,
+            transcendentals=rows * count * positions,
+        ),
+        name="attend",
+    )(place, length, queries, keys, values, *before)
+
+
+def combine_kernel(parts_ref, q_ref, k_ref, v_ref, out_ref, joined):
+    ranks = parts_ref.shape[0]
+    beams, group, _ = joined.shape
+    rows = beams * group
+
+    def by_row(v):
+        return jnp.broadcast_to(v[:, None, :], (beams, group, HEAD_DIM)).reshape(rows, HEAD_DIM)
+
+    head = iota((rows, HEAD_DIM), 0) % group
+    lane = iota((rows, HEAD_DIM), 1)
+    score = jnp.sum(q_ref[0].astype(F32) * by_row(k_ref[...]), axis=1, keepdims=True) * (
+        1.0 / HEAD_DIM**0.5
+    )
+    peaks, totals, weighted = [], [], []
+    top = score
+    for s in range(ranks):
+        block = parts_ref[s].astype(F32)
+        tail = by_row(
+            block[rows : rows + beams]
+            + block[rows + beams : rows + 2 * beams]
+            + block[rows + 2 * beams : rows + 3 * beams]
+        )
+        peak = jnp.sum(jnp.where(lane == head, tail, 0.0), axis=1, keepdims=True)
+        total = jnp.sum(jnp.where(lane == group + head, tail, 0.0), axis=1, keepdims=True)
+        top = jnp.maximum(top, peak)
+        peaks.append(peak)
+        totals.append(total)
+        weighted.append(block[:rows])
+    new = jnp.exp(score - top)
+    everything = new
+    result = new.astype(BF16).astype(F32) * by_row(v_ref[...])
+    for peak, total, block in zip(peaks, totals, weighted):
+        factor = jnp.exp(peak - top)
+        everything += total * factor
+        result += block * factor
+    joined[...] = (result / everything).reshape(joined.shape)
+    for g in range(group):
+        out_ref[:, g * HEAD_DIM : (g + 1) * HEAD_DIM] = joined[:, g, :].astype(BF16)
+
+
+def combine(parts, query, key_new, value_new):
+    beams = key_new.shape[0]
+    group = query.shape[1] // beams
+    return pl.pallas_call(
+        combine_kernel,
+        in_specs=[whole()] * 4,
+        out_specs=whole(),
+        out_shape=shape(beams, group * HEAD_DIM, dtype=BF16),
+        scratch_shapes=[pltpu.VMEM((beams, group, HEAD_DIM), F32)],
+        compiler_params=params(),
+        name="combine",
+    )(parts, query, key_new, value_new)
+
+
+def output_kernel(parity, place, x_ref, w_ref, out, w_buf, sems):
+    count, _, width = w_buf.shape
+    copies = [
+        start_columns(w_ref, ((2 * s + parity) ^ place[0]) * width, w_buf.at[s], sems.at[s])
+        for s in range(count)
+    ]
+    for s in range(count):
+        for copy in copies[s]:
+            copy.wait()
+        total = jnp.dot(x_ref[...], w_buf[s], preferred_element_type=F32)
+        out[s] = total.astype(out.dtype)
+
+
+def output(place, x, weight, ranks, parity, dtype):
+    beams, depth = x.shape
+    width = weight.shape[1] // ranks
+    half = ranks // 2
+    return pl.pallas_call(
+        lambda *refs: output_kernel(parity, *refs),
+        in_specs=[scalar(), whole(), big()],
+        out_specs=whole(),
+        out_shape=shape(half, beams, width, dtype=dtype),
+        scratch_shapes=[
+            pltpu.VMEM((half, depth, width), BF16),
+            pltpu.SemaphoreType.DMA((half, CHUNKS)),
+        ],
+        compiler_params=params(),
+        cost_estimate=pl.CostEstimate(
+            flops=beams * weight.size, bytes_accessed=weight.size, transcendentals=0
+        ),
+        name="output_sent" if parity else "output_kept",
+    )(place, x, weight)
+
+
+def residual_kernel(x_ref, kept_ref, came_ref, out_ref):
+    total = kept_ref[0] + came_ref[0].astype(F32)
+    out_ref[...] = (x_ref[...].astype(F32) + total).astype(BF16)
+
+
+def residual(x, kept, came):
+    return pl.pallas_call(
+        residual_kernel,
+        in_specs=[whole()] * 3,
+        out_specs=whole(),
+        out_shape=jax.ShapeDtypeStruct(x.shape, BF16),
+        compiler_params=params(),
+        name="residual",
+    )(x, kept, came)
+
+
+def swapped(x):
+    return lax.ppermute(x, "bank", [(0, 1), (1, 0)])
+
+
+def hop(x, bit):
+    ranks = lax.axis_size("tensor")
+    return lax.ppermute(x, "tensor", [(i, i ^ bit) for i in range(ranks)])
+
+
+def beside(came, array, sent):
+    array, _ = lax.optimization_barrier((array, sent))
+    return lax.optimization_barrier((came, fetch(array)))
+
+
+def matched_body(
+    normed_hidden_input,
+    beam_adapter_index,
+    beam_cache_length,
+    query_weight,
+    keyvalue_weight,
+    output_weight,
+    lowrank_down_factors,
+    lowrank_up_factors,
+    paged_key_cache,
+    paged_value_cache,
+):
+    x = normed_hidden_input
+    ranks = lax.axis_size("tensor")
+    place = lax.axis_index("tensor").astype(jnp.int32).reshape(1)
+    bank = lax.axis_index("bank").astype(jnp.int32).reshape(1)
+    index = (beam_adapter_index, swapped(beam_adapter_index))
+    x_other = swapped(x)
+    half = HEAD_DIM // 2
+    frequency = jnp.power(500000.0, -2.0 * jnp.arange(half, dtype=F32) / HEAD_DIM)
+    angles = beam_cache_length.astype(F32)[:, None] * frequency[None, :]
+    cosine = jnp.tile(jnp.cos(angles), (1, 2))
+    sine = jnp.sin(angles)
+    sine = jnp.concatenate([-sine, sine], axis=1)
+
+    weights = in_hbm(query_weight), in_hbm(keyvalue_weight)
+    place_x = in_hbm(x)
+    sent, inner = project(
+        place,
+        bank,
+        place_x,
+        x_other,
+        *weights,
+        ranks,
+        down=in_hbm(lowrank_down_factors.swapaxes(1, 2)),
+        index=(in_hbm(index[0]), index[1]),
+    )
+    came = hop(sent, 1)
+    (kept,) = project(place, bank, place_x, x_other, *weights, ranks, inner=inner)
+    sent, kept = halve(kept, came)
+    came, keys = beside(hop(sent, 2), paged_key_cache, sent)
+    sent, kept = halve(kept, came)
+    came, values = beside(hop(sent, 4), paged_value_cache, sent)
+    own, other = correct(bank, index, kept, came, lowrank_up_factors)
+    query, key_new, value_new = rotated(bank, own, swapped(other), cosine, sine)
+
+    def attended_part(queries, slots, **more):
+        return attend(place, beam_cache_length, queries, keys, values, slots, **more)
+
+    came = hop(query, 4)
+    done = [attended_part(query, (0,))]
+    gathered = join(query, came)
+    second = hop(gathered, 2)
+    done.append(attended_part(came, (4,)))
+    came = hop(join(gathered, second), 1)
+    done.append(attended_part(second, (2, 6)))
+    partial = attended_part(came, (1, 5, 3, 7), earlier=(0, 4, 2, 6), before=done)
+    parts = lax.all_to_all(partial, "tensor", 0, 0, tiled=True)
+    attended = combine(parts, query, key_new, value_new)
+
+    weight = in_hbm(output_weight)
+    came = hop(output(place, attended, weight, ranks, 1, BF16), 1)
+    kept = output(place, attended, weight, ranks, 0, F32)
+    sent, kept = halve(kept, came)
+    sent, kept = halve(kept, hop(sent, 2))
+    return residual(x, kept, hop(sent, 4))
 
 
 def joined(x, axis, combine):
@@ -158,8 +716,9 @@
 
 
 def solution(mesh):
+    matched = mesh.shape["tensor"] == 8 and mesh.shape["bank"] == 2
     return jax.shard_map(
-        body,
+        matched_body if matched else body,
         mesh=mesh,
         in_specs=(
             P(("groups", "bank"), "tensor"),

time: 256 us -> 79.9 us (0.31)
  blocking collectives: 115 us -> 10.2 us
  waiting for transfers between devices: 77.2 us -> 19.3 us
  Pallas kernels: 0 us -> 27.4 us
  matrix products: 26.9 us -> 0 us
  between operations: 15.3 us -> 0.15 us
  other arithmetic: 13.4 us -> 0.2 us
  starting transfers between devices: 0.17 us -> 12 us
  local copies, waits for them, and re-layouts: 7.45 us -> 10.5 us
    all_gather x3 -> x0, blocking collectives: 93.2 us -> none  [the longest x2 62.4 us: joined(): everything = jax.tree.map(lambda part: lax.all_gather(part, axis), x)]
    reduce_scatter x1 -> x0, waiting for transfers between devices: 60.6 us -> none  [body(): lax.psum_scatter(lax.dot_general(output_weight, attended_cols, (((0,), (1...]
    pallas_call x0 -> x20, Pallas kernels: none -> 27.4 us  [the longest x2 7.79 us: output(): pl.pallas_call(lambda *refs: output_kernel(parity, *refs), in_specs=[scal...]
    dot_general x8 -> x0, matrix products: 26.9 us -> none  [the longest x1 8.79 us: body(): jnp.dot(normed_hidden_input, query_weight, preferred_element_type=jnp.flo...]
    psum x1 -> x0, blocking collectives: 21.6 us -> none  [body(): inner_total = lax.psum(inner_part, 'tensor').astype(jnp.bfloat16)]
    ppermute x0 -> x12, waiting for transfers between devices: none -> 19.3 us  [the longest x9 17 us: hop(): return lax.ppermute(x, 'tensor', [(i, i ^ bit) for i in range(ranks)])]
    ppermute x0 -> x12, starting transfers between devices: none -> 12 us  [the longest x9 11.4 us: hop(): return lax.ppermute(x, 'tensor', [(i, i ^ bit) for i in range(ranks)])]
    psum x1 -> x0, waiting for transfers between devices: 10.4 us -> none  [body(): query_total, keyval = lax.psum((query_part, keyval_part), 'tensor')]
  transfers between devices with their start and end apart: 5 -> 12, of which waited for: 3 -> 8; matrix products, arithmetic and copies ran while one was open for 8% -> 0% of each run, Pallas kernels for 0% -> 19%
where the time goes in v4:
time: 79.9 us; the launch traced here: 79.6 us
  Pallas kernels  27.4 us (34%)
  waiting for transfers between devices  19.3 us (24%)
  starting transfers between devices  12 us (15%)
  local copies, waits for them, and re-layouts  10.5 us (13%)
  blocking collectives  10.2 us (13%)
    ppermute x9, waiting for transfers between devices, hop(): return lax.ppermute(x, 'tensor', [(i, i ^ bit) for i in range(ranks)])  17 us
    ppermute x9, starting transfers between devices, hop(): return lax.ppermute(x, 'tensor', [(i, i ^ bit) for i in range(ranks)])  11.4 us
    unnamed x20, local copies, waits for them, and re-layouts  10.4 us
    all_to_all x1, blocking collectives, matched_body(): parts = lax.all_to_all(partial, 'tensor', 0, 0, tiled=True)  10.2 us
    pallas_call x2, Pallas kernels, output(): pl.pallas_call(lambda *refs: output_kernel(parity, *refs), in_specs=[scal...  7.79 us
    pallas_call x2, Pallas kernels, project(): pl.pallas_call(lambda *refs: project_kernel(int(first), ranks, *refs), in...  7.65 us
    pallas_call x4, Pallas kernels, attend(): pl.pallas_call(lambda *refs: attend_kernel(slots, earlier, *refs), in_spe...  5.4 us
    pallas_call x2, Pallas kernels, fetch(): pl.pallas_call(fetch_kernel, in_specs=[big()], out_specs=whole(), out_sha...  4.56 us
  transfers between devices with their start and end apart: 12, of which 8 were waited for; matrix products, arithmetic and copies ran while one was open for 0% of the time, Pallas kernels for 19%

profile of v4, /device:TPU:0, one launch (start us, length us, event | category | flops | bytes accessed | tf_op | source)
XLA Modules:
  0.0 79.6 jit_solution(11084000383441508945)
XLA Ops:
  0.0 0.5 collective-permute-start.1
  0.5 0.1 collective-permute-start
  0.5 1.2 %collective-permute-done.refs_3_.other_index = s32[8]{0:T(128)S(1)} collective-permute-done((s32[8]{0:T(128)}, s32[8]{0:T(128)S(1)}, u32[]{:S(2)}, u32[]{:S(2)}) %collective-permute-start) | collective-permute-done | bytes 64 | tf_op jit(solution)/shard_map/ppermute | solution.py:486
  1.7 0.0 collective-permute-done.1.refs_5_.refs_3_
  1.7 0.0 copy-start.8
  1.7 4.1 %project_sent.1 = (f32[4,16,768]{2,1,0:T(8,128)S(1)}, f32[16,128]{1,0:T(8,128)S(1)}) custom-call(s32[1]{0:T(128)} %bitcast.refs_0_, s32[1]{0:T(128)} %bitcast.1.refs_1_.bank, s32[8]{0:T(128)} %own_index.1, s32[8]{0:T(128)S(1)} %collective-permute-done.refs_3_.other_index, bf16[8,1024]{1,0:T(8,128)(2,1)} %x_ref.1, ...), custom_call_target="tpu_custom_call" | custom-call | flops 83886080 | bytes 5242880 | tf_op jit(solution)/shard_map/project_sent/pallas_call | solution.py:149
  5.8 2.8 %collective-permute-start.2 = (f32[4,16,768]{2,1,0:T(8,128)S(1)}, f32[4,16,768]{2,1,0:T(8,128)S(1)}, u32[]{:S(2)}, u32[]{:S(2)}) collective-permute-start(f32[4,16,768]{2,1,0:T(8,128)S(1)} %get-tuple-element.27), channel_id=1, source_target_pairs={{0,2},{2,0},{4,6},{6,4},{8,10},{10,8},{12,14},{14,12},{1,3},{3,1},... | collective-permute-start | bytes 589832 | tf_op jit(solution)/shard_map/ppermute | solution.py:491
  8.6 0.0 copy-done.8
  8.6 3.5 %project_kept.1.kept_ref = f32[4,16,768]{2,1,0:T(8,128)S(1)} custom-call(s32[1]{0:T(128)} %bitcast.refs_0_, s32[1]{0:T(128)} %bitcast.1.refs_1_.bank, bf16[8,1024]{1,0:T(8,128)(2,1)} %x_ref.1, bf16[8,1024]{1,0:T(8,128)(2,1)S(1)} %collective-permute-done.1.refs_5_.refs_3_, bf16[1024,8192]{1,0:T(8,128)(2,1)} %refs_4_.3, bf16[1024,2048]{1,0:T(8,128)(2,1)} %refs_5_.1, ...), custom_call_target="tpu_custom_call" | custom-call | flops 83886080 | bytes 5242880 | tf_op jit(solution)/shard_map/project_kept/pallas_call | solution.py:149
  12.2 1.8 %collective-permute-done.2.came_ref = f32[4,16,768]{2,1,0:T(8,128)S(1)} collective-permute-done((f32[4,16,768]{2,1,0:T(8,128)S(1)}, f32[4,16,768]{2,1,0:T(8,128)S(1)}, u32[]{:S(2)}, u32[]{:S(2)}) %collective-permute-start.2) | collective-permute-done | bytes 196640 | tf_op jit(solution)/shard_map/ppermute | solution.py:491
  14.0 1.9 %collective-permute-start.3 = (f32[2,16,768]{2,1,0:T(8,128)S(1)}, f32[2,16,768]{2,1,0:T(8,128)S(1)}, u32[]{:S(2)}, u32[]{:S(2)}) collective-permute-start(f32[2,16,768]{2,1,0:T(8,128)S(1)} %get-tuple-element.29), channel_id=1, source_target_pairs={{0,4},{2,6},{4,0},{6,2},{8,12},{10,14},{12,8},{14,10},{1,5},{3,7},... | collective-permute-start | bytes 294920 | tf_op jit(solution)/shard_map/ppermute | solution.py:491
  15.9 2.2 %fetch.2.refs_3_ = bf16[8,256,1024]{2,1,0:T(8,128)(2,1)S(1)} custom-call(bf16[8,256,1024]{2,1,0:T(8,128)(2,1)} %ref), custom_call_target="tpu_custom_call" | custom-call | bytes 4194304 | tf_op jit(solution)/shard_map/fetch/pallas_call | solution.py:295
  18.1 0.0 copy-start
  18.1 1.9 %copy-done = bf16[8,256,1024]{2,1,0:T(8,128)(2,1)} copy-done((bf16[8,256,1024]{2,1,0:T(8,128)(2,1)}, bf16[8,256,1024]{2,1,0:T(8,128)(2,1)S(1)}, u32[]{:S(2)}) %copy-start) | copy-done | bytes 4194328
  20.1 0.0 collective-permute-done.3.came_ref
  20.1 2.7 %collective-permute-start.4 = (f32[1,16,768]{2,1,0:T(8,128)S(1)}, f32[1,16,768]{2,1,0:T(8,128)S(1)}, u32[]{:S(2)}, u32[]{:S(2)}) collective-permute-start(f32[1,16,768]{2,1,0:T(8,128)S(1)} %get-tuple-element.33), channel_id=1, source_target_pairs={{0,8},{2,10},{4,12},{6,14},{8,0},{10,2},{12,4},{14,6},{1,9},{3,11}... | collective-permute-start | bytes 147464 | tf_op jit(solution)/shard_map/ppermute | solution.py:491
  22.7 0.1 fusion
  22.9 0.0 copy-start.6
  22.9 0.0 copy-start.9
  22.9 2.4 %fetch.3.refs_4_ = bf16[8,256,1024]{2,1,0:T(8,128)(2,1)S(1)} custom-call(bf16[8,256,1024]{2,1,0:T(8,128)(2,1)} %ref.1), custom_call_target="tpu_custom_call" | custom-call | bytes 4194304 | tf_op jit(solution)/shard_map/fetch/pallas_call | solution.py:295
  25.2 0.0 copy-start.3
  25.3 2.0 %copy-done.3 = bf16[8,256,1024]{2,1,0:T(8,128)(2,1)} copy-done((bf16[8,256,1024]{2,1,0:T(8,128)(2,1)}, bf16[8,256,1024]{2,1,0:T(8,128)(2,1)S(1)}, u32[]{:S(2)}) %copy-start.3) | copy-done | bytes 4194328
  27.3 0.0 collective-permute-done.4.came_ref
  27.3 0.0 copy-done.6
  27.3 0.0 copy-done.9
  27.3 0.9 %correct.1 = (f32[8,1152]{1,0:T(8,128)S(1)}, f32[8,1152]{1,0:T(8,128)S(1)}) custom-call(s32[1]{0:T(128)} %bitcast.1.refs_1_.bank, s32[8]{0:T(128)S(1)} %copy-done.9, s32[8]{0:T(128)S(1)} %collective-permute-done.refs_3_.other_index, f32[1,16,768]{2,1,0:T(8,128)S(1)} %get-tuple-element.32.kept_ref, f32[1,16,768]{2,1,0:T(8,128)S(1)} %collective-permute-done.4.came_ref, ...), custom_call_target="tpu_custom_call" | custom-call | flops 33554432 | bytes 2097152 | tf_op jit(solution)/shard_map/correct/pallas_call | solution.py:214
  28.2 0.0 collective-permute-start.5
  28.2 0.1 pad_maximum_fusion.sin_ref
  28.3 0.1 tile.10.cos_ref
  28.4 1.1 %collective-permute-done.5.came_ref = f32[8,1152]{1,0:T(8,128)S(1)} collective-permute-done((f32[8,1152]{1,0:T(8,128)S(1)}, f32[8,1152]{1,0:T(8,128)S(1)}, u32[]{:S(2)}, u32[]{:S(2)}) %collective-permute-start.5) | collective-permute-done | bytes 36896 | tf_op jit(solution)/shard_map/ppermute | solution.py:486
  29.4 0.1 rotate.1
  29.5 0.5 collective-permute-start.6
  30.1 4.2 %collective-permute-done.6.second_ref.refs_2_ = bf16[1,64,128]{2,1,0:T(8,128)(2,1)S(1)} collective-permute-done((bf16[1,64,128]{2,1,0:T(8,128)(2,1)S(1)}, bf16[1,64,128]{2,1,0:T(8,128)(2,1)S(1)}, u32[]{:S(2)}, u32[]{:S(2)}) %collective-permute-start.6) | collective-permute-done | bytes 16416 | tf_op jit(solution)/shard_map/ppermute | solution.py:491
  34.3 0.4 collective-permute-start.7
  34.7 3.5 %collective-permute-done.7.second_ref.refs_2_ = bf16[2,64,128]{2,1,0:T(8,128)(2,1)S(1)} collective-permute-done((bf16[2,64,128]{2,1,0:T(8,128)(2,1)S(1)}, bf16[2,64,128]{2,1,0:T(8,128)(2,1)S(1)}, u32[]{:S(2)}, u32[]{:S(2)}) %collective-permute-start.7) | collective-permute-done | bytes 32800 | tf_op jit(solution)/shard_map/ppermute | solution.py:491
  38.2 1.5 %collective-permute-start.8 = (bf16[4,64,128]{2,1,0:T(8,128)(2,1)S(1)}, bf16[4,64,128]{2,1,0:T(8,128)(2,1)S(1)}, u32[]{:S(2)}, u32[]{:S(2)}) collective-permute-start(bf16[4,64,128]{2,1,0:T(8,128)(2,1)S(1)} %join.3), channel_id=1, source_target_pairs={{0,2},{2,0},{4,6},{6,4},{8,10},{10,8},{12,14},{14,12},{1,3},{3,1},... | collective-permute-start | bytes 196616 | tf_op jit(solution)/shard_map/ppermute | solution.py:491
  39.7 0.0 copy-start.1
  39.7 2.2 %copy-done.1 = bf16[8,256,1024]{2,1,0:T(8,128)(2,1)S(1)} copy-done((bf16[8,256,1024]{2,1,0:T(8,128)(2,1)S(1)}, bf16[8,256,1024]{2,1,0:T(8,128)(2,1)}, u32[]{:S(2)}) %copy-start.1) | copy-done | bytes 4194328
  41.9 0.0 copy-start.4
  41.9 2.2 %copy-done.4 = bf16[8,256,1024]{2,1,0:T(8,128)(2,1)S(1)} copy-done((bf16[8,256,1024]{2,1,0:T(8,128)(2,1)S(1)}, bf16[8,256,1024]{2,1,0:T(8,128)(2,1)}, u32[]{:S(2)}) %copy-start.4) | copy-done | bytes 4194328
  44.1 1.0 %attend.4.refs_5_ = bf16[1,96,128]{2,1,0:T(8,128)(2,1)S(1)} custom-call(s32[1]{0:T(128)} %bitcast.refs_0_, s32[8]{0:T(128)S(1)} %copy-done.8, bf16[1,64,128]{2,1,0:T(8,128)(2,1)S(1)} %get-tuple-element.38.first_ref.refs_2_.q_ref, bf16[8,256,1024]{2,1,0:T(8,128)(2,1)S(1)} %copy-done.1, bf16[8,256,1024]{2,1,0:T(8,128)(2,1)S(1)} %copy-done.4), custom_call_target="tpu_custom_call" | custom-call | flops 8388608 | bytes 1048576 | tf_op jit(solution)/shard_map/attend/pallas_call | solution.py:366
  45.1 0.0 copy-start.2
  45.1 1.0 %attend.5.refs_6_ = bf16[1,96,128]{2,1,0:T(8,128)(2,1)S(1)} custom-call(s32[1]{0:T(128)} %bitcast.refs_0_, s32[8]{0:T(128)S(1)} %copy-done.8, bf16[1,64,128]{2,1,0:T(8,128)(2,1)S(1)} %collective-permute-done.6.second_ref.refs_2_, bf16[8,256,1024]{2,1,0:T(8,128)(2,1)S(1)} %copy-done.1, bf16[8,256,1024]{2,1,0:T(8,128)(2,1)S(1)} %copy-done.4), custom_call_target="tpu_custom_call" | custom-call | flops 8388608 | bytes 1048576 | tf_op jit(solution)/shard_map/attend/pallas_call | solution.py:366
  46.1 1.2 %copy-done.2 = bf16[8,256,1024]{2,1,0:T(8,128)(2,1)S(1)} copy-done((bf16[8,256,1024]{2,1,0:T(8,128)(2,1)S(1)}, bf16[8,256,1024]{2,1,0:T(8,128)(2,1)}, u32[]{:S(2)}) %copy-start.2) | copy-done | bytes 4194328
  47.3 0.0 copy-start.5
  47.3 1.3 %attend.6.refs_7_ = bf16[2,96,128]{2,1,0:T(8,128)(2,1)S(1)} custom-call(s32[1]{0:T(128)} %bitcast.refs_0_, s32[8]{0:T(128)S(1)} %copy-done.8, bf16[2,64,128]{2,1,0:T(8,128)(2,1)S(1)} %collective-permute-done.7.second_ref.refs_2_, bf16[8,256,1024]{2,1,0:T(8,128)(2,1)S(1)} %copy-done.2, bf16[8,256,1024]{2,1,0:T(8,128)(2,1)S(1)} %copy-done.4), custom_call_target="tpu_custom_call" | custom-call | flops 16777216 | bytes 2097152 | tf_op jit(solution)/shard_map/attend/pallas_call | solution.py:366
  48.7 0.0 collective-permute-done.8.refs_2_
  48.7 0.8 %copy-done.5 = bf16[8,256,1024]{2,1,0:T(8,128)(2,1)S(1)} copy-done((bf16[8,256,1024]{2,1,0:T(8,128)(2,1)S(1)}, bf16[8,256,1024]{2,1,0:T(8,128)(2,1)}, u32[]{:S(2)}) %copy-start.5) | copy-done | bytes 4194328
  49.5 2.0 %attend.7 = bf16[8,96,128]{2,1,0:T(8,128)(2,1)S(1)} custom-call(s32[1]{0:T(128)} %bitcast.refs_0_, s32[8]{0:T(128)S(1)} %copy-done.8, bf16[4,64,128]{2,1,0:T(8,128)(2,1)S(1)} %collective-permute-done.8.refs_2_, bf16[8,256,1024]{2,1,0:T(8,128)(2,1)S(1)} %copy-done.2, bf16[8,256,1024]{2,1,0:T(8,128)(2,1)S(1)} %copy-done.5, ...), custom_call_target="tpu_custom_call" | custom-call | flops 33554432 | bytes 4194304 | tf_op jit(solution)/shard_map/attend/pallas_call | solution.py:366
  51.6 10.2 %all_to_all.5.parts_ref = bf16[8,96,128]{2,1,0:T(8,128)(2,1)S(1)} all-to-all(bf16[8,96,128]{2,1,0:T(8,128)(2,1)S(1)} %attend.7), channel_id=1, replica_groups=mesh['groups'=2,'tensor'=8,'bank'=2] {'tensor'}, dimensions={0} | all-to-all | bytes 393216 | tf_op jit(solution)/shard_map/all_to_all | solution.py:556
  61.7 0.3 combine.1.refs_1_
  62.0 3.9 %output_sent.1 = bf16[4,8,1024]{2,1,0:T(8,128)(2,1)S(1)} custom-call(s32[1]{0:T(128)} %bitcast.refs_0_, bf16[8,1024]{1,0:T(8,128)(2,1)S(1)} %combine.1.refs_1_, bf16[1024,8192]{1,0:T(8,128)(2,1)} %refs_2_.7), custom_call_target="tpu_custom_call" | custom-call | flops 67108864 | bytes 8388608 | tf_op jit(solution)/shard_map/output_sent/pallas_call | solution.py:452
  65.9 0.0 copy-start.7
  66.0 0.1 collective-permute-start.9
  66.1 3.9 %output_kept.1.kept_ref = f32[4,8,1024]{2,1,0:T(8,128)S(1)} custom-call(s32[1]{0:T(128)} %bitcast.refs_0_, bf16[8,1024]{1,0:T(8,128)(2,1)S(1)} %combine.1.refs_1_, bf16[1024,8192]{1,0:T(8,128)(2,1)} %refs_2_.7), custom_call_target="tpu_custom_call" | custom-call | flops 67108864 | bytes 8388608 | tf_op jit(solution)/shard_map/output_kept/pallas_call | solution.py:452
  70.0 0.3 collective-permute-done.9.came_ref
  70.3 1.1 %collective-permute-start.10 = (bf16[2,8,1024]{2,1,0:T(8,128)(2,1)S(1)}, bf16[2,8,1024]{2,1,0:T(8,128)(2,1)S(1)}, u32[]{:S(2)}, u32[]{:S(2)}) collective-permute-start(bf16[2,8,1024]{2,1,0:T(8,128)(2,1)S(1)} %get-tuple-element.44), channel_id=1, source_target_pairs={{0,4},{2,6},{4,0},{6,2},{8,12},{10,14},{12,8},{14,10},{1,5},{3,7},... | collective-permute-start | bytes 98312 | tf_op jit(solution)/shard_map/ppermute | solution.py:491
  71.4 2.9 %collective-permute-done.10.came_ref = bf16[2,8,1024]{2,1,0:T(8,128)(2,1)S(1)} collective-permute-done((bf16[2,8,1024]{2,1,0:T(8,128)(2,1)S(1)}, bf16[2,8,1024]{2,1,0:T(8,128)(2,1)S(1)}, u32[]{:S(2)}, u32[]{:S(2)}) %collective-permute-start.10) | collective-permute-done | bytes 32800 | tf_op jit(solution)/shard_map/ppermute | solution.py:491
  74.3 0.5 collective-permute-start.11
  74.8 4.2 %collective-permute-done.11.came_ref = bf16[1,8,1024]{2,1,0:T(8,128)(2,1)S(1)} collective-permute-done((bf16[1,8,1024]{2,1,0:T(8,128)(2,1)S(1)}, bf16[1,8,1024]{2,1,0:T(8,128)(2,1)S(1)}, u32[]{:S(2)}, u32[]{:S(2)}) %collective-permute-start.11) | collective-permute-done | bytes 16416 | tf_op jit(solution)/shard_map/ppermute | solution.py:491
  79.0 0.0 copy-done.7
  79.0 0.6 residual.1
  (9 shorter events, 0.1 us)
Async XLA Ops:
  0.0 1.7 %collective-permute-start.1 = (bf16[8,1024]{1,0:T(8,128)(2,1)}, bf16[8,1024]{1,0:T(8,128)(2,1)S(1)}, u32[]{:S(2)}, u32[]{:S(2)}) collective-permute-start(bf16[8,1024]{1,0:T(8,128)(2,1)} %x_ref.1), channel_id=1, source_target_pairs={{0,1},{1,0},{2,3},{3,2},{4,5},{5,4},{6,7},{7,6},{8,9},{9,8},{10,11... | collective-permute-start | bytes 49160 | tf_op jit(solution)/shard_map/ppermute | solution.py:486
  0.5 1.3 %collective-permute-start = (s32[8]{0:T(128)}, s32[8]{0:T(128)S(1)}, u32[]{:S(2)}, u32[]{:S(2)}) collective-permute-start(s32[8]{0:T(128)} %own_index.1), channel_id=1, source_target_pairs={{0,1},{1,0},{2,3},{3,2},{4,5},{5,4},{6,7},{7,6},{8,9},{9,8},{10,11... | collective-permute-start | bytes 104 | tf_op jit(solution)/shard_map/ppermute | solution.py:486
  1.7 6.9 %copy-start.8 = (s32[8]{0:T(128)S(1)}, s32[8]{0:T(128)}, u32[]{:S(2)}) copy-start(s32[8]{0:T(128)} %refs_1_.7) | copy-start | bytes 100
  5.8 8.2 %collective-permute-start.2 = (f32[4,16,768]{2,1,0:T(8,128)S(1)}, f32[4,16,768]{2,1,0:T(8,128)S(1)}, u32[]{:S(2)}, u32[]{:S(2)}) collective-permute-start(f32[4,16,768]{2,1,0:T(8,128)S(1)} %get-tuple-element.27), channel_id=1, source_target_pairs={{0,2},{2,0},{4,6},{6,4},{8,10},{10,8},{12,14},{14,12},{1,3},{3,1},... | collective-permute-start | bytes 589832 | tf_op jit(solution)/shard_map/ppermute | solution.py:491
  14.0 6.1 %collective-permute-start.3 = (f32[2,16,768]{2,1,0:T(8,128)S(1)}, f32[2,16,768]{2,1,0:T(8,128)S(1)}, u32[]{:S(2)}, u32[]{:S(2)}) collective-permute-start(f32[2,16,768]{2,1,0:T(8,128)S(1)} %get-tuple-element.29), channel_id=1, source_target_pairs={{0,4},{2,6},{4,0},{6,2},{8,12},{10,14},{12,8},{14,10},{1,5},{3,7},... | collective-permute-start | bytes 294920 | tf_op jit(solution)/shard_map/ppermute | solution.py:491
  18.1 2.0 %copy-start = (bf16[8,256,1024]{2,1,0:T(8,128)(2,1)}, bf16[8,256,1024]{2,1,0:T(8,128)(2,1)S(1)}, u32[]{:S(2)}) copy-start(bf16[8,256,1024]{2,1,0:T(8,128)(2,1)S(1)} %fetch.2.refs_3_) | copy-start | bytes 12582916
  20.1 7.2 %collective-permute-start.4 = (f32[1,16,768]{2,1,0:T(8,128)S(1)}, f32[1,16,768]{2,1,0:T(8,128)S(1)}, u32[]{:S(2)}, u32[]{:S(2)}) collective-permute-start(f32[1,16,768]{2,1,0:T(8,128)S(1)} %get-tuple-element.33), channel_id=1, source_target_pairs={{0,8},{2,10},{4,12},{6,14},{8,0},{10,2},{12,4},{14,6},{1,9},{3,11}... | collective-permute-start | bytes 147464 | tf_op jit(solution)/shard_map/ppermute | solution.py:491
  22.9 4.4 %copy-start.6 = (bf16[16,64,1024]{2,1,0:T(8,128)(2,1)S(1)}, bf16[16,64,1024]{2,1,0:T(8,128)(2,1)}, u32[]{:S(2)}) copy-start(bf16[16,64,1024]{2,1,0:T(8,128)(2,1)} %up_ref.1) | copy-start | bytes 6291460
  22.9 4.4 %copy-start.9 = (s32[8]{0:T(128)S(1)}, s32[8]{0:T(128)}, u32[]{:S(2)}) copy-start(s32[8]{0:T(128)} %own_index.1) | copy-start | bytes 100
  25.2 2.0 %copy-start.3 = (bf16[8,256,1024]{2,1,0:T(8,128)(2,1)}, bf16[8,256,1024]{2,1,0:T(8,128)(2,1)S(1)}, u32[]{:S(2)}) copy-start(bf16[8,256,1024]{2,1,0:T(8,128)(2,1)S(1)} %fetch.3.refs_4_) | copy-start | bytes 12582916
  28.2 1.2 %collective-permute-start.5 = (f32[8,1152]{1,0:T(8,128)S(1)}, f32[8,1152]{1,0:T(8,128)S(1)}, u32[]{:S(2)}, u32[]{:S(2)}) collective-permute-start(f32[8,1152]{1,0:T(8,128)S(1)} %get-tuple-element.37), channel_id=1, source_target_pairs={{0,1},{1,0},{2,3},{3,2},{4,5},{5,4},{6,7},{7,6},{8,9},{9,8},{10,11... | collective-permute-start | bytes 110600 | tf_op jit(solution)/shard_map/ppermute | solution.py:486
  29.5 4.8 %collective-permute-start.6 = (bf16[1,64,128]{2,1,0:T(8,128)(2,1)S(1)}, bf16[1,64,128]{2,1,0:T(8,128)(2,1)S(1)}, u32[]{:S(2)}, u32[]{:S(2)}) collective-permute-start(bf16[1,64,128]{2,1,0:T(8,128)(2,1)S(1)} %get-tuple-element.38.first_ref.refs_2_.q_ref), channel_id=1, source_target_pairs={{0,8},{2,10},{4,12},{6,14},{8,0},{10,2},{12,4},{14,6},{1,9},{3,11}... | collective-permute-start | bytes 49160 | tf_op jit(solution)/shard_map/ppermute | solution.py:491
  34.3 3.9 %collective-permute-start.7 = (bf16[2,64,128]{2,1,0:T(8,128)(2,1)S(1)}, bf16[2,64,128]{2,1,0:T(8,128)(2,1)S(1)}, u32[]{:S(2)}, u32[]{:S(2)}) collective-permute-start(bf16[2,64,128]{2,1,0:T(8,128)(2,1)S(1)} %join.2.first_ref), channel_id=1, source_target_pairs={{0,4},{2,6},{4,0},{6,2},{8,12},{10,14},{12,8},{14,10},{1,5},{3,7},... | collective-permute-start | bytes 98312 | tf_op jit(solution)/shard_map/ppermute | solution.py:491
  38.2 10.4 %collective-permute-start.8 = (bf16[4,64,128]{2,1,0:T(8,128)(2,1)S(1)}, bf16[4,64,128]{2,1,0:T(8,128)(2,1)S(1)}, u32[]{:S(2)}, u32[]{:S(2)}) collective-permute-start(bf16[4,64,128]{2,1,0:T(8,128)(2,1)S(1)} %join.3), channel_id=1, source_target_pairs={{0,2},{2,0},{4,6},{6,4},{8,10},{10,8},{12,14},{14,12},{1,3},{3,1},... | collective-permute-start | bytes 196616 | tf_op jit(solution)/shard_map/ppermute | solution.py:491
  39.7 2.2 %copy-start.1 = (bf16[8,256,1024]{2,1,0:T(8,128)(2,1)S(1)}, bf16[8,256,1024]{2,1,0:T(8,128)(2,1)}, u32[]{:S(2)}) copy-start(bf16[8,256,1024]{2,1,0:T(8,128)(2,1)} %copy-done) | copy-start | bytes 12582916
  41.9 2.2 %copy-start.4 = (bf16[8,256,1024]{2,1,0:T(8,128)(2,1)S(1)}, bf16[8,256,1024]{2,1,0:T(8,128)(2,1)}, u32[]{:S(2)}) copy-start(bf16[8,256,1024]{2,1,0:T(8,128)(2,1)} %copy-done.3) | copy-start | bytes 12582916
  45.1 2.2 %copy-start.2 = (bf16[8,256,1024]{2,1,0:T(8,128)(2,1)S(1)}, bf16[8,256,1024]{2,1,0:T(8,128)(2,1)}, u32[]{:S(2)}) copy-start(bf16[8,256,1024]{2,1,0:T(8,128)(2,1)} %copy-done) | copy-start | bytes 12582916
  47.3 2.2 %copy-start.5 = (bf16[8,256,1024]{2,1,0:T(8,128)(2,1)S(1)}, bf16[8,256,1024]{2,1,0:T(8,128)(2,1)}, u32[]{:S(2)}) copy-start(bf16[8,256,1024]{2,1,0:T(8,128)(2,1)} %copy-done.3) | copy-start | bytes 12582916
  65.9 13.1 %copy-start.7 = (bf16[8,1024]{1,0:T(8,128)(2,1)S(1)}, bf16[8,1024]{1,0:T(8,128)(2,1)}, u32[]{:S(2)}) copy-start(bf16[8,1024]{1,0:T(8,128)(2,1)} %x_ref.1) | copy-start | bytes 49156
  66.0 4.3 %collective-permute-start.9 = (bf16[4,8,1024]{2,1,0:T(8,128)(2,1)S(1)}, bf16[4,8,1024]{2,1,0:T(8,128)(2,1)S(1)}, u32[]{:S(2)}, u32[]{:S(2)}) collective-permute-start(bf16[4,8,1024]{2,1,0:T(8,128)(2,1)S(1)} %output_sent.1), channel_id=1, source_target_pairs={{0,2},{2,0},{4,6},{6,4},{8,10},{10,8},{12,14},{14,12},{1,3},{3,1},... | collective-permute-start | bytes 196616 | tf_op jit(solution)/shard_map/ppermute | solution.py:491
  70.3 4.0 %collective-permute-start.10 = (bf16[2,8,1024]{2,1,0:T(8,128)(2,1)S(1)}, bf16[2,8,1024]{2,1,0:T(8,128)(2,1)S(1)}, u32[]{:S(2)}, u32[]{:S(2)}) collective-permute-start(bf16[2,8,1024]{2,1,0:T(8,128)(2,1)S(1)} %get-tuple-element.44), channel_id=1, source_target_pairs={{0,4},{2,6},{4,0},{6,2},{8,12},{10,14},{12,8},{14,10},{1,5},{3,7},... | collective-permute-start | bytes 98312 | tf_op jit(solution)/shard_map/ppermute | solution.py:491
  74.3 4.7 %collective-permute-start.11 = (bf16[1,8,1024]{2,1,0:T(8,128)(2,1)S(1)}, bf16[1,8,1024]{2,1,0:T(8,128)(2,1)S(1)}, u32[]{:S(2)}, u32[]{:S(2)}) collective-permute-start(bf16[1,8,1024]{2,1,0:T(8,128)(2,1)S(1)} %get-tuple-element.46), channel_id=1, source_target_pairs={{0,8},{2,10},{4,12},{6,14},{8,0},{10,2},{12,4},{14,6},{1,9},{3,11}... | collective-permute-start | bytes 49160 | tf_op jit(solution)/shard_map/ppermute | solution.py:491

commit v5 on v4

--- a/solution.py
+++ b/solution.py
@@ -277,39 +277,43 @@
     )(first, second)
 
 
-def fetch_kernel(ref, out, sems):
-    part = ref.shape[0] // sems.shape[0]
+def start_head(head, sources, targets, sems):
+    columns = pl.ds(pl.multiple_of(head * HEAD_DIM, HEAD_DIM), HEAD_DIM)
     copies = [
-        pltpu.make_async_copy(
-            ref.at[pl.ds(c * part, part)], out.at[pl.ds(c * part, part)], sems.at[c]
-        )
-        for c in range(sems.shape[0])
+        pltpu.make_async_copy(source.at[:, :, columns], target, sems.at[n])
+        for n, (source, target) in enumerate(zip(sources, targets))
     ]
     for copy in copies:
         copy.start()
-    for copy in copies:
-        copy.wait()
-
-
-def fetch(array):
-    return pl.pallas_call(
-        fetch_kernel,
-        in_specs=[big()],
-        out_specs=whole(),
-        out_shape=jax.ShapeDtypeStruct(array.shape, array.dtype),
-        scratch_shapes=[pltpu.SemaphoreType.DMA((4,))],
-        compiler_params=params(),
-        cost_estimate=pl.CostEstimate(
-            flops=0, bytes_accessed=2 * array.size, transcendentals=0
-        ),
-        name="fetch",
-    )(in_hbm(array))
-
-
-def attend_kernel(slots, earlier, place, length, q_ref, k_ref, v_ref, *refs):
-    before, out_ref = refs[:-1], refs[-1]
-    beams, positions, _ = k_ref.shape
+    return copies
+
+
+def attend_kernel(slots, ahead, earlier, place, length, q_ref, k_ref, v_ref, *refs):
+    before, refs = refs[: len(refs) - 1 - 2 * bool(ahead) - 3 * (not earlier)], refs[
+        len(refs) - 1 - 2 * bool(ahead) - 3 * (not earlier) :
+    ]
+    out_ref, refs = refs[0], refs[1:]
     rows = q_ref.shape[1]
+    if earlier:
+        k_buf, v_buf = k_ref, v_ref
+    else:
+        next_refs, (k_buf, v_buf, sems) = refs[:-3], refs[-3:]
+        copies = [
+            start_head(
+                place[0] ^ slot, (k_ref, v_ref), (k_buf.at[i], v_buf.at[i]), sems.at[i]
+            )
+            for i, slot in enumerate(slots)
+        ]
+        more = [
+            start_head(
+                place[0] ^ slot,
+                (k_ref, v_ref),
+                [ref.at[i] for ref in next_refs],
+                sems.at[len(slots) + i],
+            )
+            for i, slot in enumerate(ahead)
+        ]
+    _, beams, positions, _ = k_buf.shape
     group = rows // beams
     row, lane = iota((rows, positions), 0), iota((rows, positions), 1)
     limit = jnp.zeros((rows, positions), jnp.int32)
@@ -318,14 +322,14 @@
     live = place[0] * positions + lane < limit
     row, lane = iota((rows, HEAD_DIM), 0), iota((rows, HEAD_DIM), 1)
     for i, slot in enumerate(slots):
-        head = place[0] ^ slot
-        columns = pl.ds(pl.multiple_of(head * HEAD_DIM, HEAD_DIM), HEAD_DIM)
         query = q_ref[i].astype(F32)
+        if not earlier:
+            copies[i][0].wait()
         scores = jnp.concatenate(
             [
                 lax.dot_general(
                     query[beam * group : (beam + 1) * group].astype(BF16),
-                    k_ref[beam, :, columns],
+                    k_buf[i, beam],
                     (((1,), (1,)), ((), ())),
                     preferred_element_type=F32,
                 )
@@ -337,10 +341,12 @@
         peak = jnp.max(scores, axis=1, keepdims=True)
         weights = jnp.where(live, jnp.exp(scores - peak), 0.0)
         total = jnp.sum(weights, axis=1, keepdims=True)
+        if not earlier:
+            copies[i][1].wait()
         values = [
             jnp.dot(
                 weights[beam * group : (beam + 1) * group].astype(BF16),
-                v_ref[beam, :, columns],
+                v_buf[i, beam],
                 preferred_element_type=F32,
             )
             for beam in range(beams)
@@ -351,27 +357,41 @@
         high = stats.astype(BF16).astype(F32)
         middle = (stats - high).astype(BF16).astype(F32)
         low = stats - high - middle
-        block = jnp.concatenate(values + [high, middle, low, jnp.zeros_like(low)], axis=0)
-        out_ref[head if earlier else i] = block.astype(BF16)
+        tail = high + pltpu.roll(middle, 2 * group, 1) + pltpu.roll(low, 4 * group, 1)
+        block = jnp.concatenate(values + [tail, jnp.zeros_like(tail)], axis=0)
+        out_ref[place[0] ^ slot if earlier else i] = block.astype(BF16)
     if earlier:
         done = [(ref, i) for ref in before for i in range(ref.shape[0])]
         for slot, (ref, i) in zip(earlier, done):
             out_ref[place[0] ^ slot] = ref[i]
-
-
-def attend(place, length, queries, keys, values, slots, earlier=(), before=()):
+    else:
+        for pair in more:
+            for copy in pair:
+                copy.wait()
+
+
+def attend(place, length, queries, keys, values, slots, ahead=(), earlier=(), before=()):
     count, rows, _ = queries.shape
-    beams, positions, _ = keys.shape
-    out = shape(count + len(earlier), rows + 4 * beams, HEAD_DIM, dtype=BF16)
-    return pl.pallas_call(
-        lambda *refs: attend_kernel(slots, earlier, *refs),
-        in_specs=[scalar()] * 2 + [whole()] * (3 + len(before)),
-        out_specs=whole(),
+    beams, positions = keys.shape[-3:-1]
+    out = [shape(count + len(earlier), rows + 2 * beams, HEAD_DIM, dtype=BF16)]
+    out += [shape(len(ahead), beams, positions, HEAD_DIM, dtype=BF16)] * (2 * bool(ahead))
+    scratch = []
+    if not earlier:
+        scratch = [pltpu.VMEM((count, beams, positions, HEAD_DIM), BF16)] * 2
+        scratch.append(pltpu.SemaphoreType.DMA((count + len(ahead), 2)))
+    return pl.pallas_call(
+        lambda *refs: attend_kernel(slots, ahead, earlier, *refs),
+        in_specs=[scalar()] * 2
+        + [whole()]
+        + [whole() if earlier else big()] * 2
+        + [whole()] * len(before),
+        out_specs=[whole()] * len(out),
         out_shape=out,
+        scratch_shapes=scratch,
         compiler_params=params(),
         cost_estimate=pl.CostEstimate(
             flops=4 * rows * count * positions * HEAD_DIM,
-            bytes_accessed=4 * beams * positions * HEAD_DIM * count,
+            bytes_accessed=4 * beams * positions * HEAD_DIM * (count + len(ahead)),
             transcendentals=rows * count * positions,
         ),
         name="attend",
@@ -395,11 +415,10 @@
     top = score
     for s in range(ranks):
         block = parts_ref[s].astype(F32)
-        tail = by_row(
-            block[rows : rows + beams]
-            + block[rows + beams : rows + 2 * beams]
-            + block[rows + 2 * beams : rows + 3 * beams]
-        )
+        tail = block[rows : rows + beams]
+        for turn in (2, 4):
+            tail += pltpu.roll(block[rows : rows + beams], HEAD_DIM - turn * group, 1)
+        tail = by_row(tail)
         peak = jnp.sum(jnp.where(lane == head, tail, 0.0), axis=1, keepdims=True)
         total = jnp.sum(jnp.where(lane == group + head, tail, 0.0), axis=1, keepdims=True)
         top = jnp.maximum(top, peak)
@@ -489,11 +508,6 @@
 def hop(x, bit):
     ranks = lax.axis_size("tensor")
     return lax.ppermute(x, "tensor", [(i, i ^ bit) for i in range(ranks)])
-
-
-def beside(came, array, sent):
-    array, _ = lax.optimization_barrier((array, sent))
-    return lax.optimization_barrier((came, fetch(array)))
 
 
 def matched_body(
@@ -536,23 +550,29 @@
     came = hop(sent, 1)
     (kept,) = project(place, bank, place_x, x_other, *weights, ranks, inner=inner)
     sent, kept = halve(kept, came)
-    came, keys = beside(hop(sent, 2), paged_key_cache, sent)
-    sent, kept = halve(kept, came)
-    came, values = beside(hop(sent, 4), paged_value_cache, sent)
+    sent, kept = halve(kept, hop(sent, 2))
+    came = hop(sent, 4)
     own, other = correct(bank, index, kept, came, lowrank_up_factors)
     query, key_new, value_new = rotated(bank, own, swapped(other), cosine, sine)
 
-    def attended_part(queries, slots, **more):
-        return attend(place, beam_cache_length, queries, keys, values, slots, **more)
-
+    cache = in_hbm(paged_key_cache), in_hbm(paged_value_cache)
     came = hop(query, 4)
-    done = [attended_part(query, (0,))]
+    done = attend(place, beam_cache_length, query, *cache, (0,))
     gathered = join(query, came)
     second = hop(gathered, 2)
-    done.append(attended_part(came, (4,)))
+    done += attend(place, beam_cache_length, came, *cache, (4,))
     came = hop(join(gathered, second), 1)
-    done.append(attended_part(second, (2, 6)))
-    partial = attended_part(came, (1, 5, 3, 7), earlier=(0, 4, 2, 6), before=done)
+    last = (1, 5, 3, 7)
+    block, *cache = attend(place, beam_cache_length, second, *cache, (2, 6), ahead=last)
+    (partial,) = attend(
+        place,
+        beam_cache_length,
+        came,
+        *cache,
+        last,
+        earlier=(0, 4, 2, 6),
+        before=(*done, block),
+    )
     parts = lax.all_to_all(partial, "tensor", 0, 0, tiled=True)
     attended = combine(parts, query, key_new, value_new)
 

time: 79.9 us -> 77.4 us (0.969)
  local copies, waits for them, and re-layouts: 10.5 us -> 0.1 us
  starting transfers between devices: 12 us -> 16.2 us
  blocking collectives: 10.2 us -> 12.7 us
  waiting for transfers between devices: 19.3 us -> 20.1 us
    unnamed x20 -> x8, local copies, waits for them, and re-layouts: 10.4 us -> 0.02 us
    ppermute x9, starting transfers between devices: 11.4 us -> 15.7 us  [hop(): return lax.ppermute(x, 'tensor', [(i, i ^ bit) for i in range(ranks)])]
    all_to_all x1, blocking collectives: 10.2 us -> 12.7 us  [matched_body(): parts = lax.all_to_all(partial, 'tensor', 0, 0, tiled=True)]
    ppermute x9, waiting for transfers between devices: 17 us -> 17.9 us  [hop(): return lax.ppermute(x, 'tensor', [(i, i ^ bit) for i in range(ranks)])]
    pallas_call x6 -> x4, Pallas kernels: 9.97 us -> 10.1 us  [attend(): pl.pallas_call(lambda *refs: attend_kernel(slots, ahead, earlier, *refs),...]
  transfers between devices with their start and end apart: 12 -> 12, of which waited for: 8 -> 10; matrix products, arithmetic and copies ran while one was open for 0% -> 0% of each run, Pallas kernels for 19% -> 20%
where the time goes in v5:
time: 77.4 us; the launch traced here: 77.2 us
  Pallas kernels  27.8 us (36%)
  waiting for transfers between devices  20.1 us (26%)
  starting transfers between devices  16.2 us (21%)
  blocking collectives  12.7 us (16%)
    ppermute x9, waiting for transfers between devices, hop(): return lax.ppermute(x, 'tensor', [(i, i ^ bit) for i in range(ranks)])  17.9 us
    ppermute x9, starting transfers between devices, hop(): return lax.ppermute(x, 'tensor', [(i, i ^ bit) for i in range(ranks)])  15.7 us
    all_to_all x1, blocking collectives, matched_body(): parts = lax.all_to_all(partial, 'tensor', 0, 0, tiled=True)  12.7 us
    pallas_call x4, Pallas kernels, attend(): pl.pallas_call(lambda *refs: attend_kernel(slots, ahead, earlier, *refs),...  10.1 us
    pallas_call x2, Pallas kernels, output(): pl.pallas_call(lambda *refs: output_kernel(parity, *refs), in_specs=[scal...  7.79 us
    pallas_call x2, Pallas kernels, project(): pl.pallas_call(lambda *refs: project_kernel(int(first), ranks, *refs), in...  7.75 us
    ppermute x3, waiting for transfers between devices, swapped(): return lax.ppermute(x, 'bank', [(0, 1), (1, 0)])  2.25 us
  transfers between devices with their start and end apart: 12, of which 10 were waited for; matrix products, arithmetic and copies ran while one was open for 0% of the time, Pallas kernels for 20%

profile of v5, /device:TPU:0, one launch (start us, length us, event | category | flops | bytes accessed | tf_op | source)
XLA Modules:
  0.0 77.2 jit_solution(5989835568297877702)
XLA Ops:
  0.0 0.5 collective-permute-start.1
  0.5 0.1 collective-permute-start
  0.5 1.2 %collective-permute-done.refs_3_.other_index = s32[8]{0:T(128)S(1)} collective-permute-done((s32[8]{0:T(128)}, s32[8]{0:T(128)S(1)}, u32[]{:S(2)}, u32[]{:S(2)}) %collective-permute-start) | collective-permute-done | bytes 64 | tf_op jit(solution)/shard_map/ppermute | solution.py:505
  1.7 0.0 collective-permute-done.1.refs_5_.refs_3_
  1.7 0.0 copy-start.2
  1.7 4.1 %project_sent.1 = (f32[4,16,768]{2,1,0:T(8,128)S(1)}, f32[16,128]{1,0:T(8,128)S(1)}) custom-call(s32[1]{0:T(128)} %bitcast.refs_0_, s32[1]{0:T(128)} %bitcast.1.refs_1_.bank, s32[8]{0:T(128)} %own_index.1, s32[8]{0:T(128)S(1)} %collective-permute-done.refs_3_.other_index, bf16[8,1024]{1,0:T(8,128)(2,1)} %x_ref.1, ...), custom_call_target="tpu_custom_call" | custom-call | flops 83886080 | bytes 5242880 | tf_op jit(solution)/shard_map/project_sent/pallas_call | solution.py:149
  5.8 2.8 %collective-permute-start.2 = (f32[4,16,768]{2,1,0:T(8,128)S(1)}, f32[4,16,768]{2,1,0:T(8,128)S(1)}, u32[]{:S(2)}, u32[]{:S(2)}) collective-permute-start(f32[4,16,768]{2,1,0:T(8,128)S(1)} %get-tuple-element.24), channel_id=1, source_target_pairs={{0,2},{2,0},{4,6},{6,4},{8,10},{10,8},{12,14},{14,12},{1,3},{3,1},... | collective-permute-start | bytes 589832 | tf_op jit(solution)/shard_map/ppermute | solution.py:510
  8.6 0.0 copy-done.2
  8.6 0.0 copy-start
  8.6 0.0 copy-start.3
  8.6 3.6 %project_kept.1.kept_ref = f32[4,16,768]{2,1,0:T(8,128)S(1)} custom-call(s32[1]{0:T(128)} %bitcast.refs_0_, s32[1]{0:T(128)} %bitcast.1.refs_1_.bank, bf16[8,1024]{1,0:T(8,128)(2,1)} %x_ref.1, bf16[8,1024]{1,0:T(8,128)(2,1)S(1)} %collective-permute-done.1.refs_5_.refs_3_, bf16[1024,8192]{1,0:T(8,128)(2,1)} %refs_4_.6, bf16[1024,2048]{1,0:T(8,128)(2,1)} %refs_5_.1, ...), custom_call_target="tpu_custom_call" | custom-call | flops 83886080 | bytes 5242880 | tf_op jit(solution)/shard_map/project_kept/pallas_call | solution.py:149
  12.3 1.7 %collective-permute-done.2.came_ref = f32[4,16,768]{2,1,0:T(8,128)S(1)} collective-permute-done((f32[4,16,768]{2,1,0:T(8,128)S(1)}, f32[4,16,768]{2,1,0:T(8,128)S(1)}, u32[]{:S(2)}, u32[]{:S(2)}) %collective-permute-start.2) | collective-permute-done | bytes 196640 | tf_op jit(solution)/shard_map/ppermute | solution.py:510
  14.0 1.9 %collective-permute-start.3 = (f32[2,16,768]{2,1,0:T(8,128)S(1)}, f32[2,16,768]{2,1,0:T(8,128)S(1)}, u32[]{:S(2)}, u32[]{:S(2)}) collective-permute-start(f32[2,16,768]{2,1,0:T(8,128)S(1)} %get-tuple-element.26), channel_id=1, source_target_pairs={{0,4},{2,6},{4,0},{6,2},{8,12},{10,14},{12,8},{14,10},{1,5},{3,7},... | collective-permute-start | bytes 294920 | tf_op jit(solution)/shard_map/ppermute | solution.py:510
  15.9 2.8 %collective-permute-done.3.came_ref = f32[2,16,768]{2,1,0:T(8,128)S(1)} collective-permute-done((f32[2,16,768]{2,1,0:T(8,128)S(1)}, f32[2,16,768]{2,1,0:T(8,128)S(1)}, u32[]{:S(2)}, u32[]{:S(2)}) %collective-permute-start.3) | collective-permute-done | bytes 98336 | tf_op jit(solution)/shard_map/ppermute | solution.py:510
  18.7 2.9 %collective-permute-start.4 = (f32[1,16,768]{2,1,0:T(8,128)S(1)}, f32[1,16,768]{2,1,0:T(8,128)S(1)}, u32[]{:S(2)}, u32[]{:S(2)}) collective-permute-start(f32[1,16,768]{2,1,0:T(8,128)S(1)} %get-tuple-element.28), channel_id=1, source_target_pairs={{0,8},{2,10},{4,12},{6,14},{8,0},{10,2},{12,4},{14,6},{1,9},{3,11}... | collective-permute-start | bytes 147464 | tf_op jit(solution)/shard_map/ppermute | solution.py:510
  21.6 0.1 fusion
  21.7 2.1 %collective-permute-done.4.came_ref = f32[1,16,768]{2,1,0:T(8,128)S(1)} collective-permute-done((f32[1,16,768]{2,1,0:T(8,128)S(1)}, f32[1,16,768]{2,1,0:T(8,128)S(1)}, u32[]{:S(2)}, u32[]{:S(2)}) %collective-permute-start.4) | collective-permute-done | bytes 49184 | tf_op jit(solution)/shard_map/ppermute | solution.py:510
  23.8 0.0 copy-done
  23.8 0.0 copy-done.3
  23.8 0.9 %correct.1 = (f32[8,1152]{1,0:T(8,128)S(1)}, f32[8,1152]{1,0:T(8,128)S(1)}) custom-call(s32[1]{0:T(128)} %bitcast.1.refs_1_.bank, s32[8]{0:T(128)S(1)} %copy-done.3, s32[8]{0:T(128)S(1)} %collective-permute-done.refs_3_.other_index, f32[1,16,768]{2,1,0:T(8,128)S(1)} %get-tuple-element.27.kept_ref, f32[1,16,768]{2,1,0:T(8,128)S(1)} %collective-permute-done.4.came_ref, ...), custom_call_target="tpu_custom_call" | custom-call | flops 33554432 | bytes 2097152 | tf_op jit(solution)/shard_map/correct/pallas_call | solution.py:214
  24.7 0.0 collective-permute-start.5
  24.7 0.1 pad_maximum_fusion.sin_ref
  24.8 0.1 tile.10.cos_ref
  24.9 1.1 %collective-permute-done.5.came_ref = f32[8,1152]{1,0:T(8,128)S(1)} collective-permute-done((f32[8,1152]{1,0:T(8,128)S(1)}, f32[8,1152]{1,0:T(8,128)S(1)}, u32[]{:S(2)}, u32[]{:S(2)}) %collective-permute-start.5) | collective-permute-done | bytes 36896 | tf_op jit(solution)/shard_map/ppermute | solution.py:505
  25.9 0.1 rotate.1
  26.0 2.9 %collective-permute-start.6 = (bf16[1,64,128]{2,1,0:T(8,128)(2,1)S(1)}, bf16[1,64,128]{2,1,0:T(8,128)(2,1)S(1)}, u32[]{:S(2)}, u32[]{:S(2)}) collective-permute-start(bf16[1,64,128]{2,1,0:T(8,128)(2,1)S(1)} %get-tuple-element.31.first_ref.refs_2_.q_ref), channel_id=1, source_target_pairs={{0,8},{2,10},{4,12},{6,14},{8,0},{10,2},{12,4},{14,6},{1,9},{3,11}... | collective-permute-start | bytes 49160 | tf_op jit(solution)/shard_map/ppermute | solution.py:510
  29.0 1.8 %collective-permute-done.6.second_ref.refs_2_ = bf16[1,64,128]{2,1,0:T(8,128)(2,1)S(1)} collective-permute-done((bf16[1,64,128]{2,1,0:T(8,128)(2,1)S(1)}, bf16[1,64,128]{2,1,0:T(8,128)(2,1)S(1)}, u32[]{:S(2)}, u32[]{:S(2)}) %collective-permute-start.6) | collective-permute-done | bytes 16416 | tf_op jit(solution)/shard_map/ppermute | solution.py:510
  30.7 1.9 %collective-permute-start.7 = (bf16[2,64,128]{2,1,0:T(8,128)(2,1)S(1)}, bf16[2,64,128]{2,1,0:T(8,128)(2,1)S(1)}, u32[]{:S(2)}, u32[]{:S(2)}) collective-permute-start(bf16[2,64,128]{2,1,0:T(8,128)(2,1)S(1)} %join.2.first_ref), channel_id=1, source_target_pairs={{0,4},{2,6},{4,0},{6,2},{8,12},{10,14},{12,8},{14,10},{1,5},{3,7},... | collective-permute-start | bytes 98312 | tf_op jit(solution)/shard_map/ppermute | solution.py:510
  32.6 2.0 %collective-permute-done.7.second_ref.refs_2_ = bf16[2,64,128]{2,1,0:T(8,128)(2,1)S(1)} collective-permute-done((bf16[2,64,128]{2,1,0:T(8,128)(2,1)S(1)}, bf16[2,64,128]{2,1,0:T(8,128)(2,1)S(1)}, u32[]{:S(2)}, u32[]{:S(2)}) %collective-permute-start.7) | collective-permute-done | bytes 32800 | tf_op jit(solution)/shard_map/ppermute | solution.py:510
  34.7 1.7 %collective-permute-start.8 = (bf16[4,64,128]{2,1,0:T(8,128)(2,1)S(1)}, bf16[4,64,128]{2,1,0:T(8,128)(2,1)S(1)}, u32[]{:S(2)}, u32[]{:S(2)}) collective-permute-start(bf16[4,64,128]{2,1,0:T(8,128)(2,1)S(1)} %join.3), channel_id=1, source_target_pairs={{0,2},{2,0},{4,6},{6,4},{8,10},{10,8},{12,14},{14,12},{1,3},{3,1},... | collective-permute-start | bytes 196616 | tf_op jit(solution)/shard_map/ppermute | solution.py:510
  36.4 2.2 %attend.5.refs_5_ = bf16[1,80,128]{2,1,0:T(8,128)(2,1)S(1)} custom-call(s32[1]{0:T(128)} %bitcast.refs_0_, s32[8]{0:T(128)S(1)} %copy-done.2, bf16[1,64,128]{2,1,0:T(8,128)(2,1)S(1)} %get-tuple-element.31.first_ref.refs_2_.q_ref, bf16[8,256,1024]{2,1,0:T(8,128)(2,1)} %refs_3_.5, bf16[8,256,1024]{2,1,0:T(8,128)(2,1)} %refs_4_.9), custom_call_target="tpu_custom_call" | custom-call | flops 8388608 | bytes 1048576 | tf_op jit(solution)/shard_map/attend/pallas_call | solution.py:382
  38.6 2.2 %attend.6.refs_6_ = bf16[1,80,128]{2,1,0:T(8,128)(2,1)S(1)} custom-call(s32[1]{0:T(128)} %bitcast.refs_0_, s32[8]{0:T(128)S(1)} %copy-done.2, bf16[1,64,128]{2,1,0:T(8,128)(2,1)S(1)} %collective-permute-done.6.second_ref.refs_2_, bf16[8,256,1024]{2,1,0:T(8,128)(2,1)} %refs_3_.5, bf16[8,256,1024]{2,1,0:T(8,128)(2,1)} %refs_4_.9), custom_call_target="tpu_custom_call" | custom-call | flops 8388608 | bytes 1048576 | tf_op jit(solution)/shard_map/attend/pallas_call | solution.py:382
  40.8 3.6 %attend.4 = (bf16[2,80,128]{2,1,0:T(8,128)(2,1)S(1)}, bf16[4,8,256,128]{3,2,1,0:T(8,128)(2,1)S(1)}, bf16[4,8,256,128]{3,2,1,0:T(8,128)(2,1)S(1)}) custom-call(s32[1]{0:T(128)} %bitcast.refs_0_, s32[8]{0:T(128)S(1)} %copy-done.2, bf16[2,64,128]{2,1,0:T(8,128)(2,1)S(1)} %collective-permute-done.7.second_ref.refs_2_, bf16[8,256,1024]{2,1,0:T(8,128)(2,1)} %refs_3_.5, ...), custom_call_target="tpu_custom_call" | custom-call | flops 16777216 | bytes 6291456 | tf_op jit(solution)/shard_map/attend/pallas_call | solution.py:382
  44.4 0.0 collective-permute-done.8.refs_2_
  44.4 2.1 %attend.7 = bf16[8,80,128]{2,1,0:T(8,128)(2,1)S(1)} custom-call(s32[1]{0:T(128)} %bitcast.refs_0_, s32[8]{0:T(128)S(1)} %copy-done.2, bf16[4,64,128]{2,1,0:T(8,128)(2,1)S(1)} %collective-permute-done.8.refs_2_, bf16[4,8,256,128]{3,2,1,0:T(8,128)(2,1)S(1)} %get-tuple-element.32.refs_3_, bf16[4,8,256,128]{3,2,1,0:T(8,128)(2,1)S(1)} %get-tuple-element.33.refs_4_, ...), custom_call_target="tpu_custom_call" | custom-call | flops 33554432 | bytes 4194304 | tf_op jit(solution)/shard_map/attend/pallas_call | solution.py:382
  46.5 12.7 %all_to_all.5.parts_ref = bf16[8,80,128]{2,1,0:T(8,128)(2,1)S(1)} all-to-all(bf16[8,80,128]{2,1,0:T(8,128)(2,1)S(1)} %attend.7), channel_id=1, replica_groups=mesh['groups'=2,'tensor'=8,'bank'=2] {'tensor'}, dimensions={0} | all-to-all | bytes 327680 | tf_op jit(solution)/shard_map/all_to_all | solution.py:576
  59.2 0.5 combine.1.refs_1_
  59.7 3.9 %output_sent.1 = bf16[4,8,1024]{2,1,0:T(8,128)(2,1)S(1)} custom-call(s32[1]{0:T(128)} %bitcast.refs_0_, bf16[8,1024]{1,0:T(8,128)(2,1)S(1)} %combine.1.refs_1_, bf16[1024,8192]{1,0:T(8,128)(2,1)} %refs_2_.7), custom_call_target="tpu_custom_call" | custom-call | flops 67108864 | bytes 8388608 | tf_op jit(solution)/shard_map/output_sent/pallas_call | solution.py:471
  63.6 0.0 copy-start.1
  63.6 0.2 collective-permute-start.9
  63.8 3.9 %output_kept.1.kept_ref = f32[4,8,1024]{2,1,0:T(8,128)S(1)} custom-call(s32[1]{0:T(128)} %bitcast.refs_0_, bf16[8,1024]{1,0:T(8,128)(2,1)S(1)} %combine.1.refs_1_, bf16[1024,8192]{1,0:T(8,128)(2,1)} %refs_2_.7), custom_call_target="tpu_custom_call" | custom-call | flops 67108864 | bytes 8388608 | tf_op jit(solution)/shard_map/output_kept/pallas_call | solution.py:471
  67.7 0.2 collective-permute-done.9.came_ref
  67.9 1.1 %collective-permute-start.10 = (bf16[2,8,1024]{2,1,0:T(8,128)(2,1)S(1)}, bf16[2,8,1024]{2,1,0:T(8,128)(2,1)S(1)}, u32[]{:S(2)}, u32[]{:S(2)}) collective-permute-start(bf16[2,8,1024]{2,1,0:T(8,128)(2,1)S(1)} %get-tuple-element.38), channel_id=1, source_target_pairs={{0,4},{2,6},{4,0},{6,2},{8,12},{10,14},{12,8},{14,10},{1,5},{3,7},... | collective-permute-start | bytes 98312 | tf_op jit(solution)/shard_map/ppermute | solution.py:510
  69.0 2.9 %collective-permute-done.10.came_ref = bf16[2,8,1024]{2,1,0:T(8,128)(2,1)S(1)} collective-permute-done((bf16[2,8,1024]{2,1,0:T(8,128)(2,1)S(1)}, bf16[2,8,1024]{2,1,0:T(8,128)(2,1)S(1)}, u32[]{:S(2)}, u32[]{:S(2)}) %collective-permute-start.10) | collective-permute-done | bytes 32800 | tf_op jit(solution)/shard_map/ppermute | solution.py:510
  71.9 0.4 collective-permute-start.11
  72.3 4.3 %collective-permute-done.11.came_ref = bf16[1,8,1024]{2,1,0:T(8,128)(2,1)S(1)} collective-permute-done((bf16[1,8,1024]{2,1,0:T(8,128)(2,1)S(1)}, bf16[1,8,1024]{2,1,0:T(8,128)(2,1)S(1)}, u32[]{:S(2)}, u32[]{:S(2)}) %collective-permute-start.11) | collective-permute-done | bytes 16416 | tf_op jit(solution)/shard_map/ppermute | solution.py:510
  76.6 0.0 copy-done.1
  76.6 0.6 residual.1
  (9 shorter events, 0.1 us)
Async XLA Ops:
  0.0 1.7 %collective-permute-start.1 = (bf16[8,1024]{1,0:T(8,128)(2,1)}, bf16[8,1024]{1,0:T(8,128)(2,1)S(1)}, u32[]{:S(2)}, u32[]{:S(2)}) collective-permute-start(bf16[8,1024]{1,0:T(8,128)(2,1)} %x_ref.1), channel_id=1, source_target_pairs={{0,1},{1,0},{2,3},{3,2},{4,5},{5,4},{6,7},{7,6},{8,9},{9,8},{10,11... | collective-permute-start | bytes 49160 | tf_op jit(solution)/shard_map/ppermute | solution.py:505
  0.5 1.3 %collective-permute-start = (s32[8]{0:T(128)}, s32[8]{0:T(128)S(1)}, u32[]{:S(2)}, u32[]{:S(2)}) collective-permute-start(s32[8]{0:T(128)} %own_index.1), channel_id=1, source_target_pairs={{0,1},{1,0},{2,3},{3,2},{4,5},{5,4},{6,7},{7,6},{8,9},{9,8},{10,11... | collective-permute-start | bytes 104 | tf_op jit(solution)/shard_map/ppermute | solution.py:505
  1.7 6.9 %copy-start.2 = (s32[8]{0:T(128)S(1)}, s32[8]{0:T(128)}, u32[]{:S(2)}) copy-start(s32[8]{0:T(128)} %refs_1_.7) | copy-start | bytes 100
  5.8 8.2 %collective-permute-start.2 = (f32[4,16,768]{2,1,0:T(8,128)S(1)}, f32[4,16,768]{2,1,0:T(8,128)S(1)}, u32[]{:S(2)}, u32[]{:S(2)}) collective-permute-start(f32[4,16,768]{2,1,0:T(8,128)S(1)} %get-tuple-element.24), channel_id=1, source_target_pairs={{0,2},{2,0},{4,6},{6,4},{8,10},{10,8},{12,14},{14,12},{1,3},{3,1},... | collective-permute-start | bytes 589832 | tf_op jit(solution)/shard_map/ppermute | solution.py:510
  8.6 15.1 %copy-start = (bf16[16,64,1024]{2,1,0:T(8,128)(2,1)S(1)}, bf16[16,64,1024]{2,1,0:T(8,128)(2,1)}, u32[]{:S(2)}) copy-start(bf16[16,64,1024]{2,1,0:T(8,128)(2,1)} %up_ref.1) | copy-start | bytes 6291460
  8.6 15.1 %copy-start.3 = (s32[8]{0:T(128)S(1)}, s32[8]{0:T(128)}, u32[]{:S(2)}) copy-start(s32[8]{0:T(128)} %own_index.1) | copy-start | bytes 100
  14.0 4.7 %collective-permute-start.3 = (f32[2,16,768]{2,1,0:T(8,128)S(1)}, f32[2,16,768]{2,1,0:T(8,128)S(1)}, u32[]{:S(2)}, u32[]{:S(2)}) collective-permute-start(f32[2,16,768]{2,1,0:T(8,128)S(1)} %get-tuple-element.26), channel_id=1, source_target_pairs={{0,4},{2,6},{4,0},{6,2},{8,12},{10,14},{12,8},{14,10},{1,5},{3,7},... | collective-permute-start | bytes 294920 | tf_op jit(solution)/shard_map/ppermute | solution.py:510
  18.7 5.1 %collective-permute-start.4 = (f32[1,16,768]{2,1,0:T(8,128)S(1)}, f32[1,16,768]{2,1,0:T(8,128)S(1)}, u32[]{:S(2)}, u32[]{:S(2)}) collective-permute-start(f32[1,16,768]{2,1,0:T(8,128)S(1)} %get-tuple-element.28), channel_id=1, source_target_pairs={{0,8},{2,10},{4,12},{6,14},{8,0},{10,2},{12,4},{14,6},{1,9},{3,11}... | collective-permute-start | bytes 147464 | tf_op jit(solution)/shard_map/ppermute | solution.py:510
  24.7 1.2 %collective-permute-start.5 = (f32[8,1152]{1,0:T(8,128)S(1)}, f32[8,1152]{1,0:T(8,128)S(1)}, u32[]{:S(2)}, u32[]{:S(2)}) collective-permute-start(f32[8,1152]{1,0:T(8,128)S(1)} %get-tuple-element.30), channel_id=1, source_target_pairs={{0,1},{1,0},{2,3},{3,2},{4,5},{5,4},{6,7},{7,6},{8,9},{9,8},{10,11... | collective-permute-start | bytes 110600 | tf_op jit(solution)/shard_map/ppermute | solution.py:505
  26.0 4.7 %collective-permute-start.6 = (bf16[1,64,128]{2,1,0:T(8,128)(2,1)S(1)}, bf16[1,64,128]{2,1,0:T(8,128)(2,1)S(1)}, u32[]{:S(2)}, u32[]{:S(2)}) collective-permute-start(bf16[1,64,128]{2,1,0:T(8,128)(2,1)S(1)} %get-tuple-element.31.first_ref.refs_2_.q_ref), channel_id=1, source_target_pairs={{0,8},{2,10},{4,12},{6,14},{8,0},{10,2},{12,4},{14,6},{1,9},{3,11}... | collective-permute-start | bytes 49160 | tf_op jit(solution)/shard_map/ppermute | solution.py:510
  30.7 3.9 %collective-permute-start.7 = (bf16[2,64,128]{2,1,0:T(8,128)(2,1)S(1)}, bf16[2,64,128]{2,1,0:T(8,128)(2,1)S(1)}, u32[]{:S(2)}, u32[]{:S(2)}) collective-permute-start(bf16[2,64,128]{2,1,0:T(8,128)(2,1)S(1)} %join.2.first_ref), channel_id=1, source_target_pairs={{0,4},{2,6},{4,0},{6,2},{8,12},{10,14},{12,8},{14,10},{1,5},{3,7},... | collective-permute-start | bytes 98312 | tf_op jit(solution)/shard_map/ppermute | solution.py:510
  34.7 9.8 %collective-permute-start.8 = (bf16[4,64,128]{2,1,0:T(8,128)(2,1)S(1)}, bf16[4,64,128]{2,1,0:T(8,128)(2,1)S(1)}, u32[]{:S(2)}, u32[]{:S(2)}) collective-permute-start(bf16[4,64,128]{2,1,0:T(8,128)(2,1)S(1)} %join.3), channel_id=1, source_target_pairs={{0,2},{2,0},{4,6},{6,4},{8,10},{10,8},{12,14},{14,12},{1,3},{3,1},... | collective-permute-start | bytes 196616 | tf_op jit(solution)/shard_map/ppermute | solution.py:510
  63.6 13.1 %copy-start.1 = (bf16[8,1024]{1,0:T(8,128)(2,1)S(1)}, bf16[8,1024]{1,0:T(8,128)(2,1)}, u32[]{:S(2)}) copy-start(bf16[8,1024]{1,0:T(8,128)(2,1)} %x_ref.1) | copy-start | bytes 49156
  63.6 4.3 %collective-permute-start.9 = (bf16[4,8,1024]{2,1,0:T(8,128)(2,1)S(1)}, bf16[4,8,1024]{2,1,0:T(8,128)(2,1)S(1)}, u32[]{:S(2)}, u32[]{:S(2)}) collective-permute-start(bf16[4,8,1024]{2,1,0:T(8,128)(2,1)S(1)} %output_sent.1), channel_id=1, source_target_pairs={{0,2},{2,0},{4,6},{6,4},{8,10},{10,8},{12,14},{14,12},{1,3},{3,1},... | collective-permute-start | bytes 196616 | tf_op jit(solution)/shard_map/ppermute | solution.py:510
  67.9 4.0 %collective-permute-start.10 = (bf16[2,8,1024]{2,1,0:T(8,128)(2,1)S(1)}, bf16[2,8,1024]{2,1,0:T(8,128)(2,1)S(1)}, u32[]{:S(2)}, u32[]{:S(2)}) collective-permute-start(bf16[2,8,1024]{2,1,0:T(8,128)(2,1)S(1)} %get-tuple-element.38), channel_id=1, source_target_pairs={{0,4},{2,6},{4,0},{6,2},{8,12},{10,14},{12,8},{14,10},{1,5},{3,7},... | collective-permute-start | bytes 98312 | tf_op jit(solution)/shard_map/ppermute | solution.py:510
  71.9 4.7 %collective-permute-start.11 = (bf16[1,8,1024]{2,1,0:T(8,128)(2,1)S(1)}, bf16[1,8,1024]{2,1,0:T(8,128)(2,1)S(1)}, u32[]{:S(2)}, u32[]{:S(2)}) collective-permute-start(bf16[1,8,1024]{2,1,0:T(8,128)(2,1)S(1)} %get-tuple-element.40), channel_id=1, source_target_pairs={{0,8},{2,10},{4,12},{6,14},{8,0},{10,2},{12,4},{14,6},{1,9},{3,11}... | collective-permute-start | bytes 49160 | tf_op jit(solution)/shard_map/ppermute | solution.py:510

commit v6 on v5

--- a/solution.py
+++ b/solution.py
@@ -391,7 +391,7 @@
         compiler_params=params(),
         cost_estimate=pl.CostEstimate(
             flops=4 * rows * count * positions * HEAD_DIM,
-            bytes_accessed=4 * beams * positions * HEAD_DIM * (count + len(ahead)),
+            bytes_accessed=4 * beams * positions * HEAD_DIM * (16 if earlier else count),
             transcendentals=rows * count * positions,
         ),
         name="attend",
@@ -451,32 +451,22 @@
     )(parts, query, key_new, value_new)
 
 
-def output_kernel(parity, place, x_ref, w_ref, out, w_buf, sems):
-    count, _, width = w_buf.shape
-    copies = [
-        start_columns(w_ref, ((2 * s + parity) ^ place[0]) * width, w_buf.at[s], sems.at[s])
-        for s in range(count)
-    ]
+def output_kernel(parity, place, x_ref, w_ref, out):
+    count, _, width = out.shape
     for s in range(count):
-        for copy in copies[s]:
-            copy.wait()
-        total = jnp.dot(x_ref[...], w_buf[s], preferred_element_type=F32)
+        first = ((2 * s + parity) ^ place[0]) * width
+        columns = pl.ds(pl.multiple_of(first, width), width)
+        total = jnp.dot(x_ref[...], w_ref[:, columns], preferred_element_type=F32)
         out[s] = total.astype(out.dtype)
 
 
 def output(place, x, weight, ranks, parity, dtype):
-    beams, depth = x.shape
-    width = weight.shape[1] // ranks
-    half = ranks // 2
+    beams = x.shape[0]
     return pl.pallas_call(
         lambda *refs: output_kernel(parity, *refs),
-        in_specs=[scalar(), whole(), big()],
+        in_specs=[scalar(), whole(), whole()],
         out_specs=whole(),
-        out_shape=shape(half, beams, width, dtype=dtype),
-        scratch_shapes=[
-            pltpu.VMEM((half, depth, width), BF16),
-            pltpu.SemaphoreType.DMA((half, CHUNKS)),
-        ],
+        out_shape=shape(ranks // 2, beams, weight.shape[1] // ranks, dtype=dtype),
         compiler_params=params(),
         cost_estimate=pl.CostEstimate(
             flops=beams * weight.size, bytes_accessed=weight.size, transcendentals=0
@@ -556,11 +546,14 @@
     query, key_new, value_new = rotated(bank, own, swapped(other), cosine, sine)
 
     cache = in_hbm(paged_key_cache), in_hbm(paged_value_cache)
-    came = hop(query, 4)
-    done = attend(place, beam_cache_length, query, *cache, (0,))
+    came, done = lax.optimization_barrier(
+        (hop(query, 4), attend(place, beam_cache_length, query, *cache, (0,)))
+    )
     gathered = join(query, came)
-    second = hop(gathered, 2)
-    done += attend(place, beam_cache_length, came, *cache, (4,))
+    second, more = lax.optimization_barrier(
+        (hop(gathered, 2), attend(place, beam_cache_length, came, *cache, (4,)))
+    )
+    done += more
     came = hop(join(gathered, second), 1)
     last = (1, 5, 3, 7)
     block, *cache = attend(place, beam_cache_length, second, *cache, (2, 6), ahead=last)
@@ -576,9 +569,8 @@
     parts = lax.all_to_all(partial, "tensor", 0, 0, tiled=True)
     attended = combine(parts, query, key_new, value_new)
 
-    weight = in_hbm(output_weight)
-    came = hop(output(place, attended, weight, ranks, 1, BF16), 1)
-    kept = output(place, attended, weight, ranks, 0, F32)
+    came = hop(output(place, attended, output_weight, ranks, 1, BF16), 1)
+    kept = output(place, attended, output_weight, ranks, 0, F32)
     sent, kept = halve(kept, came)
     sent, kept = halve(kept, hop(sent, 2))
     return residual(x, kept, hop(sent, 4))

time: 77.4 us -> 70.4 us (0.910)
  Pallas kernels: 27.8 us -> 22.7 us
  starting transfers between devices: 16.2 us -> 15.2 us
  blocking collectives: 12.7 us -> 11.9 us
    pallas_call x2, Pallas kernels: 7.79 us -> 2.39 us  [output(): pl.pallas_call(lambda *refs: output_kernel(parity, *refs), in_specs=[scal...]
    ppermute x9, starting transfers between devices: 15.7 us -> 14.7 us  [hop(): return lax.ppermute(x, 'tensor', [(i, i ^ bit) for i in range(ranks)])]
  transfers between devices with their start and end apart: 12 -> 12, of which waited for: 10 -> 8; matrix products, arithmetic and copies ran while one was open for 0% -> 0% of each run, Pallas kernels for 20% -> 19%
where the time goes in v6:
time: 70.4 us; the launch traced here: 70.3 us
  Pallas kernels  22.7 us (32%)
  waiting for transfers between devices  20 us (28%)
  starting transfers between devices  15.2 us (22%)
  blocking collectives  11.9 us (17%)
    ppermute x9, waiting for transfers between devices, hop(): return lax.ppermute(x, 'tensor', [(i, i ^ bit) for i in range(ranks)])  17.7 us
    ppermute x9, starting transfers between devices, hop(): return lax.ppermute(x, 'tensor', [(i, i ^ bit) for i in range(ranks)])  14.7 us
    all_to_all x1, blocking collectives, matched_body(): parts = lax.all_to_all(partial, 'tensor', 0, 0, tiled=True)  11.9 us
    pallas_call x4, Pallas kernels, attend(): pl.pallas_call(lambda *refs: attend_kernel(slots, ahead, earlier, *refs),...  10.3 us
    pallas_call x2, Pallas kernels, project(): pl.pallas_call(lambda *refs: project_kernel(int(first), ranks, *refs), in...  7.75 us
    pallas_call x2, Pallas kernels, output(): pl.pallas_call(lambda *refs: output_kernel(parity, *refs), in_specs=[scal...  2.39 us
    ppermute x3, waiting for transfers between devices, swapped(): return lax.ppermute(x, 'bank', [(0, 1), (1, 0)])  2.25 us
  transfers between devices with their start and end apart: 12, of which 8 were waited for; matrix products, arithmetic and copies ran while one was open for 0% of the time, Pallas kernels for 19%

profile of v6, /device:TPU:0, one launch (start us, length us, event | category | flops | bytes accessed | tf_op | source)
XLA Modules:
  0.0 70.3 jit_solution(7206594607099779573)
XLA Ops:
  0.0 0.5 collective-permute-start.1
  0.5 0.1 collective-permute-start
  0.5 1.2 %collective-permute-done.refs_3_.other_index = s32[8]{0:T(128)S(1)} collective-permute-done((s32[8]{0:T(128)}, s32[8]{0:T(128)S(1)}, u32[]{:S(2)}, u32[]{:S(2)}) %collective-permute-start) | collective-permute-done | bytes 64 | tf_op jit(solution)/shard_map/ppermute | solution.py:495
  1.7 0.0 collective-permute-done.1.refs_5_.refs_3_
  1.7 0.0 copy-start.2
  1.7 4.1 %project_sent.1 = (f32[4,16,768]{2,1,0:T(8,128)S(1)}, f32[16,128]{1,0:T(8,128)S(1)}) custom-call(s32[1]{0:T(128)} %bitcast.refs_0_, s32[1]{0:T(128)} %bitcast.1.refs_1_.bank, s32[8]{0:T(128)} %own_index.1, s32[8]{0:T(128)S(1)} %collective-permute-done.refs_3_.other_index, bf16[8,1024]{1,0:T(8,128)(2,1)} %x_ref.1, ...), custom_call_target="tpu_custom_call" | custom-call | flops 83886080 | bytes 5242880 | tf_op jit(solution)/shard_map/project_sent/pallas_call | solution.py:149
  5.8 2.8 %collective-permute-start.2 = (f32[4,16,768]{2,1,0:T(8,128)S(1)}, f32[4,16,768]{2,1,0:T(8,128)S(1)}, u32[]{:S(2)}, u32[]{:S(2)}) collective-permute-start(f32[4,16,768]{2,1,0:T(8,128)S(1)} %get-tuple-element.28), channel_id=1, source_target_pairs={{0,2},{2,0},{4,6},{6,4},{8,10},{10,8},{12,14},{14,12},{1,3},{3,1},... | collective-permute-start | bytes 589832 | tf_op jit(solution)/shard_map/ppermute | solution.py:500
  8.6 0.0 copy-done.2
  8.6 0.0 copy-start
  8.6 0.0 copy-start.3
  8.6 3.6 %project_kept.1.kept_ref = f32[4,16,768]{2,1,0:T(8,128)S(1)} custom-call(s32[1]{0:T(128)} %bitcast.refs_0_, s32[1]{0:T(128)} %bitcast.1.refs_1_.bank, bf16[8,1024]{1,0:T(8,128)(2,1)} %x_ref.1, bf16[8,1024]{1,0:T(8,128)(2,1)S(1)} %collective-permute-done.1.refs_5_.refs_3_, bf16[1024,8192]{1,0:T(8,128)(2,1)} %refs_4_.6, bf16[1024,2048]{1,0:T(8,128)(2,1)} %refs_5_.1, ...), custom_call_target="tpu_custom_call" | custom-call | flops 83886080 | bytes 5242880 | tf_op jit(solution)/shard_map/project_kept/pallas_call | solution.py:149
  12.3 1.7 %collective-permute-done.2.came_ref = f32[4,16,768]{2,1,0:T(8,128)S(1)} collective-permute-done((f32[4,16,768]{2,1,0:T(8,128)S(1)}, f32[4,16,768]{2,1,0:T(8,128)S(1)}, u32[]{:S(2)}, u32[]{:S(2)}) %collective-permute-start.2) | collective-permute-done | bytes 196640 | tf_op jit(solution)/shard_map/ppermute | solution.py:500
  14.0 1.9 %collective-permute-start.3 = (f32[2,16,768]{2,1,0:T(8,128)S(1)}, f32[2,16,768]{2,1,0:T(8,128)S(1)}, u32[]{:S(2)}, u32[]{:S(2)}) collective-permute-start(f32[2,16,768]{2,1,0:T(8,128)S(1)} %get-tuple-element.30), channel_id=1, source_target_pairs={{0,4},{2,6},{4,0},{6,2},{8,12},{10,14},{12,8},{14,10},{1,5},{3,7},... | collective-permute-start | bytes 294920 | tf_op jit(solution)/shard_map/ppermute | solution.py:500
  15.9 2.8 %collective-permute-done.3.came_ref = f32[2,16,768]{2,1,0:T(8,128)S(1)} collective-permute-done((f32[2,16,768]{2,1,0:T(8,128)S(1)}, f32[2,16,768]{2,1,0:T(8,128)S(1)}, u32[]{:S(2)}, u32[]{:S(2)}) %collective-permute-start.3) | collective-permute-done | bytes 98336 | tf_op jit(solution)/shard_map/ppermute | solution.py:500
  18.7 2.9 %collective-permute-start.4 = (f32[1,16,768]{2,1,0:T(8,128)S(1)}, f32[1,16,768]{2,1,0:T(8,128)S(1)}, u32[]{:S(2)}, u32[]{:S(2)}) collective-permute-start(f32[1,16,768]{2,1,0:T(8,128)S(1)} %get-tuple-element.32), channel_id=1, source_target_pairs={{0,8},{2,10},{4,12},{6,14},{8,0},{10,2},{12,4},{14,6},{1,9},{3,11}... | collective-permute-start | bytes 147464 | tf_op jit(solution)/shard_map/ppermute | solution.py:500
  21.6 0.1 fusion
  21.7 2.1 %collective-permute-done.4.came_ref = f32[1,16,768]{2,1,0:T(8,128)S(1)} collective-permute-done((f32[1,16,768]{2,1,0:T(8,128)S(1)}, f32[1,16,768]{2,1,0:T(8,128)S(1)}, u32[]{:S(2)}, u32[]{:S(2)}) %collective-permute-start.4) | collective-permute-done | bytes 49184 | tf_op jit(solution)/shard_map/ppermute | solution.py:500
  23.8 0.0 copy-done
  23.8 0.0 copy-done.3
  23.8 0.9 %correct.1 = (f32[8,1152]{1,0:T(8,128)S(1)}, f32[8,1152]{1,0:T(8,128)S(1)}) custom-call(s32[1]{0:T(128)} %bitcast.1.refs_1_.bank, s32[8]{0:T(128)S(1)} %copy-done.3, s32[8]{0:T(128)S(1)} %collective-permute-done.refs_3_.other_index, f32[1,16,768]{2,1,0:T(8,128)S(1)} %get-tuple-element.31.kept_ref, f32[1,16,768]{2,1,0:T(8,128)S(1)} %collective-permute-done.4.came_ref, ...), custom_call_target="tpu_custom_call" | custom-call | flops 33554432 | bytes 2097152 | tf_op jit(solution)/shard_map/correct/pallas_call | solution.py:214
  24.7 0.0 collective-permute-start.5
  24.7 0.1 pad_maximum_fusion.sin_ref
  24.8 0.1 tile.10.cos_ref
  24.9 1.1 %collective-permute-done.5.came_ref = f32[8,1152]{1,0:T(8,128)S(1)} collective-permute-done((f32[8,1152]{1,0:T(8,128)S(1)}, f32[8,1152]{1,0:T(8,128)S(1)}, u32[]{:S(2)}, u32[]{:S(2)}) %collective-permute-start.5) | collective-permute-done | bytes 36896 | tf_op jit(solution)/shard_map/ppermute | solution.py:495
  25.9 0.1 rotate.1
  26.0 2.9 %collective-permute-start.6 = (bf16[1,64,128]{2,1,0:T(8,128)(2,1)S(1)}, bf16[1,64,128]{2,1,0:T(8,128)(2,1)S(1)}, u32[]{:S(2)}, u32[]{:S(2)}) collective-permute-start(bf16[1,64,128]{2,1,0:T(8,128)(2,1)S(1)} %get-tuple-element.35.refs_2_.first_ref.q_ref), channel_id=1, source_target_pairs={{0,8},{2,10},{4,12},{6,14},{8,0},{10,2},{12,4},{14,6},{1,9},{3,11}... | collective-permute-start | bytes 49160 | tf_op jit(solution)/shard_map/ppermute | solution.py:500
  29.0 0.0 slice-start
  29.0 0.0 slice-start.1
  29.0 2.5 %attend.4.refs_5_ = bf16[1,80,128]{2,1,0:T(8,128)(2,1)S(1)} custom-call(s32[1]{0:T(128)} %bitcast.refs_0_, s32[8]{0:T(128)S(1)} %copy-done.2, bf16[1,64,128]{2,1,0:T(8,128)(2,1)S(1)} %get-tuple-element.35.refs_2_.first_ref.q_ref, bf16[8,256,1024]{2,1,0:T(8,128)(2,1)} %refs_3_.5, bf16[8,256,1024]{2,1,0:T(8,128)(2,1)} %refs_4_.9), custom_call_target="tpu_custom_call" | custom-call | flops 8388608 | bytes 1048576 | tf_op jit(solution)/shard_map/attend/pallas_call | solution.py:382
  31.4 0.0 collective-permute-done.6.second_ref.refs_2_
  31.5 0.0 slice-start.2
  31.5 2.0 %collective-permute-start.7 = (bf16[2,64,128]{2,1,0:T(8,128)(2,1)S(1)}, bf16[2,64,128]{2,1,0:T(8,128)(2,1)S(1)}, u32[]{:S(2)}, u32[]{:S(2)}) collective-permute-start(bf16[2,64,128]{2,1,0:T(8,128)(2,1)S(1)} %join.2.first_ref), channel_id=1, source_target_pairs={{0,4},{2,6},{4,0},{6,2},{8,12},{10,14},{12,8},{14,10},{1,5},{3,7},... | collective-permute-start | bytes 98312 | tf_op jit(solution)/shard_map/ppermute | solution.py:500
  33.5 2.2 %attend.5.refs_6_ = bf16[1,80,128]{2,1,0:T(8,128)(2,1)S(1)} custom-call(s32[1]{0:T(128)} %bitcast.refs_0_, s32[8]{0:T(128)S(1)} %copy-done.2, bf16[1,64,128]{2,1,0:T(8,128)(2,1)S(1)} %collective-permute-done.6.second_ref.refs_2_, bf16[8,256,1024]{2,1,0:T(8,128)(2,1)} %refs_3_.5, bf16[8,256,1024]{2,1,0:T(8,128)(2,1)} %refs_4_.9), custom_call_target="tpu_custom_call" | custom-call | flops 8388608 | bytes 1048576 | tf_op jit(solution)/shard_map/attend/pallas_call | solution.py:382
  35.7 0.0 collective-permute-done.7.second_ref.refs_2_
  35.7 0.0 slice-start.3
  35.7 1.6 %collective-permute-start.8 = (bf16[4,64,128]{2,1,0:T(8,128)(2,1)S(1)}, bf16[4,64,128]{2,1,0:T(8,128)(2,1)S(1)}, u32[]{:S(2)}, u32[]{:S(2)}) collective-permute-start(bf16[4,64,128]{2,1,0:T(8,128)(2,1)S(1)} %join.3), channel_id=1, source_target_pairs={{0,2},{2,0},{4,6},{6,4},{8,10},{10,8},{12,14},{14,12},{1,3},{3,1},... | collective-permute-start | bytes 196616 | tf_op jit(solution)/shard_map/ppermute | solution.py:500
  37.3 3.6 %attend.6 = (bf16[2,80,128]{2,1,0:T(8,128)(2,1)S(1)}, bf16[4,8,256,128]{3,2,1,0:T(8,128)(2,1)S(1)}, bf16[4,8,256,128]{3,2,1,0:T(8,128)(2,1)S(1)}) custom-call(s32[1]{0:T(128)} %bitcast.refs_0_, s32[8]{0:T(128)S(1)} %copy-done.2, bf16[2,64,128]{2,1,0:T(8,128)(2,1)S(1)} %collective-permute-done.7.second_ref.refs_2_, bf16[8,256,1024]{2,1,0:T(8,128)(2,1)} %refs_3_.5, ...), custom_call_target="tpu_custom_call" | custom-call | flops 16777216 | bytes 2097152 | tf_op jit(solution)/shard_map/attend/pallas_call | solution.py:382
  40.9 0.0 collective-permute-done.8.refs_2_
  40.9 2.1 %attend.7 = bf16[8,80,128]{2,1,0:T(8,128)(2,1)S(1)} custom-call(s32[1]{0:T(128)} %bitcast.refs_0_, s32[8]{0:T(128)S(1)} %copy-done.2, bf16[4,64,128]{2,1,0:T(8,128)(2,1)S(1)} %collective-permute-done.8.refs_2_, bf16[4,8,256,128]{3,2,1,0:T(8,128)(2,1)S(1)} %get-tuple-element.38.refs_3_, bf16[4,8,256,128]{3,2,1,0:T(8,128)(2,1)S(1)} %get-tuple-element.39.refs_4_, ...), custom_call_target="tpu_custom_call" | custom-call | flops 33554432 | bytes 16777216 | tf_op jit(solution)/shard_map/attend/pallas_call | solution.py:382
  43.0 11.9 %all_to_all.5.parts_ref = bf16[8,80,128]{2,1,0:T(8,128)(2,1)S(1)} all-to-all(bf16[8,80,128]{2,1,0:T(8,128)(2,1)S(1)} %attend.7), channel_id=1, replica_groups=mesh['groups'=2,'tensor'=8,'bank'=2] {'tensor'}, dimensions={0} | all-to-all | bytes 327680 | tf_op jit(solution)/shard_map/all_to_all | solution.py:569
  54.9 0.5 combine.1.refs_1_
  55.4 0.0 slice-done
  55.4 0.0 slice-done.1
  55.4 0.0 slice-done.2
  55.4 0.0 slice-done.3
  55.4 1.2 %output_sent.1 = bf16[4,8,1024]{2,1,0:T(8,128)(2,1)S(1)} custom-call(s32[1]{0:T(128)} %bitcast.refs_0_, bf16[8,1024]{1,0:T(8,128)(2,1)S(1)} %combine.1.refs_1_, bf16[1024,8192]{1,0:T(8,128)(2,1)S(1)} %bitcast.4), custom_call_target="tpu_custom_call" | custom-call | flops 67108864 | bytes 8388608 | tf_op jit(solution)/shard_map/output_sent/pallas_call | solution.py:465
  56.6 0.0 copy-start.1
  56.6 0.1 collective-permute-start.9
  56.8 1.2 %output_kept.1.kept_ref = f32[4,8,1024]{2,1,0:T(8,128)S(1)} custom-call(s32[1]{0:T(128)} %bitcast.refs_0_, bf16[8,1024]{1,0:T(8,128)(2,1)S(1)} %combine.1.refs_1_, bf16[1024,8192]{1,0:T(8,128)(2,1)S(1)} %bitcast.4), custom_call_target="tpu_custom_call" | custom-call | flops 67108864 | bytes 8388608 | tf_op jit(solution)/shard_map/output_kept/pallas_call | solution.py:465
  58.0 2.9 %collective-permute-done.9.came_ref = bf16[4,8,1024]{2,1,0:T(8,128)(2,1)S(1)} collective-permute-done((bf16[4,8,1024]{2,1,0:T(8,128)(2,1)S(1)}, bf16[4,8,1024]{2,1,0:T(8,128)(2,1)S(1)}, u32[]{:S(2)}, u32[]{:S(2)}) %collective-permute-start.9) | collective-permute-done | bytes 65568 | tf_op jit(solution)/shard_map/ppermute | solution.py:500
  60.9 0.1 collective-permute-start.10
  61.0 3.9 %collective-permute-done.10.came_ref = bf16[2,8,1024]{2,1,0:T(8,128)(2,1)S(1)} collective-permute-done((bf16[2,8,1024]{2,1,0:T(8,128)(2,1)S(1)}, bf16[2,8,1024]{2,1,0:T(8,128)(2,1)S(1)}, u32[]{:S(2)}, u32[]{:S(2)}) %collective-permute-start.10) | collective-permute-done | bytes 32800 | tf_op jit(solution)/shard_map/ppermute | solution.py:500
  64.9 0.4 collective-permute-start.11
  65.3 4.3 %collective-permute-done.11.came_ref = bf16[1,8,1024]{2,1,0:T(8,128)(2,1)S(1)} collective-permute-done((bf16[1,8,1024]{2,1,0:T(8,128)(2,1)S(1)}, bf16[1,8,1024]{2,1,0:T(8,128)(2,1)S(1)}, u32[]{:S(2)}, u32[]{:S(2)}) %collective-permute-start.11) | collective-permute-done | bytes 16416 | tf_op jit(solution)/shard_map/ppermute | solution.py:500
  69.6 0.0 copy-done.1
  69.6 0.6 residual.1
  (10 shorter events, 0.1 us)
Async XLA Ops:
  0.0 1.7 %collective-permute-start.1 = (bf16[8,1024]{1,0:T(8,128)(2,1)}, bf16[8,1024]{1,0:T(8,128)(2,1)S(1)}, u32[]{:S(2)}, u32[]{:S(2)}) collective-permute-start(bf16[8,1024]{1,0:T(8,128)(2,1)} %x_ref.1), channel_id=1, source_target_pairs={{0,1},{1,0},{2,3},{3,2},{4,5},{5,4},{6,7},{7,6},{8,9},{9,8},{10,11... | collective-permute-start | bytes 49160 | tf_op jit(solution)/shard_map/ppermute | solution.py:495
  0.5 1.3 %collective-permute-start = (s32[8]{0:T(128)}, s32[8]{0:T(128)S(1)}, u32[]{:S(2)}, u32[]{:S(2)}) collective-permute-start(s32[8]{0:T(128)} %own_index.1), channel_id=1, source_target_pairs={{0,1},{1,0},{2,3},{3,2},{4,5},{5,4},{6,7},{7,6},{8,9},{9,8},{10,11... | collective-permute-start | bytes 104 | tf_op jit(solution)/shard_map/ppermute | solution.py:495
  1.7 6.9 %copy-start.2 = (s32[8]{0:T(128)S(1)}, s32[8]{0:T(128)}, u32[]{:S(2)}) copy-start(s32[8]{0:T(128)} %refs_1_.7) | copy-start | bytes 100
  5.8 8.2 %collective-permute-start.2 = (f32[4,16,768]{2,1,0:T(8,128)S(1)}, f32[4,16,768]{2,1,0:T(8,128)S(1)}, u32[]{:S(2)}, u32[]{:S(2)}) collective-permute-start(f32[4,16,768]{2,1,0:T(8,128)S(1)} %get-tuple-element.28), channel_id=1, source_target_pairs={{0,2},{2,0},{4,6},{6,4},{8,10},{10,8},{12,14},{14,12},{1,3},{3,1},... | collective-permute-start | bytes 589832 | tf_op jit(solution)/shard_map/ppermute | solution.py:500
  8.6 15.1 %copy-start = (bf16[16,64,1024]{2,1,0:T(8,128)(2,1)S(1)}, bf16[16,64,1024]{2,1,0:T(8,128)(2,1)}, u32[]{:S(2)}) copy-start(bf16[16,64,1024]{2,1,0:T(8,128)(2,1)} %up_ref.1) | copy-start | bytes 6291460
  8.6 15.1 %copy-start.3 = (s32[8]{0:T(128)S(1)}, s32[8]{0:T(128)}, u32[]{:S(2)}) copy-start(s32[8]{0:T(128)} %own_index.1) | copy-start | bytes 100
  14.0 4.7 %collective-permute-start.3 = (f32[2,16,768]{2,1,0:T(8,128)S(1)}, f32[2,16,768]{2,1,0:T(8,128)S(1)}, u32[]{:S(2)}, u32[]{:S(2)}) collective-permute-start(f32[2,16,768]{2,1,0:T(8,128)S(1)} %get-tuple-element.30), channel_id=1, source_target_pairs={{0,4},{2,6},{4,0},{6,2},{8,12},{10,14},{12,8},{14,10},{1,5},{3,7},... | collective-permute-start | bytes 294920 | tf_op jit(solution)/shard_map/ppermute | solution.py:500
  18.7 5.1 %collective-permute-start.4 = (f32[1,16,768]{2,1,0:T(8,128)S(1)}, f32[1,16,768]{2,1,0:T(8,128)S(1)}, u32[]{:S(2)}, u32[]{:S(2)}) collective-permute-start(f32[1,16,768]{2,1,0:T(8,128)S(1)} %get-tuple-element.32), channel_id=1, source_target_pairs={{0,8},{2,10},{4,12},{6,14},{8,0},{10,2},{12,4},{14,6},{1,9},{3,11}... | collective-permute-start | bytes 147464 | tf_op jit(solution)/shard_map/ppermute | solution.py:500
  24.7 1.2 %collective-permute-start.5 = (f32[8,1152]{1,0:T(8,128)S(1)}, f32[8,1152]{1,0:T(8,128)S(1)}, u32[]{:S(2)}, u32[]{:S(2)}) collective-permute-start(f32[8,1152]{1,0:T(8,128)S(1)} %get-tuple-element.34), channel_id=1, source_target_pairs={{0,1},{1,0},{2,3},{3,2},{4,5},{5,4},{6,7},{7,6},{8,9},{9,8},{10,11... | collective-permute-start | bytes 110600 | tf_op jit(solution)/shard_map/ppermute | solution.py:495
  26.0 5.4 %collective-permute-start.6 = (bf16[1,64,128]{2,1,0:T(8,128)(2,1)S(1)}, bf16[1,64,128]{2,1,0:T(8,128)(2,1)S(1)}, u32[]{:S(2)}, u32[]{:S(2)}) collective-permute-start(bf16[1,64,128]{2,1,0:T(8,128)(2,1)S(1)} %get-tuple-element.35.refs_2_.first_ref.q_ref), channel_id=1, source_target_pairs={{0,8},{2,10},{4,12},{6,14},{8,0},{10,2},{12,4},{14,6},{1,9},{3,11}... | collective-permute-start | bytes 49160 | tf_op jit(solution)/shard_map/ppermute | solution.py:500
  29.0 26.4 %slice-start = ((s8[16777216]{0:T(1024)(128)(4,1)}), s8[4194304]{0:T(1024)(128)(4,1)S(1)}, s32[]{:S(2)}) async-start(s8[16777216]{0:T(1024)(128)(4,1)} %bitcast.3), calls=%async_computation.1 | async-start | bytes 8388608
  29.0 26.5 %slice-start.1 = ((s8[16777216]{0:T(1024)(128)(4,1)}), s8[4194304]{0:T(1024)(128)(4,1)S(1)}, s32[]{:S(2)}) async-start(s8[16777216]{0:T(1024)(128)(4,1)} %bitcast.3), calls=%async_computation.2 | async-start | bytes 8388608
  31.5 24.0 %slice-start.2 = ((s8[16777216]{0:T(1024)(128)(4,1)}), s8[4194304]{0:T(1024)(128)(4,1)S(1)}, s32[]{:S(2)}) async-start(s8[16777216]{0:T(1024)(128)(4,1)} %bitcast.3), calls=%async_computation.3 | async-start | bytes 8388608
  31.5 4.2 %collective-permute-start.7 = (bf16[2,64,128]{2,1,0:T(8,128)(2,1)S(1)}, bf16[2,64,128]{2,1,0:T(8,128)(2,1)S(1)}, u32[]{:S(2)}, u32[]{:S(2)}) collective-permute-start(bf16[2,64,128]{2,1,0:T(8,128)(2,1)S(1)} %join.2.first_ref), channel_id=1, source_target_pairs={{0,4},{2,6},{4,0},{6,2},{8,12},{10,14},{12,8},{14,10},{1,5},{3,7},... | collective-permute-start | bytes 98312 | tf_op jit(solution)/shard_map/ppermute | solution.py:500
  35.7 19.7 %slice-start.3 = ((s8[16777216]{0:T(1024)(128)(4,1)}), s8[4194304]{0:T(1024)(128)(4,1)S(1)}, s32[]{:S(2)}) async-start(s8[16777216]{0:T(1024)(128)(4,1)} %bitcast.3), calls=%async_computation.4 | async-start | bytes 8388608
  35.7 5.2 %collective-permute-start.8 = (bf16[4,64,128]{2,1,0:T(8,128)(2,1)S(1)}, bf16[4,64,128]{2,1,0:T(8,128)(2,1)S(1)}, u32[]{:S(2)}, u32[]{:S(2)}) collective-permute-start(bf16[4,64,128]{2,1,0:T(8,128)(2,1)S(1)} %join.3), channel_id=1, source_target_pairs={{0,2},{2,0},{4,6},{6,4},{8,10},{10,8},{12,14},{14,12},{1,3},{3,1},... | collective-permute-start | bytes 196616 | tf_op jit(solution)/shard_map/ppermute | solution.py:500
  56.6 13.0 %copy-start.1 = (bf16[8,1024]{1,0:T(8,128)(2,1)S(1)}, bf16[8,1024]{1,0:T(8,128)(2,1)}, u32[]{:S(2)}) copy-start(bf16[8,1024]{1,0:T(8,128)(2,1)} %x_ref.1) | copy-start | bytes 49156
  56.6 4.3 %collective-permute-start.9 = (bf16[4,8,1024]{2,1,0:T(8,128)(2,1)S(1)}, bf16[4,8,1024]{2,1,0:T(8,128)(2,1)S(1)}, u32[]{:S(2)}, u32[]{:S(2)}) collective-permute-start(bf16[4,8,1024]{2,1,0:T(8,128)(2,1)S(1)} %output_sent.1), channel_id=1, source_target_pairs={{0,2},{2,0},{4,6},{6,4},{8,10},{10,8},{12,14},{14,12},{1,3},{3,1},... | collective-permute-start | bytes 196616 | tf_op jit(solution)/shard_map/ppermute | solution.py:500
  60.9 4.0 %collective-permute-start.10 = (bf16[2,8,1024]{2,1,0:T(8,128)(2,1)S(1)}, bf16[2,8,1024]{2,1,0:T(8,128)(2,1)S(1)}, u32[]{:S(2)}, u32[]{:S(2)}) collective-permute-start(bf16[2,8,1024]{2,1,0:T(8,128)(2,1)S(1)} %get-tuple-element.46), channel_id=1, source_target_pairs={{0,4},{2,6},{4,0},{6,2},{8,12},{10,14},{12,8},{14,10},{1,5},{3,7},... | collective-permute-start | bytes 98312 | tf_op jit(solution)/shard_map/ppermute | solution.py:500
  64.9 4.7 %collective-permute-start.11 = (bf16[1,8,1024]{2,1,0:T(8,128)(2,1)S(1)}, bf16[1,8,1024]{2,1,0:T(8,128)(2,1)S(1)}, u32[]{:S(2)}, u32[]{:S(2)}) collective-permute-start(bf16[1,8,1024]{2,1,0:T(8,128)(2,1)S(1)} %get-tuple-element.48), channel_id=1, source_target_pairs={{0,8},{2,10},{4,12},{6,14},{8,0},{10,2},{12,4},{14,6},{1,9},{3,11}... | collective-permute-start | bytes 49160 | tf_op jit(solution)/shard_map/ppermute | solution.py:500

commit v7 on v4

--- a/solution.py
+++ b/solution.py
@@ -67,125 +67,165 @@
     return column - bank * count
 
 
-def project_kernel(first, ranks, place, bank, *refs):
-    if first:
-        own_index, other_index, x_ref, other_ref, w_ref, kv_ref, down_ref, out, inner = refs[:9]
-        w_buf, kv_buf, sems, kv_sems, x_buf, own_smem, other_smem, down_buf, small_sems = refs[9:]
-    else:
-        x_ref, other_ref, w_ref, kv_ref, inner, out = refs[:6]
-        w_buf, kv_buf, sems, kv_sems, x_buf, small_sems = refs[6:]
+def start_slots(parity, ranks, place, bank, w_ref, kv_ref, w_buf, kv_buf, sems, kv_sems):
     count, _, width = w_buf.shape
-    small = [pltpu.make_async_copy(x_ref, x_buf, small_sems.at[0])]
-    if first:
-        small.append(pltpu.make_async_copy(own_index, own_smem, small_sems.at[1]))
-        small.append(pltpu.make_async_copy(other_index, other_smem, small_sems.at[2]))
-    for copy in small:
-        copy.start()
     copies = []
     for s in range(count):
-        target = (2 * s + first) ^ place[0]
+        target = (2 * s + parity) ^ place[0]
         copies.append(
             start_columns(w_ref, (2 * target + bank[0]) * width, w_buf.at[s], sems.at[s])
             + start_columns(
                 kv_ref, (target + ranks * bank[0]) * HEAD_DIM, kv_buf.at[s], kv_sems.at[s]
             )
         )
-    if first:
-        down_copy = pltpu.make_async_copy(down_ref, down_buf, small_sems.at[3])
-        down_copy.start()
-    for copy in small:
-        copy.wait()
-    x = jnp.concatenate([x_buf[...].astype(F32), other_ref[...].astype(F32)], axis=0).astype(BF16)
+    return copies
+
+
+def fetch_kernel(ranks, place, bank, w_ref, kv_ref, down_ref, w_buf, kv_buf, down_buf, *sems):
+    copies = start_slots(1, ranks, place, bank, w_ref, kv_ref, w_buf, kv_buf, *sems[:2])
+    down_copy = pltpu.make_async_copy(down_ref, down_buf, sems[2])
+    down_copy.start()
+    for slot in copies:
+        for copy in slot:
+            copy.wait()
+    down_copy.wait()
+
+
+def slot_buffers(wq, ranks):
+    depth, half = wq.shape[0], ranks // 2
+    return [
+        shape(half, depth, wq.shape[1] // ranks // 2, dtype=BF16),
+        shape(half, depth, HEAD_DIM, dtype=BF16),
+    ]
+
+
+def fetch(place, bank, wq, wkv, down, ranks):
+    dma = pltpu.SemaphoreType.DMA
+    out = slot_buffers(wq, ranks) + [jax.ShapeDtypeStruct(down.shape, BF16)]
+    return pl.pallas_call(
+        lambda *refs: fetch_kernel(ranks, *refs),
+        in_specs=[scalar()] * 2 + [big()] * 3,
+        out_specs=[whole()] * 3,
+        out_shape=out,
+        scratch_shapes=[dma((ranks // 2, CHUNKS)), dma((ranks // 2, CHUNKS)), dma(())],
+        compiler_params=params(),
+        cost_estimate=pl.CostEstimate(
+            flops=0,
+            bytes_accessed=wq.size // 2 + wkv.size // 2 + 2 * down.size,
+            transcendentals=0,
+        ),
+        name="fetch",
+    )(place, bank, wq, wkv, down)
+
+
+def beam_rows(x_ref, other_ref):
+    rows = [x_ref[...].astype(F32), other_ref[...].astype(F32)]
+    return jnp.concatenate(rows, axis=0).astype(BF16)
+
+
+def project_sent_kernel(
+    bank, own_ref, came_ref, x_ref, other_ref, w_buf, kv_buf, down_buf, out, inner, column_out
+):
+    count, _, width = w_buf.shape
+    x = beam_rows(x_ref, other_ref)
+    for s in range(count):
+        out[s, :, :width] = jnp.dot(x, w_buf[s], preferred_element_type=F32)
+        out[s, :, width : width + HEAD_DIM] = jnp.dot(x, kv_buf[s], preferred_element_type=F32)
+    adapters, rank, depth = down_buf.shape
+    every = lax.dot_general(
+        x,
+        down_buf[...].reshape(adapters * rank, depth),
+        (((1,), (1,)), ((), ())),
+        preferred_element_type=F32,
+    )
+    column = adapter_column((own_ref, came_ref), bank[0], adapters)
+    column_out[...] = column
+    lane = iota(column.shape, 1)
+    per = HEAD_DIM // rank
+    total = jnp.zeros(column.shape, F32)
+    for j in range(adapters // per):
+        part = every[:, j * HEAD_DIM : (j + 1) * HEAD_DIM]
+        total += jnp.where(lane // rank + j * per == column, part, 0.0)
+    inner[...] = total
+    for s in range(count):
+        out[s, :, width + HEAD_DIM :] = total
+
+
+def project_sent(bank, index, x, other, weights):
+    half, _, width = weights[0].shape
+    rows = 2 * x.shape[0]
+    return pl.pallas_call(
+        project_sent_kernel,
+        in_specs=[scalar()] * 3 + [whole()] * 5,
+        out_specs=[whole()] * 3,
+        out_shape=[
+            shape(half, rows, width + 2 * HEAD_DIM),
+            shape(rows, HEAD_DIM),
+            shape(rows, HEAD_DIM, dtype=jnp.int32),
+        ],
+        compiler_params=params(),
+        cost_estimate=pl.CostEstimate(
+            flops=2 * rows * sum(w.size for w in weights),
+            bytes_accessed=2 * sum(w.size for w in weights),
+            transcendentals=0,
+        ),
+        name="project_sent",
+    )(bank, *index, x, other, *weights)
+
+
+def project_kept_kernel(
+    ranks, place, bank, length, x_ref, other_ref, w_ref, kv_ref, inner, out, live, *scratch
+):
+    w_buf, kv_buf = scratch[:2]
+    copies = start_slots(0, ranks, place, bank, w_ref, kv_ref, *scratch)
+    count, _, width = w_buf.shape
+    beams = x_ref.shape[0]
+    row = iota(live.shape, 0)
+    limit = jnp.zeros(live.shape, jnp.int32)
+    for beam in range(beams):
+        limit = jnp.where(row // (live.shape[0] // beams) == beam, length[beam], limit)
+    live[...] = limit
+    x = beam_rows(x_ref, other_ref)
     for s in range(count):
         for copy in copies[s]:
             copy.wait()
         out[s, :, :width] = jnp.dot(x, w_buf[s], preferred_element_type=F32)
         out[s, :, width : width + HEAD_DIM] = jnp.dot(x, kv_buf[s], preferred_element_type=F32)
-    if first:
-        down_copy.wait()
-        adapters, rank, depth = down_buf.shape
-        every = lax.dot_general(
-            x,
-            down_buf[...].reshape(adapters * rank, depth),
-            (((1,), (1,)), ((), ())),
-            preferred_element_type=F32,
-        )
-        column = adapter_column((own_smem, other_smem), bank[0], adapters)
-        lane = iota(column.shape, 1)
-        per = HEAD_DIM // rank
-        total = jnp.zeros(column.shape, F32)
-        for j in range(adapters // per):
-            part = every[:, j * HEAD_DIM : (j + 1) * HEAD_DIM]
-            total += jnp.where(lane // rank + j * per == column, part, 0.0)
-        inner[...] = total
-    for s in range(count):
         out[s, :, width + HEAD_DIM :] = inner[...]
 
 
-def project(place, bank, x, other, wq, wkv, ranks, down=None, index=None, inner=None):
-    rows, depth = x.shape
-    first = inner is None
-    width = wq.shape[1] // ranks // 2
-    half = ranks // 2
-    out = [shape(half, 2 * rows, width + 2 * HEAD_DIM)]
+def project_kept(place, bank, length, x, other, wq, wkv, inner, ranks):
+    beams, depth = x.shape
+    rows = 2 * beams
+    buffers = slot_buffers(wq, ranks)
+    half, _, width = buffers[0].shape
     dma = pltpu.SemaphoreType.DMA
-    scratch = [
-        pltpu.VMEM((half, depth, width), BF16),
-        pltpu.VMEM((half, depth, HEAD_DIM), BF16),
-        dma((half, CHUNKS)),
-        dma((half, CHUNKS)),
-        pltpu.VMEM(x.shape, BF16),
-    ]
-    if first:
-        args = (*index, x, other, wq, wkv, down)
-        specs = [big(), pl.BlockSpec(memory_space=pl.ANY), big(), whole(), big(), big(), big()]
-        out.append(shape(2 * rows, HEAD_DIM))
-        scratch += [pltpu.SMEM((rows,), jnp.int32)] * 2
-        scratch += [pltpu.VMEM(down.shape, BF16), dma((4,))]
-    else:
-        args = (x, other, wq, wkv, inner)
-        specs = [big(), whole(), big(), big(), whole()]
-        scratch += [dma((1,))]
-    return pl.pallas_call(
-        lambda *refs: project_kernel(int(first), ranks, *refs),
-        in_specs=[scalar()] * 2 + specs,
-        out_specs=[whole()] * len(out),
-        out_shape=out,
-        scratch_shapes=scratch,
+    return pl.pallas_call(
+        lambda *refs: project_kept_kernel(ranks, *refs),
+        in_specs=[scalar()] * 3 + [whole()] * 2 + [big()] * 2 + [whole()],
+        out_specs=[whole()] * 2,
+        out_shape=[
+            shape(half, rows, width + 2 * HEAD_DIM),
+            shape(beams * wq.shape[1] // ranks // HEAD_DIM, HEAD_DIM, dtype=jnp.int32),
+        ],
+        scratch_shapes=[pltpu.VMEM(b.shape, BF16) for b in buffers]
+        + [dma((half, CHUNKS)), dma((half, CHUNKS))],
         compiler_params=params(),
         cost_estimate=pl.CostEstimate(
-            flops=rows * depth * (wq.shape[1] + wkv.shape[1]),
-            bytes_accessed=(wq.size + wkv.size) // 2,
+            flops=rows * depth * (wq.shape[1] + wkv.shape[1]) // 2,
+            bytes_accessed=wq.size + wkv.size,
             transcendentals=0,
         ),
-        name="project_sent" if first else "project_kept",
-    )(place, bank, *args)
-
-
-def halve_kernel(kept_ref, came_ref, sent_out, kept_out):
-    for i in range(kept_out.shape[0]):
-        for out, j in ((kept_out, 2 * i), (sent_out, 2 * i + 1)):
-            out[i] = (kept_ref[j].astype(F32) + came_ref[j].astype(F32)).astype(out.dtype)
-
-
-def halve(kept, came):
-    half = (kept.shape[0] // 2,) + kept.shape[1:]
-    return pl.pallas_call(
-        halve_kernel,
-        in_specs=[whole()] * 2,
-        out_specs=[whole()] * 2,
-        out_shape=[shape(*half, dtype=came.dtype), shape(*half, dtype=kept.dtype)],
-        compiler_params=params(),
-        name="halve",
-    )(kept, came)
-
-
-def correct_kernel(bank, own_index, other_index, kept_ref, came_ref, up_ref, own_out, other_out):
+        name="project_kept",
+    )(place, bank, length, x, other, wq, wkv, inner)
+
+
+def correct_kernel(bank, column_ref, kept_ref, came_ref, up_ref, own_out, other_out):
     total = kept_ref[0] + came_ref[0]
     count, rank, width = up_ref.shape
     half = width // 2
     inner = total[:, half + HEAD_DIM :].astype(BF16).astype(F32)
-    column = adapter_column((own_index, other_index), bank[0], count)
+    column = column_ref[...]
     lane = iota(column.shape, 1)
     per = HEAD_DIM // rank
     spread = jnp.concatenate(
@@ -208,12 +248,12 @@
     other_out[:, width:] = total[rows:, half : half + HEAD_DIM]
 
 
-def correct(bank, index, kept, came, up):
+def correct(bank, column, kept, came, up):
     rows = kept.shape[1]
     out = shape(rows // 2, up.shape[2] + HEAD_DIM)
     return pl.pallas_call(
         correct_kernel,
-        in_specs=[scalar()] * 3 + [whole()] * 3,
+        in_specs=[scalar()] + [whole()] * 4,
         out_specs=[whole()] * 2,
         out_shape=[out, out],
         compiler_params=params(),
@@ -221,7 +261,25 @@
             flops=2 * rows * up.size, bytes_accessed=2 * up.size, transcendentals=0
         ),
         name="correct",
-    )(bank, *index, kept, came, up)
+    )(bank, column, kept, came, up)
+
+
+def halve_kernel(kept_ref, came_ref, sent_out, kept_out):
+    for i in range(kept_out.shape[0]):
+        kept_out[i] = kept_ref[2 * i] + came_ref[2 * i]
+        sent_out[i] = kept_ref[2 * i + 1] + came_ref[2 * i + 1]
+
+
+def halve(kept, came):
+    half = jax.ShapeDtypeStruct((kept.shape[0] // 2,) + kept.shape[1:], kept.dtype)
+    return pl.pallas_call(
+        halve_kernel,
+        in_specs=[whole()] * 2,
+        out_specs=[whole()] * 2,
+        out_shape=[half, half],
+        compiler_params=params(),
+        name="halve",
+    )(kept, came)
 
 
 def rotate(v, cosine, sine):
@@ -277,46 +335,16 @@
     )(first, second)
 
 
-def fetch_kernel(ref, out, sems):
-    part = ref.shape[0] // sems.shape[0]
-    copies = [
-        pltpu.make_async_copy(
-            ref.at[pl.ds(c * part, part)], out.at[pl.ds(c * part, part)], sems.at[c]
-        )
-        for c in range(sems.shape[0])
-    ]
-    for copy in copies:
-        copy.start()
-    for copy in copies:
-        copy.wait()
-
-
-def fetch(array):
-    return pl.pallas_call(
-        fetch_kernel,
-        in_specs=[big()],
-        out_specs=whole(),
-        out_shape=jax.ShapeDtypeStruct(array.shape, array.dtype),
-        scratch_shapes=[pltpu.SemaphoreType.DMA((4,))],
-        compiler_params=params(),
-        cost_estimate=pl.CostEstimate(
-            flops=0, bytes_accessed=2 * array.size, transcendentals=0
-        ),
-        name="fetch",
-    )(in_hbm(array))
-
-
-def attend_kernel(slots, earlier, place, length, q_ref, k_ref, v_ref, *refs):
+def attend_kernel(slots, earlier, place, length_ref, q_ref, k_ref, v_ref, *refs):
     before, out_ref = refs[:-1], refs[-1]
     beams, positions, _ = k_ref.shape
     rows = q_ref.shape[1]
     group = rows // beams
-    row, lane = iota((rows, positions), 0), iota((rows, positions), 1)
-    limit = jnp.zeros((rows, positions), jnp.int32)
-    for beam in range(beams):
-        limit = jnp.where(row // group == beam, length[beam], limit)
-    live = place[0] * positions + lane < limit
     row, lane = iota((rows, HEAD_DIM), 0), iota((rows, HEAD_DIM), 1)
+    left = length_ref[...] - place[0] * positions
+    live = jnp.concatenate(
+        [lane + first < left for first in range(0, positions, HEAD_DIM)], axis=1
+    )
     for i, slot in enumerate(slots):
         head = place[0] ^ slot
         columns = pl.ds(pl.multiple_of(head * HEAD_DIM, HEAD_DIM), HEAD_DIM)
@@ -351,7 +379,8 @@
         high = stats.astype(BF16).astype(F32)
         middle = (stats - high).astype(BF16).astype(F32)
         low = stats - high - middle
-        block = jnp.concatenate(values + [high, middle, low, jnp.zeros_like(low)], axis=0)
+        tail = high + pltpu.roll(middle, 2 * group, 1) + pltpu.roll(low, 4 * group, 1)
+        block = jnp.concatenate(values + [tail, jnp.zeros_like(tail)], axis=0)
         out_ref[head if earlier else i] = block.astype(BF16)
     if earlier:
         done = [(ref, i) for ref in before for i in range(ref.shape[0])]
@@ -362,16 +391,15 @@
 def attend(place, length, queries, keys, values, slots, earlier=(), before=()):
     count, rows, _ = queries.shape
     beams, positions, _ = keys.shape
-    out = shape(count + len(earlier), rows + 4 * beams, HEAD_DIM, dtype=BF16)
     return pl.pallas_call(
         lambda *refs: attend_kernel(slots, earlier, *refs),
-        in_specs=[scalar()] * 2 + [whole()] * (3 + len(before)),
+        in_specs=[scalar()] + [whole()] * (4 + len(before)),
         out_specs=whole(),
-        out_shape=out,
+        out_shape=shape(count + len(earlier), rows + 2 * beams, HEAD_DIM, dtype=BF16),
         compiler_params=params(),
         cost_estimate=pl.CostEstimate(
             flops=4 * rows * count * positions * HEAD_DIM,
-            bytes_accessed=4 * beams * positions * HEAD_DIM * count,
+            bytes_accessed=4 * beams * positions * HEAD_DIM * (16 if earlier else count),
             transcendentals=rows * count * positions,
         ),
         name="attend",
@@ -395,11 +423,10 @@
     top = score
     for s in range(ranks):
         block = parts_ref[s].astype(F32)
-        tail = by_row(
-            block[rows : rows + beams]
-            + block[rows + beams : rows + 2 * beams]
-            + block[rows + 2 * beams : rows + 3 * beams]
-        )
+        tail = block[rows : rows + beams]
+        for turn in (2, 4):
+            tail += pltpu.roll(block[rows : rows + beams], HEAD_DIM - turn * group, 1)
+        tail = by_row(tail)
         peak = jnp.sum(jnp.where(lane == head, tail, 0.0), axis=1, keepdims=True)
         total = jnp.sum(jnp.where(lane == group + head, tail, 0.0), axis=1, keepdims=True)
         top = jnp.maximum(top, peak)
@@ -432,68 +459,56 @@
     )(parts, query, key_new, value_new)
 
 
-def output_kernel(parity, place, x_ref, w_ref, out, w_buf, sems):
-    count, _, width = w_buf.shape
-    copies = [
-        start_columns(w_ref, ((2 * s + parity) ^ place[0]) * width, w_buf.at[s], sems.at[s])
-        for s in range(count)
-    ]
+def output_kernel(x_ref, w_ref, out):
+    count, _, width = out.shape
     for s in range(count):
-        for copy in copies[s]:
-            copy.wait()
-        total = jnp.dot(x_ref[...], w_buf[s], preferred_element_type=F32)
-        out[s] = total.astype(out.dtype)
-
-
-def output(place, x, weight, ranks, parity, dtype):
-    beams, depth = x.shape
-    width = weight.shape[1] // ranks
-    half = ranks // 2
-    return pl.pallas_call(
-        lambda *refs: output_kernel(parity, *refs),
-        in_specs=[scalar(), whole(), big()],
+        columns = slice(s * width, (s + 1) * width)
+        total = jnp.dot(x_ref[...], w_ref[:, columns], preferred_element_type=F32)
+        out[s] = total.astype(BF16)
+
+
+def output(x, weight, ranks):
+    beams = x.shape[0]
+    return pl.pallas_call(
+        output_kernel,
+        in_specs=[whole()] * 2,
         out_specs=whole(),
-        out_shape=shape(half, beams, width, dtype=dtype),
-        scratch_shapes=[
-            pltpu.VMEM((half, depth, width), BF16),
-            pltpu.SemaphoreType.DMA((half, CHUNKS)),
-        ],
+        out_shape=shape(ranks, beams, weight.shape[1] // ranks, dtype=BF16),
         compiler_params=params(),
         cost_estimate=pl.CostEstimate(
-            flops=beams * weight.size, bytes_accessed=weight.size, transcendentals=0
+            flops=2 * beams * weight.size, bytes_accessed=2 * weight.size, transcendentals=0
         ),
-        name="output_sent" if parity else "output_kept",
-    )(place, x, weight)
-
-
-def residual_kernel(x_ref, kept_ref, came_ref, out_ref):
-    total = kept_ref[0] + came_ref[0].astype(F32)
+        name="output",
+    )(x, weight)
+
+
+def residual_kernel(x_ref, parts_ref, out_ref):
+    total = jnp.sum(parts_ref[...].astype(F32), axis=0)
     out_ref[...] = (x_ref[...].astype(F32) + total).astype(BF16)
 
 
-def residual(x, kept, came):
+def residual(x, parts):
     return pl.pallas_call(
         residual_kernel,
-        in_specs=[whole()] * 3,
+        in_specs=[whole()] * 2,
         out_specs=whole(),
         out_shape=jax.ShapeDtypeStruct(x.shape, BF16),
         compiler_params=params(),
         name="residual",
-    )(x, kept, came)
+    )(x, parts)
 
 
 def swapped(x):
     return lax.ppermute(x, "bank", [(0, 1), (1, 0)])
+
+
+def traded(blocks):
+    return lax.all_to_all(blocks, "tensor", 0, 0, tiled=True)
 
 
 def hop(x, bit):
     ranks = lax.axis_size("tensor")
     return lax.ppermute(x, "tensor", [(i, i ^ bit) for i in range(ranks)])
-
-
-def beside(came, array, sent):
-    array, _ = lax.optimization_barrier((array, sent))
-    return lax.optimization_barrier((came, fetch(array)))
 
 
 def matched_body(
@@ -522,46 +537,30 @@
     sine = jnp.concatenate([-sine, sine], axis=1)
 
     weights = in_hbm(query_weight), in_hbm(keyvalue_weight)
-    place_x = in_hbm(x)
-    sent, inner = project(
-        place,
-        bank,
-        place_x,
-        x_other,
-        *weights,
-        ranks,
-        down=in_hbm(lowrank_down_factors.swapaxes(1, 2)),
-        index=(in_hbm(index[0]), index[1]),
-    )
+    down = in_hbm(lowrank_down_factors.swapaxes(1, 2))
+    odd = fetch(place, bank, *weights, down, ranks)
+    sent, inner, column = project_sent(bank, index, x, x_other, odd)
     came = hop(sent, 1)
-    (kept,) = project(place, bank, place_x, x_other, *weights, ranks, inner=inner)
-    sent, kept = halve(kept, came)
-    came, keys = beside(hop(sent, 2), paged_key_cache, sent)
-    sent, kept = halve(kept, came)
-    came, values = beside(hop(sent, 4), paged_value_cache, sent)
-    own, other = correct(bank, index, kept, came, lowrank_up_factors)
-    query, key_new, value_new = rotated(bank, own, swapped(other), cosine, sine)
-
-    def attended_part(queries, slots, **more):
-        return attend(place, beam_cache_length, queries, keys, values, slots, **more)
-
-    came = hop(query, 4)
-    done = [attended_part(query, (0,))]
-    gathered = join(query, came)
-    second = hop(gathered, 2)
-    done.append(attended_part(came, (4,)))
-    came = hop(join(gathered, second), 1)
-    done.append(attended_part(second, (2, 6)))
-    partial = attended_part(came, (1, 5, 3, 7), earlier=(0, 4, 2, 6), before=done)
-    parts = lax.all_to_all(partial, "tensor", 0, 0, tiled=True)
-    attended = combine(parts, query, key_new, value_new)
-
-    weight = in_hbm(output_weight)
-    came = hop(output(place, attended, weight, ranks, 1, BF16), 1)
-    kept = output(place, attended, weight, ranks, 0, F32)
+    kept, length = project_kept(
+        place, bank, beam_cache_length, x, x_other, *weights, inner, ranks
+    )
     sent, kept = halve(kept, came)
     sent, kept = halve(kept, hop(sent, 2))
-    return residual(x, kept, hop(sent, 4))
+    own, other = correct(bank, column, kept, hop(sent, 4), lowrank_up_factors)
+    query, key_new, value_new = rotated(bank, own, swapped(other), cosine, sine)
+
+    def attended_part(queries, slots, **more):
+        cache = paged_key_cache, paged_value_cache
+        return attend(place, length, queries, *cache, slots, **more)
+
+    came, done = lax.optimization_barrier((hop(query, 4), attended_part(query, (0,))))
+    gathered = join(query, came)
+    second, more = lax.optimization_barrier((hop(gathered, 2), attended_part(came, (4,))))
+    came = hop(join(gathered, second), 1)
+    done = done, more, attended_part(second, (2, 6))
+    partial = attended_part(came, (1, 5, 3, 7), earlier=(0, 4, 2, 6), before=done)
+    attended = combine(traded(partial), query, key_new, value_new)
+    return residual(x, traded(output(attended, output_weight, ranks)))
 
 
 def joined(x, axis, combine):

time: 79.9 us -> 73.9 us (0.925)
  Pallas kernels: 27.4 us -> 16.2 us
  blocking collectives: 10.2 us -> 21.3 us
  waiting for transfers between devices: 19.3 us -> 10.8 us
  starting transfers between devices: 12 us -> 14.8 us
    all_to_all x1 -> x2, blocking collectives: 10.2 us -> 21.3 us  [traded(): return lax.all_to_all(blocks, 'tensor', 0, 0, tiled=True)]
    pallas_call x8 -> x6, Pallas kernels: 21.6 us -> 12.1 us  [the longest x1 3.56 us: project_kept(): pl.pallas_call(lambda *refs: project_kept_kernel(ranks, *refs), in_specs=...]
    ppermute x9 -> x6, waiting for transfers between devices: 17 us -> 9.73 us  [hop(): return lax.ppermute(x, 'tensor', [(i, i ^ bit) for i in range(ranks)])]
    ppermute x9 -> x6, starting transfers between devices: 11.4 us -> 14.3 us  [hop(): return lax.ppermute(x, 'tensor', [(i, i ^ bit) for i in range(ranks)])]
    pallas_call x4, Pallas kernels: 5.4 us -> 3.4 us  [attend(): pl.pallas_call(lambda *refs: attend_kernel(slots, earlier, *refs), in_spe...]
    ppermute x3, waiting for transfers between devices: 2.25 us -> 1.06 us  [swapped(): return lax.ppermute(x, 'bank', [(0, 1), (1, 0)])]
    unnamed x20 -> x18, local copies, waits for them, and re-layouts: 10.4 us -> 10.2 us
  transfers between devices with their start and end apart: 12 -> 9, of which waited for: 8 -> 6; matrix products, arithmetic and copies ran while one was open for 0% -> 0% of each run, Pallas kernels for 19% -> 12%
where the time goes in v7:
time: 73.9 us; the launch traced here: 73.6 us
  blocking collectives  21.3 us (29%)
  Pallas kernels  16.2 us (22%)
  starting transfers between devices  14.8 us (20%)
  waiting for transfers between devices  10.8 us (15%)
  local copies, waits for them, and re-layouts  10.2 us (14%)
    all_to_all x2, blocking collectives, traded(): return lax.all_to_all(blocks, 'tensor', 0, 0, tiled=True)  21.3 us
    ppermute x6, starting transfers between devices, hop(): return lax.ppermute(x, 'tensor', [(i, i ^ bit) for i in range(ranks)])  14.3 us
    unnamed x18, local copies, waits for them, and re-layouts  10.2 us
    ppermute x6, waiting for transfers between devices, hop(): return lax.ppermute(x, 'tensor', [(i, i ^ bit) for i in range(ranks)])  9.73 us
    pallas_call x1, Pallas kernels, project_kept(): pl.pallas_call(lambda *refs: project_kept_kernel(ranks, *refs), in_specs=...  3.56 us
    pallas_call x1, Pallas kernels, fetch(): pl.pallas_call(lambda *refs: fetch_kernel(ranks, *refs), in_specs=[scalar...  3.43 us
    pallas_call x4, Pallas kernels, attend(): pl.pallas_call(lambda *refs: attend_kernel(slots, earlier, *refs), in_spe...  3.4 us
    pallas_call x1, Pallas kernels, output(): pl.pallas_call(output_kernel, in_specs=[whole()] * 2, out_specs=whole(),...  2.28 us
  transfers between devices with their start and end apart: 9, of which 6 were waited for; matrix products, arithmetic and copies ran while one was open for 0% of the time, Pallas kernels for 12%

profile of v7, /device:TPU:0, one launch (start us, length us, event | category | flops | bytes accessed | tf_op | source)
XLA Modules:
  0.0 73.6 jit_solution(16356714729568524891)
XLA Ops:
  0.0 0.5 collective-permute-start
  0.5 0.1 collective-permute-start.1
  0.5 0.0 copy-start.6
  0.5 0.0 copy-start.7
  0.5 3.4 %fetch.1 = (bf16[4,1024,512]{2,1,0:T(8,128)(2,1)S(1)}, bf16[4,1024,128]{2,1,0:T(8,128)(2,1)S(1)}, bf16[16,64,1024]{2,1,0:T(8,128)(2,1)S(1)}) custom-call(s32[1]{0:T(128)} %bitcast.refs_0_, s32[1]{0:T(128)} %bitcast.1.refs_1_.bank, bf16[1024,8192]{1,0:T(8,128)(2,1)} %refs_5_.1, bf16[1024,2048]{1,0:T(8,128)(2,1)} %refs_6_.1, bf16[16,64,1024]{2,1,0:T(8,128)(2,1)} %bitcast.3), custom_call_target="tpu_custom_call" | custom-call | bytes 7340032 | tf_op jit(solution)/shard_map/fetch/pallas_call | solution.py:105
  4.0 0.0 copy-start.8
  4.0 0.0 collective-permute-done.1.came_ref
  4.0 0.0 collective-permute-done.other_ref.refs_4_
  4.0 0.0 copy-done.6
  4.0 0.0 copy-done.7
  4.0 1.9 %project_sent.1 = (f32[4,16,768]{2,1,0:T(8,128)S(1)}, f32[16,128]{1,0:T(8,128)S(1)}, s32[16,128]{1,0:T(8,128)S(1)}) custom-call(s32[1]{0:T(128)} %bitcast.1.refs_1_.bank, s32[8]{0:T(128)S(1)} %copy-done.7, s32[8]{0:T(128)S(1)} %collective-permute-done.1.came_ref, bf16[8,1024]{1,0:T(8,128)(2,1)S(1)} %copy-done.6, ...), custom_call_target="tpu_custom_call" | custom-call | flops 117440512 | bytes 7340032 | tf_op jit(solution)/shard_map/project_sent/pallas_call | solution.py:157
  5.9 3.0 %collective-permute-start.2 = (f32[4,16,768]{2,1,0:T(8,128)S(1)}, f32[4,16,768]{2,1,0:T(8,128)S(1)}, u32[]{:S(2)}, u32[]{:S(2)}) collective-permute-start(f32[4,16,768]{2,1,0:T(8,128)S(1)} %get-tuple-element.33), channel_id=1, source_target_pairs={{0,2},{2,0},{4,6},{6,4},{8,10},{10,8},{12,14},{14,12},{1,3},{3,1},... | collective-permute-start | bytes 589832 | tf_op jit(solution)/shard_map/ppermute | solution.py:511
  8.9 0.0 copy-done.8
  8.9 0.0 copy-start.5
  8.9 3.6 %project_kept.1 = (f32[4,16,768]{2,1,0:T(8,128)S(1)}, s32[64,128]{1,0:T(8,128)S(1)}) custom-call(s32[1]{0:T(128)} %bitcast.refs_0_, s32[1]{0:T(128)} %bitcast.1.refs_1_.bank, s32[8]{0:T(128)S(1)} %copy-done.8, bf16[8,1024]{1,0:T(8,128)(2,1)S(1)} %copy-done.6, bf16[8,1024]{1,0:T(8,128)(2,1)S(1)} %collective-permute-done.other_ref.refs_4_, ...), custom_call_target="tpu_custom_call" | custom-call | flops 83886080 | bytes 10485760 | tf_op jit(solution)/shard_map/project_kept/pallas_call | solution.py:203
  12.4 1.5 %collective-permute-done.2.came_ref = f32[4,16,768]{2,1,0:T(8,128)S(1)} collective-permute-done((f32[4,16,768]{2,1,0:T(8,128)S(1)}, f32[4,16,768]{2,1,0:T(8,128)S(1)}, u32[]{:S(2)}, u32[]{:S(2)}) %collective-permute-start.2) | collective-permute-done | bytes 196640 | tf_op jit(solution)/shard_map/ppermute | solution.py:511
  14.0 1.9 %collective-permute-start.3 = (f32[2,16,768]{2,1,0:T(8,128)S(1)}, f32[2,16,768]{2,1,0:T(8,128)S(1)}, u32[]{:S(2)}, u32[]{:S(2)}) collective-permute-start(f32[2,16,768]{2,1,0:T(8,128)S(1)} %get-tuple-element.35), channel_id=1, source_target_pairs={{0,4},{2,6},{4,0},{6,2},{8,12},{10,14},{12,8},{14,10},{1,5},{3,7},... | collective-permute-start | bytes 294920 | tf_op jit(solution)/shard_map/ppermute | solution.py:511
  15.8 2.8 %collective-permute-done.3.came_ref = f32[2,16,768]{2,1,0:T(8,128)S(1)} collective-permute-done((f32[2,16,768]{2,1,0:T(8,128)S(1)}, f32[2,16,768]{2,1,0:T(8,128)S(1)}, u32[]{:S(2)}, u32[]{:S(2)}) %collective-permute-start.3) | collective-permute-done | bytes 98336 | tf_op jit(solution)/shard_map/ppermute | solution.py:511
  18.7 2.9 %collective-permute-start.4 = (f32[1,16,768]{2,1,0:T(8,128)S(1)}, f32[1,16,768]{2,1,0:T(8,128)S(1)}, u32[]{:S(2)}, u32[]{:S(2)}) collective-permute-start(f32[1,16,768]{2,1,0:T(8,128)S(1)} %get-tuple-element.37), channel_id=1, source_target_pairs={{0,8},{2,10},{4,12},{6,14},{8,0},{10,2},{12,4},{14,6},{1,9},{3,11}... | collective-permute-start | bytes 147464 | tf_op jit(solution)/shard_map/ppermute | solution.py:511
  21.5 0.1 fusion
  21.7 2.1 %collective-permute-done.4.came_ref = f32[1,16,768]{2,1,0:T(8,128)S(1)} collective-permute-done((f32[1,16,768]{2,1,0:T(8,128)S(1)}, f32[1,16,768]{2,1,0:T(8,128)S(1)}, u32[]{:S(2)}, u32[]{:S(2)}) %collective-permute-start.4) | collective-permute-done | bytes 49184 | tf_op jit(solution)/shard_map/ppermute | solution.py:511
  23.7 0.0 copy-done.5
  23.7 0.4 correct.1
  24.1 0.0 collective-permute-start.5
  24.1 0.1 pad_maximum_fusion.sin_ref
  24.2 0.1 tile.10.cos_ref
  24.3 1.1 %collective-permute-done.5.came_ref = f32[8,1152]{1,0:T(8,128)S(1)} collective-permute-done((f32[8,1152]{1,0:T(8,128)S(1)}, f32[8,1152]{1,0:T(8,128)S(1)}, u32[]{:S(2)}, u32[]{:S(2)}) %collective-permute-start.5) | collective-permute-done | bytes 36896 | tf_op jit(solution)/shard_map/ppermute | solution.py:502
  25.3 0.1 rotate.1
  25.4 2.9 %collective-permute-start.6 = (bf16[1,64,128]{2,1,0:T(8,128)(2,1)S(1)}, bf16[1,64,128]{2,1,0:T(8,128)(2,1)S(1)}, u32[]{:S(2)}, u32[]{:S(2)}) collective-permute-start(bf16[1,64,128]{2,1,0:T(8,128)(2,1)S(1)} %get-tuple-element.40.refs_2_.first_ref.q_ref), channel_id=1, source_target_pairs={{0,8},{2,10},{4,12},{6,14},{8,0},{10,2},{12,4},{14,6},{1,9},{3,11}... | collective-permute-start | bytes 49160 | tf_op jit(solution)/shard_map/ppermute | solution.py:511
  28.4 0.0 copy-start
  28.4 2.2 %copy-done = bf16[8,256,1024]{2,1,0:T(8,128)(2,1)S(1)} copy-done((bf16[8,256,1024]{2,1,0:T(8,128)(2,1)S(1)}, bf16[8,256,1024]{2,1,0:T(8,128)(2,1)}, u32[]{:S(2)}) %copy-start) | copy-done | bytes 4194328
  30.5 0.0 copy-start.2
  30.5 2.2 %copy-done.2 = bf16[8,256,1024]{2,1,0:T(8,128)(2,1)S(1)} copy-done((bf16[8,256,1024]{2,1,0:T(8,128)(2,1)S(1)}, bf16[8,256,1024]{2,1,0:T(8,128)(2,1)}, u32[]{:S(2)}) %copy-start.2) | copy-done | bytes 4194328
  32.7 0.0 copy-start.1
  32.7 0.5 attend.4.refs_5_
  33.2 0.0 collective-permute-done.6.second_ref.refs_2_
  33.2 2.0 %collective-permute-start.7 = (bf16[2,64,128]{2,1,0:T(8,128)(2,1)S(1)}, bf16[2,64,128]{2,1,0:T(8,128)(2,1)S(1)}, u32[]{:S(2)}, u32[]{:S(2)}) collective-permute-start(bf16[2,64,128]{2,1,0:T(8,128)(2,1)S(1)} %join.2.first_ref), channel_id=1, source_target_pairs={{0,4},{2,6},{4,0},{6,2},{8,12},{10,14},{12,8},{14,10},{1,5},{3,7},... | collective-permute-start | bytes 98312 | tf_op jit(solution)/shard_map/ppermute | solution.py:511
  35.3 0.0 copy-done.1
  35.3 0.5 attend.5.refs_6_
  35.8 1.5 %collective-permute-done.7.second_ref.refs_2_ = bf16[2,64,128]{2,1,0:T(8,128)(2,1)S(1)} collective-permute-done((bf16[2,64,128]{2,1,0:T(8,128)(2,1)S(1)}, bf16[2,64,128]{2,1,0:T(8,128)(2,1)S(1)}, u32[]{:S(2)}, u32[]{:S(2)}) %collective-permute-start.7) | collective-permute-done | bytes 32800 | tf_op jit(solution)/shard_map/ppermute | solution.py:511
  37.2 0.0 copy-start.3
  37.2 1.6 %collective-permute-start.8 = (bf16[4,64,128]{2,1,0:T(8,128)(2,1)S(1)}, bf16[4,64,128]{2,1,0:T(8,128)(2,1)S(1)}, u32[]{:S(2)}, u32[]{:S(2)}) collective-permute-start(bf16[4,64,128]{2,1,0:T(8,128)(2,1)S(1)} %join.3), channel_id=1, source_target_pairs={{0,2},{2,0},{4,6},{6,4},{8,10},{10,8},{12,14},{14,12},{1,3},{3,1},... | collective-permute-start | bytes 196616 | tf_op jit(solution)/shard_map/ppermute | solution.py:511
  38.8 0.8 %attend.6.refs_7_ = bf16[2,80,128]{2,1,0:T(8,128)(2,1)S(1)} custom-call(s32[1]{0:T(128)} %bitcast.refs_0_, s32[64,128]{1,0:T(8,128)S(1)} %get-tuple-element.30.refs_1_, bf16[2,64,128]{2,1,0:T(8,128)(2,1)S(1)} %collective-permute-done.7.second_ref.refs_2_, bf16[8,256,1024]{2,1,0:T(8,128)(2,1)S(1)} %copy-done.1, bf16[8,256,1024]{2,1,0:T(8,128)(2,1)S(1)} %copy-done.2), custom_call_target="tpu_custom_call" | custom-call | flops 16777216 | bytes 2097152 | tf_op jit(solution)/shard_map/attend/pallas_call | solution.py:394
  39.7 1.9 %collective-permute-done.8.refs_2_ = bf16[4,64,128]{2,1,0:T(8,128)(2,1)S(1)} collective-permute-done((bf16[4,64,128]{2,1,0:T(8,128)(2,1)S(1)}, bf16[4,64,128]{2,1,0:T(8,128)(2,1)S(1)}, u32[]{:S(2)}, u32[]{:S(2)}) %collective-permute-start.8) | collective-permute-done | bytes 65568 | tf_op jit(solution)/shard_map/ppermute | solution.py:511
  41.6 0.0 copy-done.3
  41.6 1.6 %attend.7 = bf16[8,80,128]{2,1,0:T(8,128)(2,1)S(1)} custom-call(s32[1]{0:T(128)} %bitcast.refs_0_, s32[64,128]{1,0:T(8,128)S(1)} %get-tuple-element.30.refs_1_, bf16[4,64,128]{2,1,0:T(8,128)(2,1)S(1)} %collective-permute-done.8.refs_2_, bf16[8,256,1024]{2,1,0:T(8,128)(2,1)S(1)} %copy-done.1, bf16[8,256,1024]{2,1,0:T(8,128)(2,1)S(1)} %copy-done.3, ...), custom_call_target="tpu_custom_call" | custom-call | flops 33554432 | bytes 16777216 | tf_op jit(solution)/shard_map/attend/pallas_call | solution.py:394
  43.1 11.5 %all_to_all.10.parts_ref = bf16[8,80,128]{2,1,0:T(8,128)(2,1)S(1)} all-to-all(bf16[8,80,128]{2,1,0:T(8,128)(2,1)S(1)} %attend.7), channel_id=1, replica_groups=mesh['groups'=2,'tensor'=8,'bank'=2] {'tensor'}, dimensions={0} | all-to-all | bytes 327680 | tf_op jit(solution)/shard_map/all_to_all | solution.py:506
  54.7 0.5 combine.1.x_ref
  55.2 0.0 copy-start.4
  55.2 5.8 %copy-done.4 = bf16[1024,8192]{1,0:T(8,128)(2,1)S(1)} copy-done((bf16[1024,8192]{1,0:T(8,128)(2,1)S(1)}, bf16[1024,8192]{1,0:T(8,128)(2,1)}, u32[]{:S(2)}) %copy-start.4) | copy-done | bytes 16777240
  60.9 2.3 %output.1 = bf16[8,8,1024]{2,1,0:T(8,128)(2,1)S(1)} custom-call(bf16[8,1024]{1,0:T(8,128)(2,1)S(1)} %combine.1.x_ref, bf16[1024,8192]{1,0:T(8,128)(2,1)S(1)} %copy-done.4), custom_call_target="tpu_custom_call" | custom-call | flops 134217728 | bytes 16777216 | tf_op jit(solution)/shard_map/output/pallas_call | solution.py:472
  63.2 9.7 %all_to_all.11.parts_ref = bf16[8,8,1024]{2,1,0:T(8,128)(2,1)S(1)} all-to-all(bf16[8,8,1024]{2,1,0:T(8,128)(2,1)S(1)} %output.1), channel_id=1, replica_groups=mesh['groups'=2,'tensor'=8,'bank'=2] {'tensor'}, dimensions={0} | all-to-all | bytes 262144 | tf_op jit(solution)/shard_map/all_to_all | solution.py:506
  73.0 0.6 residual.1
  (7 shorter events, 0.1 us)
Async XLA Ops:
  0.0 4.0 %collective-permute-start = (bf16[8,1024]{1,0:T(8,128)(2,1)}, bf16[8,1024]{1,0:T(8,128)(2,1)S(1)}, u32[]{:S(2)}, u32[]{:S(2)}) collective-permute-start(bf16[8,1024]{1,0:T(8,128)(2,1)} %x_ref.3), channel_id=1, source_target_pairs={{0,1},{1,0},{2,3},{3,2},{4,5},{5,4},{6,7},{7,6},{8,9},{9,8},{10,11... | collective-permute-start | bytes 49160 | tf_op jit(solution)/shard_map/ppermute | solution.py:502
  0.5 3.5 %collective-permute-start.1 = (s32[8]{0:T(128)}, s32[8]{0:T(128)S(1)}, u32[]{:S(2)}, u32[]{:S(2)}) collective-permute-start(s32[8]{0:T(128)} %own_ref.1), channel_id=1, source_target_pairs={{0,1},{1,0},{2,3},{3,2},{4,5},{5,4},{6,7},{7,6},{8,9},{9,8},{10,11... | collective-permute-start | bytes 104 | tf_op jit(solution)/shard_map/ppermute | solution.py:502
  0.5 3.5 %copy-start.6 = (bf16[8,1024]{1,0:T(8,128)(2,1)S(1)}, bf16[8,1024]{1,0:T(8,128)(2,1)}, u32[]{:S(2)}) copy-start(bf16[8,1024]{1,0:T(8,128)(2,1)} %x_ref.3) | copy-start | bytes 49156
  0.5 3.5 %copy-start.7 = (s32[8]{0:T(128)S(1)}, s32[8]{0:T(128)}, u32[]{:S(2)}) copy-start(s32[8]{0:T(128)} %own_ref.1) | copy-start | bytes 100
  4.0 4.9 %copy-start.8 = (s32[8]{0:T(128)S(1)}, s32[8]{0:T(128)}, u32[]{:S(2)}) copy-start(s32[8]{0:T(128)} %refs_2_.3) | copy-start | bytes 100
  5.9 8.1 %collective-permute-start.2 = (f32[4,16,768]{2,1,0:T(8,128)S(1)}, f32[4,16,768]{2,1,0:T(8,128)S(1)}, u32[]{:S(2)}, u32[]{:S(2)}) collective-permute-start(f32[4,16,768]{2,1,0:T(8,128)S(1)} %get-tuple-element.33), channel_id=1, source_target_pairs={{0,2},{2,0},{4,6},{6,4},{8,10},{10,8},{12,14},{14,12},{1,3},{3,1},... | collective-permute-start | bytes 589832 | tf_op jit(solution)/shard_map/ppermute | solution.py:511
  8.9 14.8 %copy-start.5 = (bf16[16,64,1024]{2,1,0:T(8,128)(2,1)S(1)}, bf16[16,64,1024]{2,1,0:T(8,128)(2,1)}, u32[]{:S(2)}) copy-start(bf16[16,64,1024]{2,1,0:T(8,128)(2,1)} %up_ref.1) | copy-start | bytes 6291460
  14.0 4.7 %collective-permute-start.3 = (f32[2,16,768]{2,1,0:T(8,128)S(1)}, f32[2,16,768]{2,1,0:T(8,128)S(1)}, u32[]{:S(2)}, u32[]{:S(2)}) collective-permute-start(f32[2,16,768]{2,1,0:T(8,128)S(1)} %get-tuple-element.35), channel_id=1, source_target_pairs={{0,4},{2,6},{4,0},{6,2},{8,12},{10,14},{12,8},{14,10},{1,5},{3,7},... | collective-permute-start | bytes 294920 | tf_op jit(solution)/shard_map/ppermute | solution.py:511
  18.7 5.1 %collective-permute-start.4 = (f32[1,16,768]{2,1,0:T(8,128)S(1)}, f32[1,16,768]{2,1,0:T(8,128)S(1)}, u32[]{:S(2)}, u32[]{:S(2)}) collective-permute-start(f32[1,16,768]{2,1,0:T(8,128)S(1)} %get-tuple-element.37), channel_id=1, source_target_pairs={{0,8},{2,10},{4,12},{6,14},{8,0},{10,2},{12,4},{14,6},{1,9},{3,11}... | collective-permute-start | bytes 147464 | tf_op jit(solution)/shard_map/ppermute | solution.py:511
  24.1 1.2 %collective-permute-start.5 = (f32[8,1152]{1,0:T(8,128)S(1)}, f32[8,1152]{1,0:T(8,128)S(1)}, u32[]{:S(2)}, u32[]{:S(2)}) collective-permute-start(f32[8,1152]{1,0:T(8,128)S(1)} %get-tuple-element.39), channel_id=1, source_target_pairs={{0,1},{1,0},{2,3},{3,2},{4,5},{5,4},{6,7},{7,6},{8,9},{9,8},{10,11... | collective-permute-start | bytes 110600 | tf_op jit(solution)/shard_map/ppermute | solution.py:502
  25.4 7.8 %collective-permute-start.6 = (bf16[1,64,128]{2,1,0:T(8,128)(2,1)S(1)}, bf16[1,64,128]{2,1,0:T(8,128)(2,1)S(1)}, u32[]{:S(2)}, u32[]{:S(2)}) collective-permute-start(bf16[1,64,128]{2,1,0:T(8,128)(2,1)S(1)} %get-tuple-element.40.refs_2_.first_ref.q_ref), channel_id=1, source_target_pairs={{0,8},{2,10},{4,12},{6,14},{8,0},{10,2},{12,4},{14,6},{1,9},{3,11}... | collective-permute-start | bytes 49160 | tf_op jit(solution)/shard_map/ppermute | solution.py:511
  28.4 2.2 %copy-start = (bf16[8,256,1024]{2,1,0:T(8,128)(2,1)S(1)}, bf16[8,256,1024]{2,1,0:T(8,128)(2,1)}, u32[]{:S(2)}) copy-start(bf16[8,256,1024]{2,1,0:T(8,128)(2,1)} %refs_3_.11) | copy-start | bytes 12582916
  30.5 2.2 %copy-start.2 = (bf16[8,256,1024]{2,1,0:T(8,128)(2,1)S(1)}, bf16[8,256,1024]{2,1,0:T(8,128)(2,1)}, u32[]{:S(2)}) copy-start(bf16[8,256,1024]{2,1,0:T(8,128)(2,1)} %refs_4_.7) | copy-start | bytes 12582916
  32.7 2.5 %copy-start.1 = (bf16[8,256,1024]{2,1,0:T(8,128)(2,1)S(1)}, bf16[8,256,1024]{2,1,0:T(8,128)(2,1)}, u32[]{:S(2)}) copy-start(bf16[8,256,1024]{2,1,0:T(8,128)(2,1)} %refs_3_.11) | copy-start | bytes 12582916
  33.2 4.0 %collective-permute-start.7 = (bf16[2,64,128]{2,1,0:T(8,128)(2,1)S(1)}, bf16[2,64,128]{2,1,0:T(8,128)(2,1)S(1)}, u32[]{:S(2)}, u32[]{:S(2)}) collective-permute-start(bf16[2,64,128]{2,1,0:T(8,128)(2,1)S(1)} %join.2.first_ref), channel_id=1, source_target_pairs={{0,4},{2,6},{4,0},{6,2},{8,12},{10,14},{12,8},{14,10},{1,5},{3,7},... | collective-permute-start | bytes 98312 | tf_op jit(solution)/shard_map/ppermute | solution.py:511
  37.2 4.3 %copy-start.3 = (bf16[8,256,1024]{2,1,0:T(8,128)(2,1)S(1)}, bf16[8,256,1024]{2,1,0:T(8,128)(2,1)}, u32[]{:S(2)}) copy-start(bf16[8,256,1024]{2,1,0:T(8,128)(2,1)} %refs_4_.7) | copy-start | bytes 12582916
  37.2 4.3 %collective-permute-start.8 = (bf16[4,64,128]{2,1,0:T(8,128)(2,1)S(1)}, bf16[4,64,128]{2,1,0:T(8,128)(2,1)S(1)}, u32[]{:S(2)}, u32[]{:S(2)}) collective-permute-start(bf16[4,64,128]{2,1,0:T(8,128)(2,1)S(1)} %join.3), channel_id=1, source_target_pairs={{0,2},{2,0},{4,6},{6,4},{8,10},{10,8},{12,14},{14,12},{1,3},{3,1},... | collective-permute-start | bytes 196616 | tf_op jit(solution)/shard_map/ppermute | solution.py:511
  55.2 5.8 %copy-start.4 = (bf16[1024,8192]{1,0:T(8,128)(2,1)S(1)}, bf16[1024,8192]{1,0:T(8,128)(2,1)}, u32[]{:S(2)}) copy-start(bf16[1024,8192]{1,0:T(8,128)(2,1)} %w_ref.1) | copy-start | bytes 50331652

commit v8 on v7

--- a/solution.py
+++ b/solution.py
@@ -9,7 +9,7 @@
 F32 = jnp.float32
 BF16 = jnp.bfloat16
 CHUNKS = 2
-VMEM_LIMIT = 24 * 1024 * 1024
+MIB = 1024 * 1024
 
 
 def whole():
@@ -36,8 +36,8 @@
     return lax.broadcasted_iota(jnp.int32, dims, axis)
 
 
-def params(**more):
-    return pltpu.CompilerParams(vmem_limit_bytes=VMEM_LIMIT, **more)
+def params(mib=4):
+    return pltpu.CompilerParams(vmem_limit_bytes=mib * MIB)
 
 
 def start_columns(weight, column, target, sems):
@@ -67,11 +67,11 @@
     return column - bank * count
 
 
-def start_slots(parity, ranks, place, bank, w_ref, kv_ref, w_buf, kv_buf, sems, kv_sems):
+def start_slots(parity, first, ranks, place, bank, w_ref, kv_ref, w_buf, kv_buf, sems, kv_sems):
     count, _, width = w_buf.shape
     copies = []
     for s in range(count):
-        target = (2 * s + parity) ^ place[0]
+        target = (2 * (first + s) + parity) ^ place[0]
         copies.append(
             start_columns(w_ref, (2 * target + bank[0]) * width, w_buf.at[s], sems.at[s])
             + start_columns(
@@ -81,38 +81,42 @@
     return copies
 
 
-def fetch_kernel(ranks, place, bank, w_ref, kv_ref, down_ref, w_buf, kv_buf, down_buf, *sems):
-    copies = start_slots(1, ranks, place, bank, w_ref, kv_ref, w_buf, kv_buf, *sems[:2])
-    down_copy = pltpu.make_async_copy(down_ref, down_buf, sems[2])
-    down_copy.start()
+def wait_all(copies):
     for slot in copies:
         for copy in slot:
             copy.wait()
+
+
+def fetch_kernel(ranks, place, bank, w_ref, kv_ref, down_ref, w_buf, kv_buf, down_buf, *sems):
+    down_copy = pltpu.make_async_copy(down_ref, down_buf, sems[2])
+    down_copy.start()
+    wait_all(start_slots(1, 0, ranks, place, bank, w_ref, kv_ref, w_buf, kv_buf, *sems[:2]))
     down_copy.wait()
 
 
-def slot_buffers(wq, ranks):
-    depth, half = wq.shape[0], ranks // 2
+def slot_buffers(wq, ranks, count):
+    depth = wq.shape[0]
     return [
-        shape(half, depth, wq.shape[1] // ranks // 2, dtype=BF16),
-        shape(half, depth, HEAD_DIM, dtype=BF16),
+        shape(count, depth, wq.shape[1] // ranks // 2, dtype=BF16),
+        shape(count, depth, HEAD_DIM, dtype=BF16),
     ]
 
 
+def slot_sems(count):
+    return [pltpu.SemaphoreType.DMA((count, CHUNKS))] * 2
+
+
 def fetch(place, bank, wq, wkv, down, ranks):
-    dma = pltpu.SemaphoreType.DMA
-    out = slot_buffers(wq, ranks) + [jax.ShapeDtypeStruct(down.shape, BF16)]
+    out = slot_buffers(wq, ranks, 1) + [jax.ShapeDtypeStruct(down.shape, BF16)]
     return pl.pallas_call(
         lambda *refs: fetch_kernel(ranks, *refs),
         in_specs=[scalar()] * 2 + [big()] * 3,
         out_specs=[whole()] * 3,
         out_shape=out,
-        scratch_shapes=[dma((ranks // 2, CHUNKS)), dma((ranks // 2, CHUNKS)), dma(())],
+        scratch_shapes=slot_sems(1) + [pltpu.SemaphoreType.DMA(())],
         compiler_params=params(),
         cost_estimate=pl.CostEstimate(
-            flops=0,
-            bytes_accessed=wq.size // 2 + wkv.size // 2 + 2 * down.size,
-            transcendentals=0,
+            flops=0, bytes_accessed=2 * sum(o.size for o in out), transcendentals=0
         ),
         name="fetch",
     )(place, bank, wq, wkv, down)
@@ -123,14 +127,18 @@
     return jnp.concatenate(rows, axis=0).astype(BF16)
 
 
-def project_sent_kernel(
-    bank, own_ref, came_ref, x_ref, other_ref, w_buf, kv_buf, down_buf, out, inner, column_out
-):
-    count, _, width = w_buf.shape
+def project_slot(x, w, kv, out):
+    width = w.shape[1]
+    out[:, :width] = jnp.dot(x, w[...], preferred_element_type=F32)
+    out[:, width : width + HEAD_DIM] = jnp.dot(x, kv[...], preferred_element_type=F32)
+
+
+def project_sent_kernel(ranks, place, bank, own_ref, came_ref, *refs):
+    x_ref, other_ref, w_ref, kv_ref, w_first, kv_first, down_buf, out, inner, column_out = refs[:10]
+    w_buf, kv_buf = refs[10:12]
+    copies = start_slots(1, 1, ranks, place, bank, w_ref, kv_ref, *refs[10:])
+    width = w_first.shape[2]
     x = beam_rows(x_ref, other_ref)
-    for s in range(count):
-        out[s, :, :width] = jnp.dot(x, w_buf[s], preferred_element_type=F32)
-        out[s, :, width : width + HEAD_DIM] = jnp.dot(x, kv_buf[s], preferred_element_type=F32)
     adapters, rank, depth = down_buf.shape
     every = lax.dot_general(
         x,
@@ -147,38 +155,43 @@
         part = every[:, j * HEAD_DIM : (j + 1) * HEAD_DIM]
         total += jnp.where(lane // rank + j * per == column, part, 0.0)
     inner[...] = total
-    for s in range(count):
+    for s in range(out.shape[0]):
         out[s, :, width + HEAD_DIM :] = total
-
-
-def project_sent(bank, index, x, other, weights):
-    half, _, width = weights[0].shape
-    rows = 2 * x.shape[0]
-    return pl.pallas_call(
-        project_sent_kernel,
-        in_specs=[scalar()] * 3 + [whole()] * 5,
+    project_slot(x, w_first.at[0], kv_first.at[0], out.at[0])
+    for s, slot in enumerate(copies):
+        wait_all([slot])
+        project_slot(x, w_buf.at[s], kv_buf.at[s], out.at[s + 1])
+
+
+def project_sent(place, bank, index, x, other, wq, wkv, ahead, ranks):
+    rows, half = 2 * x.shape[0], ranks // 2
+    buffers = slot_buffers(wq, ranks, half - 1)
+    return pl.pallas_call(
+        lambda *refs: project_sent_kernel(ranks, *refs),
+        in_specs=[scalar()] * 4 + [whole()] * 2 + [big()] * 2 + [whole()] * 3,
         out_specs=[whole()] * 3,
         out_shape=[
-            shape(half, rows, width + 2 * HEAD_DIM),
+            shape(half, rows, wq.shape[1] // ranks // 2 + 2 * HEAD_DIM),
             shape(rows, HEAD_DIM),
             shape(rows, HEAD_DIM, dtype=jnp.int32),
         ],
-        compiler_params=params(),
+        scratch_shapes=[pltpu.VMEM(b.shape, BF16) for b in buffers] + slot_sems(half - 1),
+        compiler_params=params(8),
         cost_estimate=pl.CostEstimate(
-            flops=2 * rows * sum(w.size for w in weights),
-            bytes_accessed=2 * sum(w.size for w in weights),
+            flops=rows * (wq.size + wkv.size) // 2,
+            bytes_accessed=(wq.size + wkv.size) // 2,
             transcendentals=0,
         ),
         name="project_sent",
-    )(bank, *index, x, other, *weights)
+    )(place, bank, *index, x, other, wq, wkv, *ahead)
 
 
 def project_kept_kernel(
     ranks, place, bank, length, x_ref, other_ref, w_ref, kv_ref, inner, out, live, *scratch
 ):
     w_buf, kv_buf = scratch[:2]
-    copies = start_slots(0, ranks, place, bank, w_ref, kv_ref, *scratch)
-    count, _, width = w_buf.shape
+    copies = start_slots(0, 0, ranks, place, bank, w_ref, kv_ref, *scratch)
+    width = w_buf.shape[2]
     beams = x_ref.shape[0]
     row = iota(live.shape, 0)
     limit = jnp.zeros(live.shape, jnp.int32)
@@ -186,31 +199,27 @@
         limit = jnp.where(row // (live.shape[0] // beams) == beam, length[beam], limit)
     live[...] = limit
     x = beam_rows(x_ref, other_ref)
-    for s in range(count):
-        for copy in copies[s]:
-            copy.wait()
-        out[s, :, :width] = jnp.dot(x, w_buf[s], preferred_element_type=F32)
-        out[s, :, width : width + HEAD_DIM] = jnp.dot(x, kv_buf[s], preferred_element_type=F32)
+    for s, slot in enumerate(copies):
+        wait_all([slot])
+        project_slot(x, w_buf.at[s], kv_buf.at[s], out.at[s])
         out[s, :, width + HEAD_DIM :] = inner[...]
 
 
 def project_kept(place, bank, length, x, other, wq, wkv, inner, ranks):
     beams, depth = x.shape
     rows = 2 * beams
-    buffers = slot_buffers(wq, ranks)
-    half, _, width = buffers[0].shape
-    dma = pltpu.SemaphoreType.DMA
+    half = ranks // 2
+    buffers = slot_buffers(wq, ranks, half)
     return pl.pallas_call(
         lambda *refs: project_kept_kernel(ranks, *refs),
         in_specs=[scalar()] * 3 + [whole()] * 2 + [big()] * 2 + [whole()],
         out_specs=[whole()] * 2,
         out_shape=[
-            shape(half, rows, width + 2 * HEAD_DIM),
+            shape(half, rows, buffers[0].shape[2] + 2 * HEAD_DIM),
             shape(beams * wq.shape[1] // ranks // HEAD_DIM, HEAD_DIM, dtype=jnp.int32),
         ],
-        scratch_shapes=[pltpu.VMEM(b.shape, BF16) for b in buffers]
-        + [dma((half, CHUNKS)), dma((half, CHUNKS))],
-        compiler_params=params(),
+        scratch_shapes=[pltpu.VMEM(b.shape, BF16) for b in buffers] + slot_sems(half),
+        compiler_params=params(8),
         cost_estimate=pl.CostEstimate(
             flops=rows * depth * (wq.shape[1] + wkv.shape[1]) // 2,
             bytes_accessed=wq.size + wkv.size,
@@ -529,17 +538,18 @@
     bank = lax.axis_index("bank").astype(jnp.int32).reshape(1)
     index = (beam_adapter_index, swapped(beam_adapter_index))
     x_other = swapped(x)
+    lane = jnp.arange(HEAD_DIM, dtype=jnp.int32)
     half = HEAD_DIM // 2
-    frequency = jnp.power(500000.0, -2.0 * jnp.arange(half, dtype=F32) / HEAD_DIM)
+    frequency = jnp.power(500000.0, -2.0 * (lane % half).astype(F32) / HEAD_DIM)
     angles = beam_cache_length.astype(F32)[:, None] * frequency[None, :]
-    cosine = jnp.tile(jnp.cos(angles), (1, 2))
-    sine = jnp.sin(angles)
-    sine = jnp.concatenate([-sine, sine], axis=1)
-
+    cosine = jnp.cos(angles)
+    sine = jnp.where(lane < half, -1.0, 1.0) * jnp.sin(angles)
     weights = in_hbm(query_weight), in_hbm(keyvalue_weight)
     down = in_hbm(lowrank_down_factors.swapaxes(1, 2))
-    odd = fetch(place, bank, *weights, down, ranks)
-    sent, inner, column = project_sent(bank, index, x, x_other, odd)
+    ahead = fetch(place, bank, *weights, down, ranks)
+    sent, inner, column = project_sent(
+        place, bank, index, x, x_other, *weights, ahead, ranks
+    )
     came = hop(sent, 1)
     kept, length = project_kept(
         place, bank, beam_cache_length, x, x_other, *weights, inner, ranks

time: 73.9 us -> 67.6 us (0.915)
  local copies, waits for them, and re-layouts: 10.2 us -> 0.04 us
  blocking collectives: 21.3 us -> 23.6 us
  waiting for transfers between devices: 10.8 us -> 11.9 us
    unnamed x18 -> x20, local copies, waits for them, and re-layouts: 10.2 us -> 0.04 us
    all_to_all x2, blocking collectives: 21.3 us -> 23.6 us  [traded(): return lax.all_to_all(blocks, 'tensor', 0, 0, tiled=True)]
    pallas_call x1, Pallas kernels: 1.86 us -> 3.72 us  [project_sent(): pl.pallas_call(lambda *refs: project_sent_kernel(ranks, *refs), in_specs=...]
    pallas_call x1, Pallas kernels: 3.43 us -> 1.97 us  [fetch(): pl.pallas_call(lambda *refs: fetch_kernel(ranks, *refs), in_specs=[scalar...]
    ppermute x6, waiting for transfers between devices: 9.73 us -> 10.8 us  [hop(): return lax.ppermute(x, 'tensor', [(i, i ^ bit) for i in range(ranks)])]
  transfers between devices with their start and end apart: 9 -> 9, of which waited for: 6 -> 7; matrix products, arithmetic and copies ran while one was open for 0% -> 0% of each run, Pallas kernels for 12% -> 11%
where the time goes in v8:
time: 67.6 us; the launch traced here: 67.4 us
  blocking collectives  23.6 us (35%)
  Pallas kernels  16.7 us (25%)
  starting transfers between devices  14.9 us (22%)
  waiting for transfers between devices  11.9 us (18%)
    all_to_all x2, blocking collectives, traded(): return lax.all_to_all(blocks, 'tensor', 0, 0, tiled=True)  23.6 us
    ppermute x6, starting transfers between devices, hop(): return lax.ppermute(x, 'tensor', [(i, i ^ bit) for i in range(ranks)])  14.4 us
    ppermute x6, waiting for transfers between devices, hop(): return lax.ppermute(x, 'tensor', [(i, i ^ bit) for i in range(ranks)])  10.8 us
    pallas_call x1, Pallas kernels, project_kept(): pl.pallas_call(lambda *refs: project_kept_kernel(ranks, *refs), in_specs=...  3.73 us
    pallas_call x1, Pallas kernels, project_sent(): pl.pallas_call(lambda *refs: project_sent_kernel(ranks, *refs), in_specs=...  3.72 us
    pallas_call x4, Pallas kernels, attend(): pl.pallas_call(lambda *refs: attend_kernel(slots, earlier, *refs), in_spe...  3.4 us
    pallas_call x1, Pallas kernels, output(): pl.pallas_call(output_kernel, in_specs=[whole()] * 2, out_specs=whole(),...  2.28 us
    pallas_call x1, Pallas kernels, fetch(): pl.pallas_call(lambda *refs: fetch_kernel(ranks, *refs), in_specs=[scalar...  1.97 us
  transfers between devices with their start and end apart: 9, of which 7 were waited for; matrix products, arithmetic and copies ran while one was open for 0% of the time, Pallas kernels for 11%

profile of v8, /device:TPU:0, one launch (start us, length us, event | category | flops | bytes accessed | tf_op | source)
XLA Modules:
  0.0 67.4 jit_solution(4556469002343290316)
XLA Ops:
  0.0 0.5 collective-permute-start
  0.5 0.1 collective-permute-start.1
  0.5 0.0 copy-start.3
  0.5 0.0 copy-start.4
  0.5 2.0 %fetch.1 = (bf16[1,1024,512]{2,1,0:T(8,128)(2,1)S(1)}, bf16[1,1024,128]{2,1,0:T(8,128)(2,1)S(1)}, bf16[16,64,1024]{2,1,0:T(8,128)(2,1)S(1)}) custom-call(s32[1]{0:T(128)} %bitcast.refs_0_, s32[1]{0:T(128)} %bitcast.1.refs_1_.bank, bf16[1024,8192]{1,0:T(8,128)(2,1)} %refs_5_.1, bf16[1024,2048]{1,0:T(8,128)(2,1)} %refs_6_.3, bf16[16,64,1024]{2,1,0:T(8,128)(2,1)} %bitcast.5), custom_call_target="tpu_custom_call" | custom-call | bytes 3407872 | tf_op jit(solution)/shard_map/fetch/pallas_call | solution.py:111
  2.5 0.0 collective-permute-done.1.refs_3_
  2.5 0.0 collective-permute-done.refs_5_.refs_4_
  2.5 0.0 copy-done.3
  2.5 0.0 copy-done.4
  2.5 0.0 copy-start.5
  2.6 3.7 %project_sent.1 = (f32[4,16,768]{2,1,0:T(8,128)S(1)}, f32[16,128]{1,0:T(8,128)S(1)}, s32[16,128]{1,0:T(8,128)S(1)}) custom-call(s32[1]{0:T(128)} %bitcast.refs_0_, s32[1]{0:T(128)} %bitcast.1.refs_1_.bank, s32[8]{0:T(128)S(1)} %copy-done.4, s32[8]{0:T(128)S(1)} %collective-permute-done.1.refs_3_, bf16[8,1024]{1,0:T(8,128)(2,1)S(1)} %copy-done.3, ...), custom_call_target="tpu_custom_call" | custom-call | flops 83886080 | bytes 5242880 | tf_op jit(solution)/shard_map/project_sent/pallas_call | solution.py:169
  6.3 3.0 %collective-permute-start.2 = (f32[4,16,768]{2,1,0:T(8,128)S(1)}, f32[4,16,768]{2,1,0:T(8,128)S(1)}, u32[]{:S(2)}, u32[]{:S(2)}) collective-permute-start(f32[4,16,768]{2,1,0:T(8,128)S(1)} %get-tuple-element.33), channel_id=1, source_target_pairs={{0,2},{2,0},{4,6},{6,4},{8,10},{10,8},{12,14},{14,12},{1,3},{3,1},... | collective-permute-start | bytes 589832 | tf_op jit(solution)/shard_map/ppermute | solution.py:520
  9.3 0.0 copy-done.5
  9.3 0.0 copy-start.2
  9.3 0.0 copy-start
  9.3 0.0 copy-start.1
  9.3 3.7 %project_kept.1 = (f32[4,16,768]{2,1,0:T(8,128)S(1)}, s32[64,128]{1,0:T(8,128)S(1)}) custom-call(s32[1]{0:T(128)} %bitcast.refs_0_, s32[1]{0:T(128)} %bitcast.1.refs_1_.bank, s32[8]{0:T(128)S(1)} %copy-done.5, bf16[8,1024]{1,0:T(8,128)(2,1)S(1)} %copy-done.3, bf16[8,1024]{1,0:T(8,128)(2,1)S(1)} %collective-permute-done.refs_5_.refs_4_, ...), custom_call_target="tpu_custom_call" | custom-call | flops 83886080 | bytes 10485760 | tf_op jit(solution)/shard_map/project_kept/pallas_call | solution.py:213
  13.1 1.3 %collective-permute-done.2.came_ref = f32[4,16,768]{2,1,0:T(8,128)S(1)} collective-permute-done((f32[4,16,768]{2,1,0:T(8,128)S(1)}, f32[4,16,768]{2,1,0:T(8,128)S(1)}, u32[]{:S(2)}, u32[]{:S(2)}) %collective-permute-start.2) | collective-permute-done | bytes 196640 | tf_op jit(solution)/shard_map/ppermute | solution.py:520
  14.4 1.9 %collective-permute-start.3 = (f32[2,16,768]{2,1,0:T(8,128)S(1)}, f32[2,16,768]{2,1,0:T(8,128)S(1)}, u32[]{:S(2)}, u32[]{:S(2)}) collective-permute-start(f32[2,16,768]{2,1,0:T(8,128)S(1)} %get-tuple-element.35), channel_id=1, source_target_pairs={{0,4},{2,6},{4,0},{6,2},{8,12},{10,14},{12,8},{14,10},{1,5},{3,7},... | collective-permute-start | bytes 294920 | tf_op jit(solution)/shard_map/ppermute | solution.py:520
  16.3 2.8 %collective-permute-done.3.came_ref = f32[2,16,768]{2,1,0:T(8,128)S(1)} collective-permute-done((f32[2,16,768]{2,1,0:T(8,128)S(1)}, f32[2,16,768]{2,1,0:T(8,128)S(1)}, u32[]{:S(2)}, u32[]{:S(2)}) %collective-permute-start.3) | collective-permute-done | bytes 98336 | tf_op jit(solution)/shard_map/ppermute | solution.py:520
  19.1 2.9 %collective-permute-start.4 = (f32[1,16,768]{2,1,0:T(8,128)S(1)}, f32[1,16,768]{2,1,0:T(8,128)S(1)}, u32[]{:S(2)}, u32[]{:S(2)}) collective-permute-start(f32[1,16,768]{2,1,0:T(8,128)S(1)} %get-tuple-element.37), channel_id=1, source_target_pairs={{0,8},{2,10},{4,12},{6,14},{8,0},{10,2},{12,4},{14,6},{1,9},{3,11}... | collective-permute-start | bytes 147464 | tf_op jit(solution)/shard_map/ppermute | solution.py:520
  22.0 2.2 %collective-permute-done.4.came_ref = f32[1,16,768]{2,1,0:T(8,128)S(1)} collective-permute-done((f32[1,16,768]{2,1,0:T(8,128)S(1)}, f32[1,16,768]{2,1,0:T(8,128)S(1)}, u32[]{:S(2)}, u32[]{:S(2)}) %collective-permute-start.4) | collective-permute-done | bytes 49184 | tf_op jit(solution)/shard_map/ppermute | solution.py:520
  24.2 0.0 copy-done.2
  24.2 0.4 correct.1
  24.5 0.0 collective-permute-start.5
  24.5 0.1 fusion
  24.7 1.1 %collective-permute-done.5.came_ref = f32[8,1152]{1,0:T(8,128)S(1)} collective-permute-done((f32[8,1152]{1,0:T(8,128)S(1)}, f32[8,1152]{1,0:T(8,128)S(1)}, u32[]{:S(2)}, u32[]{:S(2)}) %collective-permute-start.5) | collective-permute-done | bytes 36896 | tf_op jit(solution)/shard_map/ppermute | solution.py:511
  25.8 0.1 rotate.1
  25.9 2.9 %collective-permute-start.6 = (bf16[1,64,128]{2,1,0:T(8,128)(2,1)S(1)}, bf16[1,64,128]{2,1,0:T(8,128)(2,1)S(1)}, u32[]{:S(2)}, u32[]{:S(2)}) collective-permute-start(bf16[1,64,128]{2,1,0:T(8,128)(2,1)S(1)} %get-tuple-element.40.refs_2_.first_ref.q_ref), channel_id=1, source_target_pairs={{0,8},{2,10},{4,12},{6,14},{8,0},{10,2},{12,4},{14,6},{1,9},{3,11}... | collective-permute-start | bytes 49160 | tf_op jit(solution)/shard_map/ppermute | solution.py:520
  28.8 0.0 copy-done
  28.8 0.0 copy-done.1
  28.8 0.0 slice-start
  28.8 0.5 attend.4.refs_5_
  29.3 1.3 %collective-permute-done.6.second_ref.refs_2_ = bf16[1,64,128]{2,1,0:T(8,128)(2,1)S(1)} collective-permute-done((bf16[1,64,128]{2,1,0:T(8,128)(2,1)S(1)}, bf16[1,64,128]{2,1,0:T(8,128)(2,1)S(1)}, u32[]{:S(2)}, u32[]{:S(2)}) %collective-permute-start.6) | collective-permute-done | bytes 16416 | tf_op jit(solution)/shard_map/ppermute | solution.py:520
  30.6 0.0 slice-start.1
  30.6 1.9 %collective-permute-start.7 = (bf16[2,64,128]{2,1,0:T(8,128)(2,1)S(1)}, bf16[2,64,128]{2,1,0:T(8,128)(2,1)S(1)}, u32[]{:S(2)}, u32[]{:S(2)}) collective-permute-start(bf16[2,64,128]{2,1,0:T(8,128)(2,1)S(1)} %join.2.first_ref), channel_id=1, source_target_pairs={{0,4},{2,6},{4,0},{6,2},{8,12},{10,14},{12,8},{14,10},{1,5},{3,7},... | collective-permute-start | bytes 98312 | tf_op jit(solution)/shard_map/ppermute | solution.py:520
  32.5 0.5 attend.5.refs_6_
  33.0 1.5 %collective-permute-done.7.second_ref.refs_2_ = bf16[2,64,128]{2,1,0:T(8,128)(2,1)S(1)} collective-permute-done((bf16[2,64,128]{2,1,0:T(8,128)(2,1)S(1)}, bf16[2,64,128]{2,1,0:T(8,128)(2,1)S(1)}, u32[]{:S(2)}, u32[]{:S(2)}) %collective-permute-start.7) | collective-permute-done | bytes 32800 | tf_op jit(solution)/shard_map/ppermute | solution.py:520
  34.5 0.0 slice-start.2
  34.5 1.8 %collective-permute-start.8 = (bf16[4,64,128]{2,1,0:T(8,128)(2,1)S(1)}, bf16[4,64,128]{2,1,0:T(8,128)(2,1)S(1)}, u32[]{:S(2)}, u32[]{:S(2)}) collective-permute-start(bf16[4,64,128]{2,1,0:T(8,128)(2,1)S(1)} %join.3), channel_id=1, source_target_pairs={{0,2},{2,0},{4,6},{6,4},{8,10},{10,8},{12,14},{14,12},{1,3},{3,1},... | collective-permute-start | bytes 196616 | tf_op jit(solution)/shard_map/ppermute | solution.py:520
  36.3 0.8 %attend.6.refs_7_ = bf16[2,80,128]{2,1,0:T(8,128)(2,1)S(1)} custom-call(s32[1]{0:T(128)} %bitcast.refs_0_, s32[64,128]{1,0:T(8,128)S(1)} %get-tuple-element.30.refs_1_, bf16[2,64,128]{2,1,0:T(8,128)(2,1)S(1)} %collective-permute-done.7.second_ref.refs_2_, bf16[8,256,1024]{2,1,0:T(8,128)(2,1)S(1)} %copy-done, bf16[8,256,1024]{2,1,0:T(8,128)(2,1)S(1)} %copy-done.1), custom_call_target="tpu_custom_call" | custom-call | flops 16777216 | bytes 2097152 | tf_op jit(solution)/shard_map/attend/pallas_call | solution.py:403
  37.2 0.0 slice-start.3
  37.2 1.7 %collective-permute-done.8.refs_2_ = bf16[4,64,128]{2,1,0:T(8,128)(2,1)S(1)} collective-permute-done((bf16[4,64,128]{2,1,0:T(8,128)(2,1)S(1)}, bf16[4,64,128]{2,1,0:T(8,128)(2,1)S(1)}, u32[]{:S(2)}, u32[]{:S(2)}) %collective-permute-start.8) | collective-permute-done | bytes 65568 | tf_op jit(solution)/shard_map/ppermute | solution.py:520
  38.8 1.6 %attend.7 = bf16[8,80,128]{2,1,0:T(8,128)(2,1)S(1)} custom-call(s32[1]{0:T(128)} %bitcast.refs_0_, s32[64,128]{1,0:T(8,128)S(1)} %get-tuple-element.30.refs_1_, bf16[4,64,128]{2,1,0:T(8,128)(2,1)S(1)} %collective-permute-done.8.refs_2_, bf16[8,256,1024]{2,1,0:T(8,128)(2,1)S(1)} %copy-done, bf16[8,256,1024]{2,1,0:T(8,128)(2,1)S(1)} %copy-done.1, ...), custom_call_target="tpu_custom_call" | custom-call | flops 33554432 | bytes 16777216 | tf_op jit(solution)/shard_map/attend/pallas_call | solution.py:403
  40.4 13.8 %all_to_all.10.parts_ref = bf16[8,80,128]{2,1,0:T(8,128)(2,1)S(1)} all-to-all(bf16[8,80,128]{2,1,0:T(8,128)(2,1)S(1)} %attend.7), channel_id=1, replica_groups=mesh['groups'=2,'tensor'=8,'bank'=2] {'tensor'}, dimensions={0} | all-to-all | bytes 327680 | tf_op jit(solution)/shard_map/all_to_all | solution.py:515
  54.2 0.5 combine.1.x_ref
  54.7 0.0 slice-done
  54.7 0.0 slice-done.1
  54.7 0.0 slice-done.2
  54.7 0.0 slice-done.3
  54.8 2.3 %output.1 = bf16[8,8,1024]{2,1,0:T(8,128)(2,1)S(1)} custom-call(bf16[8,1024]{1,0:T(8,128)(2,1)S(1)} %combine.1.x_ref, bf16[1024,8192]{1,0:T(8,128)(2,1)S(1)} %bitcast.4), custom_call_target="tpu_custom_call" | custom-call | flops 134217728 | bytes 16777216 | tf_op jit(solution)/shard_map/output/pallas_call | solution.py:481
  57.0 9.7 %all_to_all.11.parts_ref = bf16[8,8,1024]{2,1,0:T(8,128)(2,1)S(1)} all-to-all(bf16[8,8,1024]{2,1,0:T(8,128)(2,1)S(1)} %output.1), channel_id=1, replica_groups=mesh['groups'=2,'tensor'=8,'bank'=2] {'tensor'}, dimensions={0} | all-to-all | bytes 262144 | tf_op jit(solution)/shard_map/all_to_all | solution.py:515
  66.8 0.6 residual.1
  (7 shorter events, 0.1 us)
Async XLA Ops:
  0.0 2.5 %collective-permute-start = (bf16[8,1024]{1,0:T(8,128)(2,1)}, bf16[8,1024]{1,0:T(8,128)(2,1)S(1)}, u32[]{:S(2)}, u32[]{:S(2)}) collective-permute-start(bf16[8,1024]{1,0:T(8,128)(2,1)} %x_ref.1), channel_id=1, source_target_pairs={{0,1},{1,0},{2,3},{3,2},{4,5},{5,4},{6,7},{7,6},{8,9},{9,8},{10,11... | collective-permute-start | bytes 49160 | tf_op jit(solution)/shard_map/ppermute | solution.py:511
  0.5 2.0 %collective-permute-start.1 = (s32[8]{0:T(128)}, s32[8]{0:T(128)S(1)}, u32[]{:S(2)}, u32[]{:S(2)}) collective-permute-start(s32[8]{0:T(128)} %refs_2_.4), channel_id=1, source_target_pairs={{0,1},{1,0},{2,3},{3,2},{4,5},{5,4},{6,7},{7,6},{8,9},{9,8},{10,11... | collective-permute-start | bytes 104 | tf_op jit(solution)/shard_map/ppermute | solution.py:511
  0.5 2.0 %copy-start.3 = (bf16[8,1024]{1,0:T(8,128)(2,1)S(1)}, bf16[8,1024]{1,0:T(8,128)(2,1)}, u32[]{:S(2)}) copy-start(bf16[8,1024]{1,0:T(8,128)(2,1)} %x_ref.1) | copy-start | bytes 49156
  0.5 2.0 %copy-start.4 = (s32[8]{0:T(128)S(1)}, s32[8]{0:T(128)}, u32[]{:S(2)}) copy-start(s32[8]{0:T(128)} %refs_2_.4) | copy-start | bytes 100
  2.5 6.8 %copy-start.5 = (s32[8]{0:T(128)S(1)}, s32[8]{0:T(128)}, u32[]{:S(2)}) copy-start(s32[8]{0:T(128)} %refs_2_.5) | copy-start | bytes 100
  6.3 8.1 %collective-permute-start.2 = (f32[4,16,768]{2,1,0:T(8,128)S(1)}, f32[4,16,768]{2,1,0:T(8,128)S(1)}, u32[]{:S(2)}, u32[]{:S(2)}) collective-permute-start(f32[4,16,768]{2,1,0:T(8,128)S(1)} %get-tuple-element.33), channel_id=1, source_target_pairs={{0,2},{2,0},{4,6},{6,4},{8,10},{10,8},{12,14},{14,12},{1,3},{3,1},... | collective-permute-start | bytes 589832 | tf_op jit(solution)/shard_map/ppermute | solution.py:520
  9.3 14.8 %copy-start.2 = (bf16[16,64,1024]{2,1,0:T(8,128)(2,1)S(1)}, bf16[16,64,1024]{2,1,0:T(8,128)(2,1)}, u32[]{:S(2)}) copy-start(bf16[16,64,1024]{2,1,0:T(8,128)(2,1)} %up_ref.1) | copy-start | bytes 6291460
  9.3 19.5 %copy-start = (bf16[8,256,1024]{2,1,0:T(8,128)(2,1)S(1)}, bf16[8,256,1024]{2,1,0:T(8,128)(2,1)}, u32[]{:S(2)}) copy-start(bf16[8,256,1024]{2,1,0:T(8,128)(2,1)} %refs_3_.11) | copy-start | bytes 12582916
  9.3 19.5 %copy-start.1 = (bf16[8,256,1024]{2,1,0:T(8,128)(2,1)S(1)}, bf16[8,256,1024]{2,1,0:T(8,128)(2,1)}, u32[]{:S(2)}) copy-start(bf16[8,256,1024]{2,1,0:T(8,128)(2,1)} %refs_4_.9) | copy-start | bytes 12582916
  14.4 4.7 %collective-permute-start.3 = (f32[2,16,768]{2,1,0:T(8,128)S(1)}, f32[2,16,768]{2,1,0:T(8,128)S(1)}, u32[]{:S(2)}, u32[]{:S(2)}) collective-permute-start(f32[2,16,768]{2,1,0:T(8,128)S(1)} %get-tuple-element.35), channel_id=1, source_target_pairs={{0,4},{2,6},{4,0},{6,2},{8,12},{10,14},{12,8},{14,10},{1,5},{3,7},... | collective-permute-start | bytes 294920 | tf_op jit(solution)/shard_map/ppermute | solution.py:520
  19.1 5.1 %collective-permute-start.4 = (f32[1,16,768]{2,1,0:T(8,128)S(1)}, f32[1,16,768]{2,1,0:T(8,128)S(1)}, u32[]{:S(2)}, u32[]{:S(2)}) collective-permute-start(f32[1,16,768]{2,1,0:T(8,128)S(1)} %get-tuple-element.37), channel_id=1, source_target_pairs={{0,8},{2,10},{4,12},{6,14},{8,0},{10,2},{12,4},{14,6},{1,9},{3,11}... | collective-permute-start | bytes 147464 | tf_op jit(solution)/shard_map/ppermute | solution.py:520
  24.5 1.2 %collective-permute-start.5 = (f32[8,1152]{1,0:T(8,128)S(1)}, f32[8,1152]{1,0:T(8,128)S(1)}, u32[]{:S(2)}, u32[]{:S(2)}) collective-permute-start(f32[8,1152]{1,0:T(8,128)S(1)} %get-tuple-element.39), channel_id=1, source_target_pairs={{0,1},{1,0},{2,3},{3,2},{4,5},{5,4},{6,7},{7,6},{8,9},{9,8},{10,11... | collective-permute-start | bytes 110600 | tf_op jit(solution)/shard_map/ppermute | solution.py:511
  25.9 4.7 %collective-permute-start.6 = (bf16[1,64,128]{2,1,0:T(8,128)(2,1)S(1)}, bf16[1,64,128]{2,1,0:T(8,128)(2,1)S(1)}, u32[]{:S(2)}, u32[]{:S(2)}) collective-permute-start(bf16[1,64,128]{2,1,0:T(8,128)(2,1)S(1)} %get-tuple-element.40.refs_2_.first_ref.q_ref), channel_id=1, source_target_pairs={{0,8},{2,10},{4,12},{6,14},{8,0},{10,2},{12,4},{14,6},{1,9},{3,11}... | collective-permute-start | bytes 49160 | tf_op jit(solution)/shard_map/ppermute | solution.py:520
  28.8 25.9 %slice-start = ((s8[16777216]{0:T(1024)(128)(4,1)}), s8[4194304]{0:T(1024)(128)(4,1)S(1)}, s32[]{:S(2)}) async-start(s8[16777216]{0:T(1024)(128)(4,1)} %bitcast.3), calls=%async_computation.2 | async-start | bytes 8388608
  30.6 24.1 %slice-start.1 = ((s8[16777216]{0:T(1024)(128)(4,1)}), s8[4194304]{0:T(1024)(128)(4,1)S(1)}, s32[]{:S(2)}) async-start(s8[16777216]{0:T(1024)(128)(4,1)} %bitcast.3), calls=%async_computation.3 | async-start | bytes 8388608
  30.6 3.9 %collective-permute-start.7 = (bf16[2,64,128]{2,1,0:T(8,128)(2,1)S(1)}, bf16[2,64,128]{2,1,0:T(8,128)(2,1)S(1)}, u32[]{:S(2)}, u32[]{:S(2)}) collective-permute-start(bf16[2,64,128]{2,1,0:T(8,128)(2,1)S(1)} %join.2.first_ref), channel_id=1, source_target_pairs={{0,4},{2,6},{4,0},{6,2},{8,12},{10,14},{12,8},{14,10},{1,5},{3,7},... | collective-permute-start | bytes 98312 | tf_op jit(solution)/shard_map/ppermute | solution.py:520
  34.5 20.2 %slice-start.2 = ((s8[16777216]{0:T(1024)(128)(4,1)}), s8[4194304]{0:T(1024)(128)(4,1)S(1)}, s32[]{:S(2)}) async-start(s8[16777216]{0:T(1024)(128)(4,1)} %bitcast.3), calls=%async_computation.4 | async-start | bytes 8388608
  34.5 4.3 %collective-permute-start.8 = (bf16[4,64,128]{2,1,0:T(8,128)(2,1)S(1)}, bf16[4,64,128]{2,1,0:T(8,128)(2,1)S(1)}, u32[]{:S(2)}, u32[]{:S(2)}) collective-permute-start(bf16[4,64,128]{2,1,0:T(8,128)(2,1)S(1)} %join.3), channel_id=1, source_target_pairs={{0,2},{2,0},{4,6},{6,4},{8,10},{10,8},{12,14},{14,12},{1,3},{3,1},... | collective-permute-start | bytes 196616 | tf_op jit(solution)/shard_map/ppermute | solution.py:520
  37.2 17.6 %slice-start.3 = ((s8[16777216]{0:T(1024)(128)(4,1)}), s8[4194304]{0:T(1024)(128)(4,1)S(1)}, s32[]{:S(2)}) async-start(s8[16777216]{0:T(1024)(128)(4,1)} %bitcast.3), calls=%async_computation.5 | async-start | bytes 8388608

commit v9 on v8

--- a/solution.py
+++ b/solution.py
@@ -38,6 +38,14 @@
 
 def params(mib=4):
     return pltpu.CompilerParams(vmem_limit_bytes=mib * MIB)
+
+
+def exchanged(slot):
+    return slot & ~3 | (slot & 1) << 1 | slot >> 1 & 1
+
+
+def rank_of(place, bank, slot):
+    return place ^ (slot + bank * (exchanged(slot) - slot))
 
 
 def start_columns(weight, column, target, sems):
@@ -67,11 +75,11 @@
     return column - bank * count
 
 
-def start_slots(parity, first, ranks, place, bank, w_ref, kv_ref, w_buf, kv_buf, sems, kv_sems):
+def start_slots(parity, ranks, place, bank, w_ref, kv_ref, w_buf, kv_buf, sems, kv_sems):
     count, _, width = w_buf.shape
     copies = []
     for s in range(count):
-        target = (2 * (first + s) + parity) ^ place[0]
+        target = rank_of(place[0], bank[0], 2 * s + parity)
         copies.append(
             start_columns(w_ref, (2 * target + bank[0]) * width, w_buf.at[s], sems.at[s])
             + start_columns(
@@ -90,12 +98,12 @@
 def fetch_kernel(ranks, place, bank, w_ref, kv_ref, down_ref, w_buf, kv_buf, down_buf, *sems):
     down_copy = pltpu.make_async_copy(down_ref, down_buf, sems[2])
     down_copy.start()
-    wait_all(start_slots(1, 0, ranks, place, bank, w_ref, kv_ref, w_buf, kv_buf, *sems[:2]))
+    wait_all(start_slots(1, ranks, place, bank, w_ref, kv_ref, w_buf, kv_buf, *sems[:2]))
     down_copy.wait()
 
 
-def slot_buffers(wq, ranks, count):
-    depth = wq.shape[0]
+def slot_buffers(wq, ranks):
+    count, depth = ranks // 2, wq.shape[0]
     return [
         shape(count, depth, wq.shape[1] // ranks // 2, dtype=BF16),
         shape(count, depth, HEAD_DIM, dtype=BF16),
@@ -107,13 +115,13 @@
 
 
 def fetch(place, bank, wq, wkv, down, ranks):
-    out = slot_buffers(wq, ranks, 1) + [jax.ShapeDtypeStruct(down.shape, BF16)]
+    out = slot_buffers(wq, ranks) + [jax.ShapeDtypeStruct(down.shape, BF16)]
     return pl.pallas_call(
         lambda *refs: fetch_kernel(ranks, *refs),
         in_specs=[scalar()] * 2 + [big()] * 3,
         out_specs=[whole()] * 3,
         out_shape=out,
-        scratch_shapes=slot_sems(1) + [pltpu.SemaphoreType.DMA(())],
+        scratch_shapes=slot_sems(ranks // 2) + [pltpu.SemaphoreType.DMA(())],
         compiler_params=params(),
         cost_estimate=pl.CostEstimate(
             flops=0, bytes_accessed=2 * sum(o.size for o in out), transcendentals=0
@@ -133,12 +141,20 @@
     out[:, width : width + HEAD_DIM] = jnp.dot(x, kv[...], preferred_element_type=F32)
 
 
-def project_sent_kernel(ranks, place, bank, own_ref, came_ref, *refs):
-    x_ref, other_ref, w_ref, kv_ref, w_first, kv_first, down_buf, out, inner, column_out = refs[:10]
-    w_buf, kv_buf = refs[10:12]
-    copies = start_slots(1, 1, ranks, place, bank, w_ref, kv_ref, *refs[10:])
-    width = w_first.shape[2]
+def project_sent_kernel(
+    bank, own_ref, came_ref, x_ref, other_ref, w_buf, kv_buf, down_buf, *refs
+):
+    out, inner, column_out, *index, sems = refs
+    copies = [
+        pltpu.make_async_copy(ref, held, sems.at[n])
+        for n, (ref, held) in enumerate(zip((own_ref, came_ref), index))
+    ]
+    for copy in copies:
+        copy.start()
+    width = w_buf.shape[2]
     x = beam_rows(x_ref, other_ref)
+    for s in range(out.shape[0]):
+        project_slot(x, w_buf.at[s], kv_buf.at[s], out.at[s])
     adapters, rank, depth = down_buf.shape
     every = lax.dot_general(
         x,
@@ -146,7 +162,9 @@
         (((1,), (1,)), ((), ())),
         preferred_element_type=F32,
     )
-    column = adapter_column((own_ref, came_ref), bank[0], adapters)
+    for copy in copies:
+        copy.wait()
+    column = adapter_column(index, bank[0], adapters)
     column_out[...] = column
     lane = iota(column.shape, 1)
     per = HEAD_DIM // rank
@@ -157,40 +175,37 @@
     inner[...] = total
     for s in range(out.shape[0]):
         out[s, :, width + HEAD_DIM :] = total
-    project_slot(x, w_first.at[0], kv_first.at[0], out.at[0])
-    for s, slot in enumerate(copies):
-        wait_all([slot])
-        project_slot(x, w_buf.at[s], kv_buf.at[s], out.at[s + 1])
-
-
-def project_sent(place, bank, index, x, other, wq, wkv, ahead, ranks):
-    rows, half = 2 * x.shape[0], ranks // 2
-    buffers = slot_buffers(wq, ranks, half - 1)
-    return pl.pallas_call(
-        lambda *refs: project_sent_kernel(ranks, *refs),
-        in_specs=[scalar()] * 4 + [whole()] * 2 + [big()] * 2 + [whole()] * 3,
+
+
+def project_sent(bank, index, x, other, weights):
+    half, _, width = weights[0].shape
+    rows = 2 * x.shape[0]
+    return pl.pallas_call(
+        project_sent_kernel,
+        in_specs=[scalar(), big(), pl.BlockSpec(memory_space=pl.ANY)] + [whole()] * 5,
         out_specs=[whole()] * 3,
         out_shape=[
-            shape(half, rows, wq.shape[1] // ranks // 2 + 2 * HEAD_DIM),
+            shape(half, rows, width + 2 * HEAD_DIM),
             shape(rows, HEAD_DIM),
             shape(rows, HEAD_DIM, dtype=jnp.int32),
         ],
-        scratch_shapes=[pltpu.VMEM(b.shape, BF16) for b in buffers] + slot_sems(half - 1),
-        compiler_params=params(8),
+        scratch_shapes=[pltpu.SMEM(index[0].shape, jnp.int32)] * 2
+        + [pltpu.SemaphoreType.DMA((2,))],
+        compiler_params=params(),
         cost_estimate=pl.CostEstimate(
-            flops=rows * (wq.size + wkv.size) // 2,
-            bytes_accessed=(wq.size + wkv.size) // 2,
+            flops=2 * rows * sum(w.size for w in weights),
+            bytes_accessed=2 * sum(w.size for w in weights),
             transcendentals=0,
         ),
         name="project_sent",
-    )(place, bank, *index, x, other, wq, wkv, *ahead)
+    )(bank, in_hbm(index[0]), index[1], x, other, *weights)
 
 
 def project_kept_kernel(
     ranks, place, bank, length, x_ref, other_ref, w_ref, kv_ref, inner, out, live, *scratch
 ):
     w_buf, kv_buf = scratch[:2]
-    copies = start_slots(0, 0, ranks, place, bank, w_ref, kv_ref, *scratch)
+    copies = start_slots(0, ranks, place, bank, w_ref, kv_ref, *scratch)
     width = w_buf.shape[2]
     beams = x_ref.shape[0]
     row = iota(live.shape, 0)
@@ -209,7 +224,7 @@
     beams, depth = x.shape
     rows = 2 * beams
     half = ranks // 2
-    buffers = slot_buffers(wq, ranks, half)
+    buffers = slot_buffers(wq, ranks)
     return pl.pallas_call(
         lambda *refs: project_kept_kernel(ranks, *refs),
         in_specs=[scalar()] * 3 + [whole()] * 2 + [big()] * 2 + [whole()],
@@ -344,7 +359,7 @@
     )(first, second)
 
 
-def attend_kernel(slots, earlier, place, length_ref, q_ref, k_ref, v_ref, *refs):
+def attend_kernel(slots, earlier, place, bank, length_ref, q_ref, k_ref, v_ref, *refs):
     before, out_ref = refs[:-1], refs[-1]
     beams, positions, _ = k_ref.shape
     rows = q_ref.shape[1]
@@ -355,7 +370,7 @@
         [lane + first < left for first in range(0, positions, HEAD_DIM)], axis=1
     )
     for i, slot in enumerate(slots):
-        head = place[0] ^ slot
+        head = rank_of(place[0], bank[0], slot)
         columns = pl.ds(pl.multiple_of(head * HEAD_DIM, HEAD_DIM), HEAD_DIM)
         query = q_ref[i].astype(F32)
         scores = jnp.concatenate(
@@ -394,15 +409,15 @@
     if earlier:
         done = [(ref, i) for ref in before for i in range(ref.shape[0])]
         for slot, (ref, i) in zip(earlier, done):
-            out_ref[place[0] ^ slot] = ref[i]
-
-
-def attend(place, length, queries, keys, values, slots, earlier=(), before=()):
+            out_ref[rank_of(place[0], bank[0], slot)] = ref[i]
+
+
+def attend(place, bank, length, queries, keys, values, slots, earlier=(), before=()):
     count, rows, _ = queries.shape
     beams, positions, _ = keys.shape
     return pl.pallas_call(
         lambda *refs: attend_kernel(slots, earlier, *refs),
-        in_specs=[scalar()] + [whole()] * (4 + len(before)),
+        in_specs=[scalar()] * 2 + [whole()] * (4 + len(before)),
         out_specs=whole(),
         out_shape=shape(count + len(earlier), rows + 2 * beams, HEAD_DIM, dtype=BF16),
         compiler_params=params(),
@@ -412,7 +427,7 @@
             transcendentals=rows * count * positions,
         ),
         name="attend",
-    )(place, length, queries, keys, values, *before)
+    )(place, bank, length, queries, keys, values, *before)
 
 
 def combine_kernel(parts_ref, q_ref, k_ref, v_ref, out_ref, joined):
@@ -516,8 +531,11 @@
 
 
 def hop(x, bit):
-    ranks = lax.axis_size("tensor")
-    return lax.ppermute(x, "tensor", [(i, i ^ bit) for i in range(ranks)])
+    pairs = []
+    for rank in range(lax.axis_size("tensor")):
+        for bank in range(2):
+            pairs.append((2 * rank + bank, 2 * rank_of(rank, bank, bit) + bank))
+    return lax.ppermute(x, ("tensor", "bank"), pairs)
 
 
 def matched_body(
@@ -547,9 +565,7 @@
     weights = in_hbm(query_weight), in_hbm(keyvalue_weight)
     down = in_hbm(lowrank_down_factors.swapaxes(1, 2))
     ahead = fetch(place, bank, *weights, down, ranks)
-    sent, inner, column = project_sent(
-        place, bank, index, x, x_other, *weights, ahead, ranks
-    )
+    sent, inner, column = project_sent(bank, index, x, x_other, ahead)
     came = hop(sent, 1)
     kept, length = project_kept(
         place, bank, beam_cache_length, x, x_other, *weights, inner, ranks
@@ -561,7 +577,7 @@
 
     def attended_part(queries, slots, **more):
         cache = paged_key_cache, paged_value_cache
-        return attend(place, length, queries, *cache, slots, **more)
+        return attend(place, bank, length, queries, *cache, slots, **more)
 
     came, done = lax.optimization_barrier((hop(query, 4), attended_part(query, (0,))))
     gathered = join(query, came)

time: 67.6 us -> 65.9 us (0.975)
  waiting for transfers between devices: 11.9 us -> 10.1 us
    pallas_call x1, Pallas kernels: 3.72 us -> 1.77 us  [project_sent(): pl.pallas_call(project_sent_kernel, in_specs=[scalar(), big(), pl.BlockSp...]
    ppermute x6, waiting for transfers between devices: 10.8 us -> 9.01 us  [hop(): return lax.ppermute(x, ('tensor', 'bank'), pairs)]
    pallas_call x1, Pallas kernels: 1.97 us -> 3.41 us  [fetch(): pl.pallas_call(lambda *refs: fetch_kernel(ranks, *refs), in_specs=[scalar...]
  transfers between devices with their start and end apart: 9 -> 9, of which waited for: 7 -> 6; matrix products, arithmetic and copies ran while one was open for 0% -> 0% of each run, Pallas kernels for 11% -> 14%
where the time goes in v9:
time: 65.9 us; the launch traced here: 65.8 us
  blocking collectives  23.6 us (36%)
  Pallas kernels  16.2 us (25%)
  starting transfers between devices  15.4 us (23%)
  waiting for transfers between devices  10.1 us (15%)
    all_to_all x2, blocking collectives, traded(): return lax.all_to_all(blocks, 'tensor', 0, 0, tiled=True)  23.6 us
    ppermute x6, starting transfers between devices, hop(): return lax.ppermute(x, ('tensor', 'bank'), pairs)  14.9 us
    ppermute x6, waiting for transfers between devices, hop(): return lax.ppermute(x, ('tensor', 'bank'), pairs)  9.01 us
    pallas_call x1, Pallas kernels, project_kept(): pl.pallas_call(lambda *refs: project_kept_kernel(ranks, *refs), in_specs=...  3.74 us
    pallas_call x1, Pallas kernels, fetch(): pl.pallas_call(lambda *refs: fetch_kernel(ranks, *refs), in_specs=[scalar...  3.41 us
    pallas_call x4, Pallas kernels, attend(): pl.pallas_call(lambda *refs: attend_kernel(slots, earlier, *refs), in_spe...  3.41 us
    pallas_call x1, Pallas kernels, output(): pl.pallas_call(output_kernel, in_specs=[whole()] * 2, out_specs=whole(),...  2.28 us
    pallas_call x1, Pallas kernels, project_sent(): pl.pallas_call(project_sent_kernel, in_specs=[scalar(), big(), pl.BlockSp...  1.77 us
  transfers between devices with their start and end apart: 9, of which 6 were waited for; matrix products, arithmetic and copies ran while one was open for 0% of the time, Pallas kernels for 14%

profile of v9, /device:TPU:0, one launch (start us, length us, event | category | flops | bytes accessed | tf_op | source)
XLA Modules:
  0.0 65.8 jit_solution(14999862547690634261)
XLA Ops:
  0.0 0.5 collective-permute-start
  0.5 0.1 collective-permute-start.1
  0.5 0.0 copy-start.3
  0.5 3.4 %fetch.1 = (bf16[4,1024,512]{2,1,0:T(8,128)(2,1)S(1)}, bf16[4,1024,128]{2,1,0:T(8,128)(2,1)S(1)}, bf16[16,64,1024]{2,1,0:T(8,128)(2,1)S(1)}) custom-call(s32[1]{0:T(128)} %bitcast.refs_0_, s32[1]{0:T(128)} %bitcast.1.refs_1_.bank, bf16[1024,8192]{1,0:T(8,128)(2,1)} %refs_5_.5, bf16[1024,2048]{1,0:T(8,128)(2,1)} %refs_6_.1, bf16[16,64,1024]{2,1,0:T(8,128)(2,1)} %bitcast.5), custom_call_target="tpu_custom_call" | custom-call | bytes 7340032 | tf_op jit(solution)/shard_map/fetch/pallas_call | solution.py:119
  3.9 0.0 copy-start.4
  3.9 0.0 collective-permute-done.1.came_ref
  4.0 0.0 collective-permute-done.other_ref.refs_4_
  4.0 0.0 copy-done.3
  4.0 1.8 %project_sent.1 = (f32[4,16,768]{2,1,0:T(8,128)S(1)}, f32[16,128]{1,0:T(8,128)S(1)}, s32[16,128]{1,0:T(8,128)S(1)}) custom-call(s32[1]{0:T(128)} %bitcast.1.refs_1_.bank, s32[8]{0:T(128)} %own_ref.1, s32[8]{0:T(128)S(1)} %collective-permute-done.1.came_ref, bf16[8,1024]{1,0:T(8,128)(2,1)S(1)} %copy-done.3, ...), custom_call_target="tpu_custom_call" | custom-call | flops 117440512 | bytes 7340032 | tf_op jit(solution)/shard_map/project_sent/pallas_call | solution.py:183
  5.8 3.0 %collective-permute-start.2 = (f32[4,16,768]{2,1,0:T(8,128)S(1)}, f32[4,16,768]{2,1,0:T(8,128)S(1)}, u32[]{:S(2)}, u32[]{:S(2)}) collective-permute-start(f32[4,16,768]{2,1,0:T(8,128)S(1)} %get-tuple-element.33), channel_id=1, source_target_pairs={{0,2},{1,5},{2,0},{3,7},{4,6},{5,1},{6,4},{7,3},{8,10},{9,13},{10,... | collective-permute-start | bytes 589832 | tf_op jit(solution)/shard_map/ppermute | solution.py:538
  8.8 0.0 copy-done.4
  8.8 0.0 copy-start.2
  8.8 0.0 copy-start
  8.8 0.0 copy-start.1
  8.8 3.7 %project_kept.1 = (f32[4,16,768]{2,1,0:T(8,128)S(1)}, s32[64,128]{1,0:T(8,128)S(1)}) custom-call(s32[1]{0:T(128)} %bitcast.refs_0_, s32[1]{0:T(128)} %bitcast.1.refs_1_.bank, s32[8]{0:T(128)S(1)} %copy-done.4, bf16[8,1024]{1,0:T(8,128)(2,1)S(1)} %copy-done.3, bf16[8,1024]{1,0:T(8,128)(2,1)S(1)} %collective-permute-done.other_ref.refs_4_, ...), custom_call_target="tpu_custom_call" | custom-call | flops 83886080 | bytes 10485760 | tf_op jit(solution)/shard_map/project_kept/pallas_call | solution.py:228
  12.5 0.0 collective-permute-done.2.came_ref
  12.6 2.0 %collective-permute-start.3 = (f32[2,16,768]{2,1,0:T(8,128)S(1)}, f32[2,16,768]{2,1,0:T(8,128)S(1)}, u32[]{:S(2)}, u32[]{:S(2)}) collective-permute-start(f32[2,16,768]{2,1,0:T(8,128)S(1)} %get-tuple-element.35), channel_id=1, source_target_pairs={{0,4},{1,3},{2,6},{3,1},{4,0},{5,7},{6,2},{7,5},{8,12},{9,11},{10,... | collective-permute-start | bytes 294920 | tf_op jit(solution)/shard_map/ppermute | solution.py:538
  14.6 2.7 %collective-permute-done.3.came_ref = f32[2,16,768]{2,1,0:T(8,128)S(1)} collective-permute-done((f32[2,16,768]{2,1,0:T(8,128)S(1)}, f32[2,16,768]{2,1,0:T(8,128)S(1)}, u32[]{:S(2)}, u32[]{:S(2)}) %collective-permute-start.3) | collective-permute-done | bytes 98336 | tf_op jit(solution)/shard_map/ppermute | solution.py:538
  17.3 3.0 %collective-permute-start.4 = (f32[1,16,768]{2,1,0:T(8,128)S(1)}, f32[1,16,768]{2,1,0:T(8,128)S(1)}, u32[]{:S(2)}, u32[]{:S(2)}) collective-permute-start(f32[1,16,768]{2,1,0:T(8,128)S(1)} %get-tuple-element.37), channel_id=1, source_target_pairs={{0,8},{1,9},{2,10},{3,11},{4,12},{5,13},{6,14},{7,15},{8,0},{9,1},... | collective-permute-start | bytes 147464 | tf_op jit(solution)/shard_map/ppermute | solution.py:538
  20.3 2.1 %collective-permute-done.4.came_ref = f32[1,16,768]{2,1,0:T(8,128)S(1)} collective-permute-done((f32[1,16,768]{2,1,0:T(8,128)S(1)}, f32[1,16,768]{2,1,0:T(8,128)S(1)}, u32[]{:S(2)}, u32[]{:S(2)}) %collective-permute-start.4) | collective-permute-done | bytes 49184 | tf_op jit(solution)/shard_map/ppermute | solution.py:538
  22.4 0.0 copy-done.2
  22.4 0.4 correct.1
  22.8 0.0 collective-permute-start.5
  22.8 0.1 fusion
  22.9 1.1 %collective-permute-done.5.came_ref = f32[8,1152]{1,0:T(8,128)S(1)} collective-permute-done((f32[8,1152]{1,0:T(8,128)S(1)}, f32[8,1152]{1,0:T(8,128)S(1)}, u32[]{:S(2)}, u32[]{:S(2)}) %collective-permute-start.5) | collective-permute-done | bytes 36896 | tf_op jit(solution)/shard_map/ppermute | solution.py:526
  24.0 0.1 rotate.1
  24.1 3.0 %collective-permute-start.6 = (bf16[1,64,128]{2,1,0:T(8,128)(2,1)S(1)}, bf16[1,64,128]{2,1,0:T(8,128)(2,1)S(1)}, u32[]{:S(2)}, u32[]{:S(2)}) collective-permute-start(bf16[1,64,128]{2,1,0:T(8,128)(2,1)S(1)} %get-tuple-element.40.refs_3_.first_ref.q_ref), channel_id=1, source_target_pairs={{0,8},{1,9},{2,10},{3,11},{4,12},{5,13},{6,14},{7,15},{8,0},{9,1},... | collective-permute-start | bytes 49160 | tf_op jit(solution)/shard_map/ppermute | solution.py:538
  27.1 0.0 copy-done
  27.1 0.0 copy-done.1
  27.1 0.0 slice-start
  27.1 0.5 attend.4.refs_6_
  27.6 1.2 %collective-permute-done.6.second_ref.refs_3_ = bf16[1,64,128]{2,1,0:T(8,128)(2,1)S(1)} collective-permute-done((bf16[1,64,128]{2,1,0:T(8,128)(2,1)S(1)}, bf16[1,64,128]{2,1,0:T(8,128)(2,1)S(1)}, u32[]{:S(2)}, u32[]{:S(2)}) %collective-permute-start.6) | collective-permute-done | bytes 16416 | tf_op jit(solution)/shard_map/ppermute | solution.py:538
  28.9 0.0 slice-start.1
  28.9 1.9 %collective-permute-start.7 = (bf16[2,64,128]{2,1,0:T(8,128)(2,1)S(1)}, bf16[2,64,128]{2,1,0:T(8,128)(2,1)S(1)}, u32[]{:S(2)}, u32[]{:S(2)}) collective-permute-start(bf16[2,64,128]{2,1,0:T(8,128)(2,1)S(1)} %join.2.first_ref), channel_id=1, source_target_pairs={{0,4},{1,3},{2,6},{3,1},{4,0},{5,7},{6,2},{7,5},{8,12},{9,11},{10,... | collective-permute-start | bytes 98312 | tf_op jit(solution)/shard_map/ppermute | solution.py:538
  30.8 0.5 attend.5.refs_7_
  31.3 1.5 %collective-permute-done.7.second_ref.refs_3_ = bf16[2,64,128]{2,1,0:T(8,128)(2,1)S(1)} collective-permute-done((bf16[2,64,128]{2,1,0:T(8,128)(2,1)S(1)}, bf16[2,64,128]{2,1,0:T(8,128)(2,1)S(1)}, u32[]{:S(2)}, u32[]{:S(2)}) %collective-permute-start.7) | collective-permute-done | bytes 32800 | tf_op jit(solution)/shard_map/ppermute | solution.py:538
  32.8 0.0 slice-start.2
  32.8 1.9 %collective-permute-start.8 = (bf16[4,64,128]{2,1,0:T(8,128)(2,1)S(1)}, bf16[4,64,128]{2,1,0:T(8,128)(2,1)S(1)}, u32[]{:S(2)}, u32[]{:S(2)}) collective-permute-start(bf16[4,64,128]{2,1,0:T(8,128)(2,1)S(1)} %join.3), channel_id=1, source_target_pairs={{0,2},{1,5},{2,0},{3,7},{4,6},{5,1},{6,4},{7,3},{8,10},{9,13},{10,... | collective-permute-start | bytes 196616 | tf_op jit(solution)/shard_map/ppermute | solution.py:538
  34.6 0.8 %attend.6.refs_8_ = bf16[2,80,128]{2,1,0:T(8,128)(2,1)S(1)} custom-call(s32[1]{0:T(128)} %bitcast.refs_0_, s32[1]{0:T(128)} %bitcast.1.refs_1_.bank, s32[64,128]{1,0:T(8,128)S(1)} %get-tuple-element.30.refs_2_, bf16[2,64,128]{2,1,0:T(8,128)(2,1)S(1)} %collective-permute-done.7.second_ref.refs_3_, bf16[8,256,1024]{2,1,0:T(8,128)(2,1)S(1)} %copy-done, ...), custom_call_target="tpu_custom_call" | custom-call | flops 16777216 | bytes 2097152 | tf_op jit(solution)/shard_map/attend/pallas_call | solution.py:418
  35.5 0.0 slice-start.3
  35.5 1.6 %collective-permute-done.8.refs_3_ = bf16[4,64,128]{2,1,0:T(8,128)(2,1)S(1)} collective-permute-done((bf16[4,64,128]{2,1,0:T(8,128)(2,1)S(1)}, bf16[4,64,128]{2,1,0:T(8,128)(2,1)S(1)}, u32[]{:S(2)}, u32[]{:S(2)}) %collective-permute-start.8) | collective-permute-done | bytes 65568 | tf_op jit(solution)/shard_map/ppermute | solution.py:538
  37.1 1.6 %attend.7 = bf16[8,80,128]{2,1,0:T(8,128)(2,1)S(1)} custom-call(s32[1]{0:T(128)} %bitcast.refs_0_, s32[1]{0:T(128)} %bitcast.1.refs_1_.bank, s32[64,128]{1,0:T(8,128)S(1)} %get-tuple-element.30.refs_2_, bf16[4,64,128]{2,1,0:T(8,128)(2,1)S(1)} %collective-permute-done.8.refs_3_, bf16[8,256,1024]{2,1,0:T(8,128)(2,1)S(1)} %copy-done, ...), custom_call_target="tpu_custom_call" | custom-call | flops 33554432 | bytes 16777216 | tf_op jit(solution)/shard_map/attend/pallas_call | solution.py:418
  38.7 13.9 %all_to_all.10.parts_ref = bf16[8,80,128]{2,1,0:T(8,128)(2,1)S(1)} all-to-all(bf16[8,80,128]{2,1,0:T(8,128)(2,1)S(1)} %attend.7), channel_id=1, replica_groups=mesh['groups'=2,'tensor'=8,'bank'=2] {'tensor'}, dimensions={0} | all-to-all | bytes 327680 | tf_op jit(solution)/shard_map/all_to_all | solution.py:530
  52.6 0.5 combine.1.x_ref
  53.0 0.0 slice-done
  53.1 0.0 slice-done.1
  53.1 0.0 slice-done.2
  53.1 0.0 slice-done.3
  53.1 2.3 %output.1 = bf16[8,8,1024]{2,1,0:T(8,128)(2,1)S(1)} custom-call(bf16[8,1024]{1,0:T(8,128)(2,1)S(1)} %combine.1.x_ref, bf16[1024,8192]{1,0:T(8,128)(2,1)S(1)} %bitcast.4), custom_call_target="tpu_custom_call" | custom-call | flops 134217728 | bytes 16777216 | tf_op jit(solution)/shard_map/output/pallas_call | solution.py:496
  55.4 9.7 %all_to_all.11.parts_ref = bf16[8,8,1024]{2,1,0:T(8,128)(2,1)S(1)} all-to-all(bf16[8,8,1024]{2,1,0:T(8,128)(2,1)S(1)} %output.1), channel_id=1, replica_groups=mesh['groups'=2,'tensor'=8,'bank'=2] {'tensor'}, dimensions={0} | all-to-all | bytes 262144 | tf_op jit(solution)/shard_map/all_to_all | solution.py:530
  65.1 0.6 residual.1
  (7 shorter events, 0.1 us)
Async XLA Ops:
  0.0 4.0 %collective-permute-start = (bf16[8,1024]{1,0:T(8,128)(2,1)}, bf16[8,1024]{1,0:T(8,128)(2,1)S(1)}, u32[]{:S(2)}, u32[]{:S(2)}) collective-permute-start(bf16[8,1024]{1,0:T(8,128)(2,1)} %x_ref.3), channel_id=1, source_target_pairs={{0,1},{1,0},{2,3},{3,2},{4,5},{5,4},{6,7},{7,6},{8,9},{9,8},{10,11... | collective-permute-start | bytes 49160 | tf_op jit(solution)/shard_map/ppermute | solution.py:526
  0.5 3.5 %collective-permute-start.1 = (s32[8]{0:T(128)}, s32[8]{0:T(128)S(1)}, u32[]{:S(2)}, u32[]{:S(2)}) collective-permute-start(s32[8]{0:T(128)} %own_ref.1), channel_id=1, source_target_pairs={{0,1},{1,0},{2,3},{3,2},{4,5},{5,4},{6,7},{7,6},{8,9},{9,8},{10,11... | collective-permute-start | bytes 104 | tf_op jit(solution)/shard_map/ppermute | solution.py:526
  0.5 3.5 %copy-start.3 = (bf16[8,1024]{1,0:T(8,128)(2,1)S(1)}, bf16[8,1024]{1,0:T(8,128)(2,1)}, u32[]{:S(2)}) copy-start(bf16[8,1024]{1,0:T(8,128)(2,1)} %x_ref.3) | copy-start | bytes 49156
  3.9 4.9 %copy-start.4 = (s32[8]{0:T(128)S(1)}, s32[8]{0:T(128)}, u32[]{:S(2)}) copy-start(s32[8]{0:T(128)} %refs_2_.3) | copy-start | bytes 100
  5.8 6.8 %collective-permute-start.2 = (f32[4,16,768]{2,1,0:T(8,128)S(1)}, f32[4,16,768]{2,1,0:T(8,128)S(1)}, u32[]{:S(2)}, u32[]{:S(2)}) collective-permute-start(f32[4,16,768]{2,1,0:T(8,128)S(1)} %get-tuple-element.33), channel_id=1, source_target_pairs={{0,2},{1,5},{2,0},{3,7},{4,6},{5,1},{6,4},{7,3},{8,10},{9,13},{10,... | collective-permute-start | bytes 589832 | tf_op jit(solution)/shard_map/ppermute | solution.py:538
  8.8 13.6 %copy-start.2 = (bf16[16,64,1024]{2,1,0:T(8,128)(2,1)S(1)}, bf16[16,64,1024]{2,1,0:T(8,128)(2,1)}, u32[]{:S(2)}) copy-start(bf16[16,64,1024]{2,1,0:T(8,128)(2,1)} %up_ref.1) | copy-start | bytes 6291460
  8.8 18.3 %copy-start = (bf16[8,256,1024]{2,1,0:T(8,128)(2,1)S(1)}, bf16[8,256,1024]{2,1,0:T(8,128)(2,1)}, u32[]{:S(2)}) copy-start(bf16[8,256,1024]{2,1,0:T(8,128)(2,1)} %refs_4_.7) | copy-start | bytes 12582916
  8.8 18.3 %copy-start.1 = (bf16[8,256,1024]{2,1,0:T(8,128)(2,1)S(1)}, bf16[8,256,1024]{2,1,0:T(8,128)(2,1)}, u32[]{:S(2)}) copy-start(bf16[8,256,1024]{2,1,0:T(8,128)(2,1)} %refs_5_.9) | copy-start | bytes 12582916
  12.6 4.7 %collective-permute-start.3 = (f32[2,16,768]{2,1,0:T(8,128)S(1)}, f32[2,16,768]{2,1,0:T(8,128)S(1)}, u32[]{:S(2)}, u32[]{:S(2)}) collective-permute-start(f32[2,16,768]{2,1,0:T(8,128)S(1)} %get-tuple-element.35), channel_id=1, source_target_pairs={{0,4},{1,3},{2,6},{3,1},{4,0},{5,7},{6,2},{7,5},{8,12},{9,11},{10,... | collective-permute-start | bytes 294920 | tf_op jit(solution)/shard_map/ppermute | solution.py:538
  17.3 5.1 %collective-permute-start.4 = (f32[1,16,768]{2,1,0:T(8,128)S(1)}, f32[1,16,768]{2,1,0:T(8,128)S(1)}, u32[]{:S(2)}, u32[]{:S(2)}) collective-permute-start(f32[1,16,768]{2,1,0:T(8,128)S(1)} %get-tuple-element.37), channel_id=1, source_target_pairs={{0,8},{1,9},{2,10},{3,11},{4,12},{5,13},{6,14},{7,15},{8,0},{9,1},... | collective-permute-start | bytes 147464 | tf_op jit(solution)/shard_map/ppermute | solution.py:538
  22.8 1.2 %collective-permute-start.5 = (f32[8,1152]{1,0:T(8,128)S(1)}, f32[8,1152]{1,0:T(8,128)S(1)}, u32[]{:S(2)}, u32[]{:S(2)}) collective-permute-start(f32[8,1152]{1,0:T(8,128)S(1)} %get-tuple-element.39), channel_id=1, source_target_pairs={{0,1},{1,0},{2,3},{3,2},{4,5},{5,4},{6,7},{7,6},{8,9},{9,8},{10,11... | collective-permute-start | bytes 110600 | tf_op jit(solution)/shard_map/ppermute | solution.py:526
  24.1 4.7 %collective-permute-start.6 = (bf16[1,64,128]{2,1,0:T(8,128)(2,1)S(1)}, bf16[1,64,128]{2,1,0:T(8,128)(2,1)S(1)}, u32[]{:S(2)}, u32[]{:S(2)}) collective-permute-start(bf16[1,64,128]{2,1,0:T(8,128)(2,1)S(1)} %get-tuple-element.40.refs_3_.first_ref.q_ref), channel_id=1, source_target_pairs={{0,8},{1,9},{2,10},{3,11},{4,12},{5,13},{6,14},{7,15},{8,0},{9,1},... | collective-permute-start | bytes 49160 | tf_op jit(solution)/shard_map/ppermute | solution.py:538
  27.1 25.9 %slice-start = ((s8[16777216]{0:T(1024)(128)(4,1)}), s8[4194304]{0:T(1024)(128)(4,1)S(1)}, s32[]{:S(2)}) async-start(s8[16777216]{0:T(1024)(128)(4,1)} %bitcast.3), calls=%async_computation.2 | async-start | bytes 8388608
  28.9 24.2 %slice-start.1 = ((s8[16777216]{0:T(1024)(128)(4,1)}), s8[4194304]{0:T(1024)(128)(4,1)S(1)}, s32[]{:S(2)}) async-start(s8[16777216]{0:T(1024)(128)(4,1)} %bitcast.3), calls=%async_computation.3 | async-start | bytes 8388608
  28.9 3.9 %collective-permute-start.7 = (bf16[2,64,128]{2,1,0:T(8,128)(2,1)S(1)}, bf16[2,64,128]{2,1,0:T(8,128)(2,1)S(1)}, u32[]{:S(2)}, u32[]{:S(2)}) collective-permute-start(bf16[2,64,128]{2,1,0:T(8,128)(2,1)S(1)} %join.2.first_ref), channel_id=1, source_target_pairs={{0,4},{1,3},{2,6},{3,1},{4,0},{5,7},{6,2},{7,5},{8,12},{9,11},{10,... | collective-permute-start | bytes 98312 | tf_op jit(solution)/shard_map/ppermute | solution.py:538
  32.8 20.3 %slice-start.2 = ((s8[16777216]{0:T(1024)(128)(4,1)}), s8[4194304]{0:T(1024)(128)(4,1)S(1)}, s32[]{:S(2)}) async-start(s8[16777216]{0:T(1024)(128)(4,1)} %bitcast.3), calls=%async_computation.4 | async-start | bytes 8388608
  32.8 4.3 %collective-permute-start.8 = (bf16[4,64,128]{2,1,0:T(8,128)(2,1)S(1)}, bf16[4,64,128]{2,1,0:T(8,128)(2,1)S(1)}, u32[]{:S(2)}, u32[]{:S(2)}) collective-permute-start(bf16[4,64,128]{2,1,0:T(8,128)(2,1)S(1)} %join.3), channel_id=1, source_target_pairs={{0,2},{1,5},{2,0},{3,7},{4,6},{5,1},{6,4},{7,3},{8,10},{9,13},{10,... | collective-permute-start | bytes 196616 | tf_op jit(solution)/shard_map/ppermute | solution.py:538
  35.5 17.6 %slice-start.3 = ((s8[16777216]{0:T(1024)(128)(4,1)}), s8[4194304]{0:T(1024)(128)(4,1)S(1)}, s32[]{:S(2)}) async-start(s8[16777216]{0:T(1024)(128)(4,1)} %bitcast.3), calls=%async_computation.5 | async-start | bytes 8388608

commit v10 on v9

--- a/solution.py
+++ b/solution.py
@@ -244,8 +244,11 @@
     )(place, bank, length, x, other, wq, wkv, inner)
 
 
-def correct_kernel(bank, column_ref, kept_ref, came_ref, up_ref, own_out, other_out):
-    total = kept_ref[0] + came_ref[0]
+def correct_kernel(bank, column_ref, up_ref, *refs):
+    *parts, own_out, other_out = refs
+    total = parts[0][...]
+    for part in parts[1:]:
+        total += part[...]
     count, rank, width = up_ref.shape
     half = width // 2
     inner = total[:, half + HEAD_DIM :].astype(BF16).astype(F32)
@@ -272,12 +275,12 @@
     other_out[:, width:] = total[rows:, half : half + HEAD_DIM]
 
 
-def correct(bank, column, kept, came, up):
-    rows = kept.shape[1]
+def correct(bank, column, up, parts):
+    rows = parts[0].shape[0]
     out = shape(rows // 2, up.shape[2] + HEAD_DIM)
     return pl.pallas_call(
         correct_kernel,
-        in_specs=[scalar()] + [whole()] * 4,
+        in_specs=[scalar()] + [whole()] * (2 + len(parts)),
         out_specs=[whole()] * 2,
         out_shape=[out, out],
         compiler_params=params(),
@@ -285,24 +288,22 @@
             flops=2 * rows * up.size, bytes_accessed=2 * up.size, transcendentals=0
         ),
         name="correct",
-    )(bank, column, kept, came, up)
-
-
-def halve_kernel(kept_ref, came_ref, sent_out, kept_out):
-    for i in range(kept_out.shape[0]):
-        kept_out[i] = kept_ref[2 * i] + came_ref[2 * i]
-        sent_out[i] = kept_ref[2 * i + 1] + came_ref[2 * i + 1]
-
-
-def halve(kept, came):
-    half = jax.ShapeDtypeStruct((kept.shape[0] // 2,) + kept.shape[1:], kept.dtype)
-    return pl.pallas_call(
-        halve_kernel,
+    )(bank, column, up, *parts)
+
+
+def part_kernel(kept_ref, came_ref, *outs):
+    for i, out in enumerate(outs):
+        out[...] = kept_ref[i] + came_ref[i]
+
+
+def part(kept, came):
+    return pl.pallas_call(
+        part_kernel,
         in_specs=[whole()] * 2,
-        out_specs=[whole()] * 2,
-        out_shape=[half, half],
-        compiler_params=params(),
-        name="halve",
+        out_specs=[whole()] * kept.shape[0],
+        out_shape=[shape(*kept.shape[1:])] * kept.shape[0],
+        compiler_params=params(),
+        name="part",
     )(kept, came)
 
 
@@ -342,21 +343,21 @@
     )(bank, own, came, cosine, sine)
 
 
-def join_kernel(first_ref, second_ref, out_ref):
-    half = first_ref.shape[0]
-    out_ref[:half] = first_ref[...]
-    out_ref[half:] = second_ref[...]
-
-
-def join(first, second):
+def join_kernel(*refs):
+    *parts, out_ref = refs
+    for i, part in enumerate(parts):
+        out_ref[i] = part[0]
+
+
+def join(parts):
     return pl.pallas_call(
         join_kernel,
-        in_specs=[whole()] * 2,
+        in_specs=[whole()] * len(parts),
         out_specs=whole(),
-        out_shape=shape(2 * first.shape[0], *first.shape[1:], dtype=first.dtype),
+        out_shape=shape(len(parts), *parts[0].shape[1:], dtype=parts[0].dtype),
         compiler_params=params(),
         name="join",
-    )(first, second)
+    )(*parts)
 
 
 def attend_kernel(slots, earlier, place, bank, length_ref, q_ref, k_ref, v_ref, *refs):
@@ -570,21 +571,21 @@
     kept, length = project_kept(
         place, bank, beam_cache_length, x, x_other, *weights, inner, ranks
     )
-    sent, kept = halve(kept, came)
-    sent, kept = halve(kept, hop(sent, 2))
-    own, other = correct(bank, column, kept, hop(sent, 4), lowrank_up_factors)
+    kept, *sent = part(kept, came)
+    near = tuple(range(2, ranks, 2))
+    parts = [kept] + [hop(block, slot) for block, slot in zip(sent, near)]
+    own, other = correct(bank, column, lowrank_up_factors, parts)
     query, key_new, value_new = rotated(bank, own, swapped(other), cosine, sine)
 
     def attended_part(queries, slots, **more):
         cache = paged_key_cache, paged_value_cache
         return attend(place, bank, length, queries, *cache, slots, **more)
 
-    came, done = lax.optimization_barrier((hop(query, 4), attended_part(query, (0,))))
-    gathered = join(query, came)
-    second, more = lax.optimization_barrier((hop(gathered, 2), attended_part(came, (4,))))
-    came = hop(join(gathered, second), 1)
-    done = done, more, attended_part(second, (2, 6))
-    partial = attended_part(came, (1, 5, 3, 7), earlier=(0, 4, 2, 6), before=done)
+    gathered = join([query] + [hop(query, slot) for slot in near])
+    came = hop(gathered, 1)
+    done = attended_part(gathered, (0, *near))
+    odd = tuple(slot + 1 for slot in (0, *near))
+    partial = attended_part(came, odd, earlier=(0, *near), before=(done,))
     attended = combine(traded(partial), query, key_new, value_new)
     return residual(x, traded(output(attended, output_weight, ranks)))
 

time: 65.9 us -> 63.7 us (0.967)
  starting transfers between devices: 15.4 us -> 14 us
  blocking collectives: 23.6 us -> 22.4 us
  waiting for transfers between devices: 10.1 us -> 10.8 us
    ppermute x6 -> x8, starting transfers between devices: 14.9 us -> 13.5 us  [hop(): return lax.ppermute(x, ('tensor', 'bank'), pairs)]
    all_to_all x2, blocking collectives: 23.6 us -> 22.4 us  [traded(): return lax.all_to_all(blocks, 'tensor', 0, 0, tiled=True)]
    ppermute x6 -> x8, waiting for transfers between devices: 9.01 us -> 9.69 us  [hop(): return lax.ppermute(x, ('tensor', 'bank'), pairs)]
    pallas_call x4 -> x2, Pallas kernels: 3.41 us -> 3.12 us  [attend(): pl.pallas_call(lambda *refs: attend_kernel(slots, earlier, *refs), in_spe...]
  transfers between devices with their start and end apart: 9 -> 11, of which waited for: 6 -> 6; matrix products, arithmetic and copies ran while one was open for 0% -> 0% of each run, Pallas kernels for 14% -> 14%
where the time goes in v10:
time: 63.7 us; the launch traced here: 63.5 us
  blocking collectives  22.4 us (35%)
  Pallas kernels  16 us (25%)
  starting transfers between devices  14 us (22%)
  waiting for transfers between devices  10.8 us (17%)
    all_to_all x2, blocking collectives, traded(): return lax.all_to_all(blocks, 'tensor', 0, 0, tiled=True)  22.4 us
    ppermute x8, starting transfers between devices, hop(): return lax.ppermute(x, ('tensor', 'bank'), pairs)  13.5 us
    ppermute x8, waiting for transfers between devices, hop(): return lax.ppermute(x, ('tensor', 'bank'), pairs)  9.69 us
    pallas_call x1, Pallas kernels, project_kept(): pl.pallas_call(lambda *refs: project_kept_kernel(ranks, *refs), in_specs=...  3.75 us
    pallas_call x1, Pallas kernels, fetch(): pl.pallas_call(lambda *refs: fetch_kernel(ranks, *refs), in_specs=[scalar...  3.41 us
    pallas_call x2, Pallas kernels, attend(): pl.pallas_call(lambda *refs: attend_kernel(slots, earlier, *refs), in_spe...  3.12 us
    pallas_call x1, Pallas kernels, output(): pl.pallas_call(output_kernel, in_specs=[whole()] * 2, out_specs=whole(),...  2.28 us
    pallas_call x1, Pallas kernels, project_sent(): pl.pallas_call(project_sent_kernel, in_specs=[scalar(), big(), pl.BlockSp...  1.77 us
  transfers between devices with their start and end apart: 11, of which 6 were waited for; matrix products, arithmetic and copies ran while one was open for 0% of the time, Pallas kernels for 14%

profile of v10, /device:TPU:0, one launch (start us, length us, event | category | flops | bytes accessed | tf_op | source)
XLA Modules:
  0.0 63.5 jit_solution(3721823477078387082)
XLA Ops:
  0.0 0.5 collective-permute-start
  0.5 0.1 collective-permute-start.1
  0.5 0.0 copy-start.3
  0.5 3.4 %fetch.1 = (bf16[4,1024,512]{2,1,0:T(8,128)(2,1)S(1)}, bf16[4,1024,128]{2,1,0:T(8,128)(2,1)S(1)}, bf16[16,64,1024]{2,1,0:T(8,128)(2,1)S(1)}) custom-call(s32[1]{0:T(128)} %bitcast.refs_0_, s32[1]{0:T(128)} %bitcast.1.refs_1_.bank, bf16[1024,8192]{1,0:T(8,128)(2,1)} %refs_5_.3, bf16[1024,2048]{1,0:T(8,128)(2,1)} %refs_6_.1, bf16[16,64,1024]{2,1,0:T(8,128)(2,1)} %bitcast.5), custom_call_target="tpu_custom_call" | custom-call | bytes 7340032 | tf_op jit(solution)/shard_map/fetch/pallas_call | solution.py:119
  3.9 0.0 copy-start.4
  3.9 0.0 collective-permute-done.1.came_ref
  4.0 0.0 collective-permute-done.other_ref.refs_4_
  4.0 0.0 copy-done.3
  4.0 0.0 copy-start.2
  4.0 1.8 %project_sent.1 = (f32[4,16,768]{2,1,0:T(8,128)S(1)}, f32[16,128]{1,0:T(8,128)S(1)}, s32[16,128]{1,0:T(8,128)S(1)}) custom-call(s32[1]{0:T(128)} %bitcast.1.refs_1_.bank, s32[8]{0:T(128)} %own_ref.1, s32[8]{0:T(128)S(1)} %collective-permute-done.1.came_ref, bf16[8,1024]{1,0:T(8,128)(2,1)S(1)} %copy-done.3, ...), custom_call_target="tpu_custom_call" | custom-call | flops 117440512 | bytes 7340032 | tf_op jit(solution)/shard_map/project_sent/pallas_call | solution.py:183
  5.8 3.0 %collective-permute-start.2 = (f32[4,16,768]{2,1,0:T(8,128)S(1)}, f32[4,16,768]{2,1,0:T(8,128)S(1)}, u32[]{:S(2)}, u32[]{:S(2)}) collective-permute-start(f32[4,16,768]{2,1,0:T(8,128)S(1)} %get-tuple-element.29), channel_id=1, source_target_pairs={{0,2},{1,5},{2,0},{3,7},{4,6},{5,1},{6,4},{7,3},{8,10},{9,13},{10,... | collective-permute-start | bytes 589832 | tf_op jit(solution)/shard_map/ppermute | solution.py:539
  8.8 0.0 copy-done.4
  8.8 0.0 copy-start
  8.8 0.0 copy-start.1
  8.8 0.0 slice-start
  8.8 0.0 slice-start.1
  8.8 0.0 slice-start.2
  8.8 3.8 %project_kept.1 = (f32[4,16,768]{2,1,0:T(8,128)S(1)}, s32[64,128]{1,0:T(8,128)S(1)}) custom-call(s32[1]{0:T(128)} %bitcast.refs_0_, s32[1]{0:T(128)} %bitcast.1.refs_1_.bank, s32[8]{0:T(128)S(1)} %copy-done.4, bf16[8,1024]{1,0:T(8,128)(2,1)S(1)} %copy-done.3, bf16[8,1024]{1,0:T(8,128)(2,1)S(1)} %collective-permute-done.other_ref.refs_4_, ...), custom_call_target="tpu_custom_call" | custom-call | flops 83886080 | bytes 10485760 | tf_op jit(solution)/shard_map/project_kept/pallas_call | solution.py:228
  12.6 0.0 collective-permute-done.2.came_ref
  12.6 2.0 %collective-permute-start.3 = (f32[16,768]{1,0:T(8,128)S(1)}, f32[16,768]{1,0:T(8,128)S(1)}, u32[]{:S(2)}, u32[]{:S(2)}) collective-permute-start(f32[16,768]{1,0:T(8,128)S(1)} %get-tuple-element.31), channel_id=1, source_target_pairs={{0,4},{1,3},{2,6},{3,1},{4,0},{5,7},{6,2},{7,5},{8,12},{9,11},{10,... | collective-permute-start | bytes 147464 | tf_op jit(solution)/shard_map/ppermute | solution.py:539
  14.6 2.6 %collective-permute-start.4 = (f32[16,768]{1,0:T(8,128)S(1)}, f32[16,768]{1,0:T(8,128)S(1)}, u32[]{:S(2)}, u32[]{:S(2)}) collective-permute-start(f32[16,768]{1,0:T(8,128)S(1)} %get-tuple-element.32), channel_id=1, source_target_pairs={{0,8},{1,9},{2,10},{3,11},{4,12},{5,13},{6,14},{7,15},{8,0},{9,1},... | collective-permute-start | bytes 147464 | tf_op jit(solution)/shard_map/ppermute | solution.py:539
  17.2 0.0 collective-permute-start.5
  17.2 0.0 collective-permute-done.3.refs_1_
  17.2 3.8 %collective-permute-done.4.refs_2_ = f32[16,768]{1,0:T(8,128)S(1)} collective-permute-done((f32[16,768]{1,0:T(8,128)S(1)}, f32[16,768]{1,0:T(8,128)S(1)}, u32[]{:S(2)}, u32[]{:S(2)}) %collective-permute-start.4) | collective-permute-done | bytes 49184 | tf_op jit(solution)/shard_map/ppermute | solution.py:539
  21.0 2.1 %collective-permute-done.5.refs_3_ = f32[16,768]{1,0:T(8,128)S(1)} collective-permute-done((f32[16,768]{1,0:T(8,128)S(1)}, f32[16,768]{1,0:T(8,128)S(1)}, u32[]{:S(2)}, u32[]{:S(2)}) %collective-permute-start.5) | collective-permute-done | bytes 49184 | tf_op jit(solution)/shard_map/ppermute | solution.py:539
  23.1 0.0 copy-done.2
  23.1 0.4 correct.1
  23.5 0.0 collective-permute-start.6
  23.5 0.1 fusion
  23.6 1.1 %collective-permute-done.6.came_ref = f32[8,1152]{1,0:T(8,128)S(1)} collective-permute-done((f32[8,1152]{1,0:T(8,128)S(1)}, f32[8,1152]{1,0:T(8,128)S(1)}, u32[]{:S(2)}, u32[]{:S(2)}) %collective-permute-start.6) | collective-permute-done | bytes 36896 | tf_op jit(solution)/shard_map/ppermute | solution.py:527
  24.7 0.1 rotate.1
  24.8 0.1 collective-permute-start.7
  24.9 1.4 %collective-permute-start.8 = (bf16[1,64,128]{2,1,0:T(8,128)(2,1)S(1)}, bf16[1,64,128]{2,1,0:T(8,128)(2,1)S(1)}, u32[]{:S(2)}, u32[]{:S(2)}) collective-permute-start(bf16[1,64,128]{2,1,0:T(8,128)(2,1)S(1)} %get-tuple-element.36.refs_0_.q_ref), channel_id=1, source_target_pairs={{0,8},{1,9},{2,10},{3,11},{4,12},{5,13},{6,14},{7,15},{8,0},{9,1},... | collective-permute-start | bytes 49160 | tf_op jit(solution)/shard_map/ppermute | solution.py:539
  26.3 3.0 %collective-permute-start.9 = (bf16[1,64,128]{2,1,0:T(8,128)(2,1)S(1)}, bf16[1,64,128]{2,1,0:T(8,128)(2,1)S(1)}, u32[]{:S(2)}, u32[]{:S(2)}) collective-permute-start(bf16[1,64,128]{2,1,0:T(8,128)(2,1)S(1)} %get-tuple-element.36.refs_0_.q_ref), channel_id=1, source_target_pairs={{0,12},{1,11},{2,14},{3,9},{4,8},{5,15},{6,10},{7,13},{8,4},{9,3},... | collective-permute-start | bytes 49160 | tf_op jit(solution)/shard_map/ppermute | solution.py:539
  29.3 0.0 collective-permute-done.7.refs_1_
  29.3 0.3 collective-permute-done.8.refs_2_
  29.6 2.2 %collective-permute-done.9.refs_3_ = bf16[1,64,128]{2,1,0:T(8,128)(2,1)S(1)} collective-permute-done((bf16[1,64,128]{2,1,0:T(8,128)(2,1)S(1)}, bf16[1,64,128]{2,1,0:T(8,128)(2,1)S(1)}, u32[]{:S(2)}, u32[]{:S(2)}) %collective-permute-start.9) | collective-permute-done | bytes 16416 | tf_op jit(solution)/shard_map/ppermute | solution.py:539
  31.9 1.4 %collective-permute-start.10 = (bf16[4,64,128]{2,1,0:T(8,128)(2,1)S(1)}, bf16[4,64,128]{2,1,0:T(8,128)(2,1)S(1)}, u32[]{:S(2)}, u32[]{:S(2)}) collective-permute-start(bf16[4,64,128]{2,1,0:T(8,128)(2,1)S(1)} %join.1.refs_3_), channel_id=1, source_target_pairs={{0,2},{1,5},{2,0},{3,7},{4,6},{5,1},{6,4},{7,3},{8,10},{9,13},{10,... | collective-permute-start | bytes 196616 | tf_op jit(solution)/shard_map/ppermute | solution.py:539
  33.3 0.0 copy-done
  33.3 0.0 copy-done.1
  33.3 0.0 slice-start.3
  33.3 1.6 %attend.2.refs_6_ = bf16[4,80,128]{2,1,0:T(8,128)(2,1)S(1)} custom-call(s32[1]{0:T(128)} %bitcast.refs_0_, s32[1]{0:T(128)} %bitcast.1.refs_1_.bank, s32[64,128]{1,0:T(8,128)S(1)} %get-tuple-element.26.refs_2_, bf16[4,64,128]{2,1,0:T(8,128)(2,1)S(1)} %join.1.refs_3_, bf16[8,256,1024]{2,1,0:T(8,128)(2,1)S(1)} %copy-done, bf16[8,256,1024]{2,1,0:T(8,128)(2,1)S(1)} %copy-done.1), custom_call_target="tpu_custom_call" | custom-call | flops 33554432 | bytes 4194304 | tf_op jit(solution)/shard_map/attend/pallas_call | solution.py:419
  34.9 1.3 %collective-permute-done.10.refs_3_ = bf16[4,64,128]{2,1,0:T(8,128)(2,1)S(1)} collective-permute-done((bf16[4,64,128]{2,1,0:T(8,128)(2,1)S(1)}, bf16[4,64,128]{2,1,0:T(8,128)(2,1)S(1)}, u32[]{:S(2)}, u32[]{:S(2)}) %collective-permute-start.10) | collective-permute-done | bytes 65568 | tf_op jit(solution)/shard_map/ppermute | solution.py:539
  36.1 1.6 %attend.3 = bf16[8,80,128]{2,1,0:T(8,128)(2,1)S(1)} custom-call(s32[1]{0:T(128)} %bitcast.refs_0_, s32[1]{0:T(128)} %bitcast.1.refs_1_.bank, s32[64,128]{1,0:T(8,128)S(1)} %get-tuple-element.26.refs_2_, bf16[4,64,128]{2,1,0:T(8,128)(2,1)S(1)} %collective-permute-done.10.refs_3_, bf16[8,256,1024]{2,1,0:T(8,128)(2,1)S(1)} %copy-done, ...), custom_call_target="tpu_custom_call" | custom-call | flops 33554432 | bytes 16777216 | tf_op jit(solution)/shard_map/attend/pallas_call | solution.py:419
  37.7 12.7 %all_to_all.10.parts_ref = bf16[8,80,128]{2,1,0:T(8,128)(2,1)S(1)} all-to-all(bf16[8,80,128]{2,1,0:T(8,128)(2,1)S(1)} %attend.3), channel_id=1, replica_groups=mesh['groups'=2,'tensor'=8,'bank'=2] {'tensor'}, dimensions={0} | all-to-all | bytes 327680 | tf_op jit(solution)/shard_map/all_to_all | solution.py:531
  50.3 0.5 combine.1.x_ref
  50.8 0.0 slice-done
  50.8 0.0 slice-done.1
  50.8 0.0 slice-done.2
  50.8 0.0 slice-done.3
  50.9 2.3 %output.1 = bf16[8,8,1024]{2,1,0:T(8,128)(2,1)S(1)} custom-call(bf16[8,1024]{1,0:T(8,128)(2,1)S(1)} %combine.1.x_ref, bf16[1024,8192]{1,0:T(8,128)(2,1)S(1)} %bitcast.4), custom_call_target="tpu_custom_call" | custom-call | flops 134217728 | bytes 16777216 | tf_op jit(solution)/shard_map/output/pallas_call | solution.py:497
  53.2 9.7 %all_to_all.11.parts_ref = bf16[8,8,1024]{2,1,0:T(8,128)(2,1)S(1)} all-to-all(bf16[8,8,1024]{2,1,0:T(8,128)(2,1)S(1)} %output.1), channel_id=1, replica_groups=mesh['groups'=2,'tensor'=8,'bank'=2] {'tensor'}, dimensions={0} | all-to-all | bytes 262144 | tf_op jit(solution)/shard_map/all_to_all | solution.py:531
  62.9 0.6 residual.1
  (5 shorter events, 0.0 us)
Async XLA Ops:
  0.0 4.0 %collective-permute-start = (bf16[8,1024]{1,0:T(8,128)(2,1)}, bf16[8,1024]{1,0:T(8,128)(2,1)S(1)}, u32[]{:S(2)}, u32[]{:S(2)}) collective-permute-start(bf16[8,1024]{1,0:T(8,128)(2,1)} %x_ref.3), channel_id=1, source_target_pairs={{0,1},{1,0},{2,3},{3,2},{4,5},{5,4},{6,7},{7,6},{8,9},{9,8},{10,11... | collective-permute-start | bytes 49160 | tf_op jit(solution)/shard_map/ppermute | solution.py:527
  0.5 3.5 %collective-permute-start.1 = (s32[8]{0:T(128)}, s32[8]{0:T(128)S(1)}, u32[]{:S(2)}, u32[]{:S(2)}) collective-permute-start(s32[8]{0:T(128)} %own_ref.1), channel_id=1, source_target_pairs={{0,1},{1,0},{2,3},{3,2},{4,5},{5,4},{6,7},{7,6},{8,9},{9,8},{10,11... | collective-permute-start | bytes 104 | tf_op jit(solution)/shard_map/ppermute | solution.py:527
  0.5 3.5 %copy-start.3 = (bf16[8,1024]{1,0:T(8,128)(2,1)S(1)}, bf16[8,1024]{1,0:T(8,128)(2,1)}, u32[]{:S(2)}) copy-start(bf16[8,1024]{1,0:T(8,128)(2,1)} %x_ref.3) | copy-start | bytes 49156
  3.9 4.9 %copy-start.4 = (s32[8]{0:T(128)S(1)}, s32[8]{0:T(128)}, u32[]{:S(2)}) copy-start(s32[8]{0:T(128)} %refs_2_.3) | copy-start | bytes 100
  4.0 19.1 %copy-start.2 = (bf16[16,64,1024]{2,1,0:T(8,128)(2,1)S(1)}, bf16[16,64,1024]{2,1,0:T(8,128)(2,1)}, u32[]{:S(2)}) copy-start(bf16[16,64,1024]{2,1,0:T(8,128)(2,1)} %up_ref.1) | copy-start | bytes 6291460
  5.8 6.8 %collective-permute-start.2 = (f32[4,16,768]{2,1,0:T(8,128)S(1)}, f32[4,16,768]{2,1,0:T(8,128)S(1)}, u32[]{:S(2)}, u32[]{:S(2)}) collective-permute-start(f32[4,16,768]{2,1,0:T(8,128)S(1)} %get-tuple-element.29), channel_id=1, source_target_pairs={{0,2},{1,5},{2,0},{3,7},{4,6},{5,1},{6,4},{7,3},{8,10},{9,13},{10,... | collective-permute-start | bytes 589832 | tf_op jit(solution)/shard_map/ppermute | solution.py:539
  8.8 24.5 %copy-start = (bf16[8,256,1024]{2,1,0:T(8,128)(2,1)S(1)}, bf16[8,256,1024]{2,1,0:T(8,128)(2,1)}, u32[]{:S(2)}) copy-start(bf16[8,256,1024]{2,1,0:T(8,128)(2,1)} %refs_4_.3) | copy-start | bytes 12582916
  8.8 24.5 %copy-start.1 = (bf16[8,256,1024]{2,1,0:T(8,128)(2,1)S(1)}, bf16[8,256,1024]{2,1,0:T(8,128)(2,1)}, u32[]{:S(2)}) copy-start(bf16[8,256,1024]{2,1,0:T(8,128)(2,1)} %refs_5_.5) | copy-start | bytes 12582916
  8.8 42.0 %slice-start = ((s8[16777216]{0:T(1024)(128)(4,1)}), s8[4194304]{0:T(1024)(128)(4,1)S(1)}, s32[]{:S(2)}) async-start(s8[16777216]{0:T(1024)(128)(4,1)} %bitcast.3), calls=%async_computation.2 | async-start | bytes 8388608
  8.8 42.0 %slice-start.1 = ((s8[16777216]{0:T(1024)(128)(4,1)}), s8[4194304]{0:T(1024)(128)(4,1)S(1)}, s32[]{:S(2)}) async-start(s8[16777216]{0:T(1024)(128)(4,1)} %bitcast.3), calls=%async_computation.3 | async-start | bytes 8388608
  8.8 42.0 %slice-start.2 = ((s8[16777216]{0:T(1024)(128)(4,1)}), s8[4194304]{0:T(1024)(128)(4,1)S(1)}, s32[]{:S(2)}) async-start(s8[16777216]{0:T(1024)(128)(4,1)} %bitcast.3), calls=%async_computation.4 | async-start | bytes 8388608
  12.6 4.6 %collective-permute-start.3 = (f32[16,768]{1,0:T(8,128)S(1)}, f32[16,768]{1,0:T(8,128)S(1)}, u32[]{:S(2)}, u32[]{:S(2)}) collective-permute-start(f32[16,768]{1,0:T(8,128)S(1)} %get-tuple-element.31), channel_id=1, source_target_pairs={{0,4},{1,3},{2,6},{3,1},{4,0},{5,7},{6,2},{7,5},{8,12},{9,11},{10,... | collective-permute-start | bytes 147464 | tf_op jit(solution)/shard_map/ppermute | solution.py:539
  14.6 6.4 %collective-permute-start.4 = (f32[16,768]{1,0:T(8,128)S(1)}, f32[16,768]{1,0:T(8,128)S(1)}, u32[]{:S(2)}, u32[]{:S(2)}) collective-permute-start(f32[16,768]{1,0:T(8,128)S(1)} %get-tuple-element.32), channel_id=1, source_target_pairs={{0,8},{1,9},{2,10},{3,11},{4,12},{5,13},{6,14},{7,15},{8,0},{9,1},... | collective-permute-start | bytes 147464 | tf_op jit(solution)/shard_map/ppermute | solution.py:539
  17.2 5.9 %collective-permute-start.5 = (f32[16,768]{1,0:T(8,128)S(1)}, f32[16,768]{1,0:T(8,128)S(1)}, u32[]{:S(2)}, u32[]{:S(2)}) collective-permute-start(f32[16,768]{1,0:T(8,128)S(1)} %get-tuple-element.33), channel_id=1, source_target_pairs={{0,12},{1,11},{2,14},{3,9},{4,8},{5,15},{6,10},{7,13},{8,4},{9,3},... | collective-permute-start | bytes 147464 | tf_op jit(solution)/shard_map/ppermute | solution.py:539
  23.5 1.2 %collective-permute-start.6 = (f32[8,1152]{1,0:T(8,128)S(1)}, f32[8,1152]{1,0:T(8,128)S(1)}, u32[]{:S(2)}, u32[]{:S(2)}) collective-permute-start(f32[8,1152]{1,0:T(8,128)S(1)} %get-tuple-element.35), channel_id=1, source_target_pairs={{0,1},{1,0},{2,3},{3,2},{4,5},{5,4},{6,7},{7,6},{8,9},{9,8},{10,11... | collective-permute-start | bytes 110600 | tf_op jit(solution)/shard_map/ppermute | solution.py:527
  24.8 4.5 %collective-permute-start.7 = (bf16[1,64,128]{2,1,0:T(8,128)(2,1)S(1)}, bf16[1,64,128]{2,1,0:T(8,128)(2,1)S(1)}, u32[]{:S(2)}, u32[]{:S(2)}) collective-permute-start(bf16[1,64,128]{2,1,0:T(8,128)(2,1)S(1)} %get-tuple-element.36.refs_0_.q_ref), channel_id=1, source_target_pairs={{0,4},{1,3},{2,6},{3,1},{4,0},{5,7},{6,2},{7,5},{8,12},{9,11},{10,... | collective-permute-start | bytes 49160 | tf_op jit(solution)/shard_map/ppermute | solution.py:539
  24.9 4.7 %collective-permute-start.8 = (bf16[1,64,128]{2,1,0:T(8,128)(2,1)S(1)}, bf16[1,64,128]{2,1,0:T(8,128)(2,1)S(1)}, u32[]{:S(2)}, u32[]{:S(2)}) collective-permute-start(bf16[1,64,128]{2,1,0:T(8,128)(2,1)S(1)} %get-tuple-element.36.refs_0_.q_ref), channel_id=1, source_target_pairs={{0,8},{1,9},{2,10},{3,11},{4,12},{5,13},{6,14},{7,15},{8,0},{9,1},... | collective-permute-start | bytes 49160 | tf_op jit(solution)/shard_map/ppermute | solution.py:539
  26.3 5.5 %collective-permute-start.9 = (bf16[1,64,128]{2,1,0:T(8,128)(2,1)S(1)}, bf16[1,64,128]{2,1,0:T(8,128)(2,1)S(1)}, u32[]{:S(2)}, u32[]{:S(2)}) collective-permute-start(bf16[1,64,128]{2,1,0:T(8,128)(2,1)S(1)} %get-tuple-element.36.refs_0_.q_ref), channel_id=1, source_target_pairs={{0,12},{1,11},{2,14},{3,9},{4,8},{5,15},{6,10},{7,13},{8,4},{9,3},... | collective-permute-start | bytes 49160 | tf_op jit(solution)/shard_map/ppermute | solution.py:539
  31.9 4.3 %collective-permute-start.10 = (bf16[4,64,128]{2,1,0:T(8,128)(2,1)S(1)}, bf16[4,64,128]{2,1,0:T(8,128)(2,1)S(1)}, u32[]{:S(2)}, u32[]{:S(2)}) collective-permute-start(bf16[4,64,128]{2,1,0:T(8,128)(2,1)S(1)} %join.1.refs_3_), channel_id=1, source_target_pairs={{0,2},{1,5},{2,0},{3,7},{4,6},{5,1},{6,4},{7,3},{8,10},{9,13},{10,... | collective-permute-start | bytes 196616 | tf_op jit(solution)/shard_map/ppermute | solution.py:539
  33.3 17.6 %slice-start.3 = ((s8[16777216]{0:T(1024)(128)(4,1)}), s8[4194304]{0:T(1024)(128)(4,1)S(1)}, s32[]{:S(2)}) async-start(s8[16777216]{0:T(1024)(128)(4,1)} %bitcast.3), calls=%async_computation.5 | async-start | bytes 8388608

commit v11 on v10

--- a/solution.py
+++ b/solution.py
@@ -244,11 +244,8 @@
     )(place, bank, length, x, other, wq, wkv, inner)
 
 
-def correct_kernel(bank, column_ref, up_ref, *refs):
-    *parts, own_out, other_out = refs
-    total = parts[0][...]
-    for part in parts[1:]:
-        total += part[...]
+def correct_kernel(bank, column_ref, up_ref, parts_ref, own_out, other_out):
+    total = jnp.sum(parts_ref[...], axis=0)
     count, rank, width = up_ref.shape
     half = width // 2
     inner = total[:, half + HEAD_DIM :].astype(BF16).astype(F32)
@@ -276,11 +273,11 @@
 
 
 def correct(bank, column, up, parts):
-    rows = parts[0].shape[0]
+    rows = parts.shape[1]
     out = shape(rows // 2, up.shape[2] + HEAD_DIM)
     return pl.pallas_call(
         correct_kernel,
-        in_specs=[scalar()] + [whole()] * (2 + len(parts)),
+        in_specs=[scalar()] + [whole()] * 3,
         out_specs=[whole()] * 2,
         out_shape=[out, out],
         compiler_params=params(),
@@ -288,23 +285,24 @@
             flops=2 * rows * up.size, bytes_accessed=2 * up.size, transcendentals=0
         ),
         name="correct",
-    )(bank, column, up, *parts)
-
-
-def part_kernel(kept_ref, came_ref, *outs):
-    for i, out in enumerate(outs):
-        out[...] = kept_ref[i] + came_ref[i]
-
-
-def part(kept, came):
+    )(bank, column, up, parts)
+
+
+def part_kernel(place, bank, kept_ref, came_ref, out):
+    mine = jnp.where(bank[0] == 0, place[0], exchanged(place[0])) >> 1
+    for i in range(out.shape[0]):
+        out[mine ^ i] = kept_ref[i] + came_ref[i]
+
+
+def part(place, bank, kept, came):
     return pl.pallas_call(
         part_kernel,
-        in_specs=[whole()] * 2,
-        out_specs=[whole()] * kept.shape[0],
-        out_shape=[shape(*kept.shape[1:])] * kept.shape[0],
+        in_specs=[scalar()] * 2 + [whole()] * 2,
+        out_specs=whole(),
+        out_shape=shape(*kept.shape),
         compiler_params=params(),
         name="part",
-    )(kept, came)
+    )(place, bank, kept, came)
 
 
 def rotate(v, cosine, sine):
@@ -317,7 +315,9 @@
     for g in range(width // HEAD_DIM):
         columns = slice(g * HEAD_DIM, (g + 1) * HEAD_DIM)
         rows_ref[:, g, :] = rotate(own_ref[:, columns] + came_ref[:, columns], cosine, sine)
-    q_ref[0] = rows_ref[...].reshape(q_ref.shape[1:]).astype(BF16)
+    query = rows_ref[...].reshape(q_ref.shape[1:]).astype(BF16)
+    for i in range(q_ref.shape[0]):
+        q_ref[i] = query
     own, came = own_ref[:, width:], came_ref[:, width:]
     key = jnp.where(bank[0] == 0, own, came)
     value = jnp.where(bank[0] == 0, came, own)
@@ -325,7 +325,7 @@
     v_ref[...] = value.astype(BF16).astype(F32)
 
 
-def rotated(bank, own, came, cosine, sine):
+def rotated(bank, own, came, cosine, sine, copies):
     rows = own.shape[0]
     heads = own.shape[1] // HEAD_DIM - 1
     return pl.pallas_call(
@@ -333,7 +333,7 @@
         in_specs=[scalar()] + [whole()] * 4,
         out_specs=[whole()] * 3,
         out_shape=[
-            shape(1, rows * heads, HEAD_DIM, dtype=BF16),
+            shape(copies, rows * heads, HEAD_DIM, dtype=BF16),
             shape(rows, HEAD_DIM),
             shape(rows, HEAD_DIM),
         ],
@@ -341,23 +341,6 @@
         compiler_params=params(),
         name="rotate",
     )(bank, own, came, cosine, sine)
-
-
-def join_kernel(*refs):
-    *parts, out_ref = refs
-    for i, part in enumerate(parts):
-        out_ref[i] = part[0]
-
-
-def join(parts):
-    return pl.pallas_call(
-        join_kernel,
-        in_specs=[whole()] * len(parts),
-        out_specs=whole(),
-        out_shape=shape(len(parts), *parts[0].shape[1:], dtype=parts[0].dtype),
-        compiler_params=params(),
-        name="join",
-    )(*parts)
 
 
 def attend_kernel(slots, earlier, place, bank, length_ref, q_ref, k_ref, v_ref, *refs):
@@ -365,13 +348,14 @@
     beams, positions, _ = k_ref.shape
     rows = q_ref.shape[1]
     group = rows // beams
+    root = place[0] & (1 + bank[0])
     row, lane = iota((rows, HEAD_DIM), 0), iota((rows, HEAD_DIM), 1)
     left = length_ref[...] - place[0] * positions
     live = jnp.concatenate(
         [lane + first < left for first in range(0, positions, HEAD_DIM)], axis=1
     )
     for i, slot in enumerate(slots):
-        head = rank_of(place[0], bank[0], slot)
+        head = rank_of(root, bank[0], slot)
         columns = pl.ds(pl.multiple_of(head * HEAD_DIM, HEAD_DIM), HEAD_DIM)
         query = q_ref[i].astype(F32)
         scores = jnp.concatenate(
@@ -410,7 +394,7 @@
     if earlier:
         done = [(ref, i) for ref in before for i in range(ref.shape[0])]
         for slot, (ref, i) in zip(earlier, done):
-            out_ref[rank_of(place[0], bank[0], slot)] = ref[i]
+            out_ref[rank_of(root, bank[0], slot)] = ref[i]
 
 
 def attend(place, bank, length, queries, keys, values, slots, earlier=(), before=()):
@@ -529,6 +513,17 @@
 
 def traded(blocks):
     return lax.all_to_all(blocks, "tensor", 0, 0, tiled=True)
+
+
+def traded_near(blocks):
+    groups = []
+    for bank in range(2):
+        for root in (0, 1 + bank):
+            slots = range(0, lax.axis_size("tensor"), 2)
+            groups.append([2 * rank_of(root, bank, slot) + bank for slot in slots])
+    return lax.all_to_all(
+        blocks, ("tensor", "bank"), 0, 0, axis_index_groups=groups, tiled=True
+    )
 
 
 def hop(x, bit):
@@ -571,21 +566,22 @@
     kept, length = project_kept(
         place, bank, beam_cache_length, x, x_other, *weights, inner, ranks
     )
-    kept, *sent = part(kept, came)
-    near = tuple(range(2, ranks, 2))
-    parts = [kept] + [hop(block, slot) for block, slot in zip(sent, near)]
+    parts = traded_near(part(place, bank, kept, came))
     own, other = correct(bank, column, lowrank_up_factors, parts)
-    query, key_new, value_new = rotated(bank, own, swapped(other), cosine, sine)
+    query, key_new, value_new = rotated(
+        bank, own, swapped(other), cosine, sine, ranks // 2
+    )
 
     def attended_part(queries, slots, **more):
         cache = paged_key_cache, paged_value_cache
         return attend(place, bank, length, queries, *cache, slots, **more)
 
-    gathered = join([query] + [hop(query, slot) for slot in near])
+    gathered = traded_near(query)
     came = hop(gathered, 1)
-    done = attended_part(gathered, (0, *near))
-    odd = tuple(slot + 1 for slot in (0, *near))
-    partial = attended_part(came, odd, earlier=(0, *near), before=(done,))
+    even = tuple(range(0, ranks, 2))
+    done = attended_part(gathered, even)
+    odd = tuple(slot + 1 for slot in even)
+    partial = attended_part(came, odd, earlier=even, before=(done,))
     attended = combine(traded(partial), query, key_new, value_new)
     return residual(x, traded(output(attended, output_weight, ranks)))
 

time: 63.7 us -> 75.4 us (1.18)
  local copies, waits for them, and re-layouts: 0.04 us -> 12.1 us
  blocking collectives: 22.4 us -> 28.5 us
  starting transfers between devices: 14 us -> 10.4 us
  waiting for transfers between devices: 10.8 us -> 7.44 us
    unnamed x18 -> x16, local copies, waits for them, and re-layouts: 0.04 us -> 12.1 us
    ppermute x8 -> x2, waiting for transfers between devices: 9.69 us -> 0.08 us  [hop(): return lax.ppermute(x, ('tensor', 'bank'), pairs)]
    ppermute x8 -> x2, starting transfers between devices: 13.5 us -> 4.55 us  [hop(): return lax.ppermute(x, ('tensor', 'bank'), pairs)]
    all_to_all x0 -> x1, blocking collectives: none -> 8.75 us  [traded_near(): lax.all_to_all(blocks, ('tensor', 'bank'), 0, 0, axis_index_groups=groups...]
    all_to_all x0 -> x1, waiting for transfers between devices: none -> 6.25 us  [traded_near(): lax.all_to_all(blocks, ('tensor', 'bank'), 0, 0, axis_index_groups=groups...]
    all_to_all x0 -> x1, starting transfers between devices: none -> 5.37 us  [traded_near(): lax.all_to_all(blocks, ('tensor', 'bank'), 0, 0, axis_index_groups=groups...]
    all_to_all x2, blocking collectives: 22.4 us -> 19.7 us  [traded(): return lax.all_to_all(blocks, 'tensor', 0, 0, tiled=True)]
  transfers between devices with their start and end apart: 11 -> 6, of which waited for: 6 -> 3; matrix products, arithmetic and copies ran while one was open for 0% -> 0% of each run, Pallas kernels for 14% -> 11%
where the time goes in v11:
time: 75.4 us; the launch traced here: 75 us
  blocking collectives  28.5 us (38%)
  Pallas kernels  16.4 us (22%)
  local copies, waits for them, and re-layouts  12.1 us (16%)
  starting transfers between devices  10.4 us (14%)
  waiting for transfers between devices  7.44 us (10%)
    all_to_all x2, blocking collectives, traded(): return lax.all_to_all(blocks, 'tensor', 0, 0, tiled=True)  19.7 us
    unnamed x16, local copies, waits for them, and re-layouts  12.1 us
    all_to_all x1, blocking collectives, traded_near(): lax.all_to_all(blocks, ('tensor', 'bank'), 0, 0, axis_index_groups=groups...  8.75 us
    all_to_all x1, waiting for transfers between devices, traded_near(): lax.all_to_all(blocks, ('tensor', 'bank'), 0, 0, axis_index_groups=groups...  6.25 us
    all_to_all x1, starting transfers between devices, traded_near(): lax.all_to_all(blocks, ('tensor', 'bank'), 0, 0, axis_index_groups=groups...  5.37 us
    ppermute x2, starting transfers between devices, hop(): return lax.ppermute(x, ('tensor', 'bank'), pairs)  4.55 us
    pallas_call x1, Pallas kernels, project_kept(): pl.pallas_call(lambda *refs: project_kept_kernel(ranks, *refs), in_specs=...  3.56 us
    pallas_call x1, Pallas kernels, fetch(): pl.pallas_call(lambda *refs: fetch_kernel(ranks, *refs), in_specs=[scalar...  3.41 us
  transfers between devices with their start and end apart: 6, of which 3 were waited for; matrix products, arithmetic and copies ran while one was open for 0% of the time, Pallas kernels for 11%

profile of v11, /device:TPU:0, one launch (start us, length us, event | category | flops | bytes accessed | tf_op | source)
XLA Modules:
  0.0 75.0 jit_solution(16094156630725438734)
XLA Ops:
  0.0 0.5 collective-permute-start
  0.5 0.1 collective-permute-start.1
  0.5 0.0 copy-start.6
  0.5 3.4 %fetch.1 = (bf16[4,1024,512]{2,1,0:T(8,128)(2,1)S(1)}, bf16[4,1024,128]{2,1,0:T(8,128)(2,1)S(1)}, bf16[16,64,1024]{2,1,0:T(8,128)(2,1)S(1)}) custom-call(s32[1]{0:T(128)} %bitcast.refs_0_.place, s32[1]{0:T(128)} %bitcast.1.refs_1_.bank, bf16[1024,8192]{1,0:T(8,128)(2,1)} %refs_5_.3, bf16[1024,2048]{1,0:T(8,128)(2,1)} %refs_6_.1, bf16[16,64,1024]{2,1,0:T(8,128)(2,1)} %bitcast.3), custom_call_target="tpu_custom_call" | custom-call | bytes 7340032 | tf_op jit(solution)/shard_map/fetch/pallas_call | solution.py:119
  3.9 0.0 copy-start.7
  3.9 0.0 collective-permute-done.1.came_ref
  4.0 0.0 collective-permute-done.other_ref.refs_4_
  4.0 0.0 copy-done.6
  4.0 1.8 %project_sent.1 = (f32[4,16,768]{2,1,0:T(8,128)S(1)}, f32[16,128]{1,0:T(8,128)S(1)}, s32[16,128]{1,0:T(8,128)S(1)}) custom-call(s32[1]{0:T(128)} %bitcast.1.refs_1_.bank, s32[8]{0:T(128)} %own_ref.1, s32[8]{0:T(128)S(1)} %collective-permute-done.1.came_ref, bf16[8,1024]{1,0:T(8,128)(2,1)S(1)} %copy-done.6, ...), custom_call_target="tpu_custom_call" | custom-call | flops 117440512 | bytes 7340032 | tf_op jit(solution)/shard_map/project_sent/pallas_call | solution.py:183
  5.8 3.0 %collective-permute-start.2 = (f32[4,16,768]{2,1,0:T(8,128)S(1)}, f32[4,16,768]{2,1,0:T(8,128)S(1)}, u32[]{:S(2)}, u32[]{:S(2)}) collective-permute-start(f32[4,16,768]{2,1,0:T(8,128)S(1)} %get-tuple-element.25), channel_id=1, source_target_pairs={{0,2},{1,5},{2,0},{3,7},{4,6},{5,1},{6,4},{7,3},{8,10},{9,13},{10,... | collective-permute-start | bytes 589832 | tf_op jit(solution)/shard_map/ppermute | solution.py:534
  8.8 0.0 copy-done.7
  8.8 0.0 copy-start.5
  8.8 3.6 %project_kept.1 = (f32[4,16,768]{2,1,0:T(8,128)S(1)}, s32[64,128]{1,0:T(8,128)S(1)}) custom-call(s32[1]{0:T(128)} %bitcast.refs_0_.place, s32[1]{0:T(128)} %bitcast.1.refs_1_.bank, s32[8]{0:T(128)S(1)} %copy-done.7, bf16[8,1024]{1,0:T(8,128)(2,1)S(1)} %copy-done.6, bf16[8,1024]{1,0:T(8,128)(2,1)S(1)} %collective-permute-done.other_ref.refs_4_, ...), custom_call_target="tpu_custom_call" | custom-call | flops 83886080 | bytes 10485760 | tf_op jit(solution)/shard_map/project_kept/pallas_call | solution.py:228
  12.4 0.1 collective-permute-done.2.came_ref
  12.4 0.7 part.1
  13.1 5.4 %all-to-all-start = ((f32[4,16,768]{2,1,0:T(8,128)}), f32[4,16,768]{2,1,0:T(8,128)S(1)}, u32[]{:S(2)}, u32[]{:S(2)}) async-start(f32[4,16,768]{2,1,0:T(8,128)} %part.1), calls=%async_computation | async-start | bytes 393216 | tf_op jit(solution)/shard_map/all_to_all | solution.py:524
  18.5 6.3 %all-to-all-done.parts_ref = f32[4,16,768]{2,1,0:T(8,128)S(1)} async-done(((f32[4,16,768]{2,1,0:T(8,128)}), f32[4,16,768]{2,1,0:T(8,128)S(1)}, u32[]{:S(2)}, u32[]{:S(2)}) %all-to-all-start) | async-done | bytes 196640 | tf_op jit(solution)/shard_map/all_to_all | solution.py:524
  24.8 0.0 copy-done.5
  24.8 0.4 correct.1
  25.1 0.0 collective-permute-start.3
  25.1 0.1 fusion
  25.3 1.1 %collective-permute-done.3.came_ref = f32[8,1152]{1,0:T(8,128)S(1)} collective-permute-done((f32[8,1152]{1,0:T(8,128)S(1)}, f32[8,1152]{1,0:T(8,128)S(1)}, u32[]{:S(2)}, u32[]{:S(2)}) %collective-permute-start.3) | collective-permute-done | bytes 36896 | tf_op jit(solution)/shard_map/ppermute | solution.py:511
  26.4 0.1 rotate.1
  26.5 8.8 %all_to_all.20.refs_3_ = bf16[4,64,128]{2,1,0:T(8,128)(2,1)S(1)} all-to-all(bf16[4,64,128]{2,1,0:T(8,128)(2,1)S(1)} %get-tuple-element.28.q_ref), channel_id=1, replica_groups={{0,4,8,12},{2,6,10,14},{1,3,9,11},{5,7,13,15},{16,20,24,28},{18,22,26,3..., dimensions={0} | all-to-all | bytes 131072 | tf_op jit(solution)/shard_map/all_to_all | solution.py:524
  35.2 1.5 %collective-permute-start.4 = (bf16[4,64,128]{2,1,0:T(8,128)(2,1)S(1)}, bf16[4,64,128]{2,1,0:T(8,128)(2,1)S(1)}, u32[]{:S(2)}, u32[]{:S(2)}) collective-permute-start(bf16[4,64,128]{2,1,0:T(8,128)(2,1)S(1)} %all_to_all.20.refs_3_), channel_id=1, source_target_pairs={{0,2},{1,5},{2,0},{3,7},{4,6},{5,1},{6,4},{7,3},{8,10},{9,13},{10,... | collective-permute-start | bytes 196616 | tf_op jit(solution)/shard_map/ppermute | solution.py:534
  36.7 0.0 copy-start.1
  36.7 2.2 %copy-done.1 = bf16[8,256,1024]{2,1,0:T(8,128)(2,1)S(1)} copy-done((bf16[8,256,1024]{2,1,0:T(8,128)(2,1)S(1)}, bf16[8,256,1024]{2,1,0:T(8,128)(2,1)}, u32[]{:S(2)}) %copy-start.1) | copy-done | bytes 4194328
  38.9 0.0 copy-start.3
  38.9 2.2 %copy-done.3 = bf16[8,256,1024]{2,1,0:T(8,128)(2,1)S(1)} copy-done((bf16[8,256,1024]{2,1,0:T(8,128)(2,1)S(1)}, bf16[8,256,1024]{2,1,0:T(8,128)(2,1)}, u32[]{:S(2)}) %copy-start.3) | copy-done | bytes 4194328
  41.1 0.0 copy-start.2
  41.1 0.0 copy-start.4
  41.1 1.6 %attend.2.refs_6_ = bf16[4,80,128]{2,1,0:T(8,128)(2,1)S(1)} custom-call(s32[1]{0:T(128)} %bitcast.refs_0_.place, s32[1]{0:T(128)} %bitcast.1.refs_1_.bank, s32[64,128]{1,0:T(8,128)S(1)} %get-tuple-element.22.refs_2_, bf16[4,64,128]{2,1,0:T(8,128)(2,1)S(1)} %all_to_all.20.refs_3_, bf16[8,256,1024]{2,1,0:T(8,128)(2,1)S(1)} %copy-done.1, ...), custom_call_target="tpu_custom_call" | custom-call | flops 33554432 | bytes 4194304 | tf_op jit(solution)/shard_map/attend/pallas_call | solution.py:403
  42.7 0.0 collective-permute-done.4.refs_3_
  42.7 0.6 copy-done.2
  43.3 1.3 %copy-done.4 = bf16[8,256,1024]{2,1,0:T(8,128)(2,1)S(1)} copy-done((bf16[8,256,1024]{2,1,0:T(8,128)(2,1)S(1)}, bf16[8,256,1024]{2,1,0:T(8,128)(2,1)}, u32[]{:S(2)}) %copy-start.4) | copy-done | bytes 4194328
  44.6 1.6 %attend.3 = bf16[8,80,128]{2,1,0:T(8,128)(2,1)S(1)} custom-call(s32[1]{0:T(128)} %bitcast.refs_0_.place, s32[1]{0:T(128)} %bitcast.1.refs_1_.bank, s32[64,128]{1,0:T(8,128)S(1)} %get-tuple-element.22.refs_2_, bf16[4,64,128]{2,1,0:T(8,128)(2,1)S(1)} %collective-permute-done.4.refs_3_, bf16[8,256,1024]{2,1,0:T(8,128)(2,1)S(1)} %copy-done.2, ...), custom_call_target="tpu_custom_call" | custom-call | flops 33554432 | bytes 16777216 | tf_op jit(solution)/shard_map/attend/pallas_call | solution.py:403
  46.2 10.0 %all_to_all.21.parts_ref = bf16[8,80,128]{2,1,0:T(8,128)(2,1)S(1)} all-to-all(bf16[8,80,128]{2,1,0:T(8,128)(2,1)S(1)} %attend.3), channel_id=1, replica_groups=mesh['groups'=2,'tensor'=8,'bank'=2] {'tensor'}, dimensions={0} | all-to-all | bytes 327680 | tf_op jit(solution)/shard_map/all_to_all | solution.py:515
  56.1 0.5 combine.1.x_ref
  56.6 0.0 copy-start
  56.6 5.8 %copy-done = bf16[1024,8192]{1,0:T(8,128)(2,1)S(1)} copy-done((bf16[1024,8192]{1,0:T(8,128)(2,1)S(1)}, bf16[1024,8192]{1,0:T(8,128)(2,1)}, u32[]{:S(2)}) %copy-start) | copy-done | bytes 16777240
  62.4 2.3 %output.1 = bf16[8,8,1024]{2,1,0:T(8,128)(2,1)S(1)} custom-call(bf16[8,1024]{1,0:T(8,128)(2,1)S(1)} %combine.1.x_ref, bf16[1024,8192]{1,0:T(8,128)(2,1)S(1)} %copy-done), custom_call_target="tpu_custom_call" | custom-call | flops 134217728 | bytes 16777216 | tf_op jit(solution)/shard_map/output/pallas_call | solution.py:481
  64.7 9.7 %all_to_all.22.parts_ref = bf16[8,8,1024]{2,1,0:T(8,128)(2,1)S(1)} all-to-all(bf16[8,8,1024]{2,1,0:T(8,128)(2,1)S(1)} %output.1), channel_id=1, replica_groups=mesh['groups'=2,'tensor'=8,'bank'=2] {'tensor'}, dimensions={0} | all-to-all | bytes 262144 | tf_op jit(solution)/shard_map/all_to_all | solution.py:515
  74.4 0.6 residual.1
  (2 shorter events, 0.0 us)
Async XLA Ops:
  0.0 4.0 %collective-permute-start = (bf16[8,1024]{1,0:T(8,128)(2,1)}, bf16[8,1024]{1,0:T(8,128)(2,1)S(1)}, u32[]{:S(2)}, u32[]{:S(2)}) collective-permute-start(bf16[8,1024]{1,0:T(8,128)(2,1)} %x_ref.3), channel_id=1, source_target_pairs={{0,1},{1,0},{2,3},{3,2},{4,5},{5,4},{6,7},{7,6},{8,9},{9,8},{10,11... | collective-permute-start | bytes 49160 | tf_op jit(solution)/shard_map/ppermute | solution.py:511
  0.5 3.5 %collective-permute-start.1 = (s32[8]{0:T(128)}, s32[8]{0:T(128)S(1)}, u32[]{:S(2)}, u32[]{:S(2)}) collective-permute-start(s32[8]{0:T(128)} %own_ref.1), channel_id=1, source_target_pairs={{0,1},{1,0},{2,3},{3,2},{4,5},{5,4},{6,7},{7,6},{8,9},{9,8},{10,11... | collective-permute-start | bytes 104 | tf_op jit(solution)/shard_map/ppermute | solution.py:511
  0.5 3.5 %copy-start.6 = (bf16[8,1024]{1,0:T(8,128)(2,1)S(1)}, bf16[8,1024]{1,0:T(8,128)(2,1)}, u32[]{:S(2)}) copy-start(bf16[8,1024]{1,0:T(8,128)(2,1)} %x_ref.3) | copy-start | bytes 49156
  3.9 4.9 %copy-start.7 = (s32[8]{0:T(128)S(1)}, s32[8]{0:T(128)}, u32[]{:S(2)}) copy-start(s32[8]{0:T(128)} %refs_2_.3) | copy-start | bytes 100
  5.8 6.7 %collective-permute-start.2 = (f32[4,16,768]{2,1,0:T(8,128)S(1)}, f32[4,16,768]{2,1,0:T(8,128)S(1)}, u32[]{:S(2)}, u32[]{:S(2)}) collective-permute-start(f32[4,16,768]{2,1,0:T(8,128)S(1)} %get-tuple-element.25), channel_id=1, source_target_pairs={{0,2},{1,5},{2,0},{3,7},{4,6},{5,1},{6,4},{7,3},{8,10},{9,13},{10,... | collective-permute-start | bytes 589832 | tf_op jit(solution)/shard_map/ppermute | solution.py:534
  8.8 16.0 %copy-start.5 = (bf16[16,64,1024]{2,1,0:T(8,128)(2,1)S(1)}, bf16[16,64,1024]{2,1,0:T(8,128)(2,1)}, u32[]{:S(2)}) copy-start(bf16[16,64,1024]{2,1,0:T(8,128)(2,1)} %up_ref.1) | copy-start | bytes 6291460
  13.1 11.6 %all-to-all-start = ((f32[4,16,768]{2,1,0:T(8,128)}), f32[4,16,768]{2,1,0:T(8,128)S(1)}, u32[]{:S(2)}, u32[]{:S(2)}) async-start(f32[4,16,768]{2,1,0:T(8,128)} %part.1), calls=%async_computation | async-start | bytes 393216 | tf_op jit(solution)/shard_map/all_to_all | solution.py:524
  25.1 1.2 %collective-permute-start.3 = (f32[8,1152]{1,0:T(8,128)S(1)}, f32[8,1152]{1,0:T(8,128)S(1)}, u32[]{:S(2)}, u32[]{:S(2)}) collective-permute-start(f32[8,1152]{1,0:T(8,128)S(1)} %get-tuple-element.27), channel_id=1, source_target_pairs={{0,1},{1,0},{2,3},{3,2},{4,5},{5,4},{6,7},{7,6},{8,9},{9,8},{10,11... | collective-permute-start | bytes 110600 | tf_op jit(solution)/shard_map/ppermute | solution.py:511
  35.2 7.5 %collective-permute-start.4 = (bf16[4,64,128]{2,1,0:T(8,128)(2,1)S(1)}, bf16[4,64,128]{2,1,0:T(8,128)(2,1)S(1)}, u32[]{:S(2)}, u32[]{:S(2)}) collective-permute-start(bf16[4,64,128]{2,1,0:T(8,128)(2,1)S(1)} %all_to_all.20.refs_3_), channel_id=1, source_target_pairs={{0,2},{1,5},{2,0},{3,7},{4,6},{5,1},{6,4},{7,3},{8,10},{9,13},{10,... | collective-permute-start | bytes 196616 | tf_op jit(solution)/shard_map/ppermute | solution.py:534
  36.7 2.2 %copy-start.1 = (bf16[8,256,1024]{2,1,0:T(8,128)(2,1)S(1)}, bf16[8,256,1024]{2,1,0:T(8,128)(2,1)}, u32[]{:S(2)}) copy-start(bf16[8,256,1024]{2,1,0:T(8,128)(2,1)} %refs_4_.3) | copy-start | bytes 12582916
  38.9 2.2 %copy-start.3 = (bf16[8,256,1024]{2,1,0:T(8,128)(2,1)S(1)}, bf16[8,256,1024]{2,1,0:T(8,128)(2,1)}, u32[]{:S(2)}) copy-start(bf16[8,256,1024]{2,1,0:T(8,128)(2,1)} %refs_5_.5) | copy-start | bytes 12582916
  41.1 2.2 %copy-start.2 = (bf16[8,256,1024]{2,1,0:T(8,128)(2,1)S(1)}, bf16[8,256,1024]{2,1,0:T(8,128)(2,1)}, u32[]{:S(2)}) copy-start(bf16[8,256,1024]{2,1,0:T(8,128)(2,1)} %refs_4_.3) | copy-start | bytes 12582916
  41.1 3.5 %copy-start.4 = (bf16[8,256,1024]{2,1,0:T(8,128)(2,1)S(1)}, bf16[8,256,1024]{2,1,0:T(8,128)(2,1)}, u32[]{:S(2)}) copy-start(bf16[8,256,1024]{2,1,0:T(8,128)(2,1)} %refs_5_.5) | copy-start | bytes 12582916
  56.6 5.8 %copy-start = (bf16[1024,8192]{1,0:T(8,128)(2,1)S(1)}, bf16[1024,8192]{1,0:T(8,128)(2,1)}, u32[]{:S(2)}) copy-start(bf16[1024,8192]{1,0:T(8,128)(2,1)} %w_ref.1) | copy-start | bytes 50331652

commit v12 on v10

--- a/solution.py
+++ b/solution.py
@@ -572,8 +572,8 @@
         place, bank, beam_cache_length, x, x_other, *weights, inner, ranks
     )
     kept, *sent = part(kept, came)
-    near = tuple(range(2, ranks, 2))
-    parts = [kept] + [hop(block, slot) for block, slot in zip(sent, near)]
+    near = tuple(range(ranks - 2, 0, -2))
+    parts = [kept] + [hop(sent[slot // 2 - 1], slot) for slot in near]
     own, other = correct(bank, column, lowrank_up_factors, parts)
     query, key_new, value_new = rotated(bank, own, swapped(other), cosine, sine)
 

time: 63.7 us -> 60.9 us (0.956)
  blocking collectives: 22.4 us -> 20.8 us
  waiting for transfers between devices: 10.8 us -> 10.1 us
    all_to_all x2, blocking collectives: 22.4 us -> 20.8 us  [traded(): return lax.all_to_all(blocks, 'tensor', 0, 0, tiled=True)]
    ppermute x8, waiting for transfers between devices: 9.69 us -> 9.02 us  [hop(): return lax.ppermute(x, ('tensor', 'bank'), pairs)]
where the time goes in v12:
time: 60.9 us; the launch traced here: 60.7 us
  blocking collectives  20.8 us (34%)
  Pallas kernels  16 us (26%)
  starting transfers between devices  13.5 us (22%)
  waiting for transfers between devices  10.1 us (17%)
    all_to_all x2, blocking collectives, traded(): return lax.all_to_all(blocks, 'tensor', 0, 0, tiled=True)  20.8 us
    ppermute x8, starting transfers between devices, hop(): return lax.ppermute(x, ('tensor', 'bank'), pairs)  13 us
    ppermute x8, waiting for transfers between devices, hop(): return lax.ppermute(x, ('tensor', 'bank'), pairs)  9.02 us
    pallas_call x1, Pallas kernels, project_kept(): pl.pallas_call(lambda *refs: project_kept_kernel(ranks, *refs), in_specs=...  3.75 us
    pallas_call x1, Pallas kernels, fetch(): pl.pallas_call(lambda *refs: fetch_kernel(ranks, *refs), in_specs=[scalar...  3.41 us
    pallas_call x2, Pallas kernels, attend(): pl.pallas_call(lambda *refs: attend_kernel(slots, earlier, *refs), in_spe...  3.12 us
    pallas_call x1, Pallas kernels, output(): pl.pallas_call(output_kernel, in_specs=[whole()] * 2, out_specs=whole(),...  2.28 us
    pallas_call x1, Pallas kernels, project_sent(): pl.pallas_call(project_sent_kernel, in_specs=[scalar(), big(), pl.BlockSp...  1.77 us
  transfers between devices with their start and end apart: 11, of which 6 were waited for; matrix products, arithmetic and copies ran while one was open for 0% of the time, Pallas kernels for 14%

profile of v12, /device:TPU:0, one launch (start us, length us, event | category | flops | bytes accessed | tf_op | source)
XLA Modules:
  0.0 60.7 jit_solution(3461571404991115690)
XLA Ops:
  0.0 0.5 collective-permute-start
  0.5 0.1 collective-permute-start.1
  0.5 0.0 copy-start.3
  0.5 3.4 %fetch.1 = (bf16[4,1024,512]{2,1,0:T(8,128)(2,1)S(1)}, bf16[4,1024,128]{2,1,0:T(8,128)(2,1)S(1)}, bf16[16,64,1024]{2,1,0:T(8,128)(2,1)S(1)}) custom-call(s32[1]{0:T(128)} %bitcast.refs_0_, s32[1]{0:T(128)} %bitcast.1.refs_1_.bank, bf16[1024,8192]{1,0:T(8,128)(2,1)} %refs_5_.3, bf16[1024,2048]{1,0:T(8,128)(2,1)} %refs_6_.1, bf16[16,64,1024]{2,1,0:T(8,128)(2,1)} %bitcast.5), custom_call_target="tpu_custom_call" | custom-call | bytes 7340032 | tf_op jit(solution)/shard_map/fetch/pallas_call | solution.py:119
  3.9 0.0 copy-start.4
  3.9 0.0 collective-permute-done.1.came_ref
  4.0 0.0 collective-permute-done.other_ref.refs_4_
  4.0 0.0 copy-done.3
  4.0 0.0 copy-start.2
  4.0 1.8 %project_sent.1 = (f32[4,16,768]{2,1,0:T(8,128)S(1)}, f32[16,128]{1,0:T(8,128)S(1)}, s32[16,128]{1,0:T(8,128)S(1)}) custom-call(s32[1]{0:T(128)} %bitcast.1.refs_1_.bank, s32[8]{0:T(128)} %own_ref.1, s32[8]{0:T(128)S(1)} %collective-permute-done.1.came_ref, bf16[8,1024]{1,0:T(8,128)(2,1)S(1)} %copy-done.3, ...), custom_call_target="tpu_custom_call" | custom-call | flops 117440512 | bytes 7340032 | tf_op jit(solution)/shard_map/project_sent/pallas_call | solution.py:183
  5.8 3.0 %collective-permute-start.2 = (f32[4,16,768]{2,1,0:T(8,128)S(1)}, f32[4,16,768]{2,1,0:T(8,128)S(1)}, u32[]{:S(2)}, u32[]{:S(2)}) collective-permute-start(f32[4,16,768]{2,1,0:T(8,128)S(1)} %get-tuple-element.29), channel_id=1, source_target_pairs={{0,2},{1,5},{2,0},{3,7},{4,6},{5,1},{6,4},{7,3},{8,10},{9,13},{10,... | collective-permute-start | bytes 589832 | tf_op jit(solution)/shard_map/ppermute | solution.py:539
  8.8 0.0 copy-done.4
  8.8 0.0 copy-start
  8.8 0.0 copy-start.1
  8.8 0.0 slice-start
  8.8 0.0 slice-start.1
  8.8 0.0 slice-start.2
  8.8 3.8 %project_kept.1 = (f32[4,16,768]{2,1,0:T(8,128)S(1)}, s32[64,128]{1,0:T(8,128)S(1)}) custom-call(s32[1]{0:T(128)} %bitcast.refs_0_, s32[1]{0:T(128)} %bitcast.1.refs_1_.bank, s32[8]{0:T(128)S(1)} %copy-done.4, bf16[8,1024]{1,0:T(8,128)(2,1)S(1)} %copy-done.3, bf16[8,1024]{1,0:T(8,128)(2,1)S(1)} %collective-permute-done.other_ref.refs_4_, ...), custom_call_target="tpu_custom_call" | custom-call | flops 83886080 | bytes 10485760 | tf_op jit(solution)/shard_map/project_kept/pallas_call | solution.py:228
  12.6 0.0 collective-permute-done.2.came_ref
  12.6 4.0 %collective-permute-start.3 = (f32[16,768]{1,0:T(8,128)S(1)}, f32[16,768]{1,0:T(8,128)S(1)}, u32[]{:S(2)}, u32[]{:S(2)}) collective-permute-start(f32[16,768]{1,0:T(8,128)S(1)} %get-tuple-element.31), channel_id=1, source_target_pairs={{0,12},{1,11},{2,14},{3,9},{4,8},{5,15},{6,10},{7,13},{8,4},{9,3},... | collective-permute-start | bytes 147464 | tf_op jit(solution)/shard_map/ppermute | solution.py:539
  16.6 0.0 collective-permute-start.4
  16.7 0.6 %collective-permute-start.5 = (f32[16,768]{1,0:T(8,128)S(1)}, f32[16,768]{1,0:T(8,128)S(1)}, u32[]{:S(2)}, u32[]{:S(2)}) collective-permute-start(f32[16,768]{1,0:T(8,128)S(1)} %get-tuple-element.33), channel_id=1, source_target_pairs={{0,4},{1,3},{2,6},{3,1},{4,0},{5,7},{6,2},{7,5},{8,12},{9,11},{10,... | collective-permute-start | bytes 147464 | tf_op jit(solution)/shard_map/ppermute | solution.py:539
  17.3 1.5 %collective-permute-done.3.refs_1_ = f32[16,768]{1,0:T(8,128)S(1)} collective-permute-done((f32[16,768]{1,0:T(8,128)S(1)}, f32[16,768]{1,0:T(8,128)S(1)}, u32[]{:S(2)}, u32[]{:S(2)}) %collective-permute-start.3) | collective-permute-done | bytes 49184 | tf_op jit(solution)/shard_map/ppermute | solution.py:539
  18.8 2.8 %collective-permute-done.4.refs_2_ = f32[16,768]{1,0:T(8,128)S(1)} collective-permute-done((f32[16,768]{1,0:T(8,128)S(1)}, f32[16,768]{1,0:T(8,128)S(1)}, u32[]{:S(2)}, u32[]{:S(2)}) %collective-permute-start.4) | collective-permute-done | bytes 49184 | tf_op jit(solution)/shard_map/ppermute | solution.py:539
  21.6 0.0 collective-permute-done.5.refs_3_
  21.6 0.0 copy-done.2
  21.6 0.4 correct.1
  22.0 0.0 collective-permute-start.6
  22.0 0.1 fusion
  22.2 1.1 %collective-permute-done.6.came_ref = f32[8,1152]{1,0:T(8,128)S(1)} collective-permute-done((f32[8,1152]{1,0:T(8,128)S(1)}, f32[8,1152]{1,0:T(8,128)S(1)}, u32[]{:S(2)}, u32[]{:S(2)}) %collective-permute-start.6) | collective-permute-done | bytes 36896 | tf_op jit(solution)/shard_map/ppermute | solution.py:527
  23.3 0.1 rotate.1
  23.4 2.6 %collective-permute-start.7 = (bf16[1,64,128]{2,1,0:T(8,128)(2,1)S(1)}, bf16[1,64,128]{2,1,0:T(8,128)(2,1)S(1)}, u32[]{:S(2)}, u32[]{:S(2)}) collective-permute-start(bf16[1,64,128]{2,1,0:T(8,128)(2,1)S(1)} %get-tuple-element.36.refs_0_.q_ref), channel_id=1, source_target_pairs={{0,12},{1,11},{2,14},{3,9},{4,8},{5,15},{6,10},{7,13},{8,4},{9,3},... | collective-permute-start | bytes 49160 | tf_op jit(solution)/shard_map/ppermute | solution.py:539
  26.0 0.0 collective-permute-start.8
  26.0 1.8 %collective-permute-start.9 = (bf16[1,64,128]{2,1,0:T(8,128)(2,1)S(1)}, bf16[1,64,128]{2,1,0:T(8,128)(2,1)S(1)}, u32[]{:S(2)}, u32[]{:S(2)}) collective-permute-start(bf16[1,64,128]{2,1,0:T(8,128)(2,1)S(1)} %get-tuple-element.36.refs_0_.q_ref), channel_id=1, source_target_pairs={{0,4},{1,3},{2,6},{3,1},{4,0},{5,7},{6,2},{7,5},{8,12},{9,11},{10,... | collective-permute-start | bytes 49160 | tf_op jit(solution)/shard_map/ppermute | solution.py:539
  27.8 1.1 %collective-permute-done.7.refs_1_ = bf16[1,64,128]{2,1,0:T(8,128)(2,1)S(1)} collective-permute-done((bf16[1,64,128]{2,1,0:T(8,128)(2,1)S(1)}, bf16[1,64,128]{2,1,0:T(8,128)(2,1)S(1)}, u32[]{:S(2)}, u32[]{:S(2)}) %collective-permute-start.7) | collective-permute-done | bytes 16416 | tf_op jit(solution)/shard_map/ppermute | solution.py:539
  29.0 1.6 %collective-permute-done.8.refs_2_ = bf16[1,64,128]{2,1,0:T(8,128)(2,1)S(1)} collective-permute-done((bf16[1,64,128]{2,1,0:T(8,128)(2,1)S(1)}, bf16[1,64,128]{2,1,0:T(8,128)(2,1)S(1)}, u32[]{:S(2)}, u32[]{:S(2)}) %collective-permute-start.8) | collective-permute-done | bytes 16416 | tf_op jit(solution)/shard_map/ppermute | solution.py:539
  30.6 0.0 collective-permute-done.9.refs_3_
  30.6 0.9 %collective-permute-start.10 = (bf16[4,64,128]{2,1,0:T(8,128)(2,1)S(1)}, bf16[4,64,128]{2,1,0:T(8,128)(2,1)S(1)}, u32[]{:S(2)}, u32[]{:S(2)}) collective-permute-start(bf16[4,64,128]{2,1,0:T(8,128)(2,1)S(1)} %join.1.refs_3_), channel_id=1, source_target_pairs={{0,2},{1,5},{2,0},{3,7},{4,6},{5,1},{6,4},{7,3},{8,10},{9,13},{10,... | collective-permute-start | bytes 196616 | tf_op jit(solution)/shard_map/ppermute | solution.py:539
  31.5 0.0 copy-done
  31.5 0.0 copy-done.1
  31.5 0.0 slice-start.3
  31.5 1.6 %attend.2.refs_6_ = bf16[4,80,128]{2,1,0:T(8,128)(2,1)S(1)} custom-call(s32[1]{0:T(128)} %bitcast.refs_0_, s32[1]{0:T(128)} %bitcast.1.refs_1_.bank, s32[64,128]{1,0:T(8,128)S(1)} %get-tuple-element.26.refs_2_, bf16[4,64,128]{2,1,0:T(8,128)(2,1)S(1)} %join.1.refs_3_, bf16[8,256,1024]{2,1,0:T(8,128)(2,1)S(1)} %copy-done, bf16[8,256,1024]{2,1,0:T(8,128)(2,1)S(1)} %copy-done.1), custom_call_target="tpu_custom_call" | custom-call | flops 33554432 | bytes 4194304 | tf_op jit(solution)/shard_map/attend/pallas_call | solution.py:419
  33.0 1.9 %collective-permute-done.10.refs_3_ = bf16[4,64,128]{2,1,0:T(8,128)(2,1)S(1)} collective-permute-done((bf16[4,64,128]{2,1,0:T(8,128)(2,1)S(1)}, bf16[4,64,128]{2,1,0:T(8,128)(2,1)S(1)}, u32[]{:S(2)}, u32[]{:S(2)}) %collective-permute-start.10) | collective-permute-done | bytes 65568 | tf_op jit(solution)/shard_map/ppermute | solution.py:539
  34.9 1.6 %attend.3 = bf16[8,80,128]{2,1,0:T(8,128)(2,1)S(1)} custom-call(s32[1]{0:T(128)} %bitcast.refs_0_, s32[1]{0:T(128)} %bitcast.1.refs_1_.bank, s32[64,128]{1,0:T(8,128)S(1)} %get-tuple-element.26.refs_2_, bf16[4,64,128]{2,1,0:T(8,128)(2,1)S(1)} %collective-permute-done.10.refs_3_, bf16[8,256,1024]{2,1,0:T(8,128)(2,1)S(1)} %copy-done, ...), custom_call_target="tpu_custom_call" | custom-call | flops 33554432 | bytes 16777216 | tf_op jit(solution)/shard_map/attend/pallas_call | solution.py:419
  36.5 11.0 %all_to_all.10.parts_ref = bf16[8,80,128]{2,1,0:T(8,128)(2,1)S(1)} all-to-all(bf16[8,80,128]{2,1,0:T(8,128)(2,1)S(1)} %attend.3), channel_id=1, replica_groups=mesh['groups'=2,'tensor'=8,'bank'=2] {'tensor'}, dimensions={0} | all-to-all | bytes 327680 | tf_op jit(solution)/shard_map/all_to_all | solution.py:531
  47.5 0.5 combine.1.x_ref
  48.0 0.0 slice-done
  48.0 0.0 slice-done.1
  48.0 0.0 slice-done.2
  48.0 0.0 slice-done.3
  48.1 2.3 %output.1 = bf16[8,8,1024]{2,1,0:T(8,128)(2,1)S(1)} custom-call(bf16[8,1024]{1,0:T(8,128)(2,1)S(1)} %combine.1.x_ref, bf16[1024,8192]{1,0:T(8,128)(2,1)S(1)} %bitcast.4), custom_call_target="tpu_custom_call" | custom-call | flops 134217728 | bytes 16777216 | tf_op jit(solution)/shard_map/output/pallas_call | solution.py:497
  50.4 9.7 %all_to_all.11.parts_ref = bf16[8,8,1024]{2,1,0:T(8,128)(2,1)S(1)} all-to-all(bf16[8,8,1024]{2,1,0:T(8,128)(2,1)S(1)} %output.1), channel_id=1, replica_groups=mesh['groups'=2,'tensor'=8,'bank'=2] {'tensor'}, dimensions={0} | all-to-all | bytes 262144 | tf_op jit(solution)/shard_map/all_to_all | solution.py:531
  60.1 0.6 %residual.1 = bf16[8,1024]{1,0:T(8,128)(2,1)} custom-call(bf16[8,1024]{1,0:T(8,128)(2,1)S(1)} %copy-done.3, bf16[8,8,1024]{2,1,0:T(8,128)(2,1)S(1)} %all_to_all.11.parts_ref), custom_call_target="tpu_custom_call" | custom-call | tf_op jit(solution)/shard_map/residual/pallas_call | solution.py:516
  (5 shorter events, 0.0 us)
Async XLA Ops:
  0.0 4.0 %collective-permute-start = (bf16[8,1024]{1,0:T(8,128)(2,1)}, bf16[8,1024]{1,0:T(8,128)(2,1)S(1)}, u32[]{:S(2)}, u32[]{:S(2)}) collective-permute-start(bf16[8,1024]{1,0:T(8,128)(2,1)} %x_ref.3), channel_id=1, source_target_pairs={{0,1},{1,0},{2,3},{3,2},{4,5},{5,4},{6,7},{7,6},{8,9},{9,8},{10,11... | collective-permute-start | bytes 49160 | tf_op jit(solution)/shard_map/ppermute | solution.py:527
  0.5 3.5 %collective-permute-start.1 = (s32[8]{0:T(128)}, s32[8]{0:T(128)S(1)}, u32[]{:S(2)}, u32[]{:S(2)}) collective-permute-start(s32[8]{0:T(128)} %own_ref.1), channel_id=1, source_target_pairs={{0,1},{1,0},{2,3},{3,2},{4,5},{5,4},{6,7},{7,6},{8,9},{9,8},{10,11... | collective-permute-start | bytes 104 | tf_op jit(solution)/shard_map/ppermute | solution.py:527
  0.5 3.5 %copy-start.3 = (bf16[8,1024]{1,0:T(8,128)(2,1)S(1)}, bf16[8,1024]{1,0:T(8,128)(2,1)}, u32[]{:S(2)}) copy-start(bf16[8,1024]{1,0:T(8,128)(2,1)} %x_ref.3) | copy-start | bytes 49156
  3.9 4.9 %copy-start.4 = (s32[8]{0:T(128)S(1)}, s32[8]{0:T(128)}, u32[]{:S(2)}) copy-start(s32[8]{0:T(128)} %refs_2_.3) | copy-start | bytes 100
  4.0 17.7 %copy-start.2 = (bf16[16,64,1024]{2,1,0:T(8,128)(2,1)S(1)}, bf16[16,64,1024]{2,1,0:T(8,128)(2,1)}, u32[]{:S(2)}) copy-start(bf16[16,64,1024]{2,1,0:T(8,128)(2,1)} %up_ref.1) | copy-start | bytes 6291460
  5.8 6.8 %collective-permute-start.2 = (f32[4,16,768]{2,1,0:T(8,128)S(1)}, f32[4,16,768]{2,1,0:T(8,128)S(1)}, u32[]{:S(2)}, u32[]{:S(2)}) collective-permute-start(f32[4,16,768]{2,1,0:T(8,128)S(1)} %get-tuple-element.29), channel_id=1, source_target_pairs={{0,2},{1,5},{2,0},{3,7},{4,6},{5,1},{6,4},{7,3},{8,10},{9,13},{10,... | collective-permute-start | bytes 589832 | tf_op jit(solution)/shard_map/ppermute | solution.py:539
  8.8 22.7 %copy-start = (bf16[8,256,1024]{2,1,0:T(8,128)(2,1)S(1)}, bf16[8,256,1024]{2,1,0:T(8,128)(2,1)}, u32[]{:S(2)}) copy-start(bf16[8,256,1024]{2,1,0:T(8,128)(2,1)} %refs_4_.3) | copy-start | bytes 12582916
  8.8 22.7 %copy-start.1 = (bf16[8,256,1024]{2,1,0:T(8,128)(2,1)S(1)}, bf16[8,256,1024]{2,1,0:T(8,128)(2,1)}, u32[]{:S(2)}) copy-start(bf16[8,256,1024]{2,1,0:T(8,128)(2,1)} %refs_5_.5) | copy-start | bytes 12582916
  8.8 39.2 %slice-start = ((s8[16777216]{0:T(1024)(128)(4,1)}), s8[4194304]{0:T(1024)(128)(4,1)S(1)}, s32[]{:S(2)}) async-start(s8[16777216]{0:T(1024)(128)(4,1)} %bitcast.3), calls=%async_computation.2 | async-start | bytes 8388608
  8.8 39.2 %slice-start.1 = ((s8[16777216]{0:T(1024)(128)(4,1)}), s8[4194304]{0:T(1024)(128)(4,1)S(1)}, s32[]{:S(2)}) async-start(s8[16777216]{0:T(1024)(128)(4,1)} %bitcast.3), calls=%async_computation.3 | async-start | bytes 8388608
  8.8 39.2 %slice-start.2 = ((s8[16777216]{0:T(1024)(128)(4,1)}), s8[4194304]{0:T(1024)(128)(4,1)S(1)}, s32[]{:S(2)}) async-start(s8[16777216]{0:T(1024)(128)(4,1)} %bitcast.3), calls=%async_computation.4 | async-start | bytes 8388608
  12.6 6.2 %collective-permute-start.3 = (f32[16,768]{1,0:T(8,128)S(1)}, f32[16,768]{1,0:T(8,128)S(1)}, u32[]{:S(2)}, u32[]{:S(2)}) collective-permute-start(f32[16,768]{1,0:T(8,128)S(1)} %get-tuple-element.31), channel_id=1, source_target_pairs={{0,12},{1,11},{2,14},{3,9},{4,8},{5,15},{6,10},{7,13},{8,4},{9,3},... | collective-permute-start | bytes 147464 | tf_op jit(solution)/shard_map/ppermute | solution.py:539
  16.6 5.0 %collective-permute-start.4 = (f32[16,768]{1,0:T(8,128)S(1)}, f32[16,768]{1,0:T(8,128)S(1)}, u32[]{:S(2)}, u32[]{:S(2)}) collective-permute-start(f32[16,768]{1,0:T(8,128)S(1)} %get-tuple-element.32), channel_id=1, source_target_pairs={{0,8},{1,9},{2,10},{3,11},{4,12},{5,13},{6,14},{7,15},{8,0},{9,1},... | collective-permute-start | bytes 147464 | tf_op jit(solution)/shard_map/ppermute | solution.py:539
  16.7 5.0 %collective-permute-start.5 = (f32[16,768]{1,0:T(8,128)S(1)}, f32[16,768]{1,0:T(8,128)S(1)}, u32[]{:S(2)}, u32[]{:S(2)}) collective-permute-start(f32[16,768]{1,0:T(8,128)S(1)} %get-tuple-element.33), channel_id=1, source_target_pairs={{0,4},{1,3},{2,6},{3,1},{4,0},{5,7},{6,2},{7,5},{8,12},{9,11},{10,... | collective-permute-start | bytes 147464 | tf_op jit(solution)/shard_map/ppermute | solution.py:539
  22.0 1.2 %collective-permute-start.6 = (f32[8,1152]{1,0:T(8,128)S(1)}, f32[8,1152]{1,0:T(8,128)S(1)}, u32[]{:S(2)}, u32[]{:S(2)}) collective-permute-start(f32[8,1152]{1,0:T(8,128)S(1)} %get-tuple-element.35), channel_id=1, source_target_pairs={{0,1},{1,0},{2,3},{3,2},{4,5},{5,4},{6,7},{7,6},{8,9},{9,8},{10,11... | collective-permute-start | bytes 110600 | tf_op jit(solution)/shard_map/ppermute | solution.py:527
  23.4 5.6 %collective-permute-start.7 = (bf16[1,64,128]{2,1,0:T(8,128)(2,1)S(1)}, bf16[1,64,128]{2,1,0:T(8,128)(2,1)S(1)}, u32[]{:S(2)}, u32[]{:S(2)}) collective-permute-start(bf16[1,64,128]{2,1,0:T(8,128)(2,1)S(1)} %get-tuple-element.36.refs_0_.q_ref), channel_id=1, source_target_pairs={{0,12},{1,11},{2,14},{3,9},{4,8},{5,15},{6,10},{7,13},{8,4},{9,3},... | collective-permute-start | bytes 49160 | tf_op jit(solution)/shard_map/ppermute | solution.py:539
  26.0 4.6 %collective-permute-start.8 = (bf16[1,64,128]{2,1,0:T(8,128)(2,1)S(1)}, bf16[1,64,128]{2,1,0:T(8,128)(2,1)S(1)}, u32[]{:S(2)}, u32[]{:S(2)}) collective-permute-start(bf16[1,64,128]{2,1,0:T(8,128)(2,1)S(1)} %get-tuple-element.36.refs_0_.q_ref), channel_id=1, source_target_pairs={{0,8},{1,9},{2,10},{3,11},{4,12},{5,13},{6,14},{7,15},{8,0},{9,1},... | collective-permute-start | bytes 49160 | tf_op jit(solution)/shard_map/ppermute | solution.py:539
  26.0 4.6 %collective-permute-start.9 = (bf16[1,64,128]{2,1,0:T(8,128)(2,1)S(1)}, bf16[1,64,128]{2,1,0:T(8,128)(2,1)S(1)}, u32[]{:S(2)}, u32[]{:S(2)}) collective-permute-start(bf16[1,64,128]{2,1,0:T(8,128)(2,1)S(1)} %get-tuple-element.36.refs_0_.q_ref), channel_id=1, source_target_pairs={{0,4},{1,3},{2,6},{3,1},{4,0},{5,7},{6,2},{7,5},{8,12},{9,11},{10,... | collective-permute-start | bytes 49160 | tf_op jit(solution)/shard_map/ppermute | solution.py:539
  30.6 4.3 %collective-permute-start.10 = (bf16[4,64,128]{2,1,0:T(8,128)(2,1)S(1)}, bf16[4,64,128]{2,1,0:T(8,128)(2,1)S(1)}, u32[]{:S(2)}, u32[]{:S(2)}) collective-permute-start(bf16[4,64,128]{2,1,0:T(8,128)(2,1)S(1)} %join.1.refs_3_), channel_id=1, source_target_pairs={{0,2},{1,5},{2,0},{3,7},{4,6},{5,1},{6,4},{7,3},{8,10},{9,13},{10,... | collective-permute-start | bytes 196616 | tf_op jit(solution)/shard_map/ppermute | solution.py:539
  31.5 16.6 %slice-start.3 = ((s8[16777216]{0:T(1024)(128)(4,1)}), s8[4194304]{0:T(1024)(128)(4,1)S(1)}, s32[]{:S(2)}) async-start(s8[16777216]{0:T(1024)(128)(4,1)} %bitcast.3), calls=%async_computation.5 | async-start | bytes 8388608

commit v13 on v12

--- a/solution.py
+++ b/solution.py
@@ -83,7 +83,10 @@
         copies.append(
             start_columns(w_ref, (2 * target + bank[0]) * width, w_buf.at[s], sems.at[s])
             + start_columns(
-                kv_ref, (target + ranks * bank[0]) * HEAD_DIM, kv_buf.at[s], kv_sems.at[s]
+                kv_ref,
+                (target + ranks * bank[0]) * HEAD_DIM,
+                kv_buf.at[:, pl.ds(s * HEAD_DIM, HEAD_DIM)],
+                kv_sems.at[s],
             )
         )
     return copies
@@ -106,7 +109,7 @@
     count, depth = ranks // 2, wq.shape[0]
     return [
         shape(count, depth, wq.shape[1] // ranks // 2, dtype=BF16),
-        shape(count, depth, HEAD_DIM, dtype=BF16),
+        shape(depth, count * HEAD_DIM, dtype=BF16),
     ]
 
 
@@ -135,10 +138,11 @@
     return jnp.concatenate(rows, axis=0).astype(BF16)
 
 
-def project_slot(x, w, kv, out):
-    width = w.shape[1]
-    out[:, :width] = jnp.dot(x, w[...], preferred_element_type=F32)
-    out[:, width : width + HEAD_DIM] = jnp.dot(x, kv[...], preferred_element_type=F32)
+def project_keyval(x, kv_buf, out, width):
+    keyval = jnp.dot(x, kv_buf[...], preferred_element_type=F32)
+    for s in range(out.shape[0]):
+        part = keyval[:, s * HEAD_DIM : (s + 1) * HEAD_DIM]
+        out[s, :, width : width + HEAD_DIM] = part
 
 
 def project_sent_kernel(
@@ -154,7 +158,8 @@
     width = w_buf.shape[2]
     x = beam_rows(x_ref, other_ref)
     for s in range(out.shape[0]):
-        project_slot(x, w_buf.at[s], kv_buf.at[s], out.at[s])
+        out[s, :, :width] = jnp.dot(x, w_buf[s], preferred_element_type=F32)
+    project_keyval(x, kv_buf, out, width)
     adapters, rank, depth = down_buf.shape
     every = lax.dot_general(
         x,
@@ -216,8 +221,9 @@
     x = beam_rows(x_ref, other_ref)
     for s, slot in enumerate(copies):
         wait_all([slot])
-        project_slot(x, w_buf.at[s], kv_buf.at[s], out.at[s])
+        out[s, :, :width] = jnp.dot(x, w_buf[s], preferred_element_type=F32)
         out[s, :, width + HEAD_DIM :] = inner[...]
+    project_keyval(x, kv_buf, out, width)
 
 
 def project_kept(place, bank, length, x, other, wq, wkv, inner, ranks):
@@ -581,11 +587,17 @@
         cache = paged_key_cache, paged_value_cache
         return attend(place, bank, length, queries, *cache, slots, **more)
 
-    gathered = join([query] + [hop(query, slot) for slot in near])
-    came = hop(gathered, 1)
-    done = attended_part(gathered, (0, *near))
-    odd = tuple(slot + 1 for slot in (0, *near))
-    partial = attended_part(came, odd, earlier=(0, *near), before=(done,))
+    came, done = lax.optimization_barrier((hop(query, 1), attended_part(query, (0,))))
+    pair = join([query, came])
+    pairs = [hop(pair, slot) for slot in near]
+    done = [done, attended_part(came, (1,))]
+    order, slots = [0, 2, 1], [0, 1]
+    for i in order[:-1]:
+        done.append(attended_part(pairs[i], (near[i], near[i] + 1)))
+        slots += [near[i], near[i] + 1]
+    i = order[-1]
+    last = near[i], near[i] + 1
+    partial = attended_part(pairs[i], last, earlier=tuple(slots), before=tuple(done))
     attended = combine(traded(partial), query, key_new, value_new)
     return residual(x, traded(output(attended, output_weight, ranks)))
 

time: 60.9 us -> 61.2 us (level)
    pallas_call x2 -> x5, Pallas kernels: 3.12 us -> 3.6 us  [attend(): pl.pallas_call(lambda *refs: attend_kernel(slots, earlier, *refs), in_spe...]
  transfers between devices with their start and end apart: 11 -> 11, of which waited for: 6 -> 7; matrix products, arithmetic and copies ran while one was open for 0% -> 0% of each run, Pallas kernels for 14% -> 16%
where the time goes in v13:
time: 61.2 us; the launch traced here: 61 us
  blocking collectives  21.2 us (35%)
  Pallas kernels  16.5 us (27%)
  starting transfers between devices  13.2 us (22%)
  waiting for transfers between devices  9.73 us (16%)
    all_to_all x2, blocking collectives, traded(): return lax.all_to_all(blocks, 'tensor', 0, 0, tiled=True)  21.2 us
    ppermute x8, starting transfers between devices, hop(): return lax.ppermute(x, ('tensor', 'bank'), pairs)  12.7 us
    ppermute x8, waiting for transfers between devices, hop(): return lax.ppermute(x, ('tensor', 'bank'), pairs)  8.62 us
    pallas_call x1, Pallas kernels, project_kept(): pl.pallas_call(lambda *refs: project_kept_kernel(ranks, *refs), in_specs=...  3.83 us
    pallas_call x5, Pallas kernels, attend(): pl.pallas_call(lambda *refs: attend_kernel(slots, earlier, *refs), in_spe...  3.6 us
    pallas_call x1, Pallas kernels, fetch(): pl.pallas_call(lambda *refs: fetch_kernel(ranks, *refs), in_specs=[scalar...  3.41 us
    pallas_call x1, Pallas kernels, output(): pl.pallas_call(output_kernel, in_specs=[whole()] * 2, out_specs=whole(),...  2.28 us
    pallas_call x1, Pallas kernels, project_sent(): pl.pallas_call(project_sent_kernel, in_specs=[scalar(), big(), pl.BlockSp...  1.77 us
  transfers between devices with their start and end apart: 11, of which 7 were waited for; matrix products, arithmetic and copies ran while one was open for 0% of the time, Pallas kernels for 16%

profile of v13, /device:TPU:0, one launch (start us, length us, event | category | flops | bytes accessed | tf_op | source)
XLA Modules:
  0.0 61.0 jit_solution(14005775441227787646)
XLA Ops:
  0.0 0.5 collective-permute-start
  0.5 0.1 collective-permute-start.1
  0.5 0.0 copy-start.3
  0.5 3.4 %fetch.1 = (bf16[4,1024,512]{2,1,0:T(8,128)(2,1)S(1)}, bf16[1024,512]{1,0:T(8,128)(2,1)S(1)}, bf16[16,64,1024]{2,1,0:T(8,128)(2,1)S(1)}) custom-call(s32[1]{0:T(128)} %bitcast.refs_0_, s32[1]{0:T(128)} %bitcast.1.refs_1_.bank, bf16[1024,8192]{1,0:T(8,128)(2,1)} %refs_5_.6, bf16[1024,2048]{1,0:T(8,128)(2,1)} %refs_6_.1, bf16[16,64,1024]{2,1,0:T(8,128)(2,1)} %bitcast.5), custom_call_target="tpu_custom_call" | custom-call | bytes 7340032 | tf_op jit(solution)/shard_map/fetch/pallas_call | solution.py:122
  3.9 0.0 copy-start.4
  3.9 0.0 collective-permute-done.1.came_ref
  4.0 0.0 collective-permute-done.other_ref.refs_4_
  4.0 0.0 copy-done.3
  4.0 1.8 %project_sent.1 = (f32[4,16,768]{2,1,0:T(8,128)S(1)}, f32[16,128]{1,0:T(8,128)S(1)}, s32[16,128]{1,0:T(8,128)S(1)}) custom-call(s32[1]{0:T(128)} %bitcast.1.refs_1_.bank, s32[8]{0:T(128)} %own_ref.1, s32[8]{0:T(128)S(1)} %collective-permute-done.1.came_ref, bf16[8,1024]{1,0:T(8,128)(2,1)S(1)} %copy-done.3, ...), custom_call_target="tpu_custom_call" | custom-call | flops 117440512 | bytes 7340032 | tf_op jit(solution)/shard_map/project_sent/pallas_call | solution.py:188
  5.8 3.0 %collective-permute-start.2 = (f32[4,16,768]{2,1,0:T(8,128)S(1)}, f32[4,16,768]{2,1,0:T(8,128)S(1)}, u32[]{:S(2)}, u32[]{:S(2)}) collective-permute-start(f32[4,16,768]{2,1,0:T(8,128)S(1)} %get-tuple-element.31), channel_id=1, source_target_pairs={{0,2},{1,5},{2,0},{3,7},{4,6},{5,1},{6,4},{7,3},{8,10},{9,13},{10,... | collective-permute-start | bytes 589832 | tf_op jit(solution)/shard_map/ppermute | solution.py:545
  8.8 0.0 copy-done.4
  8.8 0.0 copy-start.2
  8.8 0.0 copy-start
  8.8 0.0 copy-start.1
  8.8 3.8 %project_kept.1 = (f32[4,16,768]{2,1,0:T(8,128)S(1)}, s32[64,128]{1,0:T(8,128)S(1)}) custom-call(s32[1]{0:T(128)} %bitcast.refs_0_, s32[1]{0:T(128)} %bitcast.1.refs_1_.bank, s32[8]{0:T(128)S(1)} %copy-done.4, bf16[8,1024]{1,0:T(8,128)(2,1)S(1)} %copy-done.3, bf16[8,1024]{1,0:T(8,128)(2,1)S(1)} %collective-permute-done.other_ref.refs_4_, ...), custom_call_target="tpu_custom_call" | custom-call | flops 83886080 | bytes 10485760 | tf_op jit(solution)/shard_map/project_kept/pallas_call | solution.py:234
  12.6 0.0 collective-permute-done.2.came_ref
  12.7 3.9 %collective-permute-start.3 = (f32[16,768]{1,0:T(8,128)S(1)}, f32[16,768]{1,0:T(8,128)S(1)}, u32[]{:S(2)}, u32[]{:S(2)}) collective-permute-start(f32[16,768]{1,0:T(8,128)S(1)} %get-tuple-element.33), channel_id=1, source_target_pairs={{0,12},{1,11},{2,14},{3,9},{4,8},{5,15},{6,10},{7,13},{8,4},{9,3},... | collective-permute-start | bytes 147464 | tf_op jit(solution)/shard_map/ppermute | solution.py:545
  16.6 0.0 collective-permute-start.4
  16.6 0.6 %collective-permute-start.5 = (f32[16,768]{1,0:T(8,128)S(1)}, f32[16,768]{1,0:T(8,128)S(1)}, u32[]{:S(2)}, u32[]{:S(2)}) collective-permute-start(f32[16,768]{1,0:T(8,128)S(1)} %get-tuple-element.35), channel_id=1, source_target_pairs={{0,4},{1,3},{2,6},{3,1},{4,0},{5,7},{6,2},{7,5},{8,12},{9,11},{10,... | collective-permute-start | bytes 147464 | tf_op jit(solution)/shard_map/ppermute | solution.py:545
  17.3 1.5 %collective-permute-done.3.refs_1_ = f32[16,768]{1,0:T(8,128)S(1)} collective-permute-done((f32[16,768]{1,0:T(8,128)S(1)}, f32[16,768]{1,0:T(8,128)S(1)}, u32[]{:S(2)}, u32[]{:S(2)}) %collective-permute-start.3) | collective-permute-done | bytes 49184 | tf_op jit(solution)/shard_map/ppermute | solution.py:545
  18.8 2.8 %collective-permute-done.4.refs_2_ = f32[16,768]{1,0:T(8,128)S(1)} collective-permute-done((f32[16,768]{1,0:T(8,128)S(1)}, f32[16,768]{1,0:T(8,128)S(1)}, u32[]{:S(2)}, u32[]{:S(2)}) %collective-permute-start.4) | collective-permute-done | bytes 49184 | tf_op jit(solution)/shard_map/ppermute | solution.py:545
  21.6 0.0 collective-permute-done.5.refs_3_
  21.6 0.0 copy-done.2
  21.6 0.4 correct.1
  22.0 0.0 collective-permute-start.6
  22.0 0.1 fusion
  22.1 1.1 %collective-permute-done.6.came_ref = f32[8,1152]{1,0:T(8,128)S(1)} collective-permute-done((f32[8,1152]{1,0:T(8,128)S(1)}, f32[8,1152]{1,0:T(8,128)S(1)}, u32[]{:S(2)}, u32[]{:S(2)}) %collective-permute-start.6) | collective-permute-done | bytes 36896 | tf_op jit(solution)/shard_map/ppermute | solution.py:533
  23.2 0.1 rotate.1
  23.3 1.6 %collective-permute-start.7 = (bf16[1,64,128]{2,1,0:T(8,128)(2,1)S(1)}, bf16[1,64,128]{2,1,0:T(8,128)(2,1)S(1)}, u32[]{:S(2)}, u32[]{:S(2)}) collective-permute-start(bf16[1,64,128]{2,1,0:T(8,128)(2,1)S(1)} %get-tuple-element.38.refs_3_.refs_0_.q_ref), channel_id=1, source_target_pairs={{0,2},{1,5},{2,0},{3,7},{4,6},{5,1},{6,4},{7,3},{8,10},{9,13},{10,... | collective-permute-start | bytes 49160 | tf_op jit(solution)/shard_map/ppermute | solution.py:545
  24.9 0.0 copy-done
  24.9 0.0 copy-done.1
  24.9 0.5 attend.5.refs_6_
  25.4 1.7 %collective-permute-done.7.refs_1_.refs_3_ = bf16[1,64,128]{2,1,0:T(8,128)(2,1)S(1)} collective-permute-done((bf16[1,64,128]{2,1,0:T(8,128)(2,1)S(1)}, bf16[1,64,128]{2,1,0:T(8,128)(2,1)S(1)}, u32[]{:S(2)}, u32[]{:S(2)}) %collective-permute-start.7) | collective-permute-done | bytes 16416 | tf_op jit(solution)/shard_map/ppermute | solution.py:545
  27.1 0.1 collective-permute-start.10
  27.3 3.3 %collective-permute-start.9 = (bf16[2,64,128]{2,1,0:T(8,128)(2,1)S(1)}, bf16[2,64,128]{2,1,0:T(8,128)(2,1)S(1)}, u32[]{:S(2)}, u32[]{:S(2)}) collective-permute-start(bf16[2,64,128]{2,1,0:T(8,128)(2,1)S(1)} %join.1), channel_id=1, source_target_pairs={{0,12},{1,11},{2,14},{3,9},{4,8},{5,15},{6,10},{7,13},{8,4},{9,3},... | collective-permute-start | bytes 98312 | tf_op jit(solution)/shard_map/ppermute | solution.py:545
  30.6 0.0 collective-permute-start.8
  30.6 0.0 slice-start
  30.6 0.5 attend.6.refs_7_
  31.1 0.0 slice-start.1
  31.1 0.3 collective-permute-done.10.refs_3_
  31.4 0.9 %attend.8.refs_9_ = bf16[2,80,128]{2,1,0:T(8,128)(2,1)S(1)} custom-call(s32[1]{0:T(128)} %bitcast.refs_0_, s32[1]{0:T(128)} %bitcast.1.refs_1_.bank, s32[64,128]{1,0:T(8,128)S(1)} %get-tuple-element.28.refs_2_, bf16[2,64,128]{2,1,0:T(8,128)(2,1)S(1)} %collective-permute-done.10.refs_3_, bf16[8,256,1024]{2,1,0:T(8,128)(2,1)S(1)} %copy-done, ...), custom_call_target="tpu_custom_call" | custom-call | flops 16777216 | bytes 2097152 | tf_op jit(solution)/shard_map/attend/pallas_call | solution.py:425
  32.3 0.0 slice-start.2
  32.3 0.8 %collective-permute-done.9.refs_3_ = bf16[2,64,128]{2,1,0:T(8,128)(2,1)S(1)} collective-permute-done((bf16[2,64,128]{2,1,0:T(8,128)(2,1)S(1)}, bf16[2,64,128]{2,1,0:T(8,128)(2,1)S(1)}, u32[]{:S(2)}, u32[]{:S(2)}) %collective-permute-start.9) | collective-permute-done | bytes 32800 | tf_op jit(solution)/shard_map/ppermute | solution.py:545
  33.1 0.9 %attend.7.refs_8_ = bf16[2,80,128]{2,1,0:T(8,128)(2,1)S(1)} custom-call(s32[1]{0:T(128)} %bitcast.refs_0_, s32[1]{0:T(128)} %bitcast.1.refs_1_.bank, s32[64,128]{1,0:T(8,128)S(1)} %get-tuple-element.28.refs_2_, bf16[2,64,128]{2,1,0:T(8,128)(2,1)S(1)} %collective-permute-done.9.refs_3_, bf16[8,256,1024]{2,1,0:T(8,128)(2,1)S(1)} %copy-done, ...), custom_call_target="tpu_custom_call" | custom-call | flops 16777216 | bytes 2097152 | tf_op jit(solution)/shard_map/attend/pallas_call | solution.py:425
  34.0 0.0 slice-start.3
  34.0 1.5 %collective-permute-done.8.refs_3_ = bf16[2,64,128]{2,1,0:T(8,128)(2,1)S(1)} collective-permute-done((bf16[2,64,128]{2,1,0:T(8,128)(2,1)S(1)}, bf16[2,64,128]{2,1,0:T(8,128)(2,1)S(1)}, u32[]{:S(2)}, u32[]{:S(2)}) %collective-permute-start.8) | collective-permute-done | bytes 32800 | tf_op jit(solution)/shard_map/ppermute | solution.py:545
  35.4 0.9 %attend.9 = bf16[8,80,128]{2,1,0:T(8,128)(2,1)S(1)} custom-call(s32[1]{0:T(128)} %bitcast.refs_0_, s32[1]{0:T(128)} %bitcast.1.refs_1_.bank, s32[64,128]{1,0:T(8,128)S(1)} %get-tuple-element.28.refs_2_, bf16[2,64,128]{2,1,0:T(8,128)(2,1)S(1)} %collective-permute-done.8.refs_3_, bf16[8,256,1024]{2,1,0:T(8,128)(2,1)S(1)} %copy-done, ...), custom_call_target="tpu_custom_call" | custom-call | flops 16777216 | bytes 16777216 | tf_op jit(solution)/shard_map/attend/pallas_call | solution.py:425
  36.3 11.5 %all_to_all.10.parts_ref = bf16[8,80,128]{2,1,0:T(8,128)(2,1)S(1)} all-to-all(bf16[8,80,128]{2,1,0:T(8,128)(2,1)S(1)} %attend.9), channel_id=1, replica_groups=mesh['groups'=2,'tensor'=8,'bank'=2] {'tensor'}, dimensions={0} | all-to-all | bytes 327680 | tf_op jit(solution)/shard_map/all_to_all | solution.py:537
  47.8 0.5 combine.1.x_ref
  48.3 0.0 slice-done
  48.3 0.0 slice-done.1
  48.3 0.0 slice-done.2
  48.3 0.0 slice-done.3
  48.3 2.3 %output.1 = bf16[8,8,1024]{2,1,0:T(8,128)(2,1)S(1)} custom-call(bf16[8,1024]{1,0:T(8,128)(2,1)S(1)} %combine.1.x_ref, bf16[1024,8192]{1,0:T(8,128)(2,1)S(1)} %bitcast.4), custom_call_target="tpu_custom_call" | custom-call | flops 134217728 | bytes 16777216 | tf_op jit(solution)/shard_map/output/pallas_call | solution.py:503
  50.6 9.7 %all_to_all.11.parts_ref = bf16[8,8,1024]{2,1,0:T(8,128)(2,1)S(1)} all-to-all(bf16[8,8,1024]{2,1,0:T(8,128)(2,1)S(1)} %output.1), channel_id=1, replica_groups=mesh['groups'=2,'tensor'=8,'bank'=2] {'tensor'}, dimensions={0} | all-to-all | bytes 262144 | tf_op jit(solution)/shard_map/all_to_all | solution.py:537
  60.4 0.6 %residual.1 = bf16[8,1024]{1,0:T(8,128)(2,1)} custom-call(bf16[8,1024]{1,0:T(8,128)(2,1)S(1)} %copy-done.3, bf16[8,8,1024]{2,1,0:T(8,128)(2,1)S(1)} %all_to_all.11.parts_ref), custom_call_target="tpu_custom_call" | custom-call | tf_op jit(solution)/shard_map/residual/pallas_call | solution.py:522
  (5 shorter events, 0.0 us)
Async XLA Ops:
  0.0 4.0 %collective-permute-start = (bf16[8,1024]{1,0:T(8,128)(2,1)}, bf16[8,1024]{1,0:T(8,128)(2,1)S(1)}, u32[]{:S(2)}, u32[]{:S(2)}) collective-permute-start(bf16[8,1024]{1,0:T(8,128)(2,1)} %x_ref.3), channel_id=1, source_target_pairs={{0,1},{1,0},{2,3},{3,2},{4,5},{5,4},{6,7},{7,6},{8,9},{9,8},{10,11... | collective-permute-start | bytes 49160 | tf_op jit(solution)/shard_map/ppermute | solution.py:533
  0.5 3.5 %collective-permute-start.1 = (s32[8]{0:T(128)}, s32[8]{0:T(128)S(1)}, u32[]{:S(2)}, u32[]{:S(2)}) collective-permute-start(s32[8]{0:T(128)} %own_ref.1), channel_id=1, source_target_pairs={{0,1},{1,0},{2,3},{3,2},{4,5},{5,4},{6,7},{7,6},{8,9},{9,8},{10,11... | collective-permute-start | bytes 104 | tf_op jit(solution)/shard_map/ppermute | solution.py:533
  0.5 3.5 %copy-start.3 = (bf16[8,1024]{1,0:T(8,128)(2,1)S(1)}, bf16[8,1024]{1,0:T(8,128)(2,1)}, u32[]{:S(2)}) copy-start(bf16[8,1024]{1,0:T(8,128)(2,1)} %x_ref.3) | copy-start | bytes 49156
  3.9 4.9 %copy-start.4 = (s32[8]{0:T(128)S(1)}, s32[8]{0:T(128)}, u32[]{:S(2)}) copy-start(s32[8]{0:T(128)} %refs_2_.3) | copy-start | bytes 100
  5.8 6.9 %collective-permute-start.2 = (f32[4,16,768]{2,1,0:T(8,128)S(1)}, f32[4,16,768]{2,1,0:T(8,128)S(1)}, u32[]{:S(2)}, u32[]{:S(2)}) collective-permute-start(f32[4,16,768]{2,1,0:T(8,128)S(1)} %get-tuple-element.31), channel_id=1, source_target_pairs={{0,2},{1,5},{2,0},{3,7},{4,6},{5,1},{6,4},{7,3},{8,10},{9,13},{10,... | collective-permute-start | bytes 589832 | tf_op jit(solution)/shard_map/ppermute | solution.py:545
  8.8 12.8 %copy-start.2 = (bf16[16,64,1024]{2,1,0:T(8,128)(2,1)S(1)}, bf16[16,64,1024]{2,1,0:T(8,128)(2,1)}, u32[]{:S(2)}) copy-start(bf16[16,64,1024]{2,1,0:T(8,128)(2,1)} %up_ref.1) | copy-start | bytes 6291460
  8.8 16.1 %copy-start = (bf16[8,256,1024]{2,1,0:T(8,128)(2,1)S(1)}, bf16[8,256,1024]{2,1,0:T(8,128)(2,1)}, u32[]{:S(2)}) copy-start(bf16[8,256,1024]{2,1,0:T(8,128)(2,1)} %refs_4_.9) | copy-start | bytes 12582916
  8.8 16.1 %copy-start.1 = (bf16[8,256,1024]{2,1,0:T(8,128)(2,1)S(1)}, bf16[8,256,1024]{2,1,0:T(8,128)(2,1)}, u32[]{:S(2)}) copy-start(bf16[8,256,1024]{2,1,0:T(8,128)(2,1)} %refs_5_.11) | copy-start | bytes 12582916
  12.7 6.1 %collective-permute-start.3 = (f32[16,768]{1,0:T(8,128)S(1)}, f32[16,768]{1,0:T(8,128)S(1)}, u32[]{:S(2)}, u32[]{:S(2)}) collective-permute-start(f32[16,768]{1,0:T(8,128)S(1)} %get-tuple-element.33), channel_id=1, source_target_pairs={{0,12},{1,11},{2,14},{3,9},{4,8},{5,15},{6,10},{7,13},{8,4},{9,3},... | collective-permute-start | bytes 147464 | tf_op jit(solution)/shard_map/ppermute | solution.py:545
  16.6 5.0 %collective-permute-start.4 = (f32[16,768]{1,0:T(8,128)S(1)}, f32[16,768]{1,0:T(8,128)S(1)}, u32[]{:S(2)}, u32[]{:S(2)}) collective-permute-start(f32[16,768]{1,0:T(8,128)S(1)} %get-tuple-element.34), channel_id=1, source_target_pairs={{0,8},{1,9},{2,10},{3,11},{4,12},{5,13},{6,14},{7,15},{8,0},{9,1},... | collective-permute-start | bytes 147464 | tf_op jit(solution)/shard_map/ppermute | solution.py:545
  16.6 5.0 %collective-permute-start.5 = (f32[16,768]{1,0:T(8,128)S(1)}, f32[16,768]{1,0:T(8,128)S(1)}, u32[]{:S(2)}, u32[]{:S(2)}) collective-permute-start(f32[16,768]{1,0:T(8,128)S(1)} %get-tuple-element.35), channel_id=1, source_target_pairs={{0,4},{1,3},{2,6},{3,1},{4,0},{5,7},{6,2},{7,5},{8,12},{9,11},{10,... | collective-permute-start | bytes 147464 | tf_op jit(solution)/shard_map/ppermute | solution.py:545
  22.0 1.2 %collective-permute-start.6 = (f32[8,1152]{1,0:T(8,128)S(1)}, f32[8,1152]{1,0:T(8,128)S(1)}, u32[]{:S(2)}, u32[]{:S(2)}) collective-permute-start(f32[8,1152]{1,0:T(8,128)S(1)} %get-tuple-element.37), channel_id=1, source_target_pairs={{0,1},{1,0},{2,3},{3,2},{4,5},{5,4},{6,7},{7,6},{8,9},{9,8},{10,11... | collective-permute-start | bytes 110600 | tf_op jit(solution)/shard_map/ppermute | solution.py:533
  23.3 3.8 %collective-permute-start.7 = (bf16[1,64,128]{2,1,0:T(8,128)(2,1)S(1)}, bf16[1,64,128]{2,1,0:T(8,128)(2,1)S(1)}, u32[]{:S(2)}, u32[]{:S(2)}) collective-permute-start(bf16[1,64,128]{2,1,0:T(8,128)(2,1)S(1)} %get-tuple-element.38.refs_3_.refs_0_.q_ref), channel_id=1, source_target_pairs={{0,2},{1,5},{2,0},{3,7},{4,6},{5,1},{6,4},{7,3},{8,10},{9,13},{10,... | collective-permute-start | bytes 49160 | tf_op jit(solution)/shard_map/ppermute | solution.py:545
  27.1 4.3 %collective-permute-start.10 = (bf16[2,64,128]{2,1,0:T(8,128)(2,1)S(1)}, bf16[2,64,128]{2,1,0:T(8,128)(2,1)S(1)}, u32[]{:S(2)}, u32[]{:S(2)}) collective-permute-start(bf16[2,64,128]{2,1,0:T(8,128)(2,1)S(1)} %join.1), channel_id=1, source_target_pairs={{0,4},{1,3},{2,6},{3,1},{4,0},{5,7},{6,2},{7,5},{8,12},{9,11},{10,... | collective-permute-start | bytes 98312 | tf_op jit(solution)/shard_map/ppermute | solution.py:545
  27.3 5.8 %collective-permute-start.9 = (bf16[2,64,128]{2,1,0:T(8,128)(2,1)S(1)}, bf16[2,64,128]{2,1,0:T(8,128)(2,1)S(1)}, u32[]{:S(2)}, u32[]{:S(2)}) collective-permute-start(bf16[2,64,128]{2,1,0:T(8,128)(2,1)S(1)} %join.1), channel_id=1, source_target_pairs={{0,12},{1,11},{2,14},{3,9},{4,8},{5,15},{6,10},{7,13},{8,4},{9,3},... | collective-permute-start | bytes 98312 | tf_op jit(solution)/shard_map/ppermute | solution.py:545
  30.6 4.8 %collective-permute-start.8 = (bf16[2,64,128]{2,1,0:T(8,128)(2,1)S(1)}, bf16[2,64,128]{2,1,0:T(8,128)(2,1)S(1)}, u32[]{:S(2)}, u32[]{:S(2)}) collective-permute-start(bf16[2,64,128]{2,1,0:T(8,128)(2,1)S(1)} %join.1), channel_id=1, source_target_pairs={{0,8},{1,9},{2,10},{3,11},{4,12},{5,13},{6,14},{7,15},{8,0},{9,1},... | collective-permute-start | bytes 98312 | tf_op jit(solution)/shard_map/ppermute | solution.py:545
  30.6 17.7 %slice-start = ((s8[16777216]{0:T(1024)(128)(4,1)}), s8[4194304]{0:T(1024)(128)(4,1)S(1)}, s32[]{:S(2)}) async-start(s8[16777216]{0:T(1024)(128)(4,1)} %bitcast.3), calls=%async_computation.2 | async-start | bytes 8388608
  31.1 17.2 %slice-start.1 = ((s8[16777216]{0:T(1024)(128)(4,1)}), s8[4194304]{0:T(1024)(128)(4,1)S(1)}, s32[]{:S(2)}) async-start(s8[16777216]{0:T(1024)(128)(4,1)} %bitcast.3), calls=%async_computation.3 | async-start | bytes 8388608
  32.3 16.0 %slice-start.2 = ((s8[16777216]{0:T(1024)(128)(4,1)}), s8[4194304]{0:T(1024)(128)(4,1)S(1)}, s32[]{:S(2)}) async-start(s8[16777216]{0:T(1024)(128)(4,1)} %bitcast.3), calls=%async_computation.4 | async-start | bytes 8388608
  34.0 14.4 %slice-start.3 = ((s8[16777216]{0:T(1024)(128)(4,1)}), s8[4194304]{0:T(1024)(128)(4,1)S(1)}, s32[]{:S(2)}) async-start(s8[16777216]{0:T(1024)(128)(4,1)} %bitcast.3), calls=%async_computation.5 | async-start | bytes 8388608

commit v14 on v13

--- a/solution.py
+++ b/solution.py
@@ -66,13 +66,14 @@
 
 
 def adapter_column(refs, bank, count):
-    rows = len(refs) * refs[0].shape[0]
-    row = iota((rows, HEAD_DIM), 0)
-    column = jnp.zeros((rows, HEAD_DIM), jnp.int32)
-    for r in range(rows):
-        ref = refs[r // refs[0].shape[0]]
-        column = jnp.where(row == r, ref[r % ref.shape[0]], column)
-    return column - bank * count
+    columns = []
+    for ref in refs:
+        rows = ref.shape[1]
+        index = jnp.broadcast_to(ref[...].astype(F32), (rows, rows))
+        diagonal = iota((rows, rows), 0) == iota((rows, rows), 1)
+        columns.append(jnp.sum(jnp.where(diagonal, index, 0.0), axis=1, keepdims=True))
+    column = jnp.concatenate(columns, axis=0).astype(jnp.int32) - bank * count
+    return jnp.broadcast_to(column, (column.shape[0], HEAD_DIM))
 
 
 def start_slots(parity, ranks, place, bank, w_ref, kv_ref, w_buf, kv_buf, sems, kv_sems):
@@ -98,11 +99,8 @@
             copy.wait()
 
 
-def fetch_kernel(ranks, place, bank, w_ref, kv_ref, down_ref, w_buf, kv_buf, down_buf, *sems):
-    down_copy = pltpu.make_async_copy(down_ref, down_buf, sems[2])
-    down_copy.start()
-    wait_all(start_slots(1, ranks, place, bank, w_ref, kv_ref, w_buf, kv_buf, *sems[:2]))
-    down_copy.wait()
+def fetch_kernel(ranks, place, bank, *refs):
+    wait_all(start_slots(1, ranks, place, bank, *refs))
 
 
 def slot_buffers(wq, ranks):
@@ -117,20 +115,20 @@
     return [pltpu.SemaphoreType.DMA((count, CHUNKS))] * 2
 
 
-def fetch(place, bank, wq, wkv, down, ranks):
-    out = slot_buffers(wq, ranks) + [jax.ShapeDtypeStruct(down.shape, BF16)]
+def fetch(place, bank, wq, wkv, ranks):
+    out = slot_buffers(wq, ranks)
     return pl.pallas_call(
         lambda *refs: fetch_kernel(ranks, *refs),
-        in_specs=[scalar()] * 2 + [big()] * 3,
-        out_specs=[whole()] * 3,
+        in_specs=[scalar()] * 2 + [big()] * 2,
+        out_specs=[whole()] * 2,
         out_shape=out,
-        scratch_shapes=slot_sems(ranks // 2) + [pltpu.SemaphoreType.DMA(())],
+        scratch_shapes=slot_sems(ranks // 2),
         compiler_params=params(),
         cost_estimate=pl.CostEstimate(
             flops=0, bytes_accessed=2 * sum(o.size for o in out), transcendentals=0
         ),
         name="fetch",
-    )(place, bank, wq, wkv, down)
+    )(place, bank, wq, wkv)
 
 
 def beam_rows(x_ref, other_ref):
@@ -146,12 +144,16 @@
 
 
 def project_sent_kernel(
-    bank, own_ref, came_ref, x_ref, other_ref, w_buf, kv_buf, down_buf, *refs
+    bank, own_ref, came_ref, x_ref, other_ref, w_buf, kv_buf, down_ref, *refs
 ):
-    out, inner, column_out, *index, sems = refs
+    out, inner, column_out, down_buf, sems = refs
+    adapters, rank, depth = down_buf.shape
+    part = adapters // sems.shape[0]
     copies = [
-        pltpu.make_async_copy(ref, held, sems.at[n])
-        for n, (ref, held) in enumerate(zip((own_ref, came_ref), index))
+        pltpu.make_async_copy(
+            down_ref.at[pl.ds(c * part, part)], down_buf.at[pl.ds(c * part, part)], sems.at[c]
+        )
+        for c in range(sems.shape[0])
     ]
     for copy in copies:
         copy.start()
@@ -160,17 +162,16 @@
     for s in range(out.shape[0]):
         out[s, :, :width] = jnp.dot(x, w_buf[s], preferred_element_type=F32)
     project_keyval(x, kv_buf, out, width)
-    adapters, rank, depth = down_buf.shape
+    column = adapter_column((own_ref, came_ref), bank[0], adapters)
+    column_out[...] = column
+    for copy in copies:
+        copy.wait()
     every = lax.dot_general(
         x,
         down_buf[...].reshape(adapters * rank, depth),
         (((1,), (1,)), ((), ())),
         preferred_element_type=F32,
     )
-    for copy in copies:
-        copy.wait()
-    column = adapter_column(index, bank[0], adapters)
-    column_out[...] = column
     lane = iota(column.shape, 1)
     per = HEAD_DIM // rank
     total = jnp.zeros(column.shape, F32)
@@ -182,28 +183,27 @@
         out[s, :, width + HEAD_DIM :] = total
 
 
-def project_sent(bank, index, x, other, weights):
+def project_sent(bank, index, x, other, weights, down):
     half, _, width = weights[0].shape
     rows = 2 * x.shape[0]
     return pl.pallas_call(
         project_sent_kernel,
-        in_specs=[scalar(), big(), pl.BlockSpec(memory_space=pl.ANY)] + [whole()] * 5,
+        in_specs=[scalar()] + [whole()] * 6 + [big()],
         out_specs=[whole()] * 3,
         out_shape=[
             shape(half, rows, width + 2 * HEAD_DIM),
             shape(rows, HEAD_DIM),
             shape(rows, HEAD_DIM, dtype=jnp.int32),
         ],
-        scratch_shapes=[pltpu.SMEM(index[0].shape, jnp.int32)] * 2
-        + [pltpu.SemaphoreType.DMA((2,))],
-        compiler_params=params(),
+        scratch_shapes=[pltpu.VMEM(down.shape, BF16), pltpu.SemaphoreType.DMA((2,))],
+        compiler_params=params(8),
         cost_estimate=pl.CostEstimate(
-            flops=2 * rows * sum(w.size for w in weights),
-            bytes_accessed=2 * sum(w.size for w in weights),
+            flops=2 * rows * (sum(w.size for w in weights) + down.size),
+            bytes_accessed=2 * (sum(w.size for w in weights) + down.size),
             transcendentals=0,
         ),
         name="project_sent",
-    )(bank, in_hbm(index[0]), index[1], x, other, *weights)
+    )(bank, *[i.reshape(1, -1) for i in index], x, other, *weights, down)
 
 
 def project_kept_kernel(
@@ -571,8 +571,8 @@
     sine = jnp.where(lane < half, -1.0, 1.0) * jnp.sin(angles)
     weights = in_hbm(query_weight), in_hbm(keyvalue_weight)
     down = in_hbm(lowrank_down_factors.swapaxes(1, 2))
-    ahead = fetch(place, bank, *weights, down, ranks)
-    sent, inner, column = project_sent(bank, index, x, x_other, ahead)
+    odd = fetch(place, bank, *weights, ranks)
+    sent, inner, column = project_sent(bank, index, x, x_other, odd, down)
     came = hop(sent, 1)
     kept, length = project_kept(
         place, bank, beam_cache_length, x, x_other, *weights, inner, ranks
@@ -591,13 +591,12 @@
     pair = join([query, came])
     pairs = [hop(pair, slot) for slot in near]
     done = [done, attended_part(came, (1,))]
-    order, slots = [0, 2, 1], [0, 1]
-    for i in order[:-1]:
+    slots = [0, 1]
+    for i in range(len(near) - 1):
         done.append(attended_part(pairs[i], (near[i], near[i] + 1)))
         slots += [near[i], near[i] + 1]
-    i = order[-1]
-    last = near[i], near[i] + 1
-    partial = attended_part(pairs[i], last, earlier=tuple(slots), before=tuple(done))
+    last = near[-1], near[-1] + 1
+    partial = attended_part(pairs[-1], last, earlier=tuple(slots), before=tuple(done))
     attended = combine(traded(partial), query, key_new, value_new)
     return residual(x, traded(output(attended, output_weight, ranks)))
 

time: 61.2 us -> 61.3 us (level)
    pallas_call x1, Pallas kernels: 1.77 us -> 2.88 us  [project_sent(): pl.pallas_call(project_sent_kernel, in_specs=[scalar()] + [whole()] * 6 +...]
    pallas_call x1, Pallas kernels: 3.41 us -> 2.67 us  [fetch(): pl.pallas_call(lambda *refs: fetch_kernel(ranks, *refs), in_specs=[scalar...]
  transfers between devices with their start and end apart: 11 -> 11, of which waited for: 7 -> 6; matrix products, arithmetic and copies ran while one was open for 0% -> 0% of each run, Pallas kernels for 16% -> 15%
where the time goes in v14:
time: 61.3 us; the launch traced here: 61.1 us
  blocking collectives  20.6 us (34%)
  Pallas kernels  16.9 us (28%)
  starting transfers between devices  13.2 us (22%)
  waiting for transfers between devices  10 us (16%)
    all_to_all x2, blocking collectives, traded(): return lax.all_to_all(blocks, 'tensor', 0, 0, tiled=True)  20.6 us
    ppermute x8, starting transfers between devices, hop(): return lax.ppermute(x, ('tensor', 'bank'), pairs)  12.7 us
    ppermute x8, waiting for transfers between devices, hop(): return lax.ppermute(x, ('tensor', 'bank'), pairs)  8.93 us
    pallas_call x1, Pallas kernels, project_kept(): pl.pallas_call(lambda *refs: project_kept_kernel(ranks, *refs), in_specs=...  3.83 us
    pallas_call x5, Pallas kernels, attend(): pl.pallas_call(lambda *refs: attend_kernel(slots, earlier, *refs), in_spe...  3.59 us
    pallas_call x1, Pallas kernels, project_sent(): pl.pallas_call(project_sent_kernel, in_specs=[scalar()] + [whole()] * 6 +...  2.88 us
    pallas_call x1, Pallas kernels, fetch(): pl.pallas_call(lambda *refs: fetch_kernel(ranks, *refs), in_specs=[scalar...  2.67 us
    pallas_call x1, Pallas kernels, output(): pl.pallas_call(output_kernel, in_specs=[whole()] * 2, out_specs=whole(),...  2.28 us
  transfers between devices with their start and end apart: 11, of which 6 were waited for; matrix products, arithmetic and copies ran while one was open for 0% of the time, Pallas kernels for 15%

profile of v14, /device:TPU:0, one launch (start us, length us, event | category | flops | bytes accessed | tf_op | source)
XLA Modules:
  0.0 61.1 jit_solution(16285181791091712154)
XLA Ops:
  0.0 0.5 collective-permute-start
  0.5 0.1 collective-permute-start.1
  0.5 0.0 copy-start.3
  0.5 0.0 copy-start.4
  0.5 2.7 %fetch.1 = (bf16[4,1024,512]{2,1,0:T(8,128)(2,1)S(1)}, bf16[1024,512]{1,0:T(8,128)(2,1)S(1)}) custom-call(s32[1]{0:T(128)} %bitcast.refs_0_, s32[1]{0:T(128)} %bitcast.1.refs_1_.bank, bf16[1024,8192]{1,0:T(8,128)(2,1)} %refs_5_.6, bf16[1024,2048]{1,0:T(8,128)(2,1)} %refs_6_.1), custom_call_target="tpu_custom_call" | custom-call | bytes 5242880 | tf_op jit(solution)/shard_map/fetch/pallas_call | solution.py:120
  3.2 0.0 copy-start.5
  3.2 0.0 collective-permute-done.1
  3.2 0.0 collective-permute-done.other_ref.refs_4_
  3.2 0.0 copy-done.3
  3.2 0.0 copy-done.4
  3.2 2.9 %project_sent.1 = (f32[4,16,768]{2,1,0:T(8,128)S(1)}, f32[16,128]{1,0:T(8,128)S(1)}, s32[16,128]{1,0:T(8,128)S(1)}) custom-call(s32[1]{0:T(128)} %bitcast.1.refs_1_.bank, s32[1,8]{1,0:T(1,128)S(1)} %bitcast.7, s32[1,8]{1,0:T(1,128)S(1)} %bitcast.8, bf16[8,1024]{1,0:T(8,128)(2,1)S(1)} %copy-done.3, ...), custom_call_target="tpu_custom_call" | custom-call | flops 117440512 | bytes 7340032 | tf_op jit(solution)/shard_map/project_sent/pallas_call | solution.py:189
  6.1 3.0 %collective-permute-start.2 = (f32[4,16,768]{2,1,0:T(8,128)S(1)}, f32[4,16,768]{2,1,0:T(8,128)S(1)}, u32[]{:S(2)}, u32[]{:S(2)}) collective-permute-start(f32[4,16,768]{2,1,0:T(8,128)S(1)} %get-tuple-element.29), channel_id=1, source_target_pairs={{0,2},{1,5},{2,0},{3,7},{4,6},{5,1},{6,4},{7,3},{8,10},{9,13},{10,... | collective-permute-start | bytes 589832 | tf_op jit(solution)/shard_map/ppermute | solution.py:545
  9.2 0.0 copy-done.5
  9.2 0.0 copy-start.2
  9.2 0.0 copy-start
  9.2 0.0 copy-start.1
  9.2 3.8 %project_kept.1 = (f32[4,16,768]{2,1,0:T(8,128)S(1)}, s32[64,128]{1,0:T(8,128)S(1)}) custom-call(s32[1]{0:T(128)} %bitcast.refs_0_, s32[1]{0:T(128)} %bitcast.1.refs_1_.bank, s32[8]{0:T(128)S(1)} %copy-done.5, bf16[8,1024]{1,0:T(8,128)(2,1)S(1)} %copy-done.3, bf16[8,1024]{1,0:T(8,128)(2,1)S(1)} %collective-permute-done.other_ref.refs_4_, ...), custom_call_target="tpu_custom_call" | custom-call | flops 83886080 | bytes 10485760 | tf_op jit(solution)/shard_map/project_kept/pallas_call | solution.py:234
  13.0 0.0 collective-permute-done.2.came_ref
  13.1 3.9 %collective-permute-start.3 = (f32[16,768]{1,0:T(8,128)S(1)}, f32[16,768]{1,0:T(8,128)S(1)}, u32[]{:S(2)}, u32[]{:S(2)}) collective-permute-start(f32[16,768]{1,0:T(8,128)S(1)} %get-tuple-element.31), channel_id=1, source_target_pairs={{0,12},{1,11},{2,14},{3,9},{4,8},{5,15},{6,10},{7,13},{8,4},{9,3},... | collective-permute-start | bytes 147464 | tf_op jit(solution)/shard_map/ppermute | solution.py:545
  17.0 0.0 collective-permute-start.4
  17.0 0.6 %collective-permute-start.5 = (f32[16,768]{1,0:T(8,128)S(1)}, f32[16,768]{1,0:T(8,128)S(1)}, u32[]{:S(2)}, u32[]{:S(2)}) collective-permute-start(f32[16,768]{1,0:T(8,128)S(1)} %get-tuple-element.33), channel_id=1, source_target_pairs={{0,4},{1,3},{2,6},{3,1},{4,0},{5,7},{6,2},{7,5},{8,12},{9,11},{10,... | collective-permute-start | bytes 147464 | tf_op jit(solution)/shard_map/ppermute | solution.py:545
  17.7 1.5 %collective-permute-done.3.refs_1_ = f32[16,768]{1,0:T(8,128)S(1)} collective-permute-done((f32[16,768]{1,0:T(8,128)S(1)}, f32[16,768]{1,0:T(8,128)S(1)}, u32[]{:S(2)}, u32[]{:S(2)}) %collective-permute-start.3) | collective-permute-done | bytes 49184 | tf_op jit(solution)/shard_map/ppermute | solution.py:545
  19.2 2.8 %collective-permute-done.4.refs_2_ = f32[16,768]{1,0:T(8,128)S(1)} collective-permute-done((f32[16,768]{1,0:T(8,128)S(1)}, f32[16,768]{1,0:T(8,128)S(1)}, u32[]{:S(2)}, u32[]{:S(2)}) %collective-permute-start.4) | collective-permute-done | bytes 49184 | tf_op jit(solution)/shard_map/ppermute | solution.py:545
  22.0 0.0 collective-permute-done.5.refs_3_
  22.0 0.0 copy-done.2
  22.0 0.4 correct.1
  22.4 0.0 collective-permute-start.6
  22.4 0.1 fusion
  22.5 1.1 %collective-permute-done.6.came_ref = f32[8,1152]{1,0:T(8,128)S(1)} collective-permute-done((f32[8,1152]{1,0:T(8,128)S(1)}, f32[8,1152]{1,0:T(8,128)S(1)}, u32[]{:S(2)}, u32[]{:S(2)}) %collective-permute-start.6) | collective-permute-done | bytes 36896 | tf_op jit(solution)/shard_map/ppermute | solution.py:533
  23.6 0.1 rotate.1
  23.7 1.6 %collective-permute-start.7 = (bf16[1,64,128]{2,1,0:T(8,128)(2,1)S(1)}, bf16[1,64,128]{2,1,0:T(8,128)(2,1)S(1)}, u32[]{:S(2)}, u32[]{:S(2)}) collective-permute-start(bf16[1,64,128]{2,1,0:T(8,128)(2,1)S(1)} %get-tuple-element.36.refs_3_.refs_0_.q_ref), channel_id=1, source_target_pairs={{0,2},{1,5},{2,0},{3,7},{4,6},{5,1},{6,4},{7,3},{8,10},{9,13},{10,... | collective-permute-start | bytes 49160 | tf_op jit(solution)/shard_map/ppermute | solution.py:545
  25.3 0.0 copy-done
  25.3 0.0 copy-done.1
  25.3 0.5 attend.5.refs_6_
  25.8 1.7 %collective-permute-done.7.refs_1_.refs_3_ = bf16[1,64,128]{2,1,0:T(8,128)(2,1)S(1)} collective-permute-done((bf16[1,64,128]{2,1,0:T(8,128)(2,1)S(1)}, bf16[1,64,128]{2,1,0:T(8,128)(2,1)S(1)}, u32[]{:S(2)}, u32[]{:S(2)}) %collective-permute-start.7) | collective-permute-done | bytes 16416 | tf_op jit(solution)/shard_map/ppermute | solution.py:545
  27.5 2.0 %collective-permute-start.10 = (bf16[2,64,128]{2,1,0:T(8,128)(2,1)S(1)}, bf16[2,64,128]{2,1,0:T(8,128)(2,1)S(1)}, u32[]{:S(2)}, u32[]{:S(2)}) collective-permute-start(bf16[2,64,128]{2,1,0:T(8,128)(2,1)S(1)} %join.1), channel_id=1, source_target_pairs={{0,8},{1,9},{2,10},{3,11},{4,12},{5,13},{6,14},{7,15},{8,0},{9,1},... | collective-permute-start | bytes 98312 | tf_op jit(solution)/shard_map/ppermute | solution.py:545
  29.5 0.5 collective-permute-start.9
  30.1 0.9 %collective-permute-start.8 = (bf16[2,64,128]{2,1,0:T(8,128)(2,1)S(1)}, bf16[2,64,128]{2,1,0:T(8,128)(2,1)S(1)}, u32[]{:S(2)}, u32[]{:S(2)}) collective-permute-start(bf16[2,64,128]{2,1,0:T(8,128)(2,1)S(1)} %join.1), channel_id=1, source_target_pairs={{0,4},{1,3},{2,6},{3,1},{4,0},{5,7},{6,2},{7,5},{8,12},{9,11},{10,... | collective-permute-start | bytes 98312 | tf_op jit(solution)/shard_map/ppermute | solution.py:545
  31.0 0.0 slice-start
  31.0 0.5 attend.6.refs_7_
  31.5 0.0 slice-start.1
  31.5 0.8 %collective-permute-done.10.refs_3_ = bf16[2,64,128]{2,1,0:T(8,128)(2,1)S(1)} collective-permute-done((bf16[2,64,128]{2,1,0:T(8,128)(2,1)S(1)}, bf16[2,64,128]{2,1,0:T(8,128)(2,1)S(1)}, u32[]{:S(2)}, u32[]{:S(2)}) %collective-permute-start.10) | collective-permute-done | bytes 32800 | tf_op jit(solution)/shard_map/ppermute | solution.py:545
  32.3 0.9 %attend.8.refs_9_ = bf16[2,80,128]{2,1,0:T(8,128)(2,1)S(1)} custom-call(s32[1]{0:T(128)} %bitcast.refs_0_, s32[1]{0:T(128)} %bitcast.1.refs_1_.bank, s32[64,128]{1,0:T(8,128)S(1)} %get-tuple-element.26.refs_2_, bf16[2,64,128]{2,1,0:T(8,128)(2,1)S(1)} %collective-permute-done.10.refs_3_, bf16[8,256,1024]{2,1,0:T(8,128)(2,1)S(1)} %copy-done, ...), custom_call_target="tpu_custom_call" | custom-call | flops 16777216 | bytes 2097152 | tf_op jit(solution)/shard_map/attend/pallas_call | solution.py:425
  33.2 0.0 slice-start.2
  33.2 2.1 %collective-permute-done.9.refs_3_ = bf16[2,64,128]{2,1,0:T(8,128)(2,1)S(1)} collective-permute-done((bf16[2,64,128]{2,1,0:T(8,128)(2,1)S(1)}, bf16[2,64,128]{2,1,0:T(8,128)(2,1)S(1)}, u32[]{:S(2)}, u32[]{:S(2)}) %collective-permute-start.9) | collective-permute-done | bytes 32800 | tf_op jit(solution)/shard_map/ppermute | solution.py:545
  35.3 0.8 %attend.7.refs_8_ = bf16[2,80,128]{2,1,0:T(8,128)(2,1)S(1)} custom-call(s32[1]{0:T(128)} %bitcast.refs_0_, s32[1]{0:T(128)} %bitcast.1.refs_1_.bank, s32[64,128]{1,0:T(8,128)S(1)} %get-tuple-element.26.refs_2_, bf16[2,64,128]{2,1,0:T(8,128)(2,1)S(1)} %collective-permute-done.9.refs_3_, bf16[8,256,1024]{2,1,0:T(8,128)(2,1)S(1)} %copy-done, ...), custom_call_target="tpu_custom_call" | custom-call | flops 16777216 | bytes 2097152 | tf_op jit(solution)/shard_map/attend/pallas_call | solution.py:425
  36.1 0.0 slice-start.3
  36.1 0.0 collective-permute-done.8.refs_3_
  36.1 0.9 %attend.9 = bf16[8,80,128]{2,1,0:T(8,128)(2,1)S(1)} custom-call(s32[1]{0:T(128)} %bitcast.refs_0_, s32[1]{0:T(128)} %bitcast.1.refs_1_.bank, s32[64,128]{1,0:T(8,128)S(1)} %get-tuple-element.26.refs_2_, bf16[2,64,128]{2,1,0:T(8,128)(2,1)S(1)} %collective-permute-done.8.refs_3_, bf16[8,256,1024]{2,1,0:T(8,128)(2,1)S(1)} %copy-done, ...), custom_call_target="tpu_custom_call" | custom-call | flops 16777216 | bytes 16777216 | tf_op jit(solution)/shard_map/attend/pallas_call | solution.py:425
  37.0 10.9 %all_to_all.10.parts_ref = bf16[8,80,128]{2,1,0:T(8,128)(2,1)S(1)} all-to-all(bf16[8,80,128]{2,1,0:T(8,128)(2,1)S(1)} %attend.9), channel_id=1, replica_groups=mesh['groups'=2,'tensor'=8,'bank'=2] {'tensor'}, dimensions={0} | all-to-all | bytes 327680 | tf_op jit(solution)/shard_map/all_to_all | solution.py:537
  47.9 0.5 combine.1.x_ref
  48.4 0.0 slice-done
  48.4 0.0 slice-done.1
  48.4 0.0 slice-done.2
  48.4 0.0 slice-done.3
  48.4 2.3 %output.1 = bf16[8,8,1024]{2,1,0:T(8,128)(2,1)S(1)} custom-call(bf16[8,1024]{1,0:T(8,128)(2,1)S(1)} %combine.1.x_ref, bf16[1024,8192]{1,0:T(8,128)(2,1)S(1)} %bitcast.6), custom_call_target="tpu_custom_call" | custom-call | flops 134217728 | bytes 16777216 | tf_op jit(solution)/shard_map/output/pallas_call | solution.py:503
  50.7 9.7 %all_to_all.11.parts_ref = bf16[8,8,1024]{2,1,0:T(8,128)(2,1)S(1)} all-to-all(bf16[8,8,1024]{2,1,0:T(8,128)(2,1)S(1)} %output.1), channel_id=1, replica_groups=mesh['groups'=2,'tensor'=8,'bank'=2] {'tensor'}, dimensions={0} | all-to-all | bytes 262144 | tf_op jit(solution)/shard_map/all_to_all | solution.py:537
  60.5 0.6 %residual.1 = bf16[8,1024]{1,0:T(8,128)(2,1)} custom-call(bf16[8,1024]{1,0:T(8,128)(2,1)S(1)} %copy-done.3, bf16[8,8,1024]{2,1,0:T(8,128)(2,1)S(1)} %all_to_all.11.parts_ref), custom_call_target="tpu_custom_call" | custom-call | tf_op jit(solution)/shard_map/residual/pallas_call | solution.py:522
  (5 shorter events, 0.0 us)
Async XLA Ops:
  0.0 3.2 %collective-permute-start = (bf16[8,1024]{1,0:T(8,128)(2,1)}, bf16[8,1024]{1,0:T(8,128)(2,1)S(1)}, u32[]{:S(2)}, u32[]{:S(2)}) collective-permute-start(bf16[8,1024]{1,0:T(8,128)(2,1)} %x_ref.3), channel_id=1, source_target_pairs={{0,1},{1,0},{2,3},{3,2},{4,5},{5,4},{6,7},{7,6},{8,9},{9,8},{10,11... | collective-permute-start | bytes 49160 | tf_op jit(solution)/shard_map/ppermute | solution.py:533
  0.5 2.8 %collective-permute-start.1 = (s32[8]{0:T(128)}, s32[8]{0:T(128)S(1)}, u32[]{:S(2)}, u32[]{:S(2)}) collective-permute-start(s32[8]{0:T(128)} %param.11), channel_id=1, source_target_pairs={{0,1},{1,0},{2,3},{3,2},{4,5},{5,4},{6,7},{7,6},{8,9},{9,8},{10,11... | collective-permute-start | bytes 104 | tf_op jit(solution)/shard_map/ppermute | solution.py:533
  0.5 2.7 %copy-start.3 = (bf16[8,1024]{1,0:T(8,128)(2,1)S(1)}, bf16[8,1024]{1,0:T(8,128)(2,1)}, u32[]{:S(2)}) copy-start(bf16[8,1024]{1,0:T(8,128)(2,1)} %x_ref.3) | copy-start | bytes 49156
  0.5 2.7 %copy-start.4 = (s32[8]{0:T(128)S(1)}, s32[8]{0:T(128)}, u32[]{:S(2)}) copy-start(s32[8]{0:T(128)} %param.11) | copy-start | bytes 100
  3.2 6.0 %copy-start.5 = (s32[8]{0:T(128)S(1)}, s32[8]{0:T(128)}, u32[]{:S(2)}) copy-start(s32[8]{0:T(128)} %refs_2_.3) | copy-start | bytes 100
  6.1 6.9 %collective-permute-start.2 = (f32[4,16,768]{2,1,0:T(8,128)S(1)}, f32[4,16,768]{2,1,0:T(8,128)S(1)}, u32[]{:S(2)}, u32[]{:S(2)}) collective-permute-start(f32[4,16,768]{2,1,0:T(8,128)S(1)} %get-tuple-element.29), channel_id=1, source_target_pairs={{0,2},{1,5},{2,0},{3,7},{4,6},{5,1},{6,4},{7,3},{8,10},{9,13},{10,... | collective-permute-start | bytes 589832 | tf_op jit(solution)/shard_map/ppermute | solution.py:545
  9.2 12.8 %copy-start.2 = (bf16[16,64,1024]{2,1,0:T(8,128)(2,1)S(1)}, bf16[16,64,1024]{2,1,0:T(8,128)(2,1)}, u32[]{:S(2)}) copy-start(bf16[16,64,1024]{2,1,0:T(8,128)(2,1)} %up_ref.1) | copy-start | bytes 6291460
  9.2 16.1 %copy-start = (bf16[8,256,1024]{2,1,0:T(8,128)(2,1)S(1)}, bf16[8,256,1024]{2,1,0:T(8,128)(2,1)}, u32[]{:S(2)}) copy-start(bf16[8,256,1024]{2,1,0:T(8,128)(2,1)} %refs_4_.9) | copy-start | bytes 12582916
  9.2 16.1 %copy-start.1 = (bf16[8,256,1024]{2,1,0:T(8,128)(2,1)S(1)}, bf16[8,256,1024]{2,1,0:T(8,128)(2,1)}, u32[]{:S(2)}) copy-start(bf16[8,256,1024]{2,1,0:T(8,128)(2,1)} %refs_5_.11) | copy-start | bytes 12582916
  13.1 6.1 %collective-permute-start.3 = (f32[16,768]{1,0:T(8,128)S(1)}, f32[16,768]{1,0:T(8,128)S(1)}, u32[]{:S(2)}, u32[]{:S(2)}) collective-permute-start(f32[16,768]{1,0:T(8,128)S(1)} %get-tuple-element.31), channel_id=1, source_target_pairs={{0,12},{1,11},{2,14},{3,9},{4,8},{5,15},{6,10},{7,13},{8,4},{9,3},... | collective-permute-start | bytes 147464 | tf_op jit(solution)/shard_map/ppermute | solution.py:545
  17.0 5.0 %collective-permute-start.4 = (f32[16,768]{1,0:T(8,128)S(1)}, f32[16,768]{1,0:T(8,128)S(1)}, u32[]{:S(2)}, u32[]{:S(2)}) collective-permute-start(f32[16,768]{1,0:T(8,128)S(1)} %get-tuple-element.32), channel_id=1, source_target_pairs={{0,8},{1,9},{2,10},{3,11},{4,12},{5,13},{6,14},{7,15},{8,0},{9,1},... | collective-permute-start | bytes 147464 | tf_op jit(solution)/shard_map/ppermute | solution.py:545
  17.0 5.0 %collective-permute-start.5 = (f32[16,768]{1,0:T(8,128)S(1)}, f32[16,768]{1,0:T(8,128)S(1)}, u32[]{:S(2)}, u32[]{:S(2)}) collective-permute-start(f32[16,768]{1,0:T(8,128)S(1)} %get-tuple-element.33), channel_id=1, source_target_pairs={{0,4},{1,3},{2,6},{3,1},{4,0},{5,7},{6,2},{7,5},{8,12},{9,11},{10,... | collective-permute-start | bytes 147464 | tf_op jit(solution)/shard_map/ppermute | solution.py:545
  22.4 1.2 %collective-permute-start.6 = (f32[8,1152]{1,0:T(8,128)S(1)}, f32[8,1152]{1,0:T(8,128)S(1)}, u32[]{:S(2)}, u32[]{:S(2)}) collective-permute-start(f32[8,1152]{1,0:T(8,128)S(1)} %get-tuple-element.35), channel_id=1, source_target_pairs={{0,1},{1,0},{2,3},{3,2},{4,5},{5,4},{6,7},{7,6},{8,9},{9,8},{10,11... | collective-permute-start | bytes 110600 | tf_op jit(solution)/shard_map/ppermute | solution.py:533
  23.7 3.8 %collective-permute-start.7 = (bf16[1,64,128]{2,1,0:T(8,128)(2,1)S(1)}, bf16[1,64,128]{2,1,0:T(8,128)(2,1)S(1)}, u32[]{:S(2)}, u32[]{:S(2)}) collective-permute-start(bf16[1,64,128]{2,1,0:T(8,128)(2,1)S(1)} %get-tuple-element.36.refs_3_.refs_0_.q_ref), channel_id=1, source_target_pairs={{0,2},{1,5},{2,0},{3,7},{4,6},{5,1},{6,4},{7,3},{8,10},{9,13},{10,... | collective-permute-start | bytes 49160 | tf_op jit(solution)/shard_map/ppermute | solution.py:545
  27.5 4.8 %collective-permute-start.10 = (bf16[2,64,128]{2,1,0:T(8,128)(2,1)S(1)}, bf16[2,64,128]{2,1,0:T(8,128)(2,1)S(1)}, u32[]{:S(2)}, u32[]{:S(2)}) collective-permute-start(bf16[2,64,128]{2,1,0:T(8,128)(2,1)S(1)} %join.1), channel_id=1, source_target_pairs={{0,8},{1,9},{2,10},{3,11},{4,12},{5,13},{6,14},{7,15},{8,0},{9,1},... | collective-permute-start | bytes 98312 | tf_op jit(solution)/shard_map/ppermute | solution.py:545
  29.5 5.7 %collective-permute-start.9 = (bf16[2,64,128]{2,1,0:T(8,128)(2,1)S(1)}, bf16[2,64,128]{2,1,0:T(8,128)(2,1)S(1)}, u32[]{:S(2)}, u32[]{:S(2)}) collective-permute-start(bf16[2,64,128]{2,1,0:T(8,128)(2,1)S(1)} %join.1), channel_id=1, source_target_pairs={{0,12},{1,11},{2,14},{3,9},{4,8},{5,15},{6,10},{7,13},{8,4},{9,3},... | collective-permute-start | bytes 98312 | tf_op jit(solution)/shard_map/ppermute | solution.py:545
  30.1 6.0 %collective-permute-start.8 = (bf16[2,64,128]{2,1,0:T(8,128)(2,1)S(1)}, bf16[2,64,128]{2,1,0:T(8,128)(2,1)S(1)}, u32[]{:S(2)}, u32[]{:S(2)}) collective-permute-start(bf16[2,64,128]{2,1,0:T(8,128)(2,1)S(1)} %join.1), channel_id=1, source_target_pairs={{0,4},{1,3},{2,6},{3,1},{4,0},{5,7},{6,2},{7,5},{8,12},{9,11},{10,... | collective-permute-start | bytes 98312 | tf_op jit(solution)/shard_map/ppermute | solution.py:545
  31.0 17.4 %slice-start = ((s8[16777216]{0:T(1024)(128)(4,1)}), s8[4194304]{0:T(1024)(128)(4,1)S(1)}, s32[]{:S(2)}) async-start(s8[16777216]{0:T(1024)(128)(4,1)} %bitcast.5), calls=%async_computation.2 | async-start | bytes 8388608
  31.5 16.9 %slice-start.1 = ((s8[16777216]{0:T(1024)(128)(4,1)}), s8[4194304]{0:T(1024)(128)(4,1)S(1)}, s32[]{:S(2)}) async-start(s8[16777216]{0:T(1024)(128)(4,1)} %bitcast.5), calls=%async_computation.3 | async-start | bytes 8388608
  33.2 15.2 %slice-start.2 = ((s8[16777216]{0:T(1024)(128)(4,1)}), s8[4194304]{0:T(1024)(128)(4,1)S(1)}, s32[]{:S(2)}) async-start(s8[16777216]{0:T(1024)(128)(4,1)} %bitcast.5), calls=%async_computation.4 | async-start | bytes 8388608
  36.1 12.3 %slice-start.3 = ((s8[16777216]{0:T(1024)(128)(4,1)}), s8[4194304]{0:T(1024)(128)(4,1)S(1)}, s32[]{:S(2)}) async-start(s8[16777216]{0:T(1024)(128)(4,1)} %bitcast.5), calls=%async_computation.5 | async-start | bytes 8388608

commit v15 on v12

--- a/solution.py
+++ b/solution.py
@@ -66,68 +66,66 @@
 
 
 def adapter_column(refs, bank, count):
-    rows = len(refs) * refs[0].shape[0]
-    row = iota((rows, HEAD_DIM), 0)
-    column = jnp.zeros((rows, HEAD_DIM), jnp.int32)
-    for r in range(rows):
-        ref = refs[r // refs[0].shape[0]]
-        column = jnp.where(row == r, ref[r % ref.shape[0]], column)
-    return column - bank * count
-
-
-def start_slots(parity, ranks, place, bank, w_ref, kv_ref, w_buf, kv_buf, sems, kv_sems):
+    columns = []
+    for ref in refs:
+        rows = ref.shape[1]
+        index = jnp.broadcast_to(ref[...].astype(F32), (rows, rows))
+        diagonal = iota((rows, rows), 0) == iota((rows, rows), 1)
+        columns.append(jnp.sum(jnp.where(diagonal, index, 0.0), axis=1, keepdims=True))
+    column = jnp.concatenate(columns, axis=0).astype(jnp.int32) - bank * count
+    return jnp.broadcast_to(column, (column.shape[0], HEAD_DIM))
+
+
+def start_slots(parity, place, bank, w_ref, w_buf, sems):
     count, _, width = w_buf.shape
     copies = []
     for s in range(count):
         target = rank_of(place[0], bank[0], 2 * s + parity)
-        copies.append(
-            start_columns(w_ref, (2 * target + bank[0]) * width, w_buf.at[s], sems.at[s])
-            + start_columns(
-                kv_ref, (target + ranks * bank[0]) * HEAD_DIM, kv_buf.at[s], kv_sems.at[s]
-            )
-        )
+        first = (2 * target + bank[0]) * width
+        copies.append(start_columns(w_ref, first, w_buf.at[s], sems.at[s]))
     return copies
 
 
 def wait_all(copies):
-    for slot in copies:
-        for copy in slot:
-            copy.wait()
-
-
-def fetch_kernel(ranks, place, bank, w_ref, kv_ref, down_ref, w_buf, kv_buf, down_buf, *sems):
-    down_copy = pltpu.make_async_copy(down_ref, down_buf, sems[2])
-    down_copy.start()
-    wait_all(start_slots(1, ranks, place, bank, w_ref, kv_ref, w_buf, kv_buf, *sems[:2]))
-    down_copy.wait()
-
-
-def slot_buffers(wq, ranks):
-    count, depth = ranks // 2, wq.shape[0]
+    for copy in copies:
+        copy.wait()
+
+
+def start_parts(source, target, sems):
+    part = source.shape[0] // sems.shape[0]
+    copies = []
+    for c in range(sems.shape[0]):
+        rows = pl.ds(c * part, part)
+        copies.append(pltpu.make_async_copy(source.at[rows], target.at[rows], sems.at[c]))
+        copies[-1].start()
+    return copies
+
+
+def fetch_kernel(ref, out, sems):
+    wait_all(start_parts(ref, out, sems))
+
+
+def fetch(array):
+    return pl.pallas_call(
+        fetch_kernel,
+        in_specs=[big()],
+        out_specs=whole(),
+        out_shape=jax.ShapeDtypeStruct(array.shape, array.dtype),
+        scratch_shapes=[pltpu.SemaphoreType.DMA((2,))],
+        compiler_params=params(),
+        cost_estimate=pl.CostEstimate(
+            flops=0, bytes_accessed=2 * array.size, transcendentals=0
+        ),
+        name="fetch",
+    )(array)
+
+
+def slot_scratch(wq, ranks):
+    half, depth = ranks // 2, wq.shape[0]
     return [
-        shape(count, depth, wq.shape[1] // ranks // 2, dtype=BF16),
-        shape(count, depth, HEAD_DIM, dtype=BF16),
+        pltpu.VMEM((half, depth, wq.shape[1] // ranks // 2), BF16),
+        pltpu.SemaphoreType.DMA((half, CHUNKS)),
     ]
-
-
-def slot_sems(count):
-    return [pltpu.SemaphoreType.DMA((count, CHUNKS))] * 2
-
-
-def fetch(place, bank, wq, wkv, down, ranks):
-    out = slot_buffers(wq, ranks) + [jax.ShapeDtypeStruct(down.shape, BF16)]
-    return pl.pallas_call(
-        lambda *refs: fetch_kernel(ranks, *refs),
-        in_specs=[scalar()] * 2 + [big()] * 3,
-        out_specs=[whole()] * 3,
-        out_shape=out,
-        scratch_shapes=slot_sems(ranks // 2) + [pltpu.SemaphoreType.DMA(())],
-        compiler_params=params(),
-        cost_estimate=pl.CostEstimate(
-            flops=0, bytes_accessed=2 * sum(o.size for o in out), transcendentals=0
-        ),
-        name="fetch",
-    )(place, bank, wq, wkv, down)
 
 
 def beam_rows(x_ref, other_ref):
@@ -135,36 +133,21 @@
     return jnp.concatenate(rows, axis=0).astype(BF16)
 
 
-def project_slot(x, w, kv, out):
-    width = w.shape[1]
-    out[:, :width] = jnp.dot(x, w[...], preferred_element_type=F32)
-    out[:, width : width + HEAD_DIM] = jnp.dot(x, kv[...], preferred_element_type=F32)
-
-
 def project_sent_kernel(
-    bank, own_ref, came_ref, x_ref, other_ref, w_buf, kv_buf, down_buf, *refs
+    place, bank, own_ref, came_ref, x_ref, other_ref, down_ref, w_ref, *refs
 ):
-    out, inner, column_out, *index, sems = refs
-    copies = [
-        pltpu.make_async_copy(ref, held, sems.at[n])
-        for n, (ref, held) in enumerate(zip((own_ref, came_ref), index))
-    ]
-    for copy in copies:
-        copy.start()
+    out, inner, column_out, w_buf, sems = refs
+    copies = start_slots(1, place, bank, w_ref, w_buf, sems)
     width = w_buf.shape[2]
     x = beam_rows(x_ref, other_ref)
-    for s in range(out.shape[0]):
-        project_slot(x, w_buf.at[s], kv_buf.at[s], out.at[s])
-    adapters, rank, depth = down_buf.shape
+    adapters, rank, depth = down_ref.shape
     every = lax.dot_general(
         x,
-        down_buf[...].reshape(adapters * rank, depth),
+        down_ref[...].reshape(adapters * rank, depth),
         (((1,), (1,)), ((), ())),
         preferred_element_type=F32,
     )
-    for copy in copies:
-        copy.wait()
-    column = adapter_column(index, bank[0], adapters)
+    column = adapter_column((own_ref, came_ref), bank[0], adapters)
     column_out[...] = column
     lane = iota(column.shape, 1)
     per = HEAD_DIM // rank
@@ -173,75 +156,105 @@
         part = every[:, j * HEAD_DIM : (j + 1) * HEAD_DIM]
         total += jnp.where(lane // rank + j * per == column, part, 0.0)
     inner[...] = total
-    for s in range(out.shape[0]):
-        out[s, :, width + HEAD_DIM :] = total
-
-
-def project_sent(bank, index, x, other, weights):
-    half, _, width = weights[0].shape
+    for s, slot in enumerate(copies):
+        out[s, :, width:] = total
+        wait_all(slot)
+        out[s, :, :width] = jnp.dot(x, w_buf[s], preferred_element_type=F32)
+
+
+def project_sent(place, bank, index, x, other, down, wq, ranks):
     rows = 2 * x.shape[0]
     return pl.pallas_call(
         project_sent_kernel,
-        in_specs=[scalar(), big(), pl.BlockSpec(memory_space=pl.ANY)] + [whole()] * 5,
+        in_specs=[scalar()] * 2 + [whole()] * 5 + [big()],
         out_specs=[whole()] * 3,
         out_shape=[
-            shape(half, rows, width + 2 * HEAD_DIM),
+            shape(ranks // 2, rows, wq.shape[1] // ranks // 2 + HEAD_DIM),
             shape(rows, HEAD_DIM),
             shape(rows, HEAD_DIM, dtype=jnp.int32),
         ],
-        scratch_shapes=[pltpu.SMEM(index[0].shape, jnp.int32)] * 2
-        + [pltpu.SemaphoreType.DMA((2,))],
-        compiler_params=params(),
+        scratch_shapes=slot_scratch(wq, ranks),
+        compiler_params=params(8),
         cost_estimate=pl.CostEstimate(
-            flops=2 * rows * sum(w.size for w in weights),
-            bytes_accessed=2 * sum(w.size for w in weights),
+            flops=rows * (wq.size // 2 + 2 * down.size),
+            bytes_accessed=wq.size // 2 + 2 * down.size,
             transcendentals=0,
         ),
         name="project_sent",
-    )(bank, in_hbm(index[0]), index[1], x, other, *weights)
+    )(place, bank, *[i.reshape(1, -1) for i in index], x, other, down, wq)
 
 
 def project_kept_kernel(
-    ranks, place, bank, length, x_ref, other_ref, w_ref, kv_ref, inner, out, live, *scratch
+    place, bank, length, x_ref, other_ref, w_ref, inner, out, length_out, w_buf, sems
 ):
-    w_buf, kv_buf = scratch[:2]
-    copies = start_slots(0, ranks, place, bank, w_ref, kv_ref, *scratch)
+    copies = start_slots(0, place, bank, w_ref, w_buf, sems)
     width = w_buf.shape[2]
     beams = x_ref.shape[0]
-    row = iota(live.shape, 0)
-    limit = jnp.zeros(live.shape, jnp.int32)
+    row = iota(length_out.shape, 0)
+    limit = jnp.zeros(length_out.shape, jnp.int32)
     for beam in range(beams):
-        limit = jnp.where(row // (live.shape[0] // beams) == beam, length[beam], limit)
-    live[...] = limit
+        limit = jnp.where(row // (length_out.shape[0] // beams) == beam, length[beam], limit)
+    length_out[...] = limit
     x = beam_rows(x_ref, other_ref)
     for s, slot in enumerate(copies):
-        wait_all([slot])
-        project_slot(x, w_buf.at[s], kv_buf.at[s], out.at[s])
-        out[s, :, width + HEAD_DIM :] = inner[...]
-
-
-def project_kept(place, bank, length, x, other, wq, wkv, inner, ranks):
-    beams, depth = x.shape
-    rows = 2 * beams
-    half = ranks // 2
-    buffers = slot_buffers(wq, ranks)
-    return pl.pallas_call(
-        lambda *refs: project_kept_kernel(ranks, *refs),
-        in_specs=[scalar()] * 3 + [whole()] * 2 + [big()] * 2 + [whole()],
+        out[s, :, width:] = inner[...]
+        wait_all(slot)
+        out[s, :, :width] = jnp.dot(x, w_buf[s], preferred_element_type=F32)
+
+
+def project_kept(place, bank, length, x, other, wq, inner, ranks):
+    beams = x.shape[0]
+    return pl.pallas_call(
+        project_kept_kernel,
+        in_specs=[scalar()] * 3 + [whole()] * 2 + [big(), whole()],
         out_specs=[whole()] * 2,
         out_shape=[
-            shape(half, rows, buffers[0].shape[2] + 2 * HEAD_DIM),
+            shape(ranks // 2, 2 * beams, wq.shape[1] // ranks // 2 + HEAD_DIM),
             shape(beams * wq.shape[1] // ranks // HEAD_DIM, HEAD_DIM, dtype=jnp.int32),
         ],
-        scratch_shapes=[pltpu.VMEM(b.shape, BF16) for b in buffers] + slot_sems(half),
+        scratch_shapes=slot_scratch(wq, ranks),
         compiler_params=params(8),
         cost_estimate=pl.CostEstimate(
-            flops=rows * depth * (wq.shape[1] + wkv.shape[1]) // 2,
-            bytes_accessed=wq.size + wkv.size,
-            transcendentals=0,
+            flops=beams * wq.size, bytes_accessed=2 * wq.size, transcendentals=0
         ),
         name="project_kept",
-    )(place, bank, length, x, other, wq, wkv, inner)
+    )(place, bank, length, x, other, wq, inner)
+
+
+def keyval_kernel(x_ref, w_ref, out, w_buf, sems):
+    copies = start_parts(w_ref, w_buf, sems)
+    beams = x_ref.shape[0]
+    ranks = out.shape[0]
+    part = w_buf.shape[0] // len(copies)
+    total = None
+    for c, copy in enumerate(copies):
+        copy.wait()
+        rows = slice(c * part, (c + 1) * part)
+        product = jnp.dot(x_ref[:, rows], w_buf[rows], preferred_element_type=F32)
+        total = product if total is None else total + product
+    high = total.astype(BF16).astype(F32)
+    low = total - high
+    for r in range(ranks):
+        pieces = []
+        for first in (r * HEAD_DIM, (ranks + r) * HEAD_DIM):
+            pieces += [v[:, first : first + HEAD_DIM] for v in (high, low)]
+        out[r] = jnp.concatenate(pieces, axis=0).astype(BF16)
+
+
+def keyval(x, wkv, ranks):
+    beams, depth = x.shape
+    return pl.pallas_call(
+        keyval_kernel,
+        in_specs=[whole(), big()],
+        out_specs=whole(),
+        out_shape=shape(ranks, 4 * beams, HEAD_DIM, dtype=BF16),
+        scratch_shapes=[pltpu.VMEM(wkv.shape, BF16), pltpu.SemaphoreType.DMA((4,))],
+        compiler_params=params(8),
+        cost_estimate=pl.CostEstimate(
+            flops=2 * beams * wkv.size, bytes_accessed=2 * wkv.size, transcendentals=0
+        ),
+        name="keyval",
+    )(x, wkv)
 
 
 def correct_kernel(bank, column_ref, up_ref, *refs):
@@ -251,7 +264,7 @@
         total += part[...]
     count, rank, width = up_ref.shape
     half = width // 2
-    inner = total[:, half + HEAD_DIM :].astype(BF16).astype(F32)
+    inner = total[:, half:].astype(BF16).astype(F32)
     column = column_ref[...]
     lane = iota(column.shape, 1)
     per = HEAD_DIM // rank
@@ -271,13 +284,11 @@
         part = delta[:, columns] + jnp.where(bank[0] == side, total[:, :half], 0.0)
         own_out[:, columns] = part[:rows]
         other_out[:, columns] = part[rows:]
-    own_out[:, width:] = total[:rows, half : half + HEAD_DIM]
-    other_out[:, width:] = total[rows:, half : half + HEAD_DIM]
 
 
 def correct(bank, column, up, parts):
     rows = parts[0].shape[0]
-    out = shape(rows // 2, up.shape[2] + HEAD_DIM)
+    out = shape(rows // 2, up.shape[2])
     return pl.pallas_call(
         correct_kernel,
         in_specs=[scalar()] + [whole()] * (2 + len(parts)),
@@ -311,36 +322,26 @@
     return v * cosine + pltpu.roll(v, HEAD_DIM // 2, 1) * sine
 
 
-def rotate_kernel(bank, own_ref, came_ref, cos_ref, sin_ref, q_ref, k_ref, v_ref, rows_ref):
-    width = own_ref.shape[1] - HEAD_DIM
+def rotate_kernel(own_ref, came_ref, cos_ref, sin_ref, q_ref, rows_ref):
     cosine, sine = cos_ref[...], sin_ref[...]
-    for g in range(width // HEAD_DIM):
+    for g in range(own_ref.shape[1] // HEAD_DIM):
         columns = slice(g * HEAD_DIM, (g + 1) * HEAD_DIM)
         rows_ref[:, g, :] = rotate(own_ref[:, columns] + came_ref[:, columns], cosine, sine)
     q_ref[0] = rows_ref[...].reshape(q_ref.shape[1:]).astype(BF16)
-    own, came = own_ref[:, width:], came_ref[:, width:]
-    key = jnp.where(bank[0] == 0, own, came)
-    value = jnp.where(bank[0] == 0, came, own)
-    k_ref[...] = rotate(key, cosine, sine).astype(BF16).astype(F32)
-    v_ref[...] = value.astype(BF16).astype(F32)
-
-
-def rotated(bank, own, came, cosine, sine):
-    rows = own.shape[0]
-    heads = own.shape[1] // HEAD_DIM - 1
+
+
+def rotated(own, came, cosine, sine):
+    rows, width = own.shape
+    heads = width // HEAD_DIM
     return pl.pallas_call(
         rotate_kernel,
-        in_specs=[scalar()] + [whole()] * 4,
-        out_specs=[whole()] * 3,
-        out_shape=[
-            shape(1, rows * heads, HEAD_DIM, dtype=BF16),
-            shape(rows, HEAD_DIM),
-            shape(rows, HEAD_DIM),
-        ],
+        in_specs=[whole()] * 4,
+        out_specs=whole(),
+        out_shape=shape(1, rows * heads, HEAD_DIM, dtype=BF16),
         scratch_shapes=[pltpu.VMEM((rows, heads, HEAD_DIM), F32)],
         compiler_params=params(),
         name="rotate",
-    )(bank, own, came, cosine, sine)
+    )(own, came, cosine, sine)
 
 
 def join_kernel(*refs):
@@ -406,11 +407,13 @@
         low = stats - high - middle
         tail = high + pltpu.roll(middle, 2 * group, 1) + pltpu.roll(low, 4 * group, 1)
         block = jnp.concatenate(values + [tail, jnp.zeros_like(tail)], axis=0)
-        out_ref[head if earlier else i] = block.astype(BF16)
+        out_ref[head if earlier else i, : rows + 2 * beams] = block.astype(BF16)
     if earlier:
+        *before, keyval_ref = before
         done = [(ref, i) for ref in before for i in range(ref.shape[0])]
         for slot, (ref, i) in zip(earlier, done):
-            out_ref[rank_of(place[0], bank[0], slot)] = ref[i]
+            out_ref[rank_of(place[0], bank[0], slot), : rows + 2 * beams] = ref[i]
+        out_ref[:, rows + 2 * beams :] = keyval_ref[...]
 
 
 def attend(place, bank, length, queries, keys, values, slots, earlier=(), before=()):
@@ -420,7 +423,9 @@
         lambda *refs: attend_kernel(slots, earlier, *refs),
         in_specs=[scalar()] * 2 + [whole()] * (4 + len(before)),
         out_specs=whole(),
-        out_shape=shape(count + len(earlier), rows + 2 * beams, HEAD_DIM, dtype=BF16),
+        out_shape=shape(
+            count + len(earlier), rows + (6 if earlier else 2) * beams, HEAD_DIM, dtype=BF16
+        ),
         compiler_params=params(),
         cost_estimate=pl.CostEstimate(
             flops=4 * rows * count * positions * HEAD_DIM,
@@ -431,7 +436,7 @@
     )(place, bank, length, queries, keys, values, *before)
 
 
-def combine_kernel(parts_ref, q_ref, k_ref, v_ref, out_ref, joined):
+def combine_kernel(parts_ref, q_ref, cos_ref, sin_ref, out_ref, joined):
     ranks = parts_ref.shape[0]
     beams, group, _ = joined.shape
     rows = beams * group
@@ -441,7 +446,14 @@
 
     head = iota((rows, HEAD_DIM), 0) % group
     lane = iota((rows, HEAD_DIM), 1)
-    score = jnp.sum(q_ref[0].astype(F32) * by_row(k_ref[...]), axis=1, keepdims=True) * (
+    sums = jnp.sum(parts_ref[:, rows + 2 * beams :].astype(F32), axis=0)
+    key, value = [
+        sums[i * beams : (i + 1) * beams] + sums[(i + 1) * beams : (i + 2) * beams]
+        for i in (0, 2)
+    ]
+    key = rotate(key, cos_ref[...], sin_ref[...]).astype(BF16).astype(F32)
+    value = value.astype(BF16).astype(F32)
+    score = jnp.sum(q_ref[0].astype(F32) * by_row(key), axis=1, keepdims=True) * (
         1.0 / HEAD_DIM**0.5
     )
     peaks, totals, weighted = [], [], []
@@ -460,7 +472,7 @@
         weighted.append(block[:rows])
     new = jnp.exp(score - top)
     everything = new
-    result = new.astype(BF16).astype(F32) * by_row(v_ref[...])
+    result = new.astype(BF16).astype(F32) * by_row(value)
     for peak, total, block in zip(peaks, totals, weighted):
         factor = jnp.exp(peak - top)
         everything += total * factor
@@ -470,8 +482,8 @@
         out_ref[:, g * HEAD_DIM : (g + 1) * HEAD_DIM] = joined[:, g, :].astype(BF16)
 
 
-def combine(parts, query, key_new, value_new):
-    beams = key_new.shape[0]
+def combine(parts, query, cosine, sine):
+    beams = cosine.shape[0]
     group = query.shape[1] // beams
     return pl.pallas_call(
         combine_kernel,
@@ -481,7 +493,7 @@
         scratch_shapes=[pltpu.VMEM((beams, group, HEAD_DIM), F32)],
         compiler_params=params(),
         name="combine",
-    )(parts, query, key_new, value_new)
+    )(parts, query, cosine, sine)
 
 
 def output_kernel(x_ref, w_ref, out):
@@ -563,19 +575,20 @@
     angles = beam_cache_length.astype(F32)[:, None] * frequency[None, :]
     cosine = jnp.cos(angles)
     sine = jnp.where(lane < half, -1.0, 1.0) * jnp.sin(angles)
-    weights = in_hbm(query_weight), in_hbm(keyvalue_weight)
-    down = in_hbm(lowrank_down_factors.swapaxes(1, 2))
-    ahead = fetch(place, bank, *weights, down, ranks)
-    sent, inner, column = project_sent(bank, index, x, x_other, ahead)
+    weight = in_hbm(query_weight)
+    down = fetch(in_hbm(lowrank_down_factors.swapaxes(1, 2)))
+    sent, inner, column = project_sent(place, bank, index, x, x_other, down, weight, ranks)
     came = hop(sent, 1)
     kept, length = project_kept(
-        place, bank, beam_cache_length, x, x_other, *weights, inner, ranks
+        place, bank, beam_cache_length, x, x_other, weight, inner, ranks
     )
     kept, *sent = part(kept, came)
     near = tuple(range(ranks - 2, 0, -2))
     parts = [kept] + [hop(sent[slot // 2 - 1], slot) for slot in near]
+    token_weight, _ = lax.optimization_barrier((in_hbm(keyvalue_weight), kept))
+    token, parts = lax.optimization_barrier((keyval(x, in_hbm(token_weight), ranks), parts))
     own, other = correct(bank, column, lowrank_up_factors, parts)
-    query, key_new, value_new = rotated(bank, own, swapped(other), cosine, sine)
+    query = rotated(own, swapped(other), cosine, sine)
 
     def attended_part(queries, slots, **more):
         cache = paged_key_cache, paged_value_cache
@@ -585,8 +598,8 @@
     came = hop(gathered, 1)
     done = attended_part(gathered, (0, *near))
     odd = tuple(slot + 1 for slot in (0, *near))
-    partial = attended_part(came, odd, earlier=(0, *near), before=(done,))
-    attended = combine(traded(partial), query, key_new, value_new)
+    partial = attended_part(came, odd, earlier=(0, *near), before=(done, token))
+    attended = combine(traded(partial), query, cosine, sine)
     return residual(x, traded(output(attended, output_weight, ranks)))
 
 

time: 60.9 us -> 60.6 us (level)
  waiting for transfers between devices: 10.1 us -> 6.77 us
  Pallas kernels: 16 us -> 17.5 us
  blocking collectives: 20.8 us -> 21.6 us
    ppermute x8, waiting for transfers between devices: 9.02 us -> 5.67 us  [hop(): return lax.ppermute(x, ('tensor', 'bank'), pairs)]
    pallas_call x4 -> x5, Pallas kernels: 9.04 us -> 10.6 us  [the longest x1 3.3 us: project_kept(): pl.pallas_call(project_kept_kernel, in_specs=[scalar()] * 3 + [whole()] *...]
    all_to_all x2, blocking collectives: 20.8 us -> 21.6 us  [traded(): return lax.all_to_all(blocks, 'tensor', 0, 0, tiled=True)]
  transfers between devices with their start and end apart: 11 -> 11, of which waited for: 6 -> 5; matrix products, arithmetic and copies ran while one was open for 0% -> 0% of each run, Pallas kernels for 14% -> 15%
where the time goes in v15:
time: 60.6 us; the launch traced here: 60.4 us
  blocking collectives  21.6 us (36%)
  Pallas kernels  17.5 us (29%)
  starting transfers between devices  14.1 us (23%)
  waiting for transfers between devices  6.77 us (11%)
    all_to_all x2, blocking collectives, traded(): return lax.all_to_all(blocks, 'tensor', 0, 0, tiled=True)  21.6 us
    ppermute x8, starting transfers between devices, hop(): return lax.ppermute(x, ('tensor', 'bank'), pairs)  13.6 us
    ppermute x8, waiting for transfers between devices, hop(): return lax.ppermute(x, ('tensor', 'bank'), pairs)  5.67 us
    pallas_call x1, Pallas kernels, project_kept(): pl.pallas_call(project_kept_kernel, in_specs=[scalar()] * 3 + [whole()] *...  3.3 us
    pallas_call x2, Pallas kernels, attend(): pl.pallas_call(lambda *refs: attend_kernel(slots, earlier, *refs), in_spe...  3.13 us
    pallas_call x1, Pallas kernels, project_sent(): pl.pallas_call(project_sent_kernel, in_specs=[scalar()] * 2 + [whole()] *...  3.01 us
    pallas_call x1, Pallas kernels, keyval(): pl.pallas_call(keyval_kernel, in_specs=[whole(), big()], out_specs=whole(...  2.61 us
    pallas_call x1, Pallas kernels, output(): pl.pallas_call(output_kernel, in_specs=[whole()] * 2, out_specs=whole(),...  2.28 us
  transfers between devices with their start and end apart: 11, of which 5 were waited for; matrix products, arithmetic and copies ran while one was open for 0% of the time, Pallas kernels for 15%

profile of v15, /device:TPU:0, one launch (start us, length us, event | category | flops | bytes accessed | tf_op | source)
XLA Modules:
  0.0 60.4 jit_solution(11852609410547426941)
XLA Ops:
  0.0 0.0 copy-start.3
  0.0 0.0 copy-start.4
  0.0 0.5 collective-permute-start
  0.5 0.1 collective-permute-start.1
  0.5 1.6 %fetch.1.down_ref = bf16[16,64,1024]{2,1,0:T(8,128)(2,1)S(1)} custom-call(bf16[16,64,1024]{2,1,0:T(8,128)(2,1)} %bitcast.9), custom_call_target="tpu_custom_call" | custom-call | bytes 2097152 | tf_op jit(solution)/shard_map/fetch/pallas_call | solution.py:109
  2.1 0.0 collective-permute-done.1
  2.1 0.0 collective-permute-done.other_ref
  2.1 0.0 copy-done.3
  2.1 0.0 copy-done.4
  2.1 0.0 copy-start.5
  2.1 3.0 %project_sent.1 = (f32[4,16,640]{2,1,0:T(8,128)S(1)}, f32[16,128]{1,0:T(8,128)S(1)}, s32[16,128]{1,0:T(8,128)S(1)}) custom-call(s32[1]{0:T(128)} %bitcast.place.refs_0_, s32[1]{0:T(128)} %bitcast.1.bank.refs_1_, s32[1,8]{1,0:T(1,128)S(1)} %bitcast.7, s32[1,8]{1,0:T(1,128)S(1)} %bitcast.8, bf16[8,1024]{1,0:T(8,128)(2,1)S(1)} %copy-done.3, ...), custom_call_target="tpu_custom_call" | custom-call | flops 100663296 | bytes 6291456 | tf_op jit(solution)/shard_map/project_sent/pallas_call | solution.py:167
  5.2 3.0 %collective-permute-start.2 = (f32[4,16,640]{2,1,0:T(8,128)S(1)}, f32[4,16,640]{2,1,0:T(8,128)S(1)}, u32[]{:S(2)}, u32[]{:S(2)}) collective-permute-start(f32[4,16,640]{2,1,0:T(8,128)S(1)} %get-tuple-element.26), channel_id=1, source_target_pairs={{0,2},{1,5},{2,0},{3,7},{4,6},{5,1},{6,4},{7,3},{8,10},{9,13},{10,... | collective-permute-start | bytes 491528 | tf_op jit(solution)/shard_map/ppermute | solution.py:551
  8.2 0.0 copy-done.5
  8.2 0.0 copy-start.2
  8.2 0.0 copy-start.1
  8.2 0.0 slice-start
  8.2 0.0 slice-start.1
  8.2 3.3 %project_kept.1 = (f32[4,16,640]{2,1,0:T(8,128)S(1)}, s32[64,128]{1,0:T(8,128)S(1)}) custom-call(s32[1]{0:T(128)} %bitcast.place.refs_0_, s32[1]{0:T(128)} %bitcast.1.bank.refs_1_, s32[8]{0:T(128)S(1)} %copy-done.5, bf16[8,1024]{1,0:T(8,128)(2,1)S(1)} %copy-done.3, bf16[8,1024]{1,0:T(8,128)(2,1)S(1)} %collective-permute-done.other_ref, ...), custom_call_target="tpu_custom_call" | custom-call | flops 67108864 | bytes 16777216 | tf_op jit(solution)/shard_map/project_kept/pallas_call | solution.py:207
  11.5 0.0 copy-start
  11.5 0.0 collective-permute-done.2.came_ref
  11.6 4.1 %collective-permute-start.3 = (f32[16,640]{1,0:T(8,128)S(1)}, f32[16,640]{1,0:T(8,128)S(1)}, u32[]{:S(2)}, u32[]{:S(2)}) collective-permute-start(f32[16,640]{1,0:T(8,128)S(1)} %get-tuple-element.29), channel_id=1, source_target_pairs={{0,12},{1,11},{2,14},{3,9},{4,8},{5,15},{6,10},{7,13},{8,4},{9,3},... | collective-permute-start | bytes 122888 | tf_op jit(solution)/shard_map/ppermute | solution.py:551
  15.7 0.0 collective-permute-start.4
  15.7 0.6 %collective-permute-start.5 = (f32[16,640]{1,0:T(8,128)S(1)}, f32[16,640]{1,0:T(8,128)S(1)}, u32[]{:S(2)}, u32[]{:S(2)}) collective-permute-start(f32[16,640]{1,0:T(8,128)S(1)} %get-tuple-element.31), channel_id=1, source_target_pairs={{0,4},{1,3},{2,6},{3,1},{4,0},{5,7},{6,2},{7,5},{8,12},{9,11},{10,... | collective-permute-start | bytes 122888 | tf_op jit(solution)/shard_map/ppermute | solution.py:551
  16.3 0.0 slice-start.2
  16.3 2.6 %keyval.1.refs_7_ = bf16[8,32,128]{2,1,0:T(8,128)(2,1)S(1)} custom-call(bf16[8,1024]{1,0:T(8,128)(2,1)S(1)} %copy-done.3, bf16[1024,2048]{1,0:T(8,128)(2,1)} %w_ref.5), custom_call_target="tpu_custom_call" | custom-call | flops 33554432 | bytes 4194304 | tf_op jit(solution)/shard_map/keyval/pallas_call | solution.py:246
  19.0 0.0 collective-permute-done.3.refs_1_
  19.0 1.6 %collective-permute-done.4.refs_2_ = f32[16,640]{1,0:T(8,128)S(1)} collective-permute-done((f32[16,640]{1,0:T(8,128)S(1)}, f32[16,640]{1,0:T(8,128)S(1)}, u32[]{:S(2)}, u32[]{:S(2)}) %collective-permute-start.4) | collective-permute-done | bytes 40992 | tf_op jit(solution)/shard_map/ppermute | solution.py:551
  20.6 0.0 collective-permute-done.5.refs_3_
  20.6 0.0 copy-done.2
  20.6 0.4 correct.1
  21.0 0.0 collective-permute-start.6
  21.0 0.1 fusion
  21.1 1.1 %collective-permute-done.6.came_ref = f32[8,1024]{1,0:T(8,128)S(1)} collective-permute-done((f32[8,1024]{1,0:T(8,128)S(1)}, f32[8,1024]{1,0:T(8,128)S(1)}, u32[]{:S(2)}, u32[]{:S(2)}) %collective-permute-start.6) | collective-permute-done | bytes 32800 | tf_op jit(solution)/shard_map/ppermute | solution.py:539
  22.2 0.1 rotate.1.refs_0_.q_ref
  22.3 2.2 %collective-permute-start.7 = (bf16[1,64,128]{2,1,0:T(8,128)(2,1)S(1)}, bf16[1,64,128]{2,1,0:T(8,128)(2,1)S(1)}, u32[]{:S(2)}, u32[]{:S(2)}) collective-permute-start(bf16[1,64,128]{2,1,0:T(8,128)(2,1)S(1)} %rotate.1.refs_0_.q_ref), channel_id=1, source_target_pairs={{0,12},{1,11},{2,14},{3,9},{4,8},{5,15},{6,10},{7,13},{8,4},{9,3},... | collective-permute-start | bytes 49160 | tf_op jit(solution)/shard_map/ppermute | solution.py:551
  24.5 0.0 collective-permute-start.8
  24.5 2.2 %collective-permute-start.9 = (bf16[1,64,128]{2,1,0:T(8,128)(2,1)S(1)}, bf16[1,64,128]{2,1,0:T(8,128)(2,1)S(1)}, u32[]{:S(2)}, u32[]{:S(2)}) collective-permute-start(bf16[1,64,128]{2,1,0:T(8,128)(2,1)S(1)} %rotate.1.refs_0_.q_ref), channel_id=1, source_target_pairs={{0,4},{1,3},{2,6},{3,1},{4,0},{5,7},{6,2},{7,5},{8,12},{9,11},{10,... | collective-permute-start | bytes 49160 | tf_op jit(solution)/shard_map/ppermute | solution.py:551
  26.7 1.1 %collective-permute-done.7.refs_1_ = bf16[1,64,128]{2,1,0:T(8,128)(2,1)S(1)} collective-permute-done((bf16[1,64,128]{2,1,0:T(8,128)(2,1)S(1)}, bf16[1,64,128]{2,1,0:T(8,128)(2,1)S(1)}, u32[]{:S(2)}, u32[]{:S(2)}) %collective-permute-start.7) | collective-permute-done | bytes 16416 | tf_op jit(solution)/shard_map/ppermute | solution.py:551
  27.9 1.5 %collective-permute-done.8.refs_2_ = bf16[1,64,128]{2,1,0:T(8,128)(2,1)S(1)} collective-permute-done((bf16[1,64,128]{2,1,0:T(8,128)(2,1)S(1)}, bf16[1,64,128]{2,1,0:T(8,128)(2,1)S(1)}, u32[]{:S(2)}, u32[]{:S(2)}) %collective-permute-start.8) | collective-permute-done | bytes 16416 | tf_op jit(solution)/shard_map/ppermute | solution.py:551
  29.4 0.0 collective-permute-done.9.refs_3_
  29.4 1.4 %collective-permute-start.10 = (bf16[4,64,128]{2,1,0:T(8,128)(2,1)S(1)}, bf16[4,64,128]{2,1,0:T(8,128)(2,1)S(1)}, u32[]{:S(2)}, u32[]{:S(2)}) collective-permute-start(bf16[4,64,128]{2,1,0:T(8,128)(2,1)S(1)} %join.1.refs_3_), channel_id=1, source_target_pairs={{0,2},{1,5},{2,0},{3,7},{4,6},{5,1},{6,4},{7,3},{8,10},{9,13},{10,... | collective-permute-start | bytes 196616 | tf_op jit(solution)/shard_map/ppermute | solution.py:551
  30.8 0.0 copy-done.1
  30.8 0.0 copy-done
  30.8 0.0 slice-start.3
  30.8 1.6 %attend.2.refs_6_ = bf16[4,80,128]{2,1,0:T(8,128)(2,1)S(1)} custom-call(s32[1]{0:T(128)} %bitcast.place.refs_0_, s32[1]{0:T(128)} %bitcast.1.bank.refs_1_, s32[64,128]{1,0:T(8,128)S(1)} %get-tuple-element.23.refs_2_, bf16[4,64,128]{2,1,0:T(8,128)(2,1)S(1)} %join.1.refs_3_, bf16[8,256,1024]{2,1,0:T(8,128)(2,1)S(1)} %copy-done, bf16[8,256,1024]{2,1,0:T(8,128)(2,1)S(1)} %copy-done.1), custom_call_target="tpu_custom_call" | custom-call | flops 33554432 | bytes 4194304 | tf_op jit(solution)/shard_map/attend/pallas_call | solution.py:422
  32.4 1.4 %collective-permute-done.10.refs_3_ = bf16[4,64,128]{2,1,0:T(8,128)(2,1)S(1)} collective-permute-done((bf16[4,64,128]{2,1,0:T(8,128)(2,1)S(1)}, bf16[4,64,128]{2,1,0:T(8,128)(2,1)S(1)}, u32[]{:S(2)}, u32[]{:S(2)}) %collective-permute-start.10) | collective-permute-done | bytes 65568 | tf_op jit(solution)/shard_map/ppermute | solution.py:551
  33.8 1.6 %attend.3 = bf16[8,112,128]{2,1,0:T(8,128)(2,1)S(1)} custom-call(s32[1]{0:T(128)} %bitcast.place.refs_0_, s32[1]{0:T(128)} %bitcast.1.bank.refs_1_, s32[64,128]{1,0:T(8,128)S(1)} %get-tuple-element.23.refs_2_, bf16[4,64,128]{2,1,0:T(8,128)(2,1)S(1)} %collective-permute-done.10.refs_3_, bf16[8,256,1024]{2,1,0:T(8,128)(2,1)S(1)} %copy-done, ...), custom_call_target="tpu_custom_call" | custom-call | flops 33554432 | bytes 16777216 | tf_op jit(solution)/shard_map/attend/pallas_call | solution.py:422
  35.3 11.7 %all_to_all.10.parts_ref = bf16[8,112,128]{2,1,0:T(8,128)(2,1)S(1)} all-to-all(bf16[8,112,128]{2,1,0:T(8,128)(2,1)S(1)} %attend.3), channel_id=1, replica_groups=mesh['groups'=2,'tensor'=8,'bank'=2] {'tensor'}, dimensions={0} | all-to-all | bytes 458752 | tf_op jit(solution)/shard_map/all_to_all | solution.py:543
  47.1 0.5 combine.1.x_ref
  47.6 0.0 slice-done
  47.6 0.0 slice-done.1
  47.6 0.0 slice-done.2
  47.6 0.0 slice-done.3
  47.6 2.3 %output.1 = bf16[8,8,1024]{2,1,0:T(8,128)(2,1)S(1)} custom-call(bf16[8,1024]{1,0:T(8,128)(2,1)S(1)} %combine.1.x_ref, bf16[1024,8192]{1,0:T(8,128)(2,1)S(1)} %bitcast.6), custom_call_target="tpu_custom_call" | custom-call | flops 134217728 | bytes 16777216 | tf_op jit(solution)/shard_map/output/pallas_call | solution.py:509
  49.9 9.9 %all_to_all.11.parts_ref = bf16[8,8,1024]{2,1,0:T(8,128)(2,1)S(1)} all-to-all(bf16[8,8,1024]{2,1,0:T(8,128)(2,1)S(1)} %output.1), channel_id=1, replica_groups=mesh['groups'=2,'tensor'=8,'bank'=2] {'tensor'}, dimensions={0} | all-to-all | bytes 262144 | tf_op jit(solution)/shard_map/all_to_all | solution.py:543
  59.8 0.6 %residual.1 = bf16[8,1024]{1,0:T(8,128)(2,1)} custom-call(bf16[8,1024]{1,0:T(8,128)(2,1)S(1)} %copy-done.3, bf16[8,8,1024]{2,1,0:T(8,128)(2,1)S(1)} %all_to_all.11.parts_ref), custom_call_target="tpu_custom_call" | custom-call | tf_op jit(solution)/shard_map/residual/pallas_call | solution.py:528
  (5 shorter events, 0.0 us)
Async XLA Ops:
  0.0 2.1 %copy-start.3 = (bf16[8,1024]{1,0:T(8,128)(2,1)S(1)}, bf16[8,1024]{1,0:T(8,128)(2,1)}, u32[]{:S(2)}) copy-start(bf16[8,1024]{1,0:T(8,128)(2,1)} %x_ref.7) | copy-start | bytes 49156
  0.0 2.1 %copy-start.4 = (s32[8]{0:T(128)S(1)}, s32[8]{0:T(128)}, u32[]{:S(2)}) copy-start(s32[8]{0:T(128)} %param.11) | copy-start | bytes 100
  0.0 2.1 %collective-permute-start = (bf16[8,1024]{1,0:T(8,128)(2,1)}, bf16[8,1024]{1,0:T(8,128)(2,1)S(1)}, u32[]{:S(2)}, u32[]{:S(2)}) collective-permute-start(bf16[8,1024]{1,0:T(8,128)(2,1)} %x_ref.7), channel_id=1, source_target_pairs={{0,1},{1,0},{2,3},{3,2},{4,5},{5,4},{6,7},{7,6},{8,9},{9,8},{10,11... | collective-permute-start | bytes 49160 | tf_op jit(solution)/shard_map/ppermute | solution.py:539
  0.5 1.6 %collective-permute-start.1 = (s32[8]{0:T(128)}, s32[8]{0:T(128)S(1)}, u32[]{:S(2)}, u32[]{:S(2)}) collective-permute-start(s32[8]{0:T(128)} %param.11), channel_id=1, source_target_pairs={{0,1},{1,0},{2,3},{3,2},{4,5},{5,4},{6,7},{7,6},{8,9},{9,8},{10,11... | collective-permute-start | bytes 104 | tf_op jit(solution)/shard_map/ppermute | solution.py:539
  2.1 6.1 %copy-start.5 = (s32[8]{0:T(128)S(1)}, s32[8]{0:T(128)}, u32[]{:S(2)}) copy-start(s32[8]{0:T(128)} %length.1) | copy-start | bytes 100
  5.2 6.4 %collective-permute-start.2 = (f32[4,16,640]{2,1,0:T(8,128)S(1)}, f32[4,16,640]{2,1,0:T(8,128)S(1)}, u32[]{:S(2)}, u32[]{:S(2)}) collective-permute-start(f32[4,16,640]{2,1,0:T(8,128)S(1)} %get-tuple-element.26), channel_id=1, source_target_pairs={{0,2},{1,5},{2,0},{3,7},{4,6},{5,1},{6,4},{7,3},{8,10},{9,13},{10,... | collective-permute-start | bytes 491528 | tf_op jit(solution)/shard_map/ppermute | solution.py:551
  8.2 12.4 %copy-start.2 = (bf16[16,64,1024]{2,1,0:T(8,128)(2,1)S(1)}, bf16[16,64,1024]{2,1,0:T(8,128)(2,1)}, u32[]{:S(2)}) copy-start(bf16[16,64,1024]{2,1,0:T(8,128)(2,1)} %up_ref.1) | copy-start | bytes 6291460
  8.2 22.6 %copy-start.1 = (bf16[8,256,1024]{2,1,0:T(8,128)(2,1)S(1)}, bf16[8,256,1024]{2,1,0:T(8,128)(2,1)}, u32[]{:S(2)}) copy-start(bf16[8,256,1024]{2,1,0:T(8,128)(2,1)} %refs_5_.3) | copy-start | bytes 12582916
  8.2 39.4 %slice-start = ((s8[16777216]{0:T(1024)(128)(4,1)}), s8[4194304]{0:T(1024)(128)(4,1)S(1)}, s32[]{:S(2)}) async-start(s8[16777216]{0:T(1024)(128)(4,1)} %bitcast.5), calls=%async_computation.2 | async-start | bytes 8388608
  8.2 39.4 %slice-start.1 = ((s8[16777216]{0:T(1024)(128)(4,1)}), s8[4194304]{0:T(1024)(128)(4,1)S(1)}, s32[]{:S(2)}) async-start(s8[16777216]{0:T(1024)(128)(4,1)} %bitcast.5), calls=%async_computation.3 | async-start | bytes 8388608
  11.5 19.3 %copy-start = (bf16[8,256,1024]{2,1,0:T(8,128)(2,1)S(1)}, bf16[8,256,1024]{2,1,0:T(8,128)(2,1)}, u32[]{:S(2)}) copy-start(bf16[8,256,1024]{2,1,0:T(8,128)(2,1)} %refs_4_.3) | copy-start | bytes 12582916
  11.6 7.4 %collective-permute-start.3 = (f32[16,640]{1,0:T(8,128)S(1)}, f32[16,640]{1,0:T(8,128)S(1)}, u32[]{:S(2)}, u32[]{:S(2)}) collective-permute-start(f32[16,640]{1,0:T(8,128)S(1)} %get-tuple-element.29), channel_id=1, source_target_pairs={{0,12},{1,11},{2,14},{3,9},{4,8},{5,15},{6,10},{7,13},{8,4},{9,3},... | collective-permute-start | bytes 122888 | tf_op jit(solution)/shard_map/ppermute | solution.py:551
  15.7 4.9 %collective-permute-start.4 = (f32[16,640]{1,0:T(8,128)S(1)}, f32[16,640]{1,0:T(8,128)S(1)}, u32[]{:S(2)}, u32[]{:S(2)}) collective-permute-start(f32[16,640]{1,0:T(8,128)S(1)} %get-tuple-element.30), channel_id=1, source_target_pairs={{0,8},{1,9},{2,10},{3,11},{4,12},{5,13},{6,14},{7,15},{8,0},{9,1},... | collective-permute-start | bytes 122888 | tf_op jit(solution)/shard_map/ppermute | solution.py:551
  15.7 4.9 %collective-permute-start.5 = (f32[16,640]{1,0:T(8,128)S(1)}, f32[16,640]{1,0:T(8,128)S(1)}, u32[]{:S(2)}, u32[]{:S(2)}) collective-permute-start(f32[16,640]{1,0:T(8,128)S(1)} %get-tuple-element.31), channel_id=1, source_target_pairs={{0,4},{1,3},{2,6},{3,1},{4,0},{5,7},{6,2},{7,5},{8,12},{9,11},{10,... | collective-permute-start | bytes 122888 | tf_op jit(solution)/shard_map/ppermute | solution.py:551
  16.3 31.2 %slice-start.2 = ((s8[16777216]{0:T(1024)(128)(4,1)}), s8[4194304]{0:T(1024)(128)(4,1)S(1)}, s32[]{:S(2)}) async-start(s8[16777216]{0:T(1024)(128)(4,1)} %bitcast.5), calls=%async_computation.4 | async-start | bytes 8388608
  21.0 1.2 %collective-permute-start.6 = (f32[8,1024]{1,0:T(8,128)S(1)}, f32[8,1024]{1,0:T(8,128)S(1)}, u32[]{:S(2)}, u32[]{:S(2)}) collective-permute-start(f32[8,1024]{1,0:T(8,128)S(1)} %get-tuple-element.37), channel_id=1, source_target_pairs={{0,1},{1,0},{2,3},{3,2},{4,5},{5,4},{6,7},{7,6},{8,9},{9,8},{10,11... | collective-permute-start | bytes 98312 | tf_op jit(solution)/shard_map/ppermute | solution.py:539
  22.3 5.6 %collective-permute-start.7 = (bf16[1,64,128]{2,1,0:T(8,128)(2,1)S(1)}, bf16[1,64,128]{2,1,0:T(8,128)(2,1)S(1)}, u32[]{:S(2)}, u32[]{:S(2)}) collective-permute-start(bf16[1,64,128]{2,1,0:T(8,128)(2,1)S(1)} %rotate.1.refs_0_.q_ref), channel_id=1, source_target_pairs={{0,12},{1,11},{2,14},{3,9},{4,8},{5,15},{6,10},{7,13},{8,4},{9,3},... | collective-permute-start | bytes 49160 | tf_op jit(solution)/shard_map/ppermute | solution.py:551
  24.5 4.9 %collective-permute-start.8 = (bf16[1,64,128]{2,1,0:T(8,128)(2,1)S(1)}, bf16[1,64,128]{2,1,0:T(8,128)(2,1)S(1)}, u32[]{:S(2)}, u32[]{:S(2)}) collective-permute-start(bf16[1,64,128]{2,1,0:T(8,128)(2,1)S(1)} %rotate.1.refs_0_.q_ref), channel_id=1, source_target_pairs={{0,8},{1,9},{2,10},{3,11},{4,12},{5,13},{6,14},{7,15},{8,0},{9,1},... | collective-permute-start | bytes 49160 | tf_op jit(solution)/shard_map/ppermute | solution.py:551
  24.5 4.9 %collective-permute-start.9 = (bf16[1,64,128]{2,1,0:T(8,128)(2,1)S(1)}, bf16[1,64,128]{2,1,0:T(8,128)(2,1)S(1)}, u32[]{:S(2)}, u32[]{:S(2)}) collective-permute-start(bf16[1,64,128]{2,1,0:T(8,128)(2,1)S(1)} %rotate.1.refs_0_.q_ref), channel_id=1, source_target_pairs={{0,4},{1,3},{2,6},{3,1},{4,0},{5,7},{6,2},{7,5},{8,12},{9,11},{10,... | collective-permute-start | bytes 49160 | tf_op jit(solution)/shard_map/ppermute | solution.py:551
  29.4 4.3 %collective-permute-start.10 = (bf16[4,64,128]{2,1,0:T(8,128)(2,1)S(1)}, bf16[4,64,128]{2,1,0:T(8,128)(2,1)S(1)}, u32[]{:S(2)}, u32[]{:S(2)}) collective-permute-start(bf16[4,64,128]{2,1,0:T(8,128)(2,1)S(1)} %join.1.refs_3_), channel_id=1, source_target_pairs={{0,2},{1,5},{2,0},{3,7},{4,6},{5,1},{6,4},{7,3},{8,10},{9,13},{10,... | collective-permute-start | bytes 196616 | tf_op jit(solution)/shard_map/ppermute | solution.py:551
  30.8 16.8 %slice-start.3 = ((s8[16777216]{0:T(1024)(128)(4,1)}), s8[4194304]{0:T(1024)(128)(4,1)S(1)}, s32[]{:S(2)}) async-start(s8[16777216]{0:T(1024)(128)(4,1)} %bitcast.5), calls=%async_computation.5 | async-start | bytes 8388608

commit v16 on v15

--- a/solution.py
+++ b/solution.py
@@ -40,12 +40,13 @@
     return pltpu.CompilerParams(vmem_limit_bytes=mib * MIB)
 
 
-def exchanged(slot):
-    return slot & ~3 | (slot & 1) << 1 | slot >> 1 & 1
+def turned(slot, bits):
+    return sum(bit for i, bit in enumerate(bits) if slot >> i & 1)
 
 
 def rank_of(place, bank, slot):
-    return place ^ (slot + bank * (exchanged(slot) - slot))
+    first, second = turned(slot, (4, 1, 2)), turned(slot, (4, 2, 1))
+    return place ^ (first + bank * (second - first))
 
 
 def start_columns(weight, column, target, sems):
@@ -76,11 +77,11 @@
     return jnp.broadcast_to(column, (column.shape[0], HEAD_DIM))
 
 
-def start_slots(parity, place, bank, w_ref, w_buf, sems):
+def start_slots(parity, first_slot, place, bank, w_ref, w_buf, sems):
     count, _, width = w_buf.shape
     copies = []
     for s in range(count):
-        target = rank_of(place[0], bank[0], 2 * s + parity)
+        target = rank_of(place[0], bank[0], 2 * (first_slot + s) + parity)
         first = (2 * target + bank[0]) * width
         copies.append(start_columns(w_ref, first, w_buf.at[s], sems.at[s]))
     return copies
@@ -101,30 +102,39 @@
     return copies
 
 
-def fetch_kernel(ref, out, sems):
-    wait_all(start_parts(ref, out, sems))
-
-
-def fetch(array):
+def fetch_kernel(place, bank, down_ref, w_ref, down_out, w_out, down_sems, sems):
+    copies = start_parts(down_ref, down_out, down_sems)
+    for slot in start_slots(1, 0, place, bank, w_ref, w_out, sems):
+        copies += slot
+    wait_all(copies)
+
+
+def fetch(place, bank, down, wq, ranks, slots):
+    out = [
+        jax.ShapeDtypeStruct(down.shape, BF16),
+        shape(slots, wq.shape[0], wq.shape[1] // ranks // 2, dtype=BF16),
+    ]
     return pl.pallas_call(
         fetch_kernel,
-        in_specs=[big()],
-        out_specs=whole(),
-        out_shape=jax.ShapeDtypeStruct(array.shape, array.dtype),
-        scratch_shapes=[pltpu.SemaphoreType.DMA((2,))],
+        in_specs=[scalar()] * 2 + [big()] * 2,
+        out_specs=[whole()] * 2,
+        out_shape=out,
+        scratch_shapes=[
+            pltpu.SemaphoreType.DMA((2,)),
+            pltpu.SemaphoreType.DMA((slots, CHUNKS)),
+        ],
         compiler_params=params(),
         cost_estimate=pl.CostEstimate(
-            flops=0, bytes_accessed=2 * array.size, transcendentals=0
+            flops=0, bytes_accessed=2 * sum(o.size for o in out), transcendentals=0
         ),
         name="fetch",
-    )(array)
-
-
-def slot_scratch(wq, ranks):
-    half, depth = ranks // 2, wq.shape[0]
+    )(place, bank, down, wq)
+
+
+def slot_scratch(wq, ranks, slots):
     return [
-        pltpu.VMEM((half, depth, wq.shape[1] // ranks // 2), BF16),
-        pltpu.SemaphoreType.DMA((half, CHUNKS)),
+        pltpu.VMEM((slots, wq.shape[0], wq.shape[1] // ranks // 2), BF16),
+        pltpu.SemaphoreType.DMA((slots, CHUNKS)),
     ]
 
 
@@ -134,10 +144,11 @@
 
 
 def project_sent_kernel(
-    place, bank, own_ref, came_ref, x_ref, other_ref, down_ref, w_ref, *refs
+    place, bank, own_ref, came_ref, x_ref, other_ref, down_ref, ahead_ref, w_ref, *refs
 ):
     out, inner, column_out, w_buf, sems = refs
-    copies = start_slots(1, place, bank, w_ref, w_buf, sems)
+    ahead = ahead_ref.shape[0]
+    copies = start_slots(1, ahead, place, bank, w_ref, w_buf, sems)
     width = w_buf.shape[2]
     x = beam_rows(x_ref, other_ref)
     adapters, rank, depth = down_ref.shape
@@ -156,24 +167,27 @@
         part = every[:, j * HEAD_DIM : (j + 1) * HEAD_DIM]
         total += jnp.where(lane // rank + j * per == column, part, 0.0)
     inner[...] = total
+    for s in range(out.shape[0]):
+        out[s, :, width:] = total
+    for s in range(ahead):
+        out[s, :, :width] = jnp.dot(x, ahead_ref[s], preferred_element_type=F32)
     for s, slot in enumerate(copies):
-        out[s, :, width:] = total
         wait_all(slot)
-        out[s, :, :width] = jnp.dot(x, w_buf[s], preferred_element_type=F32)
-
-
-def project_sent(place, bank, index, x, other, down, wq, ranks):
+        out[ahead + s, :, :width] = jnp.dot(x, w_buf[s], preferred_element_type=F32)
+
+
+def project_sent(place, bank, index, x, other, down, ahead, wq, ranks):
     rows = 2 * x.shape[0]
     return pl.pallas_call(
         project_sent_kernel,
-        in_specs=[scalar()] * 2 + [whole()] * 5 + [big()],
+        in_specs=[scalar()] * 2 + [whole()] * 6 + [big()],
         out_specs=[whole()] * 3,
         out_shape=[
             shape(ranks // 2, rows, wq.shape[1] // ranks // 2 + HEAD_DIM),
             shape(rows, HEAD_DIM),
             shape(rows, HEAD_DIM, dtype=jnp.int32),
         ],
-        scratch_shapes=slot_scratch(wq, ranks),
+        scratch_shapes=slot_scratch(wq, ranks, ranks // 2 - ahead.shape[0]),
         compiler_params=params(8),
         cost_estimate=pl.CostEstimate(
             flops=rows * (wq.size // 2 + 2 * down.size),
@@ -181,13 +195,13 @@
             transcendentals=0,
         ),
         name="project_sent",
-    )(place, bank, *[i.reshape(1, -1) for i in index], x, other, down, wq)
+    )(place, bank, *[i.reshape(1, -1) for i in index], x, other, down, ahead, wq)
 
 
 def project_kept_kernel(
     place, bank, length, x_ref, other_ref, w_ref, inner, out, length_out, w_buf, sems
 ):
-    copies = start_slots(0, place, bank, w_ref, w_buf, sems)
+    copies = start_slots(0, 0, place, bank, w_ref, w_buf, sems)
     width = w_buf.shape[2]
     beams = x_ref.shape[0]
     row = iota(length_out.shape, 0)
@@ -212,7 +226,7 @@
             shape(ranks // 2, 2 * beams, wq.shape[1] // ranks // 2 + HEAD_DIM),
             shape(beams * wq.shape[1] // ranks // HEAD_DIM, HEAD_DIM, dtype=jnp.int32),
         ],
-        scratch_shapes=slot_scratch(wq, ranks),
+        scratch_shapes=slot_scratch(wq, ranks, ranks // 2),
         compiler_params=params(8),
         cost_estimate=pl.CostEstimate(
             flops=beams * wq.size, bytes_accessed=2 * wq.size, transcendentals=0
@@ -235,10 +249,10 @@
     high = total.astype(BF16).astype(F32)
     low = total - high
     for r in range(ranks):
-        pieces = []
-        for first in (r * HEAD_DIM, (ranks + r) * HEAD_DIM):
-            pieces += [v[:, first : first + HEAD_DIM] for v in (high, low)]
-        out[r] = jnp.concatenate(pieces, axis=0).astype(BF16)
+        key = slice(r * HEAD_DIM, (r + 1) * HEAD_DIM)
+        value = slice((ranks + r) * HEAD_DIM, (ranks + r + 1) * HEAD_DIM)
+        pieces = [high[:, key], low[:, key], total[:, value]]
+        out[r] = jnp.concatenate(pieces, axis=0)
 
 
 def keyval(x, wkv, ranks):
@@ -247,7 +261,7 @@
         keyval_kernel,
         in_specs=[whole(), big()],
         out_specs=whole(),
-        out_shape=shape(ranks, 4 * beams, HEAD_DIM, dtype=BF16),
+        out_shape=shape(ranks, 3 * beams, HEAD_DIM),
         scratch_shapes=[pltpu.VMEM(wkv.shape, BF16), pltpu.SemaphoreType.DMA((4,))],
         compiler_params=params(8),
         cost_estimate=pl.CostEstimate(
@@ -363,6 +377,8 @@
 
 def attend_kernel(slots, earlier, place, bank, length_ref, q_ref, k_ref, v_ref, *refs):
     before, out_ref = refs[:-1], refs[-1]
+    if earlier:
+        *before, keyval_ref = before
     beams, positions, _ = k_ref.shape
     rows = q_ref.shape[1]
     group = rows // beams
@@ -406,14 +422,18 @@
         middle = (stats - high).astype(BF16).astype(F32)
         low = stats - high - middle
         tail = high + pltpu.roll(middle, 2 * group, 1) + pltpu.roll(low, 4 * group, 1)
-        block = jnp.concatenate(values + [tail, jnp.zeros_like(tail)], axis=0)
-        out_ref[head if earlier else i, : rows + 2 * beams] = block.astype(BF16)
+        if earlier:
+            block = jnp.concatenate(values + [tail, keyval_ref[head]], axis=0)
+            out_ref[head] = block.astype(BF16)
+        else:
+            block = jnp.concatenate(values + [tail, jnp.zeros_like(tail)], axis=0)
+            out_ref[i] = block.astype(BF16)
     if earlier:
-        *before, keyval_ref = before
         done = [(ref, i) for ref in before for i in range(ref.shape[0])]
         for slot, (ref, i) in zip(earlier, done):
-            out_ref[rank_of(place[0], bank[0], slot), : rows + 2 * beams] = ref[i]
-        out_ref[:, rows + 2 * beams :] = keyval_ref[...]
+            head = rank_of(place[0], bank[0], slot)
+            held = ref[i].astype(F32)[: rows + beams]
+            out_ref[head] = jnp.concatenate([held, keyval_ref[head]], axis=0).astype(BF16)
 
 
 def attend(place, bank, length, queries, keys, values, slots, earlier=(), before=()):
@@ -424,7 +444,7 @@
         in_specs=[scalar()] * 2 + [whole()] * (4 + len(before)),
         out_specs=whole(),
         out_shape=shape(
-            count + len(earlier), rows + (6 if earlier else 2) * beams, HEAD_DIM, dtype=BF16
+            count + len(earlier), rows + (4 if earlier else 2) * beams, HEAD_DIM, dtype=BF16
         ),
         compiler_params=params(),
         cost_estimate=pl.CostEstimate(
@@ -446,13 +466,10 @@
 
     head = iota((rows, HEAD_DIM), 0) % group
     lane = iota((rows, HEAD_DIM), 1)
-    sums = jnp.sum(parts_ref[:, rows + 2 * beams :].astype(F32), axis=0)
-    key, value = [
-        sums[i * beams : (i + 1) * beams] + sums[(i + 1) * beams : (i + 2) * beams]
-        for i in (0, 2)
-    ]
+    sums = jnp.sum(parts_ref[...].astype(F32)[:, rows + beams :], axis=0)
+    key = sums[:beams] + sums[beams : 2 * beams]
     key = rotate(key, cos_ref[...], sin_ref[...]).astype(BF16).astype(F32)
-    value = value.astype(BF16).astype(F32)
+    value = sums[2 * beams :].astype(BF16).astype(F32)
     score = jnp.sum(q_ref[0].astype(F32) * by_row(key), axis=1, keepdims=True) * (
         1.0 / HEAD_DIM**0.5
     )
@@ -576,8 +593,9 @@
     cosine = jnp.cos(angles)
     sine = jnp.where(lane < half, -1.0, 1.0) * jnp.sin(angles)
     weight = in_hbm(query_weight)
-    down = fetch(in_hbm(lowrank_down_factors.swapaxes(1, 2)))
-    sent, inner, column = project_sent(place, bank, index, x, x_other, down, weight, ranks)
+    down = in_hbm(lowrank_down_factors.swapaxes(1, 2))
+    ahead = fetch(place, bank, down, weight, ranks, ranks // 4)
+    sent, inner, column = project_sent(place, bank, index, x, x_other, *ahead, weight, ranks)
     came = hop(sent, 1)
     kept, length = project_kept(
         place, bank, beam_cache_length, x, x_other, weight, inner, ranks

time: 60.6 us -> 65.7 us (1.084)
  waiting for transfers between devices: 6.77 us -> 11 us
  blocking collectives: 21.6 us -> 22.4 us
    ppermute x8, waiting for transfers between devices: 5.67 us -> 9.89 us  [hop(): return lax.ppermute(x, ('tensor', 'bank'), pairs)]
    all_to_all x2, blocking collectives: 21.6 us -> 22.4 us  [traded(): return lax.all_to_all(blocks, 'tensor', 0, 0, tiled=True)]
    pallas_call x1, Pallas kernels: 1.56 us -> 2.24 us  [fetch(): pl.pallas_call(fetch_kernel, in_specs=[scalar()] * 2 + [big()] * 2, out_s...]
  transfers between devices with their start and end apart: 11 -> 11, of which waited for: 5 -> 6; matrix products, arithmetic and copies ran while one was open for 0% -> 0% of each run, Pallas kernels for 15% -> 15%
where the time goes in v16:
time: 65.7 us; the launch traced here: 65.5 us
  blocking collectives  22.4 us (34%)
  Pallas kernels  17.8 us (27%)
  starting transfers between devices  14 us (21%)
  waiting for transfers between devices  11 us (17%)
    all_to_all x2, blocking collectives, traded(): return lax.all_to_all(blocks, 'tensor', 0, 0, tiled=True)  22.4 us
    ppermute x8, starting transfers between devices, hop(): return lax.ppermute(x, ('tensor', 'bank'), pairs)  13.5 us
    ppermute x8, waiting for transfers between devices, hop(): return lax.ppermute(x, ('tensor', 'bank'), pairs)  9.89 us
    pallas_call x1, Pallas kernels, project_kept(): pl.pallas_call(project_kept_kernel, in_specs=[scalar()] * 3 + [whole()] *...  3.3 us
    pallas_call x2, Pallas kernels, attend(): pl.pallas_call(lambda *refs: attend_kernel(slots, earlier, *refs), in_spe...  3.13 us
    pallas_call x1, Pallas kernels, project_sent(): pl.pallas_call(project_sent_kernel, in_specs=[scalar()] * 2 + [whole()] *...  2.61 us
    pallas_call x1, Pallas kernels, keyval(): pl.pallas_call(keyval_kernel, in_specs=[whole(), big()], out_specs=whole(...  2.61 us
    pallas_call x1, Pallas kernels, output(): pl.pallas_call(output_kernel, in_specs=[whole()] * 2, out_specs=whole(),...  2.28 us
  transfers between devices with their start and end apart: 11, of which 6 were waited for; matrix products, arithmetic and copies ran while one was open for 0% of the time, Pallas kernels for 15%

profile of v16, /device:TPU:0, one launch (start us, length us, event | category | flops | bytes accessed | tf_op | source)
XLA Modules:
  0.0 65.5 jit_solution(15738541751586504502)
XLA Ops:
  0.0 0.5 collective-permute-start
  0.5 0.1 collective-permute-start.1
  0.5 0.0 copy-start.3
  0.5 0.0 copy-start.5
  0.5 2.2 %fetch.1 = (bf16[16,64,1024]{2,1,0:T(8,128)(2,1)S(1)}, bf16[2,1024,512]{2,1,0:T(8,128)(2,1)S(1)}) custom-call(s32[1]{0:T(128)} %bitcast.place.refs_0_, s32[1]{0:T(128)} %bitcast.1.bank.refs_1_, bf16[16,64,1024]{2,1,0:T(8,128)(2,1)} %bitcast.9, bf16[1024,8192]{1,0:T(8,128)(2,1)} %w_ref.6), custom_call_target="tpu_custom_call" | custom-call | bytes 4194304 | tf_op jit(solution)/shard_map/fetch/pallas_call | solution.py:117
  2.8 0.0 collective-permute-done.1
  2.8 0.0 collective-permute-done.other_ref
  2.8 0.0 copy-done.3
  2.8 0.0 copy-done.5
  2.8 0.0 copy-start.4
  2.8 2.6 %project_sent.1 = (f32[4,16,640]{2,1,0:T(8,128)S(1)}, f32[16,128]{1,0:T(8,128)S(1)}, s32[16,128]{1,0:T(8,128)S(1)}) custom-call(s32[1]{0:T(128)} %bitcast.place.refs_0_, s32[1]{0:T(128)} %bitcast.1.bank.refs_1_, s32[1,8]{1,0:T(1,128)S(1)} %bitcast.7, s32[1,8]{1,0:T(1,128)S(1)} %bitcast.8, bf16[8,1024]{1,0:T(8,128)(2,1)S(1)} %copy-done.3, ...), custom_call_target="tpu_custom_call" | custom-call | flops 100663296 | bytes 6291456 | tf_op jit(solution)/shard_map/project_sent/pallas_call | solution.py:181
  5.4 4.1 %collective-permute-start.2 = (f32[4,16,640]{2,1,0:T(8,128)S(1)}, f32[4,16,640]{2,1,0:T(8,128)S(1)}, u32[]{:S(2)}, u32[]{:S(2)}) collective-permute-start(f32[4,16,640]{2,1,0:T(8,128)S(1)} %get-tuple-element.30), channel_id=1, source_target_pairs={{0,8},{1,9},{2,10},{3,11},{4,12},{5,13},{6,14},{7,15},{8,0},{9,1},... | collective-permute-start | bytes 491528 | tf_op jit(solution)/shard_map/ppermute | solution.py:568
  9.5 0.0 copy-done.4
  9.5 0.0 copy-start.2
  9.5 0.0 copy-start.1
  9.5 0.0 slice-start
  9.5 0.0 slice-start.1
  9.6 3.3 %project_kept.1 = (f32[4,16,640]{2,1,0:T(8,128)S(1)}, s32[64,128]{1,0:T(8,128)S(1)}) custom-call(s32[1]{0:T(128)} %bitcast.place.refs_0_, s32[1]{0:T(128)} %bitcast.1.bank.refs_1_, s32[8]{0:T(128)S(1)} %copy-done.4, bf16[8,1024]{1,0:T(8,128)(2,1)S(1)} %copy-done.3, bf16[8,1024]{1,0:T(8,128)(2,1)S(1)} %collective-permute-done.other_ref, ...), custom_call_target="tpu_custom_call" | custom-call | flops 67108864 | bytes 16777216 | tf_op jit(solution)/shard_map/project_kept/pallas_call | solution.py:221
  12.9 0.0 copy-start
  12.9 4.5 %collective-permute-done.2.came_ref = f32[4,16,640]{2,1,0:T(8,128)S(1)} collective-permute-done((f32[4,16,640]{2,1,0:T(8,128)S(1)}, f32[4,16,640]{2,1,0:T(8,128)S(1)}, u32[]{:S(2)}, u32[]{:S(2)}) %collective-permute-start.2) | collective-permute-done | bytes 163872 | tf_op jit(solution)/shard_map/ppermute | solution.py:568
  17.4 1.7 %collective-permute-start.3 = (f32[16,640]{1,0:T(8,128)S(1)}, f32[16,640]{1,0:T(8,128)S(1)}, u32[]{:S(2)}, u32[]{:S(2)}) collective-permute-start(f32[16,640]{1,0:T(8,128)S(1)} %get-tuple-element.33), channel_id=1, source_target_pairs={{0,6},{1,7},{2,4},{3,5},{4,2},{5,3},{6,0},{7,1},{8,14},{9,15},{10,... | collective-permute-start | bytes 122888 | tf_op jit(solution)/shard_map/ppermute | solution.py:568
  19.2 1.4 %collective-permute-start.4 = (f32[16,640]{1,0:T(8,128)S(1)}, f32[16,640]{1,0:T(8,128)S(1)}, u32[]{:S(2)}, u32[]{:S(2)}) collective-permute-start(f32[16,640]{1,0:T(8,128)S(1)} %get-tuple-element.34), channel_id=1, source_target_pairs={{0,4},{1,3},{2,6},{3,1},{4,0},{5,7},{6,2},{7,5},{8,12},{9,11},{10,... | collective-permute-start | bytes 122888 | tf_op jit(solution)/shard_map/ppermute | solution.py:568
  20.5 0.5 collective-permute-start.5
  21.0 0.0 slice-start.2
  21.0 2.6 %keyval.1.refs_7_ = f32[8,24,128]{2,1,0:T(8,128)S(1)} custom-call(bf16[8,1024]{1,0:T(8,128)(2,1)S(1)} %copy-done.3, bf16[1024,2048]{1,0:T(8,128)(2,1)} %w_ref.7), custom_call_target="tpu_custom_call" | custom-call | flops 33554432 | bytes 4194304 | tf_op jit(solution)/shard_map/keyval/pallas_call | solution.py:260
  23.6 0.0 collective-permute-done.3.refs_1_
  23.6 0.0 collective-permute-done.4.refs_2_
  23.7 0.9 %collective-permute-done.5.refs_3_ = f32[16,640]{1,0:T(8,128)S(1)} collective-permute-done((f32[16,640]{1,0:T(8,128)S(1)}, f32[16,640]{1,0:T(8,128)S(1)}, u32[]{:S(2)}, u32[]{:S(2)}) %collective-permute-start.5) | collective-permute-done | bytes 40992 | tf_op jit(solution)/shard_map/ppermute | solution.py:568
  24.5 0.0 copy-done.2
  24.5 0.4 correct.1
  24.9 0.0 collective-permute-start.6
  24.9 0.1 fusion
  25.0 1.1 %collective-permute-done.6.came_ref = f32[8,1024]{1,0:T(8,128)S(1)} collective-permute-done((f32[8,1024]{1,0:T(8,128)S(1)}, f32[8,1024]{1,0:T(8,128)S(1)}, u32[]{:S(2)}, u32[]{:S(2)}) %collective-permute-start.6) | collective-permute-done | bytes 32800 | tf_op jit(solution)/shard_map/ppermute | solution.py:556
  26.1 0.1 rotate.1.refs_0_.q_ref
  26.2 0.9 %collective-permute-start.7 = (bf16[1,64,128]{2,1,0:T(8,128)(2,1)S(1)}, bf16[1,64,128]{2,1,0:T(8,128)(2,1)S(1)}, u32[]{:S(2)}, u32[]{:S(2)}) collective-permute-start(bf16[1,64,128]{2,1,0:T(8,128)(2,1)S(1)} %rotate.1.refs_0_.q_ref), channel_id=1, source_target_pairs={{0,6},{1,7},{2,4},{3,5},{4,2},{5,3},{6,0},{7,1},{8,14},{9,15},{10,... | collective-permute-start | bytes 49160 | tf_op jit(solution)/shard_map/ppermute | solution.py:568
  27.1 1.4 %collective-permute-start.8 = (bf16[1,64,128]{2,1,0:T(8,128)(2,1)S(1)}, bf16[1,64,128]{2,1,0:T(8,128)(2,1)S(1)}, u32[]{:S(2)}, u32[]{:S(2)}) collective-permute-start(bf16[1,64,128]{2,1,0:T(8,128)(2,1)S(1)} %rotate.1.refs_0_.q_ref), channel_id=1, source_target_pairs={{0,4},{1,3},{2,6},{3,1},{4,0},{5,7},{6,2},{7,5},{8,12},{9,11},{10,... | collective-permute-start | bytes 49160 | tf_op jit(solution)/shard_map/ppermute | solution.py:568
  28.5 1.3 %collective-permute-start.9 = (bf16[1,64,128]{2,1,0:T(8,128)(2,1)S(1)}, bf16[1,64,128]{2,1,0:T(8,128)(2,1)S(1)}, u32[]{:S(2)}, u32[]{:S(2)}) collective-permute-start(bf16[1,64,128]{2,1,0:T(8,128)(2,1)S(1)} %rotate.1.refs_0_.q_ref), channel_id=1, source_target_pairs={{0,2},{1,5},{2,0},{3,7},{4,6},{5,1},{6,4},{7,3},{8,10},{9,13},{10,... | collective-permute-start | bytes 49160 | tf_op jit(solution)/shard_map/ppermute | solution.py:568
  29.8 1.3 %collective-permute-done.7.refs_1_ = bf16[1,64,128]{2,1,0:T(8,128)(2,1)S(1)} collective-permute-done((bf16[1,64,128]{2,1,0:T(8,128)(2,1)S(1)}, bf16[1,64,128]{2,1,0:T(8,128)(2,1)S(1)}, u32[]{:S(2)}, u32[]{:S(2)}) %collective-permute-start.7) | collective-permute-done | bytes 16416 | tf_op jit(solution)/shard_map/ppermute | solution.py:568
  31.1 0.0 collective-permute-done.8.refs_2_
  31.1 1.1 %collective-permute-done.9.refs_3_ = bf16[1,64,128]{2,1,0:T(8,128)(2,1)S(1)} collective-permute-done((bf16[1,64,128]{2,1,0:T(8,128)(2,1)S(1)}, bf16[1,64,128]{2,1,0:T(8,128)(2,1)S(1)}, u32[]{:S(2)}, u32[]{:S(2)}) %collective-permute-start.9) | collective-permute-done | bytes 16416 | tf_op jit(solution)/shard_map/ppermute | solution.py:568
  32.2 2.2 %collective-permute-start.10 = (bf16[4,64,128]{2,1,0:T(8,128)(2,1)S(1)}, bf16[4,64,128]{2,1,0:T(8,128)(2,1)S(1)}, u32[]{:S(2)}, u32[]{:S(2)}) collective-permute-start(bf16[4,64,128]{2,1,0:T(8,128)(2,1)S(1)} %join.1.refs_3_), channel_id=1, source_target_pairs={{0,8},{1,9},{2,10},{3,11},{4,12},{5,13},{6,14},{7,15},{8,0},{9,1},... | collective-permute-start | bytes 196616 | tf_op jit(solution)/shard_map/ppermute | solution.py:568
  34.5 0.0 copy-done.1
  34.5 0.0 copy-done
  34.5 0.0 slice-start.3
  34.5 1.6 %attend.2.refs_6_ = bf16[4,80,128]{2,1,0:T(8,128)(2,1)S(1)} custom-call(s32[1]{0:T(128)} %bitcast.place.refs_0_, s32[1]{0:T(128)} %bitcast.1.bank.refs_1_, s32[64,128]{1,0:T(8,128)S(1)} %get-tuple-element.27.refs_2_, bf16[4,64,128]{2,1,0:T(8,128)(2,1)S(1)} %join.1.refs_3_, bf16[8,256,1024]{2,1,0:T(8,128)(2,1)S(1)} %copy-done, bf16[8,256,1024]{2,1,0:T(8,128)(2,1)S(1)} %copy-done.1), custom_call_target="tpu_custom_call" | custom-call | flops 33554432 | bytes 4194304 | tf_op jit(solution)/shard_map/attend/pallas_call | solution.py:442
  36.1 2.0 %collective-permute-done.10.refs_3_ = bf16[4,64,128]{2,1,0:T(8,128)(2,1)S(1)} collective-permute-done((bf16[4,64,128]{2,1,0:T(8,128)(2,1)S(1)}, bf16[4,64,128]{2,1,0:T(8,128)(2,1)S(1)}, u32[]{:S(2)}, u32[]{:S(2)}) %collective-permute-start.10) | collective-permute-done | bytes 65568 | tf_op jit(solution)/shard_map/ppermute | solution.py:568
  38.1 1.6 %attend.3 = bf16[8,96,128]{2,1,0:T(8,128)(2,1)S(1)} custom-call(s32[1]{0:T(128)} %bitcast.place.refs_0_, s32[1]{0:T(128)} %bitcast.1.bank.refs_1_, s32[64,128]{1,0:T(8,128)S(1)} %get-tuple-element.27.refs_2_, bf16[4,64,128]{2,1,0:T(8,128)(2,1)S(1)} %collective-permute-done.10.refs_3_, bf16[8,256,1024]{2,1,0:T(8,128)(2,1)S(1)} %copy-done, ...), custom_call_target="tpu_custom_call" | custom-call | flops 33554432 | bytes 16777216 | tf_op jit(solution)/shard_map/attend/pallas_call | solution.py:442
  39.7 12.6 %all_to_all.10.parts_ref = bf16[8,96,128]{2,1,0:T(8,128)(2,1)S(1)} all-to-all(bf16[8,96,128]{2,1,0:T(8,128)(2,1)S(1)} %attend.3), channel_id=1, replica_groups=mesh['groups'=2,'tensor'=8,'bank'=2] {'tensor'}, dimensions={0} | all-to-all | bytes 393216 | tf_op jit(solution)/shard_map/all_to_all | solution.py:560
  52.3 0.5 combine.1.x_ref
  52.8 0.0 slice-done
  52.8 0.0 slice-done.1
  52.8 0.0 slice-done.2
  52.8 0.0 slice-done.3
  52.8 2.3 %output.1 = bf16[8,8,1024]{2,1,0:T(8,128)(2,1)S(1)} custom-call(bf16[8,1024]{1,0:T(8,128)(2,1)S(1)} %combine.1.x_ref, bf16[1024,8192]{1,0:T(8,128)(2,1)S(1)} %bitcast.6), custom_call_target="tpu_custom_call" | custom-call | flops 134217728 | bytes 16777216 | tf_op jit(solution)/shard_map/output/pallas_call | solution.py:526
  55.1 9.8 %all_to_all.11.parts_ref = bf16[8,8,1024]{2,1,0:T(8,128)(2,1)S(1)} all-to-all(bf16[8,8,1024]{2,1,0:T(8,128)(2,1)S(1)} %output.1), channel_id=1, replica_groups=mesh['groups'=2,'tensor'=8,'bank'=2] {'tensor'}, dimensions={0} | all-to-all | bytes 262144 | tf_op jit(solution)/shard_map/all_to_all | solution.py:560
  64.9 0.6 residual.1
  (5 shorter events, 0.0 us)
Async XLA Ops:
  0.0 2.8 %collective-permute-start = (bf16[8,1024]{1,0:T(8,128)(2,1)}, bf16[8,1024]{1,0:T(8,128)(2,1)S(1)}, u32[]{:S(2)}, u32[]{:S(2)}) collective-permute-start(bf16[8,1024]{1,0:T(8,128)(2,1)} %x_ref.7), channel_id=1, source_target_pairs={{0,1},{1,0},{2,3},{3,2},{4,5},{5,4},{6,7},{7,6},{8,9},{9,8},{10,11... | collective-permute-start | bytes 49160 | tf_op jit(solution)/shard_map/ppermute | solution.py:556
  0.5 2.3 %collective-permute-start.1 = (s32[8]{0:T(128)}, s32[8]{0:T(128)S(1)}, u32[]{:S(2)}, u32[]{:S(2)}) collective-permute-start(s32[8]{0:T(128)} %param.11), channel_id=1, source_target_pairs={{0,1},{1,0},{2,3},{3,2},{4,5},{5,4},{6,7},{7,6},{8,9},{9,8},{10,11... | collective-permute-start | bytes 104 | tf_op jit(solution)/shard_map/ppermute | solution.py:556
  0.5 2.3 %copy-start.3 = (bf16[8,1024]{1,0:T(8,128)(2,1)S(1)}, bf16[8,1024]{1,0:T(8,128)(2,1)}, u32[]{:S(2)}) copy-start(bf16[8,1024]{1,0:T(8,128)(2,1)} %x_ref.7) | copy-start | bytes 49156
  0.5 2.3 %copy-start.5 = (s32[8]{0:T(128)S(1)}, s32[8]{0:T(128)}, u32[]{:S(2)}) copy-start(s32[8]{0:T(128)} %param.11) | copy-start | bytes 100
  2.8 6.7 %copy-start.4 = (s32[8]{0:T(128)S(1)}, s32[8]{0:T(128)}, u32[]{:S(2)}) copy-start(s32[8]{0:T(128)} %length.1) | copy-start | bytes 100
  5.4 12.0 %collective-permute-start.2 = (f32[4,16,640]{2,1,0:T(8,128)S(1)}, f32[4,16,640]{2,1,0:T(8,128)S(1)}, u32[]{:S(2)}, u32[]{:S(2)}) collective-permute-start(f32[4,16,640]{2,1,0:T(8,128)S(1)} %get-tuple-element.30), channel_id=1, source_target_pairs={{0,8},{1,9},{2,10},{3,11},{4,12},{5,13},{6,14},{7,15},{8,0},{9,1},... | collective-permute-start | bytes 491528 | tf_op jit(solution)/shard_map/ppermute | solution.py:568
  9.5 15.0 %copy-start.2 = (bf16[16,64,1024]{2,1,0:T(8,128)(2,1)S(1)}, bf16[16,64,1024]{2,1,0:T(8,128)(2,1)}, u32[]{:S(2)}) copy-start(bf16[16,64,1024]{2,1,0:T(8,128)(2,1)} %up_ref.1) | copy-start | bytes 6291460
  9.5 24.9 %copy-start.1 = (bf16[8,256,1024]{2,1,0:T(8,128)(2,1)S(1)}, bf16[8,256,1024]{2,1,0:T(8,128)(2,1)}, u32[]{:S(2)}) copy-start(bf16[8,256,1024]{2,1,0:T(8,128)(2,1)} %refs_5_.3) | copy-start | bytes 12582916
  9.5 43.2 %slice-start = ((s8[16777216]{0:T(1024)(128)(4,1)}), s8[4194304]{0:T(1024)(128)(4,1)S(1)}, s32[]{:S(2)}) async-start(s8[16777216]{0:T(1024)(128)(4,1)} %bitcast.5), calls=%async_computation.2 | async-start | bytes 8388608
  9.5 43.2 %slice-start.1 = ((s8[16777216]{0:T(1024)(128)(4,1)}), s8[4194304]{0:T(1024)(128)(4,1)S(1)}, s32[]{:S(2)}) async-start(s8[16777216]{0:T(1024)(128)(4,1)} %bitcast.5), calls=%async_computation.3 | async-start | bytes 8388608
  12.9 21.6 %copy-start = (bf16[8,256,1024]{2,1,0:T(8,128)(2,1)S(1)}, bf16[8,256,1024]{2,1,0:T(8,128)(2,1)}, u32[]{:S(2)}) copy-start(bf16[8,256,1024]{2,1,0:T(8,128)(2,1)} %refs_4_.3) | copy-start | bytes 12582916
  17.4 6.2 %collective-permute-start.3 = (f32[16,640]{1,0:T(8,128)S(1)}, f32[16,640]{1,0:T(8,128)S(1)}, u32[]{:S(2)}, u32[]{:S(2)}) collective-permute-start(f32[16,640]{1,0:T(8,128)S(1)} %get-tuple-element.33), channel_id=1, source_target_pairs={{0,6},{1,7},{2,4},{3,5},{4,2},{5,3},{6,0},{7,1},{8,14},{9,15},{10,... | collective-permute-start | bytes 122888 | tf_op jit(solution)/shard_map/ppermute | solution.py:568
  19.2 4.5 %collective-permute-start.4 = (f32[16,640]{1,0:T(8,128)S(1)}, f32[16,640]{1,0:T(8,128)S(1)}, u32[]{:S(2)}, u32[]{:S(2)}) collective-permute-start(f32[16,640]{1,0:T(8,128)S(1)} %get-tuple-element.34), channel_id=1, source_target_pairs={{0,4},{1,3},{2,6},{3,1},{4,0},{5,7},{6,2},{7,5},{8,12},{9,11},{10,... | collective-permute-start | bytes 122888 | tf_op jit(solution)/shard_map/ppermute | solution.py:568
  20.5 4.0 %collective-permute-start.5 = (f32[16,640]{1,0:T(8,128)S(1)}, f32[16,640]{1,0:T(8,128)S(1)}, u32[]{:S(2)}, u32[]{:S(2)}) collective-permute-start(f32[16,640]{1,0:T(8,128)S(1)} %get-tuple-element.35), channel_id=1, source_target_pairs={{0,2},{1,5},{2,0},{3,7},{4,6},{5,1},{6,4},{7,3},{8,10},{9,13},{10,... | collective-permute-start | bytes 122888 | tf_op jit(solution)/shard_map/ppermute | solution.py:568
  21.0 31.8 %slice-start.2 = ((s8[16777216]{0:T(1024)(128)(4,1)}), s8[4194304]{0:T(1024)(128)(4,1)S(1)}, s32[]{:S(2)}) async-start(s8[16777216]{0:T(1024)(128)(4,1)} %bitcast.5), calls=%async_computation.4 | async-start | bytes 8388608
  24.9 1.2 %collective-permute-start.6 = (f32[8,1024]{1,0:T(8,128)S(1)}, f32[8,1024]{1,0:T(8,128)S(1)}, u32[]{:S(2)}, u32[]{:S(2)}) collective-permute-start(f32[8,1024]{1,0:T(8,128)S(1)} %get-tuple-element.41), channel_id=1, source_target_pairs={{0,1},{1,0},{2,3},{3,2},{4,5},{5,4},{6,7},{7,6},{8,9},{9,8},{10,11... | collective-permute-start | bytes 98312 | tf_op jit(solution)/shard_map/ppermute | solution.py:556
  26.2 4.9 %collective-permute-start.7 = (bf16[1,64,128]{2,1,0:T(8,128)(2,1)S(1)}, bf16[1,64,128]{2,1,0:T(8,128)(2,1)S(1)}, u32[]{:S(2)}, u32[]{:S(2)}) collective-permute-start(bf16[1,64,128]{2,1,0:T(8,128)(2,1)S(1)} %rotate.1.refs_0_.q_ref), channel_id=1, source_target_pairs={{0,6},{1,7},{2,4},{3,5},{4,2},{5,3},{6,0},{7,1},{8,14},{9,15},{10,... | collective-permute-start | bytes 49160 | tf_op jit(solution)/shard_map/ppermute | solution.py:568
  27.1 4.0 %collective-permute-start.8 = (bf16[1,64,128]{2,1,0:T(8,128)(2,1)S(1)}, bf16[1,64,128]{2,1,0:T(8,128)(2,1)S(1)}, u32[]{:S(2)}, u32[]{:S(2)}) collective-permute-start(bf16[1,64,128]{2,1,0:T(8,128)(2,1)S(1)} %rotate.1.refs_0_.q_ref), channel_id=1, source_target_pairs={{0,4},{1,3},{2,6},{3,1},{4,0},{5,7},{6,2},{7,5},{8,12},{9,11},{10,... | collective-permute-start | bytes 49160 | tf_op jit(solution)/shard_map/ppermute | solution.py:568
  28.5 3.7 %collective-permute-start.9 = (bf16[1,64,128]{2,1,0:T(8,128)(2,1)S(1)}, bf16[1,64,128]{2,1,0:T(8,128)(2,1)S(1)}, u32[]{:S(2)}, u32[]{:S(2)}) collective-permute-start(bf16[1,64,128]{2,1,0:T(8,128)(2,1)S(1)} %rotate.1.refs_0_.q_ref), channel_id=1, source_target_pairs={{0,2},{1,5},{2,0},{3,7},{4,6},{5,1},{6,4},{7,3},{8,10},{9,13},{10,... | collective-permute-start | bytes 49160 | tf_op jit(solution)/shard_map/ppermute | solution.py:568
  32.2 5.9 %collective-permute-start.10 = (bf16[4,64,128]{2,1,0:T(8,128)(2,1)S(1)}, bf16[4,64,128]{2,1,0:T(8,128)(2,1)S(1)}, u32[]{:S(2)}, u32[]{:S(2)}) collective-permute-start(bf16[4,64,128]{2,1,0:T(8,128)(2,1)S(1)} %join.1.refs_3_), channel_id=1, source_target_pairs={{0,8},{1,9},{2,10},{3,11},{4,12},{5,13},{6,14},{7,15},{8,0},{9,1},... | collective-permute-start | bytes 196616 | tf_op jit(solution)/shard_map/ppermute | solution.py:568
  34.5 18.3 %slice-start.3 = ((s8[16777216]{0:T(1024)(128)(4,1)}), s8[4194304]{0:T(1024)(128)(4,1)S(1)}, s32[]{:S(2)}) async-start(s8[16777216]{0:T(1024)(128)(4,1)} %bitcast.5), calls=%async_computation.5 | async-start | bytes 8388608

commit v17 on v15

--- a/solution.py
+++ b/solution.py
@@ -235,10 +235,10 @@
     high = total.astype(BF16).astype(F32)
     low = total - high
     for r in range(ranks):
-        pieces = []
-        for first in (r * HEAD_DIM, (ranks + r) * HEAD_DIM):
-            pieces += [v[:, first : first + HEAD_DIM] for v in (high, low)]
-        out[r] = jnp.concatenate(pieces, axis=0).astype(BF16)
+        key = slice(r * HEAD_DIM, (r + 1) * HEAD_DIM)
+        value = slice((ranks + r) * HEAD_DIM, (ranks + r + 1) * HEAD_DIM)
+        pieces = [high[:, key], low[:, key], total[:, value]]
+        out[r] = jnp.concatenate(pieces, axis=0)
 
 
 def keyval(x, wkv, ranks):
@@ -247,7 +247,7 @@
         keyval_kernel,
         in_specs=[whole(), big()],
         out_specs=whole(),
-        out_shape=shape(ranks, 4 * beams, HEAD_DIM, dtype=BF16),
+        out_shape=shape(ranks, 3 * beams, HEAD_DIM),
         scratch_shapes=[pltpu.VMEM(wkv.shape, BF16), pltpu.SemaphoreType.DMA((4,))],
         compiler_params=params(8),
         cost_estimate=pl.CostEstimate(
@@ -363,6 +363,8 @@
 
 def attend_kernel(slots, earlier, place, bank, length_ref, q_ref, k_ref, v_ref, *refs):
     before, out_ref = refs[:-1], refs[-1]
+    if earlier:
+        *before, keyval_ref = before
     beams, positions, _ = k_ref.shape
     rows = q_ref.shape[1]
     group = rows // beams
@@ -406,14 +408,18 @@
         middle = (stats - high).astype(BF16).astype(F32)
         low = stats - high - middle
         tail = high + pltpu.roll(middle, 2 * group, 1) + pltpu.roll(low, 4 * group, 1)
-        block = jnp.concatenate(values + [tail, jnp.zeros_like(tail)], axis=0)
-        out_ref[head if earlier else i, : rows + 2 * beams] = block.astype(BF16)
+        if earlier:
+            block = jnp.concatenate(values + [tail, keyval_ref[head]], axis=0)
+            out_ref[head] = block.astype(BF16)
+        else:
+            block = jnp.concatenate(values + [tail, jnp.zeros_like(tail)], axis=0)
+            out_ref[i] = block.astype(BF16)
     if earlier:
-        *before, keyval_ref = before
         done = [(ref, i) for ref in before for i in range(ref.shape[0])]
         for slot, (ref, i) in zip(earlier, done):
-            out_ref[rank_of(place[0], bank[0], slot), : rows + 2 * beams] = ref[i]
-        out_ref[:, rows + 2 * beams :] = keyval_ref[...]
+            head = rank_of(place[0], bank[0], slot)
+            held = ref[i].astype(F32)[: rows + beams]
+            out_ref[head] = jnp.concatenate([held, keyval_ref[head]], axis=0).astype(BF16)
 
 
 def attend(place, bank, length, queries, keys, values, slots, earlier=(), before=()):
@@ -424,7 +430,7 @@
         in_specs=[scalar()] * 2 + [whole()] * (4 + len(before)),
         out_specs=whole(),
         out_shape=shape(
-            count + len(earlier), rows + (6 if earlier else 2) * beams, HEAD_DIM, dtype=BF16
+            count + len(earlier), rows + (4 if earlier else 2) * beams, HEAD_DIM, dtype=BF16
         ),
         compiler_params=params(),
         cost_estimate=pl.CostEstimate(
@@ -446,13 +452,10 @@
 
     head = iota((rows, HEAD_DIM), 0) % group
     lane = iota((rows, HEAD_DIM), 1)
-    sums = jnp.sum(parts_ref[:, rows + 2 * beams :].astype(F32), axis=0)
-    key, value = [
-        sums[i * beams : (i + 1) * beams] + sums[(i + 1) * beams : (i + 2) * beams]
-        for i in (0, 2)
-    ]
+    sums = jnp.sum(parts_ref[...].astype(F32)[:, rows + beams :], axis=0)
+    key = sums[:beams] + sums[beams : 2 * beams]
     key = rotate(key, cos_ref[...], sin_ref[...]).astype(BF16).astype(F32)
-    value = value.astype(BF16).astype(F32)
+    value = sums[2 * beams :].astype(BF16).astype(F32)
     score = jnp.sum(q_ref[0].astype(F32) * by_row(key), axis=1, keepdims=True) * (
         1.0 / HEAD_DIM**0.5
     )
@@ -594,11 +597,20 @@
         cache = paged_key_cache, paged_value_cache
         return attend(place, bank, length, queries, *cache, slots, **more)
 
-    gathered = join([query] + [hop(query, slot) for slot in near])
-    came = hop(gathered, 1)
-    done = attended_part(gathered, (0, *near))
-    odd = tuple(slot + 1 for slot in (0, *near))
-    partial = attended_part(came, odd, earlier=(0, *near), before=(done, token))
+    came, done = lax.optimization_barrier((hop(query, 1), attended_part(query, (0,))))
+    pair = join([query, came])
+    pairs = [hop(pair, slot) for slot in near[:-1]]
+    done = [done, attended_part(came, (1,))]
+    held, _ = lax.optimization_barrier((pair, done[1]))
+    pairs.append(hop(held, near[-1]))
+    slots = [0, 1]
+    for i in (0, 2):
+        slots += [near[i], near[i] + 1]
+        done.append(attended_part(pairs[i], tuple(slots[-2:])))
+    last = near[1], near[1] + 1
+    partial = attended_part(
+        pairs[1], last, earlier=tuple(slots), before=(*done, token)
+    )
     attended = combine(traded(partial), query, cosine, sine)
     return residual(x, traded(output(attended, output_weight, ranks)))
 

time: 60.6 us -> 61 us (level)
  waiting for transfers between devices: 6.77 us -> 7.68 us
  starting transfers between devices: 14.1 us -> 13.4 us
    ppermute x8, waiting for transfers between devices: 5.67 us -> 6.58 us  [hop(): return lax.ppermute(x, ('tensor', 'bank'), pairs)]
    ppermute x8, starting transfers between devices: 13.6 us -> 12.9 us  [hop(): return lax.ppermute(x, ('tensor', 'bank'), pairs)]
    pallas_call x2 -> x5, Pallas kernels: 3.13 us -> 3.6 us  [attend(): pl.pallas_call(lambda *refs: attend_kernel(slots, earlier, *refs), in_spe...]
  transfers between devices with their start and end apart: 11 -> 11, of which waited for: 5 -> 6; matrix products, arithmetic and copies ran while one was open for 0% -> 0% of each run, Pallas kernels for 15% -> 16%
where the time goes in v17:
time: 61 us; the launch traced here: 60.8 us
  blocking collectives  21.5 us (35%)
  Pallas kernels  17.8 us (29%)
  starting transfers between devices  13.4 us (22%)
  waiting for transfers between devices  7.68 us (13%)
    all_to_all x2, blocking collectives, traded(): return lax.all_to_all(blocks, 'tensor', 0, 0, tiled=True)  21.5 us
    ppermute x8, starting transfers between devices, hop(): return lax.ppermute(x, ('tensor', 'bank'), pairs)  12.9 us
    ppermute x8, waiting for transfers between devices, hop(): return lax.ppermute(x, ('tensor', 'bank'), pairs)  6.58 us
    pallas_call x5, Pallas kernels, attend(): pl.pallas_call(lambda *refs: attend_kernel(slots, earlier, *refs), in_spe...  3.6 us
    pallas_call x1, Pallas kernels, project_kept(): pl.pallas_call(project_kept_kernel, in_specs=[scalar()] * 3 + [whole()] *...  3.29 us
    pallas_call x1, Pallas kernels, project_sent(): pl.pallas_call(project_sent_kernel, in_specs=[scalar()] * 2 + [whole()] *...  3.01 us
    pallas_call x1, Pallas kernels, keyval(): pl.pallas_call(keyval_kernel, in_specs=[whole(), big()], out_specs=whole(...  2.46 us
    pallas_call x1, Pallas kernels, output(): pl.pallas_call(output_kernel, in_specs=[whole()] * 2, out_specs=whole(),...  2.28 us
  transfers between devices with their start and end apart: 11, of which 6 were waited for; matrix products, arithmetic and copies ran while one was open for 0% of the time, Pallas kernels for 16%

profile of v17, /device:TPU:0, one launch (start us, length us, event | category | flops | bytes accessed | tf_op | source)
XLA Modules:
  0.0 60.8 jit_solution(17392067754055747443)
XLA Ops:
  0.0 0.0 copy-start.3
  0.0 0.0 copy-start.4
  0.0 0.5 collective-permute-start
  0.5 0.1 collective-permute-start.1
  0.5 1.6 %fetch.1.down_ref = bf16[16,64,1024]{2,1,0:T(8,128)(2,1)S(1)} custom-call(bf16[16,64,1024]{2,1,0:T(8,128)(2,1)} %bitcast.9), custom_call_target="tpu_custom_call" | custom-call | bytes 2097152 | tf_op jit(solution)/shard_map/fetch/pallas_call | solution.py:109
  2.1 0.0 collective-permute-done.1
  2.1 0.0 collective-permute-done.other_ref
  2.1 0.0 copy-done.3
  2.1 0.0 copy-done.4
  2.1 0.0 copy-start.5
  2.1 3.0 %project_sent.1 = (f32[4,16,640]{2,1,0:T(8,128)S(1)}, f32[16,128]{1,0:T(8,128)S(1)}, s32[16,128]{1,0:T(8,128)S(1)}) custom-call(s32[1]{0:T(128)} %bitcast.place.refs_0_, s32[1]{0:T(128)} %bitcast.1.bank.refs_1_, s32[1,8]{1,0:T(1,128)S(1)} %bitcast.7, s32[1,8]{1,0:T(1,128)S(1)} %bitcast.8, bf16[8,1024]{1,0:T(8,128)(2,1)S(1)} %copy-done.3, ...), custom_call_target="tpu_custom_call" | custom-call | flops 100663296 | bytes 6291456 | tf_op jit(solution)/shard_map/project_sent/pallas_call | solution.py:167
  5.2 3.0 %collective-permute-start.2 = (f32[4,16,640]{2,1,0:T(8,128)S(1)}, f32[4,16,640]{2,1,0:T(8,128)S(1)}, u32[]{:S(2)}, u32[]{:S(2)}) collective-permute-start(f32[4,16,640]{2,1,0:T(8,128)S(1)} %get-tuple-element.29), channel_id=1, source_target_pairs={{0,2},{1,5},{2,0},{3,7},{4,6},{5,1},{6,4},{7,3},{8,10},{9,13},{10,... | collective-permute-start | bytes 491528 | tf_op jit(solution)/shard_map/ppermute | solution.py:554
  8.2 0.0 copy-done.5
  8.2 0.0 copy-start.2
  8.2 0.0 copy-start.1
  8.2 3.3 %project_kept.1 = (f32[4,16,640]{2,1,0:T(8,128)S(1)}, s32[64,128]{1,0:T(8,128)S(1)}) custom-call(s32[1]{0:T(128)} %bitcast.place.refs_0_, s32[1]{0:T(128)} %bitcast.1.bank.refs_1_, s32[8]{0:T(128)S(1)} %copy-done.5, bf16[8,1024]{1,0:T(8,128)(2,1)S(1)} %copy-done.3, bf16[8,1024]{1,0:T(8,128)(2,1)S(1)} %collective-permute-done.other_ref, ...), custom_call_target="tpu_custom_call" | custom-call | flops 67108864 | bytes 16777216 | tf_op jit(solution)/shard_map/project_kept/pallas_call | solution.py:207
  11.5 0.0 copy-start
  11.5 0.0 collective-permute-done.2.came_ref
  11.5 4.1 %collective-permute-start.3 = (f32[16,640]{1,0:T(8,128)S(1)}, f32[16,640]{1,0:T(8,128)S(1)}, u32[]{:S(2)}, u32[]{:S(2)}) collective-permute-start(f32[16,640]{1,0:T(8,128)S(1)} %get-tuple-element.32), channel_id=1, source_target_pairs={{0,12},{1,11},{2,14},{3,9},{4,8},{5,15},{6,10},{7,13},{8,4},{9,3},... | collective-permute-start | bytes 122888 | tf_op jit(solution)/shard_map/ppermute | solution.py:554
  15.7 0.0 collective-permute-start.4
  15.7 0.6 %collective-permute-start.5 = (f32[16,640]{1,0:T(8,128)S(1)}, f32[16,640]{1,0:T(8,128)S(1)}, u32[]{:S(2)}, u32[]{:S(2)}) collective-permute-start(f32[16,640]{1,0:T(8,128)S(1)} %get-tuple-element.34), channel_id=1, source_target_pairs={{0,4},{1,3},{2,6},{3,1},{4,0},{5,7},{6,2},{7,5},{8,12},{9,11},{10,... | collective-permute-start | bytes 122888 | tf_op jit(solution)/shard_map/ppermute | solution.py:554
  16.3 2.5 %keyval.1.refs_10_ = f32[8,24,128]{2,1,0:T(8,128)S(1)} custom-call(bf16[8,1024]{1,0:T(8,128)(2,1)S(1)} %copy-done.3, bf16[1024,2048]{1,0:T(8,128)(2,1)} %w_ref.5), custom_call_target="tpu_custom_call" | custom-call | flops 33554432 | bytes 4194304 | tf_op jit(solution)/shard_map/keyval/pallas_call | solution.py:246
  18.8 0.0 collective-permute-done.3.refs_1_
  18.8 1.8 %collective-permute-done.4.refs_2_ = f32[16,640]{1,0:T(8,128)S(1)} collective-permute-done((f32[16,640]{1,0:T(8,128)S(1)}, f32[16,640]{1,0:T(8,128)S(1)}, u32[]{:S(2)}, u32[]{:S(2)}) %collective-permute-start.4) | collective-permute-done | bytes 40992 | tf_op jit(solution)/shard_map/ppermute | solution.py:554
  20.6 0.0 collective-permute-done.5.refs_3_
  20.6 0.0 copy-done.2
  20.6 0.4 correct.1
  21.0 0.0 collective-permute-start.6
  21.0 0.1 fusion
  21.1 1.1 %collective-permute-done.6.came_ref = f32[8,1024]{1,0:T(8,128)S(1)} collective-permute-done((f32[8,1024]{1,0:T(8,128)S(1)}, f32[8,1024]{1,0:T(8,128)S(1)}, u32[]{:S(2)}, u32[]{:S(2)}) %collective-permute-start.6) | collective-permute-done | bytes 32800 | tf_op jit(solution)/shard_map/ppermute | solution.py:542
  22.2 0.1 rotate.1.refs_3_.refs_0_.q_ref
  22.3 1.6 %collective-permute-start.7 = (bf16[1,64,128]{2,1,0:T(8,128)(2,1)S(1)}, bf16[1,64,128]{2,1,0:T(8,128)(2,1)S(1)}, u32[]{:S(2)}, u32[]{:S(2)}) collective-permute-start(bf16[1,64,128]{2,1,0:T(8,128)(2,1)S(1)} %rotate.1.refs_3_.refs_0_.q_ref), channel_id=1, source_target_pairs={{0,2},{1,5},{2,0},{3,7},{4,6},{5,1},{6,4},{7,3},{8,10},{9,13},{10,... | collective-permute-start | bytes 49160 | tf_op jit(solution)/shard_map/ppermute | solution.py:554
  23.9 0.0 copy-done.1
  23.9 0.0 copy-done
  23.9 0.5 attend.5.refs_6_
  24.4 1.7 %collective-permute-done.7.refs_1_.refs_3_ = bf16[1,64,128]{2,1,0:T(8,128)(2,1)S(1)} collective-permute-done((bf16[1,64,128]{2,1,0:T(8,128)(2,1)S(1)}, bf16[1,64,128]{2,1,0:T(8,128)(2,1)S(1)}, u32[]{:S(2)}, u32[]{:S(2)}) %collective-permute-start.7) | collective-permute-done | bytes 16416 | tf_op jit(solution)/shard_map/ppermute | solution.py:554
  26.1 0.0 slice-start
  26.1 0.5 attend.6.refs_7_
  26.6 0.0 slice-start.1
  26.6 0.1 collective-permute-start.10
  26.7 3.5 %collective-permute-start.9 = (bf16[2,64,128]{2,1,0:T(8,128)(2,1)S(1)}, bf16[2,64,128]{2,1,0:T(8,128)(2,1)S(1)}, u32[]{:S(2)}, u32[]{:S(2)}) collective-permute-start(bf16[2,64,128]{2,1,0:T(8,128)(2,1)S(1)} %join.1), channel_id=1, source_target_pairs={{0,12},{1,11},{2,14},{3,9},{4,8},{5,15},{6,10},{7,13},{8,4},{9,3},... | collective-permute-start | bytes 98312 | tf_op jit(solution)/shard_map/ppermute | solution.py:554
  30.1 0.0 collective-permute-start.8
  30.1 0.8 %collective-permute-done.10.refs_3_ = bf16[2,64,128]{2,1,0:T(8,128)(2,1)S(1)} collective-permute-done((bf16[2,64,128]{2,1,0:T(8,128)(2,1)S(1)}, bf16[2,64,128]{2,1,0:T(8,128)(2,1)S(1)}, u32[]{:S(2)}, u32[]{:S(2)}) %collective-permute-start.10) | collective-permute-done | bytes 32800 | tf_op jit(solution)/shard_map/ppermute | solution.py:554
  30.9 0.8 %attend.8.refs_9_ = bf16[2,80,128]{2,1,0:T(8,128)(2,1)S(1)} custom-call(s32[1]{0:T(128)} %bitcast.place.refs_0_, s32[1]{0:T(128)} %bitcast.1.bank.refs_1_, s32[64,128]{1,0:T(8,128)S(1)} %get-tuple-element.26.refs_2_, bf16[2,64,128]{2,1,0:T(8,128)(2,1)S(1)} %collective-permute-done.10.refs_3_, bf16[8,256,1024]{2,1,0:T(8,128)(2,1)S(1)} %copy-done, ...), custom_call_target="tpu_custom_call" | custom-call | flops 16777216 | bytes 2097152 | tf_op jit(solution)/shard_map/attend/pallas_call | solution.py:428
  31.8 0.0 slice-start.2
  31.8 1.1 %collective-permute-done.9.refs_3_ = bf16[2,64,128]{2,1,0:T(8,128)(2,1)S(1)} collective-permute-done((bf16[2,64,128]{2,1,0:T(8,128)(2,1)S(1)}, bf16[2,64,128]{2,1,0:T(8,128)(2,1)S(1)}, u32[]{:S(2)}, u32[]{:S(2)}) %collective-permute-start.9) | collective-permute-done | bytes 32800 | tf_op jit(solution)/shard_map/ppermute | solution.py:554
  32.8 0.9 %attend.7.refs_8_ = bf16[2,80,128]{2,1,0:T(8,128)(2,1)S(1)} custom-call(s32[1]{0:T(128)} %bitcast.place.refs_0_, s32[1]{0:T(128)} %bitcast.1.bank.refs_1_, s32[64,128]{1,0:T(8,128)S(1)} %get-tuple-element.26.refs_2_, bf16[2,64,128]{2,1,0:T(8,128)(2,1)S(1)} %collective-permute-done.9.refs_3_, bf16[8,256,1024]{2,1,0:T(8,128)(2,1)S(1)} %copy-done, ...), custom_call_target="tpu_custom_call" | custom-call | flops 16777216 | bytes 2097152 | tf_op jit(solution)/shard_map/attend/pallas_call | solution.py:428
  33.7 0.0 slice-start.3
  33.7 1.2 %collective-permute-done.8.refs_3_ = bf16[2,64,128]{2,1,0:T(8,128)(2,1)S(1)} collective-permute-done((bf16[2,64,128]{2,1,0:T(8,128)(2,1)S(1)}, bf16[2,64,128]{2,1,0:T(8,128)(2,1)S(1)}, u32[]{:S(2)}, u32[]{:S(2)}) %collective-permute-start.8) | collective-permute-done | bytes 32800 | tf_op jit(solution)/shard_map/ppermute | solution.py:554
  35.0 0.9 %attend.9 = bf16[8,96,128]{2,1,0:T(8,128)(2,1)S(1)} custom-call(s32[1]{0:T(128)} %bitcast.place.refs_0_, s32[1]{0:T(128)} %bitcast.1.bank.refs_1_, s32[64,128]{1,0:T(8,128)S(1)} %get-tuple-element.26.refs_2_, bf16[2,64,128]{2,1,0:T(8,128)(2,1)S(1)} %collective-permute-done.8.refs_3_, bf16[8,256,1024]{2,1,0:T(8,128)(2,1)S(1)} %copy-done, ...), custom_call_target="tpu_custom_call" | custom-call | flops 16777216 | bytes 16777216 | tf_op jit(solution)/shard_map/attend/pallas_call | solution.py:428
  35.8 11.7 %all_to_all.10.parts_ref = bf16[8,96,128]{2,1,0:T(8,128)(2,1)S(1)} all-to-all(bf16[8,96,128]{2,1,0:T(8,128)(2,1)S(1)} %attend.9), channel_id=1, replica_groups=mesh['groups'=2,'tensor'=8,'bank'=2] {'tensor'}, dimensions={0} | all-to-all | bytes 393216 | tf_op jit(solution)/shard_map/all_to_all | solution.py:546
  47.5 0.5 combine.1.x_ref
  48.0 0.0 slice-done
  48.0 0.0 slice-done.1
  48.1 0.0 slice-done.2
  48.1 0.0 slice-done.3
  48.1 2.3 %output.1 = bf16[8,8,1024]{2,1,0:T(8,128)(2,1)S(1)} custom-call(bf16[8,1024]{1,0:T(8,128)(2,1)S(1)} %combine.1.x_ref, bf16[1024,8192]{1,0:T(8,128)(2,1)S(1)} %bitcast.6), custom_call_target="tpu_custom_call" | custom-call | flops 134217728 | bytes 16777216 | tf_op jit(solution)/shard_map/output/pallas_call | solution.py:512
  50.4 9.8 %all_to_all.11.parts_ref = bf16[8,8,1024]{2,1,0:T(8,128)(2,1)S(1)} all-to-all(bf16[8,8,1024]{2,1,0:T(8,128)(2,1)S(1)} %output.1), channel_id=1, replica_groups=mesh['groups'=2,'tensor'=8,'bank'=2] {'tensor'}, dimensions={0} | all-to-all | bytes 262144 | tf_op jit(solution)/shard_map/all_to_all | solution.py:546
  60.1 0.6 %residual.1 = bf16[8,1024]{1,0:T(8,128)(2,1)} custom-call(bf16[8,1024]{1,0:T(8,128)(2,1)S(1)} %copy-done.3, bf16[8,8,1024]{2,1,0:T(8,128)(2,1)S(1)} %all_to_all.11.parts_ref), custom_call_target="tpu_custom_call" | custom-call | tf_op jit(solution)/shard_map/residual/pallas_call | solution.py:531
  (5 shorter events, 0.0 us)
Async XLA Ops:
  0.0 2.1 %copy-start.3 = (bf16[8,1024]{1,0:T(8,128)(2,1)S(1)}, bf16[8,1024]{1,0:T(8,128)(2,1)}, u32[]{:S(2)}) copy-start(bf16[8,1024]{1,0:T(8,128)(2,1)} %x_ref.7) | copy-start | bytes 49156
  0.0 2.1 %copy-start.4 = (s32[8]{0:T(128)S(1)}, s32[8]{0:T(128)}, u32[]{:S(2)}) copy-start(s32[8]{0:T(128)} %param.11) | copy-start | bytes 100
  0.0 2.1 %collective-permute-start = (bf16[8,1024]{1,0:T(8,128)(2,1)}, bf16[8,1024]{1,0:T(8,128)(2,1)S(1)}, u32[]{:S(2)}, u32[]{:S(2)}) collective-permute-start(bf16[8,1024]{1,0:T(8,128)(2,1)} %x_ref.7), channel_id=1, source_target_pairs={{0,1},{1,0},{2,3},{3,2},{4,5},{5,4},{6,7},{7,6},{8,9},{9,8},{10,11... | collective-permute-start | bytes 49160 | tf_op jit(solution)/shard_map/ppermute | solution.py:542
  0.5 1.6 %collective-permute-start.1 = (s32[8]{0:T(128)}, s32[8]{0:T(128)S(1)}, u32[]{:S(2)}, u32[]{:S(2)}) collective-permute-start(s32[8]{0:T(128)} %param.11), channel_id=1, source_target_pairs={{0,1},{1,0},{2,3},{3,2},{4,5},{5,4},{6,7},{7,6},{8,9},{9,8},{10,11... | collective-permute-start | bytes 104 | tf_op jit(solution)/shard_map/ppermute | solution.py:542
  2.1 6.1 %copy-start.5 = (s32[8]{0:T(128)S(1)}, s32[8]{0:T(128)}, u32[]{:S(2)}) copy-start(s32[8]{0:T(128)} %length.1) | copy-start | bytes 100
  5.2 6.3 %collective-permute-start.2 = (f32[4,16,640]{2,1,0:T(8,128)S(1)}, f32[4,16,640]{2,1,0:T(8,128)S(1)}, u32[]{:S(2)}, u32[]{:S(2)}) collective-permute-start(f32[4,16,640]{2,1,0:T(8,128)S(1)} %get-tuple-element.29), channel_id=1, source_target_pairs={{0,2},{1,5},{2,0},{3,7},{4,6},{5,1},{6,4},{7,3},{8,10},{9,13},{10,... | collective-permute-start | bytes 491528 | tf_op jit(solution)/shard_map/ppermute | solution.py:554
  8.2 12.4 %copy-start.2 = (bf16[16,64,1024]{2,1,0:T(8,128)(2,1)S(1)}, bf16[16,64,1024]{2,1,0:T(8,128)(2,1)}, u32[]{:S(2)}) copy-start(bf16[16,64,1024]{2,1,0:T(8,128)(2,1)} %up_ref.1) | copy-start | bytes 6291460
  8.2 15.7 %copy-start.1 = (bf16[8,256,1024]{2,1,0:T(8,128)(2,1)S(1)}, bf16[8,256,1024]{2,1,0:T(8,128)(2,1)}, u32[]{:S(2)}) copy-start(bf16[8,256,1024]{2,1,0:T(8,128)(2,1)} %refs_5_.9) | copy-start | bytes 12582916
  11.5 12.4 %copy-start = (bf16[8,256,1024]{2,1,0:T(8,128)(2,1)S(1)}, bf16[8,256,1024]{2,1,0:T(8,128)(2,1)}, u32[]{:S(2)}) copy-start(bf16[8,256,1024]{2,1,0:T(8,128)(2,1)} %refs_4_.9) | copy-start | bytes 12582916
  11.5 7.3 %collective-permute-start.3 = (f32[16,640]{1,0:T(8,128)S(1)}, f32[16,640]{1,0:T(8,128)S(1)}, u32[]{:S(2)}, u32[]{:S(2)}) collective-permute-start(f32[16,640]{1,0:T(8,128)S(1)} %get-tuple-element.32), channel_id=1, source_target_pairs={{0,12},{1,11},{2,14},{3,9},{4,8},{5,15},{6,10},{7,13},{8,4},{9,3},... | collective-permute-start | bytes 122888 | tf_op jit(solution)/shard_map/ppermute | solution.py:554
  15.7 4.9 %collective-permute-start.4 = (f32[16,640]{1,0:T(8,128)S(1)}, f32[16,640]{1,0:T(8,128)S(1)}, u32[]{:S(2)}, u32[]{:S(2)}) collective-permute-start(f32[16,640]{1,0:T(8,128)S(1)} %get-tuple-element.33), channel_id=1, source_target_pairs={{0,8},{1,9},{2,10},{3,11},{4,12},{5,13},{6,14},{7,15},{8,0},{9,1},... | collective-permute-start | bytes 122888 | tf_op jit(solution)/shard_map/ppermute | solution.py:554
  15.7 4.9 %collective-permute-start.5 = (f32[16,640]{1,0:T(8,128)S(1)}, f32[16,640]{1,0:T(8,128)S(1)}, u32[]{:S(2)}, u32[]{:S(2)}) collective-permute-start(f32[16,640]{1,0:T(8,128)S(1)} %get-tuple-element.34), channel_id=1, source_target_pairs={{0,4},{1,3},{2,6},{3,1},{4,0},{5,7},{6,2},{7,5},{8,12},{9,11},{10,... | collective-permute-start | bytes 122888 | tf_op jit(solution)/shard_map/ppermute | solution.py:554
  21.0 1.2 %collective-permute-start.6 = (f32[8,1024]{1,0:T(8,128)S(1)}, f32[8,1024]{1,0:T(8,128)S(1)}, u32[]{:S(2)}, u32[]{:S(2)}) collective-permute-start(f32[8,1024]{1,0:T(8,128)S(1)} %get-tuple-element.40), channel_id=1, source_target_pairs={{0,1},{1,0},{2,3},{3,2},{4,5},{5,4},{6,7},{7,6},{8,9},{9,8},{10,11... | collective-permute-start | bytes 98312 | tf_op jit(solution)/shard_map/ppermute | solution.py:542
  22.3 3.8 %collective-permute-start.7 = (bf16[1,64,128]{2,1,0:T(8,128)(2,1)S(1)}, bf16[1,64,128]{2,1,0:T(8,128)(2,1)S(1)}, u32[]{:S(2)}, u32[]{:S(2)}) collective-permute-start(bf16[1,64,128]{2,1,0:T(8,128)(2,1)S(1)} %rotate.1.refs_3_.refs_0_.q_ref), channel_id=1, source_target_pairs={{0,2},{1,5},{2,0},{3,7},{4,6},{5,1},{6,4},{7,3},{8,10},{9,13},{10,... | collective-permute-start | bytes 49160 | tf_op jit(solution)/shard_map/ppermute | solution.py:554
  26.1 21.9 %slice-start = ((s8[16777216]{0:T(1024)(128)(4,1)}), s8[4194304]{0:T(1024)(128)(4,1)S(1)}, s32[]{:S(2)}) async-start(s8[16777216]{0:T(1024)(128)(4,1)} %bitcast.5), calls=%async_computation.2 | async-start | bytes 8388608
  26.6 21.4 %slice-start.1 = ((s8[16777216]{0:T(1024)(128)(4,1)}), s8[4194304]{0:T(1024)(128)(4,1)S(1)}, s32[]{:S(2)}) async-start(s8[16777216]{0:T(1024)(128)(4,1)} %bitcast.5), calls=%async_computation.3 | async-start | bytes 8388608
  26.6 4.3 %collective-permute-start.10 = (bf16[2,64,128]{2,1,0:T(8,128)(2,1)S(1)}, bf16[2,64,128]{2,1,0:T(8,128)(2,1)S(1)}, u32[]{:S(2)}, u32[]{:S(2)}) collective-permute-start(bf16[2,64,128]{2,1,0:T(8,128)(2,1)S(1)} %join.1), channel_id=1, source_target_pairs={{0,4},{1,3},{2,6},{3,1},{4,0},{5,7},{6,2},{7,5},{8,12},{9,11},{10,... | collective-permute-start | bytes 98312 | tf_op jit(solution)/shard_map/ppermute | solution.py:554
  26.7 6.2 %collective-permute-start.9 = (bf16[2,64,128]{2,1,0:T(8,128)(2,1)S(1)}, bf16[2,64,128]{2,1,0:T(8,128)(2,1)S(1)}, u32[]{:S(2)}, u32[]{:S(2)}) collective-permute-start(bf16[2,64,128]{2,1,0:T(8,128)(2,1)S(1)} %join.1), channel_id=1, source_target_pairs={{0,12},{1,11},{2,14},{3,9},{4,8},{5,15},{6,10},{7,13},{8,4},{9,3},... | collective-permute-start | bytes 98312 | tf_op jit(solution)/shard_map/ppermute | solution.py:554
  30.1 4.8 %collective-permute-start.8 = (bf16[2,64,128]{2,1,0:T(8,128)(2,1)S(1)}, bf16[2,64,128]{2,1,0:T(8,128)(2,1)S(1)}, u32[]{:S(2)}, u32[]{:S(2)}) collective-permute-start(bf16[2,64,128]{2,1,0:T(8,128)(2,1)S(1)} %join.1), channel_id=1, source_target_pairs={{0,8},{1,9},{2,10},{3,11},{4,12},{5,13},{6,14},{7,15},{8,0},{9,1},... | collective-permute-start | bytes 98312 | tf_op jit(solution)/shard_map/ppermute | solution.py:554
  31.8 16.3 %slice-start.2 = ((s8[16777216]{0:T(1024)(128)(4,1)}), s8[4194304]{0:T(1024)(128)(4,1)S(1)}, s32[]{:S(2)}) async-start(s8[16777216]{0:T(1024)(128)(4,1)} %bitcast.5), calls=%async_computation.4 | async-start | bytes 8388608
  33.7 14.4 %slice-start.3 = ((s8[16777216]{0:T(1024)(128)(4,1)}), s8[4194304]{0:T(1024)(128)(4,1)S(1)}, s32[]{:S(2)}) async-start(s8[16777216]{0:T(1024)(128)(4,1)} %bitcast.5), calls=%async_computation.5 | async-start | bytes 8388608

commit v18 on v17

--- a/solution.py
+++ b/solution.py
@@ -586,7 +586,7 @@
         place, bank, beam_cache_length, x, x_other, weight, inner, ranks
     )
     kept, *sent = part(kept, came)
-    near = tuple(range(ranks - 2, 0, -2))
+    near = 4, 6, 2
     parts = [kept] + [hop(sent[slot // 2 - 1], slot) for slot in near]
     token_weight, _ = lax.optimization_barrier((in_hbm(keyvalue_weight), kept))
     token, parts = lax.optimization_barrier((keyval(x, in_hbm(token_weight), ranks), parts))
@@ -597,20 +597,11 @@
         cache = paged_key_cache, paged_value_cache
         return attend(place, bank, length, queries, *cache, slots, **more)
 
-    came, done = lax.optimization_barrier((hop(query, 1), attended_part(query, (0,))))
-    pair = join([query, came])
-    pairs = [hop(pair, slot) for slot in near[:-1]]
-    done = [done, attended_part(came, (1,))]
-    held, _ = lax.optimization_barrier((pair, done[1]))
-    pairs.append(hop(held, near[-1]))
-    slots = [0, 1]
-    for i in (0, 2):
-        slots += [near[i], near[i] + 1]
-        done.append(attended_part(pairs[i], tuple(slots[-2:])))
-    last = near[1], near[1] + 1
-    partial = attended_part(
-        pairs[1], last, earlier=tuple(slots), before=(*done, token)
-    )
+    gathered = join([query] + [hop(query, slot) for slot in near])
+    came = hop(gathered, 1)
+    done = attended_part(gathered, (0, *near))
+    odd = tuple(slot + 1 for slot in (0, *near))
+    partial = attended_part(came, odd, earlier=(0, *near), before=(done, token))
     attended = combine(traded(partial), query, cosine, sine)
     return residual(x, traded(output(attended, output_weight, ranks)))
 

time: 61 us -> 60.2 us (0.987)
    pallas_call x5 -> x2, Pallas kernels: 3.6 us -> 3.12 us  [attend(): pl.pallas_call(lambda *refs: attend_kernel(slots, earlier, *refs), in_spe...]
  transfers between devices with their start and end apart: 11 -> 11, of which waited for: 6 -> 5; matrix products, arithmetic and copies ran while one was open for 0% -> 0% of each run, Pallas kernels for 16% -> 15%
where the time goes in v18:
time: 60.2 us; the launch traced here: 60 us
  blocking collectives  21.5 us (36%)
  Pallas kernels  17.5 us (29%)
  starting transfers between devices  13.4 us (22%)
  waiting for transfers between devices  7.17 us (12%)
    all_to_all x2, blocking collectives, traded(): return lax.all_to_all(blocks, 'tensor', 0, 0, tiled=True)  21.5 us
    ppermute x8, starting transfers between devices, hop(): return lax.ppermute(x, ('tensor', 'bank'), pairs)  12.8 us
    ppermute x8, waiting for transfers between devices, hop(): return lax.ppermute(x, ('tensor', 'bank'), pairs)  6.07 us
    pallas_call x1, Pallas kernels, project_kept(): pl.pallas_call(project_kept_kernel, in_specs=[scalar()] * 3 + [whole()] *...  3.3 us
    pallas_call x2, Pallas kernels, attend(): pl.pallas_call(lambda *refs: attend_kernel(slots, earlier, *refs), in_spe...  3.12 us
    pallas_call x1, Pallas kernels, project_sent(): pl.pallas_call(project_sent_kernel, in_specs=[scalar()] * 2 + [whole()] *...  3.01 us
    pallas_call x1, Pallas kernels, keyval(): pl.pallas_call(keyval_kernel, in_specs=[whole(), big()], out_specs=whole(...  2.61 us
    pallas_call x1, Pallas kernels, output(): pl.pallas_call(output_kernel, in_specs=[whole()] * 2, out_specs=whole(),...  2.28 us
  transfers between devices with their start and end apart: 11, of which 5 were waited for; matrix products, arithmetic and copies ran while one was open for 0% of the time, Pallas kernels for 15%

profile of v18, /device:TPU:0, one launch (start us, length us, event | category | flops | bytes accessed | tf_op | source)
XLA Modules:
  0.0 60.0 jit_solution(2455249392374925129)
XLA Ops:
  0.0 0.0 copy-start.3
  0.0 0.0 copy-start.4
  0.0 0.5 collective-permute-start
  0.5 0.1 collective-permute-start.1
  0.5 1.6 %fetch.1.down_ref = bf16[16,64,1024]{2,1,0:T(8,128)(2,1)S(1)} custom-call(bf16[16,64,1024]{2,1,0:T(8,128)(2,1)} %bitcast.9), custom_call_target="tpu_custom_call" | custom-call | bytes 2097152 | tf_op jit(solution)/shard_map/fetch/pallas_call | solution.py:109
  2.1 0.0 collective-permute-done.1
  2.1 0.0 collective-permute-done.other_ref
  2.1 0.0 copy-done.3
  2.1 0.0 copy-done.4
  2.1 0.0 copy-start.5
  2.1 3.0 %project_sent.1 = (f32[4,16,640]{2,1,0:T(8,128)S(1)}, f32[16,128]{1,0:T(8,128)S(1)}, s32[16,128]{1,0:T(8,128)S(1)}) custom-call(s32[1]{0:T(128)} %bitcast.place.refs_0_, s32[1]{0:T(128)} %bitcast.1.bank.refs_1_, s32[1,8]{1,0:T(1,128)S(1)} %bitcast.7, s32[1,8]{1,0:T(1,128)S(1)} %bitcast.8, bf16[8,1024]{1,0:T(8,128)(2,1)S(1)} %copy-done.3, ...), custom_call_target="tpu_custom_call" | custom-call | flops 100663296 | bytes 6291456 | tf_op jit(solution)/shard_map/project_sent/pallas_call | solution.py:167
  5.2 3.0 %collective-permute-start.2 = (f32[4,16,640]{2,1,0:T(8,128)S(1)}, f32[4,16,640]{2,1,0:T(8,128)S(1)}, u32[]{:S(2)}, u32[]{:S(2)}) collective-permute-start(f32[4,16,640]{2,1,0:T(8,128)S(1)} %get-tuple-element.26), channel_id=1, source_target_pairs={{0,2},{1,5},{2,0},{3,7},{4,6},{5,1},{6,4},{7,3},{8,10},{9,13},{10,... | collective-permute-start | bytes 491528 | tf_op jit(solution)/shard_map/ppermute | solution.py:554
  8.2 0.0 copy-done.5
  8.2 0.0 copy-start.2
  8.2 0.0 copy-start.1
  8.2 0.0 slice-start
  8.2 0.0 slice-start.1
  8.2 3.3 %project_kept.1 = (f32[4,16,640]{2,1,0:T(8,128)S(1)}, s32[64,128]{1,0:T(8,128)S(1)}) custom-call(s32[1]{0:T(128)} %bitcast.place.refs_0_, s32[1]{0:T(128)} %bitcast.1.bank.refs_1_, s32[8]{0:T(128)S(1)} %copy-done.5, bf16[8,1024]{1,0:T(8,128)(2,1)S(1)} %copy-done.3, bf16[8,1024]{1,0:T(8,128)(2,1)S(1)} %collective-permute-done.other_ref, ...), custom_call_target="tpu_custom_call" | custom-call | flops 67108864 | bytes 16777216 | tf_op jit(solution)/shard_map/project_kept/pallas_call | solution.py:207
  11.5 0.0 copy-start
  11.5 0.0 collective-permute-done.2.came_ref
  11.6 3.1 %collective-permute-start.3 = (f32[16,640]{1,0:T(8,128)S(1)}, f32[16,640]{1,0:T(8,128)S(1)}, u32[]{:S(2)}, u32[]{:S(2)}) collective-permute-start(f32[16,640]{1,0:T(8,128)S(1)} %get-tuple-element.29), channel_id=1, source_target_pairs={{0,8},{1,9},{2,10},{3,11},{4,12},{5,13},{6,14},{7,15},{8,0},{9,1},... | collective-permute-start | bytes 122888 | tf_op jit(solution)/shard_map/ppermute | solution.py:554
  14.7 1.3 %collective-permute-start.4 = (f32[16,640]{1,0:T(8,128)S(1)}, f32[16,640]{1,0:T(8,128)S(1)}, u32[]{:S(2)}, u32[]{:S(2)}) collective-permute-start(f32[16,640]{1,0:T(8,128)S(1)} %get-tuple-element.30), channel_id=1, source_target_pairs={{0,12},{1,11},{2,14},{3,9},{4,8},{5,15},{6,10},{7,13},{8,4},{9,3},... | collective-permute-start | bytes 122888 | tf_op jit(solution)/shard_map/ppermute | solution.py:554
  16.0 0.2 collective-permute-start.5
  16.3 0.0 slice-start.2
  16.3 2.6 %keyval.1.refs_7_ = f32[8,24,128]{2,1,0:T(8,128)S(1)} custom-call(bf16[8,1024]{1,0:T(8,128)(2,1)S(1)} %copy-done.3, bf16[1024,2048]{1,0:T(8,128)(2,1)} %w_ref.5), custom_call_target="tpu_custom_call" | custom-call | flops 33554432 | bytes 4194304 | tf_op jit(solution)/shard_map/keyval/pallas_call | solution.py:246
  18.9 0.0 collective-permute-done.3.refs_1_
  18.9 1.6 %collective-permute-done.4.refs_2_ = f32[16,640]{1,0:T(8,128)S(1)} collective-permute-done((f32[16,640]{1,0:T(8,128)S(1)}, f32[16,640]{1,0:T(8,128)S(1)}, u32[]{:S(2)}, u32[]{:S(2)}) %collective-permute-start.4) | collective-permute-done | bytes 40992 | tf_op jit(solution)/shard_map/ppermute | solution.py:554
  20.5 0.0 collective-permute-done.5.refs_3_
  20.5 0.0 copy-done.2
  20.5 0.4 correct.1
  20.9 0.0 collective-permute-start.6
  20.9 0.1 fusion
  21.0 1.1 %collective-permute-done.6.came_ref = f32[8,1024]{1,0:T(8,128)S(1)} collective-permute-done((f32[8,1024]{1,0:T(8,128)S(1)}, f32[8,1024]{1,0:T(8,128)S(1)}, u32[]{:S(2)}, u32[]{:S(2)}) %collective-permute-start.6) | collective-permute-done | bytes 32800 | tf_op jit(solution)/shard_map/ppermute | solution.py:542
  22.1 0.1 rotate.1.refs_0_.q_ref
  22.2 1.3 %collective-permute-start.7 = (bf16[1,64,128]{2,1,0:T(8,128)(2,1)S(1)}, bf16[1,64,128]{2,1,0:T(8,128)(2,1)S(1)}, u32[]{:S(2)}, u32[]{:S(2)}) collective-permute-start(bf16[1,64,128]{2,1,0:T(8,128)(2,1)S(1)} %rotate.1.refs_0_.q_ref), channel_id=1, source_target_pairs={{0,8},{1,9},{2,10},{3,11},{4,12},{5,13},{6,14},{7,15},{8,0},{9,1},... | collective-permute-start | bytes 49160 | tf_op jit(solution)/shard_map/ppermute | solution.py:554
  23.5 1.3 %collective-permute-start.8 = (bf16[1,64,128]{2,1,0:T(8,128)(2,1)S(1)}, bf16[1,64,128]{2,1,0:T(8,128)(2,1)S(1)}, u32[]{:S(2)}, u32[]{:S(2)}) collective-permute-start(bf16[1,64,128]{2,1,0:T(8,128)(2,1)S(1)} %rotate.1.refs_0_.q_ref), channel_id=1, source_target_pairs={{0,12},{1,11},{2,14},{3,9},{4,8},{5,15},{6,10},{7,13},{8,4},{9,3},... | collective-permute-start | bytes 49160 | tf_op jit(solution)/shard_map/ppermute | solution.py:554
  24.9 0.9 %collective-permute-start.9 = (bf16[1,64,128]{2,1,0:T(8,128)(2,1)S(1)}, bf16[1,64,128]{2,1,0:T(8,128)(2,1)S(1)}, u32[]{:S(2)}, u32[]{:S(2)}) collective-permute-start(bf16[1,64,128]{2,1,0:T(8,128)(2,1)S(1)} %rotate.1.refs_0_.q_ref), channel_id=1, source_target_pairs={{0,4},{1,3},{2,6},{3,1},{4,0},{5,7},{6,2},{7,5},{8,12},{9,11},{10,... | collective-permute-start | bytes 49160 | tf_op jit(solution)/shard_map/ppermute | solution.py:554
  25.7 1.1 %collective-permute-done.7.refs_1_ = bf16[1,64,128]{2,1,0:T(8,128)(2,1)S(1)} collective-permute-done((bf16[1,64,128]{2,1,0:T(8,128)(2,1)S(1)}, bf16[1,64,128]{2,1,0:T(8,128)(2,1)S(1)}, u32[]{:S(2)}, u32[]{:S(2)}) %collective-permute-start.7) | collective-permute-done | bytes 16416 | tf_op jit(solution)/shard_map/ppermute | solution.py:554
  26.9 2.2 %collective-permute-done.8.refs_2_ = bf16[1,64,128]{2,1,0:T(8,128)(2,1)S(1)} collective-permute-done((bf16[1,64,128]{2,1,0:T(8,128)(2,1)S(1)}, bf16[1,64,128]{2,1,0:T(8,128)(2,1)S(1)}, u32[]{:S(2)}, u32[]{:S(2)}) %collective-permute-start.8) | collective-permute-done | bytes 16416 | tf_op jit(solution)/shard_map/ppermute | solution.py:554
  29.1 0.0 collective-permute-done.9.refs_3_
  29.1 1.6 %collective-permute-start.10 = (bf16[4,64,128]{2,1,0:T(8,128)(2,1)S(1)}, bf16[4,64,128]{2,1,0:T(8,128)(2,1)S(1)}, u32[]{:S(2)}, u32[]{:S(2)}) collective-permute-start(bf16[4,64,128]{2,1,0:T(8,128)(2,1)S(1)} %join.1.refs_3_), channel_id=1, source_target_pairs={{0,2},{1,5},{2,0},{3,7},{4,6},{5,1},{6,4},{7,3},{8,10},{9,13},{10,... | collective-permute-start | bytes 196616 | tf_op jit(solution)/shard_map/ppermute | solution.py:554
  30.6 0.0 copy-done.1
  30.7 0.0 copy-done
  30.7 0.0 slice-start.3
  30.7 1.6 %attend.2.refs_6_ = bf16[4,80,128]{2,1,0:T(8,128)(2,1)S(1)} custom-call(s32[1]{0:T(128)} %bitcast.place.refs_0_, s32[1]{0:T(128)} %bitcast.1.bank.refs_1_, s32[64,128]{1,0:T(8,128)S(1)} %get-tuple-element.23.refs_2_, bf16[4,64,128]{2,1,0:T(8,128)(2,1)S(1)} %join.1.refs_3_, bf16[8,256,1024]{2,1,0:T(8,128)(2,1)S(1)} %copy-done, bf16[8,256,1024]{2,1,0:T(8,128)(2,1)S(1)} %copy-done.1), custom_call_target="tpu_custom_call" | custom-call | flops 33554432 | bytes 4194304 | tf_op jit(solution)/shard_map/attend/pallas_call | solution.py:428
  32.2 1.2 %collective-permute-done.10.refs_3_ = bf16[4,64,128]{2,1,0:T(8,128)(2,1)S(1)} collective-permute-done((bf16[4,64,128]{2,1,0:T(8,128)(2,1)S(1)}, bf16[4,64,128]{2,1,0:T(8,128)(2,1)S(1)}, u32[]{:S(2)}, u32[]{:S(2)}) %collective-permute-start.10) | collective-permute-done | bytes 65568 | tf_op jit(solution)/shard_map/ppermute | solution.py:554
  33.4 1.6 %attend.3 = bf16[8,96,128]{2,1,0:T(8,128)(2,1)S(1)} custom-call(s32[1]{0:T(128)} %bitcast.place.refs_0_, s32[1]{0:T(128)} %bitcast.1.bank.refs_1_, s32[64,128]{1,0:T(8,128)S(1)} %get-tuple-element.23.refs_2_, bf16[4,64,128]{2,1,0:T(8,128)(2,1)S(1)} %collective-permute-done.10.refs_3_, bf16[8,256,1024]{2,1,0:T(8,128)(2,1)S(1)} %copy-done, ...), custom_call_target="tpu_custom_call" | custom-call | flops 33554432 | bytes 16777216 | tf_op jit(solution)/shard_map/attend/pallas_call | solution.py:428
  35.0 11.8 %all_to_all.10.parts_ref = bf16[8,96,128]{2,1,0:T(8,128)(2,1)S(1)} all-to-all(bf16[8,96,128]{2,1,0:T(8,128)(2,1)S(1)} %attend.3), channel_id=1, replica_groups=mesh['groups'=2,'tensor'=8,'bank'=2] {'tensor'}, dimensions={0} | all-to-all | bytes 393216 | tf_op jit(solution)/shard_map/all_to_all | solution.py:546
  46.7 0.5 combine.1.x_ref
  47.2 0.0 slice-done
  47.2 0.0 slice-done.1
  47.2 0.0 slice-done.2
  47.2 0.0 slice-done.3
  47.3 2.3 %output.1 = bf16[8,8,1024]{2,1,0:T(8,128)(2,1)S(1)} custom-call(bf16[8,1024]{1,0:T(8,128)(2,1)S(1)} %combine.1.x_ref, bf16[1024,8192]{1,0:T(8,128)(2,1)S(1)} %bitcast.6), custom_call_target="tpu_custom_call" | custom-call | flops 134217728 | bytes 16777216 | tf_op jit(solution)/shard_map/output/pallas_call | solution.py:512
  49.5 9.8 %all_to_all.11.parts_ref = bf16[8,8,1024]{2,1,0:T(8,128)(2,1)S(1)} all-to-all(bf16[8,8,1024]{2,1,0:T(8,128)(2,1)S(1)} %output.1), channel_id=1, replica_groups=mesh['groups'=2,'tensor'=8,'bank'=2] {'tensor'}, dimensions={0} | all-to-all | bytes 262144 | tf_op jit(solution)/shard_map/all_to_all | solution.py:546
  59.3 0.6 %residual.1 = bf16[8,1024]{1,0:T(8,128)(2,1)} custom-call(bf16[8,1024]{1,0:T(8,128)(2,1)S(1)} %copy-done.3, bf16[8,8,1024]{2,1,0:T(8,128)(2,1)S(1)} %all_to_all.11.parts_ref), custom_call_target="tpu_custom_call" | custom-call | tf_op jit(solution)/shard_map/residual/pallas_call | solution.py:531
  (5 shorter events, 0.0 us)
Async XLA Ops:
  0.0 2.1 %copy-start.3 = (bf16[8,1024]{1,0:T(8,128)(2,1)S(1)}, bf16[8,1024]{1,0:T(8,128)(2,1)}, u32[]{:S(2)}) copy-start(bf16[8,1024]{1,0:T(8,128)(2,1)} %x_ref.7) | copy-start | bytes 49156
  0.0 2.1 %copy-start.4 = (s32[8]{0:T(128)S(1)}, s32[8]{0:T(128)}, u32[]{:S(2)}) copy-start(s32[8]{0:T(128)} %param.11) | copy-start | bytes 100
  0.0 2.1 %collective-permute-start = (bf16[8,1024]{1,0:T(8,128)(2,1)}, bf16[8,1024]{1,0:T(8,128)(2,1)S(1)}, u32[]{:S(2)}, u32[]{:S(2)}) collective-permute-start(bf16[8,1024]{1,0:T(8,128)(2,1)} %x_ref.7), channel_id=1, source_target_pairs={{0,1},{1,0},{2,3},{3,2},{4,5},{5,4},{6,7},{7,6},{8,9},{9,8},{10,11... | collective-permute-start | bytes 49160 | tf_op jit(solution)/shard_map/ppermute | solution.py:542
  0.5 1.6 %collective-permute-start.1 = (s32[8]{0:T(128)}, s32[8]{0:T(128)S(1)}, u32[]{:S(2)}, u32[]{:S(2)}) collective-permute-start(s32[8]{0:T(128)} %param.11), channel_id=1, source_target_pairs={{0,1},{1,0},{2,3},{3,2},{4,5},{5,4},{6,7},{7,6},{8,9},{9,8},{10,11... | collective-permute-start | bytes 104 | tf_op jit(solution)/shard_map/ppermute | solution.py:542
  2.1 6.1 %copy-start.5 = (s32[8]{0:T(128)S(1)}, s32[8]{0:T(128)}, u32[]{:S(2)}) copy-start(s32[8]{0:T(128)} %length.1) | copy-start | bytes 100
  5.2 6.4 %collective-permute-start.2 = (f32[4,16,640]{2,1,0:T(8,128)S(1)}, f32[4,16,640]{2,1,0:T(8,128)S(1)}, u32[]{:S(2)}, u32[]{:S(2)}) collective-permute-start(f32[4,16,640]{2,1,0:T(8,128)S(1)} %get-tuple-element.26), channel_id=1, source_target_pairs={{0,2},{1,5},{2,0},{3,7},{4,6},{5,1},{6,4},{7,3},{8,10},{9,13},{10,... | collective-permute-start | bytes 491528 | tf_op jit(solution)/shard_map/ppermute | solution.py:554
  8.2 12.3 %copy-start.2 = (bf16[16,64,1024]{2,1,0:T(8,128)(2,1)S(1)}, bf16[16,64,1024]{2,1,0:T(8,128)(2,1)}, u32[]{:S(2)}) copy-start(bf16[16,64,1024]{2,1,0:T(8,128)(2,1)} %up_ref.1) | copy-start | bytes 6291460
  8.2 22.5 %copy-start.1 = (bf16[8,256,1024]{2,1,0:T(8,128)(2,1)S(1)}, bf16[8,256,1024]{2,1,0:T(8,128)(2,1)}, u32[]{:S(2)}) copy-start(bf16[8,256,1024]{2,1,0:T(8,128)(2,1)} %refs_5_.3) | copy-start | bytes 12582916
  8.2 39.0 %slice-start = ((s8[16777216]{0:T(1024)(128)(4,1)}), s8[4194304]{0:T(1024)(128)(4,1)S(1)}, s32[]{:S(2)}) async-start(s8[16777216]{0:T(1024)(128)(4,1)} %bitcast.5), calls=%async_computation.2 | async-start | bytes 8388608
  8.2 39.0 %slice-start.1 = ((s8[16777216]{0:T(1024)(128)(4,1)}), s8[4194304]{0:T(1024)(128)(4,1)S(1)}, s32[]{:S(2)}) async-start(s8[16777216]{0:T(1024)(128)(4,1)} %bitcast.5), calls=%async_computation.3 | async-start | bytes 8388608
  11.5 19.1 %copy-start = (bf16[8,256,1024]{2,1,0:T(8,128)(2,1)S(1)}, bf16[8,256,1024]{2,1,0:T(8,128)(2,1)}, u32[]{:S(2)}) copy-start(bf16[8,256,1024]{2,1,0:T(8,128)(2,1)} %refs_4_.3) | copy-start | bytes 12582916
  11.6 7.3 %collective-permute-start.3 = (f32[16,640]{1,0:T(8,128)S(1)}, f32[16,640]{1,0:T(8,128)S(1)}, u32[]{:S(2)}, u32[]{:S(2)}) collective-permute-start(f32[16,640]{1,0:T(8,128)S(1)} %get-tuple-element.29), channel_id=1, source_target_pairs={{0,8},{1,9},{2,10},{3,11},{4,12},{5,13},{6,14},{7,15},{8,0},{9,1},... | collective-permute-start | bytes 122888 | tf_op jit(solution)/shard_map/ppermute | solution.py:554
  14.7 5.8 %collective-permute-start.4 = (f32[16,640]{1,0:T(8,128)S(1)}, f32[16,640]{1,0:T(8,128)S(1)}, u32[]{:S(2)}, u32[]{:S(2)}) collective-permute-start(f32[16,640]{1,0:T(8,128)S(1)} %get-tuple-element.30), channel_id=1, source_target_pairs={{0,12},{1,11},{2,14},{3,9},{4,8},{5,15},{6,10},{7,13},{8,4},{9,3},... | collective-permute-start | bytes 122888 | tf_op jit(solution)/shard_map/ppermute | solution.py:554
  16.0 4.5 %collective-permute-start.5 = (f32[16,640]{1,0:T(8,128)S(1)}, f32[16,640]{1,0:T(8,128)S(1)}, u32[]{:S(2)}, u32[]{:S(2)}) collective-permute-start(f32[16,640]{1,0:T(8,128)S(1)} %get-tuple-element.31), channel_id=1, source_target_pairs={{0,4},{1,3},{2,6},{3,1},{4,0},{5,7},{6,2},{7,5},{8,12},{9,11},{10,... | collective-permute-start | bytes 122888 | tf_op jit(solution)/shard_map/ppermute | solution.py:554
  16.3 31.0 %slice-start.2 = ((s8[16777216]{0:T(1024)(128)(4,1)}), s8[4194304]{0:T(1024)(128)(4,1)S(1)}, s32[]{:S(2)}) async-start(s8[16777216]{0:T(1024)(128)(4,1)} %bitcast.5), calls=%async_computation.4 | async-start | bytes 8388608
  20.9 1.2 %collective-permute-start.6 = (f32[8,1024]{1,0:T(8,128)S(1)}, f32[8,1024]{1,0:T(8,128)S(1)}, u32[]{:S(2)}, u32[]{:S(2)}) collective-permute-start(f32[8,1024]{1,0:T(8,128)S(1)} %get-tuple-element.37), channel_id=1, source_target_pairs={{0,1},{1,0},{2,3},{3,2},{4,5},{5,4},{6,7},{7,6},{8,9},{9,8},{10,11... | collective-permute-start | bytes 98312 | tf_op jit(solution)/shard_map/ppermute | solution.py:542
  22.2 4.7 %collective-permute-start.7 = (bf16[1,64,128]{2,1,0:T(8,128)(2,1)S(1)}, bf16[1,64,128]{2,1,0:T(8,128)(2,1)S(1)}, u32[]{:S(2)}, u32[]{:S(2)}) collective-permute-start(bf16[1,64,128]{2,1,0:T(8,128)(2,1)S(1)} %rotate.1.refs_0_.q_ref), channel_id=1, source_target_pairs={{0,8},{1,9},{2,10},{3,11},{4,12},{5,13},{6,14},{7,15},{8,0},{9,1},... | collective-permute-start | bytes 49160 | tf_op jit(solution)/shard_map/ppermute | solution.py:554
  23.5 5.5 %collective-permute-start.8 = (bf16[1,64,128]{2,1,0:T(8,128)(2,1)S(1)}, bf16[1,64,128]{2,1,0:T(8,128)(2,1)S(1)}, u32[]{:S(2)}, u32[]{:S(2)}) collective-permute-start(bf16[1,64,128]{2,1,0:T(8,128)(2,1)S(1)} %rotate.1.refs_0_.q_ref), channel_id=1, source_target_pairs={{0,12},{1,11},{2,14},{3,9},{4,8},{5,15},{6,10},{7,13},{8,4},{9,3},... | collective-permute-start | bytes 49160 | tf_op jit(solution)/shard_map/ppermute | solution.py:554
  24.9 4.2 %collective-permute-start.9 = (bf16[1,64,128]{2,1,0:T(8,128)(2,1)S(1)}, bf16[1,64,128]{2,1,0:T(8,128)(2,1)S(1)}, u32[]{:S(2)}, u32[]{:S(2)}) collective-permute-start(bf16[1,64,128]{2,1,0:T(8,128)(2,1)S(1)} %rotate.1.refs_0_.q_ref), channel_id=1, source_target_pairs={{0,4},{1,3},{2,6},{3,1},{4,0},{5,7},{6,2},{7,5},{8,12},{9,11},{10,... | collective-permute-start | bytes 49160 | tf_op jit(solution)/shard_map/ppermute | solution.py:554
  29.1 4.3 %collective-permute-start.10 = (bf16[4,64,128]{2,1,0:T(8,128)(2,1)S(1)}, bf16[4,64,128]{2,1,0:T(8,128)(2,1)S(1)}, u32[]{:S(2)}, u32[]{:S(2)}) collective-permute-start(bf16[4,64,128]{2,1,0:T(8,128)(2,1)S(1)} %join.1.refs_3_), channel_id=1, source_target_pairs={{0,2},{1,5},{2,0},{3,7},{4,6},{5,1},{6,4},{7,3},{8,10},{9,13},{10,... | collective-permute-start | bytes 196616 | tf_op jit(solution)/shard_map/ppermute | solution.py:554
  30.7 16.6 %slice-start.3 = ((s8[16777216]{0:T(1024)(128)(4,1)}), s8[4194304]{0:T(1024)(128)(4,1)S(1)}, s32[]{:S(2)}) async-start(s8[16777216]{0:T(1024)(128)(4,1)} %bitcast.5), calls=%async_computation.5 | async-start | bytes 8388608

commit v19 on v18

--- a/solution.py
+++ b/solution.py
@@ -156,10 +156,11 @@
         part = every[:, j * HEAD_DIM : (j + 1) * HEAD_DIM]
         total += jnp.where(lane // rank + j * per == column, part, 0.0)
     inner[...] = total
+    out[:, len(copies) * width :] = total
     for s, slot in enumerate(copies):
-        out[s, :, width:] = total
         wait_all(slot)
-        out[s, :, :width] = jnp.dot(x, w_buf[s], preferred_element_type=F32)
+        columns = slice(s * width, (s + 1) * width)
+        out[:, columns] = jnp.dot(x, w_buf[s], preferred_element_type=F32)
 
 
 def project_sent(place, bank, index, x, other, down, wq, ranks):
@@ -169,7 +170,7 @@
         in_specs=[scalar()] * 2 + [whole()] * 5 + [big()],
         out_specs=[whole()] * 3,
         out_shape=[
-            shape(ranks // 2, rows, wq.shape[1] // ranks // 2 + HEAD_DIM),
+            shape(rows, wq.shape[1] // 4 + HEAD_DIM),
             shape(rows, HEAD_DIM),
             shape(rows, HEAD_DIM, dtype=jnp.int32),
         ],
@@ -185,7 +186,7 @@
 
 
 def project_kept_kernel(
-    place, bank, length, x_ref, other_ref, w_ref, inner, out, length_out, w_buf, sems
+    place, bank, length, x_ref, other_ref, w_ref, out, length_out, w_buf, sems
 ):
     copies = start_slots(0, place, bank, w_ref, w_buf, sems)
     width = w_buf.shape[2]
@@ -197,19 +198,19 @@
     length_out[...] = limit
     x = beam_rows(x_ref, other_ref)
     for s, slot in enumerate(copies):
-        out[s, :, width:] = inner[...]
         wait_all(slot)
-        out[s, :, :width] = jnp.dot(x, w_buf[s], preferred_element_type=F32)
-
-
-def project_kept(place, bank, length, x, other, wq, inner, ranks):
+        columns = slice(s * width, (s + 1) * width)
+        out[:, columns] = jnp.dot(x, w_buf[s], preferred_element_type=F32)
+
+
+def project_kept(place, bank, length, x, other, wq, ranks):
     beams = x.shape[0]
     return pl.pallas_call(
         project_kept_kernel,
-        in_specs=[scalar()] * 3 + [whole()] * 2 + [big(), whole()],
+        in_specs=[scalar()] * 3 + [whole()] * 2 + [big()],
         out_specs=[whole()] * 2,
         out_shape=[
-            shape(ranks // 2, 2 * beams, wq.shape[1] // ranks // 2 + HEAD_DIM),
+            shape(2 * beams, wq.shape[1] // 4),
             shape(beams * wq.shape[1] // ranks // HEAD_DIM, HEAD_DIM, dtype=jnp.int32),
         ],
         scratch_shapes=slot_scratch(wq, ranks),
@@ -218,7 +219,7 @@
             flops=beams * wq.size, bytes_accessed=2 * wq.size, transcendentals=0
         ),
         name="project_kept",
-    )(place, bank, length, x, other, wq, inner)
+    )(place, bank, length, x, other, wq)
 
 
 def keyval_kernel(x_ref, w_ref, out, w_buf, sems):
@@ -302,20 +303,25 @@
     )(bank, column, up, *parts)
 
 
-def part_kernel(kept_ref, came_ref, *outs):
+def part_kernel(kept_ref, inner_ref, came_ref, *outs):
+    width = outs[0].shape[1] - HEAD_DIM
+    inner = inner_ref[...] + came_ref[:, len(outs) * width :]
     for i, out in enumerate(outs):
-        out[...] = kept_ref[i] + came_ref[i]
-
-
-def part(kept, came):
+        columns = slice(i * width, (i + 1) * width)
+        out[:, :width] = kept_ref[:, columns] + came_ref[:, columns]
+        out[:, width:] = inner
+
+
+def part(kept, inner, came, slots):
+    rows, width = kept.shape
     return pl.pallas_call(
         part_kernel,
-        in_specs=[whole()] * 2,
-        out_specs=[whole()] * kept.shape[0],
-        out_shape=[shape(*kept.shape[1:])] * kept.shape[0],
+        in_specs=[whole()] * 3,
+        out_specs=[whole()] * slots,
+        out_shape=[shape(rows, width // slots + HEAD_DIM)] * slots,
         compiler_params=params(),
         name="part",
-    )(kept, came)
+    )(kept, inner, came)
 
 
 def rotate(v, cosine, sine):
@@ -450,37 +456,44 @@
     def by_row(v):
         return jnp.broadcast_to(v[:, None, :], (beams, group, HEAD_DIM)).reshape(rows, HEAD_DIM)
 
-    head = iota((rows, HEAD_DIM), 0) % group
     lane = iota((rows, HEAD_DIM), 1)
-    sums = jnp.sum(parts_ref[...].astype(F32)[:, rows + beams :], axis=0)
+    own_lane = lane == iota((rows, HEAD_DIM), 0) % group
+
+    def spread(v):
+        return jnp.sum(jnp.where(own_lane, by_row(v), 0.0), axis=1, keepdims=True)
+
+    blocks = [parts_ref[s].astype(F32) for s in range(ranks)]
+    sums = blocks[0][rows + beams :]
+    for block in blocks[1:]:
+        sums += block[rows + beams :]
     key = sums[:beams] + sums[beams : 2 * beams]
     key = rotate(key, cos_ref[...], sin_ref[...]).astype(BF16).astype(F32)
     value = sums[2 * beams :].astype(BF16).astype(F32)
     score = jnp.sum(q_ref[0].astype(F32) * by_row(key), axis=1, keepdims=True) * (
         1.0 / HEAD_DIM**0.5
     )
-    peaks, totals, weighted = [], [], []
+    score = jnp.where(own_lane, score, 0.0).reshape(beams, group, HEAD_DIM)
+    score = jnp.sum(score, axis=1)
+    used = iota((beams, HEAD_DIM), 1) < group
+    peaks, totals = [], []
     top = score
-    for s in range(ranks):
-        block = parts_ref[s].astype(F32)
+    for block in blocks:
         tail = block[rows : rows + beams]
+        stats = tail
         for turn in (2, 4):
-            tail += pltpu.roll(block[rows : rows + beams], HEAD_DIM - turn * group, 1)
-        tail = by_row(tail)
-        peak = jnp.sum(jnp.where(lane == head, tail, 0.0), axis=1, keepdims=True)
-        total = jnp.sum(jnp.where(lane == group + head, tail, 0.0), axis=1, keepdims=True)
-        top = jnp.maximum(top, peak)
-        peaks.append(peak)
-        totals.append(total)
-        weighted.append(block[:rows])
+            stats = stats + pltpu.roll(tail, HEAD_DIM - turn * group, 1)
+        peaks.append(jnp.where(used, stats, 0.0))
+        totals.append(jnp.where(used, pltpu.roll(stats, HEAD_DIM - group, 1), 0.0))
+        top = jnp.maximum(top, peaks[-1])
+    factors = [jnp.exp(peak - top) for peak in peaks]
     new = jnp.exp(score - top)
     everything = new
-    result = new.astype(BF16).astype(F32) * by_row(value)
-    for peak, total, block in zip(peaks, totals, weighted):
-        factor = jnp.exp(peak - top)
-        everything += total * factor
-        result += block * factor
-    joined[...] = (result / everything).reshape(joined.shape)
+    for factor, total in zip(factors, totals):
+        everything += factor * total
+    result = spread(new.astype(BF16).astype(F32) / everything) * by_row(value)
+    for block, factor in zip(blocks, factors):
+        result += spread(factor / everything) * block[:rows]
+    joined[...] = result.reshape(joined.shape)
     for g in range(group):
         out_ref[:, g * HEAD_DIM : (g + 1) * HEAD_DIM] = joined[:, g, :].astype(BF16)
 
@@ -583,9 +596,9 @@
     sent, inner, column = project_sent(place, bank, index, x, x_other, down, weight, ranks)
     came = hop(sent, 1)
     kept, length = project_kept(
-        place, bank, beam_cache_length, x, x_other, weight, inner, ranks
-    )
-    kept, *sent = part(kept, came)
+        place, bank, beam_cache_length, x, x_other, weight, ranks
+    )
+    kept, *sent = part(kept, inner, came, ranks // 2)
     near = 4, 6, 2
     parts = [kept] + [hop(sent[slot // 2 - 1], slot) for slot in near]
     token_weight, _ = lax.optimization_barrier((in_hbm(keyvalue_weight), kept))

time: 60.2 us -> 59.8 us (level)
  no operation moved by 1% of the time
where the time goes in v19:
time: 59.8 us; the launch traced here: 59.6 us
  blocking collectives  21.5 us (36%)
  Pallas kernels  17.4 us (29%)
  starting transfers between devices  13.1 us (22%)
  waiting for transfers between devices  7.17 us (12%)
    all_to_all x2, blocking collectives, traded(): return lax.all_to_all(blocks, 'tensor', 0, 0, tiled=True)  21.5 us
    ppermute x8, starting transfers between devices, hop(): return lax.ppermute(x, ('tensor', 'bank'), pairs)  12.6 us
    ppermute x8, waiting for transfers between devices, hop(): return lax.ppermute(x, ('tensor', 'bank'), pairs)  6.07 us
    pallas_call x1, Pallas kernels, project_kept(): pl.pallas_call(project_kept_kernel, in_specs=[scalar()] * 3 + [whole()] *...  3.3 us
    pallas_call x2, Pallas kernels, attend(): pl.pallas_call(lambda *refs: attend_kernel(slots, earlier, *refs), in_spe...  3.12 us
    pallas_call x1, Pallas kernels, project_sent(): pl.pallas_call(project_sent_kernel, in_specs=[scalar()] * 2 + [whole()] *...  3.01 us
    pallas_call x1, Pallas kernels, keyval(): pl.pallas_call(keyval_kernel, in_specs=[whole(), big()], out_specs=whole(...  2.61 us
    pallas_call x1, Pallas kernels, output(): pl.pallas_call(output_kernel, in_specs=[whole()] * 2, out_specs=whole(),...  2.28 us
  transfers between devices with their start and end apart: 11, of which 5 were waited for; matrix products, arithmetic and copies ran while one was open for 0% of the time, Pallas kernels for 15%

profile of v19, /device:TPU:0, one launch (start us, length us, event | category | flops | bytes accessed | tf_op | source)
XLA Modules:
  0.0 59.6 jit_solution(9671815400724530185)
XLA Ops:
  0.0 0.0 copy-start.3
  0.0 0.0 copy-start.4
  0.0 0.5 collective-permute-start
  0.5 0.1 collective-permute-start.1
  0.5 1.6 %fetch.1.down_ref = bf16[16,64,1024]{2,1,0:T(8,128)(2,1)S(1)} custom-call(bf16[16,64,1024]{2,1,0:T(8,128)(2,1)} %bitcast.9), custom_call_target="tpu_custom_call" | custom-call | bytes 2097152 | tf_op jit(solution)/shard_map/fetch/pallas_call | solution.py:109
  2.1 0.0 collective-permute-done.1
  2.1 0.0 collective-permute-done.other_ref
  2.1 0.0 copy-done.3
  2.1 0.0 copy-done.4
  2.1 0.0 copy-start.5
  2.1 3.0 %project_sent.1 = (f32[16,2176]{1,0:T(8,128)S(1)}, f32[16,128]{1,0:T(8,128)S(1)}, s32[16,128]{1,0:T(8,128)S(1)}) custom-call(s32[1]{0:T(128)} %bitcast.place.refs_0_, s32[1]{0:T(128)} %bitcast.1.bank.refs_1_, s32[1,8]{1,0:T(1,128)S(1)} %bitcast.7, s32[1,8]{1,0:T(1,128)S(1)} %bitcast.8, bf16[8,1024]{1,0:T(8,128)(2,1)S(1)} %copy-done.3, ...), custom_call_target="tpu_custom_call" | custom-call | flops 100663296 | bytes 6291456 | tf_op jit(solution)/shard_map/project_sent/pallas_call | solution.py:168
  5.2 3.0 %collective-permute-start.2 = (f32[16,2176]{1,0:T(8,128)S(1)}, f32[16,2176]{1,0:T(8,128)S(1)}, u32[]{:S(2)}, u32[]{:S(2)}) collective-permute-start(f32[16,2176]{1,0:T(8,128)S(1)} %get-tuple-element.26), channel_id=1, source_target_pairs={{0,2},{1,5},{2,0},{3,7},{4,6},{5,1},{6,4},{7,3},{8,10},{9,13},{10,... | collective-permute-start | bytes 417800 | tf_op jit(solution)/shard_map/ppermute | solution.py:567
  8.2 0.0 copy-done.5
  8.2 0.0 copy-start.2
  8.2 0.0 copy-start.1
  8.2 0.0 slice-start
  8.2 0.0 slice-start.1
  8.2 3.3 %project_kept.1 = (f32[16,2048]{1,0:T(8,128)S(1)}, s32[64,128]{1,0:T(8,128)S(1)}) custom-call(s32[1]{0:T(128)} %bitcast.place.refs_0_, s32[1]{0:T(128)} %bitcast.1.bank.refs_1_, s32[8]{0:T(128)S(1)} %copy-done.5, bf16[8,1024]{1,0:T(8,128)(2,1)S(1)} %copy-done.3, bf16[8,1024]{1,0:T(8,128)(2,1)S(1)} %collective-permute-done.other_ref, bf16[1024,8192]{1,0:T(8,128)(2,1)} %w_ref.4), custom_call_target="tpu_custom_call" | custom-call | flops 67108864 | bytes 16777216 | tf_op jit(solution)/shard_map/project_kept/pallas_call | solution.py:208
  11.5 0.0 copy-start
  11.5 0.0 collective-permute-done.2.came_ref
  11.6 2.8 %collective-permute-start.3 = (f32[16,640]{1,0:T(8,128)S(1)}, f32[16,640]{1,0:T(8,128)S(1)}, u32[]{:S(2)}, u32[]{:S(2)}) collective-permute-start(f32[16,640]{1,0:T(8,128)S(1)} %get-tuple-element.29), channel_id=1, source_target_pairs={{0,8},{1,9},{2,10},{3,11},{4,12},{5,13},{6,14},{7,15},{8,0},{9,1},... | collective-permute-start | bytes 122888 | tf_op jit(solution)/shard_map/ppermute | solution.py:567
  14.4 1.3 %collective-permute-start.4 = (f32[16,640]{1,0:T(8,128)S(1)}, f32[16,640]{1,0:T(8,128)S(1)}, u32[]{:S(2)}, u32[]{:S(2)}) collective-permute-start(f32[16,640]{1,0:T(8,128)S(1)} %get-tuple-element.30), channel_id=1, source_target_pairs={{0,12},{1,11},{2,14},{3,9},{4,8},{5,15},{6,10},{7,13},{8,4},{9,3},... | collective-permute-start | bytes 122888 | tf_op jit(solution)/shard_map/ppermute | solution.py:567
  15.7 0.2 collective-permute-start.5
  16.0 0.0 slice-start.2
  16.0 2.6 %keyval.1.refs_7_ = f32[8,24,128]{2,1,0:T(8,128)S(1)} custom-call(bf16[8,1024]{1,0:T(8,128)(2,1)S(1)} %copy-done.3, bf16[1024,2048]{1,0:T(8,128)(2,1)} %w_ref.5), custom_call_target="tpu_custom_call" | custom-call | flops 33554432 | bytes 4194304 | tf_op jit(solution)/shard_map/keyval/pallas_call | solution.py:247
  18.6 0.0 collective-permute-done.3.refs_1_
  18.6 1.6 %collective-permute-done.4.refs_2_ = f32[16,640]{1,0:T(8,128)S(1)} collective-permute-done((f32[16,640]{1,0:T(8,128)S(1)}, f32[16,640]{1,0:T(8,128)S(1)}, u32[]{:S(2)}, u32[]{:S(2)}) %collective-permute-start.4) | collective-permute-done | bytes 40992 | tf_op jit(solution)/shard_map/ppermute | solution.py:567
  20.2 0.0 collective-permute-done.5.refs_3_
  20.2 0.0 copy-done.2
  20.2 0.4 correct.1
  20.6 0.0 collective-permute-start.6
  20.6 0.1 fusion
  20.7 1.1 %collective-permute-done.6.came_ref = f32[8,1024]{1,0:T(8,128)S(1)} collective-permute-done((f32[8,1024]{1,0:T(8,128)S(1)}, f32[8,1024]{1,0:T(8,128)S(1)}, u32[]{:S(2)}, u32[]{:S(2)}) %collective-permute-start.6) | collective-permute-done | bytes 32800 | tf_op jit(solution)/shard_map/ppermute | solution.py:555
  21.8 0.1 rotate.1.refs_0_.q_ref
  21.9 1.3 %collective-permute-start.7 = (bf16[1,64,128]{2,1,0:T(8,128)(2,1)S(1)}, bf16[1,64,128]{2,1,0:T(8,128)(2,1)S(1)}, u32[]{:S(2)}, u32[]{:S(2)}) collective-permute-start(bf16[1,64,128]{2,1,0:T(8,128)(2,1)S(1)} %rotate.1.refs_0_.q_ref), channel_id=1, source_target_pairs={{0,8},{1,9},{2,10},{3,11},{4,12},{5,13},{6,14},{7,15},{8,0},{9,1},... | collective-permute-start | bytes 49160 | tf_op jit(solution)/shard_map/ppermute | solution.py:567
  23.2 1.3 %collective-permute-start.8 = (bf16[1,64,128]{2,1,0:T(8,128)(2,1)S(1)}, bf16[1,64,128]{2,1,0:T(8,128)(2,1)S(1)}, u32[]{:S(2)}, u32[]{:S(2)}) collective-permute-start(bf16[1,64,128]{2,1,0:T(8,128)(2,1)S(1)} %rotate.1.refs_0_.q_ref), channel_id=1, source_target_pairs={{0,12},{1,11},{2,14},{3,9},{4,8},{5,15},{6,10},{7,13},{8,4},{9,3},... | collective-permute-start | bytes 49160 | tf_op jit(solution)/shard_map/ppermute | solution.py:567
  24.6 0.9 %collective-permute-start.9 = (bf16[1,64,128]{2,1,0:T(8,128)(2,1)S(1)}, bf16[1,64,128]{2,1,0:T(8,128)(2,1)S(1)}, u32[]{:S(2)}, u32[]{:S(2)}) collective-permute-start(bf16[1,64,128]{2,1,0:T(8,128)(2,1)S(1)} %rotate.1.refs_0_.q_ref), channel_id=1, source_target_pairs={{0,4},{1,3},{2,6},{3,1},{4,0},{5,7},{6,2},{7,5},{8,12},{9,11},{10,... | collective-permute-start | bytes 49160 | tf_op jit(solution)/shard_map/ppermute | solution.py:567
  25.5 1.1 %collective-permute-done.7.refs_1_ = bf16[1,64,128]{2,1,0:T(8,128)(2,1)S(1)} collective-permute-done((bf16[1,64,128]{2,1,0:T(8,128)(2,1)S(1)}, bf16[1,64,128]{2,1,0:T(8,128)(2,1)S(1)}, u32[]{:S(2)}, u32[]{:S(2)}) %collective-permute-start.7) | collective-permute-done | bytes 16416 | tf_op jit(solution)/shard_map/ppermute | solution.py:567
  26.6 2.2 %collective-permute-done.8.refs_2_ = bf16[1,64,128]{2,1,0:T(8,128)(2,1)S(1)} collective-permute-done((bf16[1,64,128]{2,1,0:T(8,128)(2,1)S(1)}, bf16[1,64,128]{2,1,0:T(8,128)(2,1)S(1)}, u32[]{:S(2)}, u32[]{:S(2)}) %collective-permute-start.8) | collective-permute-done | bytes 16416 | tf_op jit(solution)/shard_map/ppermute | solution.py:567
  28.8 0.0 collective-permute-done.9.refs_3_
  28.8 1.6 %collective-permute-start.10 = (bf16[4,64,128]{2,1,0:T(8,128)(2,1)S(1)}, bf16[4,64,128]{2,1,0:T(8,128)(2,1)S(1)}, u32[]{:S(2)}, u32[]{:S(2)}) collective-permute-start(bf16[4,64,128]{2,1,0:T(8,128)(2,1)S(1)} %join.1.refs_3_), channel_id=1, source_target_pairs={{0,2},{1,5},{2,0},{3,7},{4,6},{5,1},{6,4},{7,3},{8,10},{9,13},{10,... | collective-permute-start | bytes 196616 | tf_op jit(solution)/shard_map/ppermute | solution.py:567
  30.4 0.0 copy-done.1
  30.4 0.0 copy-done
  30.4 0.0 slice-start.3
  30.4 1.6 %attend.2.refs_6_ = bf16[4,80,128]{2,1,0:T(8,128)(2,1)S(1)} custom-call(s32[1]{0:T(128)} %bitcast.place.refs_0_, s32[1]{0:T(128)} %bitcast.1.bank.refs_1_, s32[64,128]{1,0:T(8,128)S(1)} %get-tuple-element.22.refs_2_, bf16[4,64,128]{2,1,0:T(8,128)(2,1)S(1)} %join.1.refs_3_, bf16[8,256,1024]{2,1,0:T(8,128)(2,1)S(1)} %copy-done, bf16[8,256,1024]{2,1,0:T(8,128)(2,1)S(1)} %copy-done.1), custom_call_target="tpu_custom_call" | custom-call | flops 33554432 | bytes 4194304 | tf_op jit(solution)/shard_map/attend/pallas_call | solution.py:434
  32.0 1.2 %collective-permute-done.10.refs_3_ = bf16[4,64,128]{2,1,0:T(8,128)(2,1)S(1)} collective-permute-done((bf16[4,64,128]{2,1,0:T(8,128)(2,1)S(1)}, bf16[4,64,128]{2,1,0:T(8,128)(2,1)S(1)}, u32[]{:S(2)}, u32[]{:S(2)}) %collective-permute-start.10) | collective-permute-done | bytes 65568 | tf_op jit(solution)/shard_map/ppermute | solution.py:567
  33.1 1.6 %attend.3 = bf16[8,96,128]{2,1,0:T(8,128)(2,1)S(1)} custom-call(s32[1]{0:T(128)} %bitcast.place.refs_0_, s32[1]{0:T(128)} %bitcast.1.bank.refs_1_, s32[64,128]{1,0:T(8,128)S(1)} %get-tuple-element.22.refs_2_, bf16[4,64,128]{2,1,0:T(8,128)(2,1)S(1)} %collective-permute-done.10.refs_3_, bf16[8,256,1024]{2,1,0:T(8,128)(2,1)S(1)} %copy-done, ...), custom_call_target="tpu_custom_call" | custom-call | flops 33554432 | bytes 16777216 | tf_op jit(solution)/shard_map/attend/pallas_call | solution.py:434
  34.7 11.8 %all_to_all.10.parts_ref = bf16[8,96,128]{2,1,0:T(8,128)(2,1)S(1)} all-to-all(bf16[8,96,128]{2,1,0:T(8,128)(2,1)S(1)} %attend.3), channel_id=1, replica_groups=mesh['groups'=2,'tensor'=8,'bank'=2] {'tensor'}, dimensions={0} | all-to-all | bytes 393216 | tf_op jit(solution)/shard_map/all_to_all | solution.py:559
  46.5 0.4 combine.1.x_ref
  46.9 0.0 slice-done
  46.9 0.0 slice-done.1
  46.9 0.0 slice-done.2
  46.9 0.0 slice-done.3
  46.9 2.3 %output.1 = bf16[8,8,1024]{2,1,0:T(8,128)(2,1)S(1)} custom-call(bf16[8,1024]{1,0:T(8,128)(2,1)S(1)} %combine.1.x_ref, bf16[1024,8192]{1,0:T(8,128)(2,1)S(1)} %bitcast.6), custom_call_target="tpu_custom_call" | custom-call | flops 134217728 | bytes 16777216 | tf_op jit(solution)/shard_map/output/pallas_call | solution.py:525
  49.2 9.8 %all_to_all.11.parts_ref = bf16[8,8,1024]{2,1,0:T(8,128)(2,1)S(1)} all-to-all(bf16[8,8,1024]{2,1,0:T(8,128)(2,1)S(1)} %output.1), channel_id=1, replica_groups=mesh['groups'=2,'tensor'=8,'bank'=2] {'tensor'}, dimensions={0} | all-to-all | bytes 262144 | tf_op jit(solution)/shard_map/all_to_all | solution.py:559
  59.0 0.6 %residual.1 = bf16[8,1024]{1,0:T(8,128)(2,1)} custom-call(bf16[8,1024]{1,0:T(8,128)(2,1)S(1)} %copy-done.3, bf16[8,8,1024]{2,1,0:T(8,128)(2,1)S(1)} %all_to_all.11.parts_ref), custom_call_target="tpu_custom_call" | custom-call | tf_op jit(solution)/shard_map/residual/pallas_call | solution.py:544
  (5 shorter events, 0.0 us)
Async XLA Ops:
  0.0 2.1 %copy-start.3 = (bf16[8,1024]{1,0:T(8,128)(2,1)S(1)}, bf16[8,1024]{1,0:T(8,128)(2,1)}, u32[]{:S(2)}) copy-start(bf16[8,1024]{1,0:T(8,128)(2,1)} %x_ref.7) | copy-start | bytes 49156
  0.0 2.1 %copy-start.4 = (s32[8]{0:T(128)S(1)}, s32[8]{0:T(128)}, u32[]{:S(2)}) copy-start(s32[8]{0:T(128)} %param.11) | copy-start | bytes 100
  0.0 2.1 %collective-permute-start = (bf16[8,1024]{1,0:T(8,128)(2,1)}, bf16[8,1024]{1,0:T(8,128)(2,1)S(1)}, u32[]{:S(2)}, u32[]{:S(2)}) collective-permute-start(bf16[8,1024]{1,0:T(8,128)(2,1)} %x_ref.7), channel_id=1, source_target_pairs={{0,1},{1,0},{2,3},{3,2},{4,5},{5,4},{6,7},{7,6},{8,9},{9,8},{10,11... | collective-permute-start | bytes 49160 | tf_op jit(solution)/shard_map/ppermute | solution.py:555
  0.5 1.6 %collective-permute-start.1 = (s32[8]{0:T(128)}, s32[8]{0:T(128)S(1)}, u32[]{:S(2)}, u32[]{:S(2)}) collective-permute-start(s32[8]{0:T(128)} %param.11), channel_id=1, source_target_pairs={{0,1},{1,0},{2,3},{3,2},{4,5},{5,4},{6,7},{7,6},{8,9},{9,8},{10,11... | collective-permute-start | bytes 104 | tf_op jit(solution)/shard_map/ppermute | solution.py:555
  2.1 6.1 %copy-start.5 = (s32[8]{0:T(128)S(1)}, s32[8]{0:T(128)}, u32[]{:S(2)}) copy-start(s32[8]{0:T(128)} %length.1) | copy-start | bytes 100
  5.2 6.4 %collective-permute-start.2 = (f32[16,2176]{1,0:T(8,128)S(1)}, f32[16,2176]{1,0:T(8,128)S(1)}, u32[]{:S(2)}, u32[]{:S(2)}) collective-permute-start(f32[16,2176]{1,0:T(8,128)S(1)} %get-tuple-element.26), channel_id=1, source_target_pairs={{0,2},{1,5},{2,0},{3,7},{4,6},{5,1},{6,4},{7,3},{8,10},{9,13},{10,... | collective-permute-start | bytes 417800 | tf_op jit(solution)/shard_map/ppermute | solution.py:567
  8.2 12.0 %copy-start.2 = (bf16[16,64,1024]{2,1,0:T(8,128)(2,1)S(1)}, bf16[16,64,1024]{2,1,0:T(8,128)(2,1)}, u32[]{:S(2)}) copy-start(bf16[16,64,1024]{2,1,0:T(8,128)(2,1)} %up_ref.1) | copy-start | bytes 6291460
  8.2 22.2 %copy-start.1 = (bf16[8,256,1024]{2,1,0:T(8,128)(2,1)S(1)}, bf16[8,256,1024]{2,1,0:T(8,128)(2,1)}, u32[]{:S(2)}) copy-start(bf16[8,256,1024]{2,1,0:T(8,128)(2,1)} %refs_5_.3) | copy-start | bytes 12582916
  8.2 38.7 %slice-start = ((s8[16777216]{0:T(1024)(128)(4,1)}), s8[4194304]{0:T(1024)(128)(4,1)S(1)}, s32[]{:S(2)}) async-start(s8[16777216]{0:T(1024)(128)(4,1)} %bitcast.5), calls=%async_computation.2 | async-start | bytes 8388608
  8.2 38.7 %slice-start.1 = ((s8[16777216]{0:T(1024)(128)(4,1)}), s8[4194304]{0:T(1024)(128)(4,1)S(1)}, s32[]{:S(2)}) async-start(s8[16777216]{0:T(1024)(128)(4,1)} %bitcast.5), calls=%async_computation.3 | async-start | bytes 8388608
  11.5 18.9 %copy-start = (bf16[8,256,1024]{2,1,0:T(8,128)(2,1)S(1)}, bf16[8,256,1024]{2,1,0:T(8,128)(2,1)}, u32[]{:S(2)}) copy-start(bf16[8,256,1024]{2,1,0:T(8,128)(2,1)} %refs_4_.3) | copy-start | bytes 12582916
  11.6 7.1 %collective-permute-start.3 = (f32[16,640]{1,0:T(8,128)S(1)}, f32[16,640]{1,0:T(8,128)S(1)}, u32[]{:S(2)}, u32[]{:S(2)}) collective-permute-start(f32[16,640]{1,0:T(8,128)S(1)} %get-tuple-element.29), channel_id=1, source_target_pairs={{0,8},{1,9},{2,10},{3,11},{4,12},{5,13},{6,14},{7,15},{8,0},{9,1},... | collective-permute-start | bytes 122888 | tf_op jit(solution)/shard_map/ppermute | solution.py:567
  14.4 5.8 %collective-permute-start.4 = (f32[16,640]{1,0:T(8,128)S(1)}, f32[16,640]{1,0:T(8,128)S(1)}, u32[]{:S(2)}, u32[]{:S(2)}) collective-permute-start(f32[16,640]{1,0:T(8,128)S(1)} %get-tuple-element.30), channel_id=1, source_target_pairs={{0,12},{1,11},{2,14},{3,9},{4,8},{5,15},{6,10},{7,13},{8,4},{9,3},... | collective-permute-start | bytes 122888 | tf_op jit(solution)/shard_map/ppermute | solution.py:567
  15.7 4.5 %collective-permute-start.5 = (f32[16,640]{1,0:T(8,128)S(1)}, f32[16,640]{1,0:T(8,128)S(1)}, u32[]{:S(2)}, u32[]{:S(2)}) collective-permute-start(f32[16,640]{1,0:T(8,128)S(1)} %get-tuple-element.31), channel_id=1, source_target_pairs={{0,4},{1,3},{2,6},{3,1},{4,0},{5,7},{6,2},{7,5},{8,12},{9,11},{10,... | collective-permute-start | bytes 122888 | tf_op jit(solution)/shard_map/ppermute | solution.py:567
  16.0 30.9 %slice-start.2 = ((s8[16777216]{0:T(1024)(128)(4,1)}), s8[4194304]{0:T(1024)(128)(4,1)S(1)}, s32[]{:S(2)}) async-start(s8[16777216]{0:T(1024)(128)(4,1)} %bitcast.5), calls=%async_computation.4 | async-start | bytes 8388608
  20.6 1.2 %collective-permute-start.6 = (f32[8,1024]{1,0:T(8,128)S(1)}, f32[8,1024]{1,0:T(8,128)S(1)}, u32[]{:S(2)}, u32[]{:S(2)}) collective-permute-start(f32[8,1024]{1,0:T(8,128)S(1)} %get-tuple-element.37), channel_id=1, source_target_pairs={{0,1},{1,0},{2,3},{3,2},{4,5},{5,4},{6,7},{7,6},{8,9},{9,8},{10,11... | collective-permute-start | bytes 98312 | tf_op jit(solution)/shard_map/ppermute | solution.py:555
  21.9 4.7 %collective-permute-start.7 = (bf16[1,64,128]{2,1,0:T(8,128)(2,1)S(1)}, bf16[1,64,128]{2,1,0:T(8,128)(2,1)S(1)}, u32[]{:S(2)}, u32[]{:S(2)}) collective-permute-start(bf16[1,64,128]{2,1,0:T(8,128)(2,1)S(1)} %rotate.1.refs_0_.q_ref), channel_id=1, source_target_pairs={{0,8},{1,9},{2,10},{3,11},{4,12},{5,13},{6,14},{7,15},{8,0},{9,1},... | collective-permute-start | bytes 49160 | tf_op jit(solution)/shard_map/ppermute | solution.py:567
  23.2 5.5 %collective-permute-start.8 = (bf16[1,64,128]{2,1,0:T(8,128)(2,1)S(1)}, bf16[1,64,128]{2,1,0:T(8,128)(2,1)S(1)}, u32[]{:S(2)}, u32[]{:S(2)}) collective-permute-start(bf16[1,64,128]{2,1,0:T(8,128)(2,1)S(1)} %rotate.1.refs_0_.q_ref), channel_id=1, source_target_pairs={{0,12},{1,11},{2,14},{3,9},{4,8},{5,15},{6,10},{7,13},{8,4},{9,3},... | collective-permute-start | bytes 49160 | tf_op jit(solution)/shard_map/ppermute | solution.py:567
  24.6 4.2 %collective-permute-start.9 = (bf16[1,64,128]{2,1,0:T(8,128)(2,1)S(1)}, bf16[1,64,128]{2,1,0:T(8,128)(2,1)S(1)}, u32[]{:S(2)}, u32[]{:S(2)}) collective-permute-start(bf16[1,64,128]{2,1,0:T(8,128)(2,1)S(1)} %rotate.1.refs_0_.q_ref), channel_id=1, source_target_pairs={{0,4},{1,3},{2,6},{3,1},{4,0},{5,7},{6,2},{7,5},{8,12},{9,11},{10,... | collective-permute-start | bytes 49160 | tf_op jit(solution)/shard_map/ppermute | solution.py:567
  28.8 4.3 %collective-permute-start.10 = (bf16[4,64,128]{2,1,0:T(8,128)(2,1)S(1)}, bf16[4,64,128]{2,1,0:T(8,128)(2,1)S(1)}, u32[]{:S(2)}, u32[]{:S(2)}) collective-permute-start(bf16[4,64,128]{2,1,0:T(8,128)(2,1)S(1)} %join.1.refs_3_), channel_id=1, source_target_pairs={{0,2},{1,5},{2,0},{3,7},{4,6},{5,1},{6,4},{7,3},{8,10},{9,13},{10,... | collective-permute-start | bytes 196616 | tf_op jit(solution)/shard_map/ppermute | solution.py:567
  30.4 16.5 %slice-start.3 = ((s8[16777216]{0:T(1024)(128)(4,1)}), s8[4194304]{0:T(1024)(128)(4,1)S(1)}, s32[]{:S(2)}) async-start(s8[16777216]{0:T(1024)(128)(4,1)} %bitcast.5), calls=%async_computation.5 | async-start | bytes 8388608

commit v20 on v19

--- a/solution.py
+++ b/solution.py
@@ -222,17 +222,9 @@
     )(place, bank, length, x, other, wq)
 
 
-def keyval_kernel(x_ref, w_ref, out, w_buf, sems):
-    copies = start_parts(w_ref, w_buf, sems)
-    beams = x_ref.shape[0]
+def keyval_kernel(x_ref, w_ref, out):
     ranks = out.shape[0]
-    part = w_buf.shape[0] // len(copies)
-    total = None
-    for c, copy in enumerate(copies):
-        copy.wait()
-        rows = slice(c * part, (c + 1) * part)
-        product = jnp.dot(x_ref[:, rows], w_buf[rows], preferred_element_type=F32)
-        total = product if total is None else total + product
+    total = jnp.dot(x_ref[...], w_ref[...], preferred_element_type=F32)
     high = total.astype(BF16).astype(F32)
     low = total - high
     for r in range(ranks):
@@ -246,11 +238,10 @@
     beams, depth = x.shape
     return pl.pallas_call(
         keyval_kernel,
-        in_specs=[whole(), big()],
+        in_specs=[whole()] * 2,
         out_specs=whole(),
         out_shape=shape(ranks, 3 * beams, HEAD_DIM),
-        scratch_shapes=[pltpu.VMEM(wkv.shape, BF16), pltpu.SemaphoreType.DMA((4,))],
-        compiler_params=params(8),
+        compiler_params=params(),
         cost_estimate=pl.CostEstimate(
             flops=2 * beams * wkv.size, bytes_accessed=2 * wkv.size, transcendentals=0
         ),
@@ -601,8 +592,8 @@
     kept, *sent = part(kept, inner, came, ranks // 2)
     near = 4, 6, 2
     parts = [kept] + [hop(sent[slot // 2 - 1], slot) for slot in near]
-    token_weight, _ = lax.optimization_barrier((in_hbm(keyvalue_weight), kept))
-    token, parts = lax.optimization_barrier((keyval(x, in_hbm(token_weight), ranks), parts))
+    own_x, _ = lax.optimization_barrier((x, kept))
+    token, parts = lax.optimization_barrier((keyval(own_x, keyvalue_weight, ranks), parts))
     own, other = correct(bank, column, lowrank_up_factors, parts)
     query = rotated(own, swapped(other), cosine, sine)
 

time: 59.8 us -> 59.8 us (level)
  waiting for transfers between devices: 7.17 us -> 9.1 us
  Pallas kernels: 17.4 us -> 15.5 us
    pallas_call x1, Pallas kernels: 2.61 us -> 0.65 us  [keyval(): pl.pallas_call(keyval_kernel, in_specs=[whole()] * 2, out_specs=whole(),...]
    ppermute x8, waiting for transfers between devices: 6.07 us -> 8 us  [hop(): return lax.ppermute(x, ('tensor', 'bank'), pairs)]
  transfers between devices with their start and end apart: 11 -> 11, of which waited for: 5 -> 5; matrix products, arithmetic and copies ran while one was open for 0% -> 0% of each run, Pallas kernels for 15% -> 12%
where the time goes in v20:
time: 59.8 us; the launch traced here: 59.6 us
  blocking collectives  21.5 us (36%)
  Pallas kernels  15.5 us (26%)
  starting transfers between devices  13.1 us (22%)
  waiting for transfers between devices  9.1 us (15%)
    all_to_all x2, blocking collectives, traded(): return lax.all_to_all(blocks, 'tensor', 0, 0, tiled=True)  21.5 us
    ppermute x8, starting transfers between devices, hop(): return lax.ppermute(x, ('tensor', 'bank'), pairs)  12.6 us
    ppermute x8, waiting for transfers between devices, hop(): return lax.ppermute(x, ('tensor', 'bank'), pairs)  8 us
    pallas_call x1, Pallas kernels, project_kept(): pl.pallas_call(project_kept_kernel, in_specs=[scalar()] * 3 + [whole()] *...  3.3 us
    pallas_call x2, Pallas kernels, attend(): pl.pallas_call(lambda *refs: attend_kernel(slots, earlier, *refs), in_spe...  3.12 us
    pallas_call x1, Pallas kernels, project_sent(): pl.pallas_call(project_sent_kernel, in_specs=[scalar()] * 2 + [whole()] *...  3.01 us
    pallas_call x1, Pallas kernels, output(): pl.pallas_call(output_kernel, in_specs=[whole()] * 2, out_specs=whole(),...  2.28 us
    pallas_call x1, Pallas kernels, fetch(): pl.pallas_call(fetch_kernel, in_specs=[big()], out_specs=whole(), out_sha...  1.56 us
  transfers between devices with their start and end apart: 11, of which 5 were waited for; matrix products, arithmetic and copies ran while one was open for 0% of the time, Pallas kernels for 12%

profile of v20, /device:TPU:0, one launch (start us, length us, event | category | flops | bytes accessed | tf_op | source)
XLA Modules:
  0.0 59.6 jit_solution(9170810280132090824)
XLA Ops:
  0.0 0.0 copy-start.4
  0.0 0.0 copy-start.5
  0.0 0.5 collective-permute-start
  0.5 0.1 collective-permute-start.1
  0.5 1.6 %fetch.1.down_ref = bf16[16,64,1024]{2,1,0:T(8,128)(2,1)S(1)} custom-call(bf16[16,64,1024]{2,1,0:T(8,128)(2,1)} %bitcast.9), custom_call_target="tpu_custom_call" | custom-call | bytes 2097152 | tf_op jit(solution)/shard_map/fetch/pallas_call | solution.py:109
  2.1 0.0 collective-permute-done.1
  2.1 0.0 collective-permute-done.other_ref
  2.1 0.0 copy-done.4
  2.1 0.0 copy-done.5
  2.1 0.0 copy-start.6
  2.1 3.0 %project_sent.1 = (f32[16,2176]{1,0:T(8,128)S(1)}, f32[16,128]{1,0:T(8,128)S(1)}, s32[16,128]{1,0:T(8,128)S(1)}) custom-call(s32[1]{0:T(128)} %bitcast.place.refs_0_, s32[1]{0:T(128)} %bitcast.1.bank.refs_1_, s32[1,8]{1,0:T(1,128)S(1)} %bitcast.7, s32[1,8]{1,0:T(1,128)S(1)} %bitcast.8, bf16[8,1024]{1,0:T(8,128)(2,1)S(1)} %copy-done.4, ...), custom_call_target="tpu_custom_call" | custom-call | flops 100663296 | bytes 6291456 | tf_op jit(solution)/shard_map/project_sent/pallas_call | solution.py:168
  5.2 0.0 copy-start.2
  5.2 3.0 %collective-permute-start.2 = (f32[16,2176]{1,0:T(8,128)S(1)}, f32[16,2176]{1,0:T(8,128)S(1)}, u32[]{:S(2)}, u32[]{:S(2)}) collective-permute-start(f32[16,2176]{1,0:T(8,128)S(1)} %get-tuple-element.26), channel_id=1, source_target_pairs={{0,2},{1,5},{2,0},{3,7},{4,6},{5,1},{6,4},{7,3},{8,10},{9,13},{10,... | collective-permute-start | bytes 417800 | tf_op jit(solution)/shard_map/ppermute | solution.py:558
  8.2 0.0 copy-done.6
  8.2 0.0 copy-start.3
  8.2 0.0 copy-start.1
  8.2 0.0 slice-start
  8.2 0.0 slice-start.1
  8.2 3.3 %project_kept.1 = (f32[16,2048]{1,0:T(8,128)S(1)}, s32[64,128]{1,0:T(8,128)S(1)}) custom-call(s32[1]{0:T(128)} %bitcast.place.refs_0_, s32[1]{0:T(128)} %bitcast.1.bank.refs_1_, s32[8]{0:T(128)S(1)} %copy-done.6, bf16[8,1024]{1,0:T(8,128)(2,1)S(1)} %copy-done.4, bf16[8,1024]{1,0:T(8,128)(2,1)S(1)} %collective-permute-done.other_ref, bf16[1024,8192]{1,0:T(8,128)(2,1)} %w_ref.5), custom_call_target="tpu_custom_call" | custom-call | flops 67108864 | bytes 16777216 | tf_op jit(solution)/shard_map/project_kept/pallas_call | solution.py:208
  11.5 0.0 copy-start
  11.5 0.0 collective-permute-done.2.came_ref
  11.6 2.8 %collective-permute-start.3 = (f32[16,640]{1,0:T(8,128)S(1)}, f32[16,640]{1,0:T(8,128)S(1)}, u32[]{:S(2)}, u32[]{:S(2)}) collective-permute-start(f32[16,640]{1,0:T(8,128)S(1)} %get-tuple-element.29), channel_id=1, source_target_pairs={{0,8},{1,9},{2,10},{3,11},{4,12},{5,13},{6,14},{7,15},{8,0},{9,1},... | collective-permute-start | bytes 122888 | tf_op jit(solution)/shard_map/ppermute | solution.py:558
  14.4 1.3 %collective-permute-start.4 = (f32[16,640]{1,0:T(8,128)S(1)}, f32[16,640]{1,0:T(8,128)S(1)}, u32[]{:S(2)}, u32[]{:S(2)}) collective-permute-start(f32[16,640]{1,0:T(8,128)S(1)} %get-tuple-element.30), channel_id=1, source_target_pairs={{0,12},{1,11},{2,14},{3,9},{4,8},{5,15},{6,10},{7,13},{8,4},{9,3},... | collective-permute-start | bytes 122888 | tf_op jit(solution)/shard_map/ppermute | solution.py:558
  15.8 0.2 collective-permute-start.5
  16.0 0.0 copy-done.2
  16.0 0.0 slice-start.2
  16.0 0.6 %keyval.1.refs_7_ = f32[8,24,128]{2,1,0:T(8,128)S(1)} custom-call(bf16[8,1024]{1,0:T(8,128)(2,1)S(1)} %copy-done.4, bf16[1024,2048]{1,0:T(8,128)(2,1)S(1)} %copy-done.2), custom_call_target="tpu_custom_call" | custom-call | flops 33554432 | bytes 4194304 | tf_op jit(solution)/shard_map/keyval/pallas_call | solution.py:239
  16.7 0.0 collective-permute-done.3.refs_1_
  16.7 3.5 %collective-permute-done.4.refs_2_ = f32[16,640]{1,0:T(8,128)S(1)} collective-permute-done((f32[16,640]{1,0:T(8,128)S(1)}, f32[16,640]{1,0:T(8,128)S(1)}, u32[]{:S(2)}, u32[]{:S(2)}) %collective-permute-start.4) | collective-permute-done | bytes 40992 | tf_op jit(solution)/shard_map/ppermute | solution.py:558
  20.2 0.0 collective-permute-done.5.refs_3_
  20.2 0.0 copy-done.3
  20.2 0.4 correct.1
  20.6 0.0 collective-permute-start.6
  20.6 0.1 fusion
  20.7 1.1 %collective-permute-done.6.came_ref = f32[8,1024]{1,0:T(8,128)S(1)} collective-permute-done((f32[8,1024]{1,0:T(8,128)S(1)}, f32[8,1024]{1,0:T(8,128)S(1)}, u32[]{:S(2)}, u32[]{:S(2)}) %collective-permute-start.6) | collective-permute-done | bytes 32800 | tf_op jit(solution)/shard_map/ppermute | solution.py:546
  21.8 0.1 rotate.1.refs_0_.q_ref
  21.9 1.3 %collective-permute-start.7 = (bf16[1,64,128]{2,1,0:T(8,128)(2,1)S(1)}, bf16[1,64,128]{2,1,0:T(8,128)(2,1)S(1)}, u32[]{:S(2)}, u32[]{:S(2)}) collective-permute-start(bf16[1,64,128]{2,1,0:T(8,128)(2,1)S(1)} %rotate.1.refs_0_.q_ref), channel_id=1, source_target_pairs={{0,8},{1,9},{2,10},{3,11},{4,12},{5,13},{6,14},{7,15},{8,0},{9,1},... | collective-permute-start | bytes 49160 | tf_op jit(solution)/shard_map/ppermute | solution.py:558
  23.2 1.2 %collective-permute-start.8 = (bf16[1,64,128]{2,1,0:T(8,128)(2,1)S(1)}, bf16[1,64,128]{2,1,0:T(8,128)(2,1)S(1)}, u32[]{:S(2)}, u32[]{:S(2)}) collective-permute-start(bf16[1,64,128]{2,1,0:T(8,128)(2,1)S(1)} %rotate.1.refs_0_.q_ref), channel_id=1, source_target_pairs={{0,12},{1,11},{2,14},{3,9},{4,8},{5,15},{6,10},{7,13},{8,4},{9,3},... | collective-permute-start | bytes 49160 | tf_op jit(solution)/shard_map/ppermute | solution.py:558
  24.4 1.1 %collective-permute-start.9 = (bf16[1,64,128]{2,1,0:T(8,128)(2,1)S(1)}, bf16[1,64,128]{2,1,0:T(8,128)(2,1)S(1)}, u32[]{:S(2)}, u32[]{:S(2)}) collective-permute-start(bf16[1,64,128]{2,1,0:T(8,128)(2,1)S(1)} %rotate.1.refs_0_.q_ref), channel_id=1, source_target_pairs={{0,4},{1,3},{2,6},{3,1},{4,0},{5,7},{6,2},{7,5},{8,12},{9,11},{10,... | collective-permute-start | bytes 49160 | tf_op jit(solution)/shard_map/ppermute | solution.py:558
  25.5 1.1 %collective-permute-done.7.refs_1_ = bf16[1,64,128]{2,1,0:T(8,128)(2,1)S(1)} collective-permute-done((bf16[1,64,128]{2,1,0:T(8,128)(2,1)S(1)}, bf16[1,64,128]{2,1,0:T(8,128)(2,1)S(1)}, u32[]{:S(2)}, u32[]{:S(2)}) %collective-permute-start.7) | collective-permute-done | bytes 16416 | tf_op jit(solution)/shard_map/ppermute | solution.py:558
  26.6 2.1 %collective-permute-done.8.refs_2_ = bf16[1,64,128]{2,1,0:T(8,128)(2,1)S(1)} collective-permute-done((bf16[1,64,128]{2,1,0:T(8,128)(2,1)S(1)}, bf16[1,64,128]{2,1,0:T(8,128)(2,1)S(1)}, u32[]{:S(2)}, u32[]{:S(2)}) %collective-permute-start.8) | collective-permute-done | bytes 16416 | tf_op jit(solution)/shard_map/ppermute | solution.py:558
  28.8 0.0 collective-permute-done.9.refs_3_
  28.8 1.6 %collective-permute-start.10 = (bf16[4,64,128]{2,1,0:T(8,128)(2,1)S(1)}, bf16[4,64,128]{2,1,0:T(8,128)(2,1)S(1)}, u32[]{:S(2)}, u32[]{:S(2)}) collective-permute-start(bf16[4,64,128]{2,1,0:T(8,128)(2,1)S(1)} %join.1.refs_3_), channel_id=1, source_target_pairs={{0,2},{1,5},{2,0},{3,7},{4,6},{5,1},{6,4},{7,3},{8,10},{9,13},{10,... | collective-permute-start | bytes 196616 | tf_op jit(solution)/shard_map/ppermute | solution.py:558
  30.4 0.0 copy-done.1
  30.4 0.0 copy-done
  30.4 0.0 slice-start.3
  30.4 1.6 %attend.2.refs_6_ = bf16[4,80,128]{2,1,0:T(8,128)(2,1)S(1)} custom-call(s32[1]{0:T(128)} %bitcast.place.refs_0_, s32[1]{0:T(128)} %bitcast.1.bank.refs_1_, s32[64,128]{1,0:T(8,128)S(1)} %get-tuple-element.22.refs_2_, bf16[4,64,128]{2,1,0:T(8,128)(2,1)S(1)} %join.1.refs_3_, bf16[8,256,1024]{2,1,0:T(8,128)(2,1)S(1)} %copy-done, bf16[8,256,1024]{2,1,0:T(8,128)(2,1)S(1)} %copy-done.1), custom_call_target="tpu_custom_call" | custom-call | flops 33554432 | bytes 4194304 | tf_op jit(solution)/shard_map/attend/pallas_call | solution.py:425
  31.9 1.2 %collective-permute-done.10.refs_3_ = bf16[4,64,128]{2,1,0:T(8,128)(2,1)S(1)} collective-permute-done((bf16[4,64,128]{2,1,0:T(8,128)(2,1)S(1)}, bf16[4,64,128]{2,1,0:T(8,128)(2,1)S(1)}, u32[]{:S(2)}, u32[]{:S(2)}) %collective-permute-start.10) | collective-permute-done | bytes 65568 | tf_op jit(solution)/shard_map/ppermute | solution.py:558
  33.1 1.6 %attend.3 = bf16[8,96,128]{2,1,0:T(8,128)(2,1)S(1)} custom-call(s32[1]{0:T(128)} %bitcast.place.refs_0_, s32[1]{0:T(128)} %bitcast.1.bank.refs_1_, s32[64,128]{1,0:T(8,128)S(1)} %get-tuple-element.22.refs_2_, bf16[4,64,128]{2,1,0:T(8,128)(2,1)S(1)} %collective-permute-done.10.refs_3_, bf16[8,256,1024]{2,1,0:T(8,128)(2,1)S(1)} %copy-done, ...), custom_call_target="tpu_custom_call" | custom-call | flops 33554432 | bytes 16777216 | tf_op jit(solution)/shard_map/attend/pallas_call | solution.py:425
  34.7 11.8 %all_to_all.10.parts_ref = bf16[8,96,128]{2,1,0:T(8,128)(2,1)S(1)} all-to-all(bf16[8,96,128]{2,1,0:T(8,128)(2,1)S(1)} %attend.3), channel_id=1, replica_groups=mesh['groups'=2,'tensor'=8,'bank'=2] {'tensor'}, dimensions={0} | all-to-all | bytes 393216 | tf_op jit(solution)/shard_map/all_to_all | solution.py:550
  46.4 0.4 combine.1.x_ref
  46.9 0.0 slice-done
  46.9 0.0 slice-done.1
  46.9 0.0 slice-done.2
  46.9 0.0 slice-done.3
  46.9 2.3 %output.1 = bf16[8,8,1024]{2,1,0:T(8,128)(2,1)S(1)} custom-call(bf16[8,1024]{1,0:T(8,128)(2,1)S(1)} %combine.1.x_ref, bf16[1024,8192]{1,0:T(8,128)(2,1)S(1)} %bitcast.6), custom_call_target="tpu_custom_call" | custom-call | flops 134217728 | bytes 16777216 | tf_op jit(solution)/shard_map/output/pallas_call | solution.py:516
  49.2 9.8 %all_to_all.11.parts_ref = bf16[8,8,1024]{2,1,0:T(8,128)(2,1)S(1)} all-to-all(bf16[8,8,1024]{2,1,0:T(8,128)(2,1)S(1)} %output.1), channel_id=1, replica_groups=mesh['groups'=2,'tensor'=8,'bank'=2] {'tensor'}, dimensions={0} | all-to-all | bytes 262144 | tf_op jit(solution)/shard_map/all_to_all | solution.py:550
  59.0 0.6 %residual.1 = bf16[8,1024]{1,0:T(8,128)(2,1)} custom-call(bf16[8,1024]{1,0:T(8,128)(2,1)S(1)} %copy-done.4, bf16[8,8,1024]{2,1,0:T(8,128)(2,1)S(1)} %all_to_all.11.parts_ref), custom_call_target="tpu_custom_call" | custom-call | tf_op jit(solution)/shard_map/residual/pallas_call | solution.py:535
  (5 shorter events, 0.0 us)
Async XLA Ops:
  0.0 2.1 %copy-start.4 = (bf16[8,1024]{1,0:T(8,128)(2,1)S(1)}, bf16[8,1024]{1,0:T(8,128)(2,1)}, u32[]{:S(2)}) copy-start(bf16[8,1024]{1,0:T(8,128)(2,1)} %x_ref.6) | copy-start | bytes 49156
  0.0 2.1 %copy-start.5 = (s32[8]{0:T(128)S(1)}, s32[8]{0:T(128)}, u32[]{:S(2)}) copy-start(s32[8]{0:T(128)} %param.11) | copy-start | bytes 100
  0.0 2.1 %collective-permute-start = (bf16[8,1024]{1,0:T(8,128)(2,1)}, bf16[8,1024]{1,0:T(8,128)(2,1)S(1)}, u32[]{:S(2)}, u32[]{:S(2)}) collective-permute-start(bf16[8,1024]{1,0:T(8,128)(2,1)} %x_ref.6), channel_id=1, source_target_pairs={{0,1},{1,0},{2,3},{3,2},{4,5},{5,4},{6,7},{7,6},{8,9},{9,8},{10,11... | collective-permute-start | bytes 49160 | tf_op jit(solution)/shard_map/ppermute | solution.py:546
  0.5 1.6 %collective-permute-start.1 = (s32[8]{0:T(128)}, s32[8]{0:T(128)S(1)}, u32[]{:S(2)}, u32[]{:S(2)}) collective-permute-start(s32[8]{0:T(128)} %param.11), channel_id=1, source_target_pairs={{0,1},{1,0},{2,3},{3,2},{4,5},{5,4},{6,7},{7,6},{8,9},{9,8},{10,11... | collective-permute-start | bytes 104 | tf_op jit(solution)/shard_map/ppermute | solution.py:546
  2.1 6.1 %copy-start.6 = (s32[8]{0:T(128)S(1)}, s32[8]{0:T(128)}, u32[]{:S(2)}) copy-start(s32[8]{0:T(128)} %length.1) | copy-start | bytes 100
  5.2 10.8 %copy-start.2 = (bf16[1024,2048]{1,0:T(8,128)(2,1)S(1)}, bf16[1024,2048]{1,0:T(8,128)(2,1)}, u32[]{:S(2)}) copy-start(bf16[1024,2048]{1,0:T(8,128)(2,1)} %w_ref.6) | copy-start | bytes 12582916
  5.2 6.4 %collective-permute-start.2 = (f32[16,2176]{1,0:T(8,128)S(1)}, f32[16,2176]{1,0:T(8,128)S(1)}, u32[]{:S(2)}, u32[]{:S(2)}) collective-permute-start(f32[16,2176]{1,0:T(8,128)S(1)} %get-tuple-element.26), channel_id=1, source_target_pairs={{0,2},{1,5},{2,0},{3,7},{4,6},{5,1},{6,4},{7,3},{8,10},{9,13},{10,... | collective-permute-start | bytes 417800 | tf_op jit(solution)/shard_map/ppermute | solution.py:558
  8.2 12.0 %copy-start.3 = (bf16[16,64,1024]{2,1,0:T(8,128)(2,1)S(1)}, bf16[16,64,1024]{2,1,0:T(8,128)(2,1)}, u32[]{:S(2)}) copy-start(bf16[16,64,1024]{2,1,0:T(8,128)(2,1)} %up_ref.1) | copy-start | bytes 6291460
  8.2 22.2 %copy-start.1 = (bf16[8,256,1024]{2,1,0:T(8,128)(2,1)S(1)}, bf16[8,256,1024]{2,1,0:T(8,128)(2,1)}, u32[]{:S(2)}) copy-start(bf16[8,256,1024]{2,1,0:T(8,128)(2,1)} %refs_5_.3) | copy-start | bytes 12582916
  8.2 38.7 %slice-start = ((s8[16777216]{0:T(1024)(128)(4,1)}), s8[4194304]{0:T(1024)(128)(4,1)S(1)}, s32[]{:S(2)}) async-start(s8[16777216]{0:T(1024)(128)(4,1)} %bitcast.5), calls=%async_computation.2 | async-start | bytes 8388608
  8.2 38.7 %slice-start.1 = ((s8[16777216]{0:T(1024)(128)(4,1)}), s8[4194304]{0:T(1024)(128)(4,1)S(1)}, s32[]{:S(2)}) async-start(s8[16777216]{0:T(1024)(128)(4,1)} %bitcast.5), calls=%async_computation.3 | async-start | bytes 8388608
  11.5 18.8 %copy-start = (bf16[8,256,1024]{2,1,0:T(8,128)(2,1)S(1)}, bf16[8,256,1024]{2,1,0:T(8,128)(2,1)}, u32[]{:S(2)}) copy-start(bf16[8,256,1024]{2,1,0:T(8,128)(2,1)} %refs_4_.3) | copy-start | bytes 12582916
  11.6 5.1 %collective-permute-start.3 = (f32[16,640]{1,0:T(8,128)S(1)}, f32[16,640]{1,0:T(8,128)S(1)}, u32[]{:S(2)}, u32[]{:S(2)}) collective-permute-start(f32[16,640]{1,0:T(8,128)S(1)} %get-tuple-element.29), channel_id=1, source_target_pairs={{0,8},{1,9},{2,10},{3,11},{4,12},{5,13},{6,14},{7,15},{8,0},{9,1},... | collective-permute-start | bytes 122888 | tf_op jit(solution)/shard_map/ppermute | solution.py:558
  14.4 5.8 %collective-permute-start.4 = (f32[16,640]{1,0:T(8,128)S(1)}, f32[16,640]{1,0:T(8,128)S(1)}, u32[]{:S(2)}, u32[]{:S(2)}) collective-permute-start(f32[16,640]{1,0:T(8,128)S(1)} %get-tuple-element.30), channel_id=1, source_target_pairs={{0,12},{1,11},{2,14},{3,9},{4,8},{5,15},{6,10},{7,13},{8,4},{9,3},... | collective-permute-start | bytes 122888 | tf_op jit(solution)/shard_map/ppermute | solution.py:558
  15.8 4.5 %collective-permute-start.5 = (f32[16,640]{1,0:T(8,128)S(1)}, f32[16,640]{1,0:T(8,128)S(1)}, u32[]{:S(2)}, u32[]{:S(2)}) collective-permute-start(f32[16,640]{1,0:T(8,128)S(1)} %get-tuple-element.31), channel_id=1, source_target_pairs={{0,4},{1,3},{2,6},{3,1},{4,0},{5,7},{6,2},{7,5},{8,12},{9,11},{10,... | collective-permute-start | bytes 122888 | tf_op jit(solution)/shard_map/ppermute | solution.py:558
  16.0 30.9 %slice-start.2 = ((s8[16777216]{0:T(1024)(128)(4,1)}), s8[4194304]{0:T(1024)(128)(4,1)S(1)}, s32[]{:S(2)}) async-start(s8[16777216]{0:T(1024)(128)(4,1)} %bitcast.5), calls=%async_computation.4 | async-start | bytes 8388608
  20.6 1.2 %collective-permute-start.6 = (f32[8,1024]{1,0:T(8,128)S(1)}, f32[8,1024]{1,0:T(8,128)S(1)}, u32[]{:S(2)}, u32[]{:S(2)}) collective-permute-start(f32[8,1024]{1,0:T(8,128)S(1)} %get-tuple-element.37), channel_id=1, source_target_pairs={{0,1},{1,0},{2,3},{3,2},{4,5},{5,4},{6,7},{7,6},{8,9},{9,8},{10,11... | collective-permute-start | bytes 98312 | tf_op jit(solution)/shard_map/ppermute | solution.py:546
  21.9 4.7 %collective-permute-start.7 = (bf16[1,64,128]{2,1,0:T(8,128)(2,1)S(1)}, bf16[1,64,128]{2,1,0:T(8,128)(2,1)S(1)}, u32[]{:S(2)}, u32[]{:S(2)}) collective-permute-start(bf16[1,64,128]{2,1,0:T(8,128)(2,1)S(1)} %rotate.1.refs_0_.q_ref), channel_id=1, source_target_pairs={{0,8},{1,9},{2,10},{3,11},{4,12},{5,13},{6,14},{7,15},{8,0},{9,1},... | collective-permute-start | bytes 49160 | tf_op jit(solution)/shard_map/ppermute | solution.py:558
  23.2 5.5 %collective-permute-start.8 = (bf16[1,64,128]{2,1,0:T(8,128)(2,1)S(1)}, bf16[1,64,128]{2,1,0:T(8,128)(2,1)S(1)}, u32[]{:S(2)}, u32[]{:S(2)}) collective-permute-start(bf16[1,64,128]{2,1,0:T(8,128)(2,1)S(1)} %rotate.1.refs_0_.q_ref), channel_id=1, source_target_pairs={{0,12},{1,11},{2,14},{3,9},{4,8},{5,15},{6,10},{7,13},{8,4},{9,3},... | collective-permute-start | bytes 49160 | tf_op jit(solution)/shard_map/ppermute | solution.py:558
  24.4 4.4 %collective-permute-start.9 = (bf16[1,64,128]{2,1,0:T(8,128)(2,1)S(1)}, bf16[1,64,128]{2,1,0:T(8,128)(2,1)S(1)}, u32[]{:S(2)}, u32[]{:S(2)}) collective-permute-start(bf16[1,64,128]{2,1,0:T(8,128)(2,1)S(1)} %rotate.1.refs_0_.q_ref), channel_id=1, source_target_pairs={{0,4},{1,3},{2,6},{3,1},{4,0},{5,7},{6,2},{7,5},{8,12},{9,11},{10,... | collective-permute-start | bytes 49160 | tf_op jit(solution)/shard_map/ppermute | solution.py:558
  28.8 4.3 %collective-permute-start.10 = (bf16[4,64,128]{2,1,0:T(8,128)(2,1)S(1)}, bf16[4,64,128]{2,1,0:T(8,128)(2,1)S(1)}, u32[]{:S(2)}, u32[]{:S(2)}) collective-permute-start(bf16[4,64,128]{2,1,0:T(8,128)(2,1)S(1)} %join.1.refs_3_), channel_id=1, source_target_pairs={{0,2},{1,5},{2,0},{3,7},{4,6},{5,1},{6,4},{7,3},{8,10},{9,13},{10,... | collective-permute-start | bytes 196616 | tf_op jit(solution)/shard_map/ppermute | solution.py:558
  30.4 16.5 %slice-start.3 = ((s8[16777216]{0:T(1024)(128)(4,1)}), s8[4194304]{0:T(1024)(128)(4,1)S(1)}, s32[]{:S(2)}) async-start(s8[16777216]{0:T(1024)(128)(4,1)} %bitcast.5), calls=%async_computation.5 | async-start | bytes 8388608

commit v21 on v20

--- a/solution.py
+++ b/solution.py
@@ -46,23 +46,6 @@
 
 def rank_of(place, bank, slot):
     return place ^ (slot + bank * (exchanged(slot) - slot))
-
-
-def start_columns(weight, column, target, sems):
-    depth, width = target.shape
-    part = depth // CHUNKS
-    copies = []
-    for c in range(CHUNKS):
-        rows = pl.ds(c * part, part)
-        copies.append(
-            pltpu.make_async_copy(
-                weight.at[rows, pl.ds(pl.multiple_of(column, width), width)],
-                target.at[rows, :],
-                sems.at[c],
-            )
-        )
-        copies[-1].start()
-    return copies
 
 
 def adapter_column(refs, bank, count):
@@ -77,13 +60,33 @@
 
 
 def start_slots(parity, place, bank, w_ref, w_buf, sems):
-    count, _, width = w_buf.shape
+    count, depth, width = w_buf.shape
+    part = depth // CHUNKS
     copies = []
-    for s in range(count):
-        target = rank_of(place[0], bank[0], 2 * s + parity)
-        first = (2 * target + bank[0]) * width
-        copies.append(start_columns(w_ref, first, w_buf.at[s], sems.at[s]))
+    for c in range(CHUNKS):
+        rows = pl.ds(c * part, part)
+        copies.append([])
+        for s in range(count):
+            target = rank_of(place[0], bank[0], 2 * s + parity)
+            columns = pl.ds(pl.multiple_of((2 * target + bank[0]) * width, width), width)
+            copy = pltpu.make_async_copy(
+                w_ref.at[rows, columns], w_buf.at[s, rows], sems.at[s, c]
+            )
+            copy.start()
+            copies[-1].append(copy)
     return copies
+
+
+def slot_products(x, copies, w_buf, out):
+    count, depth, width = w_buf.shape
+    part = depth // CHUNKS
+    for c, chunk in enumerate(copies):
+        rows = slice(c * part, (c + 1) * part)
+        for s, copy in enumerate(chunk):
+            copy.wait()
+            columns = slice(s * width, (s + 1) * width)
+            product = jnp.dot(x[:, rows], w_buf[s, rows], preferred_element_type=F32)
+            out[:, columns] = product if c == 0 else out[:, columns] + product
 
 
 def wait_all(copies):
@@ -138,7 +141,6 @@
 ):
     out, inner, column_out, w_buf, sems = refs
     copies = start_slots(1, place, bank, w_ref, w_buf, sems)
-    width = w_buf.shape[2]
     x = beam_rows(x_ref, other_ref)
     adapters, rank, depth = down_ref.shape
     every = lax.dot_general(
@@ -156,11 +158,8 @@
         part = every[:, j * HEAD_DIM : (j + 1) * HEAD_DIM]
         total += jnp.where(lane // rank + j * per == column, part, 0.0)
     inner[...] = total
-    out[:, len(copies) * width :] = total
-    for s, slot in enumerate(copies):
-        wait_all(slot)
-        columns = slice(s * width, (s + 1) * width)
-        out[:, columns] = jnp.dot(x, w_buf[s], preferred_element_type=F32)
+    out[:, out.shape[1] - HEAD_DIM :] = total
+    slot_products(x, copies, w_buf, out)
 
 
 def project_sent(place, bank, index, x, other, down, wq, ranks):
@@ -189,7 +188,6 @@
     place, bank, length, x_ref, other_ref, w_ref, out, length_out, w_buf, sems
 ):
     copies = start_slots(0, place, bank, w_ref, w_buf, sems)
-    width = w_buf.shape[2]
     beams = x_ref.shape[0]
     row = iota(length_out.shape, 0)
     limit = jnp.zeros(length_out.shape, jnp.int32)
@@ -197,10 +195,7 @@
         limit = jnp.where(row // (length_out.shape[0] // beams) == beam, length[beam], limit)
     length_out[...] = limit
     x = beam_rows(x_ref, other_ref)
-    for s, slot in enumerate(copies):
-        wait_all(slot)
-        columns = slice(s * width, (s + 1) * width)
-        out[:, columns] = jnp.dot(x, w_buf[s], preferred_element_type=F32)
+    slot_products(x, copies, w_buf, out)
 
 
 def project_kept(place, bank, length, x, other, wq, ranks):

time: 59.8 us -> 59.8 us (level)
  no operation moved by 1% of the time
where the time goes in v21:
time: 59.8 us; the launch traced here: 59.6 us
  blocking collectives  21.5 us (36%)
  Pallas kernels  15.5 us (26%)
  starting transfers between devices  13.1 us (22%)
  waiting for transfers between devices  9.1 us (15%)
    all_to_all x2, blocking collectives, traded(): return lax.all_to_all(blocks, 'tensor', 0, 0, tiled=True)  21.5 us
    ppermute x8, starting transfers between devices, hop(): return lax.ppermute(x, ('tensor', 'bank'), pairs)  12.6 us
    ppermute x8, waiting for transfers between devices, hop(): return lax.ppermute(x, ('tensor', 'bank'), pairs)  8 us
    pallas_call x1, Pallas kernels, project_kept(): pl.pallas_call(project_kept_kernel, in_specs=[scalar()] * 3 + [whole()] *...  3.3 us
    pallas_call x2, Pallas kernels, attend(): pl.pallas_call(lambda *refs: attend_kernel(slots, earlier, *refs), in_spe...  3.12 us
    pallas_call x1, Pallas kernels, project_sent(): pl.pallas_call(project_sent_kernel, in_specs=[scalar()] * 2 + [whole()] *...  3.01 us
    pallas_call x1, Pallas kernels, output(): pl.pallas_call(output_kernel, in_specs=[whole()] * 2, out_specs=whole(),...  2.28 us
    pallas_call x1, Pallas kernels, fetch(): pl.pallas_call(fetch_kernel, in_specs=[big()], out_specs=whole(), out_sha...  1.56 us
  transfers between devices with their start and end apart: 11, of which 5 were waited for; matrix products, arithmetic and copies ran while one was open for 0% of the time, Pallas kernels for 12%

profile of v21, /device:TPU:0, one launch (start us, length us, event | category | flops | bytes accessed | tf_op | source)
XLA Modules:
  0.0 59.6 jit_solution(14697041879242559623)
XLA Ops:
  0.0 0.0 copy-start.4
  0.0 0.0 copy-start.5
  0.0 0.5 collective-permute-start
  0.5 0.1 collective-permute-start.1
  0.5 1.6 %fetch.1.down_ref = bf16[16,64,1024]{2,1,0:T(8,128)(2,1)S(1)} custom-call(bf16[16,64,1024]{2,1,0:T(8,128)(2,1)} %bitcast.9), custom_call_target="tpu_custom_call" | custom-call | bytes 2097152 | tf_op jit(solution)/shard_map/fetch/pallas_call | solution.py:112
  2.1 0.0 collective-permute-done.1
  2.1 0.0 collective-permute-done.other_ref
  2.1 0.0 copy-done.4
  2.1 0.0 copy-done.5
  2.1 0.0 copy-start.6
  2.1 3.0 %project_sent.1 = (f32[16,2176]{1,0:T(8,128)S(1)}, f32[16,128]{1,0:T(8,128)S(1)}, s32[16,128]{1,0:T(8,128)S(1)}) custom-call(s32[1]{0:T(128)} %bitcast.place.refs_0_, s32[1]{0:T(128)} %bitcast.1.bank.refs_1_, s32[1,8]{1,0:T(1,128)S(1)} %bitcast.7, s32[1,8]{1,0:T(1,128)S(1)} %bitcast.8, bf16[8,1024]{1,0:T(8,128)(2,1)S(1)} %copy-done.4, ...), custom_call_target="tpu_custom_call" | custom-call | flops 100663296 | bytes 6291456 | tf_op jit(solution)/shard_map/project_sent/pallas_call | solution.py:167
  5.2 0.0 copy-start.2
  5.2 3.0 %collective-permute-start.2 = (f32[16,2176]{1,0:T(8,128)S(1)}, f32[16,2176]{1,0:T(8,128)S(1)}, u32[]{:S(2)}, u32[]{:S(2)}) collective-permute-start(f32[16,2176]{1,0:T(8,128)S(1)} %get-tuple-element.26), channel_id=1, source_target_pairs={{0,2},{1,5},{2,0},{3,7},{4,6},{5,1},{6,4},{7,3},{8,10},{9,13},{10,... | collective-permute-start | bytes 417800 | tf_op jit(solution)/shard_map/ppermute | solution.py:553
  8.2 0.0 copy-done.6
  8.2 0.0 copy-start.3
  8.2 0.0 copy-start.1
  8.2 0.0 slice-start
  8.2 0.0 slice-start.1
  8.2 3.3 %project_kept.1 = (f32[16,2048]{1,0:T(8,128)S(1)}, s32[64,128]{1,0:T(8,128)S(1)}) custom-call(s32[1]{0:T(128)} %bitcast.place.refs_0_, s32[1]{0:T(128)} %bitcast.1.bank.refs_1_, s32[8]{0:T(128)S(1)} %copy-done.6, bf16[8,1024]{1,0:T(8,128)(2,1)S(1)} %copy-done.4, bf16[8,1024]{1,0:T(8,128)(2,1)S(1)} %collective-permute-done.other_ref, bf16[1024,8192]{1,0:T(8,128)(2,1)} %w_ref.5), custom_call_target="tpu_custom_call" | custom-call | flops 67108864 | bytes 16777216 | tf_op jit(solution)/shard_map/project_kept/pallas_call | solution.py:203
  11.5 0.0 copy-start
  11.5 0.0 collective-permute-done.2.came_ref
  11.6 2.8 %collective-permute-start.3 = (f32[16,640]{1,0:T(8,128)S(1)}, f32[16,640]{1,0:T(8,128)S(1)}, u32[]{:S(2)}, u32[]{:S(2)}) collective-permute-start(f32[16,640]{1,0:T(8,128)S(1)} %get-tuple-element.29), channel_id=1, source_target_pairs={{0,8},{1,9},{2,10},{3,11},{4,12},{5,13},{6,14},{7,15},{8,0},{9,1},... | collective-permute-start | bytes 122888 | tf_op jit(solution)/shard_map/ppermute | solution.py:553
  14.4 1.3 %collective-permute-start.4 = (f32[16,640]{1,0:T(8,128)S(1)}, f32[16,640]{1,0:T(8,128)S(1)}, u32[]{:S(2)}, u32[]{:S(2)}) collective-permute-start(f32[16,640]{1,0:T(8,128)S(1)} %get-tuple-element.30), channel_id=1, source_target_pairs={{0,12},{1,11},{2,14},{3,9},{4,8},{5,15},{6,10},{7,13},{8,4},{9,3},... | collective-permute-start | bytes 122888 | tf_op jit(solution)/shard_map/ppermute | solution.py:553
  15.8 0.2 collective-permute-start.5
  16.0 0.0 copy-done.2
  16.0 0.0 slice-start.2
  16.0 0.6 %keyval.1.refs_7_ = f32[8,24,128]{2,1,0:T(8,128)S(1)} custom-call(bf16[8,1024]{1,0:T(8,128)(2,1)S(1)} %copy-done.4, bf16[1024,2048]{1,0:T(8,128)(2,1)S(1)} %copy-done.2), custom_call_target="tpu_custom_call" | custom-call | flops 33554432 | bytes 4194304 | tf_op jit(solution)/shard_map/keyval/pallas_call | solution.py:234
  16.7 0.0 collective-permute-done.3.refs_1_
  16.7 3.5 %collective-permute-done.4.refs_2_ = f32[16,640]{1,0:T(8,128)S(1)} collective-permute-done((f32[16,640]{1,0:T(8,128)S(1)}, f32[16,640]{1,0:T(8,128)S(1)}, u32[]{:S(2)}, u32[]{:S(2)}) %collective-permute-start.4) | collective-permute-done | bytes 40992 | tf_op jit(solution)/shard_map/ppermute | solution.py:553
  20.2 0.0 collective-permute-done.5.refs_3_
  20.2 0.0 copy-done.3
  20.2 0.4 correct.1
  20.6 0.0 collective-permute-start.6
  20.6 0.1 fusion
  20.7 1.1 %collective-permute-done.6.came_ref = f32[8,1024]{1,0:T(8,128)S(1)} collective-permute-done((f32[8,1024]{1,0:T(8,128)S(1)}, f32[8,1024]{1,0:T(8,128)S(1)}, u32[]{:S(2)}, u32[]{:S(2)}) %collective-permute-start.6) | collective-permute-done | bytes 32800 | tf_op jit(solution)/shard_map/ppermute | solution.py:541
  21.8 0.1 rotate.1.refs_0_.q_ref
  21.9 1.3 %collective-permute-start.7 = (bf16[1,64,128]{2,1,0:T(8,128)(2,1)S(1)}, bf16[1,64,128]{2,1,0:T(8,128)(2,1)S(1)}, u32[]{:S(2)}, u32[]{:S(2)}) collective-permute-start(bf16[1,64,128]{2,1,0:T(8,128)(2,1)S(1)} %rotate.1.refs_0_.q_ref), channel_id=1, source_target_pairs={{0,8},{1,9},{2,10},{3,11},{4,12},{5,13},{6,14},{7,15},{8,0},{9,1},... | collective-permute-start | bytes 49160 | tf_op jit(solution)/shard_map/ppermute | solution.py:553
  23.2 1.2 %collective-permute-start.8 = (bf16[1,64,128]{2,1,0:T(8,128)(2,1)S(1)}, bf16[1,64,128]{2,1,0:T(8,128)(2,1)S(1)}, u32[]{:S(2)}, u32[]{:S(2)}) collective-permute-start(bf16[1,64,128]{2,1,0:T(8,128)(2,1)S(1)} %rotate.1.refs_0_.q_ref), channel_id=1, source_target_pairs={{0,12},{1,11},{2,14},{3,9},{4,8},{5,15},{6,10},{7,13},{8,4},{9,3},... | collective-permute-start | bytes 49160 | tf_op jit(solution)/shard_map/ppermute | solution.py:553
  24.4 1.1 %collective-permute-start.9 = (bf16[1,64,128]{2,1,0:T(8,128)(2,1)S(1)}, bf16[1,64,128]{2,1,0:T(8,128)(2,1)S(1)}, u32[]{:S(2)}, u32[]{:S(2)}) collective-permute-start(bf16[1,64,128]{2,1,0:T(8,128)(2,1)S(1)} %rotate.1.refs_0_.q_ref), channel_id=1, source_target_pairs={{0,4},{1,3},{2,6},{3,1},{4,0},{5,7},{6,2},{7,5},{8,12},{9,11},{10,... | collective-permute-start | bytes 49160 | tf_op jit(solution)/shard_map/ppermute | solution.py:553
  25.5 1.1 %collective-permute-done.7.refs_1_ = bf16[1,64,128]{2,1,0:T(8,128)(2,1)S(1)} collective-permute-done((bf16[1,64,128]{2,1,0:T(8,128)(2,1)S(1)}, bf16[1,64,128]{2,1,0:T(8,128)(2,1)S(1)}, u32[]{:S(2)}, u32[]{:S(2)}) %collective-permute-start.7) | collective-permute-done | bytes 16416 | tf_op jit(solution)/shard_map/ppermute | solution.py:553
  26.6 2.1 %collective-permute-done.8.refs_2_ = bf16[1,64,128]{2,1,0:T(8,128)(2,1)S(1)} collective-permute-done((bf16[1,64,128]{2,1,0:T(8,128)(2,1)S(1)}, bf16[1,64,128]{2,1,0:T(8,128)(2,1)S(1)}, u32[]{:S(2)}, u32[]{:S(2)}) %collective-permute-start.8) | collective-permute-done | bytes 16416 | tf_op jit(solution)/shard_map/ppermute | solution.py:553
  28.8 0.0 collective-permute-done.9.refs_3_
  28.8 1.6 %collective-permute-start.10 = (bf16[4,64,128]{2,1,0:T(8,128)(2,1)S(1)}, bf16[4,64,128]{2,1,0:T(8,128)(2,1)S(1)}, u32[]{:S(2)}, u32[]{:S(2)}) collective-permute-start(bf16[4,64,128]{2,1,0:T(8,128)(2,1)S(1)} %join.1.refs_3_), channel_id=1, source_target_pairs={{0,2},{1,5},{2,0},{3,7},{4,6},{5,1},{6,4},{7,3},{8,10},{9,13},{10,... | collective-permute-start | bytes 196616 | tf_op jit(solution)/shard_map/ppermute | solution.py:553
  30.4 0.0 copy-done.1
  30.4 0.0 copy-done
  30.4 0.0 slice-start.3
  30.4 1.6 %attend.2.refs_6_ = bf16[4,80,128]{2,1,0:T(8,128)(2,1)S(1)} custom-call(s32[1]{0:T(128)} %bitcast.place.refs_0_, s32[1]{0:T(128)} %bitcast.1.bank.refs_1_, s32[64,128]{1,0:T(8,128)S(1)} %get-tuple-element.22.refs_2_, bf16[4,64,128]{2,1,0:T(8,128)(2,1)S(1)} %join.1.refs_3_, bf16[8,256,1024]{2,1,0:T(8,128)(2,1)S(1)} %copy-done, bf16[8,256,1024]{2,1,0:T(8,128)(2,1)S(1)} %copy-done.1), custom_call_target="tpu_custom_call" | custom-call | flops 33554432 | bytes 4194304 | tf_op jit(solution)/shard_map/attend/pallas_call | solution.py:420
  31.9 1.2 %collective-permute-done.10.refs_3_ = bf16[4,64,128]{2,1,0:T(8,128)(2,1)S(1)} collective-permute-done((bf16[4,64,128]{2,1,0:T(8,128)(2,1)S(1)}, bf16[4,64,128]{2,1,0:T(8,128)(2,1)S(1)}, u32[]{:S(2)}, u32[]{:S(2)}) %collective-permute-start.10) | collective-permute-done | bytes 65568 | tf_op jit(solution)/shard_map/ppermute | solution.py:553
  33.1 1.6 %attend.3 = bf16[8,96,128]{2,1,0:T(8,128)(2,1)S(1)} custom-call(s32[1]{0:T(128)} %bitcast.place.refs_0_, s32[1]{0:T(128)} %bitcast.1.bank.refs_1_, s32[64,128]{1,0:T(8,128)S(1)} %get-tuple-element.22.refs_2_, bf16[4,64,128]{2,1,0:T(8,128)(2,1)S(1)} %collective-permute-done.10.refs_3_, bf16[8,256,1024]{2,1,0:T(8,128)(2,1)S(1)} %copy-done, ...), custom_call_target="tpu_custom_call" | custom-call | flops 33554432 | bytes 16777216 | tf_op jit(solution)/shard_map/attend/pallas_call | solution.py:420
  34.7 11.8 %all_to_all.10.parts_ref = bf16[8,96,128]{2,1,0:T(8,128)(2,1)S(1)} all-to-all(bf16[8,96,128]{2,1,0:T(8,128)(2,1)S(1)} %attend.3), channel_id=1, replica_groups=mesh['groups'=2,'tensor'=8,'bank'=2] {'tensor'}, dimensions={0} | all-to-all | bytes 393216 | tf_op jit(solution)/shard_map/all_to_all | solution.py:545
  46.4 0.4 combine.1.x_ref
  46.9 0.0 slice-done
  46.9 0.0 slice-done.1
  46.9 0.0 slice-done.2
  46.9 0.0 slice-done.3
  46.9 2.3 %output.1 = bf16[8,8,1024]{2,1,0:T(8,128)(2,1)S(1)} custom-call(bf16[8,1024]{1,0:T(8,128)(2,1)S(1)} %combine.1.x_ref, bf16[1024,8192]{1,0:T(8,128)(2,1)S(1)} %bitcast.6), custom_call_target="tpu_custom_call" | custom-call | flops 134217728 | bytes 16777216 | tf_op jit(solution)/shard_map/output/pallas_call | solution.py:511
  49.2 9.8 %all_to_all.11.parts_ref = bf16[8,8,1024]{2,1,0:T(8,128)(2,1)S(1)} all-to-all(bf16[8,8,1024]{2,1,0:T(8,128)(2,1)S(1)} %output.1), channel_id=1, replica_groups=mesh['groups'=2,'tensor'=8,'bank'=2] {'tensor'}, dimensions={0} | all-to-all | bytes 262144 | tf_op jit(solution)/shard_map/all_to_all | solution.py:545
  59.0 0.6 %residual.1 = bf16[8,1024]{1,0:T(8,128)(2,1)} custom-call(bf16[8,1024]{1,0:T(8,128)(2,1)S(1)} %copy-done.4, bf16[8,8,1024]{2,1,0:T(8,128)(2,1)S(1)} %all_to_all.11.parts_ref), custom_call_target="tpu_custom_call" | custom-call | tf_op jit(solution)/shard_map/residual/pallas_call | solution.py:530
  (5 shorter events, 0.0 us)
Async XLA Ops:
  0.0 2.1 %copy-start.4 = (bf16[8,1024]{1,0:T(8,128)(2,1)S(1)}, bf16[8,1024]{1,0:T(8,128)(2,1)}, u32[]{:S(2)}) copy-start(bf16[8,1024]{1,0:T(8,128)(2,1)} %x_ref.6) | copy-start | bytes 49156
  0.0 2.1 %copy-start.5 = (s32[8]{0:T(128)S(1)}, s32[8]{0:T(128)}, u32[]{:S(2)}) copy-start(s32[8]{0:T(128)} %param.11) | copy-start | bytes 100
  0.0 2.1 %collective-permute-start = (bf16[8,1024]{1,0:T(8,128)(2,1)}, bf16[8,1024]{1,0:T(8,128)(2,1)S(1)}, u32[]{:S(2)}, u32[]{:S(2)}) collective-permute-start(bf16[8,1024]{1,0:T(8,128)(2,1)} %x_ref.6), channel_id=1, source_target_pairs={{0,1},{1,0},{2,3},{3,2},{4,5},{5,4},{6,7},{7,6},{8,9},{9,8},{10,11... | collective-permute-start | bytes 49160 | tf_op jit(solution)/shard_map/ppermute | solution.py:541
  0.5 1.6 %collective-permute-start.1 = (s32[8]{0:T(128)}, s32[8]{0:T(128)S(1)}, u32[]{:S(2)}, u32[]{:S(2)}) collective-permute-start(s32[8]{0:T(128)} %param.11), channel_id=1, source_target_pairs={{0,1},{1,0},{2,3},{3,2},{4,5},{5,4},{6,7},{7,6},{8,9},{9,8},{10,11... | collective-permute-start | bytes 104 | tf_op jit(solution)/shard_map/ppermute | solution.py:541
  2.1 6.1 %copy-start.6 = (s32[8]{0:T(128)S(1)}, s32[8]{0:T(128)}, u32[]{:S(2)}) copy-start(s32[8]{0:T(128)} %length.1) | copy-start | bytes 100
  5.2 10.8 %copy-start.2 = (bf16[1024,2048]{1,0:T(8,128)(2,1)S(1)}, bf16[1024,2048]{1,0:T(8,128)(2,1)}, u32[]{:S(2)}) copy-start(bf16[1024,2048]{1,0:T(8,128)(2,1)} %w_ref.6) | copy-start | bytes 12582916
  5.2 6.4 %collective-permute-start.2 = (f32[16,2176]{1,0:T(8,128)S(1)}, f32[16,2176]{1,0:T(8,128)S(1)}, u32[]{:S(2)}, u32[]{:S(2)}) collective-permute-start(f32[16,2176]{1,0:T(8,128)S(1)} %get-tuple-element.26), channel_id=1, source_target_pairs={{0,2},{1,5},{2,0},{3,7},{4,6},{5,1},{6,4},{7,3},{8,10},{9,13},{10,... | collective-permute-start | bytes 417800 | tf_op jit(solution)/shard_map/ppermute | solution.py:553
  8.2 12.0 %copy-start.3 = (bf16[16,64,1024]{2,1,0:T(8,128)(2,1)S(1)}, bf16[16,64,1024]{2,1,0:T(8,128)(2,1)}, u32[]{:S(2)}) copy-start(bf16[16,64,1024]{2,1,0:T(8,128)(2,1)} %up_ref.1) | copy-start | bytes 6291460
  8.2 22.2 %copy-start.1 = (bf16[8,256,1024]{2,1,0:T(8,128)(2,1)S(1)}, bf16[8,256,1024]{2,1,0:T(8,128)(2,1)}, u32[]{:S(2)}) copy-start(bf16[8,256,1024]{2,1,0:T(8,128)(2,1)} %refs_5_.3) | copy-start | bytes 12582916
  8.2 38.7 %slice-start = ((s8[16777216]{0:T(1024)(128)(4,1)}), s8[4194304]{0:T(1024)(128)(4,1)S(1)}, s32[]{:S(2)}) async-start(s8[16777216]{0:T(1024)(128)(4,1)} %bitcast.5), calls=%async_computation.2 | async-start | bytes 8388608
  8.2 38.7 %slice-start.1 = ((s8[16777216]{0:T(1024)(128)(4,1)}), s8[4194304]{0:T(1024)(128)(4,1)S(1)}, s32[]{:S(2)}) async-start(s8[16777216]{0:T(1024)(128)(4,1)} %bitcast.5), calls=%async_computation.3 | async-start | bytes 8388608
  11.5 18.8 %copy-start = (bf16[8,256,1024]{2,1,0:T(8,128)(2,1)S(1)}, bf16[8,256,1024]{2,1,0:T(8,128)(2,1)}, u32[]{:S(2)}) copy-start(bf16[8,256,1024]{2,1,0:T(8,128)(2,1)} %refs_4_.3) | copy-start | bytes 12582916
  11.6 5.1 %collective-permute-start.3 = (f32[16,640]{1,0:T(8,128)S(1)}, f32[16,640]{1,0:T(8,128)S(1)}, u32[]{:S(2)}, u32[]{:S(2)}) collective-permute-start(f32[16,640]{1,0:T(8,128)S(1)} %get-tuple-element.29), channel_id=1, source_target_pairs={{0,8},{1,9},{2,10},{3,11},{4,12},{5,13},{6,14},{7,15},{8,0},{9,1},... | collective-permute-start | bytes 122888 | tf_op jit(solution)/shard_map/ppermute | solution.py:553
  14.4 5.8 %collective-permute-start.4 = (f32[16,640]{1,0:T(8,128)S(1)}, f32[16,640]{1,0:T(8,128)S(1)}, u32[]{:S(2)}, u32[]{:S(2)}) collective-permute-start(f32[16,640]{1,0:T(8,128)S(1)} %get-tuple-element.30), channel_id=1, source_target_pairs={{0,12},{1,11},{2,14},{3,9},{4,8},{5,15},{6,10},{7,13},{8,4},{9,3},... | collective-permute-start | bytes 122888 | tf_op jit(solution)/shard_map/ppermute | solution.py:553
  15.8 4.5 %collective-permute-start.5 = (f32[16,640]{1,0:T(8,128)S(1)}, f32[16,640]{1,0:T(8,128)S(1)}, u32[]{:S(2)}, u32[]{:S(2)}) collective-permute-start(f32[16,640]{1,0:T(8,128)S(1)} %get-tuple-element.31), channel_id=1, source_target_pairs={{0,4},{1,3},{2,6},{3,1},{4,0},{5,7},{6,2},{7,5},{8,12},{9,11},{10,... | collective-permute-start | bytes 122888 | tf_op jit(solution)/shard_map/ppermute | solution.py:553
  16.0 30.9 %slice-start.2 = ((s8[16777216]{0:T(1024)(128)(4,1)}), s8[4194304]{0:T(1024)(128)(4,1)S(1)}, s32[]{:S(2)}) async-start(s8[16777216]{0:T(1024)(128)(4,1)} %bitcast.5), calls=%async_computation.4 | async-start | bytes 8388608
  20.6 1.2 %collective-permute-start.6 = (f32[8,1024]{1,0:T(8,128)S(1)}, f32[8,1024]{1,0:T(8,128)S(1)}, u32[]{:S(2)}, u32[]{:S(2)}) collective-permute-start(f32[8,1024]{1,0:T(8,128)S(1)} %get-tuple-element.37), channel_id=1, source_target_pairs={{0,1},{1,0},{2,3},{3,2},{4,5},{5,4},{6,7},{7,6},{8,9},{9,8},{10,11... | collective-permute-start | bytes 98312 | tf_op jit(solution)/shard_map/ppermute | solution.py:541
  21.9 4.7 %collective-permute-start.7 = (bf16[1,64,128]{2,1,0:T(8,128)(2,1)S(1)}, bf16[1,64,128]{2,1,0:T(8,128)(2,1)S(1)}, u32[]{:S(2)}, u32[]{:S(2)}) collective-permute-start(bf16[1,64,128]{2,1,0:T(8,128)(2,1)S(1)} %rotate.1.refs_0_.q_ref), channel_id=1, source_target_pairs={{0,8},{1,9},{2,10},{3,11},{4,12},{5,13},{6,14},{7,15},{8,0},{9,1},... | collective-permute-start | bytes 49160 | tf_op jit(solution)/shard_map/ppermute | solution.py:553
  23.2 5.5 %collective-permute-start.8 = (bf16[1,64,128]{2,1,0:T(8,128)(2,1)S(1)}, bf16[1,64,128]{2,1,0:T(8,128)(2,1)S(1)}, u32[]{:S(2)}, u32[]{:S(2)}) collective-permute-start(bf16[1,64,128]{2,1,0:T(8,128)(2,1)S(1)} %rotate.1.refs_0_.q_ref), channel_id=1, source_target_pairs={{0,12},{1,11},{2,14},{3,9},{4,8},{5,15},{6,10},{7,13},{8,4},{9,3},... | collective-permute-start | bytes 49160 | tf_op jit(solution)/shard_map/ppermute | solution.py:553
  24.4 4.4 %collective-permute-start.9 = (bf16[1,64,128]{2,1,0:T(8,128)(2,1)S(1)}, bf16[1,64,128]{2,1,0:T(8,128)(2,1)S(1)}, u32[]{:S(2)}, u32[]{:S(2)}) collective-permute-start(bf16[1,64,128]{2,1,0:T(8,128)(2,1)S(1)} %rotate.1.refs_0_.q_ref), channel_id=1, source_target_pairs={{0,4},{1,3},{2,6},{3,1},{4,0},{5,7},{6,2},{7,5},{8,12},{9,11},{10,... | collective-permute-start | bytes 49160 | tf_op jit(solution)/shard_map/ppermute | solution.py:553
  28.8 4.3 %collective-permute-start.10 = (bf16[4,64,128]{2,1,0:T(8,128)(2,1)S(1)}, bf16[4,64,128]{2,1,0:T(8,128)(2,1)S(1)}, u32[]{:S(2)}, u32[]{:S(2)}) collective-permute-start(bf16[4,64,128]{2,1,0:T(8,128)(2,1)S(1)} %join.1.refs_3_), channel_id=1, source_target_pairs={{0,2},{1,5},{2,0},{3,7},{4,6},{5,1},{6,4},{7,3},{8,10},{9,13},{10,... | collective-permute-start | bytes 196616 | tf_op jit(solution)/shard_map/ppermute | solution.py:553
  30.4 16.5 %slice-start.3 = ((s8[16777216]{0:T(1024)(128)(4,1)}), s8[4194304]{0:T(1024)(128)(4,1)S(1)}, s32[]{:S(2)}) async-start(s8[16777216]{0:T(1024)(128)(4,1)} %bitcast.5), calls=%async_computation.5 | async-start | bytes 8388608

commit v22 on v21

--- a/solution.py
+++ b/solution.py
@@ -143,12 +143,14 @@
     copies = start_slots(1, place, bank, w_ref, w_buf, sems)
     x = beam_rows(x_ref, other_ref)
     adapters, rank, depth = down_ref.shape
+    wide = jnp.concatenate([x, jnp.zeros((HEAD_DIM - x.shape[0], depth), BF16)], axis=0)
     every = lax.dot_general(
-        x,
         down_ref[...].reshape(adapters * rank, depth),
+        wide,
         (((1,), (1,)), ((), ())),
         preferred_element_type=F32,
     )
+    every = jnp.transpose(every)[: x.shape[0]]
     column = adapter_column((own_ref, came_ref), bank[0], adapters)
     column_out[...] = column
     lane = iota(column.shape, 1)

time: 59.8 us -> 60.6 us (1.013)
  Pallas kernels: 15.5 us -> 16.3 us
    pallas_call x1, Pallas kernels: 3.01 us -> 3.82 us  [project_sent(): pl.pallas_call(project_sent_kernel, in_specs=[scalar()] * 2 + [whole()] *...]
where the time goes in v22:
time: 60.6 us; the launch traced here: 60.4 us
  blocking collectives  21.5 us (35%)
  Pallas kernels  16.3 us (27%)
  starting transfers between devices  13.1 us (22%)
  waiting for transfers between devices  9.1 us (15%)
    all_to_all x2, blocking collectives, traded(): return lax.all_to_all(blocks, 'tensor', 0, 0, tiled=True)  21.5 us
    ppermute x8, starting transfers between devices, hop(): return lax.ppermute(x, ('tensor', 'bank'), pairs)  12.6 us
    ppermute x8, waiting for transfers between devices, hop(): return lax.ppermute(x, ('tensor', 'bank'), pairs)  8 us
    pallas_call x1, Pallas kernels, project_sent(): pl.pallas_call(project_sent_kernel, in_specs=[scalar()] * 2 + [whole()] *...  3.82 us
    pallas_call x1, Pallas kernels, project_kept(): pl.pallas_call(project_kept_kernel, in_specs=[scalar()] * 3 + [whole()] *...  3.3 us
    pallas_call x2, Pallas kernels, attend(): pl.pallas_call(lambda *refs: attend_kernel(slots, earlier, *refs), in_spe...  3.12 us
    pallas_call x1, Pallas kernels, output(): pl.pallas_call(output_kernel, in_specs=[whole()] * 2, out_specs=whole(),...  2.28 us
    pallas_call x1, Pallas kernels, fetch(): pl.pallas_call(fetch_kernel, in_specs=[big()], out_specs=whole(), out_sha...  1.56 us
  transfers between devices with their start and end apart: 11, of which 5 were waited for; matrix products, arithmetic and copies ran while one was open for 0% of the time, Pallas kernels for 12%

profile of v22, /device:TPU:0, one launch (start us, length us, event | category | flops | bytes accessed | tf_op | source)
XLA Modules:
  0.0 60.4 jit_solution(8439466675935514512)
XLA Ops:
  0.0 0.0 copy-start.4
  0.0 0.0 copy-start.5
  0.0 0.5 collective-permute-start
  0.5 0.1 collective-permute-start.1
  0.5 1.6 %fetch.1.down_ref = bf16[16,64,1024]{2,1,0:T(8,128)(2,1)S(1)} custom-call(bf16[16,64,1024]{2,1,0:T(8,128)(2,1)} %bitcast.9), custom_call_target="tpu_custom_call" | custom-call | bytes 2097152 | tf_op jit(solution)/shard_map/fetch/pallas_call | solution.py:112
  2.1 0.0 collective-permute-done.1
  2.1 0.0 collective-permute-done.other_ref
  2.1 0.0 copy-done.4
  2.1 0.0 copy-done.5
  2.1 0.0 copy-start.6
  2.1 3.8 %project_sent.1 = (f32[16,2176]{1,0:T(8,128)S(1)}, f32[16,128]{1,0:T(8,128)S(1)}, s32[16,128]{1,0:T(8,128)S(1)}) custom-call(s32[1]{0:T(128)} %bitcast.place.refs_0_, s32[1]{0:T(128)} %bitcast.1.bank.refs_1_, s32[1,8]{1,0:T(1,128)S(1)} %bitcast.7, s32[1,8]{1,0:T(1,128)S(1)} %bitcast.8, bf16[8,1024]{1,0:T(8,128)(2,1)S(1)} %copy-done.4, ...), custom_call_target="tpu_custom_call" | custom-call | flops 100663296 | bytes 6291456 | tf_op jit(solution)/shard_map/project_sent/pallas_call | solution.py:169
  6.0 0.0 copy-start.2
  6.0 3.0 %collective-permute-start.2 = (f32[16,2176]{1,0:T(8,128)S(1)}, f32[16,2176]{1,0:T(8,128)S(1)}, u32[]{:S(2)}, u32[]{:S(2)}) collective-permute-start(f32[16,2176]{1,0:T(8,128)S(1)} %get-tuple-element.26), channel_id=1, source_target_pairs={{0,2},{1,5},{2,0},{3,7},{4,6},{5,1},{6,4},{7,3},{8,10},{9,13},{10,... | collective-permute-start | bytes 417800 | tf_op jit(solution)/shard_map/ppermute | solution.py:555
  9.0 0.0 copy-done.6
  9.0 0.0 copy-start.3
  9.0 0.0 copy-start.1
  9.0 0.0 slice-start
  9.0 0.0 slice-start.1
  9.0 3.3 %project_kept.1 = (f32[16,2048]{1,0:T(8,128)S(1)}, s32[64,128]{1,0:T(8,128)S(1)}) custom-call(s32[1]{0:T(128)} %bitcast.place.refs_0_, s32[1]{0:T(128)} %bitcast.1.bank.refs_1_, s32[8]{0:T(128)S(1)} %copy-done.6, bf16[8,1024]{1,0:T(8,128)(2,1)S(1)} %copy-done.4, bf16[8,1024]{1,0:T(8,128)(2,1)S(1)} %collective-permute-done.other_ref, bf16[1024,8192]{1,0:T(8,128)(2,1)} %w_ref.5), custom_call_target="tpu_custom_call" | custom-call | flops 67108864 | bytes 16777216 | tf_op jit(solution)/shard_map/project_kept/pallas_call | solution.py:205
  12.3 0.0 copy-start
  12.4 0.0 collective-permute-done.2.came_ref
  12.4 2.8 %collective-permute-start.3 = (f32[16,640]{1,0:T(8,128)S(1)}, f32[16,640]{1,0:T(8,128)S(1)}, u32[]{:S(2)}, u32[]{:S(2)}) collective-permute-start(f32[16,640]{1,0:T(8,128)S(1)} %get-tuple-element.29), channel_id=1, source_target_pairs={{0,8},{1,9},{2,10},{3,11},{4,12},{5,13},{6,14},{7,15},{8,0},{9,1},... | collective-permute-start | bytes 122888 | tf_op jit(solution)/shard_map/ppermute | solution.py:555
  15.2 1.3 %collective-permute-start.4 = (f32[16,640]{1,0:T(8,128)S(1)}, f32[16,640]{1,0:T(8,128)S(1)}, u32[]{:S(2)}, u32[]{:S(2)}) collective-permute-start(f32[16,640]{1,0:T(8,128)S(1)} %get-tuple-element.30), channel_id=1, source_target_pairs={{0,12},{1,11},{2,14},{3,9},{4,8},{5,15},{6,10},{7,13},{8,4},{9,3},... | collective-permute-start | bytes 122888 | tf_op jit(solution)/shard_map/ppermute | solution.py:555
  16.6 0.2 collective-permute-start.5
  16.8 0.0 copy-done.2
  16.8 0.0 slice-start.2
  16.8 0.6 %keyval.1.refs_7_ = f32[8,24,128]{2,1,0:T(8,128)S(1)} custom-call(bf16[8,1024]{1,0:T(8,128)(2,1)S(1)} %copy-done.4, bf16[1024,2048]{1,0:T(8,128)(2,1)S(1)} %copy-done.2), custom_call_target="tpu_custom_call" | custom-call | flops 33554432 | bytes 4194304 | tf_op jit(solution)/shard_map/keyval/pallas_call | solution.py:236
  17.5 0.0 collective-permute-done.3.refs_1_
  17.5 3.5 %collective-permute-done.4.refs_2_ = f32[16,640]{1,0:T(8,128)S(1)} collective-permute-done((f32[16,640]{1,0:T(8,128)S(1)}, f32[16,640]{1,0:T(8,128)S(1)}, u32[]{:S(2)}, u32[]{:S(2)}) %collective-permute-start.4) | collective-permute-done | bytes 40992 | tf_op jit(solution)/shard_map/ppermute | solution.py:555
  21.0 0.0 collective-permute-done.5.refs_3_
  21.0 0.0 copy-done.3
  21.0 0.4 correct.1
  21.4 0.0 collective-permute-start.6
  21.4 0.1 fusion
  21.5 1.1 %collective-permute-done.6.came_ref = f32[8,1024]{1,0:T(8,128)S(1)} collective-permute-done((f32[8,1024]{1,0:T(8,128)S(1)}, f32[8,1024]{1,0:T(8,128)S(1)}, u32[]{:S(2)}, u32[]{:S(2)}) %collective-permute-start.6) | collective-permute-done | bytes 32800 | tf_op jit(solution)/shard_map/ppermute | solution.py:543
  22.6 0.1 rotate.1.refs_0_.q_ref
  22.7 1.3 %collective-permute-start.7 = (bf16[1,64,128]{2,1,0:T(8,128)(2,1)S(1)}, bf16[1,64,128]{2,1,0:T(8,128)(2,1)S(1)}, u32[]{:S(2)}, u32[]{:S(2)}) collective-permute-start(bf16[1,64,128]{2,1,0:T(8,128)(2,1)S(1)} %rotate.1.refs_0_.q_ref), channel_id=1, source_target_pairs={{0,8},{1,9},{2,10},{3,11},{4,12},{5,13},{6,14},{7,15},{8,0},{9,1},... | collective-permute-start | bytes 49160 | tf_op jit(solution)/shard_map/ppermute | solution.py:555
  24.0 1.2 %collective-permute-start.8 = (bf16[1,64,128]{2,1,0:T(8,128)(2,1)S(1)}, bf16[1,64,128]{2,1,0:T(8,128)(2,1)S(1)}, u32[]{:S(2)}, u32[]{:S(2)}) collective-permute-start(bf16[1,64,128]{2,1,0:T(8,128)(2,1)S(1)} %rotate.1.refs_0_.q_ref), channel_id=1, source_target_pairs={{0,12},{1,11},{2,14},{3,9},{4,8},{5,15},{6,10},{7,13},{8,4},{9,3},... | collective-permute-start | bytes 49160 | tf_op jit(solution)/shard_map/ppermute | solution.py:555
  25.2 1.1 %collective-permute-start.9 = (bf16[1,64,128]{2,1,0:T(8,128)(2,1)S(1)}, bf16[1,64,128]{2,1,0:T(8,128)(2,1)S(1)}, u32[]{:S(2)}, u32[]{:S(2)}) collective-permute-start(bf16[1,64,128]{2,1,0:T(8,128)(2,1)S(1)} %rotate.1.refs_0_.q_ref), channel_id=1, source_target_pairs={{0,4},{1,3},{2,6},{3,1},{4,0},{5,7},{6,2},{7,5},{8,12},{9,11},{10,... | collective-permute-start | bytes 49160 | tf_op jit(solution)/shard_map/ppermute | solution.py:555
  26.3 1.1 %collective-permute-done.7.refs_1_ = bf16[1,64,128]{2,1,0:T(8,128)(2,1)S(1)} collective-permute-done((bf16[1,64,128]{2,1,0:T(8,128)(2,1)S(1)}, bf16[1,64,128]{2,1,0:T(8,128)(2,1)S(1)}, u32[]{:S(2)}, u32[]{:S(2)}) %collective-permute-start.7) | collective-permute-done | bytes 16416 | tf_op jit(solution)/shard_map/ppermute | solution.py:555
  27.4 2.1 %collective-permute-done.8.refs_2_ = bf16[1,64,128]{2,1,0:T(8,128)(2,1)S(1)} collective-permute-done((bf16[1,64,128]{2,1,0:T(8,128)(2,1)S(1)}, bf16[1,64,128]{2,1,0:T(8,128)(2,1)S(1)}, u32[]{:S(2)}, u32[]{:S(2)}) %collective-permute-start.8) | collective-permute-done | bytes 16416 | tf_op jit(solution)/shard_map/ppermute | solution.py:555
  29.6 0.0 collective-permute-done.9.refs_3_
  29.6 1.6 %collective-permute-start.10 = (bf16[4,64,128]{2,1,0:T(8,128)(2,1)S(1)}, bf16[4,64,128]{2,1,0:T(8,128)(2,1)S(1)}, u32[]{:S(2)}, u32[]{:S(2)}) collective-permute-start(bf16[4,64,128]{2,1,0:T(8,128)(2,1)S(1)} %join.1.refs_3_), channel_id=1, source_target_pairs={{0,2},{1,5},{2,0},{3,7},{4,6},{5,1},{6,4},{7,3},{8,10},{9,13},{10,... | collective-permute-start | bytes 196616 | tf_op jit(solution)/shard_map/ppermute | solution.py:555
  31.2 0.0 copy-done.1
  31.2 0.0 copy-done
  31.2 0.0 slice-start.3
  31.2 1.6 %attend.2.refs_6_ = bf16[4,80,128]{2,1,0:T(8,128)(2,1)S(1)} custom-call(s32[1]{0:T(128)} %bitcast.place.refs_0_, s32[1]{0:T(128)} %bitcast.1.bank.refs_1_, s32[64,128]{1,0:T(8,128)S(1)} %get-tuple-element.22.refs_2_, bf16[4,64,128]{2,1,0:T(8,128)(2,1)S(1)} %join.1.refs_3_, bf16[8,256,1024]{2,1,0:T(8,128)(2,1)S(1)} %copy-done, bf16[8,256,1024]{2,1,0:T(8,128)(2,1)S(1)} %copy-done.1), custom_call_target="tpu_custom_call" | custom-call | flops 33554432 | bytes 4194304 | tf_op jit(solution)/shard_map/attend/pallas_call | solution.py:422
  32.7 1.2 %collective-permute-done.10.refs_3_ = bf16[4,64,128]{2,1,0:T(8,128)(2,1)S(1)} collective-permute-done((bf16[4,64,128]{2,1,0:T(8,128)(2,1)S(1)}, bf16[4,64,128]{2,1,0:T(8,128)(2,1)S(1)}, u32[]{:S(2)}, u32[]{:S(2)}) %collective-permute-start.10) | collective-permute-done | bytes 65568 | tf_op jit(solution)/shard_map/ppermute | solution.py:555
  33.9 1.6 %attend.3 = bf16[8,96,128]{2,1,0:T(8,128)(2,1)S(1)} custom-call(s32[1]{0:T(128)} %bitcast.place.refs_0_, s32[1]{0:T(128)} %bitcast.1.bank.refs_1_, s32[64,128]{1,0:T(8,128)S(1)} %get-tuple-element.22.refs_2_, bf16[4,64,128]{2,1,0:T(8,128)(2,1)S(1)} %collective-permute-done.10.refs_3_, bf16[8,256,1024]{2,1,0:T(8,128)(2,1)S(1)} %copy-done, ...), custom_call_target="tpu_custom_call" | custom-call | flops 33554432 | bytes 16777216 | tf_op jit(solution)/shard_map/attend/pallas_call | solution.py:422
  35.5 11.8 %all_to_all.10.parts_ref = bf16[8,96,128]{2,1,0:T(8,128)(2,1)S(1)} all-to-all(bf16[8,96,128]{2,1,0:T(8,128)(2,1)S(1)} %attend.3), channel_id=1, replica_groups=mesh['groups'=2,'tensor'=8,'bank'=2] {'tensor'}, dimensions={0} | all-to-all | bytes 393216 | tf_op jit(solution)/shard_map/all_to_all | solution.py:547
  47.3 0.4 combine.1.x_ref
  47.7 0.0 slice-done
  47.7 0.0 slice-done.1
  47.7 0.0 slice-done.2
  47.7 0.0 slice-done.3
  47.7 2.3 %output.1 = bf16[8,8,1024]{2,1,0:T(8,128)(2,1)S(1)} custom-call(bf16[8,1024]{1,0:T(8,128)(2,1)S(1)} %combine.1.x_ref, bf16[1024,8192]{1,0:T(8,128)(2,1)S(1)} %bitcast.6), custom_call_target="tpu_custom_call" | custom-call | flops 134217728 | bytes 16777216 | tf_op jit(solution)/shard_map/output/pallas_call | solution.py:513
  50.0 9.8 %all_to_all.11.parts_ref = bf16[8,8,1024]{2,1,0:T(8,128)(2,1)S(1)} all-to-all(bf16[8,8,1024]{2,1,0:T(8,128)(2,1)S(1)} %output.1), channel_id=1, replica_groups=mesh['groups'=2,'tensor'=8,'bank'=2] {'tensor'}, dimensions={0} | all-to-all | bytes 262144 | tf_op jit(solution)/shard_map/all_to_all | solution.py:547
  59.8 0.6 %residual.1 = bf16[8,1024]{1,0:T(8,128)(2,1)} custom-call(bf16[8,1024]{1,0:T(8,128)(2,1)S(1)} %copy-done.4, bf16[8,8,1024]{2,1,0:T(8,128)(2,1)S(1)} %all_to_all.11.parts_ref), custom_call_target="tpu_custom_call" | custom-call | tf_op jit(solution)/shard_map/residual/pallas_call | solution.py:532
  (5 shorter events, 0.0 us)
Async XLA Ops:
  0.0 2.1 %copy-start.4 = (bf16[8,1024]{1,0:T(8,128)(2,1)S(1)}, bf16[8,1024]{1,0:T(8,128)(2,1)}, u32[]{:S(2)}) copy-start(bf16[8,1024]{1,0:T(8,128)(2,1)} %x_ref.6) | copy-start | bytes 49156
  0.0 2.1 %copy-start.5 = (s32[8]{0:T(128)S(1)}, s32[8]{0:T(128)}, u32[]{:S(2)}) copy-start(s32[8]{0:T(128)} %param.11) | copy-start | bytes 100
  0.0 2.1 %collective-permute-start = (bf16[8,1024]{1,0:T(8,128)(2,1)}, bf16[8,1024]{1,0:T(8,128)(2,1)S(1)}, u32[]{:S(2)}, u32[]{:S(2)}) collective-permute-start(bf16[8,1024]{1,0:T(8,128)(2,1)} %x_ref.6), channel_id=1, source_target_pairs={{0,1},{1,0},{2,3},{3,2},{4,5},{5,4},{6,7},{7,6},{8,9},{9,8},{10,11... | collective-permute-start | bytes 49160 | tf_op jit(solution)/shard_map/ppermute | solution.py:543
  0.5 1.6 %collective-permute-start.1 = (s32[8]{0:T(128)}, s32[8]{0:T(128)S(1)}, u32[]{:S(2)}, u32[]{:S(2)}) collective-permute-start(s32[8]{0:T(128)} %param.11), channel_id=1, source_target_pairs={{0,1},{1,0},{2,3},{3,2},{4,5},{5,4},{6,7},{7,6},{8,9},{9,8},{10,11... | collective-permute-start | bytes 104 | tf_op jit(solution)/shard_map/ppermute | solution.py:543
  2.1 6.9 %copy-start.6 = (s32[8]{0:T(128)S(1)}, s32[8]{0:T(128)}, u32[]{:S(2)}) copy-start(s32[8]{0:T(128)} %length.1) | copy-start | bytes 100
  6.0 10.8 %copy-start.2 = (bf16[1024,2048]{1,0:T(8,128)(2,1)S(1)}, bf16[1024,2048]{1,0:T(8,128)(2,1)}, u32[]{:S(2)}) copy-start(bf16[1024,2048]{1,0:T(8,128)(2,1)} %w_ref.6) | copy-start | bytes 12582916
  6.0 6.4 %collective-permute-start.2 = (f32[16,2176]{1,0:T(8,128)S(1)}, f32[16,2176]{1,0:T(8,128)S(1)}, u32[]{:S(2)}, u32[]{:S(2)}) collective-permute-start(f32[16,2176]{1,0:T(8,128)S(1)} %get-tuple-element.26), channel_id=1, source_target_pairs={{0,2},{1,5},{2,0},{3,7},{4,6},{5,1},{6,4},{7,3},{8,10},{9,13},{10,... | collective-permute-start | bytes 417800 | tf_op jit(solution)/shard_map/ppermute | solution.py:555
  9.0 12.0 %copy-start.3 = (bf16[16,64,1024]{2,1,0:T(8,128)(2,1)S(1)}, bf16[16,64,1024]{2,1,0:T(8,128)(2,1)}, u32[]{:S(2)}) copy-start(bf16[16,64,1024]{2,1,0:T(8,128)(2,1)} %up_ref.1) | copy-start | bytes 6291460
  9.0 22.2 %copy-start.1 = (bf16[8,256,1024]{2,1,0:T(8,128)(2,1)S(1)}, bf16[8,256,1024]{2,1,0:T(8,128)(2,1)}, u32[]{:S(2)}) copy-start(bf16[8,256,1024]{2,1,0:T(8,128)(2,1)} %refs_5_.3) | copy-start | bytes 12582916
  9.0 38.7 %slice-start = ((s8[16777216]{0:T(1024)(128)(4,1)}), s8[4194304]{0:T(1024)(128)(4,1)S(1)}, s32[]{:S(2)}) async-start(s8[16777216]{0:T(1024)(128)(4,1)} %bitcast.5), calls=%async_computation.2 | async-start | bytes 8388608
  9.0 38.7 %slice-start.1 = ((s8[16777216]{0:T(1024)(128)(4,1)}), s8[4194304]{0:T(1024)(128)(4,1)S(1)}, s32[]{:S(2)}) async-start(s8[16777216]{0:T(1024)(128)(4,1)} %bitcast.5), calls=%async_computation.3 | async-start | bytes 8388608
  12.3 18.8 %copy-start = (bf16[8,256,1024]{2,1,0:T(8,128)(2,1)S(1)}, bf16[8,256,1024]{2,1,0:T(8,128)(2,1)}, u32[]{:S(2)}) copy-start(bf16[8,256,1024]{2,1,0:T(8,128)(2,1)} %refs_4_.3) | copy-start | bytes 12582916
  12.4 5.1 %collective-permute-start.3 = (f32[16,640]{1,0:T(8,128)S(1)}, f32[16,640]{1,0:T(8,128)S(1)}, u32[]{:S(2)}, u32[]{:S(2)}) collective-permute-start(f32[16,640]{1,0:T(8,128)S(1)} %get-tuple-element.29), channel_id=1, source_target_pairs={{0,8},{1,9},{2,10},{3,11},{4,12},{5,13},{6,14},{7,15},{8,0},{9,1},... | collective-permute-start | bytes 122888 | tf_op jit(solution)/shard_map/ppermute | solution.py:555
  15.2 5.8 %collective-permute-start.4 = (f32[16,640]{1,0:T(8,128)S(1)}, f32[16,640]{1,0:T(8,128)S(1)}, u32[]{:S(2)}, u32[]{:S(2)}) collective-permute-start(f32[16,640]{1,0:T(8,128)S(1)} %get-tuple-element.30), channel_id=1, source_target_pairs={{0,12},{1,11},{2,14},{3,9},{4,8},{5,15},{6,10},{7,13},{8,4},{9,3},... | collective-permute-start | bytes 122888 | tf_op jit(solution)/shard_map/ppermute | solution.py:555
  16.6 4.5 %collective-permute-start.5 = (f32[16,640]{1,0:T(8,128)S(1)}, f32[16,640]{1,0:T(8,128)S(1)}, u32[]{:S(2)}, u32[]{:S(2)}) collective-permute-start(f32[16,640]{1,0:T(8,128)S(1)} %get-tuple-element.31), channel_id=1, source_target_pairs={{0,4},{1,3},{2,6},{3,1},{4,0},{5,7},{6,2},{7,5},{8,12},{9,11},{10,... | collective-permute-start | bytes 122888 | tf_op jit(solution)/shard_map/ppermute | solution.py:555
  16.8 30.9 %slice-start.2 = ((s8[16777216]{0:T(1024)(128)(4,1)}), s8[4194304]{0:T(1024)(128)(4,1)S(1)}, s32[]{:S(2)}) async-start(s8[16777216]{0:T(1024)(128)(4,1)} %bitcast.5), calls=%async_computation.4 | async-start | bytes 8388608
  21.4 1.2 %collective-permute-start.6 = (f32[8,1024]{1,0:T(8,128)S(1)}, f32[8,1024]{1,0:T(8,128)S(1)}, u32[]{:S(2)}, u32[]{:S(2)}) collective-permute-start(f32[8,1024]{1,0:T(8,128)S(1)} %get-tuple-element.37), channel_id=1, source_target_pairs={{0,1},{1,0},{2,3},{3,2},{4,5},{5,4},{6,7},{7,6},{8,9},{9,8},{10,11... | collective-permute-start | bytes 98312 | tf_op jit(solution)/shard_map/ppermute | solution.py:543
  22.7 4.7 %collective-permute-start.7 = (bf16[1,64,128]{2,1,0:T(8,128)(2,1)S(1)}, bf16[1,64,128]{2,1,0:T(8,128)(2,1)S(1)}, u32[]{:S(2)}, u32[]{:S(2)}) collective-permute-start(bf16[1,64,128]{2,1,0:T(8,128)(2,1)S(1)} %rotate.1.refs_0_.q_ref), channel_id=1, source_target_pairs={{0,8},{1,9},{2,10},{3,11},{4,12},{5,13},{6,14},{7,15},{8,0},{9,1},... | collective-permute-start | bytes 49160 | tf_op jit(solution)/shard_map/ppermute | solution.py:555
  24.0 5.5 %collective-permute-start.8 = (bf16[1,64,128]{2,1,0:T(8,128)(2,1)S(1)}, bf16[1,64,128]{2,1,0:T(8,128)(2,1)S(1)}, u32[]{:S(2)}, u32[]{:S(2)}) collective-permute-start(bf16[1,64,128]{2,1,0:T(8,128)(2,1)S(1)} %rotate.1.refs_0_.q_ref), channel_id=1, source_target_pairs={{0,12},{1,11},{2,14},{3,9},{4,8},{5,15},{6,10},{7,13},{8,4},{9,3},... | collective-permute-start | bytes 49160 | tf_op jit(solution)/shard_map/ppermute | solution.py:555
  25.2 4.4 %collective-permute-start.9 = (bf16[1,64,128]{2,1,0:T(8,128)(2,1)S(1)}, bf16[1,64,128]{2,1,0:T(8,128)(2,1)S(1)}, u32[]{:S(2)}, u32[]{:S(2)}) collective-permute-start(bf16[1,64,128]{2,1,0:T(8,128)(2,1)S(1)} %rotate.1.refs_0_.q_ref), channel_id=1, source_target_pairs={{0,4},{1,3},{2,6},{3,1},{4,0},{5,7},{6,2},{7,5},{8,12},{9,11},{10,... | collective-permute-start | bytes 49160 | tf_op jit(solution)/shard_map/ppermute | solution.py:555
  29.6 4.3 %collective-permute-start.10 = (bf16[4,64,128]{2,1,0:T(8,128)(2,1)S(1)}, bf16[4,64,128]{2,1,0:T(8,128)(2,1)S(1)}, u32[]{:S(2)}, u32[]{:S(2)}) collective-permute-start(bf16[4,64,128]{2,1,0:T(8,128)(2,1)S(1)} %join.1.refs_3_), channel_id=1, source_target_pairs={{0,2},{1,5},{2,0},{3,7},{4,6},{5,1},{6,4},{7,3},{8,10},{9,13},{10,... | collective-permute-start | bytes 196616 | tf_op jit(solution)/shard_map/ppermute | solution.py:555
  31.2 16.5 %slice-start.3 = ((s8[16777216]{0:T(1024)(128)(4,1)}), s8[4194304]{0:T(1024)(128)(4,1)S(1)}, s32[]{:S(2)}) async-start(s8[16777216]{0:T(1024)(128)(4,1)} %bitcast.5), calls=%async_computation.5 | async-start | bytes 8388608

commit v23 on v21

--- a/solution.py
+++ b/solution.py
@@ -8,7 +8,7 @@
 HEAD_DIM = 128
 F32 = jnp.float32
 BF16 = jnp.bfloat16
-CHUNKS = 2
+CHUNKS = 1
 MIB = 1024 * 1024
 
 

time: 59.8 us -> 59.8 us (level)
  no operation moved by 1% of the time
where the time goes in v23:
time: 59.8 us; the launch traced here: 59.6 us
  blocking collectives  21.5 us (36%)
  Pallas kernels  15.4 us (26%)
  starting transfers between devices  13.1 us (22%)
  waiting for transfers between devices  9.1 us (15%)
    all_to_all x2, blocking collectives, traded(): return lax.all_to_all(blocks, 'tensor', 0, 0, tiled=True)  21.5 us
    ppermute x8, starting transfers between devices, hop(): return lax.ppermute(x, ('tensor', 'bank'), pairs)  12.6 us
    ppermute x8, waiting for transfers between devices, hop(): return lax.ppermute(x, ('tensor', 'bank'), pairs)  8 us
    pallas_call x1, Pallas kernels, project_kept(): pl.pallas_call(project_kept_kernel, in_specs=[scalar()] * 3 + [whole()] *...  3.29 us
    pallas_call x2, Pallas kernels, attend(): pl.pallas_call(lambda *refs: attend_kernel(slots, earlier, *refs), in_spe...  3.12 us
    pallas_call x1, Pallas kernels, project_sent(): pl.pallas_call(project_sent_kernel, in_specs=[scalar()] * 2 + [whole()] *...  3 us
    pallas_call x1, Pallas kernels, output(): pl.pallas_call(output_kernel, in_specs=[whole()] * 2, out_specs=whole(),...  2.28 us
    pallas_call x1, Pallas kernels, fetch(): pl.pallas_call(fetch_kernel, in_specs=[big()], out_specs=whole(), out_sha...  1.56 us
  transfers between devices with their start and end apart: 11, of which 5 were waited for; matrix products, arithmetic and copies ran while one was open for 0% of the time, Pallas kernels for 12%

profile of v23, /device:TPU:0, one launch (start us, length us, event | category | flops | bytes accessed | tf_op | source)
XLA Modules:
  0.0 59.6 jit_solution(1404435598059665680)
XLA Ops:
  0.0 0.0 copy-start.4
  0.0 0.0 copy-start.5
  0.0 0.5 collective-permute-start
  0.5 0.1 collective-permute-start.1
  0.5 1.6 %fetch.1.down_ref = bf16[16,64,1024]{2,1,0:T(8,128)(2,1)S(1)} custom-call(bf16[16,64,1024]{2,1,0:T(8,128)(2,1)} %bitcast.9), custom_call_target="tpu_custom_call" | custom-call | bytes 2097152 | tf_op jit(solution)/shard_map/fetch/pallas_call | solution.py:112
  2.1 0.0 collective-permute-done.1
  2.1 0.0 collective-permute-done.other_ref
  2.1 0.0 copy-done.4
  2.1 0.0 copy-done.5
  2.1 0.0 copy-start.6
  2.1 3.0 %project_sent.1 = (f32[16,2176]{1,0:T(8,128)S(1)}, f32[16,128]{1,0:T(8,128)S(1)}, s32[16,128]{1,0:T(8,128)S(1)}) custom-call(s32[1]{0:T(128)} %bitcast.place.refs_0_, s32[1]{0:T(128)} %bitcast.1.bank.refs_1_, s32[1,8]{1,0:T(1,128)S(1)} %bitcast.7, s32[1,8]{1,0:T(1,128)S(1)} %bitcast.8, bf16[8,1024]{1,0:T(8,128)(2,1)S(1)} %copy-done.4, ...), custom_call_target="tpu_custom_call" | custom-call | flops 100663296 | bytes 6291456 | tf_op jit(solution)/shard_map/project_sent/pallas_call | solution.py:167
  5.2 0.0 copy-start.2
  5.2 3.0 %collective-permute-start.2 = (f32[16,2176]{1,0:T(8,128)S(1)}, f32[16,2176]{1,0:T(8,128)S(1)}, u32[]{:S(2)}, u32[]{:S(2)}) collective-permute-start(f32[16,2176]{1,0:T(8,128)S(1)} %get-tuple-element.26), channel_id=1, source_target_pairs={{0,2},{1,5},{2,0},{3,7},{4,6},{5,1},{6,4},{7,3},{8,10},{9,13},{10,... | collective-permute-start | bytes 417800 | tf_op jit(solution)/shard_map/ppermute | solution.py:553
  8.2 0.0 copy-done.6
  8.2 0.0 copy-start.3
  8.2 0.0 copy-start.1
  8.2 0.0 slice-start
  8.2 0.0 slice-start.1
  8.2 3.3 %project_kept.1 = (f32[16,2048]{1,0:T(8,128)S(1)}, s32[64,128]{1,0:T(8,128)S(1)}) custom-call(s32[1]{0:T(128)} %bitcast.place.refs_0_, s32[1]{0:T(128)} %bitcast.1.bank.refs_1_, s32[8]{0:T(128)S(1)} %copy-done.6, bf16[8,1024]{1,0:T(8,128)(2,1)S(1)} %copy-done.4, bf16[8,1024]{1,0:T(8,128)(2,1)S(1)} %collective-permute-done.other_ref, bf16[1024,8192]{1,0:T(8,128)(2,1)} %w_ref.5), custom_call_target="tpu_custom_call" | custom-call | flops 67108864 | bytes 16777216 | tf_op jit(solution)/shard_map/project_kept/pallas_call | solution.py:203
  11.5 0.0 copy-start
  11.5 0.0 collective-permute-done.2.came_ref
  11.6 2.8 %collective-permute-start.3 = (f32[16,640]{1,0:T(8,128)S(1)}, f32[16,640]{1,0:T(8,128)S(1)}, u32[]{:S(2)}, u32[]{:S(2)}) collective-permute-start(f32[16,640]{1,0:T(8,128)S(1)} %get-tuple-element.29), channel_id=1, source_target_pairs={{0,8},{1,9},{2,10},{3,11},{4,12},{5,13},{6,14},{7,15},{8,0},{9,1},... | collective-permute-start | bytes 122888 | tf_op jit(solution)/shard_map/ppermute | solution.py:553
  14.4 1.3 %collective-permute-start.4 = (f32[16,640]{1,0:T(8,128)S(1)}, f32[16,640]{1,0:T(8,128)S(1)}, u32[]{:S(2)}, u32[]{:S(2)}) collective-permute-start(f32[16,640]{1,0:T(8,128)S(1)} %get-tuple-element.30), channel_id=1, source_target_pairs={{0,12},{1,11},{2,14},{3,9},{4,8},{5,15},{6,10},{7,13},{8,4},{9,3},... | collective-permute-start | bytes 122888 | tf_op jit(solution)/shard_map/ppermute | solution.py:553
  15.7 0.2 collective-permute-start.5
  16.0 0.0 copy-done.2
  16.0 0.0 slice-start.2
  16.0 0.6 %keyval.1.refs_7_ = f32[8,24,128]{2,1,0:T(8,128)S(1)} custom-call(bf16[8,1024]{1,0:T(8,128)(2,1)S(1)} %copy-done.4, bf16[1024,2048]{1,0:T(8,128)(2,1)S(1)} %copy-done.2), custom_call_target="tpu_custom_call" | custom-call | flops 33554432 | bytes 4194304 | tf_op jit(solution)/shard_map/keyval/pallas_call | solution.py:234
  16.7 0.0 collective-permute-done.3.refs_1_
  16.7 3.5 %collective-permute-done.4.refs_2_ = f32[16,640]{1,0:T(8,128)S(1)} collective-permute-done((f32[16,640]{1,0:T(8,128)S(1)}, f32[16,640]{1,0:T(8,128)S(1)}, u32[]{:S(2)}, u32[]{:S(2)}) %collective-permute-start.4) | collective-permute-done | bytes 40992 | tf_op jit(solution)/shard_map/ppermute | solution.py:553
  20.2 0.0 collective-permute-done.5.refs_3_
  20.2 0.0 copy-done.3
  20.2 0.4 correct.1
  20.6 0.0 collective-permute-start.6
  20.6 0.1 fusion
  20.7 1.1 %collective-permute-done.6.came_ref = f32[8,1024]{1,0:T(8,128)S(1)} collective-permute-done((f32[8,1024]{1,0:T(8,128)S(1)}, f32[8,1024]{1,0:T(8,128)S(1)}, u32[]{:S(2)}, u32[]{:S(2)}) %collective-permute-start.6) | collective-permute-done | bytes 32800 | tf_op jit(solution)/shard_map/ppermute | solution.py:541
  21.8 0.1 rotate.1.refs_0_.q_ref
  21.9 1.3 %collective-permute-start.7 = (bf16[1,64,128]{2,1,0:T(8,128)(2,1)S(1)}, bf16[1,64,128]{2,1,0:T(8,128)(2,1)S(1)}, u32[]{:S(2)}, u32[]{:S(2)}) collective-permute-start(bf16[1,64,128]{2,1,0:T(8,128)(2,1)S(1)} %rotate.1.refs_0_.q_ref), channel_id=1, source_target_pairs={{0,8},{1,9},{2,10},{3,11},{4,12},{5,13},{6,14},{7,15},{8,0},{9,1},... | collective-permute-start | bytes 49160 | tf_op jit(solution)/shard_map/ppermute | solution.py:553
  23.2 1.2 %collective-permute-start.8 = (bf16[1,64,128]{2,1,0:T(8,128)(2,1)S(1)}, bf16[1,64,128]{2,1,0:T(8,128)(2,1)S(1)}, u32[]{:S(2)}, u32[]{:S(2)}) collective-permute-start(bf16[1,64,128]{2,1,0:T(8,128)(2,1)S(1)} %rotate.1.refs_0_.q_ref), channel_id=1, source_target_pairs={{0,12},{1,11},{2,14},{3,9},{4,8},{5,15},{6,10},{7,13},{8,4},{9,3},... | collective-permute-start | bytes 49160 | tf_op jit(solution)/shard_map/ppermute | solution.py:553
  24.4 1.1 %collective-permute-start.9 = (bf16[1,64,128]{2,1,0:T(8,128)(2,1)S(1)}, bf16[1,64,128]{2,1,0:T(8,128)(2,1)S(1)}, u32[]{:S(2)}, u32[]{:S(2)}) collective-permute-start(bf16[1,64,128]{2,1,0:T(8,128)(2,1)S(1)} %rotate.1.refs_0_.q_ref), channel_id=1, source_target_pairs={{0,4},{1,3},{2,6},{3,1},{4,0},{5,7},{6,2},{7,5},{8,12},{9,11},{10,... | collective-permute-start | bytes 49160 | tf_op jit(solution)/shard_map/ppermute | solution.py:553
  25.5 1.1 %collective-permute-done.7.refs_1_ = bf16[1,64,128]{2,1,0:T(8,128)(2,1)S(1)} collective-permute-done((bf16[1,64,128]{2,1,0:T(8,128)(2,1)S(1)}, bf16[1,64,128]{2,1,0:T(8,128)(2,1)S(1)}, u32[]{:S(2)}, u32[]{:S(2)}) %collective-permute-start.7) | collective-permute-done | bytes 16416 | tf_op jit(solution)/shard_map/ppermute | solution.py:553
  26.6 2.1 %collective-permute-done.8.refs_2_ = bf16[1,64,128]{2,1,0:T(8,128)(2,1)S(1)} collective-permute-done((bf16[1,64,128]{2,1,0:T(8,128)(2,1)S(1)}, bf16[1,64,128]{2,1,0:T(8,128)(2,1)S(1)}, u32[]{:S(2)}, u32[]{:S(2)}) %collective-permute-start.8) | collective-permute-done | bytes 16416 | tf_op jit(solution)/shard_map/ppermute | solution.py:553
  28.7 0.0 collective-permute-done.9.refs_3_
  28.8 1.6 %collective-permute-start.10 = (bf16[4,64,128]{2,1,0:T(8,128)(2,1)S(1)}, bf16[4,64,128]{2,1,0:T(8,128)(2,1)S(1)}, u32[]{:S(2)}, u32[]{:S(2)}) collective-permute-start(bf16[4,64,128]{2,1,0:T(8,128)(2,1)S(1)} %join.1.refs_3_), channel_id=1, source_target_pairs={{0,2},{1,5},{2,0},{3,7},{4,6},{5,1},{6,4},{7,3},{8,10},{9,13},{10,... | collective-permute-start | bytes 196616 | tf_op jit(solution)/shard_map/ppermute | solution.py:553
  30.3 0.0 copy-done.1
  30.3 0.0 copy-done
  30.4 0.0 slice-start.3
  30.4 1.6 %attend.2.refs_6_ = bf16[4,80,128]{2,1,0:T(8,128)(2,1)S(1)} custom-call(s32[1]{0:T(128)} %bitcast.place.refs_0_, s32[1]{0:T(128)} %bitcast.1.bank.refs_1_, s32[64,128]{1,0:T(8,128)S(1)} %get-tuple-element.22.refs_2_, bf16[4,64,128]{2,1,0:T(8,128)(2,1)S(1)} %join.1.refs_3_, bf16[8,256,1024]{2,1,0:T(8,128)(2,1)S(1)} %copy-done, bf16[8,256,1024]{2,1,0:T(8,128)(2,1)S(1)} %copy-done.1), custom_call_target="tpu_custom_call" | custom-call | flops 33554432 | bytes 4194304 | tf_op jit(solution)/shard_map/attend/pallas_call | solution.py:420
  31.9 1.2 %collective-permute-done.10.refs_3_ = bf16[4,64,128]{2,1,0:T(8,128)(2,1)S(1)} collective-permute-done((bf16[4,64,128]{2,1,0:T(8,128)(2,1)S(1)}, bf16[4,64,128]{2,1,0:T(8,128)(2,1)S(1)}, u32[]{:S(2)}, u32[]{:S(2)}) %collective-permute-start.10) | collective-permute-done | bytes 65568 | tf_op jit(solution)/shard_map/ppermute | solution.py:553
  33.1 1.6 %attend.3 = bf16[8,96,128]{2,1,0:T(8,128)(2,1)S(1)} custom-call(s32[1]{0:T(128)} %bitcast.place.refs_0_, s32[1]{0:T(128)} %bitcast.1.bank.refs_1_, s32[64,128]{1,0:T(8,128)S(1)} %get-tuple-element.22.refs_2_, bf16[4,64,128]{2,1,0:T(8,128)(2,1)S(1)} %collective-permute-done.10.refs_3_, bf16[8,256,1024]{2,1,0:T(8,128)(2,1)S(1)} %copy-done, ...), custom_call_target="tpu_custom_call" | custom-call | flops 33554432 | bytes 16777216 | tf_op jit(solution)/shard_map/attend/pallas_call | solution.py:420
  34.7 11.8 %all_to_all.10.parts_ref = bf16[8,96,128]{2,1,0:T(8,128)(2,1)S(1)} all-to-all(bf16[8,96,128]{2,1,0:T(8,128)(2,1)S(1)} %attend.3), channel_id=1, replica_groups=mesh['groups'=2,'tensor'=8,'bank'=2] {'tensor'}, dimensions={0} | all-to-all | bytes 393216 | tf_op jit(solution)/shard_map/all_to_all | solution.py:545
  46.4 0.4 combine.1.x_ref
  46.8 0.0 slice-done
  46.9 0.0 slice-done.1
  46.9 0.0 slice-done.2
  46.9 0.0 slice-done.3
  46.9 2.3 %output.1 = bf16[8,8,1024]{2,1,0:T(8,128)(2,1)S(1)} custom-call(bf16[8,1024]{1,0:T(8,128)(2,1)S(1)} %combine.1.x_ref, bf16[1024,8192]{1,0:T(8,128)(2,1)S(1)} %bitcast.6), custom_call_target="tpu_custom_call" | custom-call | flops 134217728 | bytes 16777216 | tf_op jit(solution)/shard_map/output/pallas_call | solution.py:511
  49.2 9.8 %all_to_all.11.parts_ref = bf16[8,8,1024]{2,1,0:T(8,128)(2,1)S(1)} all-to-all(bf16[8,8,1024]{2,1,0:T(8,128)(2,1)S(1)} %output.1), channel_id=1, replica_groups=mesh['groups'=2,'tensor'=8,'bank'=2] {'tensor'}, dimensions={0} | all-to-all | bytes 262144 | tf_op jit(solution)/shard_map/all_to_all | solution.py:545
  58.9 0.6 %residual.1 = bf16[8,1024]{1,0:T(8,128)(2,1)} custom-call(bf16[8,1024]{1,0:T(8,128)(2,1)S(1)} %copy-done.4, bf16[8,8,1024]{2,1,0:T(8,128)(2,1)S(1)} %all_to_all.11.parts_ref), custom_call_target="tpu_custom_call" | custom-call | tf_op jit(solution)/shard_map/residual/pallas_call | solution.py:530
  (5 shorter events, 0.0 us)
Async XLA Ops:
  0.0 2.1 %copy-start.4 = (bf16[8,1024]{1,0:T(8,128)(2,1)S(1)}, bf16[8,1024]{1,0:T(8,128)(2,1)}, u32[]{:S(2)}) copy-start(bf16[8,1024]{1,0:T(8,128)(2,1)} %x_ref.6) | copy-start | bytes 49156
  0.0 2.1 %copy-start.5 = (s32[8]{0:T(128)S(1)}, s32[8]{0:T(128)}, u32[]{:S(2)}) copy-start(s32[8]{0:T(128)} %param.11) | copy-start | bytes 100
  0.0 2.1 %collective-permute-start = (bf16[8,1024]{1,0:T(8,128)(2,1)}, bf16[8,1024]{1,0:T(8,128)(2,1)S(1)}, u32[]{:S(2)}, u32[]{:S(2)}) collective-permute-start(bf16[8,1024]{1,0:T(8,128)(2,1)} %x_ref.6), channel_id=1, source_target_pairs={{0,1},{1,0},{2,3},{3,2},{4,5},{5,4},{6,7},{7,6},{8,9},{9,8},{10,11... | collective-permute-start | bytes 49160 | tf_op jit(solution)/shard_map/ppermute | solution.py:541
  0.5 1.6 %collective-permute-start.1 = (s32[8]{0:T(128)}, s32[8]{0:T(128)S(1)}, u32[]{:S(2)}, u32[]{:S(2)}) collective-permute-start(s32[8]{0:T(128)} %param.11), channel_id=1, source_target_pairs={{0,1},{1,0},{2,3},{3,2},{4,5},{5,4},{6,7},{7,6},{8,9},{9,8},{10,11... | collective-permute-start | bytes 104 | tf_op jit(solution)/shard_map/ppermute | solution.py:541
  2.1 6.0 %copy-start.6 = (s32[8]{0:T(128)S(1)}, s32[8]{0:T(128)}, u32[]{:S(2)}) copy-start(s32[8]{0:T(128)} %length.1) | copy-start | bytes 100
  5.2 10.8 %copy-start.2 = (bf16[1024,2048]{1,0:T(8,128)(2,1)S(1)}, bf16[1024,2048]{1,0:T(8,128)(2,1)}, u32[]{:S(2)}) copy-start(bf16[1024,2048]{1,0:T(8,128)(2,1)} %w_ref.6) | copy-start | bytes 12582916
  5.2 6.4 %collective-permute-start.2 = (f32[16,2176]{1,0:T(8,128)S(1)}, f32[16,2176]{1,0:T(8,128)S(1)}, u32[]{:S(2)}, u32[]{:S(2)}) collective-permute-start(f32[16,2176]{1,0:T(8,128)S(1)} %get-tuple-element.26), channel_id=1, source_target_pairs={{0,2},{1,5},{2,0},{3,7},{4,6},{5,1},{6,4},{7,3},{8,10},{9,13},{10,... | collective-permute-start | bytes 417800 | tf_op jit(solution)/shard_map/ppermute | solution.py:553
  8.2 12.0 %copy-start.3 = (bf16[16,64,1024]{2,1,0:T(8,128)(2,1)S(1)}, bf16[16,64,1024]{2,1,0:T(8,128)(2,1)}, u32[]{:S(2)}) copy-start(bf16[16,64,1024]{2,1,0:T(8,128)(2,1)} %up_ref.1) | copy-start | bytes 6291460
  8.2 22.2 %copy-start.1 = (bf16[8,256,1024]{2,1,0:T(8,128)(2,1)S(1)}, bf16[8,256,1024]{2,1,0:T(8,128)(2,1)}, u32[]{:S(2)}) copy-start(bf16[8,256,1024]{2,1,0:T(8,128)(2,1)} %refs_5_.3) | copy-start | bytes 12582916
  8.2 38.7 %slice-start = ((s8[16777216]{0:T(1024)(128)(4,1)}), s8[4194304]{0:T(1024)(128)(4,1)S(1)}, s32[]{:S(2)}) async-start(s8[16777216]{0:T(1024)(128)(4,1)} %bitcast.5), calls=%async_computation.2 | async-start | bytes 8388608
  8.2 38.7 %slice-start.1 = ((s8[16777216]{0:T(1024)(128)(4,1)}), s8[4194304]{0:T(1024)(128)(4,1)S(1)}, s32[]{:S(2)}) async-start(s8[16777216]{0:T(1024)(128)(4,1)} %bitcast.5), calls=%async_computation.3 | async-start | bytes 8388608
  11.5 18.8 %copy-start = (bf16[8,256,1024]{2,1,0:T(8,128)(2,1)S(1)}, bf16[8,256,1024]{2,1,0:T(8,128)(2,1)}, u32[]{:S(2)}) copy-start(bf16[8,256,1024]{2,1,0:T(8,128)(2,1)} %refs_4_.3) | copy-start | bytes 12582916
  11.6 5.1 %collective-permute-start.3 = (f32[16,640]{1,0:T(8,128)S(1)}, f32[16,640]{1,0:T(8,128)S(1)}, u32[]{:S(2)}, u32[]{:S(2)}) collective-permute-start(f32[16,640]{1,0:T(8,128)S(1)} %get-tuple-element.29), channel_id=1, source_target_pairs={{0,8},{1,9},{2,10},{3,11},{4,12},{5,13},{6,14},{7,15},{8,0},{9,1},... | collective-permute-start | bytes 122888 | tf_op jit(solution)/shard_map/ppermute | solution.py:553
  14.4 5.8 %collective-permute-start.4 = (f32[16,640]{1,0:T(8,128)S(1)}, f32[16,640]{1,0:T(8,128)S(1)}, u32[]{:S(2)}, u32[]{:S(2)}) collective-permute-start(f32[16,640]{1,0:T(8,128)S(1)} %get-tuple-element.30), channel_id=1, source_target_pairs={{0,12},{1,11},{2,14},{3,9},{4,8},{5,15},{6,10},{7,13},{8,4},{9,3},... | collective-permute-start | bytes 122888 | tf_op jit(solution)/shard_map/ppermute | solution.py:553
  15.7 4.5 %collective-permute-start.5 = (f32[16,640]{1,0:T(8,128)S(1)}, f32[16,640]{1,0:T(8,128)S(1)}, u32[]{:S(2)}, u32[]{:S(2)}) collective-permute-start(f32[16,640]{1,0:T(8,128)S(1)} %get-tuple-element.31), channel_id=1, source_target_pairs={{0,4},{1,3},{2,6},{3,1},{4,0},{5,7},{6,2},{7,5},{8,12},{9,11},{10,... | collective-permute-start | bytes 122888 | tf_op jit(solution)/shard_map/ppermute | solution.py:553
  16.0 30.9 %slice-start.2 = ((s8[16777216]{0:T(1024)(128)(4,1)}), s8[4194304]{0:T(1024)(128)(4,1)S(1)}, s32[]{:S(2)}) async-start(s8[16777216]{0:T(1024)(128)(4,1)} %bitcast.5), calls=%async_computation.4 | async-start | bytes 8388608
  20.6 1.2 %collective-permute-start.6 = (f32[8,1024]{1,0:T(8,128)S(1)}, f32[8,1024]{1,0:T(8,128)S(1)}, u32[]{:S(2)}, u32[]{:S(2)}) collective-permute-start(f32[8,1024]{1,0:T(8,128)S(1)} %get-tuple-element.37), channel_id=1, source_target_pairs={{0,1},{1,0},{2,3},{3,2},{4,5},{5,4},{6,7},{7,6},{8,9},{9,8},{10,11... | collective-permute-start | bytes 98312 | tf_op jit(solution)/shard_map/ppermute | solution.py:541
  21.9 4.7 %collective-permute-start.7 = (bf16[1,64,128]{2,1,0:T(8,128)(2,1)S(1)}, bf16[1,64,128]{2,1,0:T(8,128)(2,1)S(1)}, u32[]{:S(2)}, u32[]{:S(2)}) collective-permute-start(bf16[1,64,128]{2,1,0:T(8,128)(2,1)S(1)} %rotate.1.refs_0_.q_ref), channel_id=1, source_target_pairs={{0,8},{1,9},{2,10},{3,11},{4,12},{5,13},{6,14},{7,15},{8,0},{9,1},... | collective-permute-start | bytes 49160 | tf_op jit(solution)/shard_map/ppermute | solution.py:553
  23.2 5.5 %collective-permute-start.8 = (bf16[1,64,128]{2,1,0:T(8,128)(2,1)S(1)}, bf16[1,64,128]{2,1,0:T(8,128)(2,1)S(1)}, u32[]{:S(2)}, u32[]{:S(2)}) collective-permute-start(bf16[1,64,128]{2,1,0:T(8,128)(2,1)S(1)} %rotate.1.refs_0_.q_ref), channel_id=1, source_target_pairs={{0,12},{1,11},{2,14},{3,9},{4,8},{5,15},{6,10},{7,13},{8,4},{9,3},... | collective-permute-start | bytes 49160 | tf_op jit(solution)/shard_map/ppermute | solution.py:553
  24.4 4.4 %collective-permute-start.9 = (bf16[1,64,128]{2,1,0:T(8,128)(2,1)S(1)}, bf16[1,64,128]{2,1,0:T(8,128)(2,1)S(1)}, u32[]{:S(2)}, u32[]{:S(2)}) collective-permute-start(bf16[1,64,128]{2,1,0:T(8,128)(2,1)S(1)} %rotate.1.refs_0_.q_ref), channel_id=1, source_target_pairs={{0,4},{1,3},{2,6},{3,1},{4,0},{5,7},{6,2},{7,5},{8,12},{9,11},{10,... | collective-permute-start | bytes 49160 | tf_op jit(solution)/shard_map/ppermute | solution.py:553
  28.8 4.3 %collective-permute-start.10 = (bf16[4,64,128]{2,1,0:T(8,128)(2,1)S(1)}, bf16[4,64,128]{2,1,0:T(8,128)(2,1)S(1)}, u32[]{:S(2)}, u32[]{:S(2)}) collective-permute-start(bf16[4,64,128]{2,1,0:T(8,128)(2,1)S(1)} %join.1.refs_3_), channel_id=1, source_target_pairs={{0,2},{1,5},{2,0},{3,7},{4,6},{5,1},{6,4},{7,3},{8,10},{9,13},{10,... | collective-permute-start | bytes 196616 | tf_op jit(solution)/shard_map/ppermute | solution.py:553
  30.4 16.5 %slice-start.3 = ((s8[16777216]{0:T(1024)(128)(4,1)}), s8[4194304]{0:T(1024)(128)(4,1)S(1)}, s32[]{:S(2)}) async-start(s8[16777216]{0:T(1024)(128)(4,1)} %bitcast.5), calls=%async_computation.5 | async-start | bytes 8388608

commit v24 on v21

--- a/solution.py
+++ b/solution.py
@@ -484,41 +484,33 @@
         out_ref[:, g * HEAD_DIM : (g + 1) * HEAD_DIM] = joined[:, g, :].astype(BF16)
 
 
-def combine(parts, query, cosine, sine):
-    beams = cosine.shape[0]
-    group = query.shape[1] // beams
-    return pl.pallas_call(
-        combine_kernel,
-        in_specs=[whole()] * 4,
-        out_specs=whole(),
-        out_shape=shape(beams, group * HEAD_DIM, dtype=BF16),
-        scratch_shapes=[pltpu.VMEM((beams, group, HEAD_DIM), F32)],
-        compiler_params=params(),
-        name="combine",
-    )(parts, query, cosine, sine)
-
-
-def output_kernel(x_ref, w_ref, out):
+def output_kernel(parts_ref, q_ref, cos_ref, sin_ref, w_ref, out, joined, attended):
+    combine_kernel(parts_ref, q_ref, cos_ref, sin_ref, attended, joined)
     count, _, width = out.shape
     for s in range(count):
         columns = slice(s * width, (s + 1) * width)
-        total = jnp.dot(x_ref[...], w_ref[:, columns], preferred_element_type=F32)
+        total = jnp.dot(attended[...], w_ref[:, columns], preferred_element_type=F32)
         out[s] = total.astype(BF16)
 
 
-def output(x, weight, ranks):
-    beams = x.shape[0]
+def output(parts, query, cosine, sine, weight, ranks):
+    beams = cosine.shape[0]
+    group = query.shape[1] // beams
     return pl.pallas_call(
         output_kernel,
-        in_specs=[whole()] * 2,
+        in_specs=[whole()] * 5,
         out_specs=whole(),
         out_shape=shape(ranks, beams, weight.shape[1] // ranks, dtype=BF16),
+        scratch_shapes=[
+            pltpu.VMEM((beams, group, HEAD_DIM), F32),
+            pltpu.VMEM((beams, group * HEAD_DIM), BF16),
+        ],
         compiler_params=params(),
         cost_estimate=pl.CostEstimate(
             flops=2 * beams * weight.size, bytes_accessed=2 * weight.size, transcendentals=0
         ),
         name="output",
-    )(x, weight)
+    )(parts, query, cosine, sine, weight)
 
 
 def residual_kernel(x_ref, parts_ref, out_ref):
@@ -601,8 +593,8 @@
     done = attended_part(gathered, (0, *near))
     odd = tuple(slot + 1 for slot in (0, *near))
     partial = attended_part(came, odd, earlier=(0, *near), before=(done, token))
-    attended = combine(traded(partial), query, cosine, sine)
-    return residual(x, traded(output(attended, output_weight, ranks)))
+    mixed = output(traded(partial), query, cosine, sine, output_weight, ranks)
+    return residual(x, traded(mixed))
 
 
 def joined(x, axis, combine):

time: 59.8 us -> 59.8 us (level)
    pallas_call x2 -> x1, Pallas kernels: 2.69 us -> 2.67 us  [output(): pl.pallas_call(output_kernel, in_specs=[whole()] * 5, out_specs=whole(),...]
where the time goes in v24:
time: 59.8 us; the launch traced here: 59.5 us
  blocking collectives  21.5 us (36%)
  Pallas kernels  15.5 us (26%)
  starting transfers between devices  13.1 us (22%)
  waiting for transfers between devices  9.1 us (15%)
    all_to_all x2, blocking collectives, traded(): return lax.all_to_all(blocks, 'tensor', 0, 0, tiled=True)  21.5 us
    ppermute x8, starting transfers between devices, hop(): return lax.ppermute(x, ('tensor', 'bank'), pairs)  12.6 us
    ppermute x8, waiting for transfers between devices, hop(): return lax.ppermute(x, ('tensor', 'bank'), pairs)  8 us
    pallas_call x1, Pallas kernels, project_kept(): pl.pallas_call(project_kept_kernel, in_specs=[scalar()] * 3 + [whole()] *...  3.3 us
    pallas_call x2, Pallas kernels, attend(): pl.pallas_call(lambda *refs: attend_kernel(slots, earlier, *refs), in_spe...  3.13 us
    pallas_call x1, Pallas kernels, project_sent(): pl.pallas_call(project_sent_kernel, in_specs=[scalar()] * 2 + [whole()] *...  3.01 us
    pallas_call x1, Pallas kernels, output(): pl.pallas_call(output_kernel, in_specs=[whole()] * 5, out_specs=whole(),...  2.67 us
    pallas_call x1, Pallas kernels, fetch(): pl.pallas_call(fetch_kernel, in_specs=[big()], out_specs=whole(), out_sha...  1.56 us
  transfers between devices with their start and end apart: 11, of which 5 were waited for; matrix products, arithmetic and copies ran while one was open for 0% of the time, Pallas kernels for 12%

profile of v24, /device:TPU:0, one launch (start us, length us, event | category | flops | bytes accessed | tf_op | source)
XLA Modules:
  0.0 59.5 jit_solution(17069724467874787527)
XLA Ops:
  0.0 0.0 copy-start.4
  0.0 0.0 copy-start.5
  0.0 0.5 collective-permute-start
  0.5 0.1 collective-permute-start.1
  0.5 1.6 %fetch.1.down_ref = bf16[16,64,1024]{2,1,0:T(8,128)(2,1)S(1)} custom-call(bf16[16,64,1024]{2,1,0:T(8,128)(2,1)} %bitcast.9), custom_call_target="tpu_custom_call" | custom-call | bytes 2097152 | tf_op jit(solution)/shard_map/fetch/pallas_call | solution.py:112
  2.1 0.0 collective-permute-done.1
  2.1 0.0 collective-permute-done.other_ref
  2.1 0.0 copy-done.4
  2.1 0.0 copy-done.5
  2.1 0.0 copy-start.6
  2.1 3.0 %project_sent.1 = (f32[16,2176]{1,0:T(8,128)S(1)}, f32[16,128]{1,0:T(8,128)S(1)}, s32[16,128]{1,0:T(8,128)S(1)}) custom-call(s32[1]{0:T(128)} %bitcast.place.refs_0_, s32[1]{0:T(128)} %bitcast.1.bank.refs_1_, s32[1,8]{1,0:T(1,128)S(1)} %bitcast.7, s32[1,8]{1,0:T(1,128)S(1)} %bitcast.8, bf16[8,1024]{1,0:T(8,128)(2,1)S(1)} %copy-done.4, ...), custom_call_target="tpu_custom_call" | custom-call | flops 100663296 | bytes 6291456 | tf_op jit(solution)/shard_map/project_sent/pallas_call | solution.py:167
  5.2 0.0 copy-start.2
  5.2 3.0 %collective-permute-start.2 = (f32[16,2176]{1,0:T(8,128)S(1)}, f32[16,2176]{1,0:T(8,128)S(1)}, u32[]{:S(2)}, u32[]{:S(2)}) collective-permute-start(f32[16,2176]{1,0:T(8,128)S(1)} %get-tuple-element.26), channel_id=1, source_target_pairs={{0,2},{1,5},{2,0},{3,7},{4,6},{5,1},{6,4},{7,3},{8,10},{9,13},{10,... | collective-permute-start | bytes 417800 | tf_op jit(solution)/shard_map/ppermute | solution.py:545
  8.2 0.0 copy-done.6
  8.2 0.0 copy-start.3
  8.2 0.0 copy-start.1
  8.2 0.0 slice-start
  8.2 0.0 slice-start.1
  8.2 3.3 %project_kept.1 = (f32[16,2048]{1,0:T(8,128)S(1)}, s32[64,128]{1,0:T(8,128)S(1)}) custom-call(s32[1]{0:T(128)} %bitcast.place.refs_0_, s32[1]{0:T(128)} %bitcast.1.bank.refs_1_, s32[8]{0:T(128)S(1)} %copy-done.6, bf16[8,1024]{1,0:T(8,128)(2,1)S(1)} %copy-done.4, bf16[8,1024]{1,0:T(8,128)(2,1)S(1)} %collective-permute-done.other_ref, bf16[1024,8192]{1,0:T(8,128)(2,1)} %w_ref.5), custom_call_target="tpu_custom_call" | custom-call | flops 67108864 | bytes 16777216 | tf_op jit(solution)/shard_map/project_kept/pallas_call | solution.py:203
  11.5 0.0 copy-start
  11.5 0.0 collective-permute-done.2.came_ref
  11.6 2.8 %collective-permute-start.3 = (f32[16,640]{1,0:T(8,128)S(1)}, f32[16,640]{1,0:T(8,128)S(1)}, u32[]{:S(2)}, u32[]{:S(2)}) collective-permute-start(f32[16,640]{1,0:T(8,128)S(1)} %get-tuple-element.29), channel_id=1, source_target_pairs={{0,8},{1,9},{2,10},{3,11},{4,12},{5,13},{6,14},{7,15},{8,0},{9,1},... | collective-permute-start | bytes 122888 | tf_op jit(solution)/shard_map/ppermute | solution.py:545
  14.4 1.3 %collective-permute-start.4 = (f32[16,640]{1,0:T(8,128)S(1)}, f32[16,640]{1,0:T(8,128)S(1)}, u32[]{:S(2)}, u32[]{:S(2)}) collective-permute-start(f32[16,640]{1,0:T(8,128)S(1)} %get-tuple-element.30), channel_id=1, source_target_pairs={{0,12},{1,11},{2,14},{3,9},{4,8},{5,15},{6,10},{7,13},{8,4},{9,3},... | collective-permute-start | bytes 122888 | tf_op jit(solution)/shard_map/ppermute | solution.py:545
  15.8 0.2 collective-permute-start.5
  16.0 0.0 copy-done.2
  16.0 0.0 slice-start.2
  16.0 0.6 %keyval.1.refs_7_ = f32[8,24,128]{2,1,0:T(8,128)S(1)} custom-call(bf16[8,1024]{1,0:T(8,128)(2,1)S(1)} %copy-done.4, bf16[1024,2048]{1,0:T(8,128)(2,1)S(1)} %copy-done.2), custom_call_target="tpu_custom_call" | custom-call | flops 33554432 | bytes 4194304 | tf_op jit(solution)/shard_map/keyval/pallas_call | solution.py:234
  16.7 0.0 collective-permute-done.3.refs_1_
  16.7 3.5 %collective-permute-done.4.refs_2_ = f32[16,640]{1,0:T(8,128)S(1)} collective-permute-done((f32[16,640]{1,0:T(8,128)S(1)}, f32[16,640]{1,0:T(8,128)S(1)}, u32[]{:S(2)}, u32[]{:S(2)}) %collective-permute-start.4) | collective-permute-done | bytes 40992 | tf_op jit(solution)/shard_map/ppermute | solution.py:545
  20.2 0.0 collective-permute-done.5.refs_3_
  20.2 0.0 copy-done.3
  20.2 0.4 correct.1
  20.6 0.0 collective-permute-start.6
  20.6 0.1 fusion
  20.7 1.1 %collective-permute-done.6.came_ref = f32[8,1024]{1,0:T(8,128)S(1)} collective-permute-done((f32[8,1024]{1,0:T(8,128)S(1)}, f32[8,1024]{1,0:T(8,128)S(1)}, u32[]{:S(2)}, u32[]{:S(2)}) %collective-permute-start.6) | collective-permute-done | bytes 32800 | tf_op jit(solution)/shard_map/ppermute | solution.py:533
  21.8 0.1 rotate.1.refs_0_.q_ref
  21.9 1.3 %collective-permute-start.7 = (bf16[1,64,128]{2,1,0:T(8,128)(2,1)S(1)}, bf16[1,64,128]{2,1,0:T(8,128)(2,1)S(1)}, u32[]{:S(2)}, u32[]{:S(2)}) collective-permute-start(bf16[1,64,128]{2,1,0:T(8,128)(2,1)S(1)} %rotate.1.refs_0_.q_ref), channel_id=1, source_target_pairs={{0,8},{1,9},{2,10},{3,11},{4,12},{5,13},{6,14},{7,15},{8,0},{9,1},... | collective-permute-start | bytes 49160 | tf_op jit(solution)/shard_map/ppermute | solution.py:545
  23.2 1.2 %collective-permute-start.8 = (bf16[1,64,128]{2,1,0:T(8,128)(2,1)S(1)}, bf16[1,64,128]{2,1,0:T(8,128)(2,1)S(1)}, u32[]{:S(2)}, u32[]{:S(2)}) collective-permute-start(bf16[1,64,128]{2,1,0:T(8,128)(2,1)S(1)} %rotate.1.refs_0_.q_ref), channel_id=1, source_target_pairs={{0,12},{1,11},{2,14},{3,9},{4,8},{5,15},{6,10},{7,13},{8,4},{9,3},... | collective-permute-start | bytes 49160 | tf_op jit(solution)/shard_map/ppermute | solution.py:545
  24.4 1.1 %collective-permute-start.9 = (bf16[1,64,128]{2,1,0:T(8,128)(2,1)S(1)}, bf16[1,64,128]{2,1,0:T(8,128)(2,1)S(1)}, u32[]{:S(2)}, u32[]{:S(2)}) collective-permute-start(bf16[1,64,128]{2,1,0:T(8,128)(2,1)S(1)} %rotate.1.refs_0_.q_ref), channel_id=1, source_target_pairs={{0,4},{1,3},{2,6},{3,1},{4,0},{5,7},{6,2},{7,5},{8,12},{9,11},{10,... | collective-permute-start | bytes 49160 | tf_op jit(solution)/shard_map/ppermute | solution.py:545
  25.5 1.1 %collective-permute-done.7.refs_1_ = bf16[1,64,128]{2,1,0:T(8,128)(2,1)S(1)} collective-permute-done((bf16[1,64,128]{2,1,0:T(8,128)(2,1)S(1)}, bf16[1,64,128]{2,1,0:T(8,128)(2,1)S(1)}, u32[]{:S(2)}, u32[]{:S(2)}) %collective-permute-start.7) | collective-permute-done | bytes 16416 | tf_op jit(solution)/shard_map/ppermute | solution.py:545
  26.6 2.1 %collective-permute-done.8.refs_2_ = bf16[1,64,128]{2,1,0:T(8,128)(2,1)S(1)} collective-permute-done((bf16[1,64,128]{2,1,0:T(8,128)(2,1)S(1)}, bf16[1,64,128]{2,1,0:T(8,128)(2,1)S(1)}, u32[]{:S(2)}, u32[]{:S(2)}) %collective-permute-start.8) | collective-permute-done | bytes 16416 | tf_op jit(solution)/shard_map/ppermute | solution.py:545
  28.8 0.0 collective-permute-done.9.refs_3_
  28.8 1.6 %collective-permute-start.10 = (bf16[4,64,128]{2,1,0:T(8,128)(2,1)S(1)}, bf16[4,64,128]{2,1,0:T(8,128)(2,1)S(1)}, u32[]{:S(2)}, u32[]{:S(2)}) collective-permute-start(bf16[4,64,128]{2,1,0:T(8,128)(2,1)S(1)} %join.1.refs_3_), channel_id=1, source_target_pairs={{0,2},{1,5},{2,0},{3,7},{4,6},{5,1},{6,4},{7,3},{8,10},{9,13},{10,... | collective-permute-start | bytes 196616 | tf_op jit(solution)/shard_map/ppermute | solution.py:545
  30.4 0.0 copy-done.1
  30.4 0.0 copy-done
  30.4 0.0 slice-start.3
  30.4 1.6 %attend.2.refs_6_ = bf16[4,80,128]{2,1,0:T(8,128)(2,1)S(1)} custom-call(s32[1]{0:T(128)} %bitcast.place.refs_0_, s32[1]{0:T(128)} %bitcast.1.bank.refs_1_, s32[64,128]{1,0:T(8,128)S(1)} %get-tuple-element.22.refs_2_, bf16[4,64,128]{2,1,0:T(8,128)(2,1)S(1)} %join.1.refs_3_, bf16[8,256,1024]{2,1,0:T(8,128)(2,1)S(1)} %copy-done, bf16[8,256,1024]{2,1,0:T(8,128)(2,1)S(1)} %copy-done.1), custom_call_target="tpu_custom_call" | custom-call | flops 33554432 | bytes 4194304 | tf_op jit(solution)/shard_map/attend/pallas_call | solution.py:420
  31.9 1.2 %collective-permute-done.10.refs_3_ = bf16[4,64,128]{2,1,0:T(8,128)(2,1)S(1)} collective-permute-done((bf16[4,64,128]{2,1,0:T(8,128)(2,1)S(1)}, bf16[4,64,128]{2,1,0:T(8,128)(2,1)S(1)}, u32[]{:S(2)}, u32[]{:S(2)}) %collective-permute-start.10) | collective-permute-done | bytes 65568 | tf_op jit(solution)/shard_map/ppermute | solution.py:545
  33.1 1.6 %attend.3 = bf16[8,96,128]{2,1,0:T(8,128)(2,1)S(1)} custom-call(s32[1]{0:T(128)} %bitcast.place.refs_0_, s32[1]{0:T(128)} %bitcast.1.bank.refs_1_, s32[64,128]{1,0:T(8,128)S(1)} %get-tuple-element.22.refs_2_, bf16[4,64,128]{2,1,0:T(8,128)(2,1)S(1)} %collective-permute-done.10.refs_3_, bf16[8,256,1024]{2,1,0:T(8,128)(2,1)S(1)} %copy-done, ...), custom_call_target="tpu_custom_call" | custom-call | flops 33554432 | bytes 16777216 | tf_op jit(solution)/shard_map/attend/pallas_call | solution.py:420
  34.7 11.8 %all_to_all.10.parts_ref = bf16[8,96,128]{2,1,0:T(8,128)(2,1)S(1)} all-to-all(bf16[8,96,128]{2,1,0:T(8,128)(2,1)S(1)} %attend.3), channel_id=1, replica_groups=mesh['groups'=2,'tensor'=8,'bank'=2] {'tensor'}, dimensions={0} | all-to-all | bytes 393216 | tf_op jit(solution)/shard_map/all_to_all | solution.py:537
  46.4 0.0 slice-done
  46.4 0.0 slice-done.1
  46.4 0.0 slice-done.2
  46.4 0.0 slice-done.3
  46.5 2.7 %output.1 = bf16[8,8,1024]{2,1,0:T(8,128)(2,1)S(1)} custom-call(bf16[8,96,128]{2,1,0:T(8,128)(2,1)S(1)} %all_to_all.10.parts_ref, bf16[1,64,128]{2,1,0:T(8,128)(2,1)S(1)} %rotate.1.refs_0_.q_ref, f32[8,128]{1,0:T(8,128)S(1)} %get-tuple-element.40.cos_ref, f32[8,128]{1,0:T(8,128)S(1)} %get-tuple-element.39.sin_ref, bf16[1024,8192]{1,0:T(8,128)(2,1)S(1)} %bitcast.6), custom_call_target="tpu_custom_call" | custom-call | flops 134217728 | bytes 16777216 | tf_op jit(solution)/shard_map/output/pallas_call | solution.py:499
  49.1 9.8 %all_to_all.11.parts_ref = bf16[8,8,1024]{2,1,0:T(8,128)(2,1)S(1)} all-to-all(bf16[8,8,1024]{2,1,0:T(8,128)(2,1)S(1)} %output.1), channel_id=1, replica_groups=mesh['groups'=2,'tensor'=8,'bank'=2] {'tensor'}, dimensions={0} | all-to-all | bytes 262144 | tf_op jit(solution)/shard_map/all_to_all | solution.py:537
  58.9 0.6 %residual.1 = bf16[8,1024]{1,0:T(8,128)(2,1)} custom-call(bf16[8,1024]{1,0:T(8,128)(2,1)S(1)} %copy-done.4, bf16[8,8,1024]{2,1,0:T(8,128)(2,1)S(1)} %all_to_all.11.parts_ref), custom_call_target="tpu_custom_call" | custom-call | tf_op jit(solution)/shard_map/residual/pallas_call | solution.py:522
  (5 shorter events, 0.0 us)
Async XLA Ops:
  0.0 2.1 %copy-start.4 = (bf16[8,1024]{1,0:T(8,128)(2,1)S(1)}, bf16[8,1024]{1,0:T(8,128)(2,1)}, u32[]{:S(2)}) copy-start(bf16[8,1024]{1,0:T(8,128)(2,1)} %x_ref.6) | copy-start | bytes 49156
  0.0 2.1 %copy-start.5 = (s32[8]{0:T(128)S(1)}, s32[8]{0:T(128)}, u32[]{:S(2)}) copy-start(s32[8]{0:T(128)} %param.11) | copy-start | bytes 100
  0.0 2.1 %collective-permute-start = (bf16[8,1024]{1,0:T(8,128)(2,1)}, bf16[8,1024]{1,0:T(8,128)(2,1)S(1)}, u32[]{:S(2)}, u32[]{:S(2)}) collective-permute-start(bf16[8,1024]{1,0:T(8,128)(2,1)} %x_ref.6), channel_id=1, source_target_pairs={{0,1},{1,0},{2,3},{3,2},{4,5},{5,4},{6,7},{7,6},{8,9},{9,8},{10,11... | collective-permute-start | bytes 49160 | tf_op jit(solution)/shard_map/ppermute | solution.py:533
  0.5 1.6 %collective-permute-start.1 = (s32[8]{0:T(128)}, s32[8]{0:T(128)S(1)}, u32[]{:S(2)}, u32[]{:S(2)}) collective-permute-start(s32[8]{0:T(128)} %param.11), channel_id=1, source_target_pairs={{0,1},{1,0},{2,3},{3,2},{4,5},{5,4},{6,7},{7,6},{8,9},{9,8},{10,11... | collective-permute-start | bytes 104 | tf_op jit(solution)/shard_map/ppermute | solution.py:533
  2.1 6.1 %copy-start.6 = (s32[8]{0:T(128)S(1)}, s32[8]{0:T(128)}, u32[]{:S(2)}) copy-start(s32[8]{0:T(128)} %length.1) | copy-start | bytes 100
  5.2 10.8 %copy-start.2 = (bf16[1024,2048]{1,0:T(8,128)(2,1)S(1)}, bf16[1024,2048]{1,0:T(8,128)(2,1)}, u32[]{:S(2)}) copy-start(bf16[1024,2048]{1,0:T(8,128)(2,1)} %w_ref.6) | copy-start | bytes 12582916
  5.2 6.4 %collective-permute-start.2 = (f32[16,2176]{1,0:T(8,128)S(1)}, f32[16,2176]{1,0:T(8,128)S(1)}, u32[]{:S(2)}, u32[]{:S(2)}) collective-permute-start(f32[16,2176]{1,0:T(8,128)S(1)} %get-tuple-element.26), channel_id=1, source_target_pairs={{0,2},{1,5},{2,0},{3,7},{4,6},{5,1},{6,4},{7,3},{8,10},{9,13},{10,... | collective-permute-start | bytes 417800 | tf_op jit(solution)/shard_map/ppermute | solution.py:545
  8.2 12.0 %copy-start.3 = (bf16[16,64,1024]{2,1,0:T(8,128)(2,1)S(1)}, bf16[16,64,1024]{2,1,0:T(8,128)(2,1)}, u32[]{:S(2)}) copy-start(bf16[16,64,1024]{2,1,0:T(8,128)(2,1)} %up_ref.1) | copy-start | bytes 6291460
  8.2 22.2 %copy-start.1 = (bf16[8,256,1024]{2,1,0:T(8,128)(2,1)S(1)}, bf16[8,256,1024]{2,1,0:T(8,128)(2,1)}, u32[]{:S(2)}) copy-start(bf16[8,256,1024]{2,1,0:T(8,128)(2,1)} %refs_5_.3) | copy-start | bytes 12582916
  8.2 38.2 %slice-start = ((s8[16777216]{0:T(1024)(128)(4,1)}), s8[4194304]{0:T(1024)(128)(4,1)S(1)}, s32[]{:S(2)}) async-start(s8[16777216]{0:T(1024)(128)(4,1)} %bitcast.5), calls=%async_computation.2 | async-start | bytes 8388608
  8.2 38.2 %slice-start.1 = ((s8[16777216]{0:T(1024)(128)(4,1)}), s8[4194304]{0:T(1024)(128)(4,1)S(1)}, s32[]{:S(2)}) async-start(s8[16777216]{0:T(1024)(128)(4,1)} %bitcast.5), calls=%async_computation.3 | async-start | bytes 8388608
  11.5 18.8 %copy-start = (bf16[8,256,1024]{2,1,0:T(8,128)(2,1)S(1)}, bf16[8,256,1024]{2,1,0:T(8,128)(2,1)}, u32[]{:S(2)}) copy-start(bf16[8,256,1024]{2,1,0:T(8,128)(2,1)} %refs_4_.3) | copy-start | bytes 12582916
  11.6 5.1 %collective-permute-start.3 = (f32[16,640]{1,0:T(8,128)S(1)}, f32[16,640]{1,0:T(8,128)S(1)}, u32[]{:S(2)}, u32[]{:S(2)}) collective-permute-start(f32[16,640]{1,0:T(8,128)S(1)} %get-tuple-element.29), channel_id=1, source_target_pairs={{0,8},{1,9},{2,10},{3,11},{4,12},{5,13},{6,14},{7,15},{8,0},{9,1},... | collective-permute-start | bytes 122888 | tf_op jit(solution)/shard_map/ppermute | solution.py:545
  14.4 5.8 %collective-permute-start.4 = (f32[16,640]{1,0:T(8,128)S(1)}, f32[16,640]{1,0:T(8,128)S(1)}, u32[]{:S(2)}, u32[]{:S(2)}) collective-permute-start(f32[16,640]{1,0:T(8,128)S(1)} %get-tuple-element.30), channel_id=1, source_target_pairs={{0,12},{1,11},{2,14},{3,9},{4,8},{5,15},{6,10},{7,13},{8,4},{9,3},... | collective-permute-start | bytes 122888 | tf_op jit(solution)/shard_map/ppermute | solution.py:545
  15.8 4.5 %collective-permute-start.5 = (f32[16,640]{1,0:T(8,128)S(1)}, f32[16,640]{1,0:T(8,128)S(1)}, u32[]{:S(2)}, u32[]{:S(2)}) collective-permute-start(f32[16,640]{1,0:T(8,128)S(1)} %get-tuple-element.31), channel_id=1, source_target_pairs={{0,4},{1,3},{2,6},{3,1},{4,0},{5,7},{6,2},{7,5},{8,12},{9,11},{10,... | collective-permute-start | bytes 122888 | tf_op jit(solution)/shard_map/ppermute | solution.py:545
  16.0 30.4 %slice-start.2 = ((s8[16777216]{0:T(1024)(128)(4,1)}), s8[4194304]{0:T(1024)(128)(4,1)S(1)}, s32[]{:S(2)}) async-start(s8[16777216]{0:T(1024)(128)(4,1)} %bitcast.5), calls=%async_computation.4 | async-start | bytes 8388608
  20.6 1.2 %collective-permute-start.6 = (f32[8,1024]{1,0:T(8,128)S(1)}, f32[8,1024]{1,0:T(8,128)S(1)}, u32[]{:S(2)}, u32[]{:S(2)}) collective-permute-start(f32[8,1024]{1,0:T(8,128)S(1)} %get-tuple-element.37), channel_id=1, source_target_pairs={{0,1},{1,0},{2,3},{3,2},{4,5},{5,4},{6,7},{7,6},{8,9},{9,8},{10,11... | collective-permute-start | bytes 98312 | tf_op jit(solution)/shard_map/ppermute | solution.py:533
  21.9 4.7 %collective-permute-start.7 = (bf16[1,64,128]{2,1,0:T(8,128)(2,1)S(1)}, bf16[1,64,128]{2,1,0:T(8,128)(2,1)S(1)}, u32[]{:S(2)}, u32[]{:S(2)}) collective-permute-start(bf16[1,64,128]{2,1,0:T(8,128)(2,1)S(1)} %rotate.1.refs_0_.q_ref), channel_id=1, source_target_pairs={{0,8},{1,9},{2,10},{3,11},{4,12},{5,13},{6,14},{7,15},{8,0},{9,1},... | collective-permute-start | bytes 49160 | tf_op jit(solution)/shard_map/ppermute | solution.py:545
  23.2 5.5 %collective-permute-start.8 = (bf16[1,64,128]{2,1,0:T(8,128)(2,1)S(1)}, bf16[1,64,128]{2,1,0:T(8,128)(2,1)S(1)}, u32[]{:S(2)}, u32[]{:S(2)}) collective-permute-start(bf16[1,64,128]{2,1,0:T(8,128)(2,1)S(1)} %rotate.1.refs_0_.q_ref), channel_id=1, source_target_pairs={{0,12},{1,11},{2,14},{3,9},{4,8},{5,15},{6,10},{7,13},{8,4},{9,3},... | collective-permute-start | bytes 49160 | tf_op jit(solution)/shard_map/ppermute | solution.py:545
  24.4 4.4 %collective-permute-start.9 = (bf16[1,64,128]{2,1,0:T(8,128)(2,1)S(1)}, bf16[1,64,128]{2,1,0:T(8,128)(2,1)S(1)}, u32[]{:S(2)}, u32[]{:S(2)}) collective-permute-start(bf16[1,64,128]{2,1,0:T(8,128)(2,1)S(1)} %rotate.1.refs_0_.q_ref), channel_id=1, source_target_pairs={{0,4},{1,3},{2,6},{3,1},{4,0},{5,7},{6,2},{7,5},{8,12},{9,11},{10,... | collective-permute-start | bytes 49160 | tf_op jit(solution)/shard_map/ppermute | solution.py:545
  28.8 4.3 %collective-permute-start.10 = (bf16[4,64,128]{2,1,0:T(8,128)(2,1)S(1)}, bf16[4,64,128]{2,1,0:T(8,128)(2,1)S(1)}, u32[]{:S(2)}, u32[]{:S(2)}) collective-permute-start(bf16[4,64,128]{2,1,0:T(8,128)(2,1)S(1)} %join.1.refs_3_), channel_id=1, source_target_pairs={{0,2},{1,5},{2,0},{3,7},{4,6},{5,1},{6,4},{7,3},{8,10},{9,13},{10,... | collective-permute-start | bytes 196616 | tf_op jit(solution)/shard_map/ppermute | solution.py:545
  30.4 16.1 %slice-start.3 = ((s8[16777216]{0:T(1024)(128)(4,1)}), s8[4194304]{0:T(1024)(128)(4,1)S(1)}, s32[]{:S(2)}) async-start(s8[16777216]{0:T(1024)(128)(4,1)} %bitcast.5), calls=%async_computation.5 | async-start | bytes 8388608

commit v25 on v24

--- a/solution.py
+++ b/solution.py
@@ -8,7 +8,7 @@
 HEAD_DIM = 128
 F32 = jnp.float32
 BF16 = jnp.bfloat16
-CHUNKS = 2
+CHUNKS = 4
 MIB = 1024 * 1024
 
 

time: 59.8 us -> 59.7 us (level)
  no operation moved by 1% of the time
where the time goes in v25:
time: 59.7 us; the launch traced here: 59.4 us
  blocking collectives  21.5 us (36%)
  Pallas kernels  15.5 us (26%)
  starting transfers between devices  12.9 us (22%)
  waiting for transfers between devices  9.1 us (15%)
    all_to_all x2, blocking collectives, traded(): return lax.all_to_all(blocks, 'tensor', 0, 0, tiled=True)  21.5 us
    ppermute x8, starting transfers between devices, hop(): return lax.ppermute(x, ('tensor', 'bank'), pairs)  12.4 us
    ppermute x8, waiting for transfers between devices, hop(): return lax.ppermute(x, ('tensor', 'bank'), pairs)  8 us
    pallas_call x1, Pallas kernels, project_kept(): pl.pallas_call(project_kept_kernel, in_specs=[scalar()] * 3 + [whole()] *...  3.47 us
    pallas_call x2, Pallas kernels, attend(): pl.pallas_call(lambda *refs: attend_kernel(slots, earlier, *refs), in_spe...  3.13 us
    pallas_call x1, Pallas kernels, project_sent(): pl.pallas_call(project_sent_kernel, in_specs=[scalar()] * 2 + [whole()] *...  2.93 us
    pallas_call x1, Pallas kernels, output(): pl.pallas_call(output_kernel, in_specs=[whole()] * 5, out_specs=whole(),...  2.67 us
    pallas_call x1, Pallas kernels, fetch(): pl.pallas_call(fetch_kernel, in_specs=[big()], out_specs=whole(), out_sha...  1.56 us
  transfers between devices with their start and end apart: 11, of which 5 were waited for; matrix products, arithmetic and copies ran while one was open for 0% of the time, Pallas kernels for 12%

profile of v25, /device:TPU:0, one launch (start us, length us, event | category | flops | bytes accessed | tf_op | source)
XLA Modules:
  0.0 59.4 jit_solution(12129885582273260637)
XLA Ops:
  0.0 0.0 copy-start.4
  0.0 0.0 copy-start.5
  0.0 0.5 collective-permute-start
  0.5 0.1 collective-permute-start.1
  0.5 1.6 %fetch.1.down_ref = bf16[16,64,1024]{2,1,0:T(8,128)(2,1)S(1)} custom-call(bf16[16,64,1024]{2,1,0:T(8,128)(2,1)} %bitcast.9), custom_call_target="tpu_custom_call" | custom-call | bytes 2097152 | tf_op jit(solution)/shard_map/fetch/pallas_call | solution.py:112
  2.1 0.0 collective-permute-done.1
  2.1 0.0 collective-permute-done.other_ref
  2.1 0.0 copy-done.4
  2.1 0.0 copy-done.5
  2.1 0.0 copy-start.6
  2.1 2.9 %project_sent.1 = (f32[16,2176]{1,0:T(8,128)S(1)}, f32[16,128]{1,0:T(8,128)S(1)}, s32[16,128]{1,0:T(8,128)S(1)}) custom-call(s32[1]{0:T(128)} %bitcast.place.refs_0_, s32[1]{0:T(128)} %bitcast.1.bank.refs_1_, s32[1,8]{1,0:T(1,128)S(1)} %bitcast.7, s32[1,8]{1,0:T(1,128)S(1)} %bitcast.8, bf16[8,1024]{1,0:T(8,128)(2,1)S(1)} %copy-done.4, ...), custom_call_target="tpu_custom_call" | custom-call | flops 100663296 | bytes 6291456 | tf_op jit(solution)/shard_map/project_sent/pallas_call | solution.py:167
  5.1 0.0 copy-start.2
  5.1 3.0 %collective-permute-start.2 = (f32[16,2176]{1,0:T(8,128)S(1)}, f32[16,2176]{1,0:T(8,128)S(1)}, u32[]{:S(2)}, u32[]{:S(2)}) collective-permute-start(f32[16,2176]{1,0:T(8,128)S(1)} %get-tuple-element.26), channel_id=1, source_target_pairs={{0,2},{1,5},{2,0},{3,7},{4,6},{5,1},{6,4},{7,3},{8,10},{9,13},{10,... | collective-permute-start | bytes 417800 | tf_op jit(solution)/shard_map/ppermute | solution.py:545
  8.1 0.0 copy-done.6
  8.1 0.0 copy-start.3
  8.1 0.0 copy-start.1
  8.1 0.0 slice-start
  8.1 0.0 slice-start.1
  8.1 3.5 %project_kept.1 = (f32[16,2048]{1,0:T(8,128)S(1)}, s32[64,128]{1,0:T(8,128)S(1)}) custom-call(s32[1]{0:T(128)} %bitcast.place.refs_0_, s32[1]{0:T(128)} %bitcast.1.bank.refs_1_, s32[8]{0:T(128)S(1)} %copy-done.6, bf16[8,1024]{1,0:T(8,128)(2,1)S(1)} %copy-done.4, bf16[8,1024]{1,0:T(8,128)(2,1)S(1)} %collective-permute-done.other_ref, bf16[1024,8192]{1,0:T(8,128)(2,1)} %w_ref.5), custom_call_target="tpu_custom_call" | custom-call | flops 67108864 | bytes 16777216 | tf_op jit(solution)/shard_map/project_kept/pallas_call | solution.py:203
  11.6 0.0 copy-start
  11.6 0.0 collective-permute-done.2.came_ref
  11.7 2.7 %collective-permute-start.3 = (f32[16,640]{1,0:T(8,128)S(1)}, f32[16,640]{1,0:T(8,128)S(1)}, u32[]{:S(2)}, u32[]{:S(2)}) collective-permute-start(f32[16,640]{1,0:T(8,128)S(1)} %get-tuple-element.29), channel_id=1, source_target_pairs={{0,8},{1,9},{2,10},{3,11},{4,12},{5,13},{6,14},{7,15},{8,0},{9,1},... | collective-permute-start | bytes 122888 | tf_op jit(solution)/shard_map/ppermute | solution.py:545
  14.3 1.3 %collective-permute-start.4 = (f32[16,640]{1,0:T(8,128)S(1)}, f32[16,640]{1,0:T(8,128)S(1)}, u32[]{:S(2)}, u32[]{:S(2)}) collective-permute-start(f32[16,640]{1,0:T(8,128)S(1)} %get-tuple-element.30), channel_id=1, source_target_pairs={{0,12},{1,11},{2,14},{3,9},{4,8},{5,15},{6,10},{7,13},{8,4},{9,3},... | collective-permute-start | bytes 122888 | tf_op jit(solution)/shard_map/ppermute | solution.py:545
  15.7 0.2 collective-permute-start.5
  15.9 0.0 copy-done.2
  15.9 0.0 slice-start.2
  15.9 0.6 %keyval.1.refs_7_ = f32[8,24,128]{2,1,0:T(8,128)S(1)} custom-call(bf16[8,1024]{1,0:T(8,128)(2,1)S(1)} %copy-done.4, bf16[1024,2048]{1,0:T(8,128)(2,1)S(1)} %copy-done.2), custom_call_target="tpu_custom_call" | custom-call | flops 33554432 | bytes 4194304 | tf_op jit(solution)/shard_map/keyval/pallas_call | solution.py:234
  16.6 0.0 collective-permute-done.3.refs_1_
  16.6 3.5 %collective-permute-done.4.refs_2_ = f32[16,640]{1,0:T(8,128)S(1)} collective-permute-done((f32[16,640]{1,0:T(8,128)S(1)}, f32[16,640]{1,0:T(8,128)S(1)}, u32[]{:S(2)}, u32[]{:S(2)}) %collective-permute-start.4) | collective-permute-done | bytes 40992 | tf_op jit(solution)/shard_map/ppermute | solution.py:545
  20.1 0.0 collective-permute-done.5.refs_3_
  20.1 0.0 copy-done.3
  20.1 0.4 correct.1
  20.5 0.0 collective-permute-start.6
  20.5 0.1 fusion
  20.6 1.1 %collective-permute-done.6.came_ref = f32[8,1024]{1,0:T(8,128)S(1)} collective-permute-done((f32[8,1024]{1,0:T(8,128)S(1)}, f32[8,1024]{1,0:T(8,128)S(1)}, u32[]{:S(2)}, u32[]{:S(2)}) %collective-permute-start.6) | collective-permute-done | bytes 32800 | tf_op jit(solution)/shard_map/ppermute | solution.py:533
  21.7 0.1 rotate.1.refs_0_.q_ref
  21.8 1.3 %collective-permute-start.7 = (bf16[1,64,128]{2,1,0:T(8,128)(2,1)S(1)}, bf16[1,64,128]{2,1,0:T(8,128)(2,1)S(1)}, u32[]{:S(2)}, u32[]{:S(2)}) collective-permute-start(bf16[1,64,128]{2,1,0:T(8,128)(2,1)S(1)} %rotate.1.refs_0_.q_ref), channel_id=1, source_target_pairs={{0,8},{1,9},{2,10},{3,11},{4,12},{5,13},{6,14},{7,15},{8,0},{9,1},... | collective-permute-start | bytes 49160 | tf_op jit(solution)/shard_map/ppermute | solution.py:545
  23.1 1.2 %collective-permute-start.8 = (bf16[1,64,128]{2,1,0:T(8,128)(2,1)S(1)}, bf16[1,64,128]{2,1,0:T(8,128)(2,1)S(1)}, u32[]{:S(2)}, u32[]{:S(2)}) collective-permute-start(bf16[1,64,128]{2,1,0:T(8,128)(2,1)S(1)} %rotate.1.refs_0_.q_ref), channel_id=1, source_target_pairs={{0,12},{1,11},{2,14},{3,9},{4,8},{5,15},{6,10},{7,13},{8,4},{9,3},... | collective-permute-start | bytes 49160 | tf_op jit(solution)/shard_map/ppermute | solution.py:545
  24.3 1.1 %collective-permute-start.9 = (bf16[1,64,128]{2,1,0:T(8,128)(2,1)S(1)}, bf16[1,64,128]{2,1,0:T(8,128)(2,1)S(1)}, u32[]{:S(2)}, u32[]{:S(2)}) collective-permute-start(bf16[1,64,128]{2,1,0:T(8,128)(2,1)S(1)} %rotate.1.refs_0_.q_ref), channel_id=1, source_target_pairs={{0,4},{1,3},{2,6},{3,1},{4,0},{5,7},{6,2},{7,5},{8,12},{9,11},{10,... | collective-permute-start | bytes 49160 | tf_op jit(solution)/shard_map/ppermute | solution.py:545
  25.4 1.1 %collective-permute-done.7.refs_1_ = bf16[1,64,128]{2,1,0:T(8,128)(2,1)S(1)} collective-permute-done((bf16[1,64,128]{2,1,0:T(8,128)(2,1)S(1)}, bf16[1,64,128]{2,1,0:T(8,128)(2,1)S(1)}, u32[]{:S(2)}, u32[]{:S(2)}) %collective-permute-start.7) | collective-permute-done | bytes 16416 | tf_op jit(solution)/shard_map/ppermute | solution.py:545
  26.5 2.1 %collective-permute-done.8.refs_2_ = bf16[1,64,128]{2,1,0:T(8,128)(2,1)S(1)} collective-permute-done((bf16[1,64,128]{2,1,0:T(8,128)(2,1)S(1)}, bf16[1,64,128]{2,1,0:T(8,128)(2,1)S(1)}, u32[]{:S(2)}, u32[]{:S(2)}) %collective-permute-start.8) | collective-permute-done | bytes 16416 | tf_op jit(solution)/shard_map/ppermute | solution.py:545
  28.7 0.0 collective-permute-done.9.refs_3_
  28.7 1.6 %collective-permute-start.10 = (bf16[4,64,128]{2,1,0:T(8,128)(2,1)S(1)}, bf16[4,64,128]{2,1,0:T(8,128)(2,1)S(1)}, u32[]{:S(2)}, u32[]{:S(2)}) collective-permute-start(bf16[4,64,128]{2,1,0:T(8,128)(2,1)S(1)} %join.1.refs_3_), channel_id=1, source_target_pairs={{0,2},{1,5},{2,0},{3,7},{4,6},{5,1},{6,4},{7,3},{8,10},{9,13},{10,... | collective-permute-start | bytes 196616 | tf_op jit(solution)/shard_map/ppermute | solution.py:545
  30.3 0.0 copy-done.1
  30.3 0.0 copy-done
  30.3 0.0 slice-start.3
  30.3 1.6 %attend.2.refs_6_ = bf16[4,80,128]{2,1,0:T(8,128)(2,1)S(1)} custom-call(s32[1]{0:T(128)} %bitcast.place.refs_0_, s32[1]{0:T(128)} %bitcast.1.bank.refs_1_, s32[64,128]{1,0:T(8,128)S(1)} %get-tuple-element.22.refs_2_, bf16[4,64,128]{2,1,0:T(8,128)(2,1)S(1)} %join.1.refs_3_, bf16[8,256,1024]{2,1,0:T(8,128)(2,1)S(1)} %copy-done, bf16[8,256,1024]{2,1,0:T(8,128)(2,1)S(1)} %copy-done.1), custom_call_target="tpu_custom_call" | custom-call | flops 33554432 | bytes 4194304 | tf_op jit(solution)/shard_map/attend/pallas_call | solution.py:420
  31.9 1.2 %collective-permute-done.10.refs_3_ = bf16[4,64,128]{2,1,0:T(8,128)(2,1)S(1)} collective-permute-done((bf16[4,64,128]{2,1,0:T(8,128)(2,1)S(1)}, bf16[4,64,128]{2,1,0:T(8,128)(2,1)S(1)}, u32[]{:S(2)}, u32[]{:S(2)}) %collective-permute-start.10) | collective-permute-done | bytes 65568 | tf_op jit(solution)/shard_map/ppermute | solution.py:545
  33.0 1.6 %attend.3 = bf16[8,96,128]{2,1,0:T(8,128)(2,1)S(1)} custom-call(s32[1]{0:T(128)} %bitcast.place.refs_0_, s32[1]{0:T(128)} %bitcast.1.bank.refs_1_, s32[64,128]{1,0:T(8,128)S(1)} %get-tuple-element.22.refs_2_, bf16[4,64,128]{2,1,0:T(8,128)(2,1)S(1)} %collective-permute-done.10.refs_3_, bf16[8,256,1024]{2,1,0:T(8,128)(2,1)S(1)} %copy-done, ...), custom_call_target="tpu_custom_call" | custom-call | flops 33554432 | bytes 16777216 | tf_op jit(solution)/shard_map/attend/pallas_call | solution.py:420
  34.6 11.8 %all_to_all.10.parts_ref = bf16[8,96,128]{2,1,0:T(8,128)(2,1)S(1)} all-to-all(bf16[8,96,128]{2,1,0:T(8,128)(2,1)S(1)} %attend.3), channel_id=1, replica_groups=mesh['groups'=2,'tensor'=8,'bank'=2] {'tensor'}, dimensions={0} | all-to-all | bytes 393216 | tf_op jit(solution)/shard_map/all_to_all | solution.py:537
  46.4 0.0 slice-done
  46.4 0.0 slice-done.1
  46.4 0.0 slice-done.2
  46.4 0.0 slice-done.3
  46.4 2.7 %output.1 = bf16[8,8,1024]{2,1,0:T(8,128)(2,1)S(1)} custom-call(bf16[8,96,128]{2,1,0:T(8,128)(2,1)S(1)} %all_to_all.10.parts_ref, bf16[1,64,128]{2,1,0:T(8,128)(2,1)S(1)} %rotate.1.refs_0_.q_ref, f32[8,128]{1,0:T(8,128)S(1)} %get-tuple-element.40.cos_ref, f32[8,128]{1,0:T(8,128)S(1)} %get-tuple-element.39.sin_ref, bf16[1024,8192]{1,0:T(8,128)(2,1)S(1)} %bitcast.6), custom_call_target="tpu_custom_call" | custom-call | flops 134217728 | bytes 16777216 | tf_op jit(solution)/shard_map/output/pallas_call | solution.py:499
  49.1 9.8 %all_to_all.11.parts_ref = bf16[8,8,1024]{2,1,0:T(8,128)(2,1)S(1)} all-to-all(bf16[8,8,1024]{2,1,0:T(8,128)(2,1)S(1)} %output.1), channel_id=1, replica_groups=mesh['groups'=2,'tensor'=8,'bank'=2] {'tensor'}, dimensions={0} | all-to-all | bytes 262144 | tf_op jit(solution)/shard_map/all_to_all | solution.py:537
  58.8 0.6 %residual.1 = bf16[8,1024]{1,0:T(8,128)(2,1)} custom-call(bf16[8,1024]{1,0:T(8,128)(2,1)S(1)} %copy-done.4, bf16[8,8,1024]{2,1,0:T(8,128)(2,1)S(1)} %all_to_all.11.parts_ref), custom_call_target="tpu_custom_call" | custom-call | tf_op jit(solution)/shard_map/residual/pallas_call | solution.py:522
  (5 shorter events, 0.0 us)
Async XLA Ops:
  0.0 2.1 %copy-start.4 = (bf16[8,1024]{1,0:T(8,128)(2,1)S(1)}, bf16[8,1024]{1,0:T(8,128)(2,1)}, u32[]{:S(2)}) copy-start(bf16[8,1024]{1,0:T(8,128)(2,1)} %x_ref.6) | copy-start | bytes 49156
  0.0 2.1 %copy-start.5 = (s32[8]{0:T(128)S(1)}, s32[8]{0:T(128)}, u32[]{:S(2)}) copy-start(s32[8]{0:T(128)} %param.11) | copy-start | bytes 100
  0.0 2.1 %collective-permute-start = (bf16[8,1024]{1,0:T(8,128)(2,1)}, bf16[8,1024]{1,0:T(8,128)(2,1)S(1)}, u32[]{:S(2)}, u32[]{:S(2)}) collective-permute-start(bf16[8,1024]{1,0:T(8,128)(2,1)} %x_ref.6), channel_id=1, source_target_pairs={{0,1},{1,0},{2,3},{3,2},{4,5},{5,4},{6,7},{7,6},{8,9},{9,8},{10,11... | collective-permute-start | bytes 49160 | tf_op jit(solution)/shard_map/ppermute | solution.py:533
  0.5 1.6 %collective-permute-start.1 = (s32[8]{0:T(128)}, s32[8]{0:T(128)S(1)}, u32[]{:S(2)}, u32[]{:S(2)}) collective-permute-start(s32[8]{0:T(128)} %param.11), channel_id=1, source_target_pairs={{0,1},{1,0},{2,3},{3,2},{4,5},{5,4},{6,7},{7,6},{8,9},{9,8},{10,11... | collective-permute-start | bytes 104 | tf_op jit(solution)/shard_map/ppermute | solution.py:533
  2.1 6.0 %copy-start.6 = (s32[8]{0:T(128)S(1)}, s32[8]{0:T(128)}, u32[]{:S(2)}) copy-start(s32[8]{0:T(128)} %length.1) | copy-start | bytes 100
  5.1 10.8 %copy-start.2 = (bf16[1024,2048]{1,0:T(8,128)(2,1)S(1)}, bf16[1024,2048]{1,0:T(8,128)(2,1)}, u32[]{:S(2)}) copy-start(bf16[1024,2048]{1,0:T(8,128)(2,1)} %w_ref.6) | copy-start | bytes 12582916
  5.1 6.5 %collective-permute-start.2 = (f32[16,2176]{1,0:T(8,128)S(1)}, f32[16,2176]{1,0:T(8,128)S(1)}, u32[]{:S(2)}, u32[]{:S(2)}) collective-permute-start(f32[16,2176]{1,0:T(8,128)S(1)} %get-tuple-element.26), channel_id=1, source_target_pairs={{0,2},{1,5},{2,0},{3,7},{4,6},{5,1},{6,4},{7,3},{8,10},{9,13},{10,... | collective-permute-start | bytes 417800 | tf_op jit(solution)/shard_map/ppermute | solution.py:545
  8.1 12.0 %copy-start.3 = (bf16[16,64,1024]{2,1,0:T(8,128)(2,1)S(1)}, bf16[16,64,1024]{2,1,0:T(8,128)(2,1)}, u32[]{:S(2)}) copy-start(bf16[16,64,1024]{2,1,0:T(8,128)(2,1)} %up_ref.1) | copy-start | bytes 6291460
  8.1 22.2 %copy-start.1 = (bf16[8,256,1024]{2,1,0:T(8,128)(2,1)S(1)}, bf16[8,256,1024]{2,1,0:T(8,128)(2,1)}, u32[]{:S(2)}) copy-start(bf16[8,256,1024]{2,1,0:T(8,128)(2,1)} %refs_5_.3) | copy-start | bytes 12582916
  8.1 38.2 %slice-start = ((s8[16777216]{0:T(1024)(128)(4,1)}), s8[4194304]{0:T(1024)(128)(4,1)S(1)}, s32[]{:S(2)}) async-start(s8[16777216]{0:T(1024)(128)(4,1)} %bitcast.5), calls=%async_computation.2 | async-start | bytes 8388608
  8.1 38.2 %slice-start.1 = ((s8[16777216]{0:T(1024)(128)(4,1)}), s8[4194304]{0:T(1024)(128)(4,1)S(1)}, s32[]{:S(2)}) async-start(s8[16777216]{0:T(1024)(128)(4,1)} %bitcast.5), calls=%async_computation.3 | async-start | bytes 8388608
  11.6 18.7 %copy-start = (bf16[8,256,1024]{2,1,0:T(8,128)(2,1)S(1)}, bf16[8,256,1024]{2,1,0:T(8,128)(2,1)}, u32[]{:S(2)}) copy-start(bf16[8,256,1024]{2,1,0:T(8,128)(2,1)} %refs_4_.3) | copy-start | bytes 12582916
  11.7 5.0 %collective-permute-start.3 = (f32[16,640]{1,0:T(8,128)S(1)}, f32[16,640]{1,0:T(8,128)S(1)}, u32[]{:S(2)}, u32[]{:S(2)}) collective-permute-start(f32[16,640]{1,0:T(8,128)S(1)} %get-tuple-element.29), channel_id=1, source_target_pairs={{0,8},{1,9},{2,10},{3,11},{4,12},{5,13},{6,14},{7,15},{8,0},{9,1},... | collective-permute-start | bytes 122888 | tf_op jit(solution)/shard_map/ppermute | solution.py:545
  14.3 5.8 %collective-permute-start.4 = (f32[16,640]{1,0:T(8,128)S(1)}, f32[16,640]{1,0:T(8,128)S(1)}, u32[]{:S(2)}, u32[]{:S(2)}) collective-permute-start(f32[16,640]{1,0:T(8,128)S(1)} %get-tuple-element.30), channel_id=1, source_target_pairs={{0,12},{1,11},{2,14},{3,9},{4,8},{5,15},{6,10},{7,13},{8,4},{9,3},... | collective-permute-start | bytes 122888 | tf_op jit(solution)/shard_map/ppermute | solution.py:545
  15.7 4.5 %collective-permute-start.5 = (f32[16,640]{1,0:T(8,128)S(1)}, f32[16,640]{1,0:T(8,128)S(1)}, u32[]{:S(2)}, u32[]{:S(2)}) collective-permute-start(f32[16,640]{1,0:T(8,128)S(1)} %get-tuple-element.31), channel_id=1, source_target_pairs={{0,4},{1,3},{2,6},{3,1},{4,0},{5,7},{6,2},{7,5},{8,12},{9,11},{10,... | collective-permute-start | bytes 122888 | tf_op jit(solution)/shard_map/ppermute | solution.py:545
  15.9 30.4 %slice-start.2 = ((s8[16777216]{0:T(1024)(128)(4,1)}), s8[4194304]{0:T(1024)(128)(4,1)S(1)}, s32[]{:S(2)}) async-start(s8[16777216]{0:T(1024)(128)(4,1)} %bitcast.5), calls=%async_computation.4 | async-start | bytes 8388608
  20.5 1.2 %collective-permute-start.6 = (f32[8,1024]{1,0:T(8,128)S(1)}, f32[8,1024]{1,0:T(8,128)S(1)}, u32[]{:S(2)}, u32[]{:S(2)}) collective-permute-start(f32[8,1024]{1,0:T(8,128)S(1)} %get-tuple-element.37), channel_id=1, source_target_pairs={{0,1},{1,0},{2,3},{3,2},{4,5},{5,4},{6,7},{7,6},{8,9},{9,8},{10,11... | collective-permute-start | bytes 98312 | tf_op jit(solution)/shard_map/ppermute | solution.py:533
  21.8 4.7 %collective-permute-start.7 = (bf16[1,64,128]{2,1,0:T(8,128)(2,1)S(1)}, bf16[1,64,128]{2,1,0:T(8,128)(2,1)S(1)}, u32[]{:S(2)}, u32[]{:S(2)}) collective-permute-start(bf16[1,64,128]{2,1,0:T(8,128)(2,1)S(1)} %rotate.1.refs_0_.q_ref), channel_id=1, source_target_pairs={{0,8},{1,9},{2,10},{3,11},{4,12},{5,13},{6,14},{7,15},{8,0},{9,1},... | collective-permute-start | bytes 49160 | tf_op jit(solution)/shard_map/ppermute | solution.py:545
  23.1 5.5 %collective-permute-start.8 = (bf16[1,64,128]{2,1,0:T(8,128)(2,1)S(1)}, bf16[1,64,128]{2,1,0:T(8,128)(2,1)S(1)}, u32[]{:S(2)}, u32[]{:S(2)}) collective-permute-start(bf16[1,64,128]{2,1,0:T(8,128)(2,1)S(1)} %rotate.1.refs_0_.q_ref), channel_id=1, source_target_pairs={{0,12},{1,11},{2,14},{3,9},{4,8},{5,15},{6,10},{7,13},{8,4},{9,3},... | collective-permute-start | bytes 49160 | tf_op jit(solution)/shard_map/ppermute | solution.py:545
  24.3 4.3 %collective-permute-start.9 = (bf16[1,64,128]{2,1,0:T(8,128)(2,1)S(1)}, bf16[1,64,128]{2,1,0:T(8,128)(2,1)S(1)}, u32[]{:S(2)}, u32[]{:S(2)}) collective-permute-start(bf16[1,64,128]{2,1,0:T(8,128)(2,1)S(1)} %rotate.1.refs_0_.q_ref), channel_id=1, source_target_pairs={{0,4},{1,3},{2,6},{3,1},{4,0},{5,7},{6,2},{7,5},{8,12},{9,11},{10,... | collective-permute-start | bytes 49160 | tf_op jit(solution)/shard_map/ppermute | solution.py:545
  28.7 4.3 %collective-permute-start.10 = (bf16[4,64,128]{2,1,0:T(8,128)(2,1)S(1)}, bf16[4,64,128]{2,1,0:T(8,128)(2,1)S(1)}, u32[]{:S(2)}, u32[]{:S(2)}) collective-permute-start(bf16[4,64,128]{2,1,0:T(8,128)(2,1)S(1)} %join.1.refs_3_), channel_id=1, source_target_pairs={{0,2},{1,5},{2,0},{3,7},{4,6},{5,1},{6,4},{7,3},{8,10},{9,13},{10,... | collective-permute-start | bytes 196616 | tf_op jit(solution)/shard_map/ppermute | solution.py:545
  30.3 16.1 %slice-start.3 = ((s8[16777216]{0:T(1024)(128)(4,1)}), s8[4194304]{0:T(1024)(128)(4,1)S(1)}, s32[]{:S(2)}) async-start(s8[16777216]{0:T(1024)(128)(4,1)} %bitcast.5), calls=%async_computation.5 | async-start | bytes 8388608
